TPU v7x, 32 devices: a whole 2x2x4 slice. The times are simulated.
32 devices in a mesh: groups: 2 (over y), ex: 4 (over z), ey: 4 (over x, core).
Axes of the slice: x: 2, y: 2, z: 4, core: 2. Of those that a mesh axis runs over, the one named last changes fastest.
Arguments:
- inputs: bfloat16 [2048, 4096], P(('groups', 'ex'), 'ey'), parts along dimension 0, may hold values from -6 to 6
- grad_output: bfloat16 [2048, 4096], P(('groups', 'ex'), 'ey'), parts along dimension 0, may hold values from -6 to 6
- routes: int32 [2048, 8], P(('groups', 'ex')), parts along dimension 0, may hold values from 0 to 127, as said below
- gate_probs: bfloat16 [2048, 8], P(('groups', 'ex')), parts along dimension 0, may hold values from 0.19921875 to 1
- gate_up: bfloat16 [4, 2, 1536, 4096], P('ex', None, None, 'ey'), may hold values from -0.09375 to 0.09375
- down_proj: bfloat16 [4, 1536, 4096], P('ex', None, 'ey'), may hold values from -0.15625 to 0.15625
Outputs:
- grad_inputs: bfloat16 [2048, 4096], P(('groups', 'ex'), 'ey'), parts along dimension 0
- grad_gate_up: bfloat16 [4, 4, 1536, 4096], P('ex', 'groups', None, 'ey'), parts along dimension 1
- grad_down: bfloat16 [4, 3072, 4096], P('ex', 'groups', 'ey'), parts along dimension 1
There are 2 independent parts, one for each index of `groups`. A program takes and returns all parts, laid end to end along the dimension named above; an argument that names none is the same for every part. Nothing has to cross between parts.
Inputs may be any that keep to these rules, and one draw needn't show every extreme that they name: `routes`: each row names 8 different experts. Within the 256 rows of one index of ex (aligned blocks), every expert is named by either no row or exactly 40 rows, except at most one expert of the block, which is named by fewer.
All inputs are finite; a program needn't handle non-finite values.
Results may differ from a plain program's by a relative error of at most 0.017.
Values may be sent and summed in bfloat16 or wider, within the bound.
No kernel may reach another device: no remote copies, remote signals or barrier semaphores. Data moves between devices by JAX's collectives and lax.ppermute only.
A program may use at most 64 MiB of HBM per device.

v0:
```python
import jax
import jax.numpy as jnp
from jax import lax
from jax.sharding import PartitionSpec as P

EXPERTS = 128


def entering(value, axis, join, neutral):
    count, mine = (lax.axis_size(axis), lax.axis_index(axis))
    pieces = lax.all_gather(value, axis)
    so_far = jnp.full_like(value, 0) + jnp.asarray(neutral, value.dtype)

    def step(position, so_far):
        longer = join(so_far, pieces[position])
        return jnp.where(position < mine, longer, so_far)

    return lax.fori_loop(0, count - 1, step, so_far)


def swiglu_backward(gate_sum, up_sum, grad_act):
    sigmoid_gate = jax.nn.sigmoid(gate_sum)
    silu_gate = gate_sum * sigmoid_gate
    activation = (silu_gate * up_sum).astype(jnp.bfloat16)
    grad_gate = (grad_act * up_sum * sigmoid_gate * (1.0 + gate_sum * (1.0 - sigmoid_gate))).astype(
        jnp.bfloat16
    )
    grad_up = (grad_act * silu_gate).astype(jnp.bfloat16)
    return (activation, grad_gate, grad_up)


def take_slots(grad_rows, slot_index, capacity):
    usable = (slot_index >= 0) & (slot_index < capacity)
    clipped = jnp.clip(slot_index, 0, capacity - 1).astype(jnp.int32)
    picked = jnp.take(grad_rows, clipped, axis=0)
    return jnp.where(usable[:, None], picked, 0.0)


def local(inputs, grad_output, routes, gate_probs, gate_up, down_proj):
    expert_count = lax.axis_size("ex")
    my_expert = lax.axis_index("ex")
    token_rows = inputs.shape[0]
    capacity = 5 * token_rows * expert_count * routes.shape[1] // (4 * EXPERTS)
    expert_iota = jnp.arange(expert_count, dtype=jnp.int32)
    slot_iota = jnp.arange(capacity, dtype=jnp.int32)
    matches = routes[:, :, None] == expert_iota[None, None, :]
    routed = jnp.any(matches, axis=1).astype(jnp.int32)
    expert_prob = jnp.sum(
        jnp.where(matches, gate_probs.astype(jnp.float32)[:, :, None], 0.0), axis=1
    ).astype(jnp.bfloat16)
    local_rank = jnp.cumsum(routed, axis=0) - routed
    local_count = jnp.sum(routed, axis=0)
    offsets = entering(
        local_count, "ex", lambda earlier, later: earlier + later, jnp.zeros_like(local_count)
    )
    global_slot = offsets[None, :] + local_rank
    slot_table = jnp.where(routed == 1, global_slot, -1)
    all_slots = lax.all_gather(slot_table, "ex", axis=0, tiled=True)
    my_slots = lax.dynamic_slice_in_dim(all_slots, my_expert, 1, 1)[:, 0]
    piece_in = lax.all_gather(inputs, "ex", axis=0, tiled=True)
    piece_grad = lax.all_gather(grad_output, "ex", axis=0, tiled=True)
    piece_prob = lax.all_gather(expert_prob, "ex", axis=0, tiled=True)
    piece_slots = my_slots
    selector = (piece_slots[None, :] == slot_iota[:, None]).astype(jnp.bfloat16)
    prob_column = lax.dynamic_slice_in_dim(piece_prob, my_expert, 1, 1).astype(jnp.float32)
    scaled = (piece_grad.astype(jnp.float32) * prob_column).astype(jnp.bfloat16)
    new_in = jnp.dot(selector, piece_in, preferred_element_type=jnp.float32)
    new_grad = jnp.dot(selector, scaled, preferred_element_type=jnp.float32)
    rows_in = new_in.astype(jnp.bfloat16)
    rows_grad = new_grad.astype(jnp.bfloat16)
    gate_weight = gate_up[0, 0]
    up_weight = gate_up[0, 1]
    down_weight = down_proj[0]
    contract_width = (((1,), (1,)), ((), ()))
    gate_part = lax.dot_general(
        rows_in, gate_weight, contract_width, preferred_element_type=jnp.float32
    )
    up_part = lax.dot_general(
        rows_in, up_weight, contract_width, preferred_element_type=jnp.float32
    )
    grad_part = lax.dot_general(
        rows_grad, down_weight, contract_width, preferred_element_type=jnp.float32
    )
    gate_sum, up_sum, grad_act = (
        lax.psum(gate_part.astype(jnp.bfloat16), "ey").astype(jnp.float32),
        lax.psum(up_part.astype(jnp.bfloat16), "ey").astype(jnp.float32),
        lax.psum(grad_part.astype(jnp.bfloat16), "ey").astype(jnp.float32),
    )
    activation, grad_gate, grad_up = swiglu_backward(gate_sum, up_sum, grad_act)
    contract_slots = (((0,), (0,)), ((), ()))
    down_grad = lax.dot_general(
        activation, rows_grad, contract_slots, preferred_element_type=jnp.float32
    )
    gate_grad = lax.dot_general(
        grad_gate, rows_in, contract_slots, preferred_element_type=jnp.float32
    )
    up_grad = lax.dot_general(grad_up, rows_in, contract_slots, preferred_element_type=jnp.float32)
    pair_grad = jnp.stack([gate_grad, up_grad]).astype(jnp.bfloat16)[None]
    grad_rows = jnp.dot(grad_gate, gate_weight, preferred_element_type=jnp.float32) + jnp.dot(
        grad_up, up_weight, preferred_element_type=jnp.float32
    )
    piece_slots = my_slots
    grad_inputs = lax.psum_scatter(
        take_slots(grad_rows, piece_slots, capacity).astype(jnp.bfloat16),
        "ex",
        scatter_dimension=0,
        tiled=True,
    )
    return (grad_inputs, pair_grad, down_grad.astype(jnp.bfloat16)[None])


def solution(mesh):
    return jax.shard_map(
        local,
        mesh=mesh,
        in_specs=(
            P(("groups", "ex"), "ey"),
            P(("groups", "ex"), "ey"),
            P(("groups", "ex"), None),
            P(("groups", "ex"), None),
            P("ex", None, None, "ey"),
            P("ex", None, "ey"),
        ),
        out_specs=(
            P(("groups", "ex"), "ey"),
            P("ex", "groups", None, "ey"),
            P("ex", "groups", "ey"),
        ),
        check_vma=False,
    )
```

profile of v0, /device:TPU:0, one launch (start us, length us, event | category | flops | bytes accessed | tf_op | source)
XLA Modules:
  0.0 208.4 jit_solution(14577458342184116713)
XLA Ops:
  8.7 1.2 dynamic-slice
  10.6 0.7 fusion.44
  11.7 9.9 %all-reduce = s32[16]{0:T(128)S(1)} all-reduce(s32[16]{0:T(128)S(1)} %dynamic-update-slice), channel_id=2, replica_groups=mesh['groups'=2,'ex'=4,'ey'=4] {'ex'}, use_global_device_ids=true, to_apply=%add | all-reduce | flops 16 | bytes 128
  21.7 1.2 reduce-window.6
  23.9 0.7 select_reduce_fusion
  24.6 12.0 %all_gather.22 = bf16[1024,4]{0,1:T(4,128)(2,1)S(1)} all-gather(bf16[256,4]{0,1:T(4,128)(2,1)S(1)} %select_reduce_fusion), channel_id=1, replica_groups=mesh['groups'=2,'ex'=4,'ey'=4] {'ex'}, dimensions={0}, use_global_device_ids=true | all-gather | bytes 10240 | tf_op jit(solution)/shard_map/all_gather | solution.py:62
  36.9 13.5 %all_gather.20 = s32[1024,4]{0,1:T(4,128)S(1)} all-gather(s32[256,4]{0,1:T(4,128)S(1)} %fusion.46), channel_id=1, replica_groups=mesh['groups'=2,'ex'=4,'ey'=4] {'ex'}, dimensions={0}, use_global_device_ids=true | all-gather | bytes 20480 | tf_op jit(solution)/shard_map/all_gather | solution.py:58
  51.0 7.6 %all-gather.6.cloned.1.call-done = bf16[1024,1024]{1,0:T(8,128)(2,1)} async-done(((bf16[256,1024]{1,0:T(8,128)(2,1)}), bf16[1024,1024]{1,0:T(8,128)(2,1)}) %all-gather.6.cloned.1.call-update) | async-done | bytes 2097168 | tf_op jit(solution)/shard_map/all_gather | solution.py:60
  58.6 2.1 convolution_convert_fusion.3
  60.7 3.7 %fusion.20 = bf16[80,1536]{1,0:T(8,128)(2,1)} fusion(bf16[80,1024]{1,0:T(8,128)(2,1)S(1)} %convolution_convert_fusion.3, bf16[1,2,1536,1024]{3,2,1,0:T(8,128)(2,1)} %param.12), kind=kOutput, calls=%fused_computation.27 | convolution fusion | flops 251781120 | bytes 3555328 | tf_op jit(solution)/shard_map/dot_general | solution.py:78
  64.4 3.8 %fusion.23 = bf16[80,1536]{1,0:T(8,128)(2,1)} fusion(bf16[80,1024]{1,0:T(8,128)(2,1)S(1)} %convolution_convert_fusion.3, bf16[1,2,1536,1024]{3,2,1,0:T(8,128)(2,1)} %param.12), kind=kOutput, calls=%fused_computation.28 | convolution fusion | flops 251781120 | bytes 3555328 | tf_op jit(solution)/shard_map/dot_general | solution.py:75
  68.2 36.6 %all-gather.4.cloned.1.call-done = bf16[1024,1024]{1,0:T(8,128)(2,1)} async-done(((bf16[256,1024]{1,0:T(8,128)(2,1)}), bf16[1024,1024]{1,0:T(8,128)(2,1)}) %all-gather.4.cloned.1.call-update) | async-done | bytes 2097168 | tf_op jit(solution)/shard_map/all_gather | solution.py:61
  104.9 2.2 %fusion.31 = bf16[80,1024]{1,0:T(8,128)(2,1)S(1)} fusion(bf16[1024,1024]{1,0:T(8,128)(2,1)} %all-gather.4.cloned.1.call-done, f32[1024]{0:T(1024)S(1)} %bitcast.59, s32[1024]{0:T(1024)S(1)} %bitcast.56), kind=kOutput, calls=%fused_computation.32 | convolution fusion | flops 171081728 | bytes 2269184 | tf_op jit(solution)/shard_map/dot_general | solution.py:68
  107.8 1.8 fusion.17
  110.8 32.1 %all-reduce.4.cloned.1.call-done = (bf16[80,1536]{1,0:T(8,128)(2,1)}, bf16[80,1536]{1,0:T(8,128)(2,1)}, bf16[80,1536]{1,0:T(8,128)(2,1)}) async-done(((bf16[80,1536]{1,0:T(8,128)(2,1)}, bf16[80,1536]{1,0:T(8,128)(2,1)}, bf16[80,1536]{1,0:T(8,128)(2,1)}), (bf16[80,1536]{1,0:T(8,128)(2,1)}, bf16[80,1536]{1,0:T(8,128)(2,1)}, bf16[80,1536]{1,0:T(8,128)(2,1)})) %all-reduce.4.cloned.1.call-update) | async-done | bytes 737296 | tf_op jit(solution)/shard_map/psum | solution.py:86
  142.9 3.0 %fusion.3 = f32[80,1024]{1,0:T(8,128)S(1)} fusion(bf16[1,2,1536,1024]{3,2,1,0:T(8,128)(2,1)} %param.12, bf16[80,1536]{1,0:T(8,128)(2,1)} %get-tuple-element.106, bf16[80,1536]{1,0:T(8,128)(2,1)} %get-tuple-element.107, bf16[80,1536]{1,0:T(8,128)(2,1)} %get-tuple-element.108), kind=kOutput, calls=%fused_computation.12 | convolution fusion | flops 253255680 | bytes 4210688 | tf_op jit(solution)/shard_map/dot_general | solution.py:99
  146.0 2.6 %fusion.28 = bf16[80,1024]{1,0:T(8,128)(2,1)S(1)} fusion(f32[80,1024]{1,0:T(8,128)S(1)} %fusion.3, bf16[1,2,1536,1024]{3,2,1,0:T(8,128)(2,1)} %param.12, bf16[80,1536]{1,0:T(8,128)(2,1)S(1)} %copy-done.5, bf16[80,1536]{1,0:T(8,128)(2,1)S(1)} %copy-done.1), kind=kOutput, calls=%fused_computation.31 | convolution fusion | flops 252805120 | bytes 4128768 | tf_op jit(solution)/shard_map/dot_general | solution.py:99
  148.6 5.6 %gather_fusion = bf16[1024,1024]{1,0:T(8,128)(2,1)} fusion(bf16[80,1024]{1,0:T(8,128)(2,1)S(1)} %fusion.28, s32[1024]{0:T(1024)} %broadcast_clamp_fusion), kind=kCustom, calls=%fused_computation | custom fusion | bytes 4198400 | tf_op jit(solution)/shard_map/jit(_take)/gather | solution.py:35
  154.1 3.2 %select_convert_fusion = bf16[1024,1024]{1,0:T(8,128)(2,1)} fusion(bf16[1024,1024]{1,0:T(8,128)(2,1)} %gather_fusion, pred[1024]{0:T(1024)(128)(4,1)} %get-tuple-element.111, pred[1024]{0:T(1024)(128)(4,1)} %get-tuple-element.109), kind=kLoop, calls=%fused_computation.4 | loop fusion | flops 2097152 | bytes 4196352 | tf_op jit(solution)/shard_map/convert_element_type | solution.py:104
  157.4 2.0 fusion.1
  159.5 2.7 %fusion.2 = bf16[1,1536,1024]{2,1,0:T(8,128)(2,1)} fusion(bf16[80,1024]{1,0:T(8,128)(2,1)S(1)} %copy-done.8, bf16[80,1536]{1,0:T(8,128)(2,1)S(1)} %copy-done.4, bf16[80,1536]{1,0:T(8,128)(2,1)S(1)} %copy-done.1), kind=kOutput, calls=%fused_computation.11 | convolution fusion | flops 254214144 | bytes 3801088 | tf_op jit(solution)/shard_map/dot_general | solution.py:91
  162.2 1.0 fusion
  163.2 3.2 %pad_maximum_fusion = bf16[1,2,1536,1024]{3,2,1,0:T(8,128)(2,1)} fusion(bf16[1,1,1536,1024]{3,2,1,0:T(8,128)(2,1)S(1)} %fusion.1, bf16[1,1,1536,1024]{3,2,1,0:T(8,128)(2,1)S(1)} %fusion), kind=kLoop, calls=%fused_computation.3 | loop fusion | flops 3145728 | bytes 12582912 | tf_op jit(solution)/shard_map/stack | solution.py:98
  166.5 35.4 %reduce-scatter.2.cloned.1.call-done = bf16[256,1024]{1,0:T(8,128)(2,1)} async-done(((bf16[1024,1024]{1,0:T(8,128)(2,1)}), bf16[256,1024]{1,0:T(8,128)(2,1)}) %reduce-scatter.2.cloned.1.call-update) | async-done | bytes 524304 | tf_op jit(solution)/shard_map/reduce_scatter | solution.py:103
  (49 shorter events, 5.8 us)
Async XLA Ops:
  7.2 100.6 %copy-start = (bf16[1,1536,1024]{2,1,0:T(8,128)(2,1)S(1)}, bf16[1,1536,1024]{2,1,0:T(8,128)(2,1)}, u32[]{:S(2)}) copy-start(bf16[1,1536,1024]{2,1,0:T(8,128)(2,1)} %param.13) | copy-start | bytes 9437188
  7.2 51.4 %all-gather.6.cloned.1.call-start = ((), (), s32[]{:S(2)}) async-start(), calls=%async_computation.2 | async-start | bytes 2621440 | tf_op jit(solution)/shard_map/all_gather | solution.py:60
  7.9 97.0 %all-gather.4.cloned.1.call-start = ((), (), s32[]{:S(2)}) async-start(), calls=%async_computation.1 | async-start | bytes 2621440 | tf_op jit(solution)/shard_map/all_gather | solution.py:61
  8.7 134.3 %all-reduce.4.cloned.1.call-start = ((), (), s32[]{:S(2)}) async-start(), calls=%async_computation.4 | async-start | bytes 1474560 | tf_op jit(solution)/shard_map/psum | solution.py:86
  60.7 3.7 %copy-start.2 = (bf16[80,1024]{1,0:T(8,128)(2,1)}, bf16[80,1024]{1,0:T(8,128)(2,1)S(1)}, u32[]{:S(2)}) copy-start(bf16[80,1024]{1,0:T(8,128)(2,1)S(1)} %convolution_convert_fusion.3) | copy-start | bytes 491524
  107.1 0.7 copy-start.7
  109.6 92.3 %reduce-scatter.2.cloned.1.call-start = ((), (), s32[]{:S(2)}) async-start(), calls=%async_computation.3 | async-start | bytes 2621440 | tf_op jit(solution)/shard_map/reduce_scatter | solution.py:103
  142.9 3.0 %copy-start.1 = (bf16[80,1536]{1,0:T(8,128)(2,1)S(1)}, bf16[80,1536]{1,0:T(8,128)(2,1)}, u32[]{:S(2)}) copy-start(bf16[80,1536]{1,0:T(8,128)(2,1)} %get-tuple-element.108) | copy-start | bytes 737284
  142.9 3.0 %copy-start.5 = (bf16[80,1536]{1,0:T(8,128)(2,1)S(1)}, bf16[80,1536]{1,0:T(8,128)(2,1)}, u32[]{:S(2)}) copy-start(bf16[80,1536]{1,0:T(8,128)(2,1)} %get-tuple-element.107) | copy-start | bytes 737284
  154.1 3.2 %copy-start.3 = (bf16[80,1024]{1,0:T(8,128)(2,1)S(1)}, bf16[80,1024]{1,0:T(8,128)(2,1)}, u32[]{:S(2)}) copy-start(bf16[80,1024]{1,0:T(8,128)(2,1)} %copy-done.2) | copy-start | bytes 491524
  157.4 2.1 copy-start.4
  157.4 2.1 copy-start.8
  157.4 4.8 %copy-start.6 = (bf16[80,1536]{1,0:T(8,128)(2,1)S(1)}, bf16[80,1536]{1,0:T(8,128)(2,1)}, u32[]{:S(2)}) copy-start(bf16[80,1536]{1,0:T(8,128)(2,1)} %get-tuple-element.107) | copy-start | bytes 737284
Sparse Core Ops, SparseCore 0:
  9.6 48.9 all-gather.5
  60.2 44.6 all-gather.3
  109.7 33.1 all-reduce.3
  157.5 44.3 reduce-scatter.1
where the time goes:
time: 209 us; the launch traced here: 208 us
  waiting for transfers between devices  113 us (54%)
  blocking collectives  35.4 us (17%)
  matrix products  25 us (12%)
  between operations  14.6 us (7%)
  other arithmetic  11.9 us (6%)
  local copies, waits for them, and re-layouts  8.16 us (4%)
    all_gather x1, waiting for transfers between devices, local(): piece_grad = lax.all_gather(grad_output, 'ex', axis=0, tiled=True)  36.6 us
    reduce_scatter x1, waiting for transfers between devices, local(): lax.psum_scatter(take_slots(grad_rows, piece_slots, capacity).astype(jnp....  35.4 us
    psum x1, waiting for transfers between devices, local(): lax.psum(up_part.astype(jnp.bfloat16), 'ey').astype(jnp.float32)  32.1 us
    all_gather x1, blocking collectives, local(): all_slots = lax.all_gather(slot_table, 'ex', axis=0, tiled=True)  13.5 us
    all_gather x1, blocking collectives, local(): piece_prob = lax.all_gather(expert_prob, 'ex', axis=0, tiled=True)  12 us
    unnamed x1, blocking collectives  9.89 us
    all_gather x1, waiting for transfers between devices, local(): piece_in = lax.all_gather(inputs, 'ex', axis=0, tiled=True)  7.56 us
    gather x1, local copies, waits for them, and re-layouts, take_slots(): picked = jnp.take(grad_rows, clipped, axis=0)  5.59 us
  transfers between devices with their start and end apart: 4, of which 4 were waited for; matrix products, arithmetic and copies ran while one was open for 12% of the time, Pallas kernels for 0%

commit v1 on v0

v1 whole, which is shorter than its diff:
```python
import jax
import jax.numpy as jnp
from jax import lax
from jax.sharding import PartitionSpec as P

MOST = 40
EXPERTS = 128
EMPTY = 64.0


def swap(value, axis, bit):
    count = lax.axis_size(axis)
    return lax.ppermute(value, axis, [(i, i ^ bit) for i in range(count)])


def exchange(pieces, axis):
    return [pieces[0]] + [swap(pieces[k], axis, k) for k in range(1, len(pieces))]


def local(inputs, grad_output, routes, gate_probs, gate_up, down_proj):
    experts = lax.axis_size("ex")
    me = lax.axis_index("ex")
    tokens, width = inputs.shape
    capacity = 5 * tokens * experts * routes.shape[1] // (4 * EXPERTS)
    order = me ^ jnp.arange(experts, dtype=jnp.int32)
    matches = routes[:, :, None] == order[None, None, :]
    routed = jnp.any(matches, axis=1)
    prob = jnp.sum(jnp.where(matches, gate_probs.astype(jnp.float32)[:, :, None], 0.0), axis=1)
    token = jnp.arange(tokens, dtype=jnp.int32)
    before = (token[:, None] > token[None, :]).astype(jnp.bfloat16)
    rank = jnp.dot(before, routed.astype(jnp.bfloat16), preferred_element_type=jnp.float32)
    rank = rank.astype(jnp.int32)
    picks = (rank[:, :, None] == jnp.arange(MOST, dtype=jnp.int32)) & routed[:, :, None]
    pick = picks.reshape(tokens, experts * MOST).astype(jnp.bfloat16)
    slot_prob = jnp.sum(jnp.where(picks, prob[:, :, None], 0.0), axis=0).reshape(-1)
    filled = jnp.any(picks, axis=0).reshape(-1)
    contract_rows = (((0,), (0,)), ((), ()))
    send_in = lax.dot_general(pick, inputs, contract_rows, preferred_element_type=jnp.float32)
    send_in = jnp.where(filled[:, None], send_in, EMPTY).astype(jnp.bfloat16)
    send_grad = lax.dot_general(pick, grad_output, contract_rows, preferred_element_type=jnp.float32)
    send_grad = (send_grad * slot_prob[:, None]).astype(jnp.bfloat16)
    got_in = exchange([send_in[k * MOST : (k + 1) * MOST] for k in range(experts)], "ex")
    got_grad = exchange([send_grad[k * MOST : (k + 1) * MOST] for k in range(experts)], "ex")
    got_in = jnp.concatenate(got_in, axis=0)
    got_grad = jnp.concatenate(got_grad, axis=0)

    row = jnp.arange(experts * MOST, dtype=jnp.int32)
    key = (me ^ (row // MOST)) * MOST + row % MOST
    full = got_in[:, :1] < EMPTY / 2
    earlier = (key[None, :] < key[:, None]).astype(jnp.bfloat16)
    slot = jnp.dot(earlier, full.astype(jnp.bfloat16), preferred_element_type=jnp.float32)
    place = (slot.astype(jnp.int32) == jnp.arange(capacity, dtype=jnp.int32)[None, :]) & full
    place = place.astype(jnp.bfloat16)
    rows_in = lax.dot_general(place, got_in, contract_rows, preferred_element_type=jnp.float32)
    rows_in = rows_in.astype(jnp.bfloat16)
    rows_grad = lax.dot_general(place, got_grad, contract_rows, preferred_element_type=jnp.float32)
    rows_grad = rows_grad.astype(jnp.bfloat16)

    gate_weight = gate_up[0, 0]
    up_weight = gate_up[0, 1]
    down_weight = down_proj[0]
    contract_width = (((1,), (1,)), ((), ()))

    def product(left, right):
        return lax.dot_general(left, right, contract_width, preferred_element_type=jnp.float32).astype(
            jnp.bfloat16
        )

    core = lax.axis_index("ey") & 1
    ways = lax.axis_size("ey")
    hidden = gate_weight.shape[0]
    half = hidden // 2

    def total(part):
        mine = lax.dynamic_slice_in_dim(part, core * half, half, 1)
        other = lax.dynamic_slice_in_dim(part, (1 - core) * half, half, 1)
        held = mine.astype(jnp.float32) + swap(other, "ey", 1).astype(jnp.float32)
        bit = 2
        while bit < ways:
            held = held + swap(held.astype(jnp.bfloat16), "ey", bit).astype(jnp.float32)
            bit *= 2
        return held

    gate_sum = total(product(rows_in, gate_weight))
    up_sum = total(product(rows_in, up_weight))
    grad_act = total(product(rows_grad, down_weight))
    sigmoid_gate = jax.nn.sigmoid(gate_sum)
    silu_gate = gate_sum * sigmoid_gate
    activation = (silu_gate * up_sum).astype(jnp.bfloat16)
    grad_gate = (
        grad_act * up_sum * sigmoid_gate * (1.0 + gate_sum * (1.0 - sigmoid_gate))
    ).astype(jnp.bfloat16)
    grad_up = (grad_act * silu_gate).astype(jnp.bfloat16)
    mine = jnp.stack([activation, grad_gate, grad_up])
    other = swap(mine, "ey", 1)
    low = jnp.where(core == 0, mine, other)
    high = jnp.where(core == 0, other, mine)
    whole = jnp.concatenate([low, high], axis=2)
    activation, grad_gate, grad_up = whole[0], whole[1], whole[2]

    grad_rows = jnp.dot(grad_gate, gate_weight, preferred_element_type=jnp.float32) + jnp.dot(
        grad_up, up_weight, preferred_element_type=jnp.float32
    )
    back = jnp.dot(place, grad_rows.astype(jnp.bfloat16), preferred_element_type=jnp.float32)
    back = back.astype(jnp.bfloat16)
    home = exchange([back[k * MOST : (k + 1) * MOST] for k in range(experts)], "ex")
    home = jnp.concatenate(home, axis=0)
    grad_inputs = jnp.dot(pick, home, preferred_element_type=jnp.float32).astype(jnp.bfloat16)

    def weight_grad(left, right):
        return lax.dot_general(left, right, contract_rows, preferred_element_type=jnp.float32).astype(
            jnp.bfloat16
        )

    down_grad = weight_grad(activation, rows_grad)
    pair_grad = jnp.stack([weight_grad(grad_gate, rows_in), weight_grad(grad_up, rows_in)])
    return (grad_inputs, pair_grad[None], down_grad[None])


def solution(mesh):
    return jax.shard_map(
        local,
        mesh=mesh,
        in_specs=(
            P(("groups", "ex"), "ey"),
            P(("groups", "ex"), "ey"),
            P(("groups", "ex"), None),
            P(("groups", "ex"), None),
            P("ex", None, None, "ey"),
            P("ex", None, "ey"),
        ),
        out_specs=(
            P(("groups", "ex"), "ey"),
            P("ex", "groups", None, "ey"),
            P("ex", "groups", "ey"),
        ),
        check_vma=False,
    )
```

time: 209 us -> 73.6 us (0.35)
  waiting for transfers between devices: 113 us -> 9.19 us
  blocking collectives: 35.4 us -> 0 us
  starting transfers between devices: 0.16 us -> 19.2 us
  between operations: 14.6 us -> 0.95 us
  local copies, waits for them, and re-layouts: 8.16 us -> 3.48 us
  matrix products: 25 us -> 29.6 us
    all_gather x2 -> x0, waiting for transfers between devices: 44.2 us -> none  [the longest x1 36.6 us: local(): piece_grad = lax.all_gather(grad_output, 'ex', axis=0, tiled=True)]
    reduce_scatter x1 -> x0, waiting for transfers between devices: 35.4 us -> none  [local(): lax.psum_scatter(take_slots(grad_rows, piece_slots, capacity).astype(jnp....]
    psum x1 -> x0, waiting for transfers between devices: 32.1 us -> none  [local(): lax.psum(up_part.astype(jnp.bfloat16), 'ey').astype(jnp.float32)]
    all_gather x2 -> x0, blocking collectives: 25.5 us -> none  [the longest x1 13.5 us: local(): all_slots = lax.all_gather(slot_table, 'ex', axis=0, tiled=True)]
    ppermute x0 -> x16, starting transfers between devices: none -> 19.2 us  [swap(): return lax.ppermute(value, axis, [(i, i ^ bit) for i in range(count)])]
    unnamed x1 -> x0, blocking collectives: 9.89 us -> none
    ppermute x0 -> x16, waiting for transfers between devices: none -> 9.19 us  [swap(): return lax.ppermute(value, axis, [(i, i ^ bit) for i in range(count)])]
    broadcast_in_dim x0 -> x1, other arithmetic: none -> 6.17 us  [local(): return (grad_inputs, pair_grad[None], down_grad[None])]
  transfers between devices with their start and end apart: 4 -> 16, of which waited for: 4 -> 5; matrix products, arithmetic and copies ran while one was open for 12% -> 27% of each run, Pallas kernels for 0% -> 0%
where the time goes in v1:
time: 73.6 us; the launch traced here: 73.1 us
  matrix products  29.6 us (40%)
  starting transfers between devices  19.2 us (26%)
  other arithmetic  10.7 us (15%)
  waiting for transfers between devices  9.19 us (12%)
  local copies, waits for them, and re-layouts  3.48 us (5%)
  between operations  0.95 us (1%)
    ppermute x16, starting transfers between devices, swap(): return lax.ppermute(value, axis, [(i, i ^ bit) for i in range(count)])  19.2 us
    dot_general x3, matrix products, weight_grad(): lax.dot_general(left, right, contract_rows, preferred_element_type=jnp.fl...  9.97 us
    ppermute x16, waiting for transfers between devices, swap(): return lax.ppermute(value, axis, [(i, i ^ bit) for i in range(count)])  9.19 us
    dot_general x3, matrix products, product(): lax.dot_general(left, right, contract_width, preferred_element_type=jnp.f...  7.1 us
    broadcast_in_dim x1, other arithmetic, local(): return (grad_inputs, pair_grad[None], down_grad[None])  6.17 us
    dot_general x1, matrix products, local(): jnp.dot(place, grad_rows.astype(jnp.bfloat16), preferred_element_type=jnp...  3.55 us
    dot_general x1, matrix products, local(): jnp.dot(grad_up, up_weight, preferred_element_type=jnp.float32)  3.3 us
  transfers between devices with their start and end apart: 16, of which 5 were waited for; matrix products, arithmetic and copies ran while one was open for 27% of the time, Pallas kernels for 0%

profile of v1, /device:TPU:0, one launch (start us, length us, event | category | flops | bytes accessed | tf_op | source)
XLA Modules:
  0.0 73.1 jit_solution(1167386890006530907)
XLA Ops:
  2.2 1.3 %fusion.26 = bf16[160,1024]{1,0:T(8,128)(2,1)S(1)} fusion(pred[256,160]{0,1:T(32,128)(4,1)S(1)} %fusion.70, bf16[256,1024]{1,0:T(8,128)(2,1)} %param.6, pred[160]{0:T(512)(128)(4,1)S(1)} %broadcast_in_dim.56), kind=kOutput, calls=%fused_computation.27 | convolution fusion | flops 84213760 | bytes 893088 | tf_op jit(solution)/shard_map/dot_general | solution.py:38
  4.2 3.0 %collective-permute-start = (bf16[40,1024]{1,0:T(8,128)(2,1)}, bf16[40,1024]{1,0:T(8,128)(2,1)S(1)}, u32[]{:S(2)}, u32[]{:S(2)}) collective-permute-start(bf16[40,1024]{1,0:T(8,128)(2,1)} %get-tuple-element.15), channel_id=1, source_target_pairs={{0,4},{4,0},{8,12},{12,8},{1,5},{5,1},{9,13},{13,9},{2,6},{6,2},{1... | collective-permute-start | bytes 245768 | tf_op jit(solution)/shard_map/ppermute | solution.py:13
  7.3 2.6 %collective-permute-start.1 = (bf16[40,1024]{1,0:T(8,128)(2,1)}, bf16[40,1024]{1,0:T(8,128)(2,1)S(1)}, u32[]{:S(2)}, u32[]{:S(2)}) collective-permute-start(bf16[40,1024]{1,0:T(8,128)(2,1)} %get-tuple-element.14), channel_id=1, source_target_pairs={{0,8},{4,12},{8,0},{12,4},{1,9},{5,13},{9,1},{13,5},{2,10},{6,14},... | collective-permute-start | bytes 245768 | tf_op jit(solution)/shard_map/ppermute | solution.py:13
  11.5 1.3 %fusion.27 = bf16[160,1024]{1,0:T(8,128)(2,1)S(1)} fusion(pred[256,160]{0,1:T(32,128)(4,1)S(1)} %fusion.70, bf16[256,1024]{1,0:T(8,128)(2,1)} %param.7, f32[160]{0:T(256)S(1)} %mul.58), kind=kOutput, calls=%fused_computation.28 | convolution fusion | flops 84213760 | bytes 893568 | tf_op jit(solution)/shard_map/dot_general | solution.py:40
  14.5 3.5 %collective-permute-start.8 = (bf16[40,1024]{1,0:T(8,128)(2,1)}, bf16[40,1024]{1,0:T(8,128)(2,1)}, u32[]{:S(2)}, u32[]{:S(2)}) collective-permute-start(bf16[40,1024]{1,0:T(8,128)(2,1)} %get-tuple-element.18), channel_id=1, source_target_pairs={{0,8},{4,12},{8,0},{12,4},{1,9},{5,13},{9,1},{13,5},{2,10},{6,14},... | collective-permute-start | bytes 245768 | tf_op jit(solution)/shard_map/ppermute | solution.py:13
  18.8 3.0 %fusion.17 = bf16[80,1536]{1,0:T(8,128)(2,1)S(1)} fusion(bf16[80,1024]{1,0:T(8,128)(2,1)S(1)} %convolution_convert_fusion.6, bf16[1,2,1536,1024]{3,2,1,0:T(8,128)(2,1)} %param.10), kind=kOutput, calls=%fused_computation.21 | convolution fusion | flops 251781120 | bytes 3555328 | tf_op jit(solution)/shard_map/dot_general | solution.py:65
  21.9 3.0 %fusion.20 = bf16[80,1536]{1,0:T(8,128)(2,1)S(1)} fusion(bf16[80,1024]{1,0:T(8,128)(2,1)S(1)} %convolution_convert_fusion.6, bf16[1,2,1536,1024]{3,2,1,0:T(8,128)(2,1)} %param.10), kind=kOutput, calls=%fused_computation.22 | convolution fusion | flops 251781120 | bytes 3555328 | tf_op jit(solution)/shard_map/dot_general | solution.py:65
  24.9 1.2 %convolution_convert_fusion.5 = bf16[80,1024]{1,0:T(8,128)(2,1)S(1)} fusion(bf16[40,1024]{1,0:T(8,128)(2,1)S(1)} %collective-permute-done.9, bf16[40,1024]{1,0:T(8,128)(2,1)} %collective-permute-done.8, bf16[40,1024]{1,0:T(8,128)(2,1)} %collective-permute-done.7, bf16[40,1024]{1,0:T(8,128)(2,1)S(1)} %copy-done.9, s32[160]{0:T(256)S(1)} %convert_element_type.102, ...), kind=kOutput, calls=%fused_computation.31 | convolution fusion | flops 27632640 | bytes 492320 | tf_op jit(solution)/shard_map/dot_general | solution.py:56
  26.2 1.1 %fusion.23 = bf16[80,1536]{1,0:T(8,128)(2,1)S(1)} fusion(bf16[80,1024]{1,0:T(8,128)(2,1)S(1)} %convolution_convert_fusion.5, bf16[1,1536,1024]{2,1,0:T(8,128)(2,1)S(1)} %copy-done), kind=kOutput, calls=%fused_computation.23 | convolution fusion | flops 251781120 | bytes 3555328 | tf_op jit(solution)/shard_map/dot_general | solution.py:65
  28.7 1.7 %collective-permute-start.11 = (bf16[80,768]{1,0:T(8,128)(2,1)S(1)}, bf16[80,768]{1,0:T(8,128)(2,1)S(1)}, u32[]{:S(2)}, u32[]{:S(2)}) collective-permute-start(bf16[80,768]{1,0:T(8,128)(2,1)S(1)} %fusion.67), channel_id=1, source_target_pairs={{0,2},{1,3},{2,0},{3,1},{4,6},{5,7},{6,4},{7,5},{8,10},{9,11},{10,... | collective-permute-start | bytes 368648 | tf_op jit(solution)/shard_map/ppermute | solution.py:13
  30.9 1.7 %collective-permute-start.6 = (bf16[80,768]{1,0:T(8,128)(2,1)S(1)}, bf16[80,768]{1,0:T(8,128)(2,1)S(1)}, u32[]{:S(2)}, u32[]{:S(2)}) collective-permute-start(bf16[80,768]{1,0:T(8,128)(2,1)S(1)} %fusion.66), channel_id=1, source_target_pairs={{0,2},{1,3},{2,0},{3,1},{4,6},{5,7},{6,4},{7,5},{8,10},{9,11},{10,... | collective-permute-start | bytes 368648 | tf_op jit(solution)/shard_map/ppermute | solution.py:13
  32.7 2.2 %collective-permute-done.11 = bf16[80,768]{1,0:T(8,128)(2,1)S(1)} collective-permute-done((bf16[80,768]{1,0:T(8,128)(2,1)S(1)}, bf16[80,768]{1,0:T(8,128)(2,1)S(1)}, u32[]{:S(2)}, u32[]{:S(2)}) %collective-permute-start.11) | collective-permute-done | bytes 122912 | tf_op jit(solution)/shard_map/ppermute | solution.py:13
  34.9 2.6 %collective-permute-done.4 = bf16[80,768]{1,0:T(8,128)(2,1)S(1)} collective-permute-done((bf16[80,768]{1,0:T(8,128)(2,1)S(1)}, bf16[80,768]{1,0:T(8,128)(2,1)S(1)}, u32[]{:S(2)}, u32[]{:S(2)}) %collective-permute-start.4) | collective-permute-done | bytes 122912 | tf_op jit(solution)/shard_map/ppermute | solution.py:13
  37.6 1.8 %collective-permute-done.6 = bf16[80,768]{1,0:T(8,128)(2,1)S(1)} collective-permute-done((bf16[80,768]{1,0:T(8,128)(2,1)S(1)}, bf16[80,768]{1,0:T(8,128)(2,1)S(1)}, u32[]{:S(2)}, u32[]{:S(2)}) %collective-permute-start.6) | collective-permute-done | bytes 122912 | tf_op jit(solution)/shard_map/ppermute | solution.py:13
  40.5 1.8 %collective-permute-done.12 = bf16[3,80,768]{2,1,0:T(8,128)(2,1)} collective-permute-done((bf16[3,80,768]{2,1,0:T(8,128)(2,1)S(1)}, bf16[3,80,768]{2,1,0:T(8,128)(2,1)}, u32[]{:S(2)}, u32[]{:S(2)}) %collective-permute-start.12) | collective-permute-done | bytes 368672 | tf_op jit(solution)/shard_map/ppermute | solution.py:13
  42.3 1.2 %broadcast_select_fusion = (bf16[3,80,768]{2,1,0:T(8,128)(2,1)S(1)}, bf16[3,80,768]{2,1,0:T(8,128)(2,1)S(1)}) fusion(bf16[3,80,768]{2,1,0:T(8,128)(2,1)} %collective-permute-done.12, pred[]{:T(512)S(6)} %eq.70, bf16[1,80,768]{2,1,0:T(8,128)(2,1)} %copy-done.5, bf16[1,80,768]{2,1,0:T(8,128)(2,1)} %copy-done.4, bf16[1,80,768]{2,1,0:T(8,128)(2,1)} %copy-done.3), kind=kLoop, calls=%fused_computation.40 | loop fusion | flops 737280 | bytes 1474561 | tf_op jit(solution)/shard_map/jit(_where)/select_n | solution.py:97
  43.5 3.7 %fusion = bf16[1,1536,1024]{2,1,0:T(8,128)(2,1)} fusion(bf16[80,1024]{1,0:T(8,128)(2,1)} %copy-done.8, bf16[3,80,768]{2,1,0:T(8,128)(2,1)S(1)} %get-tuple-element.7, bf16[3,80,768]{2,1,0:T(8,128)(2,1)S(1)} %get-tuple-element.6), kind=kOutput, calls=%fused_computation.4 | convolution fusion | flops 253722624 | bytes 4046848 | tf_op jit(solution)/shard_map/dot_general | solution.py:111
  47.2 3.6 %fusion.1 = bf16[1,1536,1024]{2,1,0:T(8,128)(2,1)} fusion(bf16[80,1024]{1,0:T(8,128)(2,1)} %copy-done.8, bf16[3,80,768]{2,1,0:T(8,128)(2,1)S(1)} %get-tuple-element.7, bf16[3,80,768]{2,1,0:T(8,128)(2,1)S(1)} %get-tuple-element.6), kind=kOutput, calls=%fused_computation.5 | convolution fusion | flops 253722624 | bytes 4046848 | tf_op jit(solution)/shard_map/dot_general | solution.py:111
  50.8 3.3 %fusion.5 = f32[80,1024]{1,0:T(8,128)} fusion(bf16[1,2,1536,1024]{3,2,1,0:T(8,128)(2,1)} %param.10, bf16[3,80,768]{2,1,0:T(8,128)(2,1)S(1)} %get-tuple-element.7, bf16[3,80,768]{2,1,0:T(8,128)(2,1)S(1)} %get-tuple-element.6), kind=kOutput, calls=%fused_computation.9 | convolution fusion | flops 252149760 | bytes 4210688 | tf_op jit(solution)/shard_map/dot_general | solution.py:101
  54.1 3.6 %convolution_convert_fusion.4 = bf16[160,1024]{1,0:T(8,128)(2,1)} fusion(f32[80,1024]{1,0:T(8,128)} %fusion.5, bf16[1,2,1536,1024]{3,2,1,0:T(8,128)(2,1)} %param.10, s32[160]{0:T(256)} %copy-done.10, pred[160]{0:T(512)(128)(4,1)} %copy-done.11, bf16[3,80,768]{2,1,0:T(8,128)(2,1)} %copy-done.1, bf16[3,80,768]{2,1,0:T(8,128)(2,1)S(1)} %get-tuple-element.6), kind=kOutput, calls=%fused_computation.29 | convolution fusion | flops 278717440 | bytes 4539904 | tf_op jit(solution)/shard_map/dot_general | solution.py:104
  59.3 3.8 %collective-permute-start.14 = (bf16[40,1024]{1,0:T(8,128)(2,1)S(1)}, bf16[40,1024]{1,0:T(8,128)(2,1)S(1)}, u32[]{:S(2)}, u32[]{:S(2)}) collective-permute-start(bf16[40,1024]{1,0:T(8,128)(2,1)S(1)} %get-tuple-element.10), channel_id=1, source_target_pairs={{0,8},{4,12},{8,0},{12,4},{1,9},{5,13},{9,1},{13,5},{2,10},{6,14},... | collective-permute-start | bytes 245768 | tf_op jit(solution)/shard_map/ppermute | solution.py:13
  63.1 6.2 %maximum_bitcast_fusion = bf16[1,2,1536,1024]{3,2,1,0:T(8,128)(2,1)} fusion(bf16[1,1536,1024]{2,1,0:T(8,128)(2,1)} %fusion.1, bf16[1,1536,1024]{2,1,0:T(8,128)(2,1)} %fusion), kind=kLoop, calls=%fused_computation | loop fusion | flops 3145728 | bytes 12582912 | tf_op jit(solution)/shard_map/broadcast_in_dim | solution.py:117
  69.3 2.7 %fusion.2 = bf16[1,1536,1024]{2,1,0:T(8,128)(2,1)} fusion(bf16[80,1024]{1,0:T(8,128)(2,1)S(1)} %copy-done.7, bf16[3,80,768]{2,1,0:T(8,128)(2,1)S(1)} %get-tuple-element.6, bf16[3,80,768]{2,1,0:T(8,128)(2,1)S(1)} %copy-done.2), kind=kOutput, calls=%fused_computation.6 | convolution fusion | flops 253722624 | bytes 4046848 | tf_op jit(solution)/shard_map/dot_general | solution.py:111
  72.0 1.1 %convolution_convert_fusion.3 = bf16[256,1024]{1,0:T(8,128)(2,1)} fusion(pred[256,160]{0,1:T(32,128)(4,1)S(1)} %fusion.70, bf16[40,1024]{1,0:T(8,128)(2,1)S(1)} %collective-permute-done.15, bf16[40,1024]{1,0:T(8,128)(2,1)S(1)} %collective-permute-done.14, bf16[40,1024]{1,0:T(8,128)(2,1)S(1)} %collective-permute-done.13, ...), kind=kOutput, calls=%fused_computation.24 | convolution fusion | flops 85458944 | bytes 892928 | tf_op jit(solution)/shard_map/dot_general | solution.py:108
  (75 shorter events, 11.0 us)
Async XLA Ops:
  0.6 25.5 %copy-start = (bf16[1,1536,1024]{2,1,0:T(8,128)(2,1)S(1)}, bf16[1,1536,1024]{2,1,0:T(8,128)(2,1)}, u32[]{:S(2)}) copy-start(bf16[1,1536,1024]{2,1,0:T(8,128)(2,1)} %param.11) | copy-start | bytes 9437188
  4.2 13.7 %collective-permute-start = (bf16[40,1024]{1,0:T(8,128)(2,1)}, bf16[40,1024]{1,0:T(8,128)(2,1)S(1)}, u32[]{:S(2)}, u32[]{:S(2)}) collective-permute-start(bf16[40,1024]{1,0:T(8,128)(2,1)} %get-tuple-element.15), channel_id=1, source_target_pairs={{0,4},{4,0},{8,12},{12,8},{1,5},{5,1},{9,13},{13,9},{2,6},{6,2},{1... | collective-permute-start | bytes 245768 | tf_op jit(solution)/shard_map/ppermute | solution.py:13
  7.3 10.8 %collective-permute-start.1 = (bf16[40,1024]{1,0:T(8,128)(2,1)}, bf16[40,1024]{1,0:T(8,128)(2,1)S(1)}, u32[]{:S(2)}, u32[]{:S(2)}) collective-permute-start(bf16[40,1024]{1,0:T(8,128)(2,1)} %get-tuple-element.14), channel_id=1, source_target_pairs={{0,8},{4,12},{8,0},{12,4},{1,9},{5,13},{9,1},{13,5},{2,10},{6,14},... | collective-permute-start | bytes 245768 | tf_op jit(solution)/shard_map/ppermute | solution.py:13
  9.8 8.2 %collective-permute-start.2 = (bf16[40,1024]{1,0:T(8,128)(2,1)}, bf16[40,1024]{1,0:T(8,128)(2,1)S(1)}, u32[]{:S(2)}, u32[]{:S(2)}) collective-permute-start(bf16[40,1024]{1,0:T(8,128)(2,1)} %get-tuple-element.13), channel_id=1, source_target_pairs={{0,12},{4,8},{8,4},{12,0},{1,13},{5,9},{9,5},{13,1},{2,14},{6,10},... | collective-permute-start | bytes 245768 | tf_op jit(solution)/shard_map/ppermute | solution.py:13
  13.6 11.3 %collective-permute-start.7 = (bf16[40,1024]{1,0:T(8,128)(2,1)}, bf16[40,1024]{1,0:T(8,128)(2,1)}, u32[]{:S(2)}, u32[]{:S(2)}) collective-permute-start(bf16[40,1024]{1,0:T(8,128)(2,1)} %get-tuple-element.19), channel_id=1, source_target_pairs={{0,4},{4,0},{8,12},{12,8},{1,5},{5,1},{9,13},{13,9},{2,6},{6,2},{1... | collective-permute-start | bytes 245768 | tf_op jit(solution)/shard_map/ppermute | solution.py:13
  14.5 10.4 %collective-permute-start.8 = (bf16[40,1024]{1,0:T(8,128)(2,1)}, bf16[40,1024]{1,0:T(8,128)(2,1)}, u32[]{:S(2)}, u32[]{:S(2)}) collective-permute-start(bf16[40,1024]{1,0:T(8,128)(2,1)} %get-tuple-element.18), channel_id=1, source_target_pairs={{0,8},{4,12},{8,0},{12,4},{1,9},{5,13},{9,1},{13,5},{2,10},{6,14},... | collective-permute-start | bytes 245768 | tf_op jit(solution)/shard_map/ppermute | solution.py:13
  18.0 6.9 %collective-permute-start.9 = (bf16[40,1024]{1,0:T(8,128)(2,1)}, bf16[40,1024]{1,0:T(8,128)(2,1)S(1)}, u32[]{:S(2)}, u32[]{:S(2)}) collective-permute-start(bf16[40,1024]{1,0:T(8,128)(2,1)} %get-tuple-element.17), channel_id=1, source_target_pairs={{0,12},{4,8},{8,4},{12,0},{1,13},{5,9},{9,5},{13,1},{2,14},{6,10},... | collective-permute-start | bytes 245768 | tf_op jit(solution)/shard_map/ppermute | solution.py:13
  18.2 6.7 %copy-start.11 = (pred[160]{0:T(512)(128)(4,1)}, pred[160]{0:T(512)(128)(4,1)S(1)}, u32[]{:S(2)}) copy-start(pred[160]{0:T(512)(128)(4,1)S(1)} %compare_reduce_fusion) | copy-start | bytes 484
  18.4 6.4 %copy-start.10 = (s32[160]{0:T(256)}, s32[160]{0:T(256)S(1)}, u32[]{:S(2)}) copy-start(s32[160]{0:T(256)S(1)} %convert_element_type.102) | copy-start | bytes 1924
  18.8 6.1 %copy-start.9 = (bf16[40,1024]{1,0:T(8,128)(2,1)S(1)}, bf16[40,1024]{1,0:T(8,128)(2,1)}, u32[]{:S(2)}) copy-start(bf16[40,1024]{1,0:T(8,128)(2,1)} %get-tuple-element.16) | copy-start | bytes 245764
  26.2 13.5 %copy-start.6 = (bf16[80,1024]{1,0:T(8,128)(2,1)}, bf16[80,1024]{1,0:T(8,128)(2,1)S(1)}, u32[]{:S(2)}) copy-start(bf16[80,1024]{1,0:T(8,128)(2,1)S(1)} %convolution_convert_fusion.5) | copy-start | bytes 491524
  27.3 1.4 %collective-permute-start.10 = (bf16[80,768]{1,0:T(8,128)(2,1)S(1)}, bf16[80,768]{1,0:T(8,128)(2,1)S(1)}, u32[]{:S(2)}, u32[]{:S(2)}) collective-permute-start(bf16[80,768]{1,0:T(8,128)(2,1)S(1)} %constant_dynamic-slice_fusion), channel_id=1, source_target_pairs={{0,1},{1,0},{2,3},{3,2},{4,5},{5,4},{6,7},{7,6},{8,9},{9,8},{10,11... | collective-permute-start | bytes 368648 | tf_op jit(solution)/shard_map/ppermute | solution.py:13
  27.4 3.1 %collective-permute-start.3 = (bf16[80,768]{1,0:T(8,128)(2,1)S(1)}, bf16[80,768]{1,0:T(8,128)(2,1)S(1)}, u32[]{:S(2)}, u32[]{:S(2)}) collective-permute-start(bf16[80,768]{1,0:T(8,128)(2,1)S(1)} %constant_dynamic-slice_fusion.2), channel_id=1, source_target_pairs={{0,1},{1,0},{2,3},{3,2},{4,5},{5,4},{6,7},{7,6},{8,9},{9,8},{10,11... | collective-permute-start | bytes 368648 | tf_op jit(solution)/shard_map/ppermute | solution.py:13
  27.9 3.0 %collective-permute-start.5 = (bf16[80,768]{1,0:T(8,128)(2,1)S(1)}, bf16[80,768]{1,0:T(8,128)(2,1)S(1)}, u32[]{:S(2)}, u32[]{:S(2)}) collective-permute-start(bf16[80,768]{1,0:T(8,128)(2,1)S(1)} %constant_dynamic-slice_fusion.1), channel_id=1, source_target_pairs={{0,1},{1,0},{2,3},{3,2},{4,5},{5,4},{6,7},{7,6},{8,9},{9,8},{10,11... | collective-permute-start | bytes 368648 | tf_op jit(solution)/shard_map/ppermute | solution.py:13
  28.7 6.2 %collective-permute-start.11 = (bf16[80,768]{1,0:T(8,128)(2,1)S(1)}, bf16[80,768]{1,0:T(8,128)(2,1)S(1)}, u32[]{:S(2)}, u32[]{:S(2)}) collective-permute-start(bf16[80,768]{1,0:T(8,128)(2,1)S(1)} %fusion.67), channel_id=1, source_target_pairs={{0,2},{1,3},{2,0},{3,1},{4,6},{5,7},{6,4},{7,5},{8,10},{9,11},{10,... | collective-permute-start | bytes 368648 | tf_op jit(solution)/shard_map/ppermute | solution.py:13
  30.5 7.1 %collective-permute-start.4 = (bf16[80,768]{1,0:T(8,128)(2,1)S(1)}, bf16[80,768]{1,0:T(8,128)(2,1)S(1)}, u32[]{:S(2)}, u32[]{:S(2)}) collective-permute-start(bf16[80,768]{1,0:T(8,128)(2,1)S(1)} %fusion.65), channel_id=1, source_target_pairs={{0,2},{1,3},{2,0},{3,1},{4,6},{5,7},{6,4},{7,5},{8,10},{9,11},{10,... | collective-permute-start | bytes 368648 | tf_op jit(solution)/shard_map/ppermute | solution.py:13
  30.9 8.5 %collective-permute-start.6 = (bf16[80,768]{1,0:T(8,128)(2,1)S(1)}, bf16[80,768]{1,0:T(8,128)(2,1)S(1)}, u32[]{:S(2)}, u32[]{:S(2)}) collective-permute-start(bf16[80,768]{1,0:T(8,128)(2,1)S(1)} %fusion.66), channel_id=1, source_target_pairs={{0,2},{1,3},{2,0},{3,1},{4,6},{5,7},{6,4},{7,5},{8,10},{9,11},{10,... | collective-permute-start | bytes 368648 | tf_op jit(solution)/shard_map/ppermute | solution.py:13
  40.4 1.9 %collective-permute-start.12 = (bf16[3,80,768]{2,1,0:T(8,128)(2,1)S(1)}, bf16[3,80,768]{2,1,0:T(8,128)(2,1)}, u32[]{:S(2)}, u32[]{:S(2)}) collective-permute-start(bf16[3,80,768]{2,1,0:T(8,128)(2,1)S(1)} %pad_maximum_fusion), channel_id=1, source_target_pairs={{0,1},{1,0},{2,3},{3,2},{4,5},{5,4},{6,7},{7,6},{8,9},{9,8},{10,11... | collective-permute-start | bytes 1105928 | tf_op jit(solution)/shard_map/ppermute | solution.py:13
  43.5 7.3 %copy-start.1 = (bf16[3,80,768]{2,1,0:T(8,128)(2,1)}, bf16[3,80,768]{2,1,0:T(8,128)(2,1)S(1)}, u32[]{:S(2)}) copy-start(bf16[3,80,768]{2,1,0:T(8,128)(2,1)S(1)} %get-tuple-element.7) | copy-start | bytes 1105924
  58.7 13.3 %collective-permute-start.13 = (bf16[40,1024]{1,0:T(8,128)(2,1)S(1)}, bf16[40,1024]{1,0:T(8,128)(2,1)S(1)}, u32[]{:S(2)}, u32[]{:S(2)}) collective-permute-start(bf16[40,1024]{1,0:T(8,128)(2,1)S(1)} %get-tuple-element.11), channel_id=1, source_target_pairs={{0,4},{4,0},{8,12},{12,8},{1,5},{5,1},{9,13},{13,9},{2,6},{6,2},{1... | collective-permute-start | bytes 245768 | tf_op jit(solution)/shard_map/ppermute | solution.py:13
  59.3 12.7 %collective-permute-start.14 = (bf16[40,1024]{1,0:T(8,128)(2,1)S(1)}, bf16[40,1024]{1,0:T(8,128)(2,1)S(1)}, u32[]{:S(2)}, u32[]{:S(2)}) collective-permute-start(bf16[40,1024]{1,0:T(8,128)(2,1)S(1)} %get-tuple-element.10), channel_id=1, source_target_pairs={{0,8},{4,12},{8,0},{12,4},{1,9},{5,13},{9,1},{13,5},{2,10},{6,14},... | collective-permute-start | bytes 245768 | tf_op jit(solution)/shard_map/ppermute | solution.py:13
  63.1 6.2 %copy-start.2 = (bf16[3,80,768]{2,1,0:T(8,128)(2,1)S(1)}, bf16[3,80,768]{2,1,0:T(8,128)(2,1)}, u32[]{:S(2)}) copy-start(bf16[3,80,768]{2,1,0:T(8,128)(2,1)} %copy-done.1) | copy-start | bytes 1105924
  63.1 6.2 %copy-start.7 = (bf16[80,1024]{1,0:T(8,128)(2,1)S(1)}, bf16[80,1024]{1,0:T(8,128)(2,1)}, u32[]{:S(2)}) copy-start(bf16[80,1024]{1,0:T(8,128)(2,1)} %copy-done.6) | copy-start | bytes 491524
  63.1 8.9 %collective-permute-start.15 = (bf16[40,1024]{1,0:T(8,128)(2,1)S(1)}, bf16[40,1024]{1,0:T(8,128)(2,1)S(1)}, u32[]{:S(2)}, u32[]{:S(2)}) collective-permute-start(bf16[40,1024]{1,0:T(8,128)(2,1)S(1)} %get-tuple-element.9), channel_id=1, source_target_pairs={{0,12},{4,8},{8,4},{12,0},{1,13},{5,9},{9,5},{13,1},{2,14},{6,10},... | collective-permute-start | bytes 245768 | tf_op jit(solution)/shard_map/ppermute | solution.py:13
  (4 other events, 8.1 us)

commit v2 on v1

--- a/solution.py
+++ b/solution.py
@@ -13,16 +13,16 @@
     return lax.ppermute(value, axis, [(i, i ^ bit) for i in range(count)])
 
 
-def exchange(pieces, axis):
-    return [pieces[0]] + [swap(pieces[k], axis, k) for k in range(1, len(pieces))]
+def exchange(value, axis):
+    pieces = value.reshape(lax.axis_size(axis), MOST, value.shape[1])
+    return lax.all_to_all(pieces, axis, 0, 0, tiled=True).reshape(value.shape)
 
 
 def local(inputs, grad_output, routes, gate_probs, gate_up, down_proj):
     experts = lax.axis_size("ex")
-    me = lax.axis_index("ex")
     tokens, width = inputs.shape
     capacity = 5 * tokens * experts * routes.shape[1] // (4 * EXPERTS)
-    order = me ^ jnp.arange(experts, dtype=jnp.int32)
+    order = jnp.arange(experts, dtype=jnp.int32)
     matches = routes[:, :, None] == order[None, None, :]
     routed = jnp.any(matches, axis=1)
     prob = jnp.sum(jnp.where(matches, gate_probs.astype(jnp.float32)[:, :, None], 0.0), axis=1)
@@ -39,15 +39,12 @@
     send_in = jnp.where(filled[:, None], send_in, EMPTY).astype(jnp.bfloat16)
     send_grad = lax.dot_general(pick, grad_output, contract_rows, preferred_element_type=jnp.float32)
     send_grad = (send_grad * slot_prob[:, None]).astype(jnp.bfloat16)
-    got_in = exchange([send_in[k * MOST : (k + 1) * MOST] for k in range(experts)], "ex")
-    got_grad = exchange([send_grad[k * MOST : (k + 1) * MOST] for k in range(experts)], "ex")
-    got_in = jnp.concatenate(got_in, axis=0)
-    got_grad = jnp.concatenate(got_grad, axis=0)
+    got_in = exchange(send_in, "ex")
+    got_grad = exchange(send_grad, "ex")
 
     row = jnp.arange(experts * MOST, dtype=jnp.int32)
-    key = (me ^ (row // MOST)) * MOST + row % MOST
     full = got_in[:, :1] < EMPTY / 2
-    earlier = (key[None, :] < key[:, None]).astype(jnp.bfloat16)
+    earlier = (row[None, :] < row[:, None]).astype(jnp.bfloat16)
     slot = jnp.dot(earlier, full.astype(jnp.bfloat16), preferred_element_type=jnp.float32)
     place = (slot.astype(jnp.int32) == jnp.arange(capacity, dtype=jnp.int32)[None, :]) & full
     place = place.astype(jnp.bfloat16)
@@ -103,8 +100,7 @@
     )
     back = jnp.dot(place, grad_rows.astype(jnp.bfloat16), preferred_element_type=jnp.float32)
     back = back.astype(jnp.bfloat16)
-    home = exchange([back[k * MOST : (k + 1) * MOST] for k in range(experts)], "ex")
-    home = jnp.concatenate(home, axis=0)
+    home = exchange(back, "ex")
     grad_inputs = jnp.dot(pick, home, preferred_element_type=jnp.float32).astype(jnp.bfloat16)
 
     def weight_grad(left, right):

time: 73.6 us -> 84.3 us (1.15)
  waiting for transfers between devices: 9.19 us -> 19.3 us
  matrix products: 29.6 us -> 33.8 us
  local copies, waits for them, and re-layouts: 3.48 us -> 1.02 us
  other arithmetic: 10.7 us -> 9.54 us
    ppermute x16 -> x7, starting transfers between devices: 19.2 us -> 4.49 us  [swap(): return lax.ppermute(value, axis, [(i, i ^ bit) for i in range(count)])]
    all_to_all x0 -> x3, starting transfers between devices: none -> 14.5 us  [exchange(): return lax.all_to_all(pieces, axis, 0, 0, tiled=True).reshape(value.shape)]
    all_to_all x0 -> x3, waiting for transfers between devices: none -> 9.98 us  [exchange(): return lax.all_to_all(pieces, axis, 0, 0, tiled=True).reshape(value.shape)]
    slice x3 -> x0, local copies, waits for them, and re-layouts: 2.46 us -> none  [the longest x1 1.03 us: local(): back[k * MOST:(k + 1) * MOST]]
    dot_general x3, matrix products: 9.97 us -> 11.1 us  [weight_grad(): lax.dot_general(left, right, contract_rows, preferred_element_type=jnp.fl...]
    broadcast_in_dim x1, other arithmetic: 6.17 us -> 5.17 us  [local(): return (grad_inputs, pair_grad[None], down_grad[None])]
    dot_general x1, matrix products: 1.15 us -> 2.12 us  [local(): jnp.dot(pick, home, preferred_element_type=jnp.float32).astype(jnp.bfloat16)]
    ppermute x16 -> x7, waiting for transfers between devices: 9.19 us -> 9.35 us  [swap(): return lax.ppermute(value, axis, [(i, i ^ bit) for i in range(count)])]
  transfers between devices with their start and end apart: 16 -> 10, of which waited for: 5 -> 8; matrix products, arithmetic and copies ran while one was open for 27% -> 24% of each run, Pallas kernels for 0% -> 0%
where the time goes in v2:
time: 84.3 us; the launch traced here: 83.5 us
  matrix products  33.8 us (40%)
  waiting for transfers between devices  19.3 us (23%)
  starting transfers between devices  19 us (23%)
  other arithmetic  9.54 us (11%)
  local copies, waits for them, and re-layouts  1.02 us (1%)
    all_to_all x3, starting transfers between devices, exchange(): return lax.all_to_all(pieces, axis, 0, 0, tiled=True).reshape(value.shape)  14.5 us
    dot_general x3, matrix products, weight_grad(): lax.dot_general(left, right, contract_rows, preferred_element_type=jnp.fl...  11.1 us
    all_to_all x3, waiting for transfers between devices, exchange(): return lax.all_to_all(pieces, axis, 0, 0, tiled=True).reshape(value.shape)  9.98 us
    ppermute x7, waiting for transfers between devices, swap(): return lax.ppermute(value, axis, [(i, i ^ bit) for i in range(count)])  9.35 us
    dot_general x3, matrix products, product(): lax.dot_general(left, right, contract_width, preferred_element_type=jnp.f...  7.77 us
    broadcast_in_dim x1, other arithmetic, local(): return (grad_inputs, pair_grad[None], down_grad[None])  5.17 us
    ppermute x7, starting transfers between devices, swap(): return lax.ppermute(value, axis, [(i, i ^ bit) for i in range(count)])  4.49 us
    dot_general x1, matrix products, local(): jnp.dot(place, grad_rows.astype(jnp.bfloat16), preferred_element_type=jnp...  3.52 us
  transfers between devices with their start and end apart: 10, of which 8 were waited for; matrix products, arithmetic and copies ran while one was open for 24% of the time, Pallas kernels for 0%

profile of v2, /device:TPU:0, one launch (start us, length us, event | category | flops | bytes accessed | tf_op | source)
XLA Modules:
  0.0 83.5 jit_solution(12557990426755512883)
XLA Ops:
  2.1 2.0 %fusion.27 = bf16[160,1024]{1,0:T(8,128)(2,1)} fusion(pred[256,160]{0,1:T(32,128)(4,1)S(1)} %fusion.51, bf16[256,1024]{1,0:T(8,128)(2,1)} %param.6, pred[160]{0:T(512)(128)(4,1)S(1)} %broadcast_in_dim.56), kind=kOutput, calls=%fused_computation.28 | convolution fusion | flops 84213760 | bytes 893088 | tf_op jit(solution)/shard_map/dot_general | solution.py:38
  4.2 6.3 %all-to-all-start = ((bf16[4,40,1024]{2,1,0:T(8,128)(2,1)}), bf16[4,40,1024]{2,1,0:T(8,128)(2,1)S(1)}, u32[]{:S(2)}, u32[]{:S(2)}) async-start(bf16[4,40,1024]{2,1,0:T(8,128)(2,1)} %bitcast.84), calls=%async_computation | async-start | bytes 655360 | tf_op jit(solution)/shard_map/all_to_all | solution.py:18
  12.1 2.0 %fusion.28 = bf16[160,1024]{1,0:T(8,128)(2,1)} fusion(pred[256,160]{0,1:T(32,128)(4,1)S(1)} %fusion.51, bf16[256,1024]{1,0:T(8,128)(2,1)} %param.7, f32[160]{0:T(256)S(1)} %mul.45), kind=kOutput, calls=%fused_computation.29 | convolution fusion | flops 84213760 | bytes 893568 | tf_op jit(solution)/shard_map/dot_general | solution.py:40
  14.1 6.7 %all-to-all-done = bf16[4,40,1024]{2,1,0:T(8,128)(2,1)S(1)} async-done(((bf16[4,40,1024]{2,1,0:T(8,128)(2,1)}), bf16[4,40,1024]{2,1,0:T(8,128)(2,1)S(1)}, u32[]{:S(2)}, u32[]{:S(2)}) %all-to-all-start) | async-done | bytes 327712 | tf_op jit(solution)/shard_map/all_to_all | solution.py:18
  20.8 4.1 %all-to-all-start.1 = ((bf16[4,40,1024]{2,1,0:T(8,128)(2,1)}), bf16[4,40,1024]{2,1,0:T(8,128)(2,1)}, u32[]{:S(2)}, u32[]{:S(2)}) async-start(bf16[4,40,1024]{2,1,0:T(8,128)(2,1)} %bitcast.85), calls=%async_computation.1 | async-start | bytes 655360 | tf_op jit(solution)/shard_map/all_to_all | solution.py:18
  25.5 3.0 %fusion.17 = bf16[80,1536]{1,0:T(8,128)(2,1)S(1)} fusion(bf16[80,1024]{1,0:T(8,128)(2,1)S(1)} %convolution_convert_fusion.5, bf16[1,2,1536,1024]{3,2,1,0:T(8,128)(2,1)} %param.10), kind=kOutput, calls=%fused_computation.21 | convolution fusion | flops 251781120 | bytes 3555328 | tf_op jit(solution)/shard_map/dot_general | solution.py:62
  28.6 3.7 %fusion.20 = bf16[80,1536]{1,0:T(8,128)(2,1)} fusion(bf16[80,1024]{1,0:T(8,128)(2,1)S(1)} %convolution_convert_fusion.5, bf16[1,2,1536,1024]{3,2,1,0:T(8,128)(2,1)} %param.10), kind=kOutput, calls=%fused_computation.22 | convolution fusion | flops 251781120 | bytes 3555328 | tf_op jit(solution)/shard_map/dot_general | solution.py:62
  32.3 1.4 %all-to-all-done.1 = bf16[4,40,1024]{2,1,0:T(8,128)(2,1)} async-done(((bf16[4,40,1024]{2,1,0:T(8,128)(2,1)}), bf16[4,40,1024]{2,1,0:T(8,128)(2,1)}, u32[]{:S(2)}, u32[]{:S(2)}) %all-to-all-start.1) | async-done | bytes 327712 | tf_op jit(solution)/shard_map/all_to_all | solution.py:18
  33.6 1.3 %convolution_convert_fusion.4 = bf16[80,1024]{1,0:T(8,128)(2,1)S(1)} fusion(bf16[160,1024]{1,0:T(8,128)(2,1)} %bitcast.9, s32[160]{0:T(256)S(1)} %convert_element_type.102, pred[160]{0:T(512)(128)(4,1)S(1)} %compare_reduce_fusion), kind=kOutput, calls=%fused_computation.32 | convolution fusion | flops 26321920 | bytes 492320 | tf_op jit(solution)/shard_map/dot_general | solution.py:53
  37.5 1.6 %collective-permute-start.5 = (bf16[80,768]{1,0:T(8,128)(2,1)S(1)}, bf16[80,768]{1,0:T(8,128)(2,1)S(1)}, u32[]{:S(2)}, u32[]{:S(2)}) collective-permute-start(bf16[80,768]{1,0:T(8,128)(2,1)S(1)} %fusion.47), channel_id=1, source_target_pairs={{0,2},{1,3},{2,0},{3,1},{4,6},{5,7},{6,4},{7,5},{8,10},{9,11},{10,... | collective-permute-start | bytes 368648 | tf_op jit(solution)/shard_map/ppermute | solution.py:13
  39.7 1.6 %collective-permute-start.3 = (bf16[80,768]{1,0:T(8,128)(2,1)S(1)}, bf16[80,768]{1,0:T(8,128)(2,1)S(1)}, u32[]{:S(2)}, u32[]{:S(2)}) collective-permute-start(bf16[80,768]{1,0:T(8,128)(2,1)S(1)} %fusion.46), channel_id=1, source_target_pairs={{0,2},{1,3},{2,0},{3,1},{4,6},{5,7},{6,4},{7,5},{8,10},{9,11},{10,... | collective-permute-start | bytes 368648 | tf_op jit(solution)/shard_map/ppermute | solution.py:13
  41.3 2.4 %collective-permute-done.5 = bf16[80,768]{1,0:T(8,128)(2,1)S(1)} collective-permute-done((bf16[80,768]{1,0:T(8,128)(2,1)S(1)}, bf16[80,768]{1,0:T(8,128)(2,1)S(1)}, u32[]{:S(2)}, u32[]{:S(2)}) %collective-permute-start.5) | collective-permute-done | bytes 122912 | tf_op jit(solution)/shard_map/ppermute | solution.py:13
  43.7 2.6 %collective-permute-done.1 = bf16[80,768]{1,0:T(8,128)(2,1)S(1)} collective-permute-done((bf16[80,768]{1,0:T(8,128)(2,1)S(1)}, bf16[80,768]{1,0:T(8,128)(2,1)S(1)}, u32[]{:S(2)}, u32[]{:S(2)}) %collective-permute-start.1) | collective-permute-done | bytes 122912 | tf_op jit(solution)/shard_map/ppermute | solution.py:13
  46.4 1.8 %collective-permute-done.3 = bf16[80,768]{1,0:T(8,128)(2,1)S(1)} collective-permute-done((bf16[80,768]{1,0:T(8,128)(2,1)S(1)}, bf16[80,768]{1,0:T(8,128)(2,1)S(1)}, u32[]{:S(2)}, u32[]{:S(2)}) %collective-permute-start.3) | collective-permute-done | bytes 122912 | tf_op jit(solution)/shard_map/ppermute | solution.py:13
  49.3 1.8 %collective-permute-done.6 = bf16[3,80,768]{2,1,0:T(8,128)(2,1)} collective-permute-done((bf16[3,80,768]{2,1,0:T(8,128)(2,1)S(1)}, bf16[3,80,768]{2,1,0:T(8,128)(2,1)}, u32[]{:S(2)}, u32[]{:S(2)}) %collective-permute-start.6) | collective-permute-done | bytes 368672 | tf_op jit(solution)/shard_map/ppermute | solution.py:13
  52.3 3.7 %fusion = bf16[1,1536,1024]{2,1,0:T(8,128)(2,1)} fusion(bf16[80,1024]{1,0:T(8,128)(2,1)} %copy-done.4, bf16[3,80,768]{2,1,0:T(8,128)(2,1)S(1)} %get-tuple-element.7, bf16[3,80,768]{2,1,0:T(8,128)(2,1)S(1)} %get-tuple-element.6), kind=kOutput, calls=%fused_computation.4 | convolution fusion | flops 253722624 | bytes 4046848 | tf_op jit(solution)/shard_map/dot_general | solution.py:107
  56.0 3.6 %fusion.1 = bf16[1,1536,1024]{2,1,0:T(8,128)(2,1)} fusion(bf16[80,1024]{1,0:T(8,128)(2,1)} %copy-done.4, bf16[3,80,768]{2,1,0:T(8,128)(2,1)S(1)} %get-tuple-element.7, bf16[3,80,768]{2,1,0:T(8,128)(2,1)S(1)} %get-tuple-element.6), kind=kOutput, calls=%fused_computation.5 | convolution fusion | flops 253722624 | bytes 4046848 | tf_op jit(solution)/shard_map/dot_general | solution.py:107
  59.6 3.3 %fusion.5 = f32[80,1024]{1,0:T(8,128)} fusion(bf16[1,2,1536,1024]{3,2,1,0:T(8,128)(2,1)} %param.10, bf16[3,80,768]{2,1,0:T(8,128)(2,1)S(1)} %get-tuple-element.7, bf16[3,80,768]{2,1,0:T(8,128)(2,1)S(1)} %get-tuple-element.6), kind=kOutput, calls=%fused_computation.9 | convolution fusion | flops 252149760 | bytes 4210688 | tf_op jit(solution)/shard_map/dot_general | solution.py:98
  62.9 3.5 %convolution_convert_fusion.3 = bf16[160,1024]{1,0:T(8,128)(2,1)} fusion(f32[80,1024]{1,0:T(8,128)} %fusion.5, bf16[1,2,1536,1024]{3,2,1,0:T(8,128)(2,1)} %param.10, s32[160]{0:T(256)S(1)} %convert_element_type.102, pred[160]{0:T(512)(128)(4,1)S(1)} %compare_reduce_fusion, bf16[3,80,768]{2,1,0:T(8,128)(2,1)} %copy-done.2, ...), kind=kOutput, calls=%fused_computation.30 | convolution fusion | flops 278717440 | bytes 4539168 | tf_op jit(solution)/shard_map/dot_general | solution.py:101
  66.4 4.1 %all-to-all-start.2 = ((bf16[4,40,1024]{2,1,0:T(8,128)(2,1)}), bf16[4,40,1024]{2,1,0:T(8,128)(2,1)}, u32[]{:S(2)}, u32[]{:S(2)}) async-start(bf16[4,40,1024]{2,1,0:T(8,128)(2,1)} %bitcast.86), calls=%async_computation.2 | async-start | bytes 655360 | tf_op jit(solution)/shard_map/all_to_all | solution.py:18
  70.5 3.8 %fusion.2 = bf16[1,1536,1024]{2,1,0:T(8,128)(2,1)} fusion(bf16[80,1024]{1,0:T(8,128)(2,1)} %copy-done.3, bf16[3,80,768]{2,1,0:T(8,128)(2,1)S(1)} %get-tuple-element.6, bf16[3,80,768]{2,1,0:T(8,128)(2,1)} %copy-done.2), kind=kOutput, calls=%fused_computation.6 | convolution fusion | flops 253722624 | bytes 4046848 | tf_op jit(solution)/shard_map/dot_general | solution.py:107
  74.3 5.2 %maximum_bitcast_fusion = bf16[1,2,1536,1024]{3,2,1,0:T(8,128)(2,1)} fusion(bf16[1,1536,1024]{2,1,0:T(8,128)(2,1)} %fusion.1, bf16[1,1536,1024]{2,1,0:T(8,128)(2,1)S(1)} %copy-done.1), kind=kLoop, calls=%fused_computation | loop fusion | flops 3145728 | bytes 12582912 | tf_op jit(solution)/shard_map/broadcast_in_dim | solution.py:113
  79.5 1.9 %all-to-all-done.2 = bf16[4,40,1024]{2,1,0:T(8,128)(2,1)} async-done(((bf16[4,40,1024]{2,1,0:T(8,128)(2,1)}), bf16[4,40,1024]{2,1,0:T(8,128)(2,1)}, u32[]{:S(2)}, u32[]{:S(2)}) %all-to-all-start.2) | async-done | bytes 327712 | tf_op jit(solution)/shard_map/all_to_all | solution.py:18
  81.4 2.1 %fusion.26 = bf16[256,1024]{1,0:T(8,128)(2,1)} fusion(bf16[4,40,1024]{2,1,0:T(8,128)(2,1)} %all-to-all-done.2, s32[256,4]{0,1:T(4,128)S(1)} %convolution_convert_fusion.6, pred[256,4]{0,1:T(4,128)(4,1)S(1)} %fusion.68), kind=kOutput, calls=%fused_computation.25 | convolution fusion | flops 84230144 | bytes 857088 | tf_op jit(solution)/shard_map/dot_general | solution.py:104
  (52 shorter events, 9.1 us)
Async XLA Ops:
  0.6 34.3 %copy-start = (bf16[1,1536,1024]{2,1,0:T(8,128)(2,1)S(1)}, bf16[1,1536,1024]{2,1,0:T(8,128)(2,1)}, u32[]{:S(2)}) copy-start(bf16[1,1536,1024]{2,1,0:T(8,128)(2,1)} %param.11) | copy-start | bytes 9437188
  4.2 16.6 %all-to-all-start = ((bf16[4,40,1024]{2,1,0:T(8,128)(2,1)}), bf16[4,40,1024]{2,1,0:T(8,128)(2,1)S(1)}, u32[]{:S(2)}, u32[]{:S(2)}) async-start(bf16[4,40,1024]{2,1,0:T(8,128)(2,1)} %bitcast.84), calls=%async_computation | async-start | bytes 655360 | tf_op jit(solution)/shard_map/all_to_all | solution.py:18
  20.8 12.8 %all-to-all-start.1 = ((bf16[4,40,1024]{2,1,0:T(8,128)(2,1)}), bf16[4,40,1024]{2,1,0:T(8,128)(2,1)}, u32[]{:S(2)}, u32[]{:S(2)}) async-start(bf16[4,40,1024]{2,1,0:T(8,128)(2,1)} %bitcast.85), calls=%async_computation.1 | async-start | bytes 655360 | tf_op jit(solution)/shard_map/all_to_all | solution.py:18
  25.5 3.0 %copy-start.4 = (bf16[80,1024]{1,0:T(8,128)(2,1)}, bf16[80,1024]{1,0:T(8,128)(2,1)S(1)}, u32[]{:S(2)}) copy-start(bf16[80,1024]{1,0:T(8,128)(2,1)S(1)} %convolution_convert_fusion.5) | copy-start | bytes 491524
  33.6 3.1 %copy-start.8 = (bf16[80,1536]{1,0:T(8,128)(2,1)S(1)}, bf16[80,1536]{1,0:T(8,128)(2,1)}, u32[]{:S(2)}) copy-start(bf16[80,1536]{1,0:T(8,128)(2,1)} %fusion.20) | copy-start | bytes 737284
  34.9 13.5 %copy-start.3 = (bf16[80,1024]{1,0:T(8,128)(2,1)}, bf16[80,1024]{1,0:T(8,128)(2,1)S(1)}, u32[]{:S(2)}) copy-start(bf16[80,1024]{1,0:T(8,128)(2,1)S(1)} %convolution_convert_fusion.4) | copy-start | bytes 491524
  36.1 1.4 %collective-permute-start.4 = (bf16[80,768]{1,0:T(8,128)(2,1)S(1)}, bf16[80,768]{1,0:T(8,128)(2,1)S(1)}, u32[]{:S(2)}, u32[]{:S(2)}) collective-permute-start(bf16[80,768]{1,0:T(8,128)(2,1)S(1)} %constant_dynamic-slice_fusion), channel_id=1, source_target_pairs={{0,1},{1,0},{2,3},{3,2},{4,5},{5,4},{6,7},{7,6},{8,9},{9,8},{10,11... | collective-permute-start | bytes 368648 | tf_op jit(solution)/shard_map/ppermute | solution.py:13
  36.2 2.9 %collective-permute-start = (bf16[80,768]{1,0:T(8,128)(2,1)S(1)}, bf16[80,768]{1,0:T(8,128)(2,1)S(1)}, u32[]{:S(2)}, u32[]{:S(2)}) collective-permute-start(bf16[80,768]{1,0:T(8,128)(2,1)S(1)} %constant_dynamic-slice_fusion.2), channel_id=1, source_target_pairs={{0,1},{1,0},{2,3},{3,2},{4,5},{5,4},{6,7},{7,6},{8,9},{9,8},{10,11... | collective-permute-start | bytes 368648 | tf_op jit(solution)/shard_map/ppermute | solution.py:13
  36.7 3.0 %collective-permute-start.2 = (bf16[80,768]{1,0:T(8,128)(2,1)S(1)}, bf16[80,768]{1,0:T(8,128)(2,1)S(1)}, u32[]{:S(2)}, u32[]{:S(2)}) collective-permute-start(bf16[80,768]{1,0:T(8,128)(2,1)S(1)} %constant_dynamic-slice_fusion.1), channel_id=1, source_target_pairs={{0,1},{1,0},{2,3},{3,2},{4,5},{5,4},{6,7},{7,6},{8,9},{9,8},{10,11... | collective-permute-start | bytes 368648 | tf_op jit(solution)/shard_map/ppermute | solution.py:13
  37.5 6.2 %collective-permute-start.5 = (bf16[80,768]{1,0:T(8,128)(2,1)S(1)}, bf16[80,768]{1,0:T(8,128)(2,1)S(1)}, u32[]{:S(2)}, u32[]{:S(2)}) collective-permute-start(bf16[80,768]{1,0:T(8,128)(2,1)S(1)} %fusion.47), channel_id=1, source_target_pairs={{0,2},{1,3},{2,0},{3,1},{4,6},{5,7},{6,4},{7,5},{8,10},{9,11},{10,... | collective-permute-start | bytes 368648 | tf_op jit(solution)/shard_map/ppermute | solution.py:13
  39.1 7.3 %collective-permute-start.1 = (bf16[80,768]{1,0:T(8,128)(2,1)S(1)}, bf16[80,768]{1,0:T(8,128)(2,1)S(1)}, u32[]{:S(2)}, u32[]{:S(2)}) collective-permute-start(bf16[80,768]{1,0:T(8,128)(2,1)S(1)} %fusion.45), channel_id=1, source_target_pairs={{0,2},{1,3},{2,0},{3,1},{4,6},{5,7},{6,4},{7,5},{8,10},{9,11},{10,... | collective-permute-start | bytes 368648 | tf_op jit(solution)/shard_map/ppermute | solution.py:13
  39.7 8.5 %collective-permute-start.3 = (bf16[80,768]{1,0:T(8,128)(2,1)S(1)}, bf16[80,768]{1,0:T(8,128)(2,1)S(1)}, u32[]{:S(2)}, u32[]{:S(2)}) collective-permute-start(bf16[80,768]{1,0:T(8,128)(2,1)S(1)} %fusion.46), channel_id=1, source_target_pairs={{0,2},{1,3},{2,0},{3,1},{4,6},{5,7},{6,4},{7,5},{8,10},{9,11},{10,... | collective-permute-start | bytes 368648 | tf_op jit(solution)/shard_map/ppermute | solution.py:13
  48.5 0.7 copy-start.5
  48.5 0.7 copy-start.6
  48.5 0.7 copy-start.7
  49.2 1.9 %collective-permute-start.6 = (bf16[3,80,768]{2,1,0:T(8,128)(2,1)S(1)}, bf16[3,80,768]{2,1,0:T(8,128)(2,1)}, u32[]{:S(2)}, u32[]{:S(2)}) collective-permute-start(bf16[3,80,768]{2,1,0:T(8,128)(2,1)S(1)} %pad_maximum_fusion), channel_id=1, source_target_pairs={{0,1},{1,0},{2,3},{3,2},{4,5},{5,4},{6,7},{7,6},{8,9},{9,8},{10,11... | collective-permute-start | bytes 1105928 | tf_op jit(solution)/shard_map/ppermute | solution.py:13
  52.3 7.3 %copy-start.2 = (bf16[3,80,768]{2,1,0:T(8,128)(2,1)}, bf16[3,80,768]{2,1,0:T(8,128)(2,1)S(1)}, u32[]{:S(2)}) copy-start(bf16[3,80,768]{2,1,0:T(8,128)(2,1)S(1)} %get-tuple-element.7) | copy-start | bytes 1105924
  66.4 15.0 %all-to-all-start.2 = ((bf16[4,40,1024]{2,1,0:T(8,128)(2,1)}), bf16[4,40,1024]{2,1,0:T(8,128)(2,1)}, u32[]{:S(2)}, u32[]{:S(2)}) async-start(bf16[4,40,1024]{2,1,0:T(8,128)(2,1)} %bitcast.86), calls=%async_computation.2 | async-start | bytes 655360 | tf_op jit(solution)/shard_map/all_to_all | solution.py:18
  70.5 3.8 %copy-start.1 = (bf16[1,1536,1024]{2,1,0:T(8,128)(2,1)S(1)}, bf16[1,1536,1024]{2,1,0:T(8,128)(2,1)}, u32[]{:S(2)}) copy-start(bf16[1,1536,1024]{2,1,0:T(8,128)(2,1)} %fusion) | copy-start | bytes 9437188

commit v3 on v2

v3 whole, which is shorter than its diff:
```python
import functools

import jax
import jax.numpy as jnp
from jax import lax
from jax.experimental import pallas as pl
from jax.experimental.pallas import tpu as pltpu
from jax.sharding import PartitionSpec as P

MOST = 40
EXPERTS = 128
EMPTY = 64.0
BF = jnp.bfloat16
F32 = jnp.float32
MIB = 1 << 20
VMEM = pl.BlockSpec(memory_space=pltpu.VMEM)
ANY = pl.BlockSpec(memory_space=pl.ANY)
ROWS = (((0,), (0,)), ((), ()))
LANES = (((1,), (1,)), ((), ()))
PLAIN = (((1,), (0,)), ((), ()))


def mm(left, right, dims=PLAIN):
    return lax.dot_general(left, right, dims, preferred_element_type=F32)


def iota(shape, dim):
    return lax.broadcasted_iota(jnp.int32, shape, dim)


def block_of(position, blocks):
    found = jnp.zeros_like(position)
    for k in range(1, blocks):
        found = found + (position >= k * MOST).astype(jnp.int32)
    return found


def call(body, outs, operands, specs, scratch=(), limit=16, flops=0, traffic=0, out_specs=None):
    return pl.pallas_call(
        body,
        out_shape=outs,
        in_specs=specs,
        out_specs=out_specs if out_specs is not None else jax.tree.map(lambda _: VMEM, outs),
        scratch_shapes=list(scratch),
        compiler_params=pltpu.CompilerParams(vmem_limit_bytes=limit * MIB),
        cost_estimate=pl.CostEstimate(flops=flops, bytes_accessed=traffic, transcendentals=0),
    )(*operands)


def pick_inputs(experts, routes, probs, inputs, pick_out, prob_out, *pieces):
    me = lax.axis_index("ex")
    tokens = inputs.shape[0]
    rows = experts * MOST
    owner = block_of(iota((rows, routes.shape[1]), 0), experts)
    named = jnp.zeros((rows, tokens), F32)
    weight = jnp.zeros((rows, tokens), F32)
    chosen = routes[...]
    wide = probs[...].astype(F32)
    for k in range(experts):
        spread = jnp.where(owner == k, 1.0, 0.0).astype(BF)
        hit = chosen == (me ^ k)
        named = named + mm(spread, jnp.where(hit, 1.0, 0.0).astype(BF), LANES)
        weight = weight + mm(spread, jnp.where(hit, wide, 0.0).astype(BF), LANES)
    earlier = iota((tokens, tokens), 0) < iota((tokens, tokens), 1)
    rank = mm(named.astype(BF), jnp.where(earlier, 1.0, 0.0).astype(BF)).astype(jnp.int32)
    row = iota((rows, tokens), 0)
    slot = row - block_of(row, experts) * MOST
    picks = (rank == slot) & (named > 0.5)
    pick = jnp.where(picks, 1.0, 0.0)
    prob_out[...] = jnp.sum(jnp.where(picks, weight, 0.0), axis=1, keepdims=True)
    filled = jnp.max(pick, axis=1, keepdims=True) > 0.5
    pick = pick.astype(BF)
    pick_out[...] = pick
    sent = jnp.where(filled, mm(pick, inputs[...]), EMPTY)
    for k in range(experts):
        pieces[k][...] = sent[k * MOST : (k + 1) * MOST].astype(BF)


def pick_grads(experts, pick, prob, grads, *pieces):
    sent = mm(pick[...], grads[...]) * prob[...]
    for k in range(experts):
        pieces[k][...] = sent[k * MOST : (k + 1) * MOST].astype(BF)


def stacked(pieces):
    return jnp.concatenate([piece[...].astype(F32) for piece in pieces], axis=0)


def copies(weight, index, held, sems, core, slots):
    half = held.shape[-2]
    out = []
    for slot, (matrix, own) in enumerate(slots):
        start = (core if own else 1 - core) * half
        source = weight.at[(0,) + ((matrix,) if index else ()) + (pl.ds(start, half),)]
        out.append(pltpu.make_async_copy(source, held.at[slot], sems.at[slot]))
    return out


def gate_up_parts(experts, capacity, *refs):
    pieces = refs[:experts]
    weight, place_out, rows_out, other, mine, held, sems = refs[experts:]
    core = lax.axis_index("ey") & 1
    me = lax.axis_index("ex")
    slots = [(0, False), (1, False), (0, True), (1, True)]
    loads = copies(weight, True, held, sems, core, slots)
    for load in loads:
        load.start()
    rows = experts * MOST
    got = stacked(pieces)
    full = got[:, :1] < EMPTY / 2
    key = []
    for dim in (0, 1):
        row = iota((rows, rows), dim)
        block = block_of(row, experts)
        key.append((me ^ block) * MOST + row - block * MOST)
    earlier = jnp.where(key[1] < key[0], 1.0, 0.0).astype(BF)
    wide = jnp.broadcast_to(full, (rows, capacity))
    slot = mm(earlier, jnp.where(wide, 1.0, 0.0).astype(BF)).astype(jnp.int32)
    place = jnp.where((slot == iota((rows, capacity), 1)) & wide, 1.0, 0.0).astype(BF)
    place_out[...] = place
    rows_in = mm(place, got.astype(BF), ROWS).astype(BF)
    rows_out[...] = rows_in
    for at, (matrix, own) in enumerate(slots):
        loads[at].wait()
        (mine if own else other)[matrix] = mm(rows_in, held[at], LANES).astype(BF)


def act_parts(experts, *refs):
    pieces = refs[:experts]
    place, weight, rows_out, other, mine, held, sems = refs[experts:]
    core = lax.axis_index("ey") & 1
    slots = [(0, False), (0, True)]
    loads = copies(weight, False, held, sems, core, slots)
    for load in loads:
        load.start()
    rows_grad = mm(place[...], stacked(pieces).astype(BF), ROWS).astype(BF)
    rows_out[...] = rows_grad
    for at, (_, own) in enumerate(slots):
        loads[at].wait()
        (mine if own else other)[...] = mm(rows_grad, held[at], LANES).astype(BF)


def middle(pair, pair_far, act, act_far, out):
    gate_sum = pair[0] + pair_far[0].astype(F32)
    up_sum = pair[1] + pair_far[1].astype(F32)
    grad_act = act[...] + act_far[...].astype(F32)
    sigmoid_gate = jax.nn.sigmoid(gate_sum)
    silu_gate = gate_sum * sigmoid_gate
    out[0] = (silu_gate * up_sum).astype(BF)
    out[1] = (grad_act * up_sum * sigmoid_gate * (1.0 + gate_sum * (1.0 - sigmoid_gate))).astype(BF)
    out[2] = (grad_act * silu_gate).astype(BF)


def own_rows(mine, weight, out, held, sems):
    core = lax.axis_index("ey") & 1
    loads = copies(weight, True, held, sems, core, [(0, True), (1, True)])
    for load in loads:
        load.start()
    loads[0].wait()
    total = mm(mine[1], held[0])
    loads[1].wait()
    out[...] = total + mm(mine[2], held[1])


def other_rows(experts, total_in, other, place, weight, *refs):
    pieces = refs[:experts]
    held, sems = refs[experts:]
    core = lax.axis_index("ey") & 1
    loads = copies(weight, True, held, sems, core, [(0, False), (1, False)])
    for load in loads:
        load.start()
    loads[0].wait()
    total = total_in[...] + mm(other[1], held[0])
    loads[1].wait()
    total = total + mm(other[2], held[1])
    back = mm(place[...], total.astype(BF))
    for k in range(experts):
        pieces[k][...] = back[k * MOST : (k + 1) * MOST].astype(BF)


def weight_grads(mine, other, rows_in, rows_grad, pair_out, down_out, held, sems):
    core = lax.axis_index("ey") & 1
    half = mine.shape[2]
    step = half // 2
    stores = []
    for matrix in range(3):
        right = rows_grad[...] if matrix == 0 else rows_in[...]
        for own in range(2):
            start = (core if own else 1 - core) * half
            for part in range(2):
                left = (mine if own else other)[matrix, :, part * step : (part + 1) * step]
                at = len(stores)
                held[at] = mm(left, right, ROWS).astype(BF)
                rows = pl.ds(start + part * step, step)
                target = down_out.at[0, rows] if matrix == 0 else pair_out.at[0, matrix - 1, rows]
                store = pltpu.make_async_copy(held.at[at], target, sems.at[at])
                store.start()
                stores.append(store)
    for store in stores:
        store.wait()


def combine(experts, pick, *refs):
    home = stacked(refs[:experts]).astype(BF)
    refs[experts][...] = mm(pick[...], home, ROWS).astype(BF)


def swap(value, axis, bit):
    count = lax.axis_size(axis)
    return lax.ppermute(value, axis, [(i, i ^ bit) for i in range(count)])


def exchange(pieces, axis):
    return [pieces[0]] + [swap(pieces[k], axis, k) for k in range(1, len(pieces))]


def local(inputs, grad_output, routes, gate_probs, gate_up, down_proj):
    experts = lax.axis_size("ex")
    ways = lax.axis_size("ey")
    tokens, width = inputs.shape
    hidden = gate_up.shape[2]
    half = hidden // 2
    capacity = 5 * tokens * experts * routes.shape[1] // (4 * EXPERTS)
    rows = experts * MOST
    weight_bytes = hidden * width * 2
    weight_flops = 2 * capacity * hidden * width
    sds = jax.ShapeDtypeStruct
    piece = [sds((MOST, width), BF)] * experts
    dma = lambda count: pltpu.SemaphoreType.DMA((count,))

    pick, prob, *send_in = call(
        functools.partial(pick_inputs, experts),
        [sds((rows, tokens), BF), sds((rows, 1), F32)] + piece,
        (routes, gate_probs, inputs),
        [VMEM] * 3,
        flops=2 * rows * tokens * width,
        traffic=4 * tokens * width,
    )
    got_in = exchange(send_in, "ex")
    send_grad = call(
        functools.partial(pick_grads, experts),
        piece,
        (pick, prob, grad_output),
        [VMEM] * 3,
        flops=2 * rows * tokens * width,
        traffic=4 * tokens * width,
    )
    got_grad = exchange(send_grad, "ex")

    place, rows_in, pair_other, pair_mine = call(
        functools.partial(gate_up_parts, experts, capacity),
        [
            sds((rows, capacity), BF),
            sds((capacity, width), BF),
            sds((2, capacity, half), BF),
            sds((2, capacity, half), BF),
        ],
        (*got_in, gate_up),
        [VMEM] * experts + [ANY],
        [pltpu.VMEM((4, half, width), BF), dma(4)],
        limit=20,
        flops=2 * weight_flops,
        traffic=2 * weight_bytes,
    )

    def total(mine, other):
        held = mine.astype(F32) + swap(other, "ey", 1).astype(F32)
        bit = 2
        while bit * 2 < ways:
            held = held + swap(held.astype(BF), "ey", bit).astype(F32)
            bit *= 2
        return held, swap(held.astype(BF), "ey", bit)

    pair, pair_far = total(pair_mine, pair_other)
    rows_grad, act_other, act_mine = call(
        functools.partial(act_parts, experts),
        [sds((capacity, width), BF), sds((capacity, half), BF), sds((capacity, half), BF)],
        (*got_grad, place, down_proj),
        [VMEM] * (experts + 1) + [ANY],
        [pltpu.VMEM((2, half, width), BF), dma(2)],
        flops=weight_flops,
        traffic=weight_bytes,
    )
    act, act_far = total(act_mine, act_other)
    mine = call(
        middle,
        sds((3, capacity, half), BF),
        (pair, pair_far, act, act_far),
        [VMEM] * 4,
        traffic=24 * capacity * half,
    )
    other = swap(mine, "ey", 1)
    own = call(
        own_rows,
        sds((capacity, width), F32),
        (mine, gate_up),
        [VMEM, ANY],
        [pltpu.VMEM((2, half, width), BF), dma(2)],
        flops=weight_flops,
        traffic=weight_bytes,
    )
    back = call(
        functools.partial(other_rows, experts),
        piece,
        (own, other, place, gate_up),
        [VMEM] * 3 + [ANY],
        [pltpu.VMEM((2, half, width), BF), dma(2)],
        flops=weight_flops,
        traffic=weight_bytes,
    )
    home = exchange(back, "ex")
    pair_grad, down_grad = call(
        weight_grads,
        [sds((1, 2, hidden, width), BF), sds((1, hidden, width), BF)],
        (mine, other, rows_in, rows_grad),
        [VMEM] * 4,
        [pltpu.VMEM((12, half // 2, width), BF), dma(12)],
        limit=24,
        flops=3 * weight_flops,
        traffic=3 * weight_bytes,
        out_specs=[ANY, ANY],
    )
    grad_inputs = call(
        functools.partial(combine, experts),
        sds((tokens, width), BF),
        (pick, *home),
        [VMEM] * (experts + 1),
        flops=2 * rows * tokens * width,
        traffic=4 * tokens * width,
    )
    return (grad_inputs, pair_grad, down_grad)


def solution(mesh):
    return jax.shard_map(
        local,
        mesh=mesh,
        in_specs=(
            P(("groups", "ex"), "ey"),
            P(("groups", "ex"), "ey"),
            P(("groups", "ex"), None),
            P(("groups", "ex"), None),
            P("ex", None, None, "ey"),
            P("ex", None, "ey"),
        ),
        out_specs=(
            P(("groups", "ex"), "ey"),
            P("ex", "groups", None, "ey"),
            P("ex", "groups", "ey"),
        ),
        check_vma=False,
    )
```

time: 84.3 us -> 65.1 us (0.77)
  matrix products: 33.8 us -> 0 us
  Pallas kernels: 0 us -> 14.2 us
  other arithmetic: 9.54 us -> 0.09 us
  local copies, waits for them, and re-layouts: 1.02 us -> 7.35 us
  waiting for transfers between devices: 19.3 us -> 24.7 us
  starting transfers between devices: 19 us -> 17.6 us
    dot_general x15 -> x0, matrix products: 33.8 us -> none  [the longest x3 11.1 us: weight_grad(): lax.dot_general(left, right, contract_rows, preferred_element_type=jnp.fl...]
    ppermute x7 -> x14, waiting for transfers between devices: 9.35 us -> 24.7 us  [swap(): return lax.ppermute(value, axis, [(i, i ^ bit) for i in range(count)])]
    all_to_all x3 -> x0, starting transfers between devices: 14.5 us -> none  [exchange(): return lax.all_to_all(pieces, axis, 0, 0, tiled=True).reshape(value.shape)]
    pallas_call x0 -> x9, Pallas kernels: none -> 14.2 us  [call(): pl.pallas_call(body, out_shape=outs, in_specs=specs, out_specs=out_specs...]
    ppermute x7 -> x14, starting transfers between devices: 4.49 us -> 17.6 us  [swap(): return lax.ppermute(value, axis, [(i, i ^ bit) for i in range(count)])]
    all_to_all x3 -> x0, waiting for transfers between devices: 9.98 us -> none  [exchange(): return lax.all_to_all(pieces, axis, 0, 0, tiled=True).reshape(value.shape)]
    unnamed x18 -> x12, local copies, waits for them, and re-layouts: 0.69 us -> 7.35 us
    broadcast_in_dim x1 -> x0, other arithmetic: 5.17 us -> none  [local(): return (grad_inputs, pair_grad[None], down_grad[None])]
  transfers between devices with their start and end apart: 10 -> 14, of which waited for: 8 -> 6; matrix products, arithmetic and copies ran while one was open for 24% -> 0% of each run, Pallas kernels for 0% -> 11%
where the time goes in v3:
time: 65.1 us; the launch traced here: 64.8 us
  waiting for transfers between devices  24.7 us (38%)
  starting transfers between devices  17.6 us (27%)
  Pallas kernels  14.2 us (22%)
  local copies, waits for them, and re-layouts  7.35 us (11%)
  between operations  0.78 us (1%)
    ppermute x14, waiting for transfers between devices, swap(): return lax.ppermute(value, axis, [(i, i ^ bit) for i in range(count)])  24.7 us
    ppermute x14, starting transfers between devices, swap(): return lax.ppermute(value, axis, [(i, i ^ bit) for i in range(count)])  17.6 us
    pallas_call x9, Pallas kernels, call(): pl.pallas_call(body, out_shape=outs, in_specs=specs, out_specs=out_specs...  14.2 us
    unnamed x12, local copies, waits for them, and re-layouts  7.35 us
  transfers between devices with their start and end apart: 14, of which 6 were waited for; matrix products, arithmetic and copies ran while one was open for 0% of the time, Pallas kernels for 11%

profile of v3, /device:TPU:0, one launch (start us, length us, event | category | flops | bytes accessed | tf_op | source)
XLA Modules:
  0.0 64.8 jit_solution(14941803513435599154)
XLA Ops:
  0.6 0.8 %copy.9.routes = s32[256,8]{1,0:T(8,128)S(1)} copy(s32[256,8]{0,1:T(8,128)} %param.8) | data formatting | bytes 16384 | tf_op args[2]
  2.3 1.0 %copy-done.3 = bf16[256,1024]{1,0:T(8,128)(2,1)S(1)} copy-done((bf16[256,1024]{1,0:T(8,128)(2,1)S(1)}, bf16[256,1024]{1,0:T(8,128)(2,1)}, u32[]{:S(2)}) %copy-start.3) | copy-done | bytes 524312
  4.0 3.1 %collective-permute-start = (bf16[40,1024]{1,0:T(8,128)(2,1)S(1)}, bf16[40,1024]{1,0:T(8,128)(2,1)S(1)}, u32[]{:S(2)}, u32[]{:S(2)}) collective-permute-start(bf16[40,1024]{1,0:T(8,128)(2,1)S(1)} %get-tuple-element.28), channel_id=1, source_target_pairs={{0,4},{4,0},{8,12},{12,8},{1,5},{5,1},{9,13},{13,9},{2,6},{6,2},{1... | collective-permute-start | bytes 245768 | tf_op jit(solution)/shard_map/ppermute | solution.py:210
  7.1 2.6 %collective-permute-start.1 = (bf16[40,1024]{1,0:T(8,128)(2,1)S(1)}, bf16[40,1024]{1,0:T(8,128)(2,1)S(1)}, u32[]{:S(2)}, u32[]{:S(2)}) collective-permute-start(bf16[40,1024]{1,0:T(8,128)(2,1)S(1)} %get-tuple-element.29), channel_id=1, source_target_pairs={{0,8},{4,12},{8,0},{12,4},{1,9},{5,13},{9,1},{13,5},{2,10},{6,14},... | collective-permute-start | bytes 245768 | tf_op jit(solution)/shard_map/ppermute | solution.py:210
  9.7 6.6 %collective-permute-done.1.refs_2_ = bf16[40,1024]{1,0:T(8,128)(2,1)S(1)} collective-permute-done((bf16[40,1024]{1,0:T(8,128)(2,1)S(1)}, bf16[40,1024]{1,0:T(8,128)(2,1)S(1)}, u32[]{:S(2)}, u32[]{:S(2)}) %collective-permute-start.1) | collective-permute-done | bytes 81952 | tf_op jit(solution)/shard_map/ppermute | solution.py:210
  16.3 2.8 %copy-done = bf16[1,2,1536,1024]{3,2,1,0:T(8,128)(2,1)S(1)} copy-done((bf16[1,2,1536,1024]{3,2,1,0:T(8,128)(2,1)S(1)}, bf16[1,2,1536,1024]{3,2,1,0:T(8,128)(2,1)}, u32[]{:S(2)}) %copy-start) | copy-done | bytes 6291480
  19.1 3.8 %shard_map.86 = (bf16[160,80]{1,0:T(8,128)(2,1)S(1)}, bf16[80,1024]{1,0:T(8,128)(2,1)S(1)}, bf16[2,80,768]{2,1,0:T(8,128)(2,1)S(1)}, bf16[2,80,768]{2,1,0:T(8,128)(2,1)S(1)}) custom-call(bf16[40,1024]{1,0:T(8,128)(2,1)S(1)} %get-tuple-element.27.refs_0_, bf16[40,1024]{1,0:T(8,128)(2,1)S(1)} %collective-permute-done.refs_1_, ...), custom_call_target="tpu_custom_call" | custom-call | flops 503316480 | bytes 6291456 | tf_op jit(solution)/shard_map/pallas_call | solution.py:39
  23.3 1.5 %collective-permute-start.5 = (bf16[40,1024]{1,0:T(8,128)(2,1)S(1)}, bf16[40,1024]{1,0:T(8,128)(2,1)S(1)}, u32[]{:S(2)}, u32[]{:S(2)}) collective-permute-start(bf16[40,1024]{1,0:T(8,128)(2,1)S(1)} %get-tuple-element.35), channel_id=1, source_target_pairs={{0,4},{4,0},{8,12},{12,8},{1,5},{5,1},{9,13},{13,9},{2,6},{6,2},{1... | collective-permute-start | bytes 245768 | tf_op jit(solution)/shard_map/ppermute | solution.py:210
  24.8 1.6 %collective-permute-start.6 = (bf16[40,1024]{1,0:T(8,128)(2,1)S(1)}, bf16[40,1024]{1,0:T(8,128)(2,1)S(1)}, u32[]{:S(2)}, u32[]{:S(2)}) collective-permute-start(bf16[40,1024]{1,0:T(8,128)(2,1)S(1)} %get-tuple-element.36), channel_id=1, source_target_pairs={{0,8},{4,12},{8,0},{12,4},{1,9},{5,13},{9,1},{13,5},{2,10},{6,14},... | collective-permute-start | bytes 245768 | tf_op jit(solution)/shard_map/ppermute | solution.py:210
  26.4 1.3 %collective-permute-start.7 = (bf16[40,1024]{1,0:T(8,128)(2,1)S(1)}, bf16[40,1024]{1,0:T(8,128)(2,1)S(1)}, u32[]{:S(2)}, u32[]{:S(2)}) collective-permute-start(bf16[40,1024]{1,0:T(8,128)(2,1)S(1)} %get-tuple-element.37), channel_id=1, source_target_pairs={{0,12},{4,8},{8,4},{12,0},{1,13},{5,9},{9,5},{13,1},{2,14},{6,10},... | collective-permute-start | bytes 245768 | tf_op jit(solution)/shard_map/ppermute | solution.py:210
  28.2 6.2 %collective-permute-done.6.refs_2_ = bf16[40,1024]{1,0:T(8,128)(2,1)S(1)} collective-permute-done((bf16[40,1024]{1,0:T(8,128)(2,1)S(1)}, bf16[40,1024]{1,0:T(8,128)(2,1)S(1)}, u32[]{:S(2)}, u32[]{:S(2)}) %collective-permute-start.6) | collective-permute-done | bytes 81952 | tf_op jit(solution)/shard_map/ppermute | solution.py:210
  34.3 1.9 %copy-done.2 = bf16[1,1536,1024]{2,1,0:T(8,128)(2,1)S(1)} copy-done((bf16[1,1536,1024]{2,1,0:T(8,128)(2,1)S(1)}, bf16[1,1536,1024]{2,1,0:T(8,128)(2,1)}, u32[]{:S(2)}) %copy-start.2) | copy-done | bytes 3145752
  36.2 1.9 %shard_map.88 = (bf16[80,1024]{1,0:T(8,128)(2,1)S(1)}, bf16[80,768]{1,0:T(8,128)(2,1)S(1)}, bf16[80,768]{1,0:T(8,128)(2,1)S(1)}) custom-call(bf16[40,1024]{1,0:T(8,128)(2,1)S(1)} %get-tuple-element.34.refs_0_, bf16[40,1024]{1,0:T(8,128)(2,1)S(1)} %collective-permute-done.5.refs_1_, bf16[40,1024]{1,0:T(8,128)(2,1)S(1)} %collective-permute-done.6.refs_2_, ...), custom_call_target="tpu_custom_call" | custom-call | flops 251658240 | bytes 3145728 | tf_op jit(solution)/shard_map/pallas_call | solution.py:39
  38.3 1.6 %collective-permute-start.4 = (bf16[2,80,768]{2,1,0:T(8,128)(2,1)S(1)}, bf16[2,80,768]{2,1,0:T(8,128)(2,1)S(1)}, u32[]{:S(2)}, u32[]{:S(2)}) collective-permute-start(bf16[2,80,768]{2,1,0:T(8,128)(2,1)S(1)} %get-tuple-element.49), channel_id=1, source_target_pairs={{0,2},{1,3},{2,0},{3,1},{4,6},{5,7},{6,4},{7,5},{8,10},{9,11},{10,... | collective-permute-start | bytes 737288 | tf_op jit(solution)/shard_map/ppermute | solution.py:210
  39.9 1.2 %collective-permute-start.9 = (bf16[80,768]{1,0:T(8,128)(2,1)S(1)}, bf16[80,768]{1,0:T(8,128)(2,1)S(1)}, u32[]{:S(2)}, u32[]{:S(2)}) collective-permute-start(bf16[80,768]{1,0:T(8,128)(2,1)S(1)} %get-tuple-element.51), channel_id=1, source_target_pairs={{0,2},{1,3},{2,0},{3,1},{4,6},{5,7},{6,4},{7,5},{8,10},{9,11},{10,... | collective-permute-start | bytes 368648 | tf_op jit(solution)/shard_map/ppermute | solution.py:210
  41.1 8.2 %collective-permute-done.9.act_far = bf16[80,768]{1,0:T(8,128)(2,1)S(1)} collective-permute-done((bf16[80,768]{1,0:T(8,128)(2,1)S(1)}, bf16[80,768]{1,0:T(8,128)(2,1)S(1)}, u32[]{:S(2)}, u32[]{:S(2)}) %collective-permute-start.9) | collective-permute-done | bytes 122912 | tf_op jit(solution)/shard_map/ppermute | solution.py:210
  49.6 1.0 %shard_map.90.total_in = f32[80,1024]{1,0:T(8,128)S(1)} custom-call(bf16[3,80,768]{2,1,0:T(8,128)(2,1)S(1)} %shard_map.89.mine, bf16[1,2,1536,1024]{3,2,1,0:T(8,128)(2,1)S(1)} %copy-done.1), custom_call_target="tpu_custom_call" | custom-call | flops 251658240 | bytes 3145728 | tf_op jit(solution)/shard_map/pallas_call | solution.py:39
  51.3 1.1 %shard_map.91 = (bf16[40,1024]{1,0:T(8,128)(2,1)S(1)}, bf16[40,1024]{1,0:T(8,128)(2,1)S(1)}, bf16[40,1024]{1,0:T(8,128)(2,1)S(1)}, bf16[40,1024]{1,0:T(8,128)(2,1)S(1)}) custom-call(f32[80,1024]{1,0:T(8,128)S(1)} %shard_map.90.total_in, bf16[3,80,768]{2,1,0:T(8,128)(2,1)S(1)} %collective-permute-done.10.other, ...), custom_call_target="tpu_custom_call" | custom-call | flops 251658240 | bytes 3145728 | tf_op jit(solution)/shard_map/pallas_call | solution.py:39
  52.4 1.8 %collective-permute-start.11 = (bf16[40,1024]{1,0:T(8,128)(2,1)S(1)}, bf16[40,1024]{1,0:T(8,128)(2,1)S(1)}, u32[]{:S(2)}, u32[]{:S(2)}) collective-permute-start(bf16[40,1024]{1,0:T(8,128)(2,1)S(1)} %get-tuple-element.42), channel_id=1, source_target_pairs={{0,4},{4,0},{8,12},{12,8},{1,5},{5,1},{9,13},{13,9},{2,6},{6,2},{1... | collective-permute-start | bytes 245768 | tf_op jit(solution)/shard_map/ppermute | solution.py:210
  54.2 1.1 %collective-permute-start.12 = (bf16[40,1024]{1,0:T(8,128)(2,1)S(1)}, bf16[40,1024]{1,0:T(8,128)(2,1)S(1)}, u32[]{:S(2)}, u32[]{:S(2)}) collective-permute-start(bf16[40,1024]{1,0:T(8,128)(2,1)S(1)} %get-tuple-element.43), channel_id=1, source_target_pairs={{0,8},{4,12},{8,0},{12,4},{1,9},{5,13},{9,1},{13,5},{2,10},{6,14},... | collective-permute-start | bytes 245768 | tf_op jit(solution)/shard_map/ppermute | solution.py:210
  55.3 1.6 %collective-permute-start.13 = (bf16[40,1024]{1,0:T(8,128)(2,1)S(1)}, bf16[40,1024]{1,0:T(8,128)(2,1)S(1)}, u32[]{:S(2)}, u32[]{:S(2)}) collective-permute-start(bf16[40,1024]{1,0:T(8,128)(2,1)S(1)} %get-tuple-element.44), channel_id=1, source_target_pairs={{0,12},{4,8},{8,4},{12,0},{1,13},{5,9},{9,5},{13,1},{2,14},{6,10},... | collective-permute-start | bytes 245768 | tf_op jit(solution)/shard_map/ppermute | solution.py:210
  56.8 4.1 %shard_map.93 = (bf16[1,2,1536,1024]{3,2,1,0:T(8,128)(2,1)}, bf16[1,1536,1024]{2,1,0:T(8,128)(2,1)}) custom-call(bf16[3,80,768]{2,1,0:T(8,128)(2,1)S(1)} %shard_map.89.mine, bf16[3,80,768]{2,1,0:T(8,128)(2,1)S(1)} %collective-permute-done.10.other, bf16[80,1024]{1,0:T(8,128)(2,1)S(1)} %get-tuple-element.45.rows_in, ...), custom_call_target="tpu_custom_call" | custom-call | flops 754974720 | bytes 9437184 | tf_op jit(solution)/shard_map/pallas_call | solution.py:39
  61.0 2.7 %collective-permute-done.12.refs_2_ = bf16[40,1024]{1,0:T(8,128)(2,1)S(1)} collective-permute-done((bf16[40,1024]{1,0:T(8,128)(2,1)S(1)}, bf16[40,1024]{1,0:T(8,128)(2,1)S(1)}, u32[]{:S(2)}, u32[]{:S(2)}) %collective-permute-start.12) | collective-permute-done | bytes 81952 | tf_op jit(solution)/shard_map/ppermute | solution.py:210
  63.7 1.1 %shard_map.92 = bf16[256,1024]{1,0:T(8,128)(2,1)} custom-call(bf16[160,256]{1,0:T(8,128)(2,1)S(1)} %get-tuple-element.26.pick, bf16[40,1024]{1,0:T(8,128)(2,1)S(1)} %get-tuple-element.41.refs_0_, bf16[40,1024]{1,0:T(8,128)(2,1)S(1)} %collective-permute-done.11.refs_1_, bf16[40,1024]{1,0:T(8,128)(2,1)S(1)} %collective-permute-done.12.refs_2_, ...), custom_call_target="tpu_custom_call" | custom-call | flops 83886080 | bytes 1048576 | tf_op jit(solution)/shard_map/pallas_call | solution.py:39
  (27 shorter events, 3.3 us)
Async XLA Ops:
  2.3 1.0 %copy-start.3 = (bf16[256,1024]{1,0:T(8,128)(2,1)S(1)}, bf16[256,1024]{1,0:T(8,128)(2,1)}, u32[]{:S(2)}) copy-start(bf16[256,1024]{1,0:T(8,128)(2,1)} %inputs.1) | copy-start | bytes 1572868
  3.3 19.7 %copy-start.4 = (bf16[256,1024]{1,0:T(8,128)(2,1)S(1)}, bf16[256,1024]{1,0:T(8,128)(2,1)}, u32[]{:S(2)}) copy-start(bf16[256,1024]{1,0:T(8,128)(2,1)} %grads.1) | copy-start | bytes 1572868
  4.0 5.7 %collective-permute-start = (bf16[40,1024]{1,0:T(8,128)(2,1)S(1)}, bf16[40,1024]{1,0:T(8,128)(2,1)S(1)}, u32[]{:S(2)}, u32[]{:S(2)}) collective-permute-start(bf16[40,1024]{1,0:T(8,128)(2,1)S(1)} %get-tuple-element.28), channel_id=1, source_target_pairs={{0,4},{4,0},{8,12},{12,8},{1,5},{5,1},{9,13},{13,9},{2,6},{6,2},{1... | collective-permute-start | bytes 245768 | tf_op jit(solution)/shard_map/ppermute | solution.py:210
  7.1 9.2 %collective-permute-start.1 = (bf16[40,1024]{1,0:T(8,128)(2,1)S(1)}, bf16[40,1024]{1,0:T(8,128)(2,1)S(1)}, u32[]{:S(2)}, u32[]{:S(2)}) collective-permute-start(bf16[40,1024]{1,0:T(8,128)(2,1)S(1)} %get-tuple-element.29), channel_id=1, source_target_pairs={{0,8},{4,12},{8,0},{12,4},{1,9},{5,13},{9,1},{13,5},{2,10},{6,14},... | collective-permute-start | bytes 245768 | tf_op jit(solution)/shard_map/ppermute | solution.py:210
  9.7 6.6 %collective-permute-start.2 = (bf16[40,1024]{1,0:T(8,128)(2,1)S(1)}, bf16[40,1024]{1,0:T(8,128)(2,1)S(1)}, u32[]{:S(2)}, u32[]{:S(2)}) collective-permute-start(bf16[40,1024]{1,0:T(8,128)(2,1)S(1)} %get-tuple-element.30), channel_id=1, source_target_pairs={{0,12},{4,8},{8,4},{12,0},{1,13},{5,9},{9,5},{13,1},{2,14},{6,10},... | collective-permute-start | bytes 245768 | tf_op jit(solution)/shard_map/ppermute | solution.py:210
  16.3 2.8 %copy-start = (bf16[1,2,1536,1024]{3,2,1,0:T(8,128)(2,1)S(1)}, bf16[1,2,1536,1024]{3,2,1,0:T(8,128)(2,1)}, u32[]{:S(2)}) copy-start(bf16[1,2,1536,1024]{3,2,1,0:T(8,128)(2,1)} %weight.3) | copy-start | bytes 18874372
  19.1 30.5 %copy-start.1 = (bf16[1,2,1536,1024]{3,2,1,0:T(8,128)(2,1)S(1)}, bf16[1,2,1536,1024]{3,2,1,0:T(8,128)(2,1)}, u32[]{:S(2)}) copy-start(bf16[1,2,1536,1024]{3,2,1,0:T(8,128)(2,1)} %weight.3) | copy-start | bytes 18874372
  22.9 15.3 %collective-permute-start.3 = (bf16[2,80,768]{2,1,0:T(8,128)(2,1)S(1)}, bf16[2,80,768]{2,1,0:T(8,128)(2,1)S(1)}, u32[]{:S(2)}, u32[]{:S(2)}) collective-permute-start(bf16[2,80,768]{2,1,0:T(8,128)(2,1)S(1)} %get-tuple-element.32), channel_id=1, source_target_pairs={{0,1},{1,0},{2,3},{3,2},{4,5},{5,4},{6,7},{7,6},{8,9},{9,8},{10,11... | collective-permute-start | bytes 737288 | tf_op jit(solution)/shard_map/ppermute | solution.py:210
  23.3 4.9 %collective-permute-start.5 = (bf16[40,1024]{1,0:T(8,128)(2,1)S(1)}, bf16[40,1024]{1,0:T(8,128)(2,1)S(1)}, u32[]{:S(2)}, u32[]{:S(2)}) collective-permute-start(bf16[40,1024]{1,0:T(8,128)(2,1)S(1)} %get-tuple-element.35), channel_id=1, source_target_pairs={{0,4},{4,0},{8,12},{12,8},{1,5},{5,1},{9,13},{13,9},{2,6},{6,2},{1... | collective-permute-start | bytes 245768 | tf_op jit(solution)/shard_map/ppermute | solution.py:210
  24.8 9.5 %collective-permute-start.6 = (bf16[40,1024]{1,0:T(8,128)(2,1)S(1)}, bf16[40,1024]{1,0:T(8,128)(2,1)S(1)}, u32[]{:S(2)}, u32[]{:S(2)}) collective-permute-start(bf16[40,1024]{1,0:T(8,128)(2,1)S(1)} %get-tuple-element.36), channel_id=1, source_target_pairs={{0,8},{4,12},{8,0},{12,4},{1,9},{5,13},{9,1},{13,5},{2,10},{6,14},... | collective-permute-start | bytes 245768 | tf_op jit(solution)/shard_map/ppermute | solution.py:210
  26.4 8.0 %collective-permute-start.7 = (bf16[40,1024]{1,0:T(8,128)(2,1)S(1)}, bf16[40,1024]{1,0:T(8,128)(2,1)S(1)}, u32[]{:S(2)}, u32[]{:S(2)}) collective-permute-start(bf16[40,1024]{1,0:T(8,128)(2,1)S(1)} %get-tuple-element.37), channel_id=1, source_target_pairs={{0,12},{4,8},{8,4},{12,0},{1,13},{5,9},{9,5},{13,1},{2,14},{6,10},... | collective-permute-start | bytes 245768 | tf_op jit(solution)/shard_map/ppermute | solution.py:210
  34.3 1.9 %copy-start.2 = (bf16[1,1536,1024]{2,1,0:T(8,128)(2,1)S(1)}, bf16[1,1536,1024]{2,1,0:T(8,128)(2,1)}, u32[]{:S(2)}) copy-start(bf16[1,1536,1024]{2,1,0:T(8,128)(2,1)} %refs_5_.1) | copy-start | bytes 9437188
  38.1 1.7 %collective-permute-start.8 = (bf16[80,768]{1,0:T(8,128)(2,1)S(1)}, bf16[80,768]{1,0:T(8,128)(2,1)S(1)}, u32[]{:S(2)}, u32[]{:S(2)}) collective-permute-start(bf16[80,768]{1,0:T(8,128)(2,1)S(1)} %get-tuple-element.40), channel_id=1, source_target_pairs={{0,1},{1,0},{2,3},{3,2},{4,5},{5,4},{6,7},{7,6},{8,9},{9,8},{10,11... | collective-permute-start | bytes 368648 | tf_op jit(solution)/shard_map/ppermute | solution.py:210
  38.3 11.0 %collective-permute-start.4 = (bf16[2,80,768]{2,1,0:T(8,128)(2,1)S(1)}, bf16[2,80,768]{2,1,0:T(8,128)(2,1)S(1)}, u32[]{:S(2)}, u32[]{:S(2)}) collective-permute-start(bf16[2,80,768]{2,1,0:T(8,128)(2,1)S(1)} %get-tuple-element.49), channel_id=1, source_target_pairs={{0,2},{1,3},{2,0},{3,1},{4,6},{5,7},{6,4},{7,5},{8,10},{9,11},{10,... | collective-permute-start | bytes 737288 | tf_op jit(solution)/shard_map/ppermute | solution.py:210
  39.9 9.4 %collective-permute-start.9 = (bf16[80,768]{1,0:T(8,128)(2,1)S(1)}, bf16[80,768]{1,0:T(8,128)(2,1)S(1)}, u32[]{:S(2)}, u32[]{:S(2)}) collective-permute-start(bf16[80,768]{1,0:T(8,128)(2,1)S(1)} %get-tuple-element.51), channel_id=1, source_target_pairs={{0,2},{1,3},{2,0},{3,1},{4,6},{5,7},{6,4},{7,5},{8,10},{9,11},{10,... | collective-permute-start | bytes 368648 | tf_op jit(solution)/shard_map/ppermute | solution.py:210
  49.5 1.8 %collective-permute-start.10 = (bf16[3,80,768]{2,1,0:T(8,128)(2,1)S(1)}, bf16[3,80,768]{2,1,0:T(8,128)(2,1)S(1)}, u32[]{:S(2)}, u32[]{:S(2)}) collective-permute-start(bf16[3,80,768]{2,1,0:T(8,128)(2,1)S(1)} %shard_map.89.mine), channel_id=1, source_target_pairs={{0,1},{1,0},{2,3},{3,2},{4,5},{5,4},{6,7},{7,6},{8,9},{9,8},{10,11... | collective-permute-start | bytes 1105928 | tf_op jit(solution)/shard_map/ppermute | solution.py:210
  52.4 8.6 %collective-permute-start.11 = (bf16[40,1024]{1,0:T(8,128)(2,1)S(1)}, bf16[40,1024]{1,0:T(8,128)(2,1)S(1)}, u32[]{:S(2)}, u32[]{:S(2)}) collective-permute-start(bf16[40,1024]{1,0:T(8,128)(2,1)S(1)} %get-tuple-element.42), channel_id=1, source_target_pairs={{0,4},{4,0},{8,12},{12,8},{1,5},{5,1},{9,13},{13,9},{2,6},{6,2},{1... | collective-permute-start | bytes 245768 | tf_op jit(solution)/shard_map/ppermute | solution.py:210
  54.2 9.5 %collective-permute-start.12 = (bf16[40,1024]{1,0:T(8,128)(2,1)S(1)}, bf16[40,1024]{1,0:T(8,128)(2,1)S(1)}, u32[]{:S(2)}, u32[]{:S(2)}) collective-permute-start(bf16[40,1024]{1,0:T(8,128)(2,1)S(1)} %get-tuple-element.43), channel_id=1, source_target_pairs={{0,8},{4,12},{8,0},{12,4},{1,9},{5,13},{9,1},{13,5},{2,10},{6,14},... | collective-permute-start | bytes 245768 | tf_op jit(solution)/shard_map/ppermute | solution.py:210
  55.3 8.4 %collective-permute-start.13 = (bf16[40,1024]{1,0:T(8,128)(2,1)S(1)}, bf16[40,1024]{1,0:T(8,128)(2,1)S(1)}, u32[]{:S(2)}, u32[]{:S(2)}) collective-permute-start(bf16[40,1024]{1,0:T(8,128)(2,1)S(1)} %get-tuple-element.44), channel_id=1, source_target_pairs={{0,12},{4,8},{8,4},{12,0},{1,13},{5,9},{9,5},{13,1},{2,14},{6,10},... | collective-permute-start | bytes 245768 | tf_op jit(solution)/shard_map/ppermute | solution.py:210

commit v4 on v3

v4 whole, which is shorter than its diff:
```python
import functools

import jax
import jax.numpy as jnp
from jax import lax
from jax.experimental import pallas as pl
from jax.experimental.pallas import tpu as pltpu
from jax.sharding import PartitionSpec as P

MOST = 40
EXPERTS = 128
EMPTY = 64.0
BF = jnp.bfloat16
F32 = jnp.float32
MIB = 1 << 20
GATE_COST = 18
C2COST = 100
VMEM = pl.BlockSpec(memory_space=pltpu.VMEM)
ANY = pl.BlockSpec(memory_space=pl.ANY)
HBM = pl.BlockSpec(memory_space=pltpu.HBM)
ROWS = (((0,), (0,)), ((), ()))
LANES = (((1,), (1,)), ((), ()))
PLAIN = (((1,), (0,)), ((), ()))


def mm(left, right, dims=PLAIN):
    return lax.dot_general(left, right, dims, preferred_element_type=F32)


def iota(shape, dim):
    return lax.broadcasted_iota(jnp.int32, shape, dim)


def block_of(position, blocks):
    found = jnp.zeros_like(position)
    for k in range(1, blocks):
        found = found + (position >= k * MOST).astype(jnp.int32)
    return found


def call(body, outs, operands, specs, scratch=(), limit=16, flops=0, traffic=0, out_specs=None):
    return pl.pallas_call(
        body,
        out_shape=outs,
        in_specs=specs,
        out_specs=out_specs if out_specs is not None else jax.tree.map(lambda _: VMEM, outs),
        scratch_shapes=list(scratch),
        compiler_params=pltpu.CompilerParams(vmem_limit_bytes=limit * MIB),
        cost_estimate=pl.CostEstimate(flops=flops, bytes_accessed=traffic, transcendentals=0),
    )(*operands)


def pick_rows(experts, routes_in, probs_in, inputs, grads, pick_out, *refs):
    *pieces, routes, probs, held, sems = refs
    loads = [
        pltpu.make_async_copy(source, target, sems.at[at])
        for at, (source, target) in enumerate(
            [(routes_in, routes), (probs_in, probs), (inputs, held.at[0]), (grads, held.at[1])]
        )
    ]
    for load in loads:
        load.start()
    me = lax.axis_index("ex")
    tokens = inputs.shape[0]
    rows = experts * MOST
    owner = block_of(iota((rows, routes.shape[0]), 0), experts)
    named = jnp.zeros((rows, tokens), F32)
    weight = jnp.zeros((rows, tokens), F32)
    loads[0].wait()
    loads[1].wait()
    chosen = routes[...]
    wide = probs[...].astype(F32)
    for k in range(experts):
        spread = jnp.where(owner == k, 1.0, 0.0).astype(BF)
        hit = chosen == (me ^ k)
        named = named + mm(spread, jnp.where(hit, 1.0, 0.0).astype(BF))
        weight = weight + mm(spread, jnp.where(hit, wide, 0.0).astype(BF))
    earlier = iota((tokens, tokens), 0) < iota((tokens, tokens), 1)
    rank = mm(named.astype(BF), jnp.where(earlier, 1.0, 0.0).astype(BF)).astype(jnp.int32)
    row = iota((rows, tokens), 0)
    slot = row - block_of(row, experts) * MOST
    picks = (rank == slot) & (named > 0.5)
    pick = jnp.where(picks, 1.0, 0.0)
    prob = jnp.sum(jnp.where(picks, weight, 0.0), axis=1, keepdims=True)
    filled = jnp.max(pick, axis=1, keepdims=True) > 0.5
    pick = pick.astype(BF)
    pick_out[...] = pick
    loads[2].wait()
    sent = jnp.where(filled, mm(pick, held[0]), EMPTY)
    for k in range(experts):
        pieces[k][...] = sent[k * MOST : (k + 1) * MOST].astype(BF)
    loads[3].wait()
    sent = mm(pick, held[1]) * prob
    for k in range(experts):
        pieces[experts + k][...] = sent[k * MOST : (k + 1) * MOST].astype(BF)


def stacked(pieces):
    return jnp.concatenate([piece[...].astype(F32) for piece in pieces], axis=0)


def rows_of(half, own):
    core = lax.axis_index("ey") & 1
    return pl.ds(pl.multiple_of((core if own else 1 - core) * half, 128), half)


def place_rows(experts, capacity, pieces):
    me = lax.axis_index("ex")
    rows = experts * MOST
    got = stacked(pieces)
    full = got[:, :1] < EMPTY / 2
    key = []
    for dim in (0, 1):
        row = iota((rows, rows), dim)
        block = block_of(row, experts)
        key.append((me ^ block) * MOST + row - block * MOST)
    earlier = jnp.where(key[1] < key[0], 1.0, 0.0).astype(BF)
    wide = jnp.broadcast_to(full, (rows, capacity))
    slot = mm(earlier, jnp.where(wide, 1.0, 0.0).astype(BF)).astype(jnp.int32)
    place = jnp.where((slot == iota((rows, capacity), 1)) & wide, 1.0, 0.0).astype(BF)
    return place, mm(place, got.astype(BF), ROWS).astype(BF)


def gate_up_parts(experts, capacity, own, *refs):
    pieces = refs[:experts]
    weight, held, out, *extra, sems = refs[experts:]
    half = weight.shape[2] // 2
    loads = []
    for matrix in range(2):
        source = weight.at[0, matrix, rows_of(half, own)]
        loads.append(pltpu.make_async_copy(source, held.at[matrix], sems.at[matrix]))
        loads[matrix].start()
    place, rows_in = place_rows(experts, capacity, pieces)
    if extra:
        extra[0][...] = place
        extra[1][...] = rows_in
    for matrix in range(2):
        loads[matrix].wait()
        out[matrix] = mm(rows_in, held[matrix], LANES).astype(BF)


def act_parts(experts, *refs):
    pieces = refs[:experts]
    place, weight, _, rows_out, other, mine, held, sems = refs[experts:]
    half = weight.shape[1] // 2
    loads = []
    for own in range(2):
        source = weight.at[0, rows_of(half, own == 1)]
        loads.append(pltpu.make_async_copy(source, held.at[own], sems.at[own]))
        loads[own].start()
    rows_grad = mm(place[...], stacked(pieces).astype(BF), ROWS).astype(BF)
    rows_out[...] = rows_grad
    for own, out in enumerate((other, mine)):
        loads[own].wait()
        out[...] = mm(rows_grad, held[own], LANES).astype(BF)


def gates(pair, pair_far, act_out, by_gate, by_up):
    gate_sum = pair[0] + pair_far[0].astype(F32)
    up_sum = pair[1] + pair_far[1].astype(F32)
    sigmoid_gate = jax.nn.sigmoid(gate_sum)
    silu_gate = gate_sum * sigmoid_gate
    act_out[...] = (silu_gate * up_sum).astype(BF)
    by_gate[...] = up_sum * sigmoid_gate * (1.0 + gate_sum * (1.0 - sigmoid_gate))
    by_up[...] = silu_gate


def grads_of(act, act_far, by_gate, by_up, out):
    grad_act = act[...] + act_far[...].astype(F32)
    out[0] = (grad_act * by_gate[...]).astype(BF)
    out[1] = (grad_act * by_up[...]).astype(BF)


def own_rows(mine, held, out):
    out[...] = mm(mine[0], held[0]) + mm(mine[1], held[1])


def other_rows(experts, total, other, place, held, *pieces):
    rows = total[...] + mm(other[0], held[0]) + mm(other[1], held[1])
    back = mm(place[...], rows.astype(BF))
    for k in range(experts):
        pieces[k][...] = back[k * MOST : (k + 1) * MOST].astype(BF)


def weight_grads(mine_act, other_act, mine, other, rows_in, rows_grad, pair_out, down_out, held, sems):
    core = lax.axis_index("ey") & 1
    half = mine_act.shape[1]
    step = half // 2
    stores = []
    for matrix in range(3):
        right = rows_grad[...] if matrix == 0 else rows_in[...]
        for own in range(2):
            start = (core if own else 1 - core) * half
            for part in range(2):
                columns = slice(part * step, (part + 1) * step)
                if matrix == 0:
                    left = (mine_act if own else other_act)[:, columns]
                else:
                    left = (mine if own else other)[matrix - 1, :, columns]
                at = len(stores)
                held[at] = mm(left, right, ROWS).astype(BF)
                rows = pl.ds(start + part * step, step)
                target = down_out.at[0, rows] if matrix == 0 else pair_out.at[0, matrix - 1, rows]
                store = pltpu.make_async_copy(held.at[at], target, sems.at[at])
                store.start()
                stores.append(store)
    for store in stores:
        store.wait()


def combine(experts, pick, *refs):
    home = stacked(refs[:experts]).astype(BF)
    refs[experts][...] = mm(pick[...], home, ROWS).astype(BF)


def far(value):
    return pltpu.with_memory_space_constraint(value, pltpu.HBM)


def swap(value, axis, bit):
    count = lax.axis_size(axis)
    return lax.ppermute(value, axis, [(i, i ^ bit) for i in range(count)])


def exchange(pieces, axis):
    got = list(pieces)
    for k in list(range(2, len(pieces))) + [1]:
        got[k] = swap(pieces[k], axis, k)
    return got


def local(inputs, grad_output, routes, gate_probs, gate_up, down_proj):
    experts = lax.axis_size("ex")
    ways = lax.axis_size("ey")
    tokens, width = inputs.shape
    hidden = gate_up.shape[2]
    half = hidden // 2
    capacity = 5 * tokens * experts * routes.shape[1] // (4 * EXPERTS)
    rows = experts * MOST
    weight_bytes = hidden * width * 2
    weight_flops = 2 * capacity * hidden * width
    sds = jax.ShapeDtypeStruct
    piece = [sds((MOST, width), BF)] * experts
    dma = lambda count: pltpu.SemaphoreType.DMA((count,))

    pick, *sent = call(
        functools.partial(pick_rows, experts),
        [sds((rows, tokens), BF)] + piece * 2,
        (far(routes.T), far(gate_probs.T), far(inputs), far(grad_output)),
        [HBM] * 4,
        [
            pltpu.VMEM(routes.shape[::-1], jnp.int32),
            pltpu.VMEM(routes.shape[::-1], BF),
            pltpu.VMEM((2, tokens, width), BF),
            dma(4),
        ],
        flops=4 * rows * tokens * width,
        traffic=4 * tokens * width,
    )
    got_in = exchange(sent[:experts], "ex")
    got_grad = exchange(sent[experts:], "ex")
    def pair_part(own, extra, cost):
        return call(
            functools.partial(gate_up_parts, experts, capacity, own),
            [pltpu.VMEM((2, half, width), BF), sds((2, capacity, half), BF)] + extra,
            (*got_in, far(gate_up)),
            [VMEM] * experts + [HBM],
            [dma(2)],
            flops=cost * weight_flops,
            traffic=cost * weight_bytes,
        )

    held_other, pair_other = pair_part(False, [], 1)
    held_mine, pair_mine, place, rows_in = pair_part(
        True, [sds((rows, capacity), BF), sds((capacity, width), BF)], C2COST
    )
    def total(mine, other):
        held = mine.astype(F32) + other.astype(F32)
        bit = 2
        while bit * 2 < ways:
            held = held + swap(held.astype(BF), "ey", bit).astype(F32)
            bit *= 2
        sent = held.astype(BF)
        return held, sent, swap(sent, "ey", bit)

    pair, pair_sent, pair_far = total(pair_mine, swap(pair_other, "ey", 1))
    rows_grad, act_other, act_mine = call(
        functools.partial(act_parts, experts),
        [sds((capacity, width), BF), sds((capacity, half), BF), sds((capacity, half), BF)],
        (*got_grad, place, far(down_proj), pair_sent),
        [VMEM] * (experts + 1) + [HBM, ANY],
        [pltpu.VMEM((2, half, width), BF), dma(2)],
        flops=weight_flops,
        traffic=weight_bytes,
    )
    act, _, act_far = total(act_mine, swap(act_other, "ey", 1))
    mine_act, by_gate, by_up = call(
        gates,
        [sds((capacity, half), BF)] + [sds((capacity, half), F32)] * 2,
        (pair, pair_far),
        [VMEM] * 2,
        traffic=GATE_COST * capacity * half,
    )
    other_act = swap(mine_act, "ey", 1)
    mine = call(
        grads_of,
        sds((2, capacity, half), BF),
        (act, act_far, by_gate, by_up),
        [VMEM] * 4,
        traffic=18 * capacity * half,
    )
    other = swap(mine, "ey", 1)
    own = call(
        own_rows,
        sds((capacity, width), F32),
        (mine, held_mine),
        [VMEM] * 2,
        flops=weight_flops,
        traffic=weight_bytes,
    )
    back = call(
        functools.partial(other_rows, experts),
        piece,
        (own, other, place, held_other),
        [VMEM] * 4,
        flops=weight_flops,
        traffic=weight_bytes,
    )
    home = exchange(back, "ex")
    pair_grad, down_grad = call(
        weight_grads,
        [sds((1, 2, hidden, width), BF), sds((1, hidden, width), BF)],
        (mine_act, other_act, mine, other, rows_in, rows_grad),
        [VMEM] * 6,
        [pltpu.VMEM((12, half // 2, width), BF), dma(12)],
        limit=24,
        flops=3 * weight_flops,
        traffic=3 * weight_bytes,
        out_specs=[ANY, ANY],
    )
    grad_inputs = call(
        functools.partial(combine, experts),
        sds((tokens, width), BF),
        (pick, *home),
        [VMEM] * (experts + 1),
        flops=2 * rows * tokens * width,
        traffic=4 * tokens * width,
    )
    return (grad_inputs, pair_grad, down_grad)


def solution(mesh):
    return jax.shard_map(
        local,
        mesh=mesh,
        in_specs=(
            P(("groups", "ex"), "ey"),
            P(("groups", "ex"), "ey"),
            P(("groups", "ex"), None),
            P(("groups", "ex"), None),
            P("ex", None, None, "ey"),
            P("ex", None, "ey"),
        ),
        out_specs=(
            P(("groups", "ex"), "ey"),
            P("ex", "groups", None, "ey"),
            P("ex", "groups", "ey"),
        ),
        check_vma=False,
    )
```

time: 65.1 us -> 54.7 us (0.84)
  waiting for transfers between devices: 24.7 us -> 13.8 us
  local copies, waits for them, and re-layouts: 7.35 us -> 0 us
  starting transfers between devices: 17.6 us -> 21.7 us
  Pallas kernels: 14.2 us -> 18.1 us
    ppermute x14 -> x15, waiting for transfers between devices: 24.7 us -> 13.8 us  [swap(): return lax.ppermute(value, axis, [(i, i ^ bit) for i in range(count)])]
    unnamed x12 -> x0, local copies, waits for them, and re-layouts: 7.35 us -> none
    ppermute x14 -> x15, starting transfers between devices: 17.6 us -> 21.7 us  [swap(): return lax.ppermute(value, axis, [(i, i ^ bit) for i in range(count)])]
    pallas_call x9 -> x10, Pallas kernels: 14.2 us -> 18.1 us  [call(): pl.pallas_call(body, out_shape=outs, in_specs=specs, out_specs=out_specs...]
  transfers between devices with their start and end apart: 14 -> 15, of which waited for: 6 -> 5; matrix products, arithmetic and copies ran while one was open for 0% -> 0% of each run, Pallas kernels for 11% -> 22%
where the time goes in v4:
time: 54.7 us; the launch traced here: 54.5 us
  starting transfers between devices  21.7 us (40%)
  Pallas kernels  18.1 us (33%)
  waiting for transfers between devices  13.8 us (25%)
  between operations  0.76 us (1%)
    ppermute x15, starting transfers between devices, swap(): return lax.ppermute(value, axis, [(i, i ^ bit) for i in range(count)])  21.7 us
    pallas_call x10, Pallas kernels, call(): pl.pallas_call(body, out_shape=outs, in_specs=specs, out_specs=out_specs...  18.1 us
    ppermute x15, waiting for transfers between devices, swap(): return lax.ppermute(value, axis, [(i, i ^ bit) for i in range(count)])  13.8 us
  transfers between devices with their start and end apart: 15, of which 5 were waited for; matrix products, arithmetic and copies ran while one was open for 0% of the time, Pallas kernels for 22%

profile of v4, /device:TPU:0, one launch (start us, length us, event | category | flops | bytes accessed | tf_op | source)
XLA Modules:
  0.0 54.5 jit_solution(4503924769281239755)
XLA Ops:
  0.6 1.7 %shard_map.85 = (bf16[160,256]{1,0:T(8,128)(2,1)S(1)}, bf16[40,1024]{1,0:T(8,128)(2,1)S(1)}, bf16[40,1024]{1,0:T(8,128)(2,1)S(1)}, bf16[40,1024]{1,0:T(8,128)(2,...) custom-call(s32[8,256]{1,0:T(8,128)} %bitcast.2, ...), custom_call_target="tpu_custom_call" | custom-call | flops 167772160 | bytes 1048576 | tf_op jit(solution)/shard_map/pallas_call | solution.py:42
  2.4 3.1 %collective-permute-start.3 = (bf16[40,1024]{1,0:T(8,128)(2,1)S(1)}, bf16[40,1024]{1,0:T(8,128)(2,1)S(1)}, u32[]{:S(2)}, u32[]{:S(2)}) collective-permute-start(bf16[40,1024]{1,0:T(8,128)(2,1)S(1)} %get-tuple-element.36), channel_id=1, source_target_pairs={{0,4},{4,0},{8,12},{12,8},{1,5},{5,1},{9,13},{13,9},{2,6},{6,2},{1... | collective-permute-start | bytes 245768 | tf_op jit(solution)/shard_map/ppermute | solution.py:222
  5.5 2.6 %collective-permute-start.4 = (bf16[40,1024]{1,0:T(8,128)(2,1)S(1)}, bf16[40,1024]{1,0:T(8,128)(2,1)S(1)}, u32[]{:S(2)}, u32[]{:S(2)}) collective-permute-start(bf16[40,1024]{1,0:T(8,128)(2,1)S(1)} %get-tuple-element.37), channel_id=1, source_target_pairs={{0,8},{4,12},{8,0},{12,4},{1,9},{5,13},{9,1},{13,5},{2,10},{6,14},... | collective-permute-start | bytes 245768 | tf_op jit(solution)/shard_map/ppermute | solution.py:222
  8.1 0.9 %collective-permute-start = (bf16[40,1024]{1,0:T(8,128)(2,1)S(1)}, bf16[40,1024]{1,0:T(8,128)(2,1)S(1)}, u32[]{:S(2)}, u32[]{:S(2)}) collective-permute-start(bf16[40,1024]{1,0:T(8,128)(2,1)S(1)} %get-tuple-element.32), channel_id=1, source_target_pairs={{0,4},{4,0},{8,12},{12,8},{1,5},{5,1},{9,13},{13,9},{2,6},{6,2},{1... | collective-permute-start | bytes 245768 | tf_op jit(solution)/shard_map/ppermute | solution.py:222
  9.0 3.5 %collective-permute-start.1 = (bf16[40,1024]{1,0:T(8,128)(2,1)S(1)}, bf16[40,1024]{1,0:T(8,128)(2,1)S(1)}, u32[]{:S(2)}, u32[]{:S(2)}) collective-permute-start(bf16[40,1024]{1,0:T(8,128)(2,1)S(1)} %get-tuple-element.33), channel_id=1, source_target_pairs={{0,8},{4,12},{8,0},{12,4},{1,9},{5,13},{9,1},{13,5},{2,10},{6,14},... | collective-permute-start | bytes 245768 | tf_op jit(solution)/shard_map/ppermute | solution.py:222
  12.8 3.0 %collective-permute-done.4.refs_2_ = bf16[40,1024]{1,0:T(8,128)(2,1)S(1)} collective-permute-done((bf16[40,1024]{1,0:T(8,128)(2,1)S(1)}, bf16[40,1024]{1,0:T(8,128)(2,1)S(1)}, u32[]{:S(2)}, u32[]{:S(2)}) %collective-permute-start.4) | collective-permute-done | bytes 81952 | tf_op jit(solution)/shard_map/ppermute | solution.py:222
  15.7 3.2 %shard_map.87 = (bf16[2,768,1024]{2,1,0:T(8,128)(2,1)S(1)}, bf16[2,80,768]{2,1,0:T(8,128)(2,1)S(1)}) custom-call(bf16[40,1024]{1,0:T(8,128)(2,1)S(1)} %get-tuple-element.35.refs_0_, bf16[40,1024]{1,0:T(8,128)(2,1)S(1)} %collective-permute-done.3.refs_1_, bf16[40,1024]{1,0:T(8,128)(2,1)S(1)} %collective-permute-done.4.refs_2_, ...), custom_call_target="tpu_custom_call" | custom-call | flops 251658240 | bytes 3145728 | tf_op jit(solution)/shard_map/pallas_call | solution.py:42
  19.0 3.2 %shard_map.86 = (bf16[2,768,1024]{2,1,0:T(8,128)(2,1)S(1)}, bf16[2,80,768]{2,1,0:T(8,128)(2,1)S(1)}, bf16[160,80]{1,0:T(8,128)(2,1)S(1)}, bf16[80,1024]{1,0:T(8,128)(2,1)S(1)}) custom-call(bf16[40,1024]{1,0:T(8,128)(2,1)S(1)} %get-tuple-element.35.refs_0_, bf16[40,1024]{1,0:T(8,128)(2,1)S(1)} %collective-permute-done.3.refs_1_, ...), custom_call_target="tpu_custom_call" | custom-call | flops 25165824000 | bytes 314572800 | tf_op jit(solution)/shard_map/pallas_call | solution.py:42
  22.3 3.0 %shard_map.88 = (bf16[80,1024]{1,0:T(8,128)(2,1)S(1)}, bf16[80,768]{1,0:T(8,128)(2,1)S(1)}, bf16[80,768]{1,0:T(8,128)(2,1)S(1)}) custom-call(bf16[40,1024]{1,0:T(8,128)(2,1)S(1)} %get-tuple-element.31.refs_0_, bf16[40,1024]{1,0:T(8,128)(2,1)S(1)} %collective-permute-done.refs_1_, bf16[40,1024]{1,0:T(8,128)(2,1)S(1)} %collective-permute-done.1.refs_2_, ...), custom_call_target="tpu_custom_call" | custom-call | flops 251658240 | bytes 3145728 | tf_op jit(solution)/shard_map/pallas_call | solution.py:42
  25.3 0.6 %collective-permute-start.7 = (bf16[80,768]{1,0:T(8,128)(2,1)S(1)}, bf16[80,768]{1,0:T(8,128)(2,1)S(1)}, u32[]{:S(2)}, u32[]{:S(2)}) collective-permute-start(bf16[80,768]{1,0:T(8,128)(2,1)S(1)} %get-tuple-element.43), channel_id=1, source_target_pairs={{0,1},{1,0},{2,3},{3,2},{4,5},{5,4},{6,7},{7,6},{8,9},{9,8},{10,11... | collective-permute-start | bytes 368648 | tf_op jit(solution)/shard_map/ppermute | solution.py:222
  25.9 1.5 %collective-permute-start.9 = (bf16[2,80,768]{2,1,0:T(8,128)(2,1)S(1)}, bf16[2,80,768]{2,1,0:T(8,128)(2,1)S(1)}, u32[]{:S(2)}, u32[]{:S(2)}) collective-permute-start(bf16[2,80,768]{2,1,0:T(8,128)(2,1)S(1)} %get-tuple-element.58.refs_6_), channel_id=1, source_target_pairs={{0,2},{1,3},{2,0},{3,1},{4,6},{5,7},{6,4},{7,5},{8,10},{9,11},{10,... | collective-permute-start | bytes 737288 | tf_op jit(solution)/shard_map/ppermute | solution.py:222
  27.4 1.1 %collective-permute-start.8 = (bf16[80,768]{1,0:T(8,128)(2,1)S(1)}, bf16[80,768]{1,0:T(8,128)(2,1)S(1)}, u32[]{:S(2)}, u32[]{:S(2)}) collective-permute-start(bf16[80,768]{1,0:T(8,128)(2,1)S(1)} %get-tuple-element.59), channel_id=1, source_target_pairs={{0,2},{1,3},{2,0},{3,1},{4,6},{5,7},{6,4},{7,5},{8,10},{9,11},{10,... | collective-permute-start | bytes 368648 | tf_op jit(solution)/shard_map/ppermute | solution.py:222
  28.5 6.2 %collective-permute-done.9.pair_far = bf16[2,80,768]{2,1,0:T(8,128)(2,1)S(1)} collective-permute-done((bf16[2,80,768]{2,1,0:T(8,128)(2,1)S(1)}, bf16[2,80,768]{2,1,0:T(8,128)(2,1)S(1)}, u32[]{:S(2)}, u32[]{:S(2)}) %collective-permute-start.9) | collective-permute-done | bytes 245792 | tf_op jit(solution)/shard_map/ppermute | solution.py:222
  34.8 1.6 %collective-permute-done.8.act_far = bf16[80,768]{1,0:T(8,128)(2,1)S(1)} collective-permute-done((bf16[80,768]{1,0:T(8,128)(2,1)S(1)}, bf16[80,768]{1,0:T(8,128)(2,1)S(1)}, u32[]{:S(2)}, u32[]{:S(2)}) %collective-permute-start.8) | collective-permute-done | bytes 122912 | tf_op jit(solution)/shard_map/ppermute | solution.py:222
  36.6 0.5 collective-permute-start.14
  37.1 0.7 %shard_map.91.total = f32[80,1024]{1,0:T(8,128)S(1)} custom-call(bf16[2,80,768]{2,1,0:T(8,128)(2,1)S(1)} %shard_map.90.mine, bf16[2,768,1024]{2,1,0:T(8,128)(2,1)S(1)} %get-tuple-element.46.held), custom_call_target="tpu_custom_call" | custom-call | flops 251658240 | bytes 3145728 | tf_op jit(solution)/shard_map/pallas_call | solution.py:42
  37.8 0.3 collective-permute-done.10.other
  38.1 0.8 %shard_map.92 = (bf16[40,1024]{1,0:T(8,128)(2,1)S(1)}, bf16[40,1024]{1,0:T(8,128)(2,1)S(1)}, bf16[40,1024]{1,0:T(8,128)(2,1)S(1)}, bf16[40,1024]{1,0:T(8,128)(2,1)S(1)}) custom-call(f32[80,1024]{1,0:T(8,128)S(1)} %shard_map.91.total, bf16[2,80,768]{2,1,0:T(8,128)(2,1)S(1)} %collective-permute-done.10.other, ...), custom_call_target="tpu_custom_call" | custom-call | flops 251658240 | bytes 3145728 | tf_op jit(solution)/shard_map/pallas_call | solution.py:42
  38.9 4.9 %collective-permute-start.11 = (bf16[40,1024]{1,0:T(8,128)(2,1)S(1)}, bf16[40,1024]{1,0:T(8,128)(2,1)S(1)}, u32[]{:S(2)}, u32[]{:S(2)}) collective-permute-start(bf16[40,1024]{1,0:T(8,128)(2,1)S(1)} %get-tuple-element.49), channel_id=1, source_target_pairs={{0,4},{4,0},{8,12},{12,8},{1,5},{5,1},{9,13},{13,9},{2,6},{6,2},{1... | collective-permute-start | bytes 245768 | tf_op jit(solution)/shard_map/ppermute | solution.py:222
  43.9 1.3 %collective-permute-start.12 = (bf16[40,1024]{1,0:T(8,128)(2,1)S(1)}, bf16[40,1024]{1,0:T(8,128)(2,1)S(1)}, u32[]{:S(2)}, u32[]{:S(2)}) collective-permute-start(bf16[40,1024]{1,0:T(8,128)(2,1)S(1)} %get-tuple-element.50), channel_id=1, source_target_pairs={{0,8},{4,12},{8,0},{12,4},{1,9},{5,13},{9,1},{13,5},{2,10},{6,14},... | collective-permute-start | bytes 245768 | tf_op jit(solution)/shard_map/ppermute | solution.py:222
  45.2 1.4 %collective-permute-start.13 = (bf16[40,1024]{1,0:T(8,128)(2,1)S(1)}, bf16[40,1024]{1,0:T(8,128)(2,1)S(1)}, u32[]{:S(2)}, u32[]{:S(2)}) collective-permute-start(bf16[40,1024]{1,0:T(8,128)(2,1)S(1)} %get-tuple-element.51), channel_id=1, source_target_pairs={{0,12},{4,8},{8,4},{12,0},{1,13},{5,9},{9,5},{13,1},{2,14},{6,10},... | collective-permute-start | bytes 245768 | tf_op jit(solution)/shard_map/ppermute | solution.py:222
  46.5 4.1 %shard_map.94 = (bf16[1,2,1536,1024]{3,2,1,0:T(8,128)(2,1)}, bf16[1,1536,1024]{2,1,0:T(8,128)(2,1)}) custom-call(bf16[80,768]{1,0:T(8,128)(2,1)S(1)} %get-tuple-element.52.mine_act, bf16[80,768]{1,0:T(8,128)(2,1)S(1)} %collective-permute-done.14.other_act, bf16[2,80,768]{2,1,0:T(8,128)(2,1)S(1)} %shard_map.90.mine, ...), custom_call_target="tpu_custom_call" | custom-call | flops 754974720 | bytes 9437184 | tf_op jit(solution)/shard_map/pallas_call | solution.py:42
  50.7 2.7 %collective-permute-done.12.refs_2_ = bf16[40,1024]{1,0:T(8,128)(2,1)S(1)} collective-permute-done((bf16[40,1024]{1,0:T(8,128)(2,1)S(1)}, bf16[40,1024]{1,0:T(8,128)(2,1)S(1)}, u32[]{:S(2)}, u32[]{:S(2)}) %collective-permute-start.12) | collective-permute-done | bytes 81952 | tf_op jit(solution)/shard_map/ppermute | solution.py:222
  53.4 1.1 %shard_map.93 = bf16[256,1024]{1,0:T(8,128)(2,1)} custom-call(bf16[160,256]{1,0:T(8,128)(2,1)S(1)} %get-tuple-element.30.pick, bf16[40,1024]{1,0:T(8,128)(2,1)S(1)} %get-tuple-element.48.refs_0_, bf16[40,1024]{1,0:T(8,128)(2,1)S(1)} %collective-permute-done.11.refs_1_, bf16[40,1024]{1,0:T(8,128)(2,1)S(1)} %collective-permute-done.12.refs_2_, ...), custom_call_target="tpu_custom_call" | custom-call | flops 83886080 | bytes 1048576 | tf_op jit(solution)/shard_map/pallas_call | solution.py:42
  (18 shorter events, 0.8 us)
Async XLA Ops:
  2.4 10.1 %collective-permute-start.3 = (bf16[40,1024]{1,0:T(8,128)(2,1)S(1)}, bf16[40,1024]{1,0:T(8,128)(2,1)S(1)}, u32[]{:S(2)}, u32[]{:S(2)}) collective-permute-start(bf16[40,1024]{1,0:T(8,128)(2,1)S(1)} %get-tuple-element.36), channel_id=1, source_target_pairs={{0,4},{4,0},{8,12},{12,8},{1,5},{5,1},{9,13},{13,9},{2,6},{6,2},{1... | collective-permute-start | bytes 245768 | tf_op jit(solution)/shard_map/ppermute | solution.py:222
  5.5 10.3 %collective-permute-start.4 = (bf16[40,1024]{1,0:T(8,128)(2,1)S(1)}, bf16[40,1024]{1,0:T(8,128)(2,1)S(1)}, u32[]{:S(2)}, u32[]{:S(2)}) collective-permute-start(bf16[40,1024]{1,0:T(8,128)(2,1)S(1)} %get-tuple-element.37), channel_id=1, source_target_pairs={{0,8},{4,12},{8,0},{12,4},{1,9},{5,13},{9,1},{13,5},{2,10},{6,14},... | collective-permute-start | bytes 245768 | tf_op jit(solution)/shard_map/ppermute | solution.py:222
  8.1 7.7 %collective-permute-start.5 = (bf16[40,1024]{1,0:T(8,128)(2,1)S(1)}, bf16[40,1024]{1,0:T(8,128)(2,1)S(1)}, u32[]{:S(2)}, u32[]{:S(2)}) collective-permute-start(bf16[40,1024]{1,0:T(8,128)(2,1)S(1)} %get-tuple-element.38), channel_id=1, source_target_pairs={{0,12},{4,8},{8,4},{12,0},{1,13},{5,9},{9,5},{13,1},{2,14},{6,10},... | collective-permute-start | bytes 245768 | tf_op jit(solution)/shard_map/ppermute | solution.py:222
  8.1 14.3 %collective-permute-start = (bf16[40,1024]{1,0:T(8,128)(2,1)S(1)}, bf16[40,1024]{1,0:T(8,128)(2,1)S(1)}, u32[]{:S(2)}, u32[]{:S(2)}) collective-permute-start(bf16[40,1024]{1,0:T(8,128)(2,1)S(1)} %get-tuple-element.32), channel_id=1, source_target_pairs={{0,4},{4,0},{8,12},{12,8},{1,5},{5,1},{9,13},{13,9},{2,6},{6,2},{1... | collective-permute-start | bytes 245768 | tf_op jit(solution)/shard_map/ppermute | solution.py:222
  9.0 13.4 %collective-permute-start.1 = (bf16[40,1024]{1,0:T(8,128)(2,1)S(1)}, bf16[40,1024]{1,0:T(8,128)(2,1)S(1)}, u32[]{:S(2)}, u32[]{:S(2)}) collective-permute-start(bf16[40,1024]{1,0:T(8,128)(2,1)S(1)} %get-tuple-element.33), channel_id=1, source_target_pairs={{0,8},{4,12},{8,0},{12,4},{1,9},{5,13},{9,1},{13,5},{2,10},{6,14},... | collective-permute-start | bytes 245768 | tf_op jit(solution)/shard_map/ppermute | solution.py:222
  12.5 9.9 %collective-permute-start.2 = (bf16[40,1024]{1,0:T(8,128)(2,1)S(1)}, bf16[40,1024]{1,0:T(8,128)(2,1)S(1)}, u32[]{:S(2)}, u32[]{:S(2)}) collective-permute-start(bf16[40,1024]{1,0:T(8,128)(2,1)S(1)} %get-tuple-element.34), channel_id=1, source_target_pairs={{0,12},{4,8},{8,4},{12,0},{1,13},{5,9},{9,5},{13,1},{2,14},{6,10},... | collective-permute-start | bytes 245768 | tf_op jit(solution)/shard_map/ppermute | solution.py:222
  18.9 3.3 %collective-permute-start.6 = (bf16[2,80,768]{2,1,0:T(8,128)(2,1)S(1)}, bf16[2,80,768]{2,1,0:T(8,128)(2,1)S(1)}, u32[]{:S(2)}, u32[]{:S(2)}) collective-permute-start(bf16[2,80,768]{2,1,0:T(8,128)(2,1)S(1)} %get-tuple-element.41), channel_id=1, source_target_pairs={{0,1},{1,0},{2,3},{3,2},{4,5},{5,4},{6,7},{7,6},{8,9},{9,8},{10,11... | collective-permute-start | bytes 737288 | tf_op jit(solution)/shard_map/ppermute | solution.py:222
  25.3 2.1 %collective-permute-start.7 = (bf16[80,768]{1,0:T(8,128)(2,1)S(1)}, bf16[80,768]{1,0:T(8,128)(2,1)S(1)}, u32[]{:S(2)}, u32[]{:S(2)}) collective-permute-start(bf16[80,768]{1,0:T(8,128)(2,1)S(1)} %get-tuple-element.43), channel_id=1, source_target_pairs={{0,1},{1,0},{2,3},{3,2},{4,5},{5,4},{6,7},{7,6},{8,9},{9,8},{10,11... | collective-permute-start | bytes 368648 | tf_op jit(solution)/shard_map/ppermute | solution.py:222
  25.9 8.8 %collective-permute-start.9 = (bf16[2,80,768]{2,1,0:T(8,128)(2,1)S(1)}, bf16[2,80,768]{2,1,0:T(8,128)(2,1)S(1)}, u32[]{:S(2)}, u32[]{:S(2)}) collective-permute-start(bf16[2,80,768]{2,1,0:T(8,128)(2,1)S(1)} %get-tuple-element.58.refs_6_), channel_id=1, source_target_pairs={{0,2},{1,3},{2,0},{3,1},{4,6},{5,7},{6,4},{7,5},{8,10},{9,11},{10,... | collective-permute-start | bytes 737288 | tf_op jit(solution)/shard_map/ppermute | solution.py:222
  27.4 9.0 %collective-permute-start.8 = (bf16[80,768]{1,0:T(8,128)(2,1)S(1)}, bf16[80,768]{1,0:T(8,128)(2,1)S(1)}, u32[]{:S(2)}, u32[]{:S(2)}) collective-permute-start(bf16[80,768]{1,0:T(8,128)(2,1)S(1)} %get-tuple-element.59), channel_id=1, source_target_pairs={{0,2},{1,3},{2,0},{3,1},{4,6},{5,7},{6,4},{7,5},{8,10},{9,11},{10,... | collective-permute-start | bytes 368648 | tf_op jit(solution)/shard_map/ppermute | solution.py:222
  36.5 1.6 %collective-permute-start.10 = (bf16[2,80,768]{2,1,0:T(8,128)(2,1)S(1)}, bf16[2,80,768]{2,1,0:T(8,128)(2,1)S(1)}, u32[]{:S(2)}, u32[]{:S(2)}) collective-permute-start(bf16[2,80,768]{2,1,0:T(8,128)(2,1)S(1)} %shard_map.90.mine), channel_id=1, source_target_pairs={{0,1},{1,0},{2,3},{3,2},{4,5},{5,4},{6,7},{7,6},{8,9},{9,8},{10,11... | collective-permute-start | bytes 737288 | tf_op jit(solution)/shard_map/ppermute | solution.py:222
  36.6 9.9 %collective-permute-start.14 = (bf16[80,768]{1,0:T(8,128)(2,1)S(1)}, bf16[80,768]{1,0:T(8,128)(2,1)S(1)}, u32[]{:S(2)}, u32[]{:S(2)}) collective-permute-start(bf16[80,768]{1,0:T(8,128)(2,1)S(1)} %get-tuple-element.52.mine_act), channel_id=1, source_target_pairs={{0,1},{1,0},{2,3},{3,2},{4,5},{5,4},{6,7},{7,6},{8,9},{9,8},{10,11... | collective-permute-start | bytes 368648 | tf_op jit(solution)/shard_map/ppermute | solution.py:222
  38.9 11.7 %collective-permute-start.11 = (bf16[40,1024]{1,0:T(8,128)(2,1)S(1)}, bf16[40,1024]{1,0:T(8,128)(2,1)S(1)}, u32[]{:S(2)}, u32[]{:S(2)}) collective-permute-start(bf16[40,1024]{1,0:T(8,128)(2,1)S(1)} %get-tuple-element.49), channel_id=1, source_target_pairs={{0,4},{4,0},{8,12},{12,8},{1,5},{5,1},{9,13},{13,9},{2,6},{6,2},{1... | collective-permute-start | bytes 245768 | tf_op jit(solution)/shard_map/ppermute | solution.py:222
  43.9 9.5 %collective-permute-start.12 = (bf16[40,1024]{1,0:T(8,128)(2,1)S(1)}, bf16[40,1024]{1,0:T(8,128)(2,1)S(1)}, u32[]{:S(2)}, u32[]{:S(2)}) collective-permute-start(bf16[40,1024]{1,0:T(8,128)(2,1)S(1)} %get-tuple-element.50), channel_id=1, source_target_pairs={{0,8},{4,12},{8,0},{12,4},{1,9},{5,13},{9,1},{13,5},{2,10},{6,14},... | collective-permute-start | bytes 245768 | tf_op jit(solution)/shard_map/ppermute | solution.py:222
  45.2 8.2 %collective-permute-start.13 = (bf16[40,1024]{1,0:T(8,128)(2,1)S(1)}, bf16[40,1024]{1,0:T(8,128)(2,1)S(1)}, u32[]{:S(2)}, u32[]{:S(2)}) collective-permute-start(bf16[40,1024]{1,0:T(8,128)(2,1)S(1)} %get-tuple-element.51), channel_id=1, source_target_pairs={{0,12},{4,8},{8,4},{12,0},{1,13},{5,9},{9,5},{13,1},{2,14},{6,10},... | collective-permute-start | bytes 245768 | tf_op jit(solution)/shard_map/ppermute | solution.py:222

commit v5 on v4

--- a/solution.py
+++ b/solution.py
@@ -15,6 +15,8 @@
 MIB = 1 << 20
 GATE_COST = 18
 C2COST = 100
+D0COST = 100
+WCOST = 3
 VMEM = pl.BlockSpec(memory_space=pltpu.VMEM)
 ANY = pl.BlockSpec(memory_space=pl.ANY)
 HBM = pl.BlockSpec(memory_space=pltpu.HBM)
@@ -31,10 +33,14 @@
     return lax.broadcasted_iota(jnp.int32, shape, dim)
 
 
-def block_of(position, blocks):
-    found = jnp.zeros_like(position)
-    for k in range(1, blocks):
-        found = found + (position >= k * MOST).astype(jnp.int32)
+def far_first(count):
+    return sorted(range(count), key=lambda k: (-k.bit_length(), k))
+
+
+def block_of(position, names):
+    found = jnp.full_like(position, names[0])
+    for at in range(1, len(names)):
+        found = found + (position >= at * MOST).astype(jnp.int32) * (names[at] - names[at - 1])
     return found
 
 
@@ -63,7 +69,8 @@
     me = lax.axis_index("ex")
     tokens = inputs.shape[0]
     rows = experts * MOST
-    owner = block_of(iota((rows, routes.shape[0]), 0), experts)
+    order = far_first(experts)
+    owner = block_of(iota((rows, routes.shape[0]), 0), order)
     named = jnp.zeros((rows, tokens), F32)
     weight = jnp.zeros((rows, tokens), F32)
     loads[0].wait()
@@ -78,7 +85,7 @@
     earlier = iota((tokens, tokens), 0) < iota((tokens, tokens), 1)
     rank = mm(named.astype(BF), jnp.where(earlier, 1.0, 0.0).astype(BF)).astype(jnp.int32)
     row = iota((rows, tokens), 0)
-    slot = row - block_of(row, experts) * MOST
+    slot = row - block_of(row, range(experts)) * MOST
     picks = (rank == slot) & (named > 0.5)
     pick = jnp.where(picks, 1.0, 0.0)
     prob = jnp.sum(jnp.where(picks, weight, 0.0), axis=1, keepdims=True)
@@ -112,8 +119,8 @@
     key = []
     for dim in (0, 1):
         row = iota((rows, rows), dim)
-        block = block_of(row, experts)
-        key.append((me ^ block) * MOST + row - block * MOST)
+        local_row = row - block_of(row, range(experts)) * MOST
+        key.append((me ^ block_of(row, far_first(experts))) * MOST + local_row)
     earlier = jnp.where(key[1] < key[0], 1.0, 0.0).astype(BF)
     wide = jnp.broadcast_to(full, (rows, capacity))
     slot = mm(earlier, jnp.where(wide, 1.0, 0.0).astype(BF)).astype(jnp.int32)
@@ -121,43 +128,44 @@
     return place, mm(place, got.astype(BF), ROWS).astype(BF)
 
 
-def gate_up_parts(experts, capacity, own, *refs):
+def stage(gate_up, down, _, *refs):
+    (*held, sems) = refs
+    half = down.shape[1] // 2
+    loads = []
+    for own, out in enumerate(held):
+        rows = rows_of(half, own == 1)
+        for matrix in range(3):
+            source = down.at[0, rows] if matrix == 2 else gate_up.at[0, matrix, rows]
+            loads.append(pltpu.make_async_copy(source, out.at[matrix], sems.at[len(loads)]))
+            loads[-1].start()
+    for load in loads:
+        load.wait()
+
+
+def gate_up_parts(experts, capacity, *refs):
     pieces = refs[:experts]
-    weight, held, out, *extra, sems = refs[experts:]
-    half = weight.shape[2] // 2
-    loads = []
-    for matrix in range(2):
-        source = weight.at[0, matrix, rows_of(half, own)]
-        loads.append(pltpu.make_async_copy(source, held.at[matrix], sems.at[matrix]))
-        loads[matrix].start()
+    held, out, *extra = refs[experts:]
     place, rows_in = place_rows(experts, capacity, pieces)
     if extra:
         extra[0][...] = place
         extra[1][...] = rows_in
     for matrix in range(2):
-        loads[matrix].wait()
         out[matrix] = mm(rows_in, held[matrix], LANES).astype(BF)
 
 
-def act_parts(experts, *refs):
-    pieces = refs[:experts]
-    place, weight, _, rows_out, other, mine, held, sems = refs[experts:]
-    half = weight.shape[1] // 2
-    loads = []
-    for own in range(2):
-        source = weight.at[0, rows_of(half, own == 1)]
-        loads.append(pltpu.make_async_copy(source, held.at[own], sems.at[own]))
-        loads[own].start()
-    rows_grad = mm(place[...], stacked(pieces).astype(BF), ROWS).astype(BF)
-    rows_out[...] = rows_grad
-    for own, out in enumerate((other, mine)):
-        loads[own].wait()
-        out[...] = mm(rows_grad, held[own], LANES).astype(BF)
-
-
-def gates(pair, pair_far, act_out, by_gate, by_up):
-    gate_sum = pair[0] + pair_far[0].astype(F32)
-    up_sum = pair[1] + pair_far[1].astype(F32)
+def place_grads(experts, *refs):
+    place, rows_out = refs[experts:]
+    rows_out[...] = mm(place[...], stacked(refs[:experts]).astype(BF), ROWS).astype(BF)
+
+
+def act_parts(rows_grad, held_other, held_mine, _, other, mine):
+    other[...] = mm(rows_grad[...], held_other[2], LANES).astype(BF)
+    mine[...] = mm(rows_grad[...], held_mine[2], LANES).astype(BF)
+
+
+def gates(gate, gate_far, up, up_far, act_out, by_gate, by_up):
+    gate_sum = gate[...] + gate_far[...].astype(F32)
+    up_sum = up[...] + up_far[...].astype(F32)
     sigmoid_gate = jax.nn.sigmoid(gate_sum)
     silu_gate = gate_sum * sigmoid_gate
     act_out[...] = (silu_gate * up_sum).astype(BF)
@@ -223,10 +231,8 @@
 
 
 def exchange(pieces, axis):
-    got = list(pieces)
-    for k in list(range(2, len(pieces))) + [1]:
-        got[k] = swap(pieces[k], axis, k)
-    return got
+    order = far_first(len(pieces))
+    return [swap(piece, axis, k) if k else piece for piece, k in zip(pieces, order)]
 
 
 def local(inputs, grad_output, routes, gate_probs, gate_up, down_proj):
@@ -259,46 +265,62 @@
     )
     got_in = exchange(sent[:experts], "ex")
     got_grad = exchange(sent[experts:], "ex")
-    def pair_part(own, extra, cost):
+    held_other, held_mine = call(
+        stage,
+        [pltpu.VMEM((3, half, width), BF)] * 2,
+        (far(gate_up), far(down_proj), pick),
+        [HBM, HBM, ANY],
+        [dma(6)],
+        flops=WCOST * weight_flops,
+        traffic=WCOST * weight_bytes,
+    )
+
+    def pair_part(held, extra, cost):
         return call(
-            functools.partial(gate_up_parts, experts, capacity, own),
-            [pltpu.VMEM((2, half, width), BF), sds((2, capacity, half), BF)] + extra,
-            (*got_in, far(gate_up)),
-            [VMEM] * experts + [HBM],
-            [dma(2)],
+            functools.partial(gate_up_parts, experts, capacity),
+            [sds((2, capacity, half), BF)] + extra,
+            (*got_in, held),
+            [VMEM] * (experts + 1),
             flops=cost * weight_flops,
             traffic=cost * weight_bytes,
         )
 
-    held_other, pair_other = pair_part(False, [], 1)
-    held_mine, pair_mine, place, rows_in = pair_part(
-        True, [sds((rows, capacity), BF), sds((capacity, width), BF)], C2COST
-    )
-    def total(mine, other):
-        held = mine.astype(F32) + other.astype(F32)
+    (pair_other,) = pair_part(held_other, [], 1)
+    pair_mine, place, rows_in = pair_part(
+        held_mine, [sds((rows, capacity), BF), sds((capacity, width), BF)], C2COST
+    )
+    def total(held):
         bit = 2
         while bit * 2 < ways:
             held = held + swap(held.astype(BF), "ey", bit).astype(F32)
             bit *= 2
-        sent = held.astype(BF)
-        return held, sent, swap(sent, "ey", bit)
-
-    pair, pair_sent, pair_far = total(pair_mine, swap(pair_other, "ey", 1))
-    rows_grad, act_other, act_mine = call(
-        functools.partial(act_parts, experts),
-        [sds((capacity, width), BF), sds((capacity, half), BF), sds((capacity, half), BF)],
-        (*got_grad, place, far(down_proj), pair_sent),
-        [VMEM] * (experts + 1) + [HBM, ANY],
-        [pltpu.VMEM((2, half, width), BF), dma(2)],
+        return held, swap(held.astype(BF), "ey", bit)
+
+    pair = pair_mine.astype(F32) + swap(pair_other, "ey", 1).astype(F32)
+    gate, gate_far = total(pair[0])
+    up, up_far = total(pair[1])
+    rows_grad = call(
+        functools.partial(place_grads, experts),
+        sds((capacity, width), BF),
+        (*got_grad, place),
+        [VMEM] * (experts + 1),
+        flops=D0COST * weight_flops,
+        traffic=D0COST * weight_bytes,
+    )
+    act_other, act_mine = call(
+        act_parts,
+        [sds((capacity, half), BF)] * 2,
+        (rows_grad, held_other, held_mine, gate_far),
+        [VMEM] * 3 + [ANY],
         flops=weight_flops,
         traffic=weight_bytes,
     )
-    act, _, act_far = total(act_mine, swap(act_other, "ey", 1))
+    act, act_far = total(act_mine.astype(F32) + swap(act_other, "ey", 1).astype(F32))
     mine_act, by_gate, by_up = call(
         gates,
         [sds((capacity, half), BF)] + [sds((capacity, half), F32)] * 2,
-        (pair, pair_far),
-        [VMEM] * 2,
+        (gate, gate_far, up, up_far),
+        [VMEM] * 4,
         traffic=GATE_COST * capacity * half,
     )
     other_act = swap(mine_act, "ey", 1)

time: 54.7 us -> 50.5 us (0.923)
  starting transfers between devices: 21.7 us -> 20.2 us
  Pallas kernels: 18.1 us -> 16.7 us
  waiting for transfers between devices: 13.8 us -> 12.5 us
    ppermute x15 -> x16, starting transfers between devices: 21.7 us -> 20.2 us  [swap(): return lax.ppermute(value, axis, [(i, i ^ bit) for i in range(count)])]
    pallas_call x10 -> x12, Pallas kernels: 18.1 us -> 16.7 us  [call(): pl.pallas_call(body, out_shape=outs, in_specs=specs, out_specs=out_specs...]
    ppermute x15 -> x16, waiting for transfers between devices: 13.8 us -> 12.5 us  [swap(): return lax.ppermute(value, axis, [(i, i ^ bit) for i in range(count)])]
  transfers between devices with their start and end apart: 15 -> 16, of which waited for: 5 -> 9; matrix products, arithmetic and copies ran while one was open for 0% -> 0% of each run, Pallas kernels for 22% -> 25%
where the time goes in v5:
time: 50.5 us; the launch traced here: 50.3 us
  starting transfers between devices  20.2 us (40%)
  Pallas kernels  16.7 us (33%)
  waiting for transfers between devices  12.5 us (25%)
  between operations  0.75 us (1%)
    ppermute x16, starting transfers between devices, swap(): return lax.ppermute(value, axis, [(i, i ^ bit) for i in range(count)])  20.2 us
    pallas_call x12, Pallas kernels, call(): pl.pallas_call(body, out_shape=outs, in_specs=specs, out_specs=out_specs...  16.7 us
    ppermute x16, waiting for transfers between devices, swap(): return lax.ppermute(value, axis, [(i, i ^ bit) for i in range(count)])  12.5 us
  transfers between devices with their start and end apart: 16, of which 9 were waited for; matrix products, arithmetic and copies ran while one was open for 0% of the time, Pallas kernels for 25%

profile of v5, /device:TPU:0, one launch (start us, length us, event | category | flops | bytes accessed | tf_op | source)
XLA Modules:
  0.0 50.3 jit_solution(2938523879545993667)
XLA Ops:
  0.6 1.7 %shard_map.85 = (bf16[160,256]{1,0:T(8,128)(2,1)S(1)}, bf16[40,1024]{1,0:T(8,128)(2,1)S(1)}, bf16[40,1024]{1,0:T(8,128)(2,1)S(1)}, bf16[40,1024]{1,0:T(8,128)(2,...) custom-call(s32[8,256]{1,0:T(8,128)} %bitcast.10, ...), custom_call_target="tpu_custom_call" | custom-call | flops 167772160 | bytes 1048576 | tf_op jit(solution)/shard_map/pallas_call | solution.py:48
  2.4 4.1 %collective-permute-start.3 = (bf16[40,1024]{1,0:T(8,128)(2,1)S(1)}, bf16[40,1024]{1,0:T(8,128)(2,1)S(1)}, u32[]{:S(2)}, u32[]{:S(2)}) collective-permute-start(bf16[40,1024]{1,0:T(8,128)(2,1)S(1)} %get-tuple-element.33), channel_id=1, source_target_pairs={{0,8},{4,12},{8,0},{12,4},{1,9},{5,13},{9,1},{13,5},{2,10},{6,14},... | collective-permute-start | bytes 245768 | tf_op jit(solution)/shard_map/ppermute | solution.py:230
  6.5 1.3 %collective-permute-start.4 = (bf16[40,1024]{1,0:T(8,128)(2,1)S(1)}, bf16[40,1024]{1,0:T(8,128)(2,1)S(1)}, u32[]{:S(2)}, u32[]{:S(2)}) collective-permute-start(bf16[40,1024]{1,0:T(8,128)(2,1)S(1)} %get-tuple-element.34), channel_id=1, source_target_pairs={{0,12},{4,8},{8,4},{12,0},{1,13},{5,9},{9,5},{13,1},{2,14},{6,10},... | collective-permute-start | bytes 245768 | tf_op jit(solution)/shard_map/ppermute | solution.py:230
  8.1 2.8 %collective-permute-start = (bf16[40,1024]{1,0:T(8,128)(2,1)S(1)}, bf16[40,1024]{1,0:T(8,128)(2,1)S(1)}, u32[]{:S(2)}, u32[]{:S(2)}) collective-permute-start(bf16[40,1024]{1,0:T(8,128)(2,1)S(1)} %get-tuple-element.29), channel_id=1, source_target_pairs={{0,8},{4,12},{8,0},{12,4},{1,9},{5,13},{9,1},{13,5},{2,10},{6,14},... | collective-permute-start | bytes 245768 | tf_op jit(solution)/shard_map/ppermute | solution.py:230
  10.9 1.3 %collective-permute-start.1 = (bf16[40,1024]{1,0:T(8,128)(2,1)S(1)}, bf16[40,1024]{1,0:T(8,128)(2,1)S(1)}, u32[]{:S(2)}, u32[]{:S(2)}) collective-permute-start(bf16[40,1024]{1,0:T(8,128)(2,1)S(1)} %get-tuple-element.30), channel_id=1, source_target_pairs={{0,12},{4,8},{8,4},{12,0},{1,13},{5,9},{9,5},{13,1},{2,14},{6,10},... | collective-permute-start | bytes 245768 | tf_op jit(solution)/shard_map/ppermute | solution.py:230
  12.2 3.8 %shard_map.86 = (bf16[3,768,1024]{2,1,0:T(8,128)(2,1)S(1)}, bf16[3,768,1024]{2,1,0:T(8,128)(2,1)S(1)}) custom-call(bf16[1,2,1536,1024]{3,2,1,0:T(8,128)(2,1)} %gate_up.1, bf16[1,1536,1024]{2,1,0:T(8,128)(2,1)} %down.1, bf16[160,256]{1,0:T(8,128)(2,1)S(1)} %get-tuple-element.28._.pick), custom_call_target="tpu_custom_call" | custom-call | flops 754974720 | bytes 9437184 | tf_op jit(solution)/shard_map/pallas_call | solution.py:48
  16.1 1.4 %shard_map.89 = bf16[2,80,768]{2,1,0:T(8,128)(2,1)S(1)} custom-call(bf16[40,1024]{1,0:T(8,128)(2,1)S(1)} %collective-permute-done.3.refs_0_, bf16[40,1024]{1,0:T(8,128)(2,1)S(1)} %collective-permute-done.4.refs_1_, bf16[40,1024]{1,0:T(8,128)(2,1)S(1)} %collective-permute-done.5.refs_2_, bf16[40,1024]{1,0:T(8,128)(2,1)S(1)} %get-tuple-element.36.refs_3_, ...), custom_call_target="tpu_custom_call" | custom-call | flops 251658240 | bytes 3145728 | tf_op jit(solution)/shard_map/pallas_call | solution.py:48
  17.6 1.4 %shard_map.87 = (bf16[2,80,768]{2,1,0:T(8,128)(2,1)S(1)}, bf16[160,80]{1,0:T(8,128)(2,1)S(1)}, bf16[80,1024]{1,0:T(8,128)(2,1)S(1)}) custom-call(bf16[40,1024]{1,0:T(8,128)(2,1)S(1)} %collective-permute-done.3.refs_0_, bf16[40,1024]{1,0:T(8,128)(2,1)S(1)} %collective-permute-done.4.refs_1_, bf16[40,1024]{1,0:T(8,128)(2,1)S(1)} %collective-permute-done.5.refs_2_, ...), custom_call_target="tpu_custom_call" | custom-call | flops 25165824000 | bytes 314572800 | tf_op jit(solution)/shard_map/pallas_call | solution.py:48
  19.2 1.6 %collective-permute-start.7 = (bf16[80,768]{1,0:T(8,128)(2,1)S(1)}, bf16[80,768]{1,0:T(8,128)(2,1)S(1)}, u32[]{:S(2)}, u32[]{:S(2)}) collective-permute-start(bf16[80,768]{1,0:T(8,128)(2,1)S(1)} %get-tuple-element.54), channel_id=1, source_target_pairs={{0,2},{1,3},{2,0},{3,1},{4,6},{5,7},{6,4},{7,5},{8,10},{9,11},{10,... | collective-permute-start | bytes 368648 | tf_op jit(solution)/shard_map/ppermute | solution.py:230
  21.1 3.8 %collective-permute-done.7._.gate_far = bf16[80,768]{1,0:T(8,128)(2,1)S(1)} collective-permute-done((bf16[80,768]{1,0:T(8,128)(2,1)S(1)}, bf16[80,768]{1,0:T(8,128)(2,1)S(1)}, u32[]{:S(2)}, u32[]{:S(2)}) %collective-permute-start.7) | collective-permute-done | bytes 122912 | tf_op jit(solution)/shard_map/ppermute | solution.py:230
  25.0 1.1 %shard_map.90 = (bf16[80,768]{1,0:T(8,128)(2,1)S(1)}, bf16[80,768]{1,0:T(8,128)(2,1)S(1)}) custom-call(bf16[80,1024]{1,0:T(8,128)(2,1)S(1)} %shard_map.88.rows_grad, bf16[3,768,1024]{2,1,0:T(8,128)(2,1)S(1)} %get-tuple-element.39.refs_4_.held_other.held, bf16[3,768,1024]{2,1,0:T(8,128)(2,1)S(1)} %get-tuple-element.37.refs_4_.held_mine.held, ...), custom_call_target="tpu_custom_call" | custom-call | flops 251658240 | bytes 3145728 | tf_op jit(solution)/shard_map/pallas_call | solution.py:48
  26.1 1.6 %collective-permute-start.10 = (bf16[80,768]{1,0:T(8,128)(2,1)S(1)}, bf16[80,768]{1,0:T(8,128)(2,1)S(1)}, u32[]{:S(2)}, u32[]{:S(2)}) collective-permute-start(bf16[80,768]{1,0:T(8,128)(2,1)S(1)} %get-tuple-element.53), channel_id=1, source_target_pairs={{0,2},{1,3},{2,0},{3,1},{4,6},{5,7},{6,4},{7,5},{8,10},{9,11},{10,... | collective-permute-start | bytes 368648 | tf_op jit(solution)/shard_map/ppermute | solution.py:230
  27.7 1.3 %collective-permute-start.9 = (bf16[80,768]{1,0:T(8,128)(2,1)S(1)}, bf16[80,768]{1,0:T(8,128)(2,1)S(1)}, u32[]{:S(2)}, u32[]{:S(2)}) collective-permute-start(bf16[80,768]{1,0:T(8,128)(2,1)S(1)} %get-tuple-element.57), channel_id=1, source_target_pairs={{0,2},{1,3},{2,0},{3,1},{4,6},{5,7},{6,4},{7,5},{8,10},{9,11},{10,... | collective-permute-start | bytes 368648 | tf_op jit(solution)/shard_map/ppermute | solution.py:230
  29.1 3.2 %collective-permute-done.10.up_far = bf16[80,768]{1,0:T(8,128)(2,1)S(1)} collective-permute-done((bf16[80,768]{1,0:T(8,128)(2,1)S(1)}, bf16[80,768]{1,0:T(8,128)(2,1)S(1)}, u32[]{:S(2)}, u32[]{:S(2)}) %collective-permute-start.10) | collective-permute-done | bytes 122912 | tf_op jit(solution)/shard_map/ppermute | solution.py:230
  32.5 2.0 %collective-permute-done.9.act_far = bf16[80,768]{1,0:T(8,128)(2,1)S(1)} collective-permute-done((bf16[80,768]{1,0:T(8,128)(2,1)S(1)}, bf16[80,768]{1,0:T(8,128)(2,1)S(1)}, u32[]{:S(2)}, u32[]{:S(2)}) %collective-permute-start.9) | collective-permute-done | bytes 122912 | tf_op jit(solution)/shard_map/ppermute | solution.py:230
  35.1 0.7 %shard_map.93.total = f32[80,1024]{1,0:T(8,128)S(1)} custom-call(bf16[2,80,768]{2,1,0:T(8,128)(2,1)S(1)} %shard_map.92.mine, bf16[3,768,1024]{2,1,0:T(8,128)(2,1)S(1)} %get-tuple-element.37.refs_4_.held_mine.held), custom_call_target="tpu_custom_call" | custom-call | flops 251658240 | bytes 3145728 | tf_op jit(solution)/shard_map/pallas_call | solution.py:48
  36.1 0.9 %shard_map.94 = (bf16[40,1024]{1,0:T(8,128)(2,1)S(1)}, bf16[40,1024]{1,0:T(8,128)(2,1)S(1)}, bf16[40,1024]{1,0:T(8,128)(2,1)S(1)}, bf16[40,1024]{1,0:T(8,128)(2,1)S(1)}) custom-call(f32[80,1024]{1,0:T(8,128)S(1)} %shard_map.93.total, bf16[2,80,768]{2,1,0:T(8,128)(2,1)S(1)} %collective-permute-done.11.other, ...), custom_call_target="tpu_custom_call" | custom-call | flops 251658240 | bytes 3145728 | tf_op jit(solution)/shard_map/pallas_call | solution.py:48
  37.0 4.6 %collective-permute-start.12 = (bf16[40,1024]{1,0:T(8,128)(2,1)S(1)}, bf16[40,1024]{1,0:T(8,128)(2,1)S(1)}, u32[]{:S(2)}, u32[]{:S(2)}) collective-permute-start(bf16[40,1024]{1,0:T(8,128)(2,1)S(1)} %get-tuple-element.45), channel_id=1, source_target_pairs={{0,8},{4,12},{8,0},{12,4},{1,9},{5,13},{9,1},{13,5},{2,10},{6,14},... | collective-permute-start | bytes 245768 | tf_op jit(solution)/shard_map/ppermute | solution.py:230
  41.6 0.6 %collective-permute-start.13 = (bf16[40,1024]{1,0:T(8,128)(2,1)S(1)}, bf16[40,1024]{1,0:T(8,128)(2,1)S(1)}, u32[]{:S(2)}, u32[]{:S(2)}) collective-permute-start(bf16[40,1024]{1,0:T(8,128)(2,1)S(1)} %get-tuple-element.46), channel_id=1, source_target_pairs={{0,12},{4,8},{8,4},{12,0},{1,13},{5,9},{9,5},{13,1},{2,14},{6,10},... | collective-permute-start | bytes 245768 | tf_op jit(solution)/shard_map/ppermute | solution.py:230
  42.2 4.1 %shard_map.96 = (bf16[1,2,1536,1024]{3,2,1,0:T(8,128)(2,1)}, bf16[1,1536,1024]{2,1,0:T(8,128)(2,1)}) custom-call(bf16[80,768]{1,0:T(8,128)(2,1)S(1)} %get-tuple-element.49.mine_act, bf16[80,768]{1,0:T(8,128)(2,1)S(1)} %collective-permute-done.15.other_act, bf16[2,80,768]{2,1,0:T(8,128)(2,1)S(1)} %shard_map.92.mine, ...), custom_call_target="tpu_custom_call" | custom-call | flops 754974720 | bytes 9437184 | tf_op jit(solution)/shard_map/pallas_call | solution.py:48
  46.3 1.3 %collective-permute-done.12.refs_0_ = bf16[40,1024]{1,0:T(8,128)(2,1)S(1)} collective-permute-done((bf16[40,1024]{1,0:T(8,128)(2,1)S(1)}, bf16[40,1024]{1,0:T(8,128)(2,1)S(1)}, u32[]{:S(2)}, u32[]{:S(2)}) %collective-permute-start.12) | collective-permute-done | bytes 81952 | tf_op jit(solution)/shard_map/ppermute | solution.py:230
  47.7 0.8 %collective-permute-done.13.refs_1_ = bf16[40,1024]{1,0:T(8,128)(2,1)S(1)} collective-permute-done((bf16[40,1024]{1,0:T(8,128)(2,1)S(1)}, bf16[40,1024]{1,0:T(8,128)(2,1)S(1)}, u32[]{:S(2)}, u32[]{:S(2)}) %collective-permute-start.13) | collective-permute-done | bytes 81952 | tf_op jit(solution)/shard_map/ppermute | solution.py:230
  48.5 0.7 %collective-permute-done.14.refs_2_ = bf16[40,1024]{1,0:T(8,128)(2,1)S(1)} collective-permute-done((bf16[40,1024]{1,0:T(8,128)(2,1)S(1)}, bf16[40,1024]{1,0:T(8,128)(2,1)S(1)}, u32[]{:S(2)}, u32[]{:S(2)}) %collective-permute-start.14) | collective-permute-done | bytes 81952 | tf_op jit(solution)/shard_map/ppermute | solution.py:230
  49.2 1.1 %shard_map.95 = bf16[256,1024]{1,0:T(8,128)(2,1)} custom-call(bf16[160,256]{1,0:T(8,128)(2,1)S(1)} %get-tuple-element.28._.pick, bf16[40,1024]{1,0:T(8,128)(2,1)S(1)} %collective-permute-done.12.refs_0_, bf16[40,1024]{1,0:T(8,128)(2,1)S(1)} %collective-permute-done.13.refs_1_, bf16[40,1024]{1,0:T(8,128)(2,1)S(1)} %collective-permute-done.14.refs_2_, ...), custom_call_target="tpu_custom_call" | custom-call | flops 83886080 | bytes 1048576 | tf_op jit(solution)/shard_map/pallas_call | solution.py:48
  (24 shorter events, 2.2 us)
Async XLA Ops:
  2.4 13.6 %collective-permute-start.3 = (bf16[40,1024]{1,0:T(8,128)(2,1)S(1)}, bf16[40,1024]{1,0:T(8,128)(2,1)S(1)}, u32[]{:S(2)}, u32[]{:S(2)}) collective-permute-start(bf16[40,1024]{1,0:T(8,128)(2,1)S(1)} %get-tuple-element.33), channel_id=1, source_target_pairs={{0,8},{4,12},{8,0},{12,4},{1,9},{5,13},{9,1},{13,5},{2,10},{6,14},... | collective-permute-start | bytes 245768 | tf_op jit(solution)/shard_map/ppermute | solution.py:230
  6.5 9.6 %collective-permute-start.4 = (bf16[40,1024]{1,0:T(8,128)(2,1)S(1)}, bf16[40,1024]{1,0:T(8,128)(2,1)S(1)}, u32[]{:S(2)}, u32[]{:S(2)}) collective-permute-start(bf16[40,1024]{1,0:T(8,128)(2,1)S(1)} %get-tuple-element.34), channel_id=1, source_target_pairs={{0,12},{4,8},{8,4},{12,0},{1,13},{5,9},{9,5},{13,1},{2,14},{6,10},... | collective-permute-start | bytes 245768 | tf_op jit(solution)/shard_map/ppermute | solution.py:230
  7.8 8.3 %collective-permute-start.5 = (bf16[40,1024]{1,0:T(8,128)(2,1)S(1)}, bf16[40,1024]{1,0:T(8,128)(2,1)S(1)}, u32[]{:S(2)}, u32[]{:S(2)}) collective-permute-start(bf16[40,1024]{1,0:T(8,128)(2,1)S(1)} %get-tuple-element.35), channel_id=1, source_target_pairs={{0,4},{4,0},{8,12},{12,8},{1,5},{5,1},{9,13},{13,9},{2,6},{6,2},{1... | collective-permute-start | bytes 245768 | tf_op jit(solution)/shard_map/ppermute | solution.py:230
  8.1 12.7 %collective-permute-start = (bf16[40,1024]{1,0:T(8,128)(2,1)S(1)}, bf16[40,1024]{1,0:T(8,128)(2,1)S(1)}, u32[]{:S(2)}, u32[]{:S(2)}) collective-permute-start(bf16[40,1024]{1,0:T(8,128)(2,1)S(1)} %get-tuple-element.29), channel_id=1, source_target_pairs={{0,8},{4,12},{8,0},{12,4},{1,9},{5,13},{9,1},{13,5},{2,10},{6,14},... | collective-permute-start | bytes 245768 | tf_op jit(solution)/shard_map/ppermute | solution.py:230
  10.9 9.9 %collective-permute-start.1 = (bf16[40,1024]{1,0:T(8,128)(2,1)S(1)}, bf16[40,1024]{1,0:T(8,128)(2,1)S(1)}, u32[]{:S(2)}, u32[]{:S(2)}) collective-permute-start(bf16[40,1024]{1,0:T(8,128)(2,1)S(1)} %get-tuple-element.30), channel_id=1, source_target_pairs={{0,12},{4,8},{8,4},{12,0},{1,13},{5,9},{9,5},{13,1},{2,14},{6,10},... | collective-permute-start | bytes 245768 | tf_op jit(solution)/shard_map/ppermute | solution.py:230
  16.0 4.9 %collective-permute-start.2 = (bf16[40,1024]{1,0:T(8,128)(2,1)S(1)}, bf16[40,1024]{1,0:T(8,128)(2,1)S(1)}, u32[]{:S(2)}, u32[]{:S(2)}) collective-permute-start(bf16[40,1024]{1,0:T(8,128)(2,1)S(1)} %get-tuple-element.31), channel_id=1, source_target_pairs={{0,4},{4,0},{8,12},{12,8},{1,5},{5,1},{9,13},{13,9},{2,6},{6,2},{1... | collective-permute-start | bytes 245768 | tf_op jit(solution)/shard_map/ppermute | solution.py:230
  17.6 1.6 %collective-permute-start.6 = (bf16[2,80,768]{2,1,0:T(8,128)(2,1)S(1)}, bf16[2,80,768]{2,1,0:T(8,128)(2,1)S(1)}, u32[]{:S(2)}, u32[]{:S(2)}) collective-permute-start(bf16[2,80,768]{2,1,0:T(8,128)(2,1)S(1)} %shard_map.89), channel_id=1, source_target_pairs={{0,1},{1,0},{2,3},{3,2},{4,5},{5,4},{6,7},{7,6},{8,9},{9,8},{10,11... | collective-permute-start | bytes 737288 | tf_op jit(solution)/shard_map/ppermute | solution.py:230
  19.2 5.7 %collective-permute-start.7 = (bf16[80,768]{1,0:T(8,128)(2,1)S(1)}, bf16[80,768]{1,0:T(8,128)(2,1)S(1)}, u32[]{:S(2)}, u32[]{:S(2)}) collective-permute-start(bf16[80,768]{1,0:T(8,128)(2,1)S(1)} %get-tuple-element.54), channel_id=1, source_target_pairs={{0,2},{1,3},{2,0},{3,1},{4,6},{5,7},{6,4},{7,5},{8,10},{9,11},{10,... | collective-permute-start | bytes 368648 | tf_op jit(solution)/shard_map/ppermute | solution.py:230
  26.1 1.6 %collective-permute-start.8 = (bf16[80,768]{1,0:T(8,128)(2,1)S(1)}, bf16[80,768]{1,0:T(8,128)(2,1)S(1)}, u32[]{:S(2)}, u32[]{:S(2)}) collective-permute-start(bf16[80,768]{1,0:T(8,128)(2,1)S(1)} %get-tuple-element.42), channel_id=1, source_target_pairs={{0,1},{1,0},{2,3},{3,2},{4,5},{5,4},{6,7},{7,6},{8,9},{9,8},{10,11... | collective-permute-start | bytes 368648 | tf_op jit(solution)/shard_map/ppermute | solution.py:230
  26.1 6.2 %collective-permute-start.10 = (bf16[80,768]{1,0:T(8,128)(2,1)S(1)}, bf16[80,768]{1,0:T(8,128)(2,1)S(1)}, u32[]{:S(2)}, u32[]{:S(2)}) collective-permute-start(bf16[80,768]{1,0:T(8,128)(2,1)S(1)} %get-tuple-element.53), channel_id=1, source_target_pairs={{0,2},{1,3},{2,0},{3,1},{4,6},{5,7},{6,4},{7,5},{8,10},{9,11},{10,... | collective-permute-start | bytes 368648 | tf_op jit(solution)/shard_map/ppermute | solution.py:230
  27.7 6.8 %collective-permute-start.9 = (bf16[80,768]{1,0:T(8,128)(2,1)S(1)}, bf16[80,768]{1,0:T(8,128)(2,1)S(1)}, u32[]{:S(2)}, u32[]{:S(2)}) collective-permute-start(bf16[80,768]{1,0:T(8,128)(2,1)S(1)} %get-tuple-element.57), channel_id=1, source_target_pairs={{0,2},{1,3},{2,0},{3,1},{4,6},{5,7},{6,4},{7,5},{8,10},{9,11},{10,... | collective-permute-start | bytes 368648 | tf_op jit(solution)/shard_map/ppermute | solution.py:230
  34.6 1.6 %collective-permute-start.11 = (bf16[2,80,768]{2,1,0:T(8,128)(2,1)S(1)}, bf16[2,80,768]{2,1,0:T(8,128)(2,1)S(1)}, u32[]{:S(2)}, u32[]{:S(2)}) collective-permute-start(bf16[2,80,768]{2,1,0:T(8,128)(2,1)S(1)} %shard_map.92.mine), channel_id=1, source_target_pairs={{0,1},{1,0},{2,3},{3,2},{4,5},{5,4},{6,7},{7,6},{8,9},{9,8},{10,11... | collective-permute-start | bytes 737288 | tf_op jit(solution)/shard_map/ppermute | solution.py:230
  34.6 7.6 %collective-permute-start.15 = (bf16[80,768]{1,0:T(8,128)(2,1)S(1)}, bf16[80,768]{1,0:T(8,128)(2,1)S(1)}, u32[]{:S(2)}, u32[]{:S(2)}) collective-permute-start(bf16[80,768]{1,0:T(8,128)(2,1)S(1)} %get-tuple-element.49.mine_act), channel_id=1, source_target_pairs={{0,1},{1,0},{2,3},{3,2},{4,5},{5,4},{6,7},{7,6},{8,9},{9,8},{10,11... | collective-permute-start | bytes 368648 | tf_op jit(solution)/shard_map/ppermute | solution.py:230
  37.0 10.7 %collective-permute-start.12 = (bf16[40,1024]{1,0:T(8,128)(2,1)S(1)}, bf16[40,1024]{1,0:T(8,128)(2,1)S(1)}, u32[]{:S(2)}, u32[]{:S(2)}) collective-permute-start(bf16[40,1024]{1,0:T(8,128)(2,1)S(1)} %get-tuple-element.45), channel_id=1, source_target_pairs={{0,8},{4,12},{8,0},{12,4},{1,9},{5,13},{9,1},{13,5},{2,10},{6,14},... | collective-permute-start | bytes 245768 | tf_op jit(solution)/shard_map/ppermute | solution.py:230
  41.6 6.9 %collective-permute-start.13 = (bf16[40,1024]{1,0:T(8,128)(2,1)S(1)}, bf16[40,1024]{1,0:T(8,128)(2,1)S(1)}, u32[]{:S(2)}, u32[]{:S(2)}) collective-permute-start(bf16[40,1024]{1,0:T(8,128)(2,1)S(1)} %get-tuple-element.46), channel_id=1, source_target_pairs={{0,12},{4,8},{8,4},{12,0},{1,13},{5,9},{9,5},{13,1},{2,14},{6,10},... | collective-permute-start | bytes 245768 | tf_op jit(solution)/shard_map/ppermute | solution.py:230
  42.1 7.0 %collective-permute-start.14 = (bf16[40,1024]{1,0:T(8,128)(2,1)S(1)}, bf16[40,1024]{1,0:T(8,128)(2,1)S(1)}, u32[]{:S(2)}, u32[]{:S(2)}) collective-permute-start(bf16[40,1024]{1,0:T(8,128)(2,1)S(1)} %get-tuple-element.47), channel_id=1, source_target_pairs={{0,4},{4,0},{8,12},{12,8},{1,5},{5,1},{9,13},{13,9},{2,6},{6,2},{1... | collective-permute-start | bytes 245768 | tf_op jit(solution)/shard_map/ppermute | solution.py:230

commit v6 on v5

--- a/solution.py
+++ b/solution.py
@@ -13,10 +13,11 @@
 BF = jnp.bfloat16
 F32 = jnp.float32
 MIB = 1 << 20
-GATE_COST = 18
 C2COST = 100
-D0COST = 100
 WCOST = 3
+GFLOP = 100
+D1COST = 1
+D2COST = 100
 VMEM = pl.BlockSpec(memory_space=pltpu.VMEM)
 ANY = pl.BlockSpec(memory_space=pl.ANY)
 HBM = pl.BlockSpec(memory_space=pltpu.HBM)
@@ -56,12 +57,12 @@
     )(*operands)
 
 
-def pick_rows(experts, routes_in, probs_in, inputs, grads, pick_out, *refs):
+def pick_inputs(experts, routes_in, probs_in, inputs, pick_out, prob_out, *refs):
     *pieces, routes, probs, held, sems = refs
     loads = [
         pltpu.make_async_copy(source, target, sems.at[at])
         for at, (source, target) in enumerate(
-            [(routes_in, routes), (probs_in, probs), (inputs, held.at[0]), (grads, held.at[1])]
+            [(routes_in, routes), (probs_in, probs), (inputs, held)]
         )
     ]
     for load in loads:
@@ -73,6 +74,10 @@
     owner = block_of(iota((rows, routes.shape[0]), 0), order)
     named = jnp.zeros((rows, tokens), F32)
     weight = jnp.zeros((rows, tokens), F32)
+    earlier = iota((tokens, tokens), 0) < iota((tokens, tokens), 1)
+    earlier = jnp.where(earlier, 1.0, 0.0).astype(BF)
+    row = iota((rows, tokens), 0)
+    slot = row - block_of(row, range(experts)) * MOST
     loads[0].wait()
     loads[1].wait()
     chosen = routes[...]
@@ -82,24 +87,23 @@
         hit = chosen == (me ^ k)
         named = named + mm(spread, jnp.where(hit, 1.0, 0.0).astype(BF))
         weight = weight + mm(spread, jnp.where(hit, wide, 0.0).astype(BF))
-    earlier = iota((tokens, tokens), 0) < iota((tokens, tokens), 1)
-    rank = mm(named.astype(BF), jnp.where(earlier, 1.0, 0.0).astype(BF)).astype(jnp.int32)
-    row = iota((rows, tokens), 0)
-    slot = row - block_of(row, range(experts)) * MOST
+    rank = mm(named.astype(BF), earlier).astype(jnp.int32)
     picks = (rank == slot) & (named > 0.5)
     pick = jnp.where(picks, 1.0, 0.0)
-    prob = jnp.sum(jnp.where(picks, weight, 0.0), axis=1, keepdims=True)
     filled = jnp.max(pick, axis=1, keepdims=True) > 0.5
     pick = pick.astype(BF)
     pick_out[...] = pick
+    prob_out[...] = jnp.sum(jnp.where(picks, weight, 0.0), axis=1, keepdims=True)
     loads[2].wait()
-    sent = jnp.where(filled, mm(pick, held[0]), EMPTY)
+    sent = jnp.where(filled, mm(pick, held[...]), EMPTY)
     for k in range(experts):
         pieces[k][...] = sent[k * MOST : (k + 1) * MOST].astype(BF)
-    loads[3].wait()
-    sent = mm(pick, held[1]) * prob
+
+
+def pick_grads(experts, pick, prob, grads, _, *pieces):
+    sent = mm(pick[...], grads[...]) * prob[...]
     for k in range(experts):
-        pieces[experts + k][...] = sent[k * MOST : (k + 1) * MOST].astype(BF)
+        pieces[k][...] = sent[k * MOST : (k + 1) * MOST].astype(BF)
 
 
 def stacked(pieces):
@@ -128,8 +132,8 @@
     return place, mm(place, got.astype(BF), ROWS).astype(BF)
 
 
-def stage(gate_up, down, _, *refs):
-    (*held, sems) = refs
+def stage(gate_up, down, grads, _, *refs):
+    *held, grads_out, sems = refs
     half = down.shape[1] // 2
     loads = []
     for own, out in enumerate(held):
@@ -138,6 +142,8 @@
             source = down.at[0, rows] if matrix == 2 else gate_up.at[0, matrix, rows]
             loads.append(pltpu.make_async_copy(source, out.at[matrix], sems.at[len(loads)]))
             loads[-1].start()
+    loads.append(pltpu.make_async_copy(grads, grads_out, sems.at[len(loads)]))
+    loads[-1].start()
     for load in loads:
         load.wait()
 
@@ -153,19 +159,17 @@
         out[matrix] = mm(rows_in, held[matrix], LANES).astype(BF)
 
 
-def place_grads(experts, *refs):
-    place, rows_out = refs[experts:]
-    rows_out[...] = mm(place[...], stacked(refs[:experts]).astype(BF), ROWS).astype(BF)
-
-
-def act_parts(rows_grad, held_other, held_mine, _, other, mine):
-    other[...] = mm(rows_grad[...], held_other[2], LANES).astype(BF)
-    mine[...] = mm(rows_grad[...], held_mine[2], LANES).astype(BF)
-
-
-def gates(gate, gate_far, up, up_far, act_out, by_gate, by_up):
-    gate_sum = gate[...] + gate_far[...].astype(F32)
-    up_sum = up[...] + up_far[...].astype(F32)
+def act_part(experts, own, *refs):
+    place, held = refs[experts : experts + 2]
+    rows_grad = mm(place[...], stacked(refs[:experts]).astype(BF), ROWS).astype(BF)
+    if own:
+        refs[-2][...] = rows_grad
+    refs[-1][...] = mm(rows_grad, held[2], LANES).astype(BF)
+
+
+def gates(pair, pair_far, act_out, by_gate, by_up):
+    gate_sum = pair[0] + pair_far[0].astype(F32)
+    up_sum = pair[1] + pair_far[1].astype(F32)
     sigmoid_gate = jax.nn.sigmoid(gate_sum)
     silu_gate = gate_sum * sigmoid_gate
     act_out[...] = (silu_gate * up_sum).astype(BF)
@@ -249,31 +253,40 @@
     piece = [sds((MOST, width), BF)] * experts
     dma = lambda count: pltpu.SemaphoreType.DMA((count,))
 
-    pick, *sent = call(
-        functools.partial(pick_rows, experts),
-        [sds((rows, tokens), BF)] + piece * 2,
-        (far(routes.T), far(gate_probs.T), far(inputs), far(grad_output)),
-        [HBM] * 4,
+    pick, prob, *send_in = call(
+        functools.partial(pick_inputs, experts),
+        [sds((rows, tokens), BF), sds((rows, 1), F32)] + piece,
+        (far(routes.T), far(gate_probs.T), far(inputs)),
+        [HBM] * 3,
         [
             pltpu.VMEM(routes.shape[::-1], jnp.int32),
             pltpu.VMEM(routes.shape[::-1], BF),
-            pltpu.VMEM((2, tokens, width), BF),
-            dma(4),
+            pltpu.VMEM((tokens, width), BF),
+            dma(3),
         ],
-        flops=4 * rows * tokens * width,
-        traffic=4 * tokens * width,
-    )
-    got_in = exchange(sent[:experts], "ex")
-    got_grad = exchange(sent[experts:], "ex")
-    held_other, held_mine = call(
+        flops=2 * rows * tokens * width,
+        traffic=2 * tokens * width,
+    )
+    got_in = exchange(send_in, "ex")
+    held_other, held_mine, grads = call(
         stage,
-        [pltpu.VMEM((3, half, width), BF)] * 2,
-        (far(gate_up), far(down_proj), pick),
-        [HBM, HBM, ANY],
-        [dma(6)],
+        [pltpu.VMEM((3, half, width), BF)] * 2 + [pltpu.VMEM((tokens, width), BF)],
+        (far(gate_up), far(down_proj), far(grad_output), pick),
+        [HBM] * 3 + [ANY],
+        [dma(7)],
         flops=WCOST * weight_flops,
         traffic=WCOST * weight_bytes,
     )
+    send_grad = call(
+        functools.partial(pick_grads, experts),
+        piece,
+        (pick, prob, grads, held_mine),
+        [VMEM] * 3 + [ANY],
+        flops=2 * rows * tokens * width,
+        traffic=2 * tokens * width,
+    )
+    got_grad = exchange(send_grad, "ex")
+    sent = []
 
     def pair_part(held, extra, cost):
         return call(
@@ -294,34 +307,32 @@
         while bit * 2 < ways:
             held = held + swap(held.astype(BF), "ey", bit).astype(F32)
             bit *= 2
-        return held, swap(held.astype(BF), "ey", bit)
+        sent.append(held.astype(BF))
+        return held, swap(sent[-1], "ey", bit)
+
 
     pair = pair_mine.astype(F32) + swap(pair_other, "ey", 1).astype(F32)
-    gate, gate_far = total(pair[0])
-    up, up_far = total(pair[1])
-    rows_grad = call(
-        functools.partial(place_grads, experts),
-        sds((capacity, width), BF),
-        (*got_grad, place),
-        [VMEM] * (experts + 1),
-        flops=D0COST * weight_flops,
-        traffic=D0COST * weight_bytes,
-    )
-    act_other, act_mine = call(
-        act_parts,
-        [sds((capacity, half), BF)] * 2,
-        (rows_grad, held_other, held_mine, gate_far),
-        [VMEM] * 3 + [ANY],
-        flops=weight_flops,
-        traffic=weight_bytes,
-    )
+    pair, pair_far = total(pair)
+    def act_of(own, held, outs, tied, cost):
+        return call(
+            functools.partial(act_part, experts, own),
+            outs + [sds((capacity, half), BF)],
+            (*got_grad, place, held, *tied),
+            [VMEM] * (experts + 2) + [ANY] * len(tied),
+            flops=cost * weight_flops,
+            traffic=cost * weight_bytes,
+        )
+
+    (act_other,) = act_of(False, held_other, [], sent[-1:], D1COST)
+    rows_grad, act_mine = act_of(True, held_mine, [sds((capacity, width), BF)], [], D2COST)
     act, act_far = total(act_mine.astype(F32) + swap(act_other, "ey", 1).astype(F32))
     mine_act, by_gate, by_up = call(
         gates,
         [sds((capacity, half), BF)] + [sds((capacity, half), F32)] * 2,
-        (gate, gate_far, up, up_far),
-        [VMEM] * 4,
-        traffic=GATE_COST * capacity * half,
+        (pair, pair_far),
+        [VMEM] * 2,
+        traffic=18 * capacity * half,
+        flops=GFLOP * weight_flops,
     )
     other_act = swap(mine_act, "ey", 1)
     mine = call(

time: 50.5 us -> 44.8 us (0.89)
  waiting for transfers between devices: 12.5 us -> 8.82 us
  starting transfers between devices: 20.2 us -> 18.2 us
    ppermute x16 -> x15, waiting for transfers between devices: 12.5 us -> 8.82 us  [swap(): return lax.ppermute(value, axis, [(i, i ^ bit) for i in range(count)])]
    ppermute x16 -> x15, starting transfers between devices: 20.2 us -> 18.2 us  [swap(): return lax.ppermute(value, axis, [(i, i ^ bit) for i in range(count)])]
    pallas_call x12 -> x13, Pallas kernels: 16.7 us -> 16.8 us  [call(): pl.pallas_call(body, out_shape=outs, in_specs=specs, out_specs=out_specs...]
  transfers between devices with their start and end apart: 16 -> 15, of which waited for: 9 -> 10; matrix products, arithmetic and copies ran while one was open for 0% -> 0% of each run, Pallas kernels for 25% -> 32%
where the time goes in v6:
time: 44.8 us; the launch traced here: 44.6 us
  starting transfers between devices  18.2 us (41%)
  Pallas kernels  16.8 us (38%)
  waiting for transfers between devices  8.82 us (20%)
  between operations  0.74 us (2%)
    ppermute x15, starting transfers between devices, swap(): return lax.ppermute(value, axis, [(i, i ^ bit) for i in range(count)])  18.2 us
    pallas_call x13, Pallas kernels, call(): pl.pallas_call(body, out_shape=outs, in_specs=specs, out_specs=out_specs...  16.8 us
    ppermute x15, waiting for transfers between devices, swap(): return lax.ppermute(value, axis, [(i, i ^ bit) for i in range(count)])  8.82 us
  transfers between devices with their start and end apart: 15, of which 10 were waited for; matrix products, arithmetic and copies ran while one was open for 0% of the time, Pallas kernels for 32%

profile of v6, /device:TPU:0, one launch (start us, length us, event | category | flops | bytes accessed | tf_op | source)
XLA Modules:
  0.0 44.6 jit_solution(14553412274474930509)
XLA Ops:
  0.6 1.5 %shard_map.85 = (bf16[160,256]{1,0:T(8,128)(2,1)S(1)}, f32[160,1]{1,0:T(8,128)S(1)}, bf16[40,1024]{1,0:T(8,128)(2,1)S(1)}, bf16[40,1024]{1,0:T(8,128)(2,1)S(1)},...) custom-call(s32[8,256]{1,0:T(8,128)} %bitcast.2, bf16[8,256]{1,0:T(8,128)(2,1)} %bitcast.3, ...), custom_call_target="tpu_custom_call" | custom-call | flops 83886080 | bytes 524288 | tf_op jit(solution)/shard_map/pallas_call | solution.py:49
  2.1 4.1 %collective-permute-start.3 = (bf16[40,1024]{1,0:T(8,128)(2,1)S(1)}, bf16[40,1024]{1,0:T(8,128)(2,1)S(1)}, u32[]{:S(2)}, u32[]{:S(2)}) collective-permute-start(bf16[40,1024]{1,0:T(8,128)(2,1)S(1)} %get-tuple-element.38), channel_id=1, source_target_pairs={{0,8},{4,12},{8,0},{12,4},{1,9},{5,13},{9,1},{13,5},{2,10},{6,14},... | collective-permute-start | bytes 245768 | tf_op jit(solution)/shard_map/ppermute | solution.py:234
  6.2 1.3 %collective-permute-start.4 = (bf16[40,1024]{1,0:T(8,128)(2,1)S(1)}, bf16[40,1024]{1,0:T(8,128)(2,1)S(1)}, u32[]{:S(2)}, u32[]{:S(2)}) collective-permute-start(bf16[40,1024]{1,0:T(8,128)(2,1)S(1)} %get-tuple-element.39), channel_id=1, source_target_pairs={{0,12},{4,8},{8,4},{12,0},{1,13},{5,9},{9,5},{13,1},{2,14},{6,10},... | collective-permute-start | bytes 245768 | tf_op jit(solution)/shard_map/ppermute | solution.py:234
  7.8 3.9 %shard_map.86 = (bf16[3,768,1024]{2,1,0:T(8,128)(2,1)S(1)}, bf16[3,768,1024]{2,1,0:T(8,128)(2,1)S(1)}, bf16[256,1024]{1,0:T(8,128)(2,1)S(1)}) custom-call(bf16[1,2,1536,1024]{3,2,1,0:T(8,128)(2,1)} %gate_up.1, bf16[1,1536,1024]{2,1,0:T(8,128)(2,1)} %down.1, bf16[256,1024]{1,0:T(8,128)(2,1)} %grads.1, bf16[160,256]{1,0:T(8,128)(2,1)S(1)} %get-tuple-element.30._.pick), custom_call_target="tpu_custom_call" | custom-call | flops 754974720 | bytes 9437184 | tf_op jit(solution)/shard_map/pallas_call | solution.py:49
  11.9 2.9 %collective-permute-start = (bf16[40,1024]{1,0:T(8,128)(2,1)S(1)}, bf16[40,1024]{1,0:T(8,128)(2,1)S(1)}, u32[]{:S(2)}, u32[]{:S(2)}) collective-permute-start(bf16[40,1024]{1,0:T(8,128)(2,1)S(1)} %get-tuple-element.34), channel_id=1, source_target_pairs={{0,8},{4,12},{8,0},{12,4},{1,9},{5,13},{9,1},{13,5},{2,10},{6,14},... | collective-permute-start | bytes 245768 | tf_op jit(solution)/shard_map/ppermute | solution.py:234
  14.8 1.3 %collective-permute-start.1 = (bf16[40,1024]{1,0:T(8,128)(2,1)S(1)}, bf16[40,1024]{1,0:T(8,128)(2,1)S(1)}, u32[]{:S(2)}, u32[]{:S(2)}) collective-permute-start(bf16[40,1024]{1,0:T(8,128)(2,1)S(1)} %get-tuple-element.35), channel_id=1, source_target_pairs={{0,12},{4,8},{8,4},{12,0},{1,13},{5,9},{9,5},{13,1},{2,14},{6,10},... | collective-permute-start | bytes 245768 | tf_op jit(solution)/shard_map/ppermute | solution.py:234
  16.2 1.4 %shard_map.90 = bf16[2,80,768]{2,1,0:T(8,128)(2,1)S(1)} custom-call(bf16[40,1024]{1,0:T(8,128)(2,1)S(1)} %collective-permute-done.3.refs_0_, bf16[40,1024]{1,0:T(8,128)(2,1)S(1)} %collective-permute-done.4.refs_1_, bf16[40,1024]{1,0:T(8,128)(2,1)S(1)} %collective-permute-done.5.refs_2_, bf16[40,1024]{1,0:T(8,128)(2,1)S(1)} %get-tuple-element.41.refs_3_, ...), custom_call_target="tpu_custom_call" | custom-call | flops 251658240 | bytes 3145728 | tf_op jit(solution)/shard_map/pallas_call | solution.py:49
  17.7 1.4 %shard_map.88 = (bf16[2,80,768]{2,1,0:T(8,128)(2,1)S(1)}, bf16[160,80]{1,0:T(8,128)(2,1)S(1)}, bf16[80,1024]{1,0:T(8,128)(2,1)S(1)}) custom-call(bf16[40,1024]{1,0:T(8,128)(2,1)S(1)} %collective-permute-done.3.refs_0_, bf16[40,1024]{1,0:T(8,128)(2,1)S(1)} %collective-permute-done.4.refs_1_, bf16[40,1024]{1,0:T(8,128)(2,1)S(1)} %collective-permute-done.5.refs_2_, ...), custom_call_target="tpu_custom_call" | custom-call | flops 25165824000 | bytes 314572800 | tf_op jit(solution)/shard_map/pallas_call | solution.py:49
  19.3 1.6 %collective-permute-start.9 = (bf16[2,80,768]{2,1,0:T(8,128)(2,1)S(1)}, bf16[2,80,768]{2,1,0:T(8,128)(2,1)S(1)}, u32[]{:S(2)}, u32[]{:S(2)}) collective-permute-start(bf16[2,80,768]{2,1,0:T(8,128)(2,1)S(1)} %get-tuple-element.58.refs_6_), channel_id=1, source_target_pairs={{0,2},{1,3},{2,0},{3,1},{4,6},{5,7},{6,4},{7,5},{8,10},{9,11},{10,... | collective-permute-start | bytes 737288 | tf_op jit(solution)/shard_map/ppermute | solution.py:234
  20.8 0.6 %collective-permute-done.1.refs_1_ = bf16[40,1024]{1,0:T(8,128)(2,1)S(1)} collective-permute-done((bf16[40,1024]{1,0:T(8,128)(2,1)S(1)}, bf16[40,1024]{1,0:T(8,128)(2,1)S(1)}, u32[]{:S(2)}, u32[]{:S(2)}) %collective-permute-start.1) | collective-permute-done | bytes 81952 | tf_op jit(solution)/shard_map/ppermute | solution.py:234
  21.7 0.7 %shard_map.91 = bf16[80,768]{1,0:T(8,128)(2,1)S(1)} custom-call(bf16[40,1024]{1,0:T(8,128)(2,1)S(1)} %collective-permute-done.refs_0_, bf16[40,1024]{1,0:T(8,128)(2,1)S(1)} %collective-permute-done.1.refs_1_, bf16[40,1024]{1,0:T(8,128)(2,1)S(1)} %collective-permute-done.2.refs_2_, bf16[40,1024]{1,0:T(8,128)(2,1)S(1)} %get-tuple-element.37.refs_3_, ...), custom_call_target="tpu_custom_call" | custom-call | flops 251658240 | bytes 3145728 | tf_op jit(solution)/shard_map/pallas_call | solution.py:49
  22.5 0.7 %shard_map.89 = (bf16[80,1024]{1,0:T(8,128)(2,1)S(1)}, bf16[80,768]{1,0:T(8,128)(2,1)S(1)}) custom-call(bf16[40,1024]{1,0:T(8,128)(2,1)S(1)} %collective-permute-done.refs_0_, bf16[40,1024]{1,0:T(8,128)(2,1)S(1)} %collective-permute-done.1.refs_1_, bf16[40,1024]{1,0:T(8,128)(2,1)S(1)} %collective-permute-done.2.refs_2_, ...), custom_call_target="tpu_custom_call" | custom-call | flops 25165824000 | bytes 314572800 | tf_op jit(solution)/shard_map/pallas_call | solution.py:49
  23.2 0.6 %collective-permute-done.7 = bf16[80,768]{1,0:T(8,128)(2,1)S(1)} collective-permute-done((bf16[80,768]{1,0:T(8,128)(2,1)S(1)}, bf16[80,768]{1,0:T(8,128)(2,1)S(1)}, u32[]{:S(2)}, u32[]{:S(2)}) %collective-permute-start.7) | collective-permute-done | bytes 122912 | tf_op jit(solution)/shard_map/ppermute | solution.py:234
  23.8 1.6 %collective-permute-start.8 = (bf16[80,768]{1,0:T(8,128)(2,1)S(1)}, bf16[80,768]{1,0:T(8,128)(2,1)S(1)}, u32[]{:S(2)}, u32[]{:S(2)}) collective-permute-start(bf16[80,768]{1,0:T(8,128)(2,1)S(1)} %get-tuple-element.59), channel_id=1, source_target_pairs={{0,2},{1,3},{2,0},{3,1},{4,6},{5,7},{6,4},{7,5},{8,10},{9,11},{10,... | collective-permute-start | bytes 368648 | tf_op jit(solution)/shard_map/ppermute | solution.py:234
  25.4 2.7 %collective-permute-done.9.pair_far = bf16[2,80,768]{2,1,0:T(8,128)(2,1)S(1)} collective-permute-done((bf16[2,80,768]{2,1,0:T(8,128)(2,1)S(1)}, bf16[2,80,768]{2,1,0:T(8,128)(2,1)S(1)}, u32[]{:S(2)}, u32[]{:S(2)}) %collective-permute-start.9) | collective-permute-done | bytes 245792 | tf_op jit(solution)/shard_map/ppermute | solution.py:234
  28.2 2.1 %collective-permute-done.8.act_far = bf16[80,768]{1,0:T(8,128)(2,1)S(1)} collective-permute-done((bf16[80,768]{1,0:T(8,128)(2,1)S(1)}, bf16[80,768]{1,0:T(8,128)(2,1)S(1)}, u32[]{:S(2)}, u32[]{:S(2)}) %collective-permute-start.8) | collective-permute-done | bytes 122912 | tf_op jit(solution)/shard_map/ppermute | solution.py:234
  30.9 0.7 %shard_map.94.total = f32[80,1024]{1,0:T(8,128)S(1)} custom-call(bf16[2,80,768]{2,1,0:T(8,128)(2,1)S(1)} %shard_map.93.mine, bf16[3,768,1024]{2,1,0:T(8,128)(2,1)S(1)} %get-tuple-element.33._.refs_4_.refs_5_.held), custom_call_target="tpu_custom_call" | custom-call | flops 251658240 | bytes 3145728 | tf_op jit(solution)/shard_map/pallas_call | solution.py:49
  31.9 0.8 %shard_map.95 = (bf16[40,1024]{1,0:T(8,128)(2,1)S(1)}, bf16[40,1024]{1,0:T(8,128)(2,1)S(1)}, bf16[40,1024]{1,0:T(8,128)(2,1)S(1)}, bf16[40,1024]{1,0:T(8,128)(2,1)S(1)}) custom-call(f32[80,1024]{1,0:T(8,128)S(1)} %shard_map.94.total, bf16[2,80,768]{2,1,0:T(8,128)(2,1)S(1)} %collective-permute-done.10.other, ...), custom_call_target="tpu_custom_call" | custom-call | flops 251658240 | bytes 3145728 | tf_op jit(solution)/shard_map/pallas_call | solution.py:49
  32.8 3.1 %collective-permute-start.11 = (bf16[40,1024]{1,0:T(8,128)(2,1)S(1)}, bf16[40,1024]{1,0:T(8,128)(2,1)S(1)}, u32[]{:S(2)}, u32[]{:S(2)}) collective-permute-start(bf16[40,1024]{1,0:T(8,128)(2,1)S(1)} %get-tuple-element.48), channel_id=1, source_target_pairs={{0,8},{4,12},{8,0},{12,4},{1,9},{5,13},{9,1},{13,5},{2,10},{6,14},... | collective-permute-start | bytes 245768 | tf_op jit(solution)/shard_map/ppermute | solution.py:234
  35.9 1.3 %collective-permute-start.12 = (bf16[40,1024]{1,0:T(8,128)(2,1)S(1)}, bf16[40,1024]{1,0:T(8,128)(2,1)S(1)}, u32[]{:S(2)}, u32[]{:S(2)}) collective-permute-start(bf16[40,1024]{1,0:T(8,128)(2,1)S(1)} %get-tuple-element.49), channel_id=1, source_target_pairs={{0,12},{4,8},{8,4},{12,0},{1,13},{5,9},{9,5},{13,1},{2,14},{6,10},... | collective-permute-start | bytes 245768 | tf_op jit(solution)/shard_map/ppermute | solution.py:234
  37.2 4.1 %shard_map.97 = (bf16[1,2,1536,1024]{3,2,1,0:T(8,128)(2,1)}, bf16[1,1536,1024]{2,1,0:T(8,128)(2,1)}) custom-call(bf16[80,768]{1,0:T(8,128)(2,1)S(1)} %get-tuple-element.52.mine_act, bf16[80,768]{1,0:T(8,128)(2,1)S(1)} %collective-permute-done.14.other_act, bf16[2,80,768]{2,1,0:T(8,128)(2,1)S(1)} %shard_map.93.mine, ...), custom_call_target="tpu_custom_call" | custom-call | flops 754974720 | bytes 9437184 | tf_op jit(solution)/shard_map/pallas_call | solution.py:49
  41.3 0.9 %collective-permute-done.11.refs_0_ = bf16[40,1024]{1,0:T(8,128)(2,1)S(1)} collective-permute-done((bf16[40,1024]{1,0:T(8,128)(2,1)S(1)}, bf16[40,1024]{1,0:T(8,128)(2,1)S(1)}, u32[]{:S(2)}, u32[]{:S(2)}) %collective-permute-start.11) | collective-permute-done | bytes 81952 | tf_op jit(solution)/shard_map/ppermute | solution.py:234
  42.8 0.7 %collective-permute-done.13.refs_2_ = bf16[40,1024]{1,0:T(8,128)(2,1)S(1)} collective-permute-done((bf16[40,1024]{1,0:T(8,128)(2,1)S(1)}, bf16[40,1024]{1,0:T(8,128)(2,1)S(1)}, u32[]{:S(2)}, u32[]{:S(2)}) %collective-permute-start.13) | collective-permute-done | bytes 81952 | tf_op jit(solution)/shard_map/ppermute | solution.py:234
  43.5 1.1 %shard_map.96 = bf16[256,1024]{1,0:T(8,128)(2,1)} custom-call(bf16[160,256]{1,0:T(8,128)(2,1)S(1)} %get-tuple-element.30._.pick, bf16[40,1024]{1,0:T(8,128)(2,1)S(1)} %collective-permute-done.11.refs_0_, bf16[40,1024]{1,0:T(8,128)(2,1)S(1)} %collective-permute-done.12.refs_1_, bf16[40,1024]{1,0:T(8,128)(2,1)S(1)} %collective-permute-done.13.refs_2_, ...), custom_call_target="tpu_custom_call" | custom-call | flops 83886080 | bytes 1048576 | tf_op jit(solution)/shard_map/pallas_call | solution.py:49
  (21 shorter events, 2.7 us)
Async XLA Ops:
  2.1 14.0 %collective-permute-start.3 = (bf16[40,1024]{1,0:T(8,128)(2,1)S(1)}, bf16[40,1024]{1,0:T(8,128)(2,1)S(1)}, u32[]{:S(2)}, u32[]{:S(2)}) collective-permute-start(bf16[40,1024]{1,0:T(8,128)(2,1)S(1)} %get-tuple-element.38), channel_id=1, source_target_pairs={{0,8},{4,12},{8,0},{12,4},{1,9},{5,13},{9,1},{13,5},{2,10},{6,14},... | collective-permute-start | bytes 245768 | tf_op jit(solution)/shard_map/ppermute | solution.py:234
  6.2 9.9 %collective-permute-start.4 = (bf16[40,1024]{1,0:T(8,128)(2,1)S(1)}, bf16[40,1024]{1,0:T(8,128)(2,1)S(1)}, u32[]{:S(2)}, u32[]{:S(2)}) collective-permute-start(bf16[40,1024]{1,0:T(8,128)(2,1)S(1)} %get-tuple-element.39), channel_id=1, source_target_pairs={{0,12},{4,8},{8,4},{12,0},{1,13},{5,9},{9,5},{13,1},{2,14},{6,10},... | collective-permute-start | bytes 245768 | tf_op jit(solution)/shard_map/ppermute | solution.py:234
  7.6 8.6 %collective-permute-start.5 = (bf16[40,1024]{1,0:T(8,128)(2,1)S(1)}, bf16[40,1024]{1,0:T(8,128)(2,1)S(1)}, u32[]{:S(2)}, u32[]{:S(2)}) collective-permute-start(bf16[40,1024]{1,0:T(8,128)(2,1)S(1)} %get-tuple-element.40), channel_id=1, source_target_pairs={{0,4},{4,0},{8,12},{12,8},{1,5},{5,1},{9,13},{13,9},{2,6},{6,2},{1... | collective-permute-start | bytes 245768 | tf_op jit(solution)/shard_map/ppermute | solution.py:234
  11.9 8.9 %collective-permute-start = (bf16[40,1024]{1,0:T(8,128)(2,1)S(1)}, bf16[40,1024]{1,0:T(8,128)(2,1)S(1)}, u32[]{:S(2)}, u32[]{:S(2)}) collective-permute-start(bf16[40,1024]{1,0:T(8,128)(2,1)S(1)} %get-tuple-element.34), channel_id=1, source_target_pairs={{0,8},{4,12},{8,0},{12,4},{1,9},{5,13},{9,1},{13,5},{2,10},{6,14},... | collective-permute-start | bytes 245768 | tf_op jit(solution)/shard_map/ppermute | solution.py:234
  14.8 6.6 %collective-permute-start.1 = (bf16[40,1024]{1,0:T(8,128)(2,1)S(1)}, bf16[40,1024]{1,0:T(8,128)(2,1)S(1)}, u32[]{:S(2)}, u32[]{:S(2)}) collective-permute-start(bf16[40,1024]{1,0:T(8,128)(2,1)S(1)} %get-tuple-element.35), channel_id=1, source_target_pairs={{0,12},{4,8},{8,4},{12,0},{1,13},{5,9},{9,5},{13,1},{2,14},{6,10},... | collective-permute-start | bytes 245768 | tf_op jit(solution)/shard_map/ppermute | solution.py:234
  16.2 5.5 %collective-permute-start.2 = (bf16[40,1024]{1,0:T(8,128)(2,1)S(1)}, bf16[40,1024]{1,0:T(8,128)(2,1)S(1)}, u32[]{:S(2)}, u32[]{:S(2)}) collective-permute-start(bf16[40,1024]{1,0:T(8,128)(2,1)S(1)} %get-tuple-element.36), channel_id=1, source_target_pairs={{0,4},{4,0},{8,12},{12,8},{1,5},{5,1},{9,13},{13,9},{2,6},{6,2},{1... | collective-permute-start | bytes 245768 | tf_op jit(solution)/shard_map/ppermute | solution.py:234
  17.6 1.6 %collective-permute-start.6 = (bf16[2,80,768]{2,1,0:T(8,128)(2,1)S(1)}, bf16[2,80,768]{2,1,0:T(8,128)(2,1)S(1)}, u32[]{:S(2)}, u32[]{:S(2)}) collective-permute-start(bf16[2,80,768]{2,1,0:T(8,128)(2,1)S(1)} %shard_map.90), channel_id=1, source_target_pairs={{0,1},{1,0},{2,3},{3,2},{4,5},{5,4},{6,7},{7,6},{8,9},{9,8},{10,11... | collective-permute-start | bytes 737288 | tf_op jit(solution)/shard_map/ppermute | solution.py:234
  19.3 8.8 %collective-permute-start.9 = (bf16[2,80,768]{2,1,0:T(8,128)(2,1)S(1)}, bf16[2,80,768]{2,1,0:T(8,128)(2,1)S(1)}, u32[]{:S(2)}, u32[]{:S(2)}) collective-permute-start(bf16[2,80,768]{2,1,0:T(8,128)(2,1)S(1)} %get-tuple-element.58.refs_6_), channel_id=1, source_target_pairs={{0,2},{1,3},{2,0},{3,1},{4,6},{5,7},{6,4},{7,5},{8,10},{9,11},{10,... | collective-permute-start | bytes 737288 | tf_op jit(solution)/shard_map/ppermute | solution.py:234
  22.4 1.4 %collective-permute-start.7 = (bf16[80,768]{1,0:T(8,128)(2,1)S(1)}, bf16[80,768]{1,0:T(8,128)(2,1)S(1)}, u32[]{:S(2)}, u32[]{:S(2)}) collective-permute-start(bf16[80,768]{1,0:T(8,128)(2,1)S(1)} %shard_map.91), channel_id=1, source_target_pairs={{0,1},{1,0},{2,3},{3,2},{4,5},{5,4},{6,7},{7,6},{8,9},{9,8},{10,11... | collective-permute-start | bytes 368648 | tf_op jit(solution)/shard_map/ppermute | solution.py:234
  23.8 6.4 %collective-permute-start.8 = (bf16[80,768]{1,0:T(8,128)(2,1)S(1)}, bf16[80,768]{1,0:T(8,128)(2,1)S(1)}, u32[]{:S(2)}, u32[]{:S(2)}) collective-permute-start(bf16[80,768]{1,0:T(8,128)(2,1)S(1)} %get-tuple-element.59), channel_id=1, source_target_pairs={{0,2},{1,3},{2,0},{3,1},{4,6},{5,7},{6,4},{7,5},{8,10},{9,11},{10,... | collective-permute-start | bytes 368648 | tf_op jit(solution)/shard_map/ppermute | solution.py:234
  30.3 1.6 %collective-permute-start.10 = (bf16[2,80,768]{2,1,0:T(8,128)(2,1)S(1)}, bf16[2,80,768]{2,1,0:T(8,128)(2,1)S(1)}, u32[]{:S(2)}, u32[]{:S(2)}) collective-permute-start(bf16[2,80,768]{2,1,0:T(8,128)(2,1)S(1)} %shard_map.93.mine), channel_id=1, source_target_pairs={{0,1},{1,0},{2,3},{3,2},{4,5},{5,4},{6,7},{7,6},{8,9},{9,8},{10,11... | collective-permute-start | bytes 737288 | tf_op jit(solution)/shard_map/ppermute | solution.py:234
  30.4 6.8 %collective-permute-start.14 = (bf16[80,768]{1,0:T(8,128)(2,1)S(1)}, bf16[80,768]{1,0:T(8,128)(2,1)S(1)}, u32[]{:S(2)}, u32[]{:S(2)}) collective-permute-start(bf16[80,768]{1,0:T(8,128)(2,1)S(1)} %get-tuple-element.52.mine_act), channel_id=1, source_target_pairs={{0,1},{1,0},{2,3},{3,2},{4,5},{5,4},{6,7},{7,6},{8,9},{9,8},{10,11... | collective-permute-start | bytes 368648 | tf_op jit(solution)/shard_map/ppermute | solution.py:234
  32.8 9.5 %collective-permute-start.11 = (bf16[40,1024]{1,0:T(8,128)(2,1)S(1)}, bf16[40,1024]{1,0:T(8,128)(2,1)S(1)}, u32[]{:S(2)}, u32[]{:S(2)}) collective-permute-start(bf16[40,1024]{1,0:T(8,128)(2,1)S(1)} %get-tuple-element.48), channel_id=1, source_target_pairs={{0,8},{4,12},{8,0},{12,4},{1,9},{5,13},{9,1},{13,5},{2,10},{6,14},... | collective-permute-start | bytes 245768 | tf_op jit(solution)/shard_map/ppermute | solution.py:234
  35.9 6.9 %collective-permute-start.12 = (bf16[40,1024]{1,0:T(8,128)(2,1)S(1)}, bf16[40,1024]{1,0:T(8,128)(2,1)S(1)}, u32[]{:S(2)}, u32[]{:S(2)}) collective-permute-start(bf16[40,1024]{1,0:T(8,128)(2,1)S(1)} %get-tuple-element.49), channel_id=1, source_target_pairs={{0,12},{4,8},{8,4},{12,0},{1,13},{5,9},{9,5},{13,1},{2,14},{6,10},... | collective-permute-start | bytes 245768 | tf_op jit(solution)/shard_map/ppermute | solution.py:234
  37.2 6.3 %collective-permute-start.13 = (bf16[40,1024]{1,0:T(8,128)(2,1)S(1)}, bf16[40,1024]{1,0:T(8,128)(2,1)S(1)}, u32[]{:S(2)}, u32[]{:S(2)}) collective-permute-start(bf16[40,1024]{1,0:T(8,128)(2,1)S(1)} %get-tuple-element.50), channel_id=1, source_target_pairs={{0,4},{4,0},{8,12},{12,8},{1,5},{5,1},{9,13},{13,9},{2,6},{6,2},{1... | collective-permute-start | bytes 245768 | tf_op jit(solution)/shard_map/ppermute | solution.py:234

commit v7 on v6

--- a/solution.py
+++ b/solution.py
@@ -14,7 +14,7 @@
 F32 = jnp.float32
 MIB = 1 << 20
 C2COST = 100
-WCOST = 3
+WCOST = 100
 GFLOP = 100
 D1COST = 1
 D2COST = 100
@@ -57,12 +57,12 @@
     )(*operands)
 
 
-def pick_inputs(experts, routes_in, probs_in, inputs, pick_out, prob_out, *refs):
+def pick_inputs(experts, routes_in, probs_in, inputs, grads, pick_out, prob_out, grads_out, *refs):
     *pieces, routes, probs, held, sems = refs
     loads = [
         pltpu.make_async_copy(source, target, sems.at[at])
         for at, (source, target) in enumerate(
-            [(routes_in, routes), (probs_in, probs), (inputs, held)]
+            [(routes_in, routes), (probs_in, probs), (inputs, held), (grads, grads_out)]
         )
     ]
     for load in loads:
@@ -98,16 +98,24 @@
     sent = jnp.where(filled, mm(pick, held[...]), EMPTY)
     for k in range(experts):
         pieces[k][...] = sent[k * MOST : (k + 1) * MOST].astype(BF)
-
-
-def pick_grads(experts, pick, prob, grads, _, *pieces):
+    loads[3].wait()
+
+
+def pick_grads(experts, pick, prob, grads, near_in, near, *pieces):
     sent = mm(pick[...], grads[...]) * prob[...]
-    for k in range(experts):
-        pieces[k][...] = sent[k * MOST : (k + 1) * MOST].astype(BF)
-
-
-def stacked(pieces):
-    return jnp.concatenate([piece[...].astype(F32) for piece in pieces], axis=0)
+    for at, k in enumerate(far_first(experts)):
+        rows = sent[at * MOST : (at + 1) * MOST]
+        if k == 1:
+            both = jnp.concatenate([near_in[...].astype(F32), rows], axis=0)
+            near[...] = both.astype(BF)
+        else:
+            pieces[at if k else at - 1][...] = rows.astype(BF)
+
+
+def stacked(pieces, part=0):
+    rows = [piece[...].astype(F32) for piece in pieces]
+    rows = [row[part * MOST : (part + 1) * MOST] if row.shape[0] > MOST else row for row in rows]
+    return jnp.concatenate(rows, axis=0)
 
 
 def rows_of(half, own):
@@ -132,36 +140,42 @@
     return place, mm(place, got.astype(BF), ROWS).astype(BF)
 
 
-def stage(gate_up, down, grads, _, *refs):
-    *held, grads_out, sems = refs
+def stage(far_count, gate_up, down, *refs):
+    pieces, refs = refs[:far_count], refs[far_count:]
+    held, pieces_out, sems = refs[:2], refs[2:-1], refs[-1]
     half = down.shape[1] // 2
-    loads = []
+    moves = list(zip(pieces, pieces_out))
     for own, out in enumerate(held):
         rows = rows_of(half, own == 1)
         for matrix in range(3):
             source = down.at[0, rows] if matrix == 2 else gate_up.at[0, matrix, rows]
-            loads.append(pltpu.make_async_copy(source, out.at[matrix], sems.at[len(loads)]))
-            loads[-1].start()
-    loads.append(pltpu.make_async_copy(grads, grads_out, sems.at[len(loads)]))
-    loads[-1].start()
+            moves.append((source, out.at[matrix]))
+    loads = [
+        pltpu.make_async_copy(source, target, sems.at[at]) for at, (source, target) in enumerate(moves)
+    ]
+    for load in loads:
+        load.start()
     for load in loads:
         load.wait()
 
 
-def gate_up_parts(experts, capacity, *refs):
-    pieces = refs[:experts]
-    held, out, *extra = refs[experts:]
-    place, rows_in = place_rows(experts, capacity, pieces)
-    if extra:
-        extra[0][...] = place
-        extra[1][...] = rows_in
+def other_pair(experts, capacity, *refs):
+    held, out, place_out, rows_out = refs[experts:]
+    place, rows_in = place_rows(experts, capacity, refs[:experts])
+    place_out[...] = place
+    rows_out[...] = rows_in
     for matrix in range(2):
         out[matrix] = mm(rows_in, held[matrix], LANES).astype(BF)
 
 
+def mine_pair(rows_in, held, out):
+    for matrix in range(2):
+        out[matrix] = mm(rows_in[...], held[matrix], LANES).astype(BF)
+
+
 def act_part(experts, own, *refs):
     place, held = refs[experts : experts + 2]
-    rows_grad = mm(place[...], stacked(refs[:experts]).astype(BF), ROWS).astype(BF)
+    rows_grad = mm(place[...], stacked(refs[:experts], 1).astype(BF), ROWS).astype(BF)
     if own:
         refs[-2][...] = rows_grad
     refs[-1][...] = mm(rows_grad, held[2], LANES).astype(BF)
@@ -177,7 +191,7 @@
     by_up[...] = silu_gate
 
 
-def grads_of(act, act_far, by_gate, by_up, out):
+def grads_of(act, act_far, by_gate, by_up, _, out):
     grad_act = act[...] + act_far[...].astype(F32)
     out[0] = (grad_act * by_gate[...]).astype(BF)
     out[1] = (grad_act * by_up[...]).astype(BF)
@@ -253,55 +267,68 @@
     piece = [sds((MOST, width), BF)] * experts
     dma = lambda count: pltpu.SemaphoreType.DMA((count,))
 
-    pick, prob, *send_in = call(
+    order = far_first(experts)
+    far_count = experts - 2
+    pick, prob, grads, *send_in = call(
         functools.partial(pick_inputs, experts),
-        [sds((rows, tokens), BF), sds((rows, 1), F32)] + piece,
-        (far(routes.T), far(gate_probs.T), far(inputs)),
-        [HBM] * 3,
+        [
+            sds((rows, tokens), BF),
+            sds((rows, 1), F32),
+            pltpu.VMEM((tokens, width), BF),
+        ]
+        + piece,
+        (far(routes.T), far(gate_probs.T), far(inputs), far(grad_output)),
+        [HBM] * 4,
         [
             pltpu.VMEM(routes.shape[::-1], jnp.int32),
             pltpu.VMEM(routes.shape[::-1], BF),
             pltpu.VMEM((tokens, width), BF),
-            dma(3),
+            dma(4),
         ],
         flops=2 * rows * tokens * width,
+        traffic=4 * tokens * width,
+    )
+    near, *send_grad = call(
+        functools.partial(pick_grads, experts),
+        [sds((2 * MOST, width), BF)] + piece[1:],
+        (pick, prob, grads, send_in[-2]),
+        [VMEM] * 4,
+        flops=2 * rows * tokens * width,
         traffic=2 * tokens * width,
     )
-    got_in = exchange(send_in, "ex")
-    held_other, held_mine, grads = call(
-        stage,
-        [pltpu.VMEM((3, half, width), BF)] * 2 + [pltpu.VMEM((tokens, width), BF)],
-        (far(gate_up), far(down_proj), far(grad_output), pick),
-        [HBM] * 3 + [ANY],
-        [dma(7)],
+    got_in = [swap(send_in[at], "ex", order[at]) for at in range(far_count)]
+    near = swap(near, "ex", 1)
+    got_in = got_in + [near, send_in[-1]]
+    held_other, held_mine, *far_grad = call(
+        functools.partial(stage, far_count),
+        [pltpu.VMEM((3, half, width), BF)] * 2 + piece[2:],
+        (far(gate_up), far(down_proj), *send_grad[:-1]),
+        [HBM] * 2 + [VMEM] * far_count,
+        [dma(far_count + 6)],
         flops=WCOST * weight_flops,
         traffic=WCOST * weight_bytes,
     )
-    send_grad = call(
-        functools.partial(pick_grads, experts),
-        piece,
-        (pick, prob, grads, held_mine),
-        [VMEM] * 3 + [ANY],
-        flops=2 * rows * tokens * width,
-        traffic=2 * tokens * width,
-    )
-    got_grad = exchange(send_grad, "ex")
+    got_grad = [swap(far_grad[at], "ex", order[at]) for at in range(far_count)]
+    got_grad = got_grad + [near, send_grad[-1]]
     sent = []
 
-    def pair_part(held, extra, cost):
-        return call(
-            functools.partial(gate_up_parts, experts, capacity),
-            [sds((2, capacity, half), BF)] + extra,
-            (*got_in, held),
-            [VMEM] * (experts + 1),
-            flops=cost * weight_flops,
-            traffic=cost * weight_bytes,
-        )
-
-    (pair_other,) = pair_part(held_other, [], 1)
-    pair_mine, place, rows_in = pair_part(
-        held_mine, [sds((rows, capacity), BF), sds((capacity, width), BF)], C2COST
-    )
+    pair_other, place, rows_in = call(
+        functools.partial(other_pair, experts, capacity),
+        [sds((2, capacity, half), BF), sds((rows, capacity), BF), sds((capacity, width), BF)],
+        (*got_in, held_other),
+        [VMEM] * (experts + 1),
+        flops=2 * weight_flops,
+        traffic=weight_bytes,
+    )
+    pair_mine = call(
+        mine_pair,
+        sds((2, capacity, half), BF),
+        (rows_in, held_mine),
+        [VMEM] * 2,
+        flops=C2COST * weight_flops,
+        traffic=C2COST * weight_bytes,
+    )
+
     def total(held):
         bit = 2
         while bit * 2 < ways:
@@ -338,8 +365,8 @@
     mine = call(
         grads_of,
         sds((2, capacity, half), BF),
-        (act, act_far, by_gate, by_up),
-        [VMEM] * 4,
+        (act, act_far, by_gate, by_up, other_act),
+        [VMEM] * 4 + [ANY],
         traffic=18 * capacity * half,
     )
     other = swap(mine, "ey", 1)

time: 44.8 us -> 44.4 us (level)
  starting transfers between devices: 18.2 us -> 17.3 us
  waiting for transfers between devices: 8.82 us -> 9.41 us
    ppermute x15 -> x14, starting transfers between devices: 18.2 us -> 17.3 us  [swap(): return lax.ppermute(value, axis, [(i, i ^ bit) for i in range(count)])]
    ppermute x15 -> x14, waiting for transfers between devices: 8.82 us -> 9.41 us  [swap(): return lax.ppermute(value, axis, [(i, i ^ bit) for i in range(count)])]
  transfers between devices with their start and end apart: 15 -> 14, of which waited for: 10 -> 8; matrix products, arithmetic and copies ran while one was open for 0% -> 0% of each run, Pallas kernels for 32% -> 30%
where the time goes in v7:
time: 44.4 us; the launch traced here: 44.1 us
  starting transfers between devices  17.3 us (39%)
  Pallas kernels  16.6 us (37%)
  waiting for transfers between devices  9.41 us (21%)
  between operations  0.74 us (2%)
    ppermute x14, starting transfers between devices, swap(): return lax.ppermute(value, axis, [(i, i ^ bit) for i in range(count)])  17.3 us
    pallas_call x13, Pallas kernels, call(): pl.pallas_call(body, out_shape=outs, in_specs=specs, out_specs=out_specs...  16.6 us
    ppermute x14, waiting for transfers between devices, swap(): return lax.ppermute(value, axis, [(i, i ^ bit) for i in range(count)])  9.41 us
  transfers between devices with their start and end apart: 14, of which 8 were waited for; matrix products, arithmetic and copies ran while one was open for 0% of the time, Pallas kernels for 30%

profile of v7, /device:TPU:0, one launch (start us, length us, event | category | flops | bytes accessed | tf_op | source)
XLA Modules:
  0.0 44.1 jit_solution(9614107673510978265)
XLA Ops:
  0.6 1.5 %shard_map.85 = (bf16[160,256]{1,0:T(8,128)(2,1)S(1)}, f32[160,1]{1,0:T(8,128)S(1)}, bf16[256,1024]{1,0:T(8,128)(2,1)S(1)}, bf16[40,1024]{1,0:T(8,128)(2,1)S(1)}...) custom-call(s32[8,256]{1,0:T(8,128)} %bitcast.2, ...), custom_call_target="tpu_custom_call" | custom-call | flops 83886080 | bytes 1048576 | tf_op jit(solution)/shard_map/pallas_call | solution.py:49
  2.1 4.1 %collective-permute-start.3 = (bf16[40,1024]{1,0:T(8,128)(2,1)S(1)}, bf16[40,1024]{1,0:T(8,128)(2,1)S(1)}, u32[]{:S(2)}, u32[]{:S(2)}) collective-permute-start(bf16[40,1024]{1,0:T(8,128)(2,1)S(1)} %get-tuple-element.42), channel_id=1, source_target_pairs={{0,8},{4,12},{8,0},{12,4},{1,9},{5,13},{9,1},{13,5},{2,10},{6,14},... | collective-permute-start | bytes 245768 | tf_op jit(solution)/shard_map/ppermute | solution.py:248
  6.2 1.3 %collective-permute-start.4 = (bf16[40,1024]{1,0:T(8,128)(2,1)S(1)}, bf16[40,1024]{1,0:T(8,128)(2,1)S(1)}, u32[]{:S(2)}, u32[]{:S(2)}) collective-permute-start(bf16[40,1024]{1,0:T(8,128)(2,1)S(1)} %get-tuple-element.43), channel_id=1, source_target_pairs={{0,12},{4,8},{8,4},{12,0},{1,13},{5,9},{9,5},{13,1},{2,14},{6,10},... | collective-permute-start | bytes 245768 | tf_op jit(solution)/shard_map/ppermute | solution.py:248
  8.1 4.0 %shard_map.87 = (bf16[3,768,1024]{2,1,0:T(8,128)(2,1)S(1)}, bf16[3,768,1024]{2,1,0:T(8,128)(2,1)S(1)}, bf16[40,1024]{1,0:T(8,128)(2,1)S(1)}, bf16[40,1024]{1,0:T(8,128)(2,1)S(1)}) custom-call(bf16[1,2,1536,1024]{3,2,1,0:T(8,128)(2,1)} %gate_up.1, bf16[1,1536,1024]{2,1,0:T(8,128)(2,1)} %down.1, bf16[40,1024]{1,0:T(8,128)(2,1)S(1)} %get-tuple-element.36.refs_0_, ...), custom_call_target="tpu_custom_call" | custom-call | flops 25165824000 | bytes 314572800 | tf_op jit(solution)/shard_map/pallas_call | solution.py:49
  12.1 2.9 %collective-permute-start = (bf16[40,1024]{1,0:T(8,128)(2,1)S(1)}, bf16[40,1024]{1,0:T(8,128)(2,1)S(1)}, u32[]{:S(2)}, u32[]{:S(2)}) collective-permute-start(bf16[40,1024]{1,0:T(8,128)(2,1)S(1)} %get-tuple-element.38), channel_id=1, source_target_pairs={{0,8},{4,12},{8,0},{12,4},{1,9},{5,13},{9,1},{13,5},{2,10},{6,14},... | collective-permute-start | bytes 245768 | tf_op jit(solution)/shard_map/ppermute | solution.py:248
  15.0 1.3 %collective-permute-start.1 = (bf16[40,1024]{1,0:T(8,128)(2,1)S(1)}, bf16[40,1024]{1,0:T(8,128)(2,1)S(1)}, u32[]{:S(2)}, u32[]{:S(2)}) collective-permute-start(bf16[40,1024]{1,0:T(8,128)(2,1)S(1)} %get-tuple-element.39), channel_id=1, source_target_pairs={{0,12},{4,8},{8,4},{12,0},{1,13},{5,9},{9,5},{13,1},{2,14},{6,10},... | collective-permute-start | bytes 245768 | tf_op jit(solution)/shard_map/ppermute | solution.py:248
  16.4 1.4 %shard_map.88 = (bf16[2,80,768]{2,1,0:T(8,128)(2,1)S(1)}, bf16[160,80]{1,0:T(8,128)(2,1)S(1)}, bf16[80,1024]{1,0:T(8,128)(2,1)S(1)}) custom-call(bf16[40,1024]{1,0:T(8,128)(2,1)S(1)} %collective-permute-done.3.refs_0_, bf16[40,1024]{1,0:T(8,128)(2,1)S(1)} %collective-permute-done.4.refs_1_, bf16[80,1024]{1,0:T(8,128)(2,1)S(1)} %collective-permute-done.2.refs_2_, ...), custom_call_target="tpu_custom_call" | custom-call | flops 503316480 | bytes 3145728 | tf_op jit(solution)/shard_map/pallas_call | solution.py:49
  17.9 1.1 %shard_map.90 = bf16[2,80,768]{2,1,0:T(8,128)(2,1)S(1)} custom-call(bf16[80,1024]{1,0:T(8,128)(2,1)S(1)} %get-tuple-element.49.rows_in, bf16[3,768,1024]{2,1,0:T(8,128)(2,1)S(1)} %get-tuple-element.47.refs_5_.held), custom_call_target="tpu_custom_call" | custom-call | flops 25165824000 | bytes 314572800 | tf_op jit(solution)/shard_map/pallas_call | solution.py:49
  19.5 1.7 %collective-permute-start.8 = (bf16[2,80,768]{2,1,0:T(8,128)(2,1)S(1)}, bf16[2,80,768]{2,1,0:T(8,128)(2,1)S(1)}, u32[]{:S(2)}, u32[]{:S(2)}) collective-permute-start(bf16[2,80,768]{2,1,0:T(8,128)(2,1)S(1)} %get-tuple-element.62.refs_6_), channel_id=1, source_target_pairs={{0,2},{1,3},{2,0},{3,1},{4,6},{5,7},{6,4},{7,5},{8,10},{9,11},{10,... | collective-permute-start | bytes 737288 | tf_op jit(solution)/shard_map/ppermute | solution.py:248
  21.3 0.7 %shard_map.91 = bf16[80,768]{1,0:T(8,128)(2,1)S(1)} custom-call(bf16[40,1024]{1,0:T(8,128)(2,1)S(1)} %collective-permute-done.refs_0_, bf16[40,1024]{1,0:T(8,128)(2,1)S(1)} %collective-permute-done.1.refs_1_, bf16[80,1024]{1,0:T(8,128)(2,1)S(1)} %collective-permute-done.2.refs_2_, bf16[40,1024]{1,0:T(8,128)(2,1)S(1)} %get-tuple-element.41.refs_3_, ...), custom_call_target="tpu_custom_call" | custom-call | flops 251658240 | bytes 3145728 | tf_op jit(solution)/shard_map/pallas_call | solution.py:49
  22.1 0.7 %shard_map.89 = (bf16[80,1024]{1,0:T(8,128)(2,1)S(1)}, bf16[80,768]{1,0:T(8,128)(2,1)S(1)}) custom-call(bf16[40,1024]{1,0:T(8,128)(2,1)S(1)} %collective-permute-done.refs_0_, bf16[40,1024]{1,0:T(8,128)(2,1)S(1)} %collective-permute-done.1.refs_1_, bf16[80,1024]{1,0:T(8,128)(2,1)S(1)} %collective-permute-done.2.refs_2_, ...), custom_call_target="tpu_custom_call" | custom-call | flops 25165824000 | bytes 314572800 | tf_op jit(solution)/shard_map/pallas_call | solution.py:49
  22.8 0.6 %collective-permute-done.6 = bf16[80,768]{1,0:T(8,128)(2,1)S(1)} collective-permute-done((bf16[80,768]{1,0:T(8,128)(2,1)S(1)}, bf16[80,768]{1,0:T(8,128)(2,1)S(1)}, u32[]{:S(2)}, u32[]{:S(2)}) %collective-permute-start.6) | collective-permute-done | bytes 122912 | tf_op jit(solution)/shard_map/ppermute | solution.py:248
  23.5 1.6 %collective-permute-start.7 = (bf16[80,768]{1,0:T(8,128)(2,1)S(1)}, bf16[80,768]{1,0:T(8,128)(2,1)S(1)}, u32[]{:S(2)}, u32[]{:S(2)}) collective-permute-start(bf16[80,768]{1,0:T(8,128)(2,1)S(1)} %get-tuple-element.63), channel_id=1, source_target_pairs={{0,2},{1,3},{2,0},{3,1},{4,6},{5,7},{6,4},{7,5},{8,10},{9,11},{10,... | collective-permute-start | bytes 368648 | tf_op jit(solution)/shard_map/ppermute | solution.py:248
  25.0 3.3 %collective-permute-done.8.pair_far = bf16[2,80,768]{2,1,0:T(8,128)(2,1)S(1)} collective-permute-done((bf16[2,80,768]{2,1,0:T(8,128)(2,1)S(1)}, bf16[2,80,768]{2,1,0:T(8,128)(2,1)S(1)}, u32[]{:S(2)}, u32[]{:S(2)}) %collective-permute-start.8) | collective-permute-done | bytes 245792 | tf_op jit(solution)/shard_map/ppermute | solution.py:248
  28.5 1.6 %collective-permute-done.7.act_far = bf16[80,768]{1,0:T(8,128)(2,1)S(1)} collective-permute-done((bf16[80,768]{1,0:T(8,128)(2,1)S(1)}, bf16[80,768]{1,0:T(8,128)(2,1)S(1)}, u32[]{:S(2)}, u32[]{:S(2)}) %collective-permute-start.7) | collective-permute-done | bytes 122912 | tf_op jit(solution)/shard_map/ppermute | solution.py:248
  30.3 0.7 %shard_map.94.total = f32[80,1024]{1,0:T(8,128)S(1)} custom-call(bf16[2,80,768]{2,1,0:T(8,128)(2,1)S(1)} %shard_map.93.mine, bf16[3,768,1024]{2,1,0:T(8,128)(2,1)S(1)} %get-tuple-element.47.refs_5_.held), custom_call_target="tpu_custom_call" | custom-call | flops 251658240 | bytes 3145728 | tf_op jit(solution)/shard_map/pallas_call | solution.py:49
  31.0 0.8 %collective-permute-done.10.other = bf16[2,80,768]{2,1,0:T(8,128)(2,1)S(1)} collective-permute-done((bf16[2,80,768]{2,1,0:T(8,128)(2,1)S(1)}, bf16[2,80,768]{2,1,0:T(8,128)(2,1)S(1)}, u32[]{:S(2)}, u32[]{:S(2)}) %collective-permute-start.10) | collective-permute-done | bytes 245792 | tf_op jit(solution)/shard_map/ppermute | solution.py:248
  31.8 0.8 %shard_map.95 = (bf16[40,1024]{1,0:T(8,128)(2,1)S(1)}, bf16[40,1024]{1,0:T(8,128)(2,1)S(1)}, bf16[40,1024]{1,0:T(8,128)(2,1)S(1)}, bf16[40,1024]{1,0:T(8,128)(2,1)S(1)}) custom-call(f32[80,1024]{1,0:T(8,128)S(1)} %shard_map.94.total, bf16[2,80,768]{2,1,0:T(8,128)(2,1)S(1)} %collective-permute-done.10.other, ...), custom_call_target="tpu_custom_call" | custom-call | flops 251658240 | bytes 3145728 | tf_op jit(solution)/shard_map/pallas_call | solution.py:49
  32.7 1.5 %collective-permute-start.11 = (bf16[40,1024]{1,0:T(8,128)(2,1)S(1)}, bf16[40,1024]{1,0:T(8,128)(2,1)S(1)}, u32[]{:S(2)}, u32[]{:S(2)}) collective-permute-start(bf16[40,1024]{1,0:T(8,128)(2,1)S(1)} %get-tuple-element.54), channel_id=1, source_target_pairs={{0,8},{4,12},{8,0},{12,4},{1,9},{5,13},{9,1},{13,5},{2,10},{6,14},... | collective-permute-start | bytes 245768 | tf_op jit(solution)/shard_map/ppermute | solution.py:248
  34.1 1.9 %collective-permute-start.12 = (bf16[40,1024]{1,0:T(8,128)(2,1)S(1)}, bf16[40,1024]{1,0:T(8,128)(2,1)S(1)}, u32[]{:S(2)}, u32[]{:S(2)}) collective-permute-start(bf16[40,1024]{1,0:T(8,128)(2,1)S(1)} %get-tuple-element.55), channel_id=1, source_target_pairs={{0,12},{4,8},{8,4},{12,0},{1,13},{5,9},{9,5},{13,1},{2,14},{6,10},... | collective-permute-start | bytes 245768 | tf_op jit(solution)/shard_map/ppermute | solution.py:248
  36.5 4.1 %shard_map.97 = (bf16[1,2,1536,1024]{3,2,1,0:T(8,128)(2,1)}, bf16[1,1536,1024]{2,1,0:T(8,128)(2,1)}) custom-call(bf16[80,768]{1,0:T(8,128)(2,1)S(1)} %get-tuple-element.53.mine_act, bf16[80,768]{1,0:T(8,128)(2,1)S(1)} %collective-permute-done.9._.other_act, bf16[2,80,768]{2,1,0:T(8,128)(2,1)S(1)} %shard_map.93.mine, ...), custom_call_target="tpu_custom_call" | custom-call | flops 754974720 | bytes 9437184 | tf_op jit(solution)/shard_map/pallas_call | solution.py:49
  40.6 1.7 %collective-permute-done.11.refs_0_ = bf16[40,1024]{1,0:T(8,128)(2,1)S(1)} collective-permute-done((bf16[40,1024]{1,0:T(8,128)(2,1)S(1)}, bf16[40,1024]{1,0:T(8,128)(2,1)S(1)}, u32[]{:S(2)}, u32[]{:S(2)}) %collective-permute-start.11) | collective-permute-done | bytes 81952 | tf_op jit(solution)/shard_map/ppermute | solution.py:248
  42.3 0.7 %collective-permute-done.13.refs_2_ = bf16[40,1024]{1,0:T(8,128)(2,1)S(1)} collective-permute-done((bf16[40,1024]{1,0:T(8,128)(2,1)S(1)}, bf16[40,1024]{1,0:T(8,128)(2,1)S(1)}, u32[]{:S(2)}, u32[]{:S(2)}) %collective-permute-start.13) | collective-permute-done | bytes 81952 | tf_op jit(solution)/shard_map/ppermute | solution.py:248
  43.0 1.1 %shard_map.96 = bf16[256,1024]{1,0:T(8,128)(2,1)} custom-call(bf16[160,256]{1,0:T(8,128)(2,1)S(1)} %get-tuple-element.32.pick, bf16[40,1024]{1,0:T(8,128)(2,1)S(1)} %collective-permute-done.11.refs_0_, bf16[40,1024]{1,0:T(8,128)(2,1)S(1)} %collective-permute-done.12.refs_1_, bf16[40,1024]{1,0:T(8,128)(2,1)S(1)} %collective-permute-done.13.refs_2_, ...), custom_call_target="tpu_custom_call" | custom-call | flops 83886080 | bytes 1048576 | tf_op jit(solution)/shard_map/pallas_call | solution.py:49
  (19 shorter events, 2.2 us)
Async XLA Ops:
  2.1 14.2 %collective-permute-start.3 = (bf16[40,1024]{1,0:T(8,128)(2,1)S(1)}, bf16[40,1024]{1,0:T(8,128)(2,1)S(1)}, u32[]{:S(2)}, u32[]{:S(2)}) collective-permute-start(bf16[40,1024]{1,0:T(8,128)(2,1)S(1)} %get-tuple-element.42), channel_id=1, source_target_pairs={{0,8},{4,12},{8,0},{12,4},{1,9},{5,13},{9,1},{13,5},{2,10},{6,14},... | collective-permute-start | bytes 245768 | tf_op jit(solution)/shard_map/ppermute | solution.py:248
  6.2 10.1 %collective-permute-start.4 = (bf16[40,1024]{1,0:T(8,128)(2,1)S(1)}, bf16[40,1024]{1,0:T(8,128)(2,1)S(1)}, u32[]{:S(2)}, u32[]{:S(2)}) collective-permute-start(bf16[40,1024]{1,0:T(8,128)(2,1)S(1)} %get-tuple-element.43), channel_id=1, source_target_pairs={{0,12},{4,8},{8,4},{12,0},{1,13},{5,9},{9,5},{13,1},{2,14},{6,10},... | collective-permute-start | bytes 245768 | tf_op jit(solution)/shard_map/ppermute | solution.py:248
  7.8 8.6 %collective-permute-start.2 = (bf16[80,1024]{1,0:T(8,128)(2,1)S(1)}, bf16[80,1024]{1,0:T(8,128)(2,1)S(1)}, u32[]{:S(2)}, u32[]{:S(2)}) collective-permute-start(bf16[80,1024]{1,0:T(8,128)(2,1)S(1)} %get-tuple-element.40), channel_id=1, source_target_pairs={{0,4},{4,0},{8,12},{12,8},{1,5},{5,1},{9,13},{13,9},{2,6},{6,2},{1... | collective-permute-start | bytes 491528 | tf_op jit(solution)/shard_map/ppermute | solution.py:248
  12.1 9.1 %collective-permute-start = (bf16[40,1024]{1,0:T(8,128)(2,1)S(1)}, bf16[40,1024]{1,0:T(8,128)(2,1)S(1)}, u32[]{:S(2)}, u32[]{:S(2)}) collective-permute-start(bf16[40,1024]{1,0:T(8,128)(2,1)S(1)} %get-tuple-element.38), channel_id=1, source_target_pairs={{0,8},{4,12},{8,0},{12,4},{1,9},{5,13},{9,1},{13,5},{2,10},{6,14},... | collective-permute-start | bytes 245768 | tf_op jit(solution)/shard_map/ppermute | solution.py:248
  15.0 6.3 %collective-permute-start.1 = (bf16[40,1024]{1,0:T(8,128)(2,1)S(1)}, bf16[40,1024]{1,0:T(8,128)(2,1)S(1)}, u32[]{:S(2)}, u32[]{:S(2)}) collective-permute-start(bf16[40,1024]{1,0:T(8,128)(2,1)S(1)} %get-tuple-element.39), channel_id=1, source_target_pairs={{0,12},{4,8},{8,4},{12,0},{1,13},{5,9},{9,5},{13,1},{2,14},{6,10},... | collective-permute-start | bytes 245768 | tf_op jit(solution)/shard_map/ppermute | solution.py:248
  17.8 1.6 %collective-permute-start.5 = (bf16[2,80,768]{2,1,0:T(8,128)(2,1)S(1)}, bf16[2,80,768]{2,1,0:T(8,128)(2,1)S(1)}, u32[]{:S(2)}, u32[]{:S(2)}) collective-permute-start(bf16[2,80,768]{2,1,0:T(8,128)(2,1)S(1)} %get-tuple-element.50), channel_id=1, source_target_pairs={{0,1},{1,0},{2,3},{3,2},{4,5},{5,4},{6,7},{7,6},{8,9},{9,8},{10,11... | collective-permute-start | bytes 737288 | tf_op jit(solution)/shard_map/ppermute | solution.py:248
  19.5 8.9 %collective-permute-start.8 = (bf16[2,80,768]{2,1,0:T(8,128)(2,1)S(1)}, bf16[2,80,768]{2,1,0:T(8,128)(2,1)S(1)}, u32[]{:S(2)}, u32[]{:S(2)}) collective-permute-start(bf16[2,80,768]{2,1,0:T(8,128)(2,1)S(1)} %get-tuple-element.62.refs_6_), channel_id=1, source_target_pairs={{0,2},{1,3},{2,0},{3,1},{4,6},{5,7},{6,4},{7,5},{8,10},{9,11},{10,... | collective-permute-start | bytes 737288 | tf_op jit(solution)/shard_map/ppermute | solution.py:248
  22.0 1.4 %collective-permute-start.6 = (bf16[80,768]{1,0:T(8,128)(2,1)S(1)}, bf16[80,768]{1,0:T(8,128)(2,1)S(1)}, u32[]{:S(2)}, u32[]{:S(2)}) collective-permute-start(bf16[80,768]{1,0:T(8,128)(2,1)S(1)} %shard_map.91), channel_id=1, source_target_pairs={{0,1},{1,0},{2,3},{3,2},{4,5},{5,4},{6,7},{7,6},{8,9},{9,8},{10,11... | collective-permute-start | bytes 368648 | tf_op jit(solution)/shard_map/ppermute | solution.py:248
  23.5 6.7 %collective-permute-start.7 = (bf16[80,768]{1,0:T(8,128)(2,1)S(1)}, bf16[80,768]{1,0:T(8,128)(2,1)S(1)}, u32[]{:S(2)}, u32[]{:S(2)}) collective-permute-start(bf16[80,768]{1,0:T(8,128)(2,1)S(1)} %get-tuple-element.63), channel_id=1, source_target_pairs={{0,2},{1,3},{2,0},{3,1},{4,6},{5,7},{6,4},{7,5},{8,10},{9,11},{10,... | collective-permute-start | bytes 368648 | tf_op jit(solution)/shard_map/ppermute | solution.py:248
  28.5 1.7 %collective-permute-start.9 = (bf16[80,768]{1,0:T(8,128)(2,1)S(1)}, bf16[80,768]{1,0:T(8,128)(2,1)S(1)}, u32[]{:S(2)}, u32[]{:S(2)}) collective-permute-start(bf16[80,768]{1,0:T(8,128)(2,1)S(1)} %get-tuple-element.53.mine_act), channel_id=1, source_target_pairs={{0,1},{1,0},{2,3},{3,2},{4,5},{5,4},{6,7},{7,6},{8,9},{9,8},{10,11... | collective-permute-start | bytes 368648 | tf_op jit(solution)/shard_map/ppermute | solution.py:248
  30.2 1.6 %collective-permute-start.10 = (bf16[2,80,768]{2,1,0:T(8,128)(2,1)S(1)}, bf16[2,80,768]{2,1,0:T(8,128)(2,1)S(1)}, u32[]{:S(2)}, u32[]{:S(2)}) collective-permute-start(bf16[2,80,768]{2,1,0:T(8,128)(2,1)S(1)} %shard_map.93.mine), channel_id=1, source_target_pairs={{0,1},{1,0},{2,3},{3,2},{4,5},{5,4},{6,7},{7,6},{8,9},{9,8},{10,11... | collective-permute-start | bytes 737288 | tf_op jit(solution)/shard_map/ppermute | solution.py:248
  32.7 9.6 %collective-permute-start.11 = (bf16[40,1024]{1,0:T(8,128)(2,1)S(1)}, bf16[40,1024]{1,0:T(8,128)(2,1)S(1)}, u32[]{:S(2)}, u32[]{:S(2)}) collective-permute-start(bf16[40,1024]{1,0:T(8,128)(2,1)S(1)} %get-tuple-element.54), channel_id=1, source_target_pairs={{0,8},{4,12},{8,0},{12,4},{1,9},{5,13},{9,1},{13,5},{2,10},{6,14},... | collective-permute-start | bytes 245768 | tf_op jit(solution)/shard_map/ppermute | solution.py:248
  34.1 8.2 %collective-permute-start.12 = (bf16[40,1024]{1,0:T(8,128)(2,1)S(1)}, bf16[40,1024]{1,0:T(8,128)(2,1)S(1)}, u32[]{:S(2)}, u32[]{:S(2)}) collective-permute-start(bf16[40,1024]{1,0:T(8,128)(2,1)S(1)} %get-tuple-element.55), channel_id=1, source_target_pairs={{0,12},{4,8},{8,4},{12,0},{1,13},{5,9},{9,5},{13,1},{2,14},{6,10},... | collective-permute-start | bytes 245768 | tf_op jit(solution)/shard_map/ppermute | solution.py:248
  36.0 7.0 %collective-permute-start.13 = (bf16[40,1024]{1,0:T(8,128)(2,1)S(1)}, bf16[40,1024]{1,0:T(8,128)(2,1)S(1)}, u32[]{:S(2)}, u32[]{:S(2)}) collective-permute-start(bf16[40,1024]{1,0:T(8,128)(2,1)S(1)} %get-tuple-element.56), channel_id=1, source_target_pairs={{0,4},{4,0},{8,12},{12,8},{1,5},{5,1},{9,13},{13,9},{2,6},{6,2},{1... | collective-permute-start | bytes 245768 | tf_op jit(solution)/shard_map/ppermute | solution.py:248

commit v8 on v7

--- a/solution.py
+++ b/solution.py
@@ -35,7 +35,7 @@
 
 
 def far_first(count):
-    return sorted(range(count), key=lambda k: (-k.bit_length(), k))
+    return list(reversed(range(count)))
 
 
 def block_of(position, names):
@@ -101,21 +101,14 @@
     loads[3].wait()
 
 
-def pick_grads(experts, pick, prob, grads, near_in, near, *pieces):
+def pick_grads(experts, pick, prob, grads, *pieces):
     sent = mm(pick[...], grads[...]) * prob[...]
-    for at, k in enumerate(far_first(experts)):
-        rows = sent[at * MOST : (at + 1) * MOST]
-        if k == 1:
-            both = jnp.concatenate([near_in[...].astype(F32), rows], axis=0)
-            near[...] = both.astype(BF)
-        else:
-            pieces[at if k else at - 1][...] = rows.astype(BF)
-
-
-def stacked(pieces, part=0):
-    rows = [piece[...].astype(F32) for piece in pieces]
-    rows = [row[part * MOST : (part + 1) * MOST] if row.shape[0] > MOST else row for row in rows]
-    return jnp.concatenate(rows, axis=0)
+    for k in range(experts):
+        pieces[k][...] = sent[k * MOST : (k + 1) * MOST].astype(BF)
+
+
+def stacked(pieces):
+    return jnp.concatenate([piece[...].astype(F32) for piece in pieces], axis=0)
 
 
 def rows_of(half, own):
@@ -140,16 +133,14 @@
     return place, mm(place, got.astype(BF), ROWS).astype(BF)
 
 
-def stage(far_count, gate_up, down, *refs):
+def stage(far_count, gate_up, *refs):
     pieces, refs = refs[:far_count], refs[far_count:]
     held, pieces_out, sems = refs[:2], refs[2:-1], refs[-1]
-    half = down.shape[1] // 2
+    half = gate_up.shape[2] // 2
     moves = list(zip(pieces, pieces_out))
     for own, out in enumerate(held):
-        rows = rows_of(half, own == 1)
-        for matrix in range(3):
-            source = down.at[0, rows] if matrix == 2 else gate_up.at[0, matrix, rows]
-            moves.append((source, out.at[matrix]))
+        for matrix in range(2):
+            moves.append((gate_up.at[0, matrix, rows_of(half, own == 1)], out.at[matrix]))
     loads = [
         pltpu.make_async_copy(source, target, sems.at[at]) for at, (source, target) in enumerate(moves)
     ]
@@ -159,26 +150,44 @@
         load.wait()
 
 
+def load_down(down, own, out, sem):
+    half = down.shape[1] // 2
+    return pltpu.make_async_copy(down.at[0, rows_of(half, own)], out, sem)
+
+
 def other_pair(experts, capacity, *refs):
-    held, out, place_out, rows_out = refs[experts:]
+    held, down, near, out, place_out, rows_out, down_out, near_out, sem = refs[experts:]
+    near_out[...] = near[...]
+    load = load_down(down, False, down_out, sem)
+    load.start()
     place, rows_in = place_rows(experts, capacity, refs[:experts])
     place_out[...] = place
     rows_out[...] = rows_in
     for matrix in range(2):
         out[matrix] = mm(rows_in, held[matrix], LANES).astype(BF)
-
-
-def mine_pair(rows_in, held, out):
+    load.wait()
+
+
+def mine_pair(rows_in, held, down, out, down_out, sem):
+    load = load_down(down, True, down_out, sem)
+    load.start()
     for matrix in range(2):
         out[matrix] = mm(rows_in[...], held[matrix], LANES).astype(BF)
+    load.wait()
+
+
+def pair_sum(mine, other, held_out, sent_out):
+    held = mine[...].astype(F32) + other[...].astype(F32)
+    held_out[...] = held
+    sent_out[...] = held.astype(BF)
 
 
 def act_part(experts, own, *refs):
     place, held = refs[experts : experts + 2]
-    rows_grad = mm(place[...], stacked(refs[:experts], 1).astype(BF), ROWS).astype(BF)
+    rows_grad = mm(place[...], stacked(refs[:experts]).astype(BF), ROWS).astype(BF)
     if own:
         refs[-2][...] = rows_grad
-    refs[-1][...] = mm(rows_grad, held[2], LANES).astype(BF)
+    refs[-1][...] = mm(rows_grad, held[...], LANES).astype(BF)
 
 
 def gates(pair, pair_far, act_out, by_gate, by_up):
@@ -288,58 +297,66 @@
         flops=2 * rows * tokens * width,
         traffic=4 * tokens * width,
     )
-    near, *send_grad = call(
+    send_grad = call(
         functools.partial(pick_grads, experts),
-        [sds((2 * MOST, width), BF)] + piece[1:],
-        (pick, prob, grads, send_in[-2]),
-        [VMEM] * 4,
+        piece,
+        (pick, prob, grads),
+        [VMEM] * 3,
         flops=2 * rows * tokens * width,
         traffic=2 * tokens * width,
     )
-    got_in = [swap(send_in[at], "ex", order[at]) for at in range(far_count)]
-    near = swap(near, "ex", 1)
-    got_in = got_in + [near, send_in[-1]]
+    got_in = exchange(send_in, "ex")
     held_other, held_mine, *far_grad = call(
         functools.partial(stage, far_count),
-        [pltpu.VMEM((3, half, width), BF)] * 2 + piece[2:],
-        (far(gate_up), far(down_proj), *send_grad[:-1]),
-        [HBM] * 2 + [VMEM] * far_count,
-        [dma(far_count + 6)],
+        [pltpu.VMEM((2, half, width), BF)] * 2 + piece[2:],
+        (far(gate_up), *send_grad[:far_count]),
+        [HBM] + [VMEM] * far_count,
+        [dma(far_count + 4)],
         flops=WCOST * weight_flops,
         traffic=WCOST * weight_bytes,
     )
     got_grad = [swap(far_grad[at], "ex", order[at]) for at in range(far_count)]
-    got_grad = got_grad + [near, send_grad[-1]]
-    sent = []
-
-    pair_other, place, rows_in = call(
+
+    one_dma = pltpu.SemaphoreType.DMA
+    down_half = pltpu.VMEM((half, width), BF)
+    pair_other, place, rows_in, down_other, near_grad = call(
         functools.partial(other_pair, experts, capacity),
-        [sds((2, capacity, half), BF), sds((rows, capacity), BF), sds((capacity, width), BF)],
-        (*got_in, held_other),
-        [VMEM] * (experts + 1),
+        [sds((2, capacity, half), BF), sds((rows, capacity), BF), sds((capacity, width), BF)]
+        + [down_half, piece[0]],
+        (*got_in, held_other, far(down_proj), send_grad[-2]),
+        [VMEM] * (experts + 1) + [HBM, VMEM],
+        [one_dma],
         flops=2 * weight_flops,
         traffic=weight_bytes,
     )
-    pair_mine = call(
+    pair_mine, down_mine = call(
         mine_pair,
-        sds((2, capacity, half), BF),
-        (rows_in, held_mine),
-        [VMEM] * 2,
+        [sds((2, capacity, half), BF), down_half],
+        (rows_in, held_mine, far(down_proj)),
+        [VMEM] * 2 + [HBM],
+        [one_dma],
         flops=C2COST * weight_flops,
         traffic=C2COST * weight_bytes,
     )
 
-    def total(held):
+    def total(held, sent):
         bit = 2
         while bit * 2 < ways:
-            held = held + swap(held.astype(BF), "ey", bit).astype(F32)
+            held = held + swap(sent, "ey", bit).astype(F32)
+            sent = held.astype(BF)
             bit *= 2
-        sent.append(held.astype(BF))
-        return held, swap(sent[-1], "ey", bit)
-
-
-    pair = pair_mine.astype(F32) + swap(pair_other, "ey", 1).astype(F32)
-    pair, pair_far = total(pair)
+        return held, swap(sent, "ey", bit)
+
+    pair, pair_sent = call(
+        pair_sum,
+        [sds((2, capacity, half), F32), sds((2, capacity, half), BF)],
+        (pair_mine, swap(pair_other, "ey", 1)),
+        [VMEM] * 2,
+        traffic=10 * capacity * hidden,
+    )
+    pair, pair_far = total(pair, pair_sent)
+    got_grad = got_grad + [swap(near_grad, "ex", 1), send_grad[-1]]
+
     def act_of(own, held, outs, tied, cost):
         return call(
             functools.partial(act_part, experts, own),
@@ -350,9 +367,10 @@
             traffic=cost * weight_bytes,
         )
 
-    (act_other,) = act_of(False, held_other, [], sent[-1:], D1COST)
-    rows_grad, act_mine = act_of(True, held_mine, [sds((capacity, width), BF)], [], D2COST)
-    act, act_far = total(act_mine.astype(F32) + swap(act_other, "ey", 1).astype(F32))
+    (act_other,) = act_of(False, down_other, [], [pair_sent], D1COST)
+    rows_grad, act_mine = act_of(True, down_mine, [sds((capacity, width), BF)], [], D2COST)
+    act = act_mine.astype(F32) + swap(act_other, "ey", 1).astype(F32)
+    act, act_far = total(act, act.astype(BF))
     mine_act, by_gate, by_up = call(
         gates,
         [sds((capacity, half), BF)] + [sds((capacity, half), F32)] * 2,

time: 44.4 us -> 46.4 us (1.045)
  Pallas kernels: 16.6 us -> 18.3 us
  starting transfers between devices: 17.3 us -> 18.3 us
  waiting for transfers between devices: 9.41 us -> 8.92 us
    pallas_call x13 -> x14, Pallas kernels: 16.6 us -> 18.3 us  [call(): pl.pallas_call(body, out_shape=outs, in_specs=specs, out_specs=out_specs...]
    ppermute x14 -> x15, starting transfers between devices: 17.3 us -> 18.3 us  [swap(): return lax.ppermute(value, axis, [(i, i ^ bit) for i in range(count)])]
    ppermute x14 -> x15, waiting for transfers between devices: 9.41 us -> 8.92 us  [swap(): return lax.ppermute(value, axis, [(i, i ^ bit) for i in range(count)])]
  transfers between devices with their start and end apart: 14 -> 15, of which waited for: 8 -> 5; matrix products, arithmetic and copies ran while one was open for 0% -> 0% of each run, Pallas kernels for 30% -> 32%
where the time goes in v8:
time: 46.4 us; the launch traced here: 46.2 us
  Pallas kernels  18.3 us (39%)
  starting transfers between devices  18.3 us (39%)
  waiting for transfers between devices  8.92 us (19%)
  between operations  0.77 us (2%)
    ppermute x15, starting transfers between devices, swap(): return lax.ppermute(value, axis, [(i, i ^ bit) for i in range(count)])  18.3 us
    pallas_call x14, Pallas kernels, call(): pl.pallas_call(body, out_shape=outs, in_specs=specs, out_specs=out_specs...  18.3 us
    ppermute x15, waiting for transfers between devices, swap(): return lax.ppermute(value, axis, [(i, i ^ bit) for i in range(count)])  8.92 us
  transfers between devices with their start and end apart: 15, of which 5 were waited for; matrix products, arithmetic and copies ran while one was open for 0% of the time, Pallas kernels for 32%

profile of v8, /device:TPU:0, one launch (start us, length us, event | category | flops | bytes accessed | tf_op | source)
XLA Modules:
  0.0 46.2 jit_solution(8884643032914548438)
XLA Ops:
  0.6 1.5 %shard_map.85 = (bf16[160,256]{1,0:T(8,128)(2,1)S(1)}, f32[160,1]{1,0:T(8,128)S(1)}, bf16[256,1024]{1,0:T(8,128)(2,1)S(1)}, bf16[40,1024]{1,0:T(8,128)(2,1)S(1)}...) custom-call(s32[8,256]{1,0:T(8,128)} %bitcast.2, ...), custom_call_target="tpu_custom_call" | custom-call | flops 83886080 | bytes 1048576 | tf_op jit(solution)/shard_map/pallas_call | solution.py:49
  2.1 5.1 %collective-permute-start.2 = (bf16[40,1024]{1,0:T(8,128)(2,1)S(1)}, bf16[40,1024]{1,0:T(8,128)(2,1)S(1)}, u32[]{:S(2)}, u32[]{:S(2)}) collective-permute-start(bf16[40,1024]{1,0:T(8,128)(2,1)S(1)} %get-tuple-element.45), channel_id=1, source_target_pairs={{0,12},{4,8},{8,4},{12,0},{1,13},{5,9},{9,5},{13,1},{2,14},{6,10},... | collective-permute-start | bytes 245768 | tf_op jit(solution)/shard_map/ppermute | solution.py:257
  7.2 0.6 %collective-permute-start.4 = (bf16[40,1024]{1,0:T(8,128)(2,1)S(1)}, bf16[40,1024]{1,0:T(8,128)(2,1)S(1)}, u32[]{:S(2)}, u32[]{:S(2)}) collective-permute-start(bf16[40,1024]{1,0:T(8,128)(2,1)S(1)} %get-tuple-element.47), channel_id=1, source_target_pairs={{0,4},{4,0},{8,12},{12,8},{1,5},{5,1},{9,13},{13,9},{2,6},{6,2},{1... | collective-permute-start | bytes 245768 | tf_op jit(solution)/shard_map/ppermute | solution.py:257
  8.1 3.1 %shard_map.87 = (bf16[2,768,1024]{2,1,0:T(8,128)(2,1)S(1)}, bf16[2,768,1024]{2,1,0:T(8,128)(2,1)S(1)}, bf16[40,1024]{1,0:T(8,128)(2,1)S(1)}, bf16[40,1024]{1,0:T(8,128)(2,1)S(1)}) custom-call(bf16[1,2,1536,1024]{3,2,1,0:T(8,128)(2,1)} %gate_up.1, bf16[40,1024]{1,0:T(8,128)(2,1)S(1)} %get-tuple-element.41.refs_0_, bf16[40,1024]{1,0:T(8,128)(2,1)S(1)} %get-tuple-element.42.refs_1_), custom_call_target="tpu_custom_call" | custom-call | flops 25165824000 | bytes 314572800 | tf_op jit(solution)/shard_map/pallas_call | solution.py:49
  11.3 3.8 %collective-permute-start = (bf16[40,1024]{1,0:T(8,128)(2,1)S(1)}, bf16[40,1024]{1,0:T(8,128)(2,1)S(1)}, u32[]{:S(2)}, u32[]{:S(2)}) collective-permute-start(bf16[40,1024]{1,0:T(8,128)(2,1)S(1)} %get-tuple-element.43), channel_id=1, source_target_pairs={{0,12},{4,8},{8,4},{12,0},{1,13},{5,9},{9,5},{13,1},{2,14},{6,10},... | collective-permute-start | bytes 245768 | tf_op jit(solution)/shard_map/ppermute | solution.py:257
  15.1 2.7 %shard_map.88 = (bf16[2,80,768]{2,1,0:T(8,128)(2,1)S(1)}, bf16[160,80]{1,0:T(8,128)(2,1)S(1)}, bf16[80,1024]{1,0:T(8,128)(2,1)S(1)}, bf16[768,1024]{1,0:T(8,128)(2,1)S(1)}, bf16[40,1024]{1,0:T(8,128)(2,1)S(1)}) custom-call(bf16[40,1024]{1,0:T(8,128)(2,1)S(1)} %collective-permute-done.2.refs_0_, bf16[40,1024]{1,0:T(8,128)(2,1)S(1)} %collective-permute-done.3.refs_1_, ...), custom_call_target="tpu_custom_call" | custom-call | flops 503316480 | bytes 3145728 | tf_op jit(solution)/shard_map/pallas_call | solution.py:49
  17.8 0.7 %collective-permute-start.5 = (bf16[40,1024]{1,0:T(8,128)(2,1)S(1)}, bf16[40,1024]{1,0:T(8,128)(2,1)S(1)}, u32[]{:S(2)}, u32[]{:S(2)}) collective-permute-start(bf16[40,1024]{1,0:T(8,128)(2,1)S(1)} %get-tuple-element.51), channel_id=1, source_target_pairs={{0,4},{4,0},{8,12},{12,8},{1,5},{5,1},{9,13},{13,9},{2,6},{6,2},{1... | collective-permute-start | bytes 245768 | tf_op jit(solution)/shard_map/ppermute | solution.py:257
  18.5 2.3 %shard_map.89 = (bf16[2,80,768]{2,1,0:T(8,128)(2,1)S(1)}, bf16[768,1024]{1,0:T(8,128)(2,1)S(1)}) custom-call(bf16[80,1024]{1,0:T(8,128)(2,1)S(1)} %get-tuple-element.54.rows_in, bf16[2,768,1024]{2,1,0:T(8,128)(2,1)S(1)} %get-tuple-element.55.held, bf16[1,1536,1024]{2,1,0:T(8,128)(2,1)} %down.1), custom_call_target="tpu_custom_call" | custom-call | flops 25165824000 | bytes 314572800 | tf_op jit(solution)/shard_map/pallas_call | solution.py:49
  20.9 1.7 %collective-permute-start.9 = (bf16[2,80,768]{2,1,0:T(8,128)(2,1)S(1)}, bf16[2,80,768]{2,1,0:T(8,128)(2,1)S(1)}, u32[]{:S(2)}, u32[]{:S(2)}) collective-permute-start(bf16[2,80,768]{2,1,0:T(8,128)(2,1)S(1)} %get-tuple-element.61.refs_6_), channel_id=1, source_target_pairs={{0,2},{1,3},{2,0},{3,1},{4,6},{5,7},{6,4},{7,5},{8,10},{9,11},{10,... | collective-permute-start | bytes 737288 | tf_op jit(solution)/shard_map/ppermute | solution.py:257
  22.6 0.7 %shard_map.92 = bf16[80,768]{1,0:T(8,128)(2,1)S(1)} custom-call(bf16[40,1024]{1,0:T(8,128)(2,1)S(1)} %collective-permute-done.refs_0_, bf16[40,1024]{1,0:T(8,128)(2,1)S(1)} %collective-permute-done.1.refs_1_, bf16[40,1024]{1,0:T(8,128)(2,1)S(1)} %collective-permute-done.5.refs_2_, bf16[40,1024]{1,0:T(8,128)(2,1)S(1)} %get-tuple-element.52.refs_3_, ...), custom_call_target="tpu_custom_call" | custom-call | flops 251658240 | bytes 3145728 | tf_op jit(solution)/shard_map/pallas_call | solution.py:49
  23.3 0.3 collective-permute-start.7
  23.6 0.7 %shard_map.90 = (bf16[80,1024]{1,0:T(8,128)(2,1)S(1)}, bf16[80,768]{1,0:T(8,128)(2,1)S(1)}) custom-call(bf16[40,1024]{1,0:T(8,128)(2,1)S(1)} %collective-permute-done.refs_0_, bf16[40,1024]{1,0:T(8,128)(2,1)S(1)} %collective-permute-done.1.refs_1_, bf16[40,1024]{1,0:T(8,128)(2,1)S(1)} %collective-permute-done.5.refs_2_, ...), custom_call_target="tpu_custom_call" | custom-call | flops 25165824000 | bytes 314572800 | tf_op jit(solution)/shard_map/pallas_call | solution.py:49
  24.3 0.4 collective-permute-done.7
  24.8 1.4 %collective-permute-start.8 = (bf16[80,768]{1,0:T(8,128)(2,1)S(1)}, bf16[80,768]{1,0:T(8,128)(2,1)S(1)}, u32[]{:S(2)}, u32[]{:S(2)}) collective-permute-start(bf16[80,768]{1,0:T(8,128)(2,1)S(1)} %get-tuple-element.73), channel_id=1, source_target_pairs={{0,2},{1,3},{2,0},{3,1},{4,6},{5,7},{6,4},{7,5},{8,10},{9,11},{10,... | collective-permute-start | bytes 368648 | tf_op jit(solution)/shard_map/ppermute | solution.py:257
  26.2 3.6 %collective-permute-done.9.pair_far = bf16[2,80,768]{2,1,0:T(8,128)(2,1)S(1)} collective-permute-done((bf16[2,80,768]{2,1,0:T(8,128)(2,1)S(1)}, bf16[2,80,768]{2,1,0:T(8,128)(2,1)S(1)}, u32[]{:S(2)}, u32[]{:S(2)}) %collective-permute-start.9) | collective-permute-done | bytes 245792 | tf_op jit(solution)/shard_map/ppermute | solution.py:257
  29.9 2.0 %collective-permute-done.8.act_far = bf16[80,768]{1,0:T(8,128)(2,1)S(1)} collective-permute-done((bf16[80,768]{1,0:T(8,128)(2,1)S(1)}, bf16[80,768]{1,0:T(8,128)(2,1)S(1)}, u32[]{:S(2)}, u32[]{:S(2)}) %collective-permute-start.8) | collective-permute-done | bytes 122912 | tf_op jit(solution)/shard_map/ppermute | solution.py:257
  32.1 0.7 %shard_map.95.total = f32[80,1024]{1,0:T(8,128)S(1)} custom-call(bf16[2,80,768]{2,1,0:T(8,128)(2,1)S(1)} %shard_map.94.mine, bf16[2,768,1024]{2,1,0:T(8,128)(2,1)S(1)} %get-tuple-element.55.held), custom_call_target="tpu_custom_call" | custom-call | flops 251658240 | bytes 3145728 | tf_op jit(solution)/shard_map/pallas_call | solution.py:49
  32.8 0.8 %collective-permute-done.11.other = bf16[2,80,768]{2,1,0:T(8,128)(2,1)S(1)} collective-permute-done((bf16[2,80,768]{2,1,0:T(8,128)(2,1)S(1)}, bf16[2,80,768]{2,1,0:T(8,128)(2,1)S(1)}, u32[]{:S(2)}, u32[]{:S(2)}) %collective-permute-start.11) | collective-permute-done | bytes 245792 | tf_op jit(solution)/shard_map/ppermute | solution.py:257
  33.6 0.8 %shard_map.96 = (bf16[40,1024]{1,0:T(8,128)(2,1)S(1)}, bf16[40,1024]{1,0:T(8,128)(2,1)S(1)}, bf16[40,1024]{1,0:T(8,128)(2,1)S(1)}, bf16[40,1024]{1,0:T(8,128)(2,1)S(1)}) custom-call(f32[80,1024]{1,0:T(8,128)S(1)} %shard_map.95.total, bf16[2,80,768]{2,1,0:T(8,128)(2,1)S(1)} %collective-permute-done.11.other, ...), custom_call_target="tpu_custom_call" | custom-call | flops 251658240 | bytes 3145728 | tf_op jit(solution)/shard_map/pallas_call | solution.py:49
  34.5 3.8 %collective-permute-start.12 = (bf16[40,1024]{1,0:T(8,128)(2,1)S(1)}, bf16[40,1024]{1,0:T(8,128)(2,1)S(1)}, u32[]{:S(2)}, u32[]{:S(2)}) collective-permute-start(bf16[40,1024]{1,0:T(8,128)(2,1)S(1)} %get-tuple-element.66), channel_id=1, source_target_pairs={{0,12},{4,8},{8,4},{12,0},{1,13},{5,9},{9,5},{13,1},{2,14},{6,10},... | collective-permute-start | bytes 245768 | tf_op jit(solution)/shard_map/ppermute | solution.py:257
  38.3 0.6 %collective-permute-start.14 = (bf16[40,1024]{1,0:T(8,128)(2,1)S(1)}, bf16[40,1024]{1,0:T(8,128)(2,1)S(1)}, u32[]{:S(2)}, u32[]{:S(2)}) collective-permute-start(bf16[40,1024]{1,0:T(8,128)(2,1)S(1)} %get-tuple-element.68), channel_id=1, source_target_pairs={{0,4},{4,0},{8,12},{12,8},{1,5},{5,1},{9,13},{13,9},{2,6},{6,2},{1... | collective-permute-start | bytes 245768 | tf_op jit(solution)/shard_map/ppermute | solution.py:257
  38.9 4.1 %shard_map.98 = (bf16[1,2,1536,1024]{3,2,1,0:T(8,128)(2,1)}, bf16[1,1536,1024]{2,1,0:T(8,128)(2,1)}) custom-call(bf16[80,768]{1,0:T(8,128)(2,1)S(1)} %get-tuple-element.65.mine_act, bf16[80,768]{1,0:T(8,128)(2,1)S(1)} %collective-permute-done.10._.other_act, bf16[2,80,768]{2,1,0:T(8,128)(2,1)S(1)} %shard_map.94.mine, ...), custom_call_target="tpu_custom_call" | custom-call | flops 754974720 | bytes 9437184 | tf_op jit(solution)/shard_map/pallas_call | solution.py:49
  43.0 2.1 %collective-permute-done.13.refs_1_ = bf16[40,1024]{1,0:T(8,128)(2,1)S(1)} collective-permute-done((bf16[40,1024]{1,0:T(8,128)(2,1)S(1)}, bf16[40,1024]{1,0:T(8,128)(2,1)S(1)}, u32[]{:S(2)}, u32[]{:S(2)}) %collective-permute-start.13) | collective-permute-done | bytes 81952 | tf_op jit(solution)/shard_map/ppermute | solution.py:257
  45.1 1.1 %shard_map.97 = bf16[256,1024]{1,0:T(8,128)(2,1)} custom-call(bf16[160,256]{1,0:T(8,128)(2,1)S(1)} %get-tuple-element.38.pick, bf16[40,1024]{1,0:T(8,128)(2,1)S(1)} %collective-permute-done.12.refs_0_, bf16[40,1024]{1,0:T(8,128)(2,1)S(1)} %collective-permute-done.13.refs_1_, bf16[40,1024]{1,0:T(8,128)(2,1)S(1)} %collective-permute-done.14.refs_2_, ...), custom_call_target="tpu_custom_call" | custom-call | flops 83886080 | bytes 1048576 | tf_op jit(solution)/shard_map/pallas_call | solution.py:49
  (21 shorter events, 0.7 us)
Async XLA Ops:
  2.1 12.9 %collective-permute-start.2 = (bf16[40,1024]{1,0:T(8,128)(2,1)S(1)}, bf16[40,1024]{1,0:T(8,128)(2,1)S(1)}, u32[]{:S(2)}, u32[]{:S(2)}) collective-permute-start(bf16[40,1024]{1,0:T(8,128)(2,1)S(1)} %get-tuple-element.45), channel_id=1, source_target_pairs={{0,12},{4,8},{8,4},{12,0},{1,13},{5,9},{9,5},{13,1},{2,14},{6,10},... | collective-permute-start | bytes 245768 | tf_op jit(solution)/shard_map/ppermute | solution.py:257
  7.2 7.8 %collective-permute-start.3 = (bf16[40,1024]{1,0:T(8,128)(2,1)S(1)}, bf16[40,1024]{1,0:T(8,128)(2,1)S(1)}, u32[]{:S(2)}, u32[]{:S(2)}) collective-permute-start(bf16[40,1024]{1,0:T(8,128)(2,1)S(1)} %get-tuple-element.46), channel_id=1, source_target_pairs={{0,8},{4,12},{8,0},{12,4},{1,9},{5,13},{9,1},{13,5},{2,10},{6,14},... | collective-permute-start | bytes 245768 | tf_op jit(solution)/shard_map/ppermute | solution.py:257
  7.2 7.8 %collective-permute-start.4 = (bf16[40,1024]{1,0:T(8,128)(2,1)S(1)}, bf16[40,1024]{1,0:T(8,128)(2,1)S(1)}, u32[]{:S(2)}, u32[]{:S(2)}) collective-permute-start(bf16[40,1024]{1,0:T(8,128)(2,1)S(1)} %get-tuple-element.47), channel_id=1, source_target_pairs={{0,4},{4,0},{8,12},{12,8},{1,5},{5,1},{9,13},{13,9},{2,6},{6,2},{1... | collective-permute-start | bytes 245768 | tf_op jit(solution)/shard_map/ppermute | solution.py:257
  11.3 11.4 %collective-permute-start = (bf16[40,1024]{1,0:T(8,128)(2,1)S(1)}, bf16[40,1024]{1,0:T(8,128)(2,1)S(1)}, u32[]{:S(2)}, u32[]{:S(2)}) collective-permute-start(bf16[40,1024]{1,0:T(8,128)(2,1)S(1)} %get-tuple-element.43), channel_id=1, source_target_pairs={{0,12},{4,8},{8,4},{12,0},{1,13},{5,9},{9,5},{13,1},{2,14},{6,10},... | collective-permute-start | bytes 245768 | tf_op jit(solution)/shard_map/ppermute | solution.py:257
  15.1 7.6 %collective-permute-start.1 = (bf16[40,1024]{1,0:T(8,128)(2,1)S(1)}, bf16[40,1024]{1,0:T(8,128)(2,1)S(1)}, u32[]{:S(2)}, u32[]{:S(2)}) collective-permute-start(bf16[40,1024]{1,0:T(8,128)(2,1)S(1)} %get-tuple-element.44), channel_id=1, source_target_pairs={{0,8},{4,12},{8,0},{12,4},{1,9},{5,13},{9,1},{13,5},{2,10},{6,14},... | collective-permute-start | bytes 245768 | tf_op jit(solution)/shard_map/ppermute | solution.py:257
  17.8 4.8 %collective-permute-start.5 = (bf16[40,1024]{1,0:T(8,128)(2,1)S(1)}, bf16[40,1024]{1,0:T(8,128)(2,1)S(1)}, u32[]{:S(2)}, u32[]{:S(2)}) collective-permute-start(bf16[40,1024]{1,0:T(8,128)(2,1)S(1)} %get-tuple-element.51), channel_id=1, source_target_pairs={{0,4},{4,0},{8,12},{12,8},{1,5},{5,1},{9,13},{13,9},{2,6},{6,2},{1... | collective-permute-start | bytes 245768 | tf_op jit(solution)/shard_map/ppermute | solution.py:257
  18.5 2.3 %collective-permute-start.6 = (bf16[2,80,768]{2,1,0:T(8,128)(2,1)S(1)}, bf16[2,80,768]{2,1,0:T(8,128)(2,1)S(1)}, u32[]{:S(2)}, u32[]{:S(2)}) collective-permute-start(bf16[2,80,768]{2,1,0:T(8,128)(2,1)S(1)} %get-tuple-element.60), channel_id=1, source_target_pairs={{0,1},{1,0},{2,3},{3,2},{4,5},{5,4},{6,7},{7,6},{8,9},{9,8},{10,11... | collective-permute-start | bytes 737288 | tf_op jit(solution)/shard_map/ppermute | solution.py:257
  20.9 8.8 %collective-permute-start.9 = (bf16[2,80,768]{2,1,0:T(8,128)(2,1)S(1)}, bf16[2,80,768]{2,1,0:T(8,128)(2,1)S(1)}, u32[]{:S(2)}, u32[]{:S(2)}) collective-permute-start(bf16[2,80,768]{2,1,0:T(8,128)(2,1)S(1)} %get-tuple-element.61.refs_6_), channel_id=1, source_target_pairs={{0,2},{1,3},{2,0},{3,1},{4,6},{5,7},{6,4},{7,5},{8,10},{9,11},{10,... | collective-permute-start | bytes 737288 | tf_op jit(solution)/shard_map/ppermute | solution.py:257
  23.3 1.4 %collective-permute-start.7 = (bf16[80,768]{1,0:T(8,128)(2,1)S(1)}, bf16[80,768]{1,0:T(8,128)(2,1)S(1)}, u32[]{:S(2)}, u32[]{:S(2)}) collective-permute-start(bf16[80,768]{1,0:T(8,128)(2,1)S(1)} %shard_map.92), channel_id=1, source_target_pairs={{0,1},{1,0},{2,3},{3,2},{4,5},{5,4},{6,7},{7,6},{8,9},{9,8},{10,11... | collective-permute-start | bytes 368648 | tf_op jit(solution)/shard_map/ppermute | solution.py:257
  24.8 7.2 %collective-permute-start.8 = (bf16[80,768]{1,0:T(8,128)(2,1)S(1)}, bf16[80,768]{1,0:T(8,128)(2,1)S(1)}, u32[]{:S(2)}, u32[]{:S(2)}) collective-permute-start(bf16[80,768]{1,0:T(8,128)(2,1)S(1)} %get-tuple-element.73), channel_id=1, source_target_pairs={{0,2},{1,3},{2,0},{3,1},{4,6},{5,7},{6,4},{7,5},{8,10},{9,11},{10,... | collective-permute-start | bytes 368648 | tf_op jit(solution)/shard_map/ppermute | solution.py:257
  29.9 2.1 %collective-permute-start.10 = (bf16[80,768]{1,0:T(8,128)(2,1)S(1)}, bf16[80,768]{1,0:T(8,128)(2,1)S(1)}, u32[]{:S(2)}, u32[]{:S(2)}) collective-permute-start(bf16[80,768]{1,0:T(8,128)(2,1)S(1)} %get-tuple-element.65.mine_act), channel_id=1, source_target_pairs={{0,1},{1,0},{2,3},{3,2},{4,5},{5,4},{6,7},{7,6},{8,9},{9,8},{10,11... | collective-permute-start | bytes 368648 | tf_op jit(solution)/shard_map/ppermute | solution.py:257
  32.0 1.6 %collective-permute-start.11 = (bf16[2,80,768]{2,1,0:T(8,128)(2,1)S(1)}, bf16[2,80,768]{2,1,0:T(8,128)(2,1)S(1)}, u32[]{:S(2)}, u32[]{:S(2)}) collective-permute-start(bf16[2,80,768]{2,1,0:T(8,128)(2,1)S(1)} %shard_map.94.mine), channel_id=1, source_target_pairs={{0,1},{1,0},{2,3},{3,2},{4,5},{5,4},{6,7},{7,6},{8,9},{9,8},{10,11... | collective-permute-start | bytes 737288 | tf_op jit(solution)/shard_map/ppermute | solution.py:257
  34.5 8.6 %collective-permute-start.12 = (bf16[40,1024]{1,0:T(8,128)(2,1)S(1)}, bf16[40,1024]{1,0:T(8,128)(2,1)S(1)}, u32[]{:S(2)}, u32[]{:S(2)}) collective-permute-start(bf16[40,1024]{1,0:T(8,128)(2,1)S(1)} %get-tuple-element.66), channel_id=1, source_target_pairs={{0,12},{4,8},{8,4},{12,0},{1,13},{5,9},{9,5},{13,1},{2,14},{6,10},... | collective-permute-start | bytes 245768 | tf_op jit(solution)/shard_map/ppermute | solution.py:257
  38.3 6.8 %collective-permute-start.13 = (bf16[40,1024]{1,0:T(8,128)(2,1)S(1)}, bf16[40,1024]{1,0:T(8,128)(2,1)S(1)}, u32[]{:S(2)}, u32[]{:S(2)}) collective-permute-start(bf16[40,1024]{1,0:T(8,128)(2,1)S(1)} %get-tuple-element.67), channel_id=1, source_target_pairs={{0,8},{4,12},{8,0},{12,4},{1,9},{5,13},{9,1},{13,5},{2,10},{6,14},... | collective-permute-start | bytes 245768 | tf_op jit(solution)/shard_map/ppermute | solution.py:257
  38.3 6.8 %collective-permute-start.14 = (bf16[40,1024]{1,0:T(8,128)(2,1)S(1)}, bf16[40,1024]{1,0:T(8,128)(2,1)S(1)}, u32[]{:S(2)}, u32[]{:S(2)}) collective-permute-start(bf16[40,1024]{1,0:T(8,128)(2,1)S(1)} %get-tuple-element.68), channel_id=1, source_target_pairs={{0,4},{4,0},{8,12},{12,8},{1,5},{5,1},{9,13},{13,9},{2,6},{6,2},{1... | collective-permute-start | bytes 245768 | tf_op jit(solution)/shard_map/ppermute | solution.py:257

commit v9 on v8

--- a/solution.py
+++ b/solution.py
@@ -15,6 +15,7 @@
 MIB = 1 << 20
 C2COST = 100
 WCOST = 100
+CUTS = 6
 GFLOP = 100
 D1COST = 1
 D2COST = 100
@@ -35,7 +36,27 @@
 
 
 def far_first(count):
-    return list(reversed(range(count)))
+    return sorted(range(count), key=lambda k: (-k.bit_length(), k))
+
+
+def cut(source, target, sems, first, pieces):
+    rows = target.shape[-2] // pieces
+    out = []
+    for at in range(pieces):
+        part = pl.ds(at * rows, rows)
+        out.append(pltpu.make_async_copy(source.at[part], target.at[part], sems.at[first + at]))
+    return out
+
+
+def run(loads):
+    for load in loads:
+        load.start()
+    return loads
+
+
+def wait(loads):
+    for load in loads:
+        load.wait()
 
 
 def block_of(position, names):
@@ -59,14 +80,14 @@
 
 def pick_inputs(experts, routes_in, probs_in, inputs, grads, pick_out, prob_out, grads_out, *refs):
     *pieces, routes, probs, held, sems = refs
-    loads = [
-        pltpu.make_async_copy(source, target, sems.at[at])
-        for at, (source, target) in enumerate(
-            [(routes_in, routes), (probs_in, probs), (inputs, held), (grads, grads_out)]
-        )
-    ]
-    for load in loads:
-        load.start()
+    loads = run(
+        [
+            pltpu.make_async_copy(routes_in, routes, sems.at[0]),
+            pltpu.make_async_copy(probs_in, probs, sems.at[1]),
+        ]
+    )
+    input_loads = run(cut(inputs, held, sems, 2, 4))
+    grad_loads = run(cut(grads, grads_out, sems, 6, 4))
     me = lax.axis_index("ex")
     tokens = inputs.shape[0]
     rows = experts * MOST
@@ -78,8 +99,7 @@
     earlier = jnp.where(earlier, 1.0, 0.0).astype(BF)
     row = iota((rows, tokens), 0)
     slot = row - block_of(row, range(experts)) * MOST
-    loads[0].wait()
-    loads[1].wait()
+    wait(loads)
     chosen = routes[...]
     wide = probs[...].astype(F32)
     for k in range(experts):
@@ -94,11 +114,11 @@
     pick = pick.astype(BF)
     pick_out[...] = pick
     prob_out[...] = jnp.sum(jnp.where(picks, weight, 0.0), axis=1, keepdims=True)
-    loads[2].wait()
+    wait(input_loads)
     sent = jnp.where(filled, mm(pick, held[...]), EMPTY)
     for k in range(experts):
         pieces[k][...] = sent[k * MOST : (k + 1) * MOST].astype(BF)
-    loads[3].wait()
+    wait(grad_loads)
 
 
 def pick_grads(experts, pick, prob, grads, *pieces):
@@ -137,43 +157,39 @@
     pieces, refs = refs[:far_count], refs[far_count:]
     held, pieces_out, sems = refs[:2], refs[2:-1], refs[-1]
     half = gate_up.shape[2] // 2
-    moves = list(zip(pieces, pieces_out))
+    loads = []
     for own, out in enumerate(held):
         for matrix in range(2):
-            moves.append((gate_up.at[0, matrix, rows_of(half, own == 1)], out.at[matrix]))
-    loads = [
-        pltpu.make_async_copy(source, target, sems.at[at]) for at, (source, target) in enumerate(moves)
-    ]
-    for load in loads:
-        load.start()
-    for load in loads:
-        load.wait()
-
-
-def load_down(down, own, out, sem):
+            source = gate_up.at[0, matrix, rows_of(half, own == 1)]
+            loads += cut(source, out.at[matrix], sems, len(loads), CUTS)
+    run(loads)
+    for source, target in zip(pieces, pieces_out):
+        target[...] = source[...]
+    wait(loads)
+
+
+def load_down(down, own, out, sems):
     half = down.shape[1] // 2
-    return pltpu.make_async_copy(down.at[0, rows_of(half, own)], out, sem)
+    return run(cut(down.at[0, rows_of(half, own)], out, sems, 0, CUTS))
 
 
 def other_pair(experts, capacity, *refs):
-    held, down, near, out, place_out, rows_out, down_out, near_out, sem = refs[experts:]
+    held, down, near, out, place_out, rows_out, down_out, near_out, sems = refs[experts:]
     near_out[...] = near[...]
-    load = load_down(down, False, down_out, sem)
-    load.start()
+    loads = load_down(down, False, down_out, sems)
     place, rows_in = place_rows(experts, capacity, refs[:experts])
     place_out[...] = place
     rows_out[...] = rows_in
     for matrix in range(2):
         out[matrix] = mm(rows_in, held[matrix], LANES).astype(BF)
-    load.wait()
-
-
-def mine_pair(rows_in, held, down, out, down_out, sem):
-    load = load_down(down, True, down_out, sem)
-    load.start()
+    wait(loads)
+
+
+def mine_pair(rows_in, held, down, out, down_out, sems):
+    loads = load_down(down, True, down_out, sems)
     for matrix in range(2):
         out[matrix] = mm(rows_in[...], held[matrix], LANES).astype(BF)
-    load.wait()
+    wait(loads)
 
 
 def pair_sum(mine, other, held_out, sent_out):
@@ -244,8 +260,16 @@
 
 
 def combine(experts, pick, *refs):
+    out, held, sems = refs[experts:]
     home = stacked(refs[:experts]).astype(BF)
-    refs[experts][...] = mm(pick[...], home, ROWS).astype(BF)
+    rows = out.shape[0] // held.shape[0]
+    stores = []
+    for at in range(held.shape[0]):
+        part = pick[:, at * rows : (at + 1) * rows]
+        held[at] = mm(part, home, ROWS).astype(BF)
+        target = out.at[pl.ds(at * rows, rows)]
+        stores += run([pltpu.make_async_copy(held.at[at], target, sems.at[at])])
+    wait(stores)
 
 
 def far(value):
@@ -292,7 +316,7 @@
             pltpu.VMEM(routes.shape[::-1], jnp.int32),
             pltpu.VMEM(routes.shape[::-1], BF),
             pltpu.VMEM((tokens, width), BF),
-            dma(4),
+            dma(10),
         ],
         flops=2 * rows * tokens * width,
         traffic=4 * tokens * width,
@@ -311,13 +335,12 @@
         [pltpu.VMEM((2, half, width), BF)] * 2 + piece[2:],
         (far(gate_up), *send_grad[:far_count]),
         [HBM] + [VMEM] * far_count,
-        [dma(far_count + 4)],
+        [dma(4 * CUTS)],
         flops=WCOST * weight_flops,
         traffic=WCOST * weight_bytes,
     )
     got_grad = [swap(far_grad[at], "ex", order[at]) for at in range(far_count)]
 
-    one_dma = pltpu.SemaphoreType.DMA
     down_half = pltpu.VMEM((half, width), BF)
     pair_other, place, rows_in, down_other, near_grad = call(
         functools.partial(other_pair, experts, capacity),
@@ -325,7 +348,7 @@
         + [down_half, piece[0]],
         (*got_in, held_other, far(down_proj), send_grad[-2]),
         [VMEM] * (experts + 1) + [HBM, VMEM],
-        [one_dma],
+        [dma(CUTS)],
         flops=2 * weight_flops,
         traffic=weight_bytes,
     )
@@ -334,7 +357,7 @@
         [sds((2, capacity, half), BF), down_half],
         (rows_in, held_mine, far(down_proj)),
         [VMEM] * 2 + [HBM],
-        [one_dma],
+        [dma(CUTS)],
         flops=C2COST * weight_flops,
         traffic=C2COST * weight_bytes,
     )
@@ -421,8 +444,10 @@
         sds((tokens, width), BF),
         (pick, *home),
         [VMEM] * (experts + 1),
+        [pltpu.VMEM((2, tokens // 2, width), BF), dma(2)],
         flops=2 * rows * tokens * width,
         traffic=4 * tokens * width,
+        out_specs=ANY,
     )
     return (grad_inputs, pair_grad, down_grad)
 

time: 46.4 us -> 47.4 us (1.022)
  starting transfers between devices: 18.3 us -> 19.6 us
    ppermute x15, starting transfers between devices: 18.3 us -> 19.6 us  [swap(): return lax.ppermute(value, axis, [(i, i ^ bit) for i in range(count)])]
  transfers between devices with their start and end apart: 15 -> 15, of which waited for: 5 -> 7; matrix products, arithmetic and copies ran while one was open for 0% -> 0% of each run, Pallas kernels for 32% -> 31%
where the time goes in v9:
time: 47.4 us; the launch traced here: 47.2 us
  starting transfers between devices  19.6 us (41%)
  Pallas kernels  18.1 us (38%)
  waiting for transfers between devices  8.65 us (18%)
  between operations  0.79 us (2%)
    ppermute x15, starting transfers between devices, swap(): return lax.ppermute(value, axis, [(i, i ^ bit) for i in range(count)])  19.6 us
    pallas_call x14, Pallas kernels, call(): pl.pallas_call(body, out_shape=outs, in_specs=specs, out_specs=out_specs...  18.1 us
    ppermute x15, waiting for transfers between devices, swap(): return lax.ppermute(value, axis, [(i, i ^ bit) for i in range(count)])  8.65 us
  transfers between devices with their start and end apart: 15, of which 7 were waited for; matrix products, arithmetic and copies ran while one was open for 0% of the time, Pallas kernels for 31%

profile of v9, /device:TPU:0, one launch (start us, length us, event | category | flops | bytes accessed | tf_op | source)
XLA Modules:
  0.0 47.2 jit_solution(2204213829369432204)
XLA Ops:
  0.6 1.5 %shard_map.85 = (bf16[160,256]{1,0:T(8,128)(2,1)S(1)}, f32[160,1]{1,0:T(8,128)S(1)}, bf16[256,1024]{1,0:T(8,128)(2,1)S(1)}, bf16[40,1024]{1,0:T(8,128)(2,1)S(1)}...) custom-call(s32[8,256]{1,0:T(8,128)} %bitcast.2, ...), custom_call_target="tpu_custom_call" | custom-call | flops 83886080 | bytes 1048576 | tf_op jit(solution)/shard_map/pallas_call | solution.py:70
  2.2 4.1 %collective-permute-start.2 = (bf16[40,1024]{1,0:T(8,128)(2,1)S(1)}, bf16[40,1024]{1,0:T(8,128)(2,1)S(1)}, u32[]{:S(2)}, u32[]{:S(2)}) collective-permute-start(bf16[40,1024]{1,0:T(8,128)(2,1)S(1)} %get-tuple-element.45), channel_id=1, source_target_pairs={{0,8},{4,12},{8,0},{12,4},{1,9},{5,13},{9,1},{13,5},{2,10},{6,14},... | collective-permute-start | bytes 245768 | tf_op jit(solution)/shard_map/ppermute | solution.py:281
  6.3 1.3 %collective-permute-start.3 = (bf16[40,1024]{1,0:T(8,128)(2,1)S(1)}, bf16[40,1024]{1,0:T(8,128)(2,1)S(1)}, u32[]{:S(2)}, u32[]{:S(2)}) collective-permute-start(bf16[40,1024]{1,0:T(8,128)(2,1)S(1)} %get-tuple-element.46), channel_id=1, source_target_pairs={{0,12},{4,8},{8,4},{12,0},{1,13},{5,9},{9,5},{13,1},{2,14},{6,10},... | collective-permute-start | bytes 245768 | tf_op jit(solution)/shard_map/ppermute | solution.py:281
  8.1 3.0 %shard_map.87 = (bf16[2,768,1024]{2,1,0:T(8,128)(2,1)S(1)}, bf16[2,768,1024]{2,1,0:T(8,128)(2,1)S(1)}, bf16[40,1024]{1,0:T(8,128)(2,1)S(1)}, bf16[40,1024]{1,0:T(8,128)(2,1)S(1)}) custom-call(bf16[1,2,1536,1024]{3,2,1,0:T(8,128)(2,1)} %gate_up.1, bf16[40,1024]{1,0:T(8,128)(2,1)S(1)} %get-tuple-element.41.refs_0_, bf16[40,1024]{1,0:T(8,128)(2,1)S(1)} %get-tuple-element.42.refs_1_), custom_call_target="tpu_custom_call" | custom-call | flops 25165824000 | bytes 314572800 | tf_op jit(solution)/shard_map/pallas_call | solution.py:70
  11.1 2.9 %collective-permute-start = (bf16[40,1024]{1,0:T(8,128)(2,1)S(1)}, bf16[40,1024]{1,0:T(8,128)(2,1)S(1)}, u32[]{:S(2)}, u32[]{:S(2)}) collective-permute-start(bf16[40,1024]{1,0:T(8,128)(2,1)S(1)} %get-tuple-element.43), channel_id=1, source_target_pairs={{0,8},{4,12},{8,0},{12,4},{1,9},{5,13},{9,1},{13,5},{2,10},{6,14},... | collective-permute-start | bytes 245768 | tf_op jit(solution)/shard_map/ppermute | solution.py:281
  14.0 1.3 %collective-permute-start.1 = (bf16[40,1024]{1,0:T(8,128)(2,1)S(1)}, bf16[40,1024]{1,0:T(8,128)(2,1)S(1)}, u32[]{:S(2)}, u32[]{:S(2)}) collective-permute-start(bf16[40,1024]{1,0:T(8,128)(2,1)S(1)} %get-tuple-element.44), channel_id=1, source_target_pairs={{0,12},{4,8},{8,4},{12,0},{1,13},{5,9},{9,5},{13,1},{2,14},{6,10},... | collective-permute-start | bytes 245768 | tf_op jit(solution)/shard_map/ppermute | solution.py:281
  15.3 2.7 %shard_map.88 = (bf16[2,80,768]{2,1,0:T(8,128)(2,1)S(1)}, bf16[160,80]{1,0:T(8,128)(2,1)S(1)}, bf16[80,1024]{1,0:T(8,128)(2,1)S(1)}, bf16[768,1024]{1,0:T(8,128)(2,1)S(1)}, bf16[40,1024]{1,0:T(8,128)(2,1)S(1)}) custom-call(bf16[40,1024]{1,0:T(8,128)(2,1)S(1)} %collective-permute-done.2.refs_0_, bf16[40,1024]{1,0:T(8,128)(2,1)S(1)} %collective-permute-done.3.refs_1_, ...), custom_call_target="tpu_custom_call" | custom-call | flops 503316480 | bytes 3145728 | tf_op jit(solution)/shard_map/pallas_call | solution.py:70
  18.2 2.3 %shard_map.89 = (bf16[2,80,768]{2,1,0:T(8,128)(2,1)S(1)}, bf16[768,1024]{1,0:T(8,128)(2,1)S(1)}) custom-call(bf16[80,1024]{1,0:T(8,128)(2,1)S(1)} %get-tuple-element.54.rows_in, bf16[2,768,1024]{2,1,0:T(8,128)(2,1)S(1)} %get-tuple-element.55.held, bf16[1,1536,1024]{2,1,0:T(8,128)(2,1)} %down.1), custom_call_target="tpu_custom_call" | custom-call | flops 25165824000 | bytes 314572800 | tf_op jit(solution)/shard_map/pallas_call | solution.py:70
  20.6 1.6 %collective-permute-start.9 = (bf16[2,80,768]{2,1,0:T(8,128)(2,1)S(1)}, bf16[2,80,768]{2,1,0:T(8,128)(2,1)S(1)}, u32[]{:S(2)}, u32[]{:S(2)}) collective-permute-start(bf16[2,80,768]{2,1,0:T(8,128)(2,1)S(1)} %get-tuple-element.61.refs_6_), channel_id=1, source_target_pairs={{0,2},{1,3},{2,0},{3,1},{4,6},{5,7},{6,4},{7,5},{8,10},{9,11},{10,... | collective-permute-start | bytes 737288 | tf_op jit(solution)/shard_map/ppermute | solution.py:281
  22.5 0.7 %shard_map.92 = bf16[80,768]{1,0:T(8,128)(2,1)S(1)} custom-call(bf16[40,1024]{1,0:T(8,128)(2,1)S(1)} %collective-permute-done.refs_0_, bf16[40,1024]{1,0:T(8,128)(2,1)S(1)} %collective-permute-done.1.refs_1_, bf16[40,1024]{1,0:T(8,128)(2,1)S(1)} %collective-permute-done.5.refs_2_, bf16[40,1024]{1,0:T(8,128)(2,1)S(1)} %get-tuple-element.52.refs_3_, ...), custom_call_target="tpu_custom_call" | custom-call | flops 251658240 | bytes 3145728 | tf_op jit(solution)/shard_map/pallas_call | solution.py:70
  23.3 0.7 %shard_map.90 = (bf16[80,1024]{1,0:T(8,128)(2,1)S(1)}, bf16[80,768]{1,0:T(8,128)(2,1)S(1)}) custom-call(bf16[40,1024]{1,0:T(8,128)(2,1)S(1)} %collective-permute-done.refs_0_, bf16[40,1024]{1,0:T(8,128)(2,1)S(1)} %collective-permute-done.1.refs_1_, bf16[40,1024]{1,0:T(8,128)(2,1)S(1)} %collective-permute-done.5.refs_2_, ...), custom_call_target="tpu_custom_call" | custom-call | flops 25165824000 | bytes 314572800 | tf_op jit(solution)/shard_map/pallas_call | solution.py:70
  24.0 0.6 %collective-permute-done.7 = bf16[80,768]{1,0:T(8,128)(2,1)S(1)} collective-permute-done((bf16[80,768]{1,0:T(8,128)(2,1)S(1)}, bf16[80,768]{1,0:T(8,128)(2,1)S(1)}, u32[]{:S(2)}, u32[]{:S(2)}) %collective-permute-start.7) | collective-permute-done | bytes 122912 | tf_op jit(solution)/shard_map/ppermute | solution.py:281
  24.7 1.6 %collective-permute-start.8 = (bf16[80,768]{1,0:T(8,128)(2,1)S(1)}, bf16[80,768]{1,0:T(8,128)(2,1)S(1)}, u32[]{:S(2)}, u32[]{:S(2)}) collective-permute-start(bf16[80,768]{1,0:T(8,128)(2,1)S(1)} %get-tuple-element.73), channel_id=1, source_target_pairs={{0,2},{1,3},{2,0},{3,1},{4,6},{5,7},{6,4},{7,5},{8,10},{9,11},{10,... | collective-permute-start | bytes 368648 | tf_op jit(solution)/shard_map/ppermute | solution.py:281
  26.2 3.2 %collective-permute-done.9.pair_far = bf16[2,80,768]{2,1,0:T(8,128)(2,1)S(1)} collective-permute-done((bf16[2,80,768]{2,1,0:T(8,128)(2,1)S(1)}, bf16[2,80,768]{2,1,0:T(8,128)(2,1)S(1)}, u32[]{:S(2)}, u32[]{:S(2)}) %collective-permute-start.9) | collective-permute-done | bytes 245792 | tf_op jit(solution)/shard_map/ppermute | solution.py:281
  29.6 2.0 %collective-permute-done.8.act_far = bf16[80,768]{1,0:T(8,128)(2,1)S(1)} collective-permute-done((bf16[80,768]{1,0:T(8,128)(2,1)S(1)}, bf16[80,768]{1,0:T(8,128)(2,1)S(1)}, u32[]{:S(2)}, u32[]{:S(2)}) %collective-permute-start.8) | collective-permute-done | bytes 122912 | tf_op jit(solution)/shard_map/ppermute | solution.py:281
  31.8 0.7 %shard_map.95.total = f32[80,1024]{1,0:T(8,128)S(1)} custom-call(bf16[2,80,768]{2,1,0:T(8,128)(2,1)S(1)} %shard_map.94.mine, bf16[2,768,1024]{2,1,0:T(8,128)(2,1)S(1)} %get-tuple-element.55.held), custom_call_target="tpu_custom_call" | custom-call | flops 251658240 | bytes 3145728 | tf_op jit(solution)/shard_map/pallas_call | solution.py:70
  32.5 0.8 %collective-permute-done.11.other = bf16[2,80,768]{2,1,0:T(8,128)(2,1)S(1)} collective-permute-done((bf16[2,80,768]{2,1,0:T(8,128)(2,1)S(1)}, bf16[2,80,768]{2,1,0:T(8,128)(2,1)S(1)}, u32[]{:S(2)}, u32[]{:S(2)}) %collective-permute-start.11) | collective-permute-done | bytes 245792 | tf_op jit(solution)/shard_map/ppermute | solution.py:281
  33.3 0.8 %shard_map.96 = (bf16[40,1024]{1,0:T(8,128)(2,1)S(1)}, bf16[40,1024]{1,0:T(8,128)(2,1)S(1)}, bf16[40,1024]{1,0:T(8,128)(2,1)S(1)}, bf16[40,1024]{1,0:T(8,128)(2,1)S(1)}) custom-call(f32[80,1024]{1,0:T(8,128)S(1)} %shard_map.95.total, bf16[2,80,768]{2,1,0:T(8,128)(2,1)S(1)} %collective-permute-done.11.other, ...), custom_call_target="tpu_custom_call" | custom-call | flops 251658240 | bytes 3145728 | tf_op jit(solution)/shard_map/pallas_call | solution.py:70
  34.1 4.3 %collective-permute-start.12 = (bf16[40,1024]{1,0:T(8,128)(2,1)S(1)}, bf16[40,1024]{1,0:T(8,128)(2,1)S(1)}, u32[]{:S(2)}, u32[]{:S(2)}) collective-permute-start(bf16[40,1024]{1,0:T(8,128)(2,1)S(1)} %get-tuple-element.66), channel_id=1, source_target_pairs={{0,8},{4,12},{8,0},{12,4},{1,9},{5,13},{9,1},{13,5},{2,10},{6,14},... | collective-permute-start | bytes 245768 | tf_op jit(solution)/shard_map/ppermute | solution.py:281
  38.4 1.5 %collective-permute-start.13 = (bf16[40,1024]{1,0:T(8,128)(2,1)S(1)}, bf16[40,1024]{1,0:T(8,128)(2,1)S(1)}, u32[]{:S(2)}, u32[]{:S(2)}) collective-permute-start(bf16[40,1024]{1,0:T(8,128)(2,1)S(1)} %get-tuple-element.67), channel_id=1, source_target_pairs={{0,12},{4,8},{8,4},{12,0},{1,13},{5,9},{9,5},{13,1},{2,14},{6,10},... | collective-permute-start | bytes 245768 | tf_op jit(solution)/shard_map/ppermute | solution.py:281
  40.3 4.1 %shard_map.98 = (bf16[1,2,1536,1024]{3,2,1,0:T(8,128)(2,1)}, bf16[1,1536,1024]{2,1,0:T(8,128)(2,1)}) custom-call(bf16[80,768]{1,0:T(8,128)(2,1)S(1)} %get-tuple-element.65.mine_act, bf16[80,768]{1,0:T(8,128)(2,1)S(1)} %collective-permute-done.10._.other_act, bf16[2,80,768]{2,1,0:T(8,128)(2,1)S(1)} %shard_map.94.mine, ...), custom_call_target="tpu_custom_call" | custom-call | flops 754974720 | bytes 9437184 | tf_op jit(solution)/shard_map/pallas_call | solution.py:70
  44.5 0.8 %collective-permute-done.13.refs_1_ = bf16[40,1024]{1,0:T(8,128)(2,1)S(1)} collective-permute-done((bf16[40,1024]{1,0:T(8,128)(2,1)S(1)}, bf16[40,1024]{1,0:T(8,128)(2,1)S(1)}, u32[]{:S(2)}, u32[]{:S(2)}) %collective-permute-start.13) | collective-permute-done | bytes 81952 | tf_op jit(solution)/shard_map/ppermute | solution.py:281
  45.3 0.8 %collective-permute-done.14.refs_2_ = bf16[40,1024]{1,0:T(8,128)(2,1)S(1)} collective-permute-done((bf16[40,1024]{1,0:T(8,128)(2,1)S(1)}, bf16[40,1024]{1,0:T(8,128)(2,1)S(1)}, u32[]{:S(2)}, u32[]{:S(2)}) %collective-permute-start.14) | collective-permute-done | bytes 81952 | tf_op jit(solution)/shard_map/ppermute | solution.py:281
  46.1 1.1 %shard_map.97 = bf16[256,1024]{1,0:T(8,128)(2,1)} custom-call(bf16[160,256]{1,0:T(8,128)(2,1)S(1)} %get-tuple-element.38.pick, bf16[40,1024]{1,0:T(8,128)(2,1)S(1)} %collective-permute-done.12.refs_0_, bf16[40,1024]{1,0:T(8,128)(2,1)S(1)} %collective-permute-done.13.refs_1_, bf16[40,1024]{1,0:T(8,128)(2,1)S(1)} %collective-permute-done.14.refs_2_, ...), custom_call_target="tpu_custom_call" | custom-call | flops 83886080 | bytes 1048576 | tf_op jit(solution)/shard_map/pallas_call | solution.py:70
  (21 shorter events, 2.0 us)
Async XLA Ops:
  2.2 13.1 %collective-permute-start.2 = (bf16[40,1024]{1,0:T(8,128)(2,1)S(1)}, bf16[40,1024]{1,0:T(8,128)(2,1)S(1)}, u32[]{:S(2)}, u32[]{:S(2)}) collective-permute-start(bf16[40,1024]{1,0:T(8,128)(2,1)S(1)} %get-tuple-element.45), channel_id=1, source_target_pairs={{0,8},{4,12},{8,0},{12,4},{1,9},{5,13},{9,1},{13,5},{2,10},{6,14},... | collective-permute-start | bytes 245768 | tf_op jit(solution)/shard_map/ppermute | solution.py:281
  6.3 9.1 %collective-permute-start.3 = (bf16[40,1024]{1,0:T(8,128)(2,1)S(1)}, bf16[40,1024]{1,0:T(8,128)(2,1)S(1)}, u32[]{:S(2)}, u32[]{:S(2)}) collective-permute-start(bf16[40,1024]{1,0:T(8,128)(2,1)S(1)} %get-tuple-element.46), channel_id=1, source_target_pairs={{0,12},{4,8},{8,4},{12,0},{1,13},{5,9},{9,5},{13,1},{2,14},{6,10},... | collective-permute-start | bytes 245768 | tf_op jit(solution)/shard_map/ppermute | solution.py:281
  7.6 7.7 %collective-permute-start.4 = (bf16[40,1024]{1,0:T(8,128)(2,1)S(1)}, bf16[40,1024]{1,0:T(8,128)(2,1)S(1)}, u32[]{:S(2)}, u32[]{:S(2)}) collective-permute-start(bf16[40,1024]{1,0:T(8,128)(2,1)S(1)} %get-tuple-element.47), channel_id=1, source_target_pairs={{0,4},{4,0},{8,12},{12,8},{1,5},{5,1},{9,13},{13,9},{2,6},{6,2},{1... | collective-permute-start | bytes 245768 | tf_op jit(solution)/shard_map/ppermute | solution.py:281
  11.1 11.0 %collective-permute-start = (bf16[40,1024]{1,0:T(8,128)(2,1)S(1)}, bf16[40,1024]{1,0:T(8,128)(2,1)S(1)}, u32[]{:S(2)}, u32[]{:S(2)}) collective-permute-start(bf16[40,1024]{1,0:T(8,128)(2,1)S(1)} %get-tuple-element.43), channel_id=1, source_target_pairs={{0,8},{4,12},{8,0},{12,4},{1,9},{5,13},{9,1},{13,5},{2,10},{6,14},... | collective-permute-start | bytes 245768 | tf_op jit(solution)/shard_map/ppermute | solution.py:281
  14.0 8.2 %collective-permute-start.1 = (bf16[40,1024]{1,0:T(8,128)(2,1)S(1)}, bf16[40,1024]{1,0:T(8,128)(2,1)S(1)}, u32[]{:S(2)}, u32[]{:S(2)}) collective-permute-start(bf16[40,1024]{1,0:T(8,128)(2,1)S(1)} %get-tuple-element.44), channel_id=1, source_target_pairs={{0,12},{4,8},{8,4},{12,0},{1,13},{5,9},{9,5},{13,1},{2,14},{6,10},... | collective-permute-start | bytes 245768 | tf_op jit(solution)/shard_map/ppermute | solution.py:281
  18.0 4.5 %collective-permute-start.5 = (bf16[40,1024]{1,0:T(8,128)(2,1)S(1)}, bf16[40,1024]{1,0:T(8,128)(2,1)S(1)}, u32[]{:S(2)}, u32[]{:S(2)}) collective-permute-start(bf16[40,1024]{1,0:T(8,128)(2,1)S(1)} %get-tuple-element.51), channel_id=1, source_target_pairs={{0,4},{4,0},{8,12},{12,8},{1,5},{5,1},{9,13},{13,9},{2,6},{6,2},{1... | collective-permute-start | bytes 245768 | tf_op jit(solution)/shard_map/ppermute | solution.py:281
  18.1 2.4 %collective-permute-start.6 = (bf16[2,80,768]{2,1,0:T(8,128)(2,1)S(1)}, bf16[2,80,768]{2,1,0:T(8,128)(2,1)S(1)}, u32[]{:S(2)}, u32[]{:S(2)}) collective-permute-start(bf16[2,80,768]{2,1,0:T(8,128)(2,1)S(1)} %get-tuple-element.60), channel_id=1, source_target_pairs={{0,1},{1,0},{2,3},{3,2},{4,5},{5,4},{6,7},{7,6},{8,9},{9,8},{10,11... | collective-permute-start | bytes 737288 | tf_op jit(solution)/shard_map/ppermute | solution.py:281
  20.6 8.8 %collective-permute-start.9 = (bf16[2,80,768]{2,1,0:T(8,128)(2,1)S(1)}, bf16[2,80,768]{2,1,0:T(8,128)(2,1)S(1)}, u32[]{:S(2)}, u32[]{:S(2)}) collective-permute-start(bf16[2,80,768]{2,1,0:T(8,128)(2,1)S(1)} %get-tuple-element.61.refs_6_), channel_id=1, source_target_pairs={{0,2},{1,3},{2,0},{3,1},{4,6},{5,7},{6,4},{7,5},{8,10},{9,11},{10,... | collective-permute-start | bytes 737288 | tf_op jit(solution)/shard_map/ppermute | solution.py:281
  23.2 1.4 %collective-permute-start.7 = (bf16[80,768]{1,0:T(8,128)(2,1)S(1)}, bf16[80,768]{1,0:T(8,128)(2,1)S(1)}, u32[]{:S(2)}, u32[]{:S(2)}) collective-permute-start(bf16[80,768]{1,0:T(8,128)(2,1)S(1)} %shard_map.92), channel_id=1, source_target_pairs={{0,1},{1,0},{2,3},{3,2},{4,5},{5,4},{6,7},{7,6},{8,9},{9,8},{10,11... | collective-permute-start | bytes 368648 | tf_op jit(solution)/shard_map/ppermute | solution.py:281
  24.7 7.0 %collective-permute-start.8 = (bf16[80,768]{1,0:T(8,128)(2,1)S(1)}, bf16[80,768]{1,0:T(8,128)(2,1)S(1)}, u32[]{:S(2)}, u32[]{:S(2)}) collective-permute-start(bf16[80,768]{1,0:T(8,128)(2,1)S(1)} %get-tuple-element.73), channel_id=1, source_target_pairs={{0,2},{1,3},{2,0},{3,1},{4,6},{5,7},{6,4},{7,5},{8,10},{9,11},{10,... | collective-permute-start | bytes 368648 | tf_op jit(solution)/shard_map/ppermute | solution.py:281
  29.5 2.1 %collective-permute-start.10 = (bf16[80,768]{1,0:T(8,128)(2,1)S(1)}, bf16[80,768]{1,0:T(8,128)(2,1)S(1)}, u32[]{:S(2)}, u32[]{:S(2)}) collective-permute-start(bf16[80,768]{1,0:T(8,128)(2,1)S(1)} %get-tuple-element.65.mine_act), channel_id=1, source_target_pairs={{0,1},{1,0},{2,3},{3,2},{4,5},{5,4},{6,7},{7,6},{8,9},{9,8},{10,11... | collective-permute-start | bytes 368648 | tf_op jit(solution)/shard_map/ppermute | solution.py:281
  31.7 1.6 %collective-permute-start.11 = (bf16[2,80,768]{2,1,0:T(8,128)(2,1)S(1)}, bf16[2,80,768]{2,1,0:T(8,128)(2,1)S(1)}, u32[]{:S(2)}, u32[]{:S(2)}) collective-permute-start(bf16[2,80,768]{2,1,0:T(8,128)(2,1)S(1)} %shard_map.94.mine), channel_id=1, source_target_pairs={{0,1},{1,0},{2,3},{3,2},{4,5},{5,4},{6,7},{7,6},{8,9},{9,8},{10,11... | collective-permute-start | bytes 737288 | tf_op jit(solution)/shard_map/ppermute | solution.py:281
  34.1 10.3 %collective-permute-start.12 = (bf16[40,1024]{1,0:T(8,128)(2,1)S(1)}, bf16[40,1024]{1,0:T(8,128)(2,1)S(1)}, u32[]{:S(2)}, u32[]{:S(2)}) collective-permute-start(bf16[40,1024]{1,0:T(8,128)(2,1)S(1)} %get-tuple-element.66), channel_id=1, source_target_pairs={{0,8},{4,12},{8,0},{12,4},{1,9},{5,13},{9,1},{13,5},{2,10},{6,14},... | collective-permute-start | bytes 245768 | tf_op jit(solution)/shard_map/ppermute | solution.py:281
  38.4 6.9 %collective-permute-start.13 = (bf16[40,1024]{1,0:T(8,128)(2,1)S(1)}, bf16[40,1024]{1,0:T(8,128)(2,1)S(1)}, u32[]{:S(2)}, u32[]{:S(2)}) collective-permute-start(bf16[40,1024]{1,0:T(8,128)(2,1)S(1)} %get-tuple-element.67), channel_id=1, source_target_pairs={{0,12},{4,8},{8,4},{12,0},{1,13},{5,9},{9,5},{13,1},{2,14},{6,10},... | collective-permute-start | bytes 245768 | tf_op jit(solution)/shard_map/ppermute | solution.py:281
  39.9 6.2 %collective-permute-start.14 = (bf16[40,1024]{1,0:T(8,128)(2,1)S(1)}, bf16[40,1024]{1,0:T(8,128)(2,1)S(1)}, u32[]{:S(2)}, u32[]{:S(2)}) collective-permute-start(bf16[40,1024]{1,0:T(8,128)(2,1)S(1)} %get-tuple-element.68), channel_id=1, source_target_pairs={{0,4},{4,0},{8,12},{12,8},{1,5},{5,1},{9,13},{13,9},{2,6},{6,2},{1... | collective-permute-start | bytes 245768 | tf_op jit(solution)/shard_map/ppermute | solution.py:281

commit v10 on v9

--- a/solution.py
+++ b/solution.py
@@ -15,7 +15,6 @@
 MIB = 1 << 20
 C2COST = 100
 WCOST = 100
-CUTS = 6
 GFLOP = 100
 D1COST = 1
 D2COST = 100
@@ -37,6 +36,10 @@
 
 def far_first(count):
     return sorted(range(count), key=lambda k: (-k.bit_length(), k))
+
+
+def farthest_first(count):
+    return list(reversed(range(count)))
 
 
 def cut(source, target, sems, first, pieces):
@@ -86,8 +89,8 @@
             pltpu.make_async_copy(probs_in, probs, sems.at[1]),
         ]
     )
-    input_loads = run(cut(inputs, held, sems, 2, 4))
-    grad_loads = run(cut(grads, grads_out, sems, 6, 4))
+    input_loads = run(cut(inputs, held, sems, 2, 1))
+    grad_loads = run(cut(grads, grads_out, sems, 3, 1))
     me = lax.axis_index("ex")
     tokens = inputs.shape[0]
     rows = experts * MOST
@@ -153,43 +156,34 @@
     return place, mm(place, got.astype(BF), ROWS).astype(BF)
 
 
-def stage(far_count, gate_up, *refs):
-    pieces, refs = refs[:far_count], refs[far_count:]
+def stage(count, gate_up, down, *refs):
+    pieces, refs = refs[:count], refs[count:]
     held, pieces_out, sems = refs[:2], refs[2:-1], refs[-1]
-    half = gate_up.shape[2] // 2
+    half = down.shape[1] // 2
     loads = []
     for own, out in enumerate(held):
-        for matrix in range(2):
-            source = gate_up.at[0, matrix, rows_of(half, own == 1)]
-            loads += cut(source, out.at[matrix], sems, len(loads), CUTS)
+        rows = rows_of(half, own == 1)
+        for matrix in range(3):
+            source = down.at[0, rows] if matrix == 2 else gate_up.at[0, matrix, rows]
+            loads.append(pltpu.make_async_copy(source, out.at[matrix], sems.at[len(loads)]))
     run(loads)
     for source, target in zip(pieces, pieces_out):
         target[...] = source[...]
     wait(loads)
 
 
-def load_down(down, own, out, sems):
-    half = down.shape[1] // 2
-    return run(cut(down.at[0, rows_of(half, own)], out, sems, 0, CUTS))
-
-
 def other_pair(experts, capacity, *refs):
-    held, down, near, out, place_out, rows_out, down_out, near_out, sems = refs[experts:]
-    near_out[...] = near[...]
-    loads = load_down(down, False, down_out, sems)
+    held, out, place_out, rows_out = refs[experts:]
     place, rows_in = place_rows(experts, capacity, refs[:experts])
     place_out[...] = place
     rows_out[...] = rows_in
     for matrix in range(2):
         out[matrix] = mm(rows_in, held[matrix], LANES).astype(BF)
-    wait(loads)
-
-
-def mine_pair(rows_in, held, down, out, down_out, sems):
-    loads = load_down(down, True, down_out, sems)
+
+
+def mine_pair(rows_in, held, out):
     for matrix in range(2):
         out[matrix] = mm(rows_in[...], held[matrix], LANES).astype(BF)
-    wait(loads)
 
 
 def pair_sum(mine, other, held_out, sent_out):
@@ -200,10 +194,12 @@
 
 def act_part(experts, own, *refs):
     place, held = refs[experts : experts + 2]
-    rows_grad = mm(place[...], stacked(refs[:experts]).astype(BF), ROWS).astype(BF)
+    order = far_first(experts)
+    pieces = [refs[:experts][farthest_first(experts).index(k)] for k in order]
+    rows_grad = mm(place[...], stacked(pieces).astype(BF), ROWS).astype(BF)
     if own:
         refs[-2][...] = rows_grad
-    refs[-1][...] = mm(rows_grad, held[...], LANES).astype(BF)
+    refs[-1][...] = mm(rows_grad, held[2], LANES).astype(BF)
 
 
 def gates(pair, pair_far, act_out, by_gate, by_up):
@@ -301,7 +297,6 @@
     dma = lambda count: pltpu.SemaphoreType.DMA((count,))
 
     order = far_first(experts)
-    far_count = experts - 2
     pick, prob, grads, *send_in = call(
         functools.partial(pick_inputs, experts),
         [
@@ -316,7 +311,7 @@
             pltpu.VMEM(routes.shape[::-1], jnp.int32),
             pltpu.VMEM(routes.shape[::-1], BF),
             pltpu.VMEM((tokens, width), BF),
-            dma(10),
+            dma(4),
         ],
         flops=2 * rows * tokens * width,
         traffic=4 * tokens * width,
@@ -330,34 +325,32 @@
         traffic=2 * tokens * width,
     )
     got_in = exchange(send_in, "ex")
-    held_other, held_mine, *far_grad = call(
-        functools.partial(stage, far_count),
-        [pltpu.VMEM((2, half, width), BF)] * 2 + piece[2:],
-        (far(gate_up), *send_grad[:far_count]),
-        [HBM] + [VMEM] * far_count,
-        [dma(4 * CUTS)],
+    held_other, held_mine, *send_grad = call(
+        functools.partial(stage, experts),
+        [pltpu.VMEM((3, half, width), BF)] * 2 + piece,
+        (far(gate_up), far(down_proj), *send_grad),
+        [HBM] * 2 + [VMEM] * experts,
+        [dma(6)],
         flops=WCOST * weight_flops,
         traffic=WCOST * weight_bytes,
     )
-    got_grad = [swap(far_grad[at], "ex", order[at]) for at in range(far_count)]
-
-    down_half = pltpu.VMEM((half, width), BF)
-    pair_other, place, rows_in, down_other, near_grad = call(
+    got_grad = [
+        swap(send_grad[order.index(k)], "ex", k) if k else send_grad[-1]
+        for k in farthest_first(experts)
+    ]
+    pair_other, place, rows_in = call(
         functools.partial(other_pair, experts, capacity),
-        [sds((2, capacity, half), BF), sds((rows, capacity), BF), sds((capacity, width), BF)]
-        + [down_half, piece[0]],
-        (*got_in, held_other, far(down_proj), send_grad[-2]),
-        [VMEM] * (experts + 1) + [HBM, VMEM],
-        [dma(CUTS)],
+        [sds((2, capacity, half), BF), sds((rows, capacity), BF), sds((capacity, width), BF)],
+        (*got_in, held_other),
+        [VMEM] * (experts + 1),
         flops=2 * weight_flops,
         traffic=weight_bytes,
     )
-    pair_mine, down_mine = call(
+    pair_mine = call(
         mine_pair,
-        [sds((2, capacity, half), BF), down_half],
-        (rows_in, held_mine, far(down_proj)),
-        [VMEM] * 2 + [HBM],
-        [dma(CUTS)],
+        sds((2, capacity, half), BF),
+        (rows_in, held_mine),
+        [VMEM] * 2,
         flops=C2COST * weight_flops,
         traffic=C2COST * weight_bytes,
     )
@@ -378,8 +371,6 @@
         traffic=10 * capacity * hidden,
     )
     pair, pair_far = total(pair, pair_sent)
-    got_grad = got_grad + [swap(near_grad, "ex", 1), send_grad[-1]]
-
     def act_of(own, held, outs, tied, cost):
         return call(
             functools.partial(act_part, experts, own),
@@ -390,8 +381,8 @@
             traffic=cost * weight_bytes,
         )
 
-    (act_other,) = act_of(False, down_other, [], [pair_sent], D1COST)
-    rows_grad, act_mine = act_of(True, down_mine, [sds((capacity, width), BF)], [], D2COST)
+    (act_other,) = act_of(False, held_other, [], [pair_sent], D1COST)
+    rows_grad, act_mine = act_of(True, held_mine, [sds((capacity, width), BF)], [], D2COST)
     act = act_mine.astype(F32) + swap(act_other, "ey", 1).astype(F32)
     act, act_far = total(act, act.astype(BF))
     mine_act, by_gate, by_up = call(

time: 47.4 us -> 44.2 us (0.932)
  starting transfers between devices: 19.6 us -> 17.1 us
  Pallas kernels: 18.1 us -> 16.4 us
  waiting for transfers between devices: 8.65 us -> 9.8 us
    ppermute x15, starting transfers between devices: 19.6 us -> 17.1 us  [swap(): return lax.ppermute(value, axis, [(i, i ^ bit) for i in range(count)])]
    pallas_call x14, Pallas kernels: 18.1 us -> 16.4 us  [call(): pl.pallas_call(body, out_shape=outs, in_specs=specs, out_specs=out_specs...]
    ppermute x15, waiting for transfers between devices: 8.65 us -> 9.8 us  [swap(): return lax.ppermute(value, axis, [(i, i ^ bit) for i in range(count)])]
  transfers between devices with their start and end apart: 15 -> 15, of which waited for: 7 -> 8; matrix products, arithmetic and copies ran while one was open for 0% -> 0% of each run, Pallas kernels for 31% -> 29%
where the time goes in v10:
time: 44.2 us; the launch traced here: 44 us
  starting transfers between devices  17.1 us (39%)
  Pallas kernels  16.4 us (37%)
  waiting for transfers between devices  9.8 us (22%)
  between operations  0.74 us (2%)
    ppermute x15, starting transfers between devices, swap(): return lax.ppermute(value, axis, [(i, i ^ bit) for i in range(count)])  17.1 us
    pallas_call x14, Pallas kernels, call(): pl.pallas_call(body, out_shape=outs, in_specs=specs, out_specs=out_specs...  16.4 us
    ppermute x15, waiting for transfers between devices, swap(): return lax.ppermute(value, axis, [(i, i ^ bit) for i in range(count)])  9.8 us
  transfers between devices with their start and end apart: 15, of which 8 were waited for; matrix products, arithmetic and copies ran while one was open for 0% of the time, Pallas kernels for 29%

profile of v10, /device:TPU:0, one launch (start us, length us, event | category | flops | bytes accessed | tf_op | source)
XLA Modules:
  0.0 44.0 jit_solution(5278680010234719090)
XLA Ops:
  0.6 1.5 %shard_map.85 = (bf16[160,256]{1,0:T(8,128)(2,1)S(1)}, f32[160,1]{1,0:T(8,128)S(1)}, bf16[256,1024]{1,0:T(8,128)(2,1)S(1)}, bf16[40,1024]{1,0:T(8,128)(2,1)S(1)}...) custom-call(s32[8,256]{1,0:T(8,128)} %bitcast.2, ...), custom_call_target="tpu_custom_call" | custom-call | flops 83886080 | bytes 1048576 | tf_op jit(solution)/shard_map/pallas_call | solution.py:73
  2.1 4.1 %collective-permute-start.3 = (bf16[40,1024]{1,0:T(8,128)(2,1)S(1)}, bf16[40,1024]{1,0:T(8,128)(2,1)S(1)}, u32[]{:S(2)}, u32[]{:S(2)}) collective-permute-start(bf16[40,1024]{1,0:T(8,128)(2,1)S(1)} %get-tuple-element.47), channel_id=1, source_target_pairs={{0,8},{4,12},{8,0},{12,4},{1,9},{5,13},{9,1},{13,5},{2,10},{6,14},... | collective-permute-start | bytes 245768 | tf_op jit(solution)/shard_map/ppermute | solution.py:277
  6.2 1.3 %collective-permute-start.4 = (bf16[40,1024]{1,0:T(8,128)(2,1)S(1)}, bf16[40,1024]{1,0:T(8,128)(2,1)S(1)}, u32[]{:S(2)}, u32[]{:S(2)}) collective-permute-start(bf16[40,1024]{1,0:T(8,128)(2,1)S(1)} %get-tuple-element.48), channel_id=1, source_target_pairs={{0,12},{4,8},{8,4},{12,0},{1,13},{5,9},{9,5},{13,1},{2,14},{6,10},... | collective-permute-start | bytes 245768 | tf_op jit(solution)/shard_map/ppermute | solution.py:277
  8.1 3.8 %shard_map.87 = (bf16[3,768,1024]{2,1,0:T(8,128)(2,1)S(1)}, bf16[3,768,1024]{2,1,0:T(8,128)(2,1)S(1)}, bf16[40,1024]{1,0:T(8,128)(2,1)S(1)}, bf16[40,1024]{1,0:T...) custom-call(bf16[1,2,1536,1024]{3,2,1,0:T(8,128)(2,1)} %gate_up.1, ...), custom_call_target="tpu_custom_call" | custom-call | flops 25165824000 | bytes 314572800 | tf_op jit(solution)/shard_map/pallas_call | solution.py:73
  11.9 3.0 %collective-permute-start = (bf16[40,1024]{1,0:T(8,128)(2,1)S(1)}, bf16[40,1024]{1,0:T(8,128)(2,1)S(1)}, u32[]{:S(2)}, u32[]{:S(2)}) collective-permute-start(bf16[40,1024]{1,0:T(8,128)(2,1)S(1)} %get-tuple-element.43), channel_id=1, source_target_pairs={{0,12},{4,8},{8,4},{12,0},{1,13},{5,9},{9,5},{13,1},{2,14},{6,10},... | collective-permute-start | bytes 245768 | tf_op jit(solution)/shard_map/ppermute | solution.py:277
  15.2 1.1 %collective-permute-start.2 = (bf16[40,1024]{1,0:T(8,128)(2,1)S(1)}, bf16[40,1024]{1,0:T(8,128)(2,1)S(1)}, u32[]{:S(2)}, u32[]{:S(2)}) collective-permute-start(bf16[40,1024]{1,0:T(8,128)(2,1)S(1)} %get-tuple-element.45), channel_id=1, source_target_pairs={{0,4},{4,0},{8,12},{12,8},{1,5},{5,1},{9,13},{13,9},{2,6},{6,2},{1... | collective-permute-start | bytes 245768 | tf_op jit(solution)/shard_map/ppermute | solution.py:277
  16.3 1.4 %shard_map.88 = (bf16[2,80,768]{2,1,0:T(8,128)(2,1)S(1)}, bf16[160,80]{1,0:T(8,128)(2,1)S(1)}, bf16[80,1024]{1,0:T(8,128)(2,1)S(1)}) custom-call(bf16[40,1024]{1,0:T(8,128)(2,1)S(1)} %collective-permute-done.3.refs_0_, bf16[40,1024]{1,0:T(8,128)(2,1)S(1)} %collective-permute-done.4.refs_1_, bf16[40,1024]{1,0:T(8,128)(2,1)S(1)} %collective-permute-done.5.refs_2_, ...), custom_call_target="tpu_custom_call" | custom-call | flops 503316480 | bytes 3145728 | tf_op jit(solution)/shard_map/pallas_call | solution.py:73
  17.9 1.1 %shard_map.90.mine = bf16[2,80,768]{2,1,0:T(8,128)(2,1)S(1)} custom-call(bf16[80,1024]{1,0:T(8,128)(2,1)S(1)} %get-tuple-element.55.rows_in, bf16[3,768,1024]{2,1,0:T(8,128)(2,1)S(1)} %get-tuple-element.53.refs_5_.held), custom_call_target="tpu_custom_call" | custom-call | flops 25165824000 | bytes 314572800 | tf_op jit(solution)/shard_map/pallas_call | solution.py:73
  19.4 1.6 %collective-permute-start.9 = (bf16[2,80,768]{2,1,0:T(8,128)(2,1)S(1)}, bf16[2,80,768]{2,1,0:T(8,128)(2,1)S(1)}, u32[]{:S(2)}, u32[]{:S(2)}) collective-permute-start(bf16[2,80,768]{2,1,0:T(8,128)(2,1)S(1)} %get-tuple-element.57.refs_6_), channel_id=1, source_target_pairs={{0,2},{1,3},{2,0},{3,1},{4,6},{5,7},{6,4},{7,5},{8,10},{9,11},{10,... | collective-permute-start | bytes 737288 | tf_op jit(solution)/shard_map/ppermute | solution.py:277
  21.0 1.0 %collective-permute-done.1.refs_1_ = bf16[40,1024]{1,0:T(8,128)(2,1)S(1)} collective-permute-done((bf16[40,1024]{1,0:T(8,128)(2,1)S(1)}, bf16[40,1024]{1,0:T(8,128)(2,1)S(1)}, u32[]{:S(2)}, u32[]{:S(2)}) %collective-permute-start.1) | collective-permute-done | bytes 81952 | tf_op jit(solution)/shard_map/ppermute | solution.py:277
  22.0 0.7 %shard_map.92 = bf16[80,768]{1,0:T(8,128)(2,1)S(1)} custom-call(bf16[40,1024]{1,0:T(8,128)(2,1)S(1)} %collective-permute-done.refs_0_, bf16[40,1024]{1,0:T(8,128)(2,1)S(1)} %collective-permute-done.1.refs_1_, bf16[40,1024]{1,0:T(8,128)(2,1)S(1)} %collective-permute-done.2.refs_2_, bf16[40,1024]{1,0:T(8,128)(2,1)S(1)} %get-tuple-element.46.refs_3_, ...), custom_call_target="tpu_custom_call" | custom-call | flops 251658240 | bytes 3145728 | tf_op jit(solution)/shard_map/pallas_call | solution.py:73
  22.8 0.7 %shard_map.89 = (bf16[80,1024]{1,0:T(8,128)(2,1)S(1)}, bf16[80,768]{1,0:T(8,128)(2,1)S(1)}) custom-call(bf16[40,1024]{1,0:T(8,128)(2,1)S(1)} %collective-permute-done.refs_0_, bf16[40,1024]{1,0:T(8,128)(2,1)S(1)} %collective-permute-done.1.refs_1_, bf16[40,1024]{1,0:T(8,128)(2,1)S(1)} %collective-permute-done.2.refs_2_, ...), custom_call_target="tpu_custom_call" | custom-call | flops 25165824000 | bytes 314572800 | tf_op jit(solution)/shard_map/pallas_call | solution.py:73
  24.1 1.6 %collective-permute-start.8 = (bf16[80,768]{1,0:T(8,128)(2,1)S(1)}, bf16[80,768]{1,0:T(8,128)(2,1)S(1)}, u32[]{:S(2)}, u32[]{:S(2)}) collective-permute-start(bf16[80,768]{1,0:T(8,128)(2,1)S(1)} %get-tuple-element.69), channel_id=1, source_target_pairs={{0,2},{1,3},{2,0},{3,1},{4,6},{5,7},{6,4},{7,5},{8,10},{9,11},{10,... | collective-permute-start | bytes 368648 | tf_op jit(solution)/shard_map/ppermute | solution.py:277
  25.7 2.3 %collective-permute-done.9.pair_far = bf16[2,80,768]{2,1,0:T(8,128)(2,1)S(1)} collective-permute-done((bf16[2,80,768]{2,1,0:T(8,128)(2,1)S(1)}, bf16[2,80,768]{2,1,0:T(8,128)(2,1)S(1)}, u32[]{:S(2)}, u32[]{:S(2)}) %collective-permute-start.9) | collective-permute-done | bytes 245792 | tf_op jit(solution)/shard_map/ppermute | solution.py:277
  28.2 1.9 %collective-permute-done.8.act_far = bf16[80,768]{1,0:T(8,128)(2,1)S(1)} collective-permute-done((bf16[80,768]{1,0:T(8,128)(2,1)S(1)}, bf16[80,768]{1,0:T(8,128)(2,1)S(1)}, u32[]{:S(2)}, u32[]{:S(2)}) %collective-permute-start.8) | collective-permute-done | bytes 122912 | tf_op jit(solution)/shard_map/ppermute | solution.py:277
  30.3 0.7 %shard_map.95.total = f32[80,1024]{1,0:T(8,128)S(1)} custom-call(bf16[2,80,768]{2,1,0:T(8,128)(2,1)S(1)} %shard_map.94.mine, bf16[3,768,1024]{2,1,0:T(8,128)(2,1)S(1)} %get-tuple-element.53.refs_5_.held), custom_call_target="tpu_custom_call" | custom-call | flops 251658240 | bytes 3145728 | tf_op jit(solution)/shard_map/pallas_call | solution.py:73
  30.9 0.8 %collective-permute-done.11.other = bf16[2,80,768]{2,1,0:T(8,128)(2,1)S(1)} collective-permute-done((bf16[2,80,768]{2,1,0:T(8,128)(2,1)S(1)}, bf16[2,80,768]{2,1,0:T(8,128)(2,1)S(1)}, u32[]{:S(2)}, u32[]{:S(2)}) %collective-permute-start.11) | collective-permute-done | bytes 245792 | tf_op jit(solution)/shard_map/ppermute | solution.py:277
  31.8 0.8 %shard_map.96 = (bf16[40,1024]{1,0:T(8,128)(2,1)S(1)}, bf16[40,1024]{1,0:T(8,128)(2,1)S(1)}, bf16[40,1024]{1,0:T(8,128)(2,1)S(1)}, bf16[40,1024]{1,0:T(8,128)(2,1)S(1)}) custom-call(f32[80,1024]{1,0:T(8,128)S(1)} %shard_map.95.total, bf16[2,80,768]{2,1,0:T(8,128)(2,1)S(1)} %collective-permute-done.11.other, ...), custom_call_target="tpu_custom_call" | custom-call | flops 251658240 | bytes 3145728 | tf_op jit(solution)/shard_map/pallas_call | solution.py:73
  32.6 2.0 %collective-permute-start.12 = (bf16[40,1024]{1,0:T(8,128)(2,1)S(1)}, bf16[40,1024]{1,0:T(8,128)(2,1)S(1)}, u32[]{:S(2)}, u32[]{:S(2)}) collective-permute-start(bf16[40,1024]{1,0:T(8,128)(2,1)S(1)} %get-tuple-element.62), channel_id=1, source_target_pairs={{0,8},{4,12},{8,0},{12,4},{1,9},{5,13},{9,1},{13,5},{2,10},{6,14},... | collective-permute-start | bytes 245768 | tf_op jit(solution)/shard_map/ppermute | solution.py:277
  34.6 1.3 %collective-permute-start.13 = (bf16[40,1024]{1,0:T(8,128)(2,1)S(1)}, bf16[40,1024]{1,0:T(8,128)(2,1)S(1)}, u32[]{:S(2)}, u32[]{:S(2)}) collective-permute-start(bf16[40,1024]{1,0:T(8,128)(2,1)S(1)} %get-tuple-element.63), channel_id=1, source_target_pairs={{0,12},{4,8},{8,4},{12,0},{1,13},{5,9},{9,5},{13,1},{2,14},{6,10},... | collective-permute-start | bytes 245768 | tf_op jit(solution)/shard_map/ppermute | solution.py:277
  36.2 4.1 %shard_map.98 = (bf16[1,2,1536,1024]{3,2,1,0:T(8,128)(2,1)}, bf16[1,1536,1024]{2,1,0:T(8,128)(2,1)}) custom-call(bf16[80,768]{1,0:T(8,128)(2,1)S(1)} %get-tuple-element.61.mine_act, bf16[80,768]{1,0:T(8,128)(2,1)S(1)} %collective-permute-done.10._.other_act, bf16[2,80,768]{2,1,0:T(8,128)(2,1)S(1)} %shard_map.94.mine, ...), custom_call_target="tpu_custom_call" | custom-call | flops 754974720 | bytes 9437184 | tf_op jit(solution)/shard_map/pallas_call | solution.py:73
  40.3 1.7 %collective-permute-done.12.refs_0_ = bf16[40,1024]{1,0:T(8,128)(2,1)S(1)} collective-permute-done((bf16[40,1024]{1,0:T(8,128)(2,1)S(1)}, bf16[40,1024]{1,0:T(8,128)(2,1)S(1)}, u32[]{:S(2)}, u32[]{:S(2)}) %collective-permute-start.12) | collective-permute-done | bytes 81952 | tf_op jit(solution)/shard_map/ppermute | solution.py:277
  42.0 1.0 %collective-permute-done.14.refs_2_ = bf16[40,1024]{1,0:T(8,128)(2,1)S(1)} collective-permute-done((bf16[40,1024]{1,0:T(8,128)(2,1)S(1)}, bf16[40,1024]{1,0:T(8,128)(2,1)S(1)}, u32[]{:S(2)}, u32[]{:S(2)}) %collective-permute-start.14) | collective-permute-done | bytes 81952 | tf_op jit(solution)/shard_map/ppermute | solution.py:277
  43.0 1.1 %shard_map.97 = bf16[256,1024]{1,0:T(8,128)(2,1)} custom-call(bf16[160,256]{1,0:T(8,128)(2,1)S(1)} %get-tuple-element.36.pick, bf16[40,1024]{1,0:T(8,128)(2,1)S(1)} %collective-permute-done.12.refs_0_, bf16[40,1024]{1,0:T(8,128)(2,1)S(1)} %collective-permute-done.13.refs_1_, bf16[40,1024]{1,0:T(8,128)(2,1)S(1)} %collective-permute-done.14.refs_2_, ...), custom_call_target="tpu_custom_call" | custom-call | flops 83886080 | bytes 1048576 | tf_op jit(solution)/shard_map/pallas_call | solution.py:73
  (21 shorter events, 2.7 us)
Async XLA Ops:
  2.1 13.1 %collective-permute-start.3 = (bf16[40,1024]{1,0:T(8,128)(2,1)S(1)}, bf16[40,1024]{1,0:T(8,128)(2,1)S(1)}, u32[]{:S(2)}, u32[]{:S(2)}) collective-permute-start(bf16[40,1024]{1,0:T(8,128)(2,1)S(1)} %get-tuple-element.47), channel_id=1, source_target_pairs={{0,8},{4,12},{8,0},{12,4},{1,9},{5,13},{9,1},{13,5},{2,10},{6,14},... | collective-permute-start | bytes 245768 | tf_op jit(solution)/shard_map/ppermute | solution.py:277
  6.2 10.1 %collective-permute-start.4 = (bf16[40,1024]{1,0:T(8,128)(2,1)S(1)}, bf16[40,1024]{1,0:T(8,128)(2,1)S(1)}, u32[]{:S(2)}, u32[]{:S(2)}) collective-permute-start(bf16[40,1024]{1,0:T(8,128)(2,1)S(1)} %get-tuple-element.48), channel_id=1, source_target_pairs={{0,12},{4,8},{8,4},{12,0},{1,13},{5,9},{9,5},{13,1},{2,14},{6,10},... | collective-permute-start | bytes 245768 | tf_op jit(solution)/shard_map/ppermute | solution.py:277
  7.6 8.8 %collective-permute-start.5 = (bf16[40,1024]{1,0:T(8,128)(2,1)S(1)}, bf16[40,1024]{1,0:T(8,128)(2,1)S(1)}, u32[]{:S(2)}, u32[]{:S(2)}) collective-permute-start(bf16[40,1024]{1,0:T(8,128)(2,1)S(1)} %get-tuple-element.49), channel_id=1, source_target_pairs={{0,4},{4,0},{8,12},{12,8},{1,5},{5,1},{9,13},{13,9},{2,6},{6,2},{1... | collective-permute-start | bytes 245768 | tf_op jit(solution)/shard_map/ppermute | solution.py:277
  11.9 9.1 %collective-permute-start = (bf16[40,1024]{1,0:T(8,128)(2,1)S(1)}, bf16[40,1024]{1,0:T(8,128)(2,1)S(1)}, u32[]{:S(2)}, u32[]{:S(2)}) collective-permute-start(bf16[40,1024]{1,0:T(8,128)(2,1)S(1)} %get-tuple-element.43), channel_id=1, source_target_pairs={{0,12},{4,8},{8,4},{12,0},{1,13},{5,9},{9,5},{13,1},{2,14},{6,10},... | collective-permute-start | bytes 245768 | tf_op jit(solution)/shard_map/ppermute | solution.py:277
  14.9 7.1 %collective-permute-start.1 = (bf16[40,1024]{1,0:T(8,128)(2,1)S(1)}, bf16[40,1024]{1,0:T(8,128)(2,1)S(1)}, u32[]{:S(2)}, u32[]{:S(2)}) collective-permute-start(bf16[40,1024]{1,0:T(8,128)(2,1)S(1)} %get-tuple-element.44), channel_id=1, source_target_pairs={{0,8},{4,12},{8,0},{12,4},{1,9},{5,13},{9,1},{13,5},{2,10},{6,14},... | collective-permute-start | bytes 245768 | tf_op jit(solution)/shard_map/ppermute | solution.py:277
  15.2 6.8 %collective-permute-start.2 = (bf16[40,1024]{1,0:T(8,128)(2,1)S(1)}, bf16[40,1024]{1,0:T(8,128)(2,1)S(1)}, u32[]{:S(2)}, u32[]{:S(2)}) collective-permute-start(bf16[40,1024]{1,0:T(8,128)(2,1)S(1)} %get-tuple-element.45), channel_id=1, source_target_pairs={{0,4},{4,0},{8,12},{12,8},{1,5},{5,1},{9,13},{13,9},{2,6},{6,2},{1... | collective-permute-start | bytes 245768 | tf_op jit(solution)/shard_map/ppermute | solution.py:277
  17.8 1.6 %collective-permute-start.6 = (bf16[2,80,768]{2,1,0:T(8,128)(2,1)S(1)}, bf16[2,80,768]{2,1,0:T(8,128)(2,1)S(1)}, u32[]{:S(2)}, u32[]{:S(2)}) collective-permute-start(bf16[2,80,768]{2,1,0:T(8,128)(2,1)S(1)} %get-tuple-element.56), channel_id=1, source_target_pairs={{0,1},{1,0},{2,3},{3,2},{4,5},{5,4},{6,7},{7,6},{8,9},{9,8},{10,11... | collective-permute-start | bytes 737288 | tf_op jit(solution)/shard_map/ppermute | solution.py:277
  19.4 8.5 %collective-permute-start.9 = (bf16[2,80,768]{2,1,0:T(8,128)(2,1)S(1)}, bf16[2,80,768]{2,1,0:T(8,128)(2,1)S(1)}, u32[]{:S(2)}, u32[]{:S(2)}) collective-permute-start(bf16[2,80,768]{2,1,0:T(8,128)(2,1)S(1)} %get-tuple-element.57.refs_6_), channel_id=1, source_target_pairs={{0,2},{1,3},{2,0},{3,1},{4,6},{5,7},{6,4},{7,5},{8,10},{9,11},{10,... | collective-permute-start | bytes 737288 | tf_op jit(solution)/shard_map/ppermute | solution.py:277
  22.7 1.4 %collective-permute-start.7 = (bf16[80,768]{1,0:T(8,128)(2,1)S(1)}, bf16[80,768]{1,0:T(8,128)(2,1)S(1)}, u32[]{:S(2)}, u32[]{:S(2)}) collective-permute-start(bf16[80,768]{1,0:T(8,128)(2,1)S(1)} %shard_map.92), channel_id=1, source_target_pairs={{0,1},{1,0},{2,3},{3,2},{4,5},{5,4},{6,7},{7,6},{8,9},{9,8},{10,11... | collective-permute-start | bytes 368648 | tf_op jit(solution)/shard_map/ppermute | solution.py:277
  24.1 6.0 %collective-permute-start.8 = (bf16[80,768]{1,0:T(8,128)(2,1)S(1)}, bf16[80,768]{1,0:T(8,128)(2,1)S(1)}, u32[]{:S(2)}, u32[]{:S(2)}) collective-permute-start(bf16[80,768]{1,0:T(8,128)(2,1)S(1)} %get-tuple-element.69), channel_id=1, source_target_pairs={{0,2},{1,3},{2,0},{3,1},{4,6},{5,7},{6,4},{7,5},{8,10},{9,11},{10,... | collective-permute-start | bytes 368648 | tf_op jit(solution)/shard_map/ppermute | solution.py:277
  28.1 2.0 %collective-permute-start.10 = (bf16[80,768]{1,0:T(8,128)(2,1)S(1)}, bf16[80,768]{1,0:T(8,128)(2,1)S(1)}, u32[]{:S(2)}, u32[]{:S(2)}) collective-permute-start(bf16[80,768]{1,0:T(8,128)(2,1)S(1)} %get-tuple-element.61.mine_act), channel_id=1, source_target_pairs={{0,1},{1,0},{2,3},{3,2},{4,5},{5,4},{6,7},{7,6},{8,9},{9,8},{10,11... | collective-permute-start | bytes 368648 | tf_op jit(solution)/shard_map/ppermute | solution.py:277
  30.2 1.6 %collective-permute-start.11 = (bf16[2,80,768]{2,1,0:T(8,128)(2,1)S(1)}, bf16[2,80,768]{2,1,0:T(8,128)(2,1)S(1)}, u32[]{:S(2)}, u32[]{:S(2)}) collective-permute-start(bf16[2,80,768]{2,1,0:T(8,128)(2,1)S(1)} %shard_map.94.mine), channel_id=1, source_target_pairs={{0,1},{1,0},{2,3},{3,2},{4,5},{5,4},{6,7},{7,6},{8,9},{9,8},{10,11... | collective-permute-start | bytes 737288 | tf_op jit(solution)/shard_map/ppermute | solution.py:277
  32.6 9.4 %collective-permute-start.12 = (bf16[40,1024]{1,0:T(8,128)(2,1)S(1)}, bf16[40,1024]{1,0:T(8,128)(2,1)S(1)}, u32[]{:S(2)}, u32[]{:S(2)}) collective-permute-start(bf16[40,1024]{1,0:T(8,128)(2,1)S(1)} %get-tuple-element.62), channel_id=1, source_target_pairs={{0,8},{4,12},{8,0},{12,4},{1,9},{5,13},{9,1},{13,5},{2,10},{6,14},... | collective-permute-start | bytes 245768 | tf_op jit(solution)/shard_map/ppermute | solution.py:277
  34.6 7.4 %collective-permute-start.13 = (bf16[40,1024]{1,0:T(8,128)(2,1)S(1)}, bf16[40,1024]{1,0:T(8,128)(2,1)S(1)}, u32[]{:S(2)}, u32[]{:S(2)}) collective-permute-start(bf16[40,1024]{1,0:T(8,128)(2,1)S(1)} %get-tuple-element.63), channel_id=1, source_target_pairs={{0,12},{4,8},{8,4},{12,0},{1,13},{5,9},{9,5},{13,1},{2,14},{6,10},... | collective-permute-start | bytes 245768 | tf_op jit(solution)/shard_map/ppermute | solution.py:277
  35.9 7.0 %collective-permute-start.14 = (bf16[40,1024]{1,0:T(8,128)(2,1)S(1)}, bf16[40,1024]{1,0:T(8,128)(2,1)S(1)}, u32[]{:S(2)}, u32[]{:S(2)}) collective-permute-start(bf16[40,1024]{1,0:T(8,128)(2,1)S(1)} %get-tuple-element.64), channel_id=1, source_target_pairs={{0,4},{4,0},{8,12},{12,8},{1,5},{5,1},{9,13},{13,9},{2,6},{6,2},{1... | collective-permute-start | bytes 245768 | tf_op jit(solution)/shard_map/ppermute | solution.py:277

commit v11 on v10

--- a/solution.py
+++ b/solution.py
@@ -222,11 +222,13 @@
     out[...] = mm(mine[0], held[0]) + mm(mine[1], held[1])
 
 
-def other_rows(experts, total, other, place, held, *pieces):
+def other_rows(experts, total, other, place, held, *refs):
+    pieces, whole = refs[:experts], refs[experts]
     rows = total[...] + mm(other[0], held[0]) + mm(other[1], held[1])
-    back = mm(place[...], rows.astype(BF))
-    for k in range(experts):
-        pieces[k][...] = back[k * MOST : (k + 1) * MOST].astype(BF)
+    whole[...] = mm(place[...], rows.astype(BF))
+    me = lax.axis_index("ex")
+    for piece, step in zip(pieces, shifts(experts)):
+        piece[...] = whole[place_of(lax.rem(me + step, experts), experts)].astype(BF)
 
 
 def weight_grads(mine_act, other_act, mine, other, rows_in, rows_grad, pair_out, down_out, held, sems):
@@ -256,8 +258,11 @@
 
 
 def combine(experts, pick, *refs):
-    out, held, sems = refs[experts:]
-    home = stacked(refs[:experts]).astype(BF)
+    out, whole, held, sems = refs[experts:]
+    me = lax.axis_index("ex")
+    for piece, step in zip(refs[:experts], shifts(experts)):
+        whole[place_of(lax.rem(me + experts - step, experts), experts)] = piece[...].astype(F32)
+    home = whole[...].astype(BF)
     rows = out.shape[0] // held.shape[0]
     stores = []
     for at in range(held.shape[0]):
@@ -270,6 +275,23 @@
 
 def far(value):
     return pltpu.with_memory_space_constraint(value, pltpu.HBM)
+
+
+def place_of(partner, experts):
+    k = lax.axis_index("ex") ^ partner
+    spot = jnp.int32(0)
+    for at, name in enumerate(far_first(experts)):
+        spot = spot + jnp.where(k == name, at * MOST, 0)
+    return pl.ds(pl.multiple_of(spot, 8), MOST)
+
+
+def shifts(experts):
+    return list(range(1, experts)) + [0]
+
+
+def shift(value, axis, step):
+    count = lax.axis_size(axis)
+    return lax.ppermute(value, axis, [(i, (i + step) % count) for i in range(count)])
 
 
 def swap(value, axis, bit):
@@ -415,10 +437,11 @@
         piece,
         (own, other, place, held_other),
         [VMEM] * 4,
+        [pltpu.VMEM((rows, width), F32)],
         flops=weight_flops,
         traffic=weight_bytes,
     )
-    home = exchange(back, "ex")
+    home = [shift(part, "ex", step) if step else part for part, step in zip(back, shifts(experts))]
     pair_grad, down_grad = call(
         weight_grads,
         [sds((1, 2, hidden, width), BF), sds((1, hidden, width), BF)],
@@ -435,7 +458,7 @@
         sds((tokens, width), BF),
         (pick, *home),
         [VMEM] * (experts + 1),
-        [pltpu.VMEM((2, tokens // 2, width), BF), dma(2)],
+        [pltpu.VMEM((rows, width), F32), pltpu.VMEM((2, tokens // 2, width), BF), dma(2)],
         flops=2 * rows * tokens * width,
         traffic=4 * tokens * width,
         out_specs=ANY,

time: 44.2 us -> 43.9 us (level)
  waiting for transfers between devices: 9.8 us -> 8.07 us
  starting transfers between devices: 17.1 us -> 18.4 us
    ppermute x0 -> x3, starting transfers between devices: none -> 4.88 us  [shift(): lax.ppermute(value, axis, [(i, (i + step) % count) for i in range(count)])]
    ppermute x15 -> x12, starting transfers between devices: 17.1 us -> 13.5 us  [swap(): return lax.ppermute(value, axis, [(i, i ^ bit) for i in range(count)])]
    ppermute x15 -> x12, waiting for transfers between devices: 9.8 us -> 7.12 us  [swap(): return lax.ppermute(value, axis, [(i, i ^ bit) for i in range(count)])]
    ppermute x0 -> x3, waiting for transfers between devices: none -> 0.95 us  [shift(): lax.ppermute(value, axis, [(i, (i + step) % count) for i in range(count)])]
  transfers between devices with their start and end apart: 15 -> 15, of which waited for: 8 -> 7; matrix products, arithmetic and copies ran while one was open for 0% -> 0% of each run, Pallas kernels for 29% -> 30%
where the time goes in v11:
time: 43.9 us; the launch traced here: 43.7 us
  starting transfers between devices  18.4 us (42%)
  Pallas kernels  16.4 us (37%)
  waiting for transfers between devices  8.07 us (18%)
  between operations  0.75 us (2%)
    pallas_call x14, Pallas kernels, call(): pl.pallas_call(body, out_shape=outs, in_specs=specs, out_specs=out_specs...  16.4 us
    ppermute x12, starting transfers between devices, swap(): return lax.ppermute(value, axis, [(i, i ^ bit) for i in range(count)])  13.5 us
    ppermute x12, waiting for transfers between devices, swap(): return lax.ppermute(value, axis, [(i, i ^ bit) for i in range(count)])  7.12 us
    ppermute x3, starting transfers between devices, shift(): lax.ppermute(value, axis, [(i, (i + step) % count) for i in range(count)])  4.88 us
    ppermute x3, waiting for transfers between devices, shift(): lax.ppermute(value, axis, [(i, (i + step) % count) for i in range(count)])  0.95 us
  transfers between devices with their start and end apart: 15, of which 7 were waited for; matrix products, arithmetic and copies ran while one was open for 0% of the time, Pallas kernels for 30%

profile of v11, /device:TPU:0, one launch (start us, length us, event | category | flops | bytes accessed | tf_op | source)
XLA Modules:
  0.0 43.7 jit_solution(14217610710304333199)
XLA Ops:
  0.6 1.5 %shard_map.85 = (bf16[160,256]{1,0:T(8,128)(2,1)S(1)}, f32[160,1]{1,0:T(8,128)S(1)}, bf16[256,1024]{1,0:T(8,128)(2,1)S(1)}, bf16[40,1024]{1,0:T(8,128)(2,1)S(1)}...) custom-call(s32[8,256]{1,0:T(8,128)} %bitcast.2, ...), custom_call_target="tpu_custom_call" | custom-call | flops 83886080 | bytes 1048576 | tf_op jit(solution)/shard_map/pallas_call | solution.py:73
  2.1 4.1 %collective-permute-start.3 = (bf16[40,1024]{1,0:T(8,128)(2,1)S(1)}, bf16[40,1024]{1,0:T(8,128)(2,1)S(1)}, u32[]{:S(2)}, u32[]{:S(2)}) collective-permute-start(bf16[40,1024]{1,0:T(8,128)(2,1)S(1)} %get-tuple-element.47), channel_id=1, source_target_pairs={{0,8},{4,12},{8,0},{12,4},{1,9},{5,13},{9,1},{13,5},{2,10},{6,14},... | collective-permute-start | bytes 245768 | tf_op jit(solution)/shard_map/ppermute | solution.py:299
  6.2 1.3 %collective-permute-start.4 = (bf16[40,1024]{1,0:T(8,128)(2,1)S(1)}, bf16[40,1024]{1,0:T(8,128)(2,1)S(1)}, u32[]{:S(2)}, u32[]{:S(2)}) collective-permute-start(bf16[40,1024]{1,0:T(8,128)(2,1)S(1)} %get-tuple-element.48), channel_id=1, source_target_pairs={{0,12},{4,8},{8,4},{12,0},{1,13},{5,9},{9,5},{13,1},{2,14},{6,10},... | collective-permute-start | bytes 245768 | tf_op jit(solution)/shard_map/ppermute | solution.py:299
  8.1 3.8 %shard_map.87 = (bf16[3,768,1024]{2,1,0:T(8,128)(2,1)S(1)}, bf16[3,768,1024]{2,1,0:T(8,128)(2,1)S(1)}, bf16[40,1024]{1,0:T(8,128)(2,1)S(1)}, bf16[40,1024]{1,0:T...) custom-call(bf16[1,2,1536,1024]{3,2,1,0:T(8,128)(2,1)} %gate_up.1, ...), custom_call_target="tpu_custom_call" | custom-call | flops 25165824000 | bytes 314572800 | tf_op jit(solution)/shard_map/pallas_call | solution.py:73
  11.9 3.0 %collective-permute-start = (bf16[40,1024]{1,0:T(8,128)(2,1)S(1)}, bf16[40,1024]{1,0:T(8,128)(2,1)S(1)}, u32[]{:S(2)}, u32[]{:S(2)}) collective-permute-start(bf16[40,1024]{1,0:T(8,128)(2,1)S(1)} %get-tuple-element.43), channel_id=1, source_target_pairs={{0,12},{4,8},{8,4},{12,0},{1,13},{5,9},{9,5},{13,1},{2,14},{6,10},... | collective-permute-start | bytes 245768 | tf_op jit(solution)/shard_map/ppermute | solution.py:299
  15.2 1.1 %collective-permute-start.2 = (bf16[40,1024]{1,0:T(8,128)(2,1)S(1)}, bf16[40,1024]{1,0:T(8,128)(2,1)S(1)}, u32[]{:S(2)}, u32[]{:S(2)}) collective-permute-start(bf16[40,1024]{1,0:T(8,128)(2,1)S(1)} %get-tuple-element.45), channel_id=1, source_target_pairs={{0,4},{4,0},{8,12},{12,8},{1,5},{5,1},{9,13},{13,9},{2,6},{6,2},{1... | collective-permute-start | bytes 245768 | tf_op jit(solution)/shard_map/ppermute | solution.py:299
  16.3 1.4 %shard_map.88 = (bf16[2,80,768]{2,1,0:T(8,128)(2,1)S(1)}, bf16[160,80]{1,0:T(8,128)(2,1)S(1)}, bf16[80,1024]{1,0:T(8,128)(2,1)S(1)}) custom-call(bf16[40,1024]{1,0:T(8,128)(2,1)S(1)} %collective-permute-done.3.refs_0_, bf16[40,1024]{1,0:T(8,128)(2,1)S(1)} %collective-permute-done.4.refs_1_, bf16[40,1024]{1,0:T(8,128)(2,1)S(1)} %collective-permute-done.5.refs_2_, ...), custom_call_target="tpu_custom_call" | custom-call | flops 503316480 | bytes 3145728 | tf_op jit(solution)/shard_map/pallas_call | solution.py:73
  17.9 1.1 %shard_map.90.mine = bf16[2,80,768]{2,1,0:T(8,128)(2,1)S(1)} custom-call(bf16[80,1024]{1,0:T(8,128)(2,1)S(1)} %get-tuple-element.55.rows_in, bf16[3,768,1024]{2,1,0:T(8,128)(2,1)S(1)} %get-tuple-element.53.refs_5_.held), custom_call_target="tpu_custom_call" | custom-call | flops 25165824000 | bytes 314572800 | tf_op jit(solution)/shard_map/pallas_call | solution.py:73
  19.4 1.6 %collective-permute-start.9 = (bf16[2,80,768]{2,1,0:T(8,128)(2,1)S(1)}, bf16[2,80,768]{2,1,0:T(8,128)(2,1)S(1)}, u32[]{:S(2)}, u32[]{:S(2)}) collective-permute-start(bf16[2,80,768]{2,1,0:T(8,128)(2,1)S(1)} %get-tuple-element.57.refs_6_), channel_id=1, source_target_pairs={{0,2},{1,3},{2,0},{3,1},{4,6},{5,7},{6,4},{7,5},{8,10},{9,11},{10,... | collective-permute-start | bytes 737288 | tf_op jit(solution)/shard_map/ppermute | solution.py:299
  21.0 1.0 %collective-permute-done.1.refs_1_ = bf16[40,1024]{1,0:T(8,128)(2,1)S(1)} collective-permute-done((bf16[40,1024]{1,0:T(8,128)(2,1)S(1)}, bf16[40,1024]{1,0:T(8,128)(2,1)S(1)}, u32[]{:S(2)}, u32[]{:S(2)}) %collective-permute-start.1) | collective-permute-done | bytes 81952 | tf_op jit(solution)/shard_map/ppermute | solution.py:299
  22.0 0.7 %shard_map.92 = bf16[80,768]{1,0:T(8,128)(2,1)S(1)} custom-call(bf16[40,1024]{1,0:T(8,128)(2,1)S(1)} %collective-permute-done.refs_0_, bf16[40,1024]{1,0:T(8,128)(2,1)S(1)} %collective-permute-done.1.refs_1_, bf16[40,1024]{1,0:T(8,128)(2,1)S(1)} %collective-permute-done.2.refs_2_, bf16[40,1024]{1,0:T(8,128)(2,1)S(1)} %get-tuple-element.46.refs_3_, ...), custom_call_target="tpu_custom_call" | custom-call | flops 251658240 | bytes 3145728 | tf_op jit(solution)/shard_map/pallas_call | solution.py:73
  22.8 0.7 %shard_map.89 = (bf16[80,1024]{1,0:T(8,128)(2,1)S(1)}, bf16[80,768]{1,0:T(8,128)(2,1)S(1)}) custom-call(bf16[40,1024]{1,0:T(8,128)(2,1)S(1)} %collective-permute-done.refs_0_, bf16[40,1024]{1,0:T(8,128)(2,1)S(1)} %collective-permute-done.1.refs_1_, bf16[40,1024]{1,0:T(8,128)(2,1)S(1)} %collective-permute-done.2.refs_2_, ...), custom_call_target="tpu_custom_call" | custom-call | flops 25165824000 | bytes 314572800 | tf_op jit(solution)/shard_map/pallas_call | solution.py:73
  24.1 1.6 %collective-permute-start.8 = (bf16[80,768]{1,0:T(8,128)(2,1)S(1)}, bf16[80,768]{1,0:T(8,128)(2,1)S(1)}, u32[]{:S(2)}, u32[]{:S(2)}) collective-permute-start(bf16[80,768]{1,0:T(8,128)(2,1)S(1)} %get-tuple-element.69), channel_id=1, source_target_pairs={{0,2},{1,3},{2,0},{3,1},{4,6},{5,7},{6,4},{7,5},{8,10},{9,11},{10,... | collective-permute-start | bytes 368648 | tf_op jit(solution)/shard_map/ppermute | solution.py:299
  25.7 2.3 %collective-permute-done.9.pair_far = bf16[2,80,768]{2,1,0:T(8,128)(2,1)S(1)} collective-permute-done((bf16[2,80,768]{2,1,0:T(8,128)(2,1)S(1)}, bf16[2,80,768]{2,1,0:T(8,128)(2,1)S(1)}, u32[]{:S(2)}, u32[]{:S(2)}) %collective-permute-start.9) | collective-permute-done | bytes 245792 | tf_op jit(solution)/shard_map/ppermute | solution.py:299
  28.2 1.9 %collective-permute-done.8.act_far = bf16[80,768]{1,0:T(8,128)(2,1)S(1)} collective-permute-done((bf16[80,768]{1,0:T(8,128)(2,1)S(1)}, bf16[80,768]{1,0:T(8,128)(2,1)S(1)}, u32[]{:S(2)}, u32[]{:S(2)}) %collective-permute-start.8) | collective-permute-done | bytes 122912 | tf_op jit(solution)/shard_map/ppermute | solution.py:299
  30.3 0.7 %shard_map.95.total = f32[80,1024]{1,0:T(8,128)S(1)} custom-call(bf16[2,80,768]{2,1,0:T(8,128)(2,1)S(1)} %shard_map.94.mine, bf16[3,768,1024]{2,1,0:T(8,128)(2,1)S(1)} %get-tuple-element.53.refs_5_.held), custom_call_target="tpu_custom_call" | custom-call | flops 251658240 | bytes 3145728 | tf_op jit(solution)/shard_map/pallas_call | solution.py:73
  30.9 0.8 %collective-permute-done.11.other = bf16[2,80,768]{2,1,0:T(8,128)(2,1)S(1)} collective-permute-done((bf16[2,80,768]{2,1,0:T(8,128)(2,1)S(1)}, bf16[2,80,768]{2,1,0:T(8,128)(2,1)S(1)}, u32[]{:S(2)}, u32[]{:S(2)}) %collective-permute-start.11) | collective-permute-done | bytes 245792 | tf_op jit(solution)/shard_map/ppermute | solution.py:299
  31.8 0.9 %shard_map.96 = (bf16[40,1024]{1,0:T(8,128)(2,1)S(1)}, bf16[40,1024]{1,0:T(8,128)(2,1)S(1)}, bf16[40,1024]{1,0:T(8,128)(2,1)S(1)}, bf16[40,1024]{1,0:T(8,128)(2,1)S(1)}) custom-call(f32[80,1024]{1,0:T(8,128)S(1)} %shard_map.95.total, bf16[2,80,768]{2,1,0:T(8,128)(2,1)S(1)} %collective-permute-done.11.other, ...), custom_call_target="tpu_custom_call" | custom-call | flops 251658240 | bytes 3145728 | tf_op jit(solution)/shard_map/pallas_call | solution.py:73
  32.7 0.9 %collective-permute-start.12 = (bf16[40,1024]{1,0:T(8,128)(2,1)S(1)}, bf16[40,1024]{1,0:T(8,128)(2,1)S(1)}, u32[]{:S(2)}, u32[]{:S(2)}) collective-permute-start(bf16[40,1024]{1,0:T(8,128)(2,1)S(1)} %get-tuple-element.62), channel_id=1, source_target_pairs={{0,4},{4,8},{8,12},{12,0},{1,5},{5,9},{9,13},{13,1},{2,6},{6,10},{... | collective-permute-start | bytes 245768 | tf_op jit(solution)/shard_map/ppermute | solution.py:294
  33.6 2.6 %collective-permute-start.13 = (bf16[40,1024]{1,0:T(8,128)(2,1)S(1)}, bf16[40,1024]{1,0:T(8,128)(2,1)S(1)}, u32[]{:S(2)}, u32[]{:S(2)}) collective-permute-start(bf16[40,1024]{1,0:T(8,128)(2,1)S(1)} %get-tuple-element.63), channel_id=1, source_target_pairs={{0,8},{4,12},{8,0},{12,4},{1,9},{5,13},{9,1},{13,5},{2,10},{6,14},... | collective-permute-start | bytes 245768 | tf_op jit(solution)/shard_map/ppermute | solution.py:294
  36.2 1.3 %collective-permute-start.14 = (bf16[40,1024]{1,0:T(8,128)(2,1)S(1)}, bf16[40,1024]{1,0:T(8,128)(2,1)S(1)}, u32[]{:S(2)}, u32[]{:S(2)}) collective-permute-start(bf16[40,1024]{1,0:T(8,128)(2,1)S(1)} %get-tuple-element.64), channel_id=1, source_target_pairs={{0,12},{4,0},{8,4},{12,8},{1,13},{5,1},{9,5},{13,9},{2,14},{6,2},{... | collective-permute-start | bytes 245768 | tf_op jit(solution)/shard_map/ppermute | solution.py:294
  37.5 4.1 %shard_map.98 = (bf16[1,2,1536,1024]{3,2,1,0:T(8,128)(2,1)}, bf16[1,1536,1024]{2,1,0:T(8,128)(2,1)}) custom-call(bf16[80,768]{1,0:T(8,128)(2,1)S(1)} %get-tuple-element.61.mine_act, bf16[80,768]{1,0:T(8,128)(2,1)S(1)} %collective-permute-done.10._.other_act, bf16[2,80,768]{2,1,0:T(8,128)(2,1)S(1)} %shard_map.94.mine, ...), custom_call_target="tpu_custom_call" | custom-call | flops 754974720 | bytes 9437184 | tf_op jit(solution)/shard_map/pallas_call | solution.py:73
  41.7 0.9 %collective-permute-done.13.refs_1_ = bf16[40,1024]{1,0:T(8,128)(2,1)S(1)} collective-permute-done((bf16[40,1024]{1,0:T(8,128)(2,1)S(1)}, bf16[40,1024]{1,0:T(8,128)(2,1)S(1)}, u32[]{:S(2)}, u32[]{:S(2)}) %collective-permute-start.13) | collective-permute-done | bytes 81952 | tf_op jit(solution)/shard_map/ppermute | solution.py:294
  42.6 1.1 %shard_map.97 = bf16[256,1024]{1,0:T(8,128)(2,1)} custom-call(bf16[160,256]{1,0:T(8,128)(2,1)S(1)} %get-tuple-element.36.pick, bf16[40,1024]{1,0:T(8,128)(2,1)S(1)} %collective-permute-done.12.refs_0_, bf16[40,1024]{1,0:T(8,128)(2,1)S(1)} %collective-permute-done.13.refs_1_, bf16[40,1024]{1,0:T(8,128)(2,1)S(1)} %collective-permute-done.14.refs_2_, ...), custom_call_target="tpu_custom_call" | custom-call | flops 83886080 | bytes 1048576 | tf_op jit(solution)/shard_map/pallas_call | solution.py:73
  (21 shorter events, 2.5 us)
Async XLA Ops:
  2.1 13.1 %collective-permute-start.3 = (bf16[40,1024]{1,0:T(8,128)(2,1)S(1)}, bf16[40,1024]{1,0:T(8,128)(2,1)S(1)}, u32[]{:S(2)}, u32[]{:S(2)}) collective-permute-start(bf16[40,1024]{1,0:T(8,128)(2,1)S(1)} %get-tuple-element.47), channel_id=1, source_target_pairs={{0,8},{4,12},{8,0},{12,4},{1,9},{5,13},{9,1},{13,5},{2,10},{6,14},... | collective-permute-start | bytes 245768 | tf_op jit(solution)/shard_map/ppermute | solution.py:299
  6.2 10.1 %collective-permute-start.4 = (bf16[40,1024]{1,0:T(8,128)(2,1)S(1)}, bf16[40,1024]{1,0:T(8,128)(2,1)S(1)}, u32[]{:S(2)}, u32[]{:S(2)}) collective-permute-start(bf16[40,1024]{1,0:T(8,128)(2,1)S(1)} %get-tuple-element.48), channel_id=1, source_target_pairs={{0,12},{4,8},{8,4},{12,0},{1,13},{5,9},{9,5},{13,1},{2,14},{6,10},... | collective-permute-start | bytes 245768 | tf_op jit(solution)/shard_map/ppermute | solution.py:299
  7.6 8.8 %collective-permute-start.5 = (bf16[40,1024]{1,0:T(8,128)(2,1)S(1)}, bf16[40,1024]{1,0:T(8,128)(2,1)S(1)}, u32[]{:S(2)}, u32[]{:S(2)}) collective-permute-start(bf16[40,1024]{1,0:T(8,128)(2,1)S(1)} %get-tuple-element.49), channel_id=1, source_target_pairs={{0,4},{4,0},{8,12},{12,8},{1,5},{5,1},{9,13},{13,9},{2,6},{6,2},{1... | collective-permute-start | bytes 245768 | tf_op jit(solution)/shard_map/ppermute | solution.py:299
  11.9 9.1 %collective-permute-start = (bf16[40,1024]{1,0:T(8,128)(2,1)S(1)}, bf16[40,1024]{1,0:T(8,128)(2,1)S(1)}, u32[]{:S(2)}, u32[]{:S(2)}) collective-permute-start(bf16[40,1024]{1,0:T(8,128)(2,1)S(1)} %get-tuple-element.43), channel_id=1, source_target_pairs={{0,12},{4,8},{8,4},{12,0},{1,13},{5,9},{9,5},{13,1},{2,14},{6,10},... | collective-permute-start | bytes 245768 | tf_op jit(solution)/shard_map/ppermute | solution.py:299
  14.9 7.1 %collective-permute-start.1 = (bf16[40,1024]{1,0:T(8,128)(2,1)S(1)}, bf16[40,1024]{1,0:T(8,128)(2,1)S(1)}, u32[]{:S(2)}, u32[]{:S(2)}) collective-permute-start(bf16[40,1024]{1,0:T(8,128)(2,1)S(1)} %get-tuple-element.44), channel_id=1, source_target_pairs={{0,8},{4,12},{8,0},{12,4},{1,9},{5,13},{9,1},{13,5},{2,10},{6,14},... | collective-permute-start | bytes 245768 | tf_op jit(solution)/shard_map/ppermute | solution.py:299
  15.2 6.8 %collective-permute-start.2 = (bf16[40,1024]{1,0:T(8,128)(2,1)S(1)}, bf16[40,1024]{1,0:T(8,128)(2,1)S(1)}, u32[]{:S(2)}, u32[]{:S(2)}) collective-permute-start(bf16[40,1024]{1,0:T(8,128)(2,1)S(1)} %get-tuple-element.45), channel_id=1, source_target_pairs={{0,4},{4,0},{8,12},{12,8},{1,5},{5,1},{9,13},{13,9},{2,6},{6,2},{1... | collective-permute-start | bytes 245768 | tf_op jit(solution)/shard_map/ppermute | solution.py:299
  17.8 1.6 %collective-permute-start.6 = (bf16[2,80,768]{2,1,0:T(8,128)(2,1)S(1)}, bf16[2,80,768]{2,1,0:T(8,128)(2,1)S(1)}, u32[]{:S(2)}, u32[]{:S(2)}) collective-permute-start(bf16[2,80,768]{2,1,0:T(8,128)(2,1)S(1)} %get-tuple-element.56), channel_id=1, source_target_pairs={{0,1},{1,0},{2,3},{3,2},{4,5},{5,4},{6,7},{7,6},{8,9},{9,8},{10,11... | collective-permute-start | bytes 737288 | tf_op jit(solution)/shard_map/ppermute | solution.py:299
  19.4 8.5 %collective-permute-start.9 = (bf16[2,80,768]{2,1,0:T(8,128)(2,1)S(1)}, bf16[2,80,768]{2,1,0:T(8,128)(2,1)S(1)}, u32[]{:S(2)}, u32[]{:S(2)}) collective-permute-start(bf16[2,80,768]{2,1,0:T(8,128)(2,1)S(1)} %get-tuple-element.57.refs_6_), channel_id=1, source_target_pairs={{0,2},{1,3},{2,0},{3,1},{4,6},{5,7},{6,4},{7,5},{8,10},{9,11},{10,... | collective-permute-start | bytes 737288 | tf_op jit(solution)/shard_map/ppermute | solution.py:299
  22.7 1.4 %collective-permute-start.7 = (bf16[80,768]{1,0:T(8,128)(2,1)S(1)}, bf16[80,768]{1,0:T(8,128)(2,1)S(1)}, u32[]{:S(2)}, u32[]{:S(2)}) collective-permute-start(bf16[80,768]{1,0:T(8,128)(2,1)S(1)} %shard_map.92), channel_id=1, source_target_pairs={{0,1},{1,0},{2,3},{3,2},{4,5},{5,4},{6,7},{7,6},{8,9},{9,8},{10,11... | collective-permute-start | bytes 368648 | tf_op jit(solution)/shard_map/ppermute | solution.py:299
  24.1 6.0 %collective-permute-start.8 = (bf16[80,768]{1,0:T(8,128)(2,1)S(1)}, bf16[80,768]{1,0:T(8,128)(2,1)S(1)}, u32[]{:S(2)}, u32[]{:S(2)}) collective-permute-start(bf16[80,768]{1,0:T(8,128)(2,1)S(1)} %get-tuple-element.69), channel_id=1, source_target_pairs={{0,2},{1,3},{2,0},{3,1},{4,6},{5,7},{6,4},{7,5},{8,10},{9,11},{10,... | collective-permute-start | bytes 368648 | tf_op jit(solution)/shard_map/ppermute | solution.py:299
  28.1 2.0 %collective-permute-start.10 = (bf16[80,768]{1,0:T(8,128)(2,1)S(1)}, bf16[80,768]{1,0:T(8,128)(2,1)S(1)}, u32[]{:S(2)}, u32[]{:S(2)}) collective-permute-start(bf16[80,768]{1,0:T(8,128)(2,1)S(1)} %get-tuple-element.61.mine_act), channel_id=1, source_target_pairs={{0,1},{1,0},{2,3},{3,2},{4,5},{5,4},{6,7},{7,6},{8,9},{9,8},{10,11... | collective-permute-start | bytes 368648 | tf_op jit(solution)/shard_map/ppermute | solution.py:299
  30.2 1.6 %collective-permute-start.11 = (bf16[2,80,768]{2,1,0:T(8,128)(2,1)S(1)}, bf16[2,80,768]{2,1,0:T(8,128)(2,1)S(1)}, u32[]{:S(2)}, u32[]{:S(2)}) collective-permute-start(bf16[2,80,768]{2,1,0:T(8,128)(2,1)S(1)} %shard_map.94.mine), channel_id=1, source_target_pairs={{0,1},{1,0},{2,3},{3,2},{4,5},{5,4},{6,7},{7,6},{8,9},{9,8},{10,11... | collective-permute-start | bytes 737288 | tf_op jit(solution)/shard_map/ppermute | solution.py:299
  32.7 9.0 %collective-permute-start.12 = (bf16[40,1024]{1,0:T(8,128)(2,1)S(1)}, bf16[40,1024]{1,0:T(8,128)(2,1)S(1)}, u32[]{:S(2)}, u32[]{:S(2)}) collective-permute-start(bf16[40,1024]{1,0:T(8,128)(2,1)S(1)} %get-tuple-element.62), channel_id=1, source_target_pairs={{0,4},{4,8},{8,12},{12,0},{1,5},{5,9},{9,13},{13,1},{2,6},{6,10},{... | collective-permute-start | bytes 245768 | tf_op jit(solution)/shard_map/ppermute | solution.py:294
  33.6 9.0 %collective-permute-start.13 = (bf16[40,1024]{1,0:T(8,128)(2,1)S(1)}, bf16[40,1024]{1,0:T(8,128)(2,1)S(1)}, u32[]{:S(2)}, u32[]{:S(2)}) collective-permute-start(bf16[40,1024]{1,0:T(8,128)(2,1)S(1)} %get-tuple-element.63), channel_id=1, source_target_pairs={{0,8},{4,12},{8,0},{12,4},{1,9},{5,13},{9,1},{13,5},{2,10},{6,14},... | collective-permute-start | bytes 245768 | tf_op jit(solution)/shard_map/ppermute | solution.py:294
  36.2 6.4 %collective-permute-start.14 = (bf16[40,1024]{1,0:T(8,128)(2,1)S(1)}, bf16[40,1024]{1,0:T(8,128)(2,1)S(1)}, u32[]{:S(2)}, u32[]{:S(2)}) collective-permute-start(bf16[40,1024]{1,0:T(8,128)(2,1)S(1)} %get-tuple-element.64), channel_id=1, source_target_pairs={{0,12},{4,0},{8,4},{12,8},{1,13},{5,1},{9,5},{13,9},{2,14},{6,2},{... | collective-permute-start | bytes 245768 | tf_op jit(solution)/shard_map/ppermute | solution.py:294

commit v12 on v11

--- a/solution.py
+++ b/solution.py
@@ -36,10 +36,6 @@
 
 def far_first(count):
     return sorted(range(count), key=lambda k: (-k.bit_length(), k))
-
-
-def farthest_first(count):
-    return list(reversed(range(count)))
 
 
 def cut(source, target, sems, first, pieces):
@@ -124,14 +120,19 @@
     wait(grad_loads)
 
 
-def pick_grads(experts, pick, prob, grads, *pieces):
+def pick_grads(experts, pick, prob, grads, *refs):
+    near_in, near, *pieces = refs
     sent = mm(pick[...], grads[...]) * prob[...]
-    for k in range(experts):
-        pieces[k][...] = sent[k * MOST : (k + 1) * MOST].astype(BF)
-
-
-def stacked(pieces):
-    return jnp.concatenate([piece[...].astype(F32) for piece in pieces], axis=0)
+    parts = [sent[at * MOST : (at + 1) * MOST] for at in range(experts)]
+    near[...] = jnp.concatenate([near_in[...].astype(F32), parts[-2]], axis=0).astype(BF)
+    for target, part in zip(pieces, parts[:-2] + parts[-1:]):
+        target[...] = part.astype(BF)
+
+
+def stacked(pieces, part=0):
+    rows = [piece[...].astype(F32) for piece in pieces]
+    rows = [row[part * MOST : (part + 1) * MOST] if row.shape[0] > MOST else row for row in rows]
+    return jnp.concatenate(rows, axis=0)
 
 
 def rows_of(half, own):
@@ -194,9 +195,8 @@
 
 def act_part(experts, own, *refs):
     place, held = refs[experts : experts + 2]
-    order = far_first(experts)
-    pieces = [refs[:experts][farthest_first(experts).index(k)] for k in order]
-    rows_grad = mm(place[...], stacked(pieces).astype(BF), ROWS).astype(BF)
+    pieces = refs[: experts - 2][::-1] + refs[experts - 2 : experts]
+    rows_grad = mm(place[...], stacked(pieces, 1).astype(BF), ROWS).astype(BF)
     if own:
         refs[-2][...] = rows_grad
     refs[-1][...] = mm(rows_grad, held[2], LANES).astype(BF)
@@ -319,7 +319,7 @@
     dma = lambda count: pltpu.SemaphoreType.DMA((count,))
 
     order = far_first(experts)
-    pick, prob, grads, *send_in = call(
+    pick, prob, grads, *send_in, own_in = call(
         functools.partial(pick_inputs, experts),
         [
             sds((rows, tokens), BF),
@@ -338,28 +338,27 @@
         flops=2 * rows * tokens * width,
         traffic=4 * tokens * width,
     )
-    send_grad = call(
+    near, *send_grad = call(
         functools.partial(pick_grads, experts),
-        piece,
-        (pick, prob, grads),
-        [VMEM] * 3,
+        [sds((2 * MOST, width), BF)] + piece[1:],
+        (pick, prob, grads, send_in[-1]),
+        [VMEM] * 4,
         flops=2 * rows * tokens * width,
         traffic=2 * tokens * width,
     )
-    got_in = exchange(send_in, "ex")
+    near = swap(near, "ex", 1)
+    got_in = [swap(part, "ex", k) for part, k in zip(send_in[:-1], order)] + [near, own_in]
     held_other, held_mine, *send_grad = call(
-        functools.partial(stage, experts),
-        [pltpu.VMEM((3, half, width), BF)] * 2 + piece,
+        functools.partial(stage, experts - 1),
+        [pltpu.VMEM((3, half, width), BF)] * 2 + piece[1:],
         (far(gate_up), far(down_proj), *send_grad),
-        [HBM] * 2 + [VMEM] * experts,
+        [HBM] * 2 + [VMEM] * (experts - 1),
         [dma(6)],
         flops=WCOST * weight_flops,
         traffic=WCOST * weight_bytes,
     )
-    got_grad = [
-        swap(send_grad[order.index(k)], "ex", k) if k else send_grad[-1]
-        for k in farthest_first(experts)
-    ]
+    got_grad = [swap(part, "ex", k) for part, k in zip(send_grad[:-1], order)][::-1]
+    got_grad = got_grad + [near, send_grad[-1]]
     pair_other, place, rows_in = call(
         functools.partial(other_pair, experts, capacity),
         [sds((2, capacity, half), BF), sds((rows, capacity), BF), sds((capacity, width), BF)],

time: 43.9 us -> 43.9 us (level)
  starting transfers between devices: 18.4 us -> 17.6 us
  waiting for transfers between devices: 8.07 us -> 8.84 us
    ppermute x12 -> x11, starting transfers between devices: 13.5 us -> 12.6 us  [swap(): return lax.ppermute(value, axis, [(i, i ^ bit) for i in range(count)])]
    ppermute x12 -> x11, waiting for transfers between devices: 7.12 us -> 7.54 us  [swap(): return lax.ppermute(value, axis, [(i, i ^ bit) for i in range(count)])]
  transfers between devices with their start and end apart: 15 -> 14, of which waited for: 7 -> 9; matrix products, arithmetic and copies ran while one was open for 0% -> 0% of each run, Pallas kernels for 30% -> 30%
where the time goes in v12:
time: 43.9 us; the launch traced here: 43.7 us
  starting transfers between devices  17.6 us (40%)
  Pallas kernels  16.4 us (37%)
  waiting for transfers between devices  8.84 us (20%)
  between operations  0.75 us (2%)
    pallas_call x14, Pallas kernels, call(): pl.pallas_call(body, out_shape=outs, in_specs=specs, out_specs=out_specs...  16.4 us
    ppermute x11, starting transfers between devices, swap(): return lax.ppermute(value, axis, [(i, i ^ bit) for i in range(count)])  12.6 us
    ppermute x11, waiting for transfers between devices, swap(): return lax.ppermute(value, axis, [(i, i ^ bit) for i in range(count)])  7.54 us
    ppermute x3, starting transfers between devices, shift(): lax.ppermute(value, axis, [(i, (i + step) % count) for i in range(count)])  5 us
    ppermute x3, waiting for transfers between devices, shift(): lax.ppermute(value, axis, [(i, (i + step) % count) for i in range(count)])  1.3 us
  transfers between devices with their start and end apart: 14, of which 9 were waited for; matrix products, arithmetic and copies ran while one was open for 0% of the time, Pallas kernels for 30%

profile of v12, /device:TPU:0, one launch (start us, length us, event | category | flops | bytes accessed | tf_op | source)
XLA Modules:
  0.0 43.7 jit_solution(3857452394075254713)
XLA Ops:
  0.6 1.5 %shard_map.85 = (bf16[160,256]{1,0:T(8,128)(2,1)S(1)}, f32[160,1]{1,0:T(8,128)S(1)}, bf16[256,1024]{1,0:T(8,128)(2,1)S(1)}, bf16[40,1024]{1,0:T(8,128)(2,1)S(1)}...) custom-call(s32[8,256]{1,0:T(8,128)} %bitcast.2, ...), custom_call_target="tpu_custom_call" | custom-call | flops 83886080 | bytes 1048576 | tf_op jit(solution)/shard_map/pallas_call | solution.py:69
  2.1 4.1 %collective-permute-start.3 = (bf16[40,1024]{1,0:T(8,128)(2,1)S(1)}, bf16[40,1024]{1,0:T(8,128)(2,1)S(1)}, u32[]{:S(2)}, u32[]{:S(2)}) collective-permute-start(bf16[40,1024]{1,0:T(8,128)(2,1)S(1)} %get-tuple-element.46), channel_id=1, source_target_pairs={{0,8},{4,12},{8,0},{12,4},{1,9},{5,13},{9,1},{13,5},{2,10},{6,14},... | collective-permute-start | bytes 245768 | tf_op jit(solution)/shard_map/ppermute | solution.py:299
  6.2 1.3 %collective-permute-start.4 = (bf16[40,1024]{1,0:T(8,128)(2,1)S(1)}, bf16[40,1024]{1,0:T(8,128)(2,1)S(1)}, u32[]{:S(2)}, u32[]{:S(2)}) collective-permute-start(bf16[40,1024]{1,0:T(8,128)(2,1)S(1)} %get-tuple-element.47), channel_id=1, source_target_pairs={{0,12},{4,8},{8,4},{12,0},{1,13},{5,9},{9,5},{13,1},{2,14},{6,10},... | collective-permute-start | bytes 245768 | tf_op jit(solution)/shard_map/ppermute | solution.py:299
  8.1 3.8 %shard_map.87 = (bf16[3,768,1024]{2,1,0:T(8,128)(2,1)S(1)}, bf16[3,768,1024]{2,1,0:T(8,128)(2,1)S(1)}, bf16[40,1024]{1,0:T(8,128)(2,1)S(1)}, bf16[40,1024]{1,0:T(8,128)(2,1)S(1)}, bf16[40,1024]{1,0:T(8,128)(2,1)S(1)}) custom-call(bf16[1,2,1536,1024]{3,2,1,0:T(8,128)(2,1)} %gate_up.1, bf16[1,1536,1024]{2,1,0:T(8,128)(2,1)} %down.1, ...), custom_call_target="tpu_custom_call" | custom-call | flops 25165824000 | bytes 314572800 | tf_op jit(solution)/shard_map/pallas_call | solution.py:69
  11.9 3.0 %collective-permute-start = (bf16[40,1024]{1,0:T(8,128)(2,1)S(1)}, bf16[40,1024]{1,0:T(8,128)(2,1)S(1)}, u32[]{:S(2)}, u32[]{:S(2)}) collective-permute-start(bf16[40,1024]{1,0:T(8,128)(2,1)S(1)} %get-tuple-element.42), channel_id=1, source_target_pairs={{0,12},{4,8},{8,4},{12,0},{1,13},{5,9},{9,5},{13,1},{2,14},{6,10},... | collective-permute-start | bytes 245768 | tf_op jit(solution)/shard_map/ppermute | solution.py:299
  15.5 1.4 %shard_map.88 = (bf16[2,80,768]{2,1,0:T(8,128)(2,1)S(1)}, bf16[160,80]{1,0:T(8,128)(2,1)S(1)}, bf16[80,1024]{1,0:T(8,128)(2,1)S(1)}) custom-call(bf16[40,1024]{1,0:T(8,128)(2,1)S(1)} %collective-permute-done.3.refs_0_, bf16[40,1024]{1,0:T(8,128)(2,1)S(1)} %collective-permute-done.4.refs_1_, bf16[80,1024]{1,0:T(8,128)(2,1)S(1)} %collective-permute-done.2.refs_2_, ...), custom_call_target="tpu_custom_call" | custom-call | flops 503316480 | bytes 3145728 | tf_op jit(solution)/shard_map/pallas_call | solution.py:69
  17.0 1.1 %shard_map.90.mine = bf16[2,80,768]{2,1,0:T(8,128)(2,1)S(1)} custom-call(bf16[80,1024]{1,0:T(8,128)(2,1)S(1)} %get-tuple-element.53.rows_in, bf16[3,768,1024]{2,1,0:T(8,128)(2,1)S(1)} %get-tuple-element.51.refs_5_.held), custom_call_target="tpu_custom_call" | custom-call | flops 25165824000 | bytes 314572800 | tf_op jit(solution)/shard_map/pallas_call | solution.py:69
  18.6 1.7 %collective-permute-start.8 = (bf16[2,80,768]{2,1,0:T(8,128)(2,1)S(1)}, bf16[2,80,768]{2,1,0:T(8,128)(2,1)S(1)}, u32[]{:S(2)}, u32[]{:S(2)}) collective-permute-start(bf16[2,80,768]{2,1,0:T(8,128)(2,1)S(1)} %get-tuple-element.55.refs_6_), channel_id=1, source_target_pairs={{0,2},{1,3},{2,0},{3,1},{4,6},{5,7},{6,4},{7,5},{8,10},{9,11},{10,... | collective-permute-start | bytes 737288 | tf_op jit(solution)/shard_map/ppermute | solution.py:299
  20.3 1.7 %collective-permute-done.1.refs_1_ = bf16[40,1024]{1,0:T(8,128)(2,1)S(1)} collective-permute-done((bf16[40,1024]{1,0:T(8,128)(2,1)S(1)}, bf16[40,1024]{1,0:T(8,128)(2,1)S(1)}, u32[]{:S(2)}, u32[]{:S(2)}) %collective-permute-start.1) | collective-permute-done | bytes 81952 | tf_op jit(solution)/shard_map/ppermute | solution.py:299
  22.1 0.7 %shard_map.92 = bf16[80,768]{1,0:T(8,128)(2,1)S(1)} custom-call(bf16[40,1024]{1,0:T(8,128)(2,1)S(1)} %collective-permute-done.refs_0_, bf16[40,1024]{1,0:T(8,128)(2,1)S(1)} %collective-permute-done.1.refs_1_, bf16[80,1024]{1,0:T(8,128)(2,1)S(1)} %collective-permute-done.2.refs_2_, bf16[40,1024]{1,0:T(8,128)(2,1)S(1)} %get-tuple-element.45.refs_3_, ...), custom_call_target="tpu_custom_call" | custom-call | flops 251658240 | bytes 3145728 | tf_op jit(solution)/shard_map/pallas_call | solution.py:69
  22.8 0.7 %shard_map.89 = (bf16[80,1024]{1,0:T(8,128)(2,1)S(1)}, bf16[80,768]{1,0:T(8,128)(2,1)S(1)}) custom-call(bf16[40,1024]{1,0:T(8,128)(2,1)S(1)} %collective-permute-done.refs_0_, bf16[40,1024]{1,0:T(8,128)(2,1)S(1)} %collective-permute-done.1.refs_1_, bf16[80,1024]{1,0:T(8,128)(2,1)S(1)} %collective-permute-done.2.refs_2_, ...), custom_call_target="tpu_custom_call" | custom-call | flops 25165824000 | bytes 314572800 | tf_op jit(solution)/shard_map/pallas_call | solution.py:69
  23.5 0.6 %collective-permute-done.6 = bf16[80,768]{1,0:T(8,128)(2,1)S(1)} collective-permute-done((bf16[80,768]{1,0:T(8,128)(2,1)S(1)}, bf16[80,768]{1,0:T(8,128)(2,1)S(1)}, u32[]{:S(2)}, u32[]{:S(2)}) %collective-permute-start.6) | collective-permute-done | bytes 122912 | tf_op jit(solution)/shard_map/ppermute | solution.py:299
  24.2 1.6 %collective-permute-start.7 = (bf16[80,768]{1,0:T(8,128)(2,1)S(1)}, bf16[80,768]{1,0:T(8,128)(2,1)S(1)}, u32[]{:S(2)}, u32[]{:S(2)}) collective-permute-start(bf16[80,768]{1,0:T(8,128)(2,1)S(1)} %get-tuple-element.67), channel_id=1, source_target_pairs={{0,2},{1,3},{2,0},{3,1},{4,6},{5,7},{6,4},{7,5},{8,10},{9,11},{10,... | collective-permute-start | bytes 368648 | tf_op jit(solution)/shard_map/ppermute | solution.py:299
  25.7 0.9 %collective-permute-done.8.pair_far = bf16[2,80,768]{2,1,0:T(8,128)(2,1)S(1)} collective-permute-done((bf16[2,80,768]{2,1,0:T(8,128)(2,1)S(1)}, bf16[2,80,768]{2,1,0:T(8,128)(2,1)S(1)}, u32[]{:S(2)}, u32[]{:S(2)}) %collective-permute-start.8) | collective-permute-done | bytes 245792 | tf_op jit(solution)/shard_map/ppermute | solution.py:299
  26.9 2.8 %collective-permute-done.7.act_far = bf16[80,768]{1,0:T(8,128)(2,1)S(1)} collective-permute-done((bf16[80,768]{1,0:T(8,128)(2,1)S(1)}, bf16[80,768]{1,0:T(8,128)(2,1)S(1)}, u32[]{:S(2)}, u32[]{:S(2)}) %collective-permute-start.7) | collective-permute-done | bytes 122912 | tf_op jit(solution)/shard_map/ppermute | solution.py:299
  29.8 0.7 %shard_map.95.total = f32[80,1024]{1,0:T(8,128)S(1)} custom-call(bf16[2,80,768]{2,1,0:T(8,128)(2,1)S(1)} %shard_map.94.mine, bf16[3,768,1024]{2,1,0:T(8,128)(2,1)S(1)} %get-tuple-element.51.refs_5_.held), custom_call_target="tpu_custom_call" | custom-call | flops 251658240 | bytes 3145728 | tf_op jit(solution)/shard_map/pallas_call | solution.py:69
  30.4 0.8 %collective-permute-done.10.other = bf16[2,80,768]{2,1,0:T(8,128)(2,1)S(1)} collective-permute-done((bf16[2,80,768]{2,1,0:T(8,128)(2,1)S(1)}, bf16[2,80,768]{2,1,0:T(8,128)(2,1)S(1)}, u32[]{:S(2)}, u32[]{:S(2)}) %collective-permute-start.10) | collective-permute-done | bytes 245792 | tf_op jit(solution)/shard_map/ppermute | solution.py:299
  31.3 0.9 %shard_map.96 = (bf16[40,1024]{1,0:T(8,128)(2,1)S(1)}, bf16[40,1024]{1,0:T(8,128)(2,1)S(1)}, bf16[40,1024]{1,0:T(8,128)(2,1)S(1)}, bf16[40,1024]{1,0:T(8,128)(2,1)S(1)}) custom-call(f32[80,1024]{1,0:T(8,128)S(1)} %shard_map.95.total, bf16[2,80,768]{2,1,0:T(8,128)(2,1)S(1)} %collective-permute-done.10.other, ...), custom_call_target="tpu_custom_call" | custom-call | flops 251658240 | bytes 3145728 | tf_op jit(solution)/shard_map/pallas_call | solution.py:69
  32.2 0.6 %collective-permute-start.11 = (bf16[40,1024]{1,0:T(8,128)(2,1)S(1)}, bf16[40,1024]{1,0:T(8,128)(2,1)S(1)}, u32[]{:S(2)}, u32[]{:S(2)}) collective-permute-start(bf16[40,1024]{1,0:T(8,128)(2,1)S(1)} %get-tuple-element.60), channel_id=1, source_target_pairs={{0,4},{4,8},{8,12},{12,0},{1,5},{5,9},{9,13},{13,1},{2,6},{6,10},{... | collective-permute-start | bytes 245768 | tf_op jit(solution)/shard_map/ppermute | solution.py:294
  32.8 3.7 %collective-permute-start.12 = (bf16[40,1024]{1,0:T(8,128)(2,1)S(1)}, bf16[40,1024]{1,0:T(8,128)(2,1)S(1)}, u32[]{:S(2)}, u32[]{:S(2)}) collective-permute-start(bf16[40,1024]{1,0:T(8,128)(2,1)S(1)} %get-tuple-element.61), channel_id=1, source_target_pairs={{0,8},{4,12},{8,0},{12,4},{1,9},{5,13},{9,1},{13,5},{2,10},{6,14},... | collective-permute-start | bytes 245768 | tf_op jit(solution)/shard_map/ppermute | solution.py:294
  36.5 0.6 %collective-permute-start.13 = (bf16[40,1024]{1,0:T(8,128)(2,1)S(1)}, bf16[40,1024]{1,0:T(8,128)(2,1)S(1)}, u32[]{:S(2)}, u32[]{:S(2)}) collective-permute-start(bf16[40,1024]{1,0:T(8,128)(2,1)S(1)} %get-tuple-element.62), channel_id=1, source_target_pairs={{0,12},{4,0},{8,4},{12,8},{1,13},{5,1},{9,5},{13,9},{2,14},{6,2},{... | collective-permute-start | bytes 245768 | tf_op jit(solution)/shard_map/ppermute | solution.py:294
  37.2 4.1 %shard_map.98 = (bf16[1,2,1536,1024]{3,2,1,0:T(8,128)(2,1)}, bf16[1,1536,1024]{2,1,0:T(8,128)(2,1)}) custom-call(bf16[80,768]{1,0:T(8,128)(2,1)S(1)} %get-tuple-element.59.mine_act, bf16[80,768]{1,0:T(8,128)(2,1)S(1)} %collective-permute-done.9._.other_act, bf16[2,80,768]{2,1,0:T(8,128)(2,1)S(1)} %shard_map.94.mine, ...), custom_call_target="tpu_custom_call" | custom-call | flops 754974720 | bytes 9437184 | tf_op jit(solution)/shard_map/pallas_call | solution.py:69
  41.3 1.0 %collective-permute-done.12.refs_1_ = bf16[40,1024]{1,0:T(8,128)(2,1)S(1)} collective-permute-done((bf16[40,1024]{1,0:T(8,128)(2,1)S(1)}, bf16[40,1024]{1,0:T(8,128)(2,1)S(1)}, u32[]{:S(2)}, u32[]{:S(2)}) %collective-permute-start.12) | collective-permute-done | bytes 81952 | tf_op jit(solution)/shard_map/ppermute | solution.py:294
  42.6 1.1 %shard_map.97 = bf16[256,1024]{1,0:T(8,128)(2,1)} custom-call(bf16[160,256]{1,0:T(8,128)(2,1)S(1)} %get-tuple-element.35.pick, bf16[40,1024]{1,0:T(8,128)(2,1)S(1)} %collective-permute-done.11.refs_0_, bf16[40,1024]{1,0:T(8,128)(2,1)S(1)} %collective-permute-done.12.refs_1_, bf16[40,1024]{1,0:T(8,128)(2,1)S(1)} %collective-permute-done.13.refs_2_, ...), custom_call_target="tpu_custom_call" | custom-call | flops 83886080 | bytes 1048576 | tf_op jit(solution)/shard_map/pallas_call | solution.py:69
  (19 shorter events, 2.4 us)
Async XLA Ops:
  2.1 13.1 %collective-permute-start.3 = (bf16[40,1024]{1,0:T(8,128)(2,1)S(1)}, bf16[40,1024]{1,0:T(8,128)(2,1)S(1)}, u32[]{:S(2)}, u32[]{:S(2)}) collective-permute-start(bf16[40,1024]{1,0:T(8,128)(2,1)S(1)} %get-tuple-element.46), channel_id=1, source_target_pairs={{0,8},{4,12},{8,0},{12,4},{1,9},{5,13},{9,1},{13,5},{2,10},{6,14},... | collective-permute-start | bytes 245768 | tf_op jit(solution)/shard_map/ppermute | solution.py:299
  6.2 9.0 %collective-permute-start.4 = (bf16[40,1024]{1,0:T(8,128)(2,1)S(1)}, bf16[40,1024]{1,0:T(8,128)(2,1)S(1)}, u32[]{:S(2)}, u32[]{:S(2)}) collective-permute-start(bf16[40,1024]{1,0:T(8,128)(2,1)S(1)} %get-tuple-element.47), channel_id=1, source_target_pairs={{0,12},{4,8},{8,4},{12,0},{1,13},{5,9},{9,5},{13,1},{2,14},{6,10},... | collective-permute-start | bytes 245768 | tf_op jit(solution)/shard_map/ppermute | solution.py:299
  7.8 7.7 %collective-permute-start.2 = (bf16[80,1024]{1,0:T(8,128)(2,1)S(1)}, bf16[80,1024]{1,0:T(8,128)(2,1)S(1)}, u32[]{:S(2)}, u32[]{:S(2)}) collective-permute-start(bf16[80,1024]{1,0:T(8,128)(2,1)S(1)} %get-tuple-element.44), channel_id=1, source_target_pairs={{0,4},{4,0},{8,12},{12,8},{1,5},{5,1},{9,13},{13,9},{2,6},{6,2},{1... | collective-permute-start | bytes 491528 | tf_op jit(solution)/shard_map/ppermute | solution.py:299
  11.9 8.4 %collective-permute-start = (bf16[40,1024]{1,0:T(8,128)(2,1)S(1)}, bf16[40,1024]{1,0:T(8,128)(2,1)S(1)}, u32[]{:S(2)}, u32[]{:S(2)}) collective-permute-start(bf16[40,1024]{1,0:T(8,128)(2,1)S(1)} %get-tuple-element.42), channel_id=1, source_target_pairs={{0,12},{4,8},{8,4},{12,0},{1,13},{5,9},{9,5},{13,1},{2,14},{6,10},... | collective-permute-start | bytes 245768 | tf_op jit(solution)/shard_map/ppermute | solution.py:299
  14.9 7.1 %collective-permute-start.1 = (bf16[40,1024]{1,0:T(8,128)(2,1)S(1)}, bf16[40,1024]{1,0:T(8,128)(2,1)S(1)}, u32[]{:S(2)}, u32[]{:S(2)}) collective-permute-start(bf16[40,1024]{1,0:T(8,128)(2,1)S(1)} %get-tuple-element.43), channel_id=1, source_target_pairs={{0,8},{4,12},{8,0},{12,4},{1,9},{5,13},{9,1},{13,5},{2,10},{6,14},... | collective-permute-start | bytes 245768 | tf_op jit(solution)/shard_map/ppermute | solution.py:299
  16.9 1.6 %collective-permute-start.5 = (bf16[2,80,768]{2,1,0:T(8,128)(2,1)S(1)}, bf16[2,80,768]{2,1,0:T(8,128)(2,1)S(1)}, u32[]{:S(2)}, u32[]{:S(2)}) collective-permute-start(bf16[2,80,768]{2,1,0:T(8,128)(2,1)S(1)} %get-tuple-element.54), channel_id=1, source_target_pairs={{0,1},{1,0},{2,3},{3,2},{4,5},{5,4},{6,7},{7,6},{8,9},{9,8},{10,11... | collective-permute-start | bytes 737288 | tf_op jit(solution)/shard_map/ppermute | solution.py:299
  18.6 8.1 %collective-permute-start.8 = (bf16[2,80,768]{2,1,0:T(8,128)(2,1)S(1)}, bf16[2,80,768]{2,1,0:T(8,128)(2,1)S(1)}, u32[]{:S(2)}, u32[]{:S(2)}) collective-permute-start(bf16[2,80,768]{2,1,0:T(8,128)(2,1)S(1)} %get-tuple-element.55.refs_6_), channel_id=1, source_target_pairs={{0,2},{1,3},{2,0},{3,1},{4,6},{5,7},{6,4},{7,5},{8,10},{9,11},{10,... | collective-permute-start | bytes 737288 | tf_op jit(solution)/shard_map/ppermute | solution.py:299
  22.8 1.4 %collective-permute-start.6 = (bf16[80,768]{1,0:T(8,128)(2,1)S(1)}, bf16[80,768]{1,0:T(8,128)(2,1)S(1)}, u32[]{:S(2)}, u32[]{:S(2)}) collective-permute-start(bf16[80,768]{1,0:T(8,128)(2,1)S(1)} %shard_map.92), channel_id=1, source_target_pairs={{0,1},{1,0},{2,3},{3,2},{4,5},{5,4},{6,7},{7,6},{8,9},{9,8},{10,11... | collective-permute-start | bytes 368648 | tf_op jit(solution)/shard_map/ppermute | solution.py:299
  24.2 5.4 %collective-permute-start.7 = (bf16[80,768]{1,0:T(8,128)(2,1)S(1)}, bf16[80,768]{1,0:T(8,128)(2,1)S(1)}, u32[]{:S(2)}, u32[]{:S(2)}) collective-permute-start(bf16[80,768]{1,0:T(8,128)(2,1)S(1)} %get-tuple-element.67), channel_id=1, source_target_pairs={{0,2},{1,3},{2,0},{3,1},{4,6},{5,7},{6,4},{7,5},{8,10},{9,11},{10,... | collective-permute-start | bytes 368648 | tf_op jit(solution)/shard_map/ppermute | solution.py:299
  26.8 2.8 %collective-permute-start.9 = (bf16[80,768]{1,0:T(8,128)(2,1)S(1)}, bf16[80,768]{1,0:T(8,128)(2,1)S(1)}, u32[]{:S(2)}, u32[]{:S(2)}) collective-permute-start(bf16[80,768]{1,0:T(8,128)(2,1)S(1)} %get-tuple-element.59.mine_act), channel_id=1, source_target_pairs={{0,1},{1,0},{2,3},{3,2},{4,5},{5,4},{6,7},{7,6},{8,9},{9,8},{10,11... | collective-permute-start | bytes 368648 | tf_op jit(solution)/shard_map/ppermute | solution.py:299
  29.7 1.6 %collective-permute-start.10 = (bf16[2,80,768]{2,1,0:T(8,128)(2,1)S(1)}, bf16[2,80,768]{2,1,0:T(8,128)(2,1)S(1)}, u32[]{:S(2)}, u32[]{:S(2)}) collective-permute-start(bf16[2,80,768]{2,1,0:T(8,128)(2,1)S(1)} %shard_map.94.mine), channel_id=1, source_target_pairs={{0,1},{1,0},{2,3},{3,2},{4,5},{5,4},{6,7},{7,6},{8,9},{9,8},{10,11... | collective-permute-start | bytes 737288 | tf_op jit(solution)/shard_map/ppermute | solution.py:299
  32.2 9.1 %collective-permute-start.11 = (bf16[40,1024]{1,0:T(8,128)(2,1)S(1)}, bf16[40,1024]{1,0:T(8,128)(2,1)S(1)}, u32[]{:S(2)}, u32[]{:S(2)}) collective-permute-start(bf16[40,1024]{1,0:T(8,128)(2,1)S(1)} %get-tuple-element.60), channel_id=1, source_target_pairs={{0,4},{4,8},{8,12},{12,0},{1,5},{5,9},{9,13},{13,1},{2,6},{6,10},{... | collective-permute-start | bytes 245768 | tf_op jit(solution)/shard_map/ppermute | solution.py:294
  32.8 9.5 %collective-permute-start.12 = (bf16[40,1024]{1,0:T(8,128)(2,1)S(1)}, bf16[40,1024]{1,0:T(8,128)(2,1)S(1)}, u32[]{:S(2)}, u32[]{:S(2)}) collective-permute-start(bf16[40,1024]{1,0:T(8,128)(2,1)S(1)} %get-tuple-element.61), channel_id=1, source_target_pairs={{0,8},{4,12},{8,0},{12,4},{1,9},{5,13},{9,1},{13,5},{2,10},{6,14},... | collective-permute-start | bytes 245768 | tf_op jit(solution)/shard_map/ppermute | solution.py:294
  36.5 6.1 %collective-permute-start.13 = (bf16[40,1024]{1,0:T(8,128)(2,1)S(1)}, bf16[40,1024]{1,0:T(8,128)(2,1)S(1)}, u32[]{:S(2)}, u32[]{:S(2)}) collective-permute-start(bf16[40,1024]{1,0:T(8,128)(2,1)S(1)} %get-tuple-element.62), channel_id=1, source_target_pairs={{0,12},{4,0},{8,4},{12,8},{1,13},{5,1},{9,5},{13,9},{2,14},{6,2},{... | collective-permute-start | bytes 245768 | tf_op jit(solution)/shard_map/ppermute | solution.py:294

commit v13 on v11

--- a/solution.py
+++ b/solution.py
@@ -36,10 +36,6 @@
 
 def far_first(count):
     return sorted(range(count), key=lambda k: (-k.bit_length(), k))
-
-
-def farthest_first(count):
-    return list(reversed(range(count)))
 
 
 def cut(source, target, sems, first, pieces):
@@ -181,7 +177,8 @@
         out[matrix] = mm(rows_in, held[matrix], LANES).astype(BF)
 
 
-def mine_pair(rows_in, held, out):
+def mine_pair(rows_in, held, near, out, near_out):
+    near_out[...] = near[...]
     for matrix in range(2):
         out[matrix] = mm(rows_in[...], held[matrix], LANES).astype(BF)
 
@@ -194,8 +191,7 @@
 
 def act_part(experts, own, *refs):
     place, held = refs[experts : experts + 2]
-    order = far_first(experts)
-    pieces = [refs[:experts][farthest_first(experts).index(k)] for k in order]
+    pieces = refs[: experts - 2][::-1] + refs[experts - 2 : experts]
     rows_grad = mm(place[...], stacked(pieces).astype(BF), ROWS).astype(BF)
     if own:
         refs[-2][...] = rows_grad
@@ -319,7 +315,7 @@
     dma = lambda count: pltpu.SemaphoreType.DMA((count,))
 
     order = far_first(experts)
-    pick, prob, grads, *send_in = call(
+    pick, prob, grads, *send_in, own_in = call(
         functools.partial(pick_inputs, experts),
         [
             sds((rows, tokens), BF),
@@ -338,7 +334,7 @@
         flops=2 * rows * tokens * width,
         traffic=4 * tokens * width,
     )
-    send_grad = call(
+    *send_grad, near_grad, own_grad = call(
         functools.partial(pick_grads, experts),
         piece,
         (pick, prob, grads),
@@ -346,20 +342,17 @@
         flops=2 * rows * tokens * width,
         traffic=2 * tokens * width,
     )
-    got_in = exchange(send_in, "ex")
+    got_in = exchange(send_in + [own_in], "ex")
     held_other, held_mine, *send_grad = call(
-        functools.partial(stage, experts),
-        [pltpu.VMEM((3, half, width), BF)] * 2 + piece,
+        functools.partial(stage, experts - 2),
+        [pltpu.VMEM((3, half, width), BF)] * 2 + piece[2:],
         (far(gate_up), far(down_proj), *send_grad),
-        [HBM] * 2 + [VMEM] * experts,
+        [HBM] * 2 + [VMEM] * (experts - 2),
         [dma(6)],
         flops=WCOST * weight_flops,
         traffic=WCOST * weight_bytes,
     )
-    got_grad = [
-        swap(send_grad[order.index(k)], "ex", k) if k else send_grad[-1]
-        for k in farthest_first(experts)
-    ]
+    got_grad = [swap(part, "ex", k) for part, k in zip(send_grad, order)][::-1]
     pair_other, place, rows_in = call(
         functools.partial(other_pair, experts, capacity),
         [sds((2, capacity, half), BF), sds((rows, capacity), BF), sds((capacity, width), BF)],
@@ -368,11 +361,11 @@
         flops=2 * weight_flops,
         traffic=weight_bytes,
     )
-    pair_mine = call(
+    pair_mine, near_grad = call(
         mine_pair,
-        sds((2, capacity, half), BF),
-        (rows_in, held_mine),
-        [VMEM] * 2,
+        [sds((2, capacity, half), BF), piece[0]],
+        (rows_in, held_mine, near_grad),
+        [VMEM] * 3,
         flops=C2COST * weight_flops,
         traffic=C2COST * weight_bytes,
     )
@@ -393,6 +386,8 @@
         traffic=10 * capacity * hidden,
     )
     pair, pair_far = total(pair, pair_sent)
+    got_grad = got_grad + [swap(near_grad, "ex", 1), own_grad]
+
     def act_of(own, held, outs, tied, cost):
         return call(
             functools.partial(act_part, experts, own),

time: 43.9 us -> 45 us (1.025)
  waiting for transfers between devices: 8.07 us -> 9.38 us
    ppermute x12, waiting for transfers between devices: 7.12 us -> 8.18 us  [swap(): return lax.ppermute(value, axis, [(i, i ^ bit) for i in range(count)])]
  transfers between devices with their start and end apart: 15 -> 15, of which waited for: 7 -> 6; matrix products, arithmetic and copies ran while one was open for 0% -> 0% of each run, Pallas kernels for 30% -> 29%
where the time goes in v13:
time: 45 us; the launch traced here: 44.8 us
  starting transfers between devices  18.2 us (40%)
  Pallas kernels  16.5 us (37%)
  waiting for transfers between devices  9.38 us (21%)
  between operations  0.75 us (2%)
    pallas_call x14, Pallas kernels, call(): pl.pallas_call(body, out_shape=outs, in_specs=specs, out_specs=out_specs...  16.5 us
    ppermute x12, starting transfers between devices, swap(): return lax.ppermute(value, axis, [(i, i ^ bit) for i in range(count)])  13.7 us
    ppermute x12, waiting for transfers between devices, swap(): return lax.ppermute(value, axis, [(i, i ^ bit) for i in range(count)])  8.18 us
    ppermute x3, starting transfers between devices, shift(): lax.ppermute(value, axis, [(i, (i + step) % count) for i in range(count)])  4.53 us
    ppermute x3, waiting for transfers between devices, shift(): lax.ppermute(value, axis, [(i, (i + step) % count) for i in range(count)])  1.2 us
  transfers between devices with their start and end apart: 15, of which 6 were waited for; matrix products, arithmetic and copies ran while one was open for 0% of the time, Pallas kernels for 29%

profile of v13, /device:TPU:0, one launch (start us, length us, event | category | flops | bytes accessed | tf_op | source)
XLA Modules:
  0.0 44.8 jit_solution(6897735927902749946)
XLA Ops:
  0.6 1.5 %shard_map.85 = (bf16[160,256]{1,0:T(8,128)(2,1)S(1)}, f32[160,1]{1,0:T(8,128)S(1)}, bf16[256,1024]{1,0:T(8,128)(2,1)S(1)}, bf16[40,1024]{1,0:T(8,128)(2,1)S(1)}...) custom-call(s32[8,256]{1,0:T(8,128)} %bitcast.2, ...), custom_call_target="tpu_custom_call" | custom-call | flops 83886080 | bytes 1048576 | tf_op jit(solution)/shard_map/pallas_call | solution.py:69
  2.1 4.1 %collective-permute-start.2 = (bf16[40,1024]{1,0:T(8,128)(2,1)S(1)}, bf16[40,1024]{1,0:T(8,128)(2,1)S(1)}, u32[]{:S(2)}, u32[]{:S(2)}) collective-permute-start(bf16[40,1024]{1,0:T(8,128)(2,1)S(1)} %get-tuple-element.43), channel_id=1, source_target_pairs={{0,8},{4,12},{8,0},{12,4},{1,9},{5,13},{9,1},{13,5},{2,10},{6,14},... | collective-permute-start | bytes 245768 | tf_op jit(solution)/shard_map/ppermute | solution.py:295
  6.2 1.3 %collective-permute-start.3 = (bf16[40,1024]{1,0:T(8,128)(2,1)S(1)}, bf16[40,1024]{1,0:T(8,128)(2,1)S(1)}, u32[]{:S(2)}, u32[]{:S(2)}) collective-permute-start(bf16[40,1024]{1,0:T(8,128)(2,1)S(1)} %get-tuple-element.44), channel_id=1, source_target_pairs={{0,12},{4,8},{8,4},{12,0},{1,13},{5,9},{9,5},{13,1},{2,14},{6,10},... | collective-permute-start | bytes 245768 | tf_op jit(solution)/shard_map/ppermute | solution.py:295
  8.1 3.8 %shard_map.87 = (bf16[3,768,1024]{2,1,0:T(8,128)(2,1)S(1)}, bf16[3,768,1024]{2,1,0:T(8,128)(2,1)S(1)}, bf16[40,1024]{1,0:T(8,128)(2,1)S(1)}, bf16[40,1024]{1,0:T(8,128)(2,1)S(1)}) custom-call(bf16[1,2,1536,1024]{3,2,1,0:T(8,128)(2,1)} %gate_up.1, bf16[1,1536,1024]{2,1,0:T(8,128)(2,1)} %down.1, bf16[40,1024]{1,0:T(8,128)(2,1)S(1)} %get-tuple-element.39.refs_0_, ...), custom_call_target="tpu_custom_call" | custom-call | flops 25165824000 | bytes 314572800 | tf_op jit(solution)/shard_map/pallas_call | solution.py:69
  11.9 3.0 %collective-permute-start = (bf16[40,1024]{1,0:T(8,128)(2,1)S(1)}, bf16[40,1024]{1,0:T(8,128)(2,1)S(1)}, u32[]{:S(2)}, u32[]{:S(2)}) collective-permute-start(bf16[40,1024]{1,0:T(8,128)(2,1)S(1)} %get-tuple-element.41), channel_id=1, source_target_pairs={{0,12},{4,8},{8,4},{12,0},{1,13},{5,9},{9,5},{13,1},{2,14},{6,10},... | collective-permute-start | bytes 245768 | tf_op jit(solution)/shard_map/ppermute | solution.py:295
  15.2 1.4 %shard_map.88 = (bf16[2,80,768]{2,1,0:T(8,128)(2,1)S(1)}, bf16[160,80]{1,0:T(8,128)(2,1)S(1)}, bf16[80,1024]{1,0:T(8,128)(2,1)S(1)}) custom-call(bf16[40,1024]{1,0:T(8,128)(2,1)S(1)} %collective-permute-done.2.refs_0_, bf16[40,1024]{1,0:T(8,128)(2,1)S(1)} %collective-permute-done.3.refs_1_, bf16[40,1024]{1,0:T(8,128)(2,1)S(1)} %collective-permute-done.4.refs_2_, ...), custom_call_target="tpu_custom_call" | custom-call | flops 503316480 | bytes 3145728 | tf_op jit(solution)/shard_map/pallas_call | solution.py:69
  16.7 1.1 %shard_map.89 = (bf16[2,80,768]{2,1,0:T(8,128)(2,1)S(1)}, bf16[40,1024]{1,0:T(8,128)(2,1)S(1)}) custom-call(bf16[80,1024]{1,0:T(8,128)(2,1)S(1)} %get-tuple-element.48.rows_in, bf16[3,768,1024]{2,1,0:T(8,128)(2,1)S(1)} %get-tuple-element.49.held.refs_5_, bf16[40,1024]{1,0:T(8,128)(2,1)S(1)} %get-tuple-element.50.near), custom_call_target="tpu_custom_call" | custom-call | flops 25165824000 | bytes 314572800 | tf_op jit(solution)/shard_map/pallas_call | solution.py:69
  17.8 1.2 %collective-permute-start.5 = (bf16[40,1024]{1,0:T(8,128)(2,1)S(1)}, bf16[40,1024]{1,0:T(8,128)(2,1)S(1)}, u32[]{:S(2)}, u32[]{:S(2)}) collective-permute-start(bf16[40,1024]{1,0:T(8,128)(2,1)S(1)} %get-tuple-element.51), channel_id=1, source_target_pairs={{0,4},{4,0},{8,12},{12,8},{1,5},{5,1},{9,13},{13,9},{2,6},{6,2},{1... | collective-permute-start | bytes 245768 | tf_op jit(solution)/shard_map/ppermute | solution.py:295
  19.1 1.5 %collective-permute-start.9 = (bf16[2,80,768]{2,1,0:T(8,128)(2,1)S(1)}, bf16[2,80,768]{2,1,0:T(8,128)(2,1)S(1)}, u32[]{:S(2)}, u32[]{:S(2)}) collective-permute-start(bf16[2,80,768]{2,1,0:T(8,128)(2,1)S(1)} %get-tuple-element.57.refs_6_), channel_id=1, source_target_pairs={{0,2},{1,3},{2,0},{3,1},{4,6},{5,7},{6,4},{7,5},{8,10},{9,11},{10,... | collective-permute-start | bytes 737288 | tf_op jit(solution)/shard_map/ppermute | solution.py:295
  20.6 1.5 %collective-permute-done.1.refs_1_ = bf16[40,1024]{1,0:T(8,128)(2,1)S(1)} collective-permute-done((bf16[40,1024]{1,0:T(8,128)(2,1)S(1)}, bf16[40,1024]{1,0:T(8,128)(2,1)S(1)}, u32[]{:S(2)}, u32[]{:S(2)}) %collective-permute-start.1) | collective-permute-done | bytes 81952 | tf_op jit(solution)/shard_map/ppermute | solution.py:295
  22.1 1.7 %collective-permute-done.5.refs_2_ = bf16[40,1024]{1,0:T(8,128)(2,1)S(1)} collective-permute-done((bf16[40,1024]{1,0:T(8,128)(2,1)S(1)}, bf16[40,1024]{1,0:T(8,128)(2,1)S(1)}, u32[]{:S(2)}, u32[]{:S(2)}) %collective-permute-start.5) | collective-permute-done | bytes 81952 | tf_op jit(solution)/shard_map/ppermute | solution.py:295
  23.7 0.7 %shard_map.92 = bf16[80,768]{1,0:T(8,128)(2,1)S(1)} custom-call(bf16[40,1024]{1,0:T(8,128)(2,1)S(1)} %collective-permute-done.refs_0_, bf16[40,1024]{1,0:T(8,128)(2,1)S(1)} %collective-permute-done.1.refs_1_, bf16[40,1024]{1,0:T(8,128)(2,1)S(1)} %collective-permute-done.5.refs_2_, bf16[40,1024]{1,0:T(8,128)(2,1)S(1)} %get-tuple-element.52.refs_3_, ...), custom_call_target="tpu_custom_call" | custom-call | flops 251658240 | bytes 3145728 | tf_op jit(solution)/shard_map/pallas_call | solution.py:69
  24.6 0.7 %shard_map.90 = (bf16[80,1024]{1,0:T(8,128)(2,1)S(1)}, bf16[80,768]{1,0:T(8,128)(2,1)S(1)}) custom-call(bf16[40,1024]{1,0:T(8,128)(2,1)S(1)} %collective-permute-done.refs_0_, bf16[40,1024]{1,0:T(8,128)(2,1)S(1)} %collective-permute-done.1.refs_1_, bf16[40,1024]{1,0:T(8,128)(2,1)S(1)} %collective-permute-done.5.refs_2_, ...), custom_call_target="tpu_custom_call" | custom-call | flops 25165824000 | bytes 314572800 | tf_op jit(solution)/shard_map/pallas_call | solution.py:69
  25.3 0.6 %collective-permute-done.7 = bf16[80,768]{1,0:T(8,128)(2,1)S(1)} collective-permute-done((bf16[80,768]{1,0:T(8,128)(2,1)S(1)}, bf16[80,768]{1,0:T(8,128)(2,1)S(1)}, u32[]{:S(2)}, u32[]{:S(2)}) %collective-permute-start.7) | collective-permute-done | bytes 122912 | tf_op jit(solution)/shard_map/ppermute | solution.py:295
  25.9 1.6 %collective-permute-start.8 = (bf16[80,768]{1,0:T(8,128)(2,1)S(1)}, bf16[80,768]{1,0:T(8,128)(2,1)S(1)}, u32[]{:S(2)}, u32[]{:S(2)}) collective-permute-start(bf16[80,768]{1,0:T(8,128)(2,1)S(1)} %get-tuple-element.69), channel_id=1, source_target_pairs={{0,2},{1,3},{2,0},{3,1},{4,6},{5,7},{6,4},{7,5},{8,10},{9,11},{10,... | collective-permute-start | bytes 368648 | tf_op jit(solution)/shard_map/ppermute | solution.py:295
  27.7 3.7 %collective-permute-done.8.act_far = bf16[80,768]{1,0:T(8,128)(2,1)S(1)} collective-permute-done((bf16[80,768]{1,0:T(8,128)(2,1)S(1)}, bf16[80,768]{1,0:T(8,128)(2,1)S(1)}, u32[]{:S(2)}, u32[]{:S(2)}) %collective-permute-start.8) | collective-permute-done | bytes 122912 | tf_op jit(solution)/shard_map/ppermute | solution.py:295
  31.5 0.7 %shard_map.95.total = f32[80,1024]{1,0:T(8,128)S(1)} custom-call(bf16[2,80,768]{2,1,0:T(8,128)(2,1)S(1)} %shard_map.94.mine, bf16[3,768,1024]{2,1,0:T(8,128)(2,1)S(1)} %get-tuple-element.49.held.refs_5_), custom_call_target="tpu_custom_call" | custom-call | flops 251658240 | bytes 3145728 | tf_op jit(solution)/shard_map/pallas_call | solution.py:69
  32.1 0.8 %collective-permute-done.11.other = bf16[2,80,768]{2,1,0:T(8,128)(2,1)S(1)} collective-permute-done((bf16[2,80,768]{2,1,0:T(8,128)(2,1)S(1)}, bf16[2,80,768]{2,1,0:T(8,128)(2,1)S(1)}, u32[]{:S(2)}, u32[]{:S(2)}) %collective-permute-start.11) | collective-permute-done | bytes 245792 | tf_op jit(solution)/shard_map/ppermute | solution.py:295
  33.0 0.9 %shard_map.96 = (bf16[40,1024]{1,0:T(8,128)(2,1)S(1)}, bf16[40,1024]{1,0:T(8,128)(2,1)S(1)}, bf16[40,1024]{1,0:T(8,128)(2,1)S(1)}, bf16[40,1024]{1,0:T(8,128)(2,1)S(1)}) custom-call(f32[80,1024]{1,0:T(8,128)S(1)} %shard_map.95.total, bf16[2,80,768]{2,1,0:T(8,128)(2,1)S(1)} %collective-permute-done.11.other, ...), custom_call_target="tpu_custom_call" | custom-call | flops 251658240 | bytes 3145728 | tf_op jit(solution)/shard_map/pallas_call | solution.py:69
  34.0 2.9 %collective-permute-start.13 = (bf16[40,1024]{1,0:T(8,128)(2,1)S(1)}, bf16[40,1024]{1,0:T(8,128)(2,1)S(1)}, u32[]{:S(2)}, u32[]{:S(2)}) collective-permute-start(bf16[40,1024]{1,0:T(8,128)(2,1)S(1)} %get-tuple-element.63), channel_id=1, source_target_pairs={{0,8},{4,12},{8,0},{12,4},{1,9},{5,13},{9,1},{13,5},{2,10},{6,14},... | collective-permute-start | bytes 245768 | tf_op jit(solution)/shard_map/ppermute | solution.py:290
  36.9 1.5 %collective-permute-start.14 = (bf16[40,1024]{1,0:T(8,128)(2,1)S(1)}, bf16[40,1024]{1,0:T(8,128)(2,1)S(1)}, u32[]{:S(2)}, u32[]{:S(2)}) collective-permute-start(bf16[40,1024]{1,0:T(8,128)(2,1)S(1)} %get-tuple-element.64), channel_id=1, source_target_pairs={{0,12},{4,0},{8,4},{12,8},{1,13},{5,1},{9,5},{13,9},{2,14},{6,2},{... | collective-permute-start | bytes 245768 | tf_op jit(solution)/shard_map/ppermute | solution.py:290
  38.4 4.1 %shard_map.98 = (bf16[1,2,1536,1024]{3,2,1,0:T(8,128)(2,1)}, bf16[1,1536,1024]{2,1,0:T(8,128)(2,1)}) custom-call(bf16[80,768]{1,0:T(8,128)(2,1)S(1)} %get-tuple-element.61.mine_act, bf16[80,768]{1,0:T(8,128)(2,1)S(1)} %collective-permute-done.10._.other_act, bf16[2,80,768]{2,1,0:T(8,128)(2,1)S(1)} %shard_map.94.mine, ...), custom_call_target="tpu_custom_call" | custom-call | flops 754974720 | bytes 9437184 | tf_op jit(solution)/shard_map/pallas_call | solution.py:69
  42.5 1.2 %collective-permute-done.13.refs_1_ = bf16[40,1024]{1,0:T(8,128)(2,1)S(1)} collective-permute-done((bf16[40,1024]{1,0:T(8,128)(2,1)S(1)}, bf16[40,1024]{1,0:T(8,128)(2,1)S(1)}, u32[]{:S(2)}, u32[]{:S(2)}) %collective-permute-start.13) | collective-permute-done | bytes 81952 | tf_op jit(solution)/shard_map/ppermute | solution.py:290
  43.7 1.1 %shard_map.97 = bf16[256,1024]{1,0:T(8,128)(2,1)} custom-call(bf16[160,256]{1,0:T(8,128)(2,1)S(1)} %get-tuple-element.36.pick, bf16[40,1024]{1,0:T(8,128)(2,1)S(1)} %collective-permute-done.12.refs_0_, bf16[40,1024]{1,0:T(8,128)(2,1)S(1)} %collective-permute-done.13.refs_1_, bf16[40,1024]{1,0:T(8,128)(2,1)S(1)} %collective-permute-done.14.refs_2_, ...), custom_call_target="tpu_custom_call" | custom-call | flops 83886080 | bytes 1048576 | tf_op jit(solution)/shard_map/pallas_call | solution.py:69
  (21 shorter events, 1.6 us)
Async XLA Ops:
  2.1 13.1 %collective-permute-start.2 = (bf16[40,1024]{1,0:T(8,128)(2,1)S(1)}, bf16[40,1024]{1,0:T(8,128)(2,1)S(1)}, u32[]{:S(2)}, u32[]{:S(2)}) collective-permute-start(bf16[40,1024]{1,0:T(8,128)(2,1)S(1)} %get-tuple-element.43), channel_id=1, source_target_pairs={{0,8},{4,12},{8,0},{12,4},{1,9},{5,13},{9,1},{13,5},{2,10},{6,14},... | collective-permute-start | bytes 245768 | tf_op jit(solution)/shard_map/ppermute | solution.py:295
  6.2 9.0 %collective-permute-start.3 = (bf16[40,1024]{1,0:T(8,128)(2,1)S(1)}, bf16[40,1024]{1,0:T(8,128)(2,1)S(1)}, u32[]{:S(2)}, u32[]{:S(2)}) collective-permute-start(bf16[40,1024]{1,0:T(8,128)(2,1)S(1)} %get-tuple-element.44), channel_id=1, source_target_pairs={{0,12},{4,8},{8,4},{12,0},{1,13},{5,9},{9,5},{13,1},{2,14},{6,10},... | collective-permute-start | bytes 245768 | tf_op jit(solution)/shard_map/ppermute | solution.py:295
  7.6 7.6 %collective-permute-start.4 = (bf16[40,1024]{1,0:T(8,128)(2,1)S(1)}, bf16[40,1024]{1,0:T(8,128)(2,1)S(1)}, u32[]{:S(2)}, u32[]{:S(2)}) collective-permute-start(bf16[40,1024]{1,0:T(8,128)(2,1)S(1)} %get-tuple-element.45), channel_id=1, source_target_pairs={{0,4},{4,0},{8,12},{12,8},{1,5},{5,1},{9,13},{13,9},{2,6},{6,2},{1... | collective-permute-start | bytes 245768 | tf_op jit(solution)/shard_map/ppermute | solution.py:295
  11.9 8.8 %collective-permute-start = (bf16[40,1024]{1,0:T(8,128)(2,1)S(1)}, bf16[40,1024]{1,0:T(8,128)(2,1)S(1)}, u32[]{:S(2)}, u32[]{:S(2)}) collective-permute-start(bf16[40,1024]{1,0:T(8,128)(2,1)S(1)} %get-tuple-element.41), channel_id=1, source_target_pairs={{0,12},{4,8},{8,4},{12,0},{1,13},{5,9},{9,5},{13,1},{2,14},{6,10},... | collective-permute-start | bytes 245768 | tf_op jit(solution)/shard_map/ppermute | solution.py:295
  14.9 7.2 %collective-permute-start.1 = (bf16[40,1024]{1,0:T(8,128)(2,1)S(1)}, bf16[40,1024]{1,0:T(8,128)(2,1)S(1)}, u32[]{:S(2)}, u32[]{:S(2)}) collective-permute-start(bf16[40,1024]{1,0:T(8,128)(2,1)S(1)} %get-tuple-element.42), channel_id=1, source_target_pairs={{0,8},{4,12},{8,0},{12,4},{1,9},{5,13},{9,1},{13,5},{2,10},{6,14},... | collective-permute-start | bytes 245768 | tf_op jit(solution)/shard_map/ppermute | solution.py:295
  16.6 2.4 %collective-permute-start.6 = (bf16[2,80,768]{2,1,0:T(8,128)(2,1)S(1)}, bf16[2,80,768]{2,1,0:T(8,128)(2,1)S(1)}, u32[]{:S(2)}, u32[]{:S(2)}) collective-permute-start(bf16[2,80,768]{2,1,0:T(8,128)(2,1)S(1)} %get-tuple-element.56), channel_id=1, source_target_pairs={{0,1},{1,0},{2,3},{3,2},{4,5},{5,4},{6,7},{7,6},{8,9},{9,8},{10,11... | collective-permute-start | bytes 737288 | tf_op jit(solution)/shard_map/ppermute | solution.py:295
  17.8 5.9 %collective-permute-start.5 = (bf16[40,1024]{1,0:T(8,128)(2,1)S(1)}, bf16[40,1024]{1,0:T(8,128)(2,1)S(1)}, u32[]{:S(2)}, u32[]{:S(2)}) collective-permute-start(bf16[40,1024]{1,0:T(8,128)(2,1)S(1)} %get-tuple-element.51), channel_id=1, source_target_pairs={{0,4},{4,0},{8,12},{12,8},{1,5},{5,1},{9,13},{13,9},{2,6},{6,2},{1... | collective-permute-start | bytes 245768 | tf_op jit(solution)/shard_map/ppermute | solution.py:295
  19.1 8.4 %collective-permute-start.9 = (bf16[2,80,768]{2,1,0:T(8,128)(2,1)S(1)}, bf16[2,80,768]{2,1,0:T(8,128)(2,1)S(1)}, u32[]{:S(2)}, u32[]{:S(2)}) collective-permute-start(bf16[2,80,768]{2,1,0:T(8,128)(2,1)S(1)} %get-tuple-element.57.refs_6_), channel_id=1, source_target_pairs={{0,2},{1,3},{2,0},{3,1},{4,6},{5,7},{6,4},{7,5},{8,10},{9,11},{10,... | collective-permute-start | bytes 737288 | tf_op jit(solution)/shard_map/ppermute | solution.py:295
  24.4 1.4 %collective-permute-start.7 = (bf16[80,768]{1,0:T(8,128)(2,1)S(1)}, bf16[80,768]{1,0:T(8,128)(2,1)S(1)}, u32[]{:S(2)}, u32[]{:S(2)}) collective-permute-start(bf16[80,768]{1,0:T(8,128)(2,1)S(1)} %shard_map.92), channel_id=1, source_target_pairs={{0,1},{1,0},{2,3},{3,2},{4,5},{5,4},{6,7},{7,6},{8,9},{9,8},{10,11... | collective-permute-start | bytes 368648 | tf_op jit(solution)/shard_map/ppermute | solution.py:295
  25.9 5.4 %collective-permute-start.8 = (bf16[80,768]{1,0:T(8,128)(2,1)S(1)}, bf16[80,768]{1,0:T(8,128)(2,1)S(1)}, u32[]{:S(2)}, u32[]{:S(2)}) collective-permute-start(bf16[80,768]{1,0:T(8,128)(2,1)S(1)} %get-tuple-element.69), channel_id=1, source_target_pairs={{0,2},{1,3},{2,0},{3,1},{4,6},{5,7},{6,4},{7,5},{8,10},{9,11},{10,... | collective-permute-start | bytes 368648 | tf_op jit(solution)/shard_map/ppermute | solution.py:295
  27.6 3.7 %collective-permute-start.10 = (bf16[80,768]{1,0:T(8,128)(2,1)S(1)}, bf16[80,768]{1,0:T(8,128)(2,1)S(1)}, u32[]{:S(2)}, u32[]{:S(2)}) collective-permute-start(bf16[80,768]{1,0:T(8,128)(2,1)S(1)} %get-tuple-element.61.mine_act), channel_id=1, source_target_pairs={{0,1},{1,0},{2,3},{3,2},{4,5},{5,4},{6,7},{7,6},{8,9},{9,8},{10,11... | collective-permute-start | bytes 368648 | tf_op jit(solution)/shard_map/ppermute | solution.py:295
  31.4 1.6 %collective-permute-start.11 = (bf16[2,80,768]{2,1,0:T(8,128)(2,1)S(1)}, bf16[2,80,768]{2,1,0:T(8,128)(2,1)S(1)}, u32[]{:S(2)}, u32[]{:S(2)}) collective-permute-start(bf16[2,80,768]{2,1,0:T(8,128)(2,1)S(1)} %shard_map.94.mine), channel_id=1, source_target_pairs={{0,1},{1,0},{2,3},{3,2},{4,5},{5,4},{6,7},{7,6},{8,9},{9,8},{10,11... | collective-permute-start | bytes 737288 | tf_op jit(solution)/shard_map/ppermute | solution.py:295
  33.9 8.7 %collective-permute-start.12 = (bf16[40,1024]{1,0:T(8,128)(2,1)S(1)}, bf16[40,1024]{1,0:T(8,128)(2,1)S(1)}, u32[]{:S(2)}, u32[]{:S(2)}) collective-permute-start(bf16[40,1024]{1,0:T(8,128)(2,1)S(1)} %get-tuple-element.62), channel_id=1, source_target_pairs={{0,4},{4,8},{8,12},{12,0},{1,5},{5,9},{9,13},{13,1},{2,6},{6,10},{... | collective-permute-start | bytes 245768 | tf_op jit(solution)/shard_map/ppermute | solution.py:290
  34.0 9.7 %collective-permute-start.13 = (bf16[40,1024]{1,0:T(8,128)(2,1)S(1)}, bf16[40,1024]{1,0:T(8,128)(2,1)S(1)}, u32[]{:S(2)}, u32[]{:S(2)}) collective-permute-start(bf16[40,1024]{1,0:T(8,128)(2,1)S(1)} %get-tuple-element.63), channel_id=1, source_target_pairs={{0,8},{4,12},{8,0},{12,4},{1,9},{5,13},{9,1},{13,5},{2,10},{6,14},... | collective-permute-start | bytes 245768 | tf_op jit(solution)/shard_map/ppermute | solution.py:290
  36.9 6.8 %collective-permute-start.14 = (bf16[40,1024]{1,0:T(8,128)(2,1)S(1)}, bf16[40,1024]{1,0:T(8,128)(2,1)S(1)}, u32[]{:S(2)}, u32[]{:S(2)}) collective-permute-start(bf16[40,1024]{1,0:T(8,128)(2,1)S(1)} %get-tuple-element.64), channel_id=1, source_target_pairs={{0,12},{4,0},{8,4},{12,8},{1,13},{5,1},{9,5},{13,9},{2,14},{6,2},{... | collective-permute-start | bytes 245768 | tf_op jit(solution)/shard_map/ppermute | solution.py:290

commit v14 on v12

--- a/solution.py
+++ b/solution.py
@@ -179,12 +179,12 @@
     place_out[...] = place
     rows_out[...] = rows_in
     for matrix in range(2):
-        out[matrix] = mm(rows_in, held[matrix], LANES).astype(BF)
+        out[matrix] = mm(held[matrix], rows_in, LANES).T.astype(BF)
 
 
 def mine_pair(rows_in, held, out):
     for matrix in range(2):
-        out[matrix] = mm(rows_in[...], held[matrix], LANES).astype(BF)
+        out[matrix] = mm(held[matrix], rows_in[...], LANES).T.astype(BF)
 
 
 def pair_sum(mine, other, held_out, sent_out):
@@ -199,7 +199,7 @@
     rows_grad = mm(place[...], stacked(pieces, 1).astype(BF), ROWS).astype(BF)
     if own:
         refs[-2][...] = rows_grad
-    refs[-1][...] = mm(rows_grad, held[2], LANES).astype(BF)
+    refs[-1][...] = mm(held[2], rows_grad, LANES).T.astype(BF)
 
 
 def gates(pair, pair_far, act_out, by_gate, by_up):

time: 43.9 us -> 43.9 us (level)
  no operation moved by 1% of the time
where the time goes in v14:
time: 43.9 us; the launch traced here: 43.7 us
  starting transfers between devices  17.6 us (40%)
  Pallas kernels  16.7 us (38%)
  waiting for transfers between devices  8.63 us (20%)
  between operations  0.76 us (2%)
    pallas_call x14, Pallas kernels, call(): pl.pallas_call(body, out_shape=outs, in_specs=specs, out_specs=out_specs...  16.7 us
    ppermute x11, starting transfers between devices, swap(): return lax.ppermute(value, axis, [(i, i ^ bit) for i in range(count)])  12.6 us
    ppermute x11, waiting for transfers between devices, swap(): return lax.ppermute(value, axis, [(i, i ^ bit) for i in range(count)])  7.36 us
    ppermute x3, starting transfers between devices, shift(): lax.ppermute(value, axis, [(i, (i + step) % count) for i in range(count)])  4.94 us
    ppermute x3, waiting for transfers between devices, shift(): lax.ppermute(value, axis, [(i, (i + step) % count) for i in range(count)])  1.26 us
  transfers between devices with their start and end apart: 14, of which 9 were waited for; matrix products, arithmetic and copies ran while one was open for 0% of the time, Pallas kernels for 30%

profile of v14, /device:TPU:0, one launch (start us, length us, event | category | flops | bytes accessed | tf_op | source)
XLA Modules:
  0.0 43.7 jit_solution(9791316100400487810)
XLA Ops:
  0.6 1.5 %shard_map.85 = (bf16[160,256]{1,0:T(8,128)(2,1)S(1)}, f32[160,1]{1,0:T(8,128)S(1)}, bf16[256,1024]{1,0:T(8,128)(2,1)S(1)}, bf16[40,1024]{1,0:T(8,128)(2,1)S(1)}...) custom-call(s32[8,256]{1,0:T(8,128)} %bitcast.2, ...), custom_call_target="tpu_custom_call" | custom-call | flops 83886080 | bytes 1048576 | tf_op jit(solution)/shard_map/pallas_call | solution.py:69
  2.1 4.1 %collective-permute-start.3 = (bf16[40,1024]{1,0:T(8,128)(2,1)S(1)}, bf16[40,1024]{1,0:T(8,128)(2,1)S(1)}, u32[]{:S(2)}, u32[]{:S(2)}) collective-permute-start(bf16[40,1024]{1,0:T(8,128)(2,1)S(1)} %get-tuple-element.46), channel_id=1, source_target_pairs={{0,8},{4,12},{8,0},{12,4},{1,9},{5,13},{9,1},{13,5},{2,10},{6,14},... | collective-permute-start | bytes 245768 | tf_op jit(solution)/shard_map/ppermute | solution.py:299
  6.2 1.3 %collective-permute-start.4 = (bf16[40,1024]{1,0:T(8,128)(2,1)S(1)}, bf16[40,1024]{1,0:T(8,128)(2,1)S(1)}, u32[]{:S(2)}, u32[]{:S(2)}) collective-permute-start(bf16[40,1024]{1,0:T(8,128)(2,1)S(1)} %get-tuple-element.47), channel_id=1, source_target_pairs={{0,12},{4,8},{8,4},{12,0},{1,13},{5,9},{9,5},{13,1},{2,14},{6,10},... | collective-permute-start | bytes 245768 | tf_op jit(solution)/shard_map/ppermute | solution.py:299
  8.1 3.8 %shard_map.87 = (bf16[3,768,1024]{2,1,0:T(8,128)(2,1)S(1)}, bf16[3,768,1024]{2,1,0:T(8,128)(2,1)S(1)}, bf16[40,1024]{1,0:T(8,128)(2,1)S(1)}, bf16[40,1024]{1,0:T(8,128)(2,1)S(1)}, bf16[40,1024]{1,0:T(8,128)(2,1)S(1)}) custom-call(bf16[1,2,1536,1024]{3,2,1,0:T(8,128)(2,1)} %gate_up.1, bf16[1,1536,1024]{2,1,0:T(8,128)(2,1)} %down.1, ...), custom_call_target="tpu_custom_call" | custom-call | flops 25165824000 | bytes 314572800 | tf_op jit(solution)/shard_map/pallas_call | solution.py:69
  11.9 3.0 %collective-permute-start = (bf16[40,1024]{1,0:T(8,128)(2,1)S(1)}, bf16[40,1024]{1,0:T(8,128)(2,1)S(1)}, u32[]{:S(2)}, u32[]{:S(2)}) collective-permute-start(bf16[40,1024]{1,0:T(8,128)(2,1)S(1)} %get-tuple-element.42), channel_id=1, source_target_pairs={{0,12},{4,8},{8,4},{12,0},{1,13},{5,9},{9,5},{13,1},{2,14},{6,10},... | collective-permute-start | bytes 245768 | tf_op jit(solution)/shard_map/ppermute | solution.py:299
  15.5 1.5 %shard_map.88 = (bf16[2,80,768]{2,1,0:T(8,128)(2,1)S(1)}, bf16[160,80]{1,0:T(8,128)(2,1)S(1)}, bf16[80,1024]{1,0:T(8,128)(2,1)S(1)}) custom-call(bf16[40,1024]{1,0:T(8,128)(2,1)S(1)} %collective-permute-done.3.refs_0_, bf16[40,1024]{1,0:T(8,128)(2,1)S(1)} %collective-permute-done.4.refs_1_, bf16[80,1024]{1,0:T(8,128)(2,1)S(1)} %collective-permute-done.2.refs_2_, ...), custom_call_target="tpu_custom_call" | custom-call | flops 503316480 | bytes 3145728 | tf_op jit(solution)/shard_map/pallas_call | solution.py:69
  17.1 1.1 %shard_map.90.mine = bf16[2,80,768]{2,1,0:T(8,128)(2,1)S(1)} custom-call(bf16[80,1024]{1,0:T(8,128)(2,1)S(1)} %get-tuple-element.53.rows_in, bf16[3,768,1024]{2,1,0:T(8,128)(2,1)S(1)} %get-tuple-element.51.refs_5_.held), custom_call_target="tpu_custom_call" | custom-call | flops 25165824000 | bytes 314572800 | tf_op jit(solution)/shard_map/pallas_call | solution.py:69
  18.7 1.7 %collective-permute-start.8 = (bf16[2,80,768]{2,1,0:T(8,128)(2,1)S(1)}, bf16[2,80,768]{2,1,0:T(8,128)(2,1)S(1)}, u32[]{:S(2)}, u32[]{:S(2)}) collective-permute-start(bf16[2,80,768]{2,1,0:T(8,128)(2,1)S(1)} %get-tuple-element.55.refs_6_), channel_id=1, source_target_pairs={{0,2},{1,3},{2,0},{3,1},{4,6},{5,7},{6,4},{7,5},{8,10},{9,11},{10,... | collective-permute-start | bytes 737288 | tf_op jit(solution)/shard_map/ppermute | solution.py:299
  20.4 1.7 %collective-permute-done.1.refs_1_ = bf16[40,1024]{1,0:T(8,128)(2,1)S(1)} collective-permute-done((bf16[40,1024]{1,0:T(8,128)(2,1)S(1)}, bf16[40,1024]{1,0:T(8,128)(2,1)S(1)}, u32[]{:S(2)}, u32[]{:S(2)}) %collective-permute-start.1) | collective-permute-done | bytes 81952 | tf_op jit(solution)/shard_map/ppermute | solution.py:299
  22.1 0.8 %shard_map.92 = bf16[80,768]{1,0:T(8,128)(2,1)S(1)} custom-call(bf16[40,1024]{1,0:T(8,128)(2,1)S(1)} %collective-permute-done.refs_0_, bf16[40,1024]{1,0:T(8,128)(2,1)S(1)} %collective-permute-done.1.refs_1_, bf16[80,1024]{1,0:T(8,128)(2,1)S(1)} %collective-permute-done.2.refs_2_, bf16[40,1024]{1,0:T(8,128)(2,1)S(1)} %get-tuple-element.45.refs_3_, ...), custom_call_target="tpu_custom_call" | custom-call | flops 251658240 | bytes 3145728 | tf_op jit(solution)/shard_map/pallas_call | solution.py:69
  22.9 0.8 %shard_map.89 = (bf16[80,1024]{1,0:T(8,128)(2,1)S(1)}, bf16[80,768]{1,0:T(8,128)(2,1)S(1)}) custom-call(bf16[40,1024]{1,0:T(8,128)(2,1)S(1)} %collective-permute-done.refs_0_, bf16[40,1024]{1,0:T(8,128)(2,1)S(1)} %collective-permute-done.1.refs_1_, bf16[80,1024]{1,0:T(8,128)(2,1)S(1)} %collective-permute-done.2.refs_2_, ...), custom_call_target="tpu_custom_call" | custom-call | flops 25165824000 | bytes 314572800 | tf_op jit(solution)/shard_map/pallas_call | solution.py:69
  23.8 0.5 %collective-permute-done.6 = bf16[80,768]{1,0:T(8,128)(2,1)S(1)} collective-permute-done((bf16[80,768]{1,0:T(8,128)(2,1)S(1)}, bf16[80,768]{1,0:T(8,128)(2,1)S(1)}, u32[]{:S(2)}, u32[]{:S(2)}) %collective-permute-start.6) | collective-permute-done | bytes 122912 | tf_op jit(solution)/shard_map/ppermute | solution.py:299
  24.3 1.6 %collective-permute-start.7 = (bf16[80,768]{1,0:T(8,128)(2,1)S(1)}, bf16[80,768]{1,0:T(8,128)(2,1)S(1)}, u32[]{:S(2)}, u32[]{:S(2)}) collective-permute-start(bf16[80,768]{1,0:T(8,128)(2,1)S(1)} %get-tuple-element.67), channel_id=1, source_target_pairs={{0,2},{1,3},{2,0},{3,1},{4,6},{5,7},{6,4},{7,5},{8,10},{9,11},{10,... | collective-permute-start | bytes 368648 | tf_op jit(solution)/shard_map/ppermute | solution.py:299
  25.9 0.8 %collective-permute-done.8.pair_far = bf16[2,80,768]{2,1,0:T(8,128)(2,1)S(1)} collective-permute-done((bf16[2,80,768]{2,1,0:T(8,128)(2,1)S(1)}, bf16[2,80,768]{2,1,0:T(8,128)(2,1)S(1)}, u32[]{:S(2)}, u32[]{:S(2)}) %collective-permute-start.8) | collective-permute-done | bytes 245792 | tf_op jit(solution)/shard_map/ppermute | solution.py:299
  26.9 2.8 %collective-permute-done.7.act_far = bf16[80,768]{1,0:T(8,128)(2,1)S(1)} collective-permute-done((bf16[80,768]{1,0:T(8,128)(2,1)S(1)}, bf16[80,768]{1,0:T(8,128)(2,1)S(1)}, u32[]{:S(2)}, u32[]{:S(2)}) %collective-permute-start.7) | collective-permute-done | bytes 122912 | tf_op jit(solution)/shard_map/ppermute | solution.py:299
  29.9 0.7 %shard_map.95.total = f32[80,1024]{1,0:T(8,128)S(1)} custom-call(bf16[2,80,768]{2,1,0:T(8,128)(2,1)S(1)} %shard_map.94.mine, bf16[3,768,1024]{2,1,0:T(8,128)(2,1)S(1)} %get-tuple-element.51.refs_5_.held), custom_call_target="tpu_custom_call" | custom-call | flops 251658240 | bytes 3145728 | tf_op jit(solution)/shard_map/pallas_call | solution.py:69
  30.6 0.8 %collective-permute-done.10.other = bf16[2,80,768]{2,1,0:T(8,128)(2,1)S(1)} collective-permute-done((bf16[2,80,768]{2,1,0:T(8,128)(2,1)S(1)}, bf16[2,80,768]{2,1,0:T(8,128)(2,1)S(1)}, u32[]{:S(2)}, u32[]{:S(2)}) %collective-permute-start.10) | collective-permute-done | bytes 245792 | tf_op jit(solution)/shard_map/ppermute | solution.py:299
  31.4 0.9 %shard_map.96 = (bf16[40,1024]{1,0:T(8,128)(2,1)S(1)}, bf16[40,1024]{1,0:T(8,128)(2,1)S(1)}, bf16[40,1024]{1,0:T(8,128)(2,1)S(1)}, bf16[40,1024]{1,0:T(8,128)(2,1)S(1)}) custom-call(f32[80,1024]{1,0:T(8,128)S(1)} %shard_map.95.total, bf16[2,80,768]{2,1,0:T(8,128)(2,1)S(1)} %collective-permute-done.10.other, ...), custom_call_target="tpu_custom_call" | custom-call | flops 251658240 | bytes 3145728 | tf_op jit(solution)/shard_map/pallas_call | solution.py:69
  32.3 0.6 %collective-permute-start.11 = (bf16[40,1024]{1,0:T(8,128)(2,1)S(1)}, bf16[40,1024]{1,0:T(8,128)(2,1)S(1)}, u32[]{:S(2)}, u32[]{:S(2)}) collective-permute-start(bf16[40,1024]{1,0:T(8,128)(2,1)S(1)} %get-tuple-element.60), channel_id=1, source_target_pairs={{0,4},{4,8},{8,12},{12,0},{1,5},{5,9},{9,13},{13,1},{2,6},{6,10},{... | collective-permute-start | bytes 245768 | tf_op jit(solution)/shard_map/ppermute | solution.py:294
  32.8 3.7 %collective-permute-start.12 = (bf16[40,1024]{1,0:T(8,128)(2,1)S(1)}, bf16[40,1024]{1,0:T(8,128)(2,1)S(1)}, u32[]{:S(2)}, u32[]{:S(2)}) collective-permute-start(bf16[40,1024]{1,0:T(8,128)(2,1)S(1)} %get-tuple-element.61), channel_id=1, source_target_pairs={{0,8},{4,12},{8,0},{12,4},{1,9},{5,13},{9,1},{13,5},{2,10},{6,14},... | collective-permute-start | bytes 245768 | tf_op jit(solution)/shard_map/ppermute | solution.py:294
  36.6 0.6 %collective-permute-start.13 = (bf16[40,1024]{1,0:T(8,128)(2,1)S(1)}, bf16[40,1024]{1,0:T(8,128)(2,1)S(1)}, u32[]{:S(2)}, u32[]{:S(2)}) collective-permute-start(bf16[40,1024]{1,0:T(8,128)(2,1)S(1)} %get-tuple-element.62), channel_id=1, source_target_pairs={{0,12},{4,0},{8,4},{12,8},{1,13},{5,1},{9,5},{13,9},{2,14},{6,2},{... | collective-permute-start | bytes 245768 | tf_op jit(solution)/shard_map/ppermute | solution.py:294
  37.2 4.1 %shard_map.98 = (bf16[1,2,1536,1024]{3,2,1,0:T(8,128)(2,1)}, bf16[1,1536,1024]{2,1,0:T(8,128)(2,1)}) custom-call(bf16[80,768]{1,0:T(8,128)(2,1)S(1)} %get-tuple-element.59.mine_act, bf16[80,768]{1,0:T(8,128)(2,1)S(1)} %collective-permute-done.9._.other_act, bf16[2,80,768]{2,1,0:T(8,128)(2,1)S(1)} %shard_map.94.mine, ...), custom_call_target="tpu_custom_call" | custom-call | flops 754974720 | bytes 9437184 | tf_op jit(solution)/shard_map/pallas_call | solution.py:69
  41.4 1.0 %collective-permute-done.12.refs_1_ = bf16[40,1024]{1,0:T(8,128)(2,1)S(1)} collective-permute-done((bf16[40,1024]{1,0:T(8,128)(2,1)S(1)}, bf16[40,1024]{1,0:T(8,128)(2,1)S(1)}, u32[]{:S(2)}, u32[]{:S(2)}) %collective-permute-start.12) | collective-permute-done | bytes 81952 | tf_op jit(solution)/shard_map/ppermute | solution.py:294
  42.6 1.1 %shard_map.97 = bf16[256,1024]{1,0:T(8,128)(2,1)} custom-call(bf16[160,256]{1,0:T(8,128)(2,1)S(1)} %get-tuple-element.35.pick, bf16[40,1024]{1,0:T(8,128)(2,1)S(1)} %collective-permute-done.11.refs_0_, bf16[40,1024]{1,0:T(8,128)(2,1)S(1)} %collective-permute-done.12.refs_1_, bf16[40,1024]{1,0:T(8,128)(2,1)S(1)} %collective-permute-done.13.refs_2_, ...), custom_call_target="tpu_custom_call" | custom-call | flops 83886080 | bytes 1048576 | tf_op jit(solution)/shard_map/pallas_call | solution.py:69
  (19 shorter events, 2.4 us)
Async XLA Ops:
  2.1 13.1 %collective-permute-start.3 = (bf16[40,1024]{1,0:T(8,128)(2,1)S(1)}, bf16[40,1024]{1,0:T(8,128)(2,1)S(1)}, u32[]{:S(2)}, u32[]{:S(2)}) collective-permute-start(bf16[40,1024]{1,0:T(8,128)(2,1)S(1)} %get-tuple-element.46), channel_id=1, source_target_pairs={{0,8},{4,12},{8,0},{12,4},{1,9},{5,13},{9,1},{13,5},{2,10},{6,14},... | collective-permute-start | bytes 245768 | tf_op jit(solution)/shard_map/ppermute | solution.py:299
  6.2 9.0 %collective-permute-start.4 = (bf16[40,1024]{1,0:T(8,128)(2,1)S(1)}, bf16[40,1024]{1,0:T(8,128)(2,1)S(1)}, u32[]{:S(2)}, u32[]{:S(2)}) collective-permute-start(bf16[40,1024]{1,0:T(8,128)(2,1)S(1)} %get-tuple-element.47), channel_id=1, source_target_pairs={{0,12},{4,8},{8,4},{12,0},{1,13},{5,9},{9,5},{13,1},{2,14},{6,10},... | collective-permute-start | bytes 245768 | tf_op jit(solution)/shard_map/ppermute | solution.py:299
  7.8 7.7 %collective-permute-start.2 = (bf16[80,1024]{1,0:T(8,128)(2,1)S(1)}, bf16[80,1024]{1,0:T(8,128)(2,1)S(1)}, u32[]{:S(2)}, u32[]{:S(2)}) collective-permute-start(bf16[80,1024]{1,0:T(8,128)(2,1)S(1)} %get-tuple-element.44), channel_id=1, source_target_pairs={{0,4},{4,0},{8,12},{12,8},{1,5},{5,1},{9,13},{13,9},{2,6},{6,2},{1... | collective-permute-start | bytes 491528 | tf_op jit(solution)/shard_map/ppermute | solution.py:299
  11.9 8.4 %collective-permute-start = (bf16[40,1024]{1,0:T(8,128)(2,1)S(1)}, bf16[40,1024]{1,0:T(8,128)(2,1)S(1)}, u32[]{:S(2)}, u32[]{:S(2)}) collective-permute-start(bf16[40,1024]{1,0:T(8,128)(2,1)S(1)} %get-tuple-element.42), channel_id=1, source_target_pairs={{0,12},{4,8},{8,4},{12,0},{1,13},{5,9},{9,5},{13,1},{2,14},{6,10},... | collective-permute-start | bytes 245768 | tf_op jit(solution)/shard_map/ppermute | solution.py:299
  14.9 7.1 %collective-permute-start.1 = (bf16[40,1024]{1,0:T(8,128)(2,1)S(1)}, bf16[40,1024]{1,0:T(8,128)(2,1)S(1)}, u32[]{:S(2)}, u32[]{:S(2)}) collective-permute-start(bf16[40,1024]{1,0:T(8,128)(2,1)S(1)} %get-tuple-element.43), channel_id=1, source_target_pairs={{0,8},{4,12},{8,0},{12,4},{1,9},{5,13},{9,1},{13,5},{2,10},{6,14},... | collective-permute-start | bytes 245768 | tf_op jit(solution)/shard_map/ppermute | solution.py:299
  17.0 1.6 %collective-permute-start.5 = (bf16[2,80,768]{2,1,0:T(8,128)(2,1)S(1)}, bf16[2,80,768]{2,1,0:T(8,128)(2,1)S(1)}, u32[]{:S(2)}, u32[]{:S(2)}) collective-permute-start(bf16[2,80,768]{2,1,0:T(8,128)(2,1)S(1)} %get-tuple-element.54), channel_id=1, source_target_pairs={{0,1},{1,0},{2,3},{3,2},{4,5},{5,4},{6,7},{7,6},{8,9},{9,8},{10,11... | collective-permute-start | bytes 737288 | tf_op jit(solution)/shard_map/ppermute | solution.py:299
  18.7 8.1 %collective-permute-start.8 = (bf16[2,80,768]{2,1,0:T(8,128)(2,1)S(1)}, bf16[2,80,768]{2,1,0:T(8,128)(2,1)S(1)}, u32[]{:S(2)}, u32[]{:S(2)}) collective-permute-start(bf16[2,80,768]{2,1,0:T(8,128)(2,1)S(1)} %get-tuple-element.55.refs_6_), channel_id=1, source_target_pairs={{0,2},{1,3},{2,0},{3,1},{4,6},{5,7},{6,4},{7,5},{8,10},{9,11},{10,... | collective-permute-start | bytes 737288 | tf_op jit(solution)/shard_map/ppermute | solution.py:299
  22.9 1.4 %collective-permute-start.6 = (bf16[80,768]{1,0:T(8,128)(2,1)S(1)}, bf16[80,768]{1,0:T(8,128)(2,1)S(1)}, u32[]{:S(2)}, u32[]{:S(2)}) collective-permute-start(bf16[80,768]{1,0:T(8,128)(2,1)S(1)} %shard_map.92), channel_id=1, source_target_pairs={{0,1},{1,0},{2,3},{3,2},{4,5},{5,4},{6,7},{7,6},{8,9},{9,8},{10,11... | collective-permute-start | bytes 368648 | tf_op jit(solution)/shard_map/ppermute | solution.py:299
  24.3 5.4 %collective-permute-start.7 = (bf16[80,768]{1,0:T(8,128)(2,1)S(1)}, bf16[80,768]{1,0:T(8,128)(2,1)S(1)}, u32[]{:S(2)}, u32[]{:S(2)}) collective-permute-start(bf16[80,768]{1,0:T(8,128)(2,1)S(1)} %get-tuple-element.67), channel_id=1, source_target_pairs={{0,2},{1,3},{2,0},{3,1},{4,6},{5,7},{6,4},{7,5},{8,10},{9,11},{10,... | collective-permute-start | bytes 368648 | tf_op jit(solution)/shard_map/ppermute | solution.py:299
  26.9 2.9 %collective-permute-start.9 = (bf16[80,768]{1,0:T(8,128)(2,1)S(1)}, bf16[80,768]{1,0:T(8,128)(2,1)S(1)}, u32[]{:S(2)}, u32[]{:S(2)}) collective-permute-start(bf16[80,768]{1,0:T(8,128)(2,1)S(1)} %get-tuple-element.59.mine_act), channel_id=1, source_target_pairs={{0,1},{1,0},{2,3},{3,2},{4,5},{5,4},{6,7},{7,6},{8,9},{9,8},{10,11... | collective-permute-start | bytes 368648 | tf_op jit(solution)/shard_map/ppermute | solution.py:299
  29.8 1.6 %collective-permute-start.10 = (bf16[2,80,768]{2,1,0:T(8,128)(2,1)S(1)}, bf16[2,80,768]{2,1,0:T(8,128)(2,1)S(1)}, u32[]{:S(2)}, u32[]{:S(2)}) collective-permute-start(bf16[2,80,768]{2,1,0:T(8,128)(2,1)S(1)} %shard_map.94.mine), channel_id=1, source_target_pairs={{0,1},{1,0},{2,3},{3,2},{4,5},{5,4},{6,7},{7,6},{8,9},{9,8},{10,11... | collective-permute-start | bytes 737288 | tf_op jit(solution)/shard_map/ppermute | solution.py:299
  32.3 9.1 %collective-permute-start.11 = (bf16[40,1024]{1,0:T(8,128)(2,1)S(1)}, bf16[40,1024]{1,0:T(8,128)(2,1)S(1)}, u32[]{:S(2)}, u32[]{:S(2)}) collective-permute-start(bf16[40,1024]{1,0:T(8,128)(2,1)S(1)} %get-tuple-element.60), channel_id=1, source_target_pairs={{0,4},{4,8},{8,12},{12,0},{1,5},{5,9},{9,13},{13,1},{2,6},{6,10},{... | collective-permute-start | bytes 245768 | tf_op jit(solution)/shard_map/ppermute | solution.py:294
  32.8 9.6 %collective-permute-start.12 = (bf16[40,1024]{1,0:T(8,128)(2,1)S(1)}, bf16[40,1024]{1,0:T(8,128)(2,1)S(1)}, u32[]{:S(2)}, u32[]{:S(2)}) collective-permute-start(bf16[40,1024]{1,0:T(8,128)(2,1)S(1)} %get-tuple-element.61), channel_id=1, source_target_pairs={{0,8},{4,12},{8,0},{12,4},{1,9},{5,13},{9,1},{13,5},{2,10},{6,14},... | collective-permute-start | bytes 245768 | tf_op jit(solution)/shard_map/ppermute | solution.py:294
  36.6 6.0 %collective-permute-start.13 = (bf16[40,1024]{1,0:T(8,128)(2,1)S(1)}, bf16[40,1024]{1,0:T(8,128)(2,1)S(1)}, u32[]{:S(2)}, u32[]{:S(2)}) collective-permute-start(bf16[40,1024]{1,0:T(8,128)(2,1)S(1)} %get-tuple-element.62), channel_id=1, source_target_pairs={{0,12},{4,0},{8,4},{12,8},{1,13},{5,1},{9,5},{13,9},{2,14},{6,2},{... | collective-permute-start | bytes 245768 | tf_op jit(solution)/shard_map/ppermute | solution.py:294

commit v15 on v12

--- a/solution.py
+++ b/solution.py
@@ -226,9 +226,8 @@
     pieces, whole = refs[:experts], refs[experts]
     rows = total[...] + mm(other[0], held[0]) + mm(other[1], held[1])
     whole[...] = mm(place[...], rows.astype(BF))
-    me = lax.axis_index("ex")
-    for piece, step in zip(pieces, shifts(experts)):
-        piece[...] = whole[place_of(lax.rem(me + step, experts), experts)].astype(BF)
+    for piece, step in zip(pieces, steps(experts)):
+        piece[...] = whole[place_of(ahead(step, experts), experts)].astype(BF)
 
 
 def weight_grads(mine_act, other_act, mine, other, rows_in, rows_grad, pair_out, down_out, held, sems):
@@ -259,9 +258,8 @@
 
 def combine(experts, pick, *refs):
     out, whole, held, sems = refs[experts:]
-    me = lax.axis_index("ex")
-    for piece, step in zip(refs[:experts], shifts(experts)):
-        whole[place_of(lax.rem(me + experts - step, experts), experts)] = piece[...].astype(F32)
+    for piece, step in zip(refs[:experts], steps(experts)):
+        whole[place_of(ahead(experts - step, experts), experts)] = piece[...].astype(F32)
     home = whole[...].astype(BF)
     rows = out.shape[0] // held.shape[0]
     stores = []
@@ -285,13 +283,32 @@
     return pl.ds(pl.multiple_of(spot, 8), MOST)
 
 
-def shifts(experts):
-    return list(range(1, experts)) + [0]
+def tour(count):
+    bits = count.bit_length() - 1
+    return [sum(((i >> b) & 1) << (bits - 1 - b) for b in range(bits)) for i in range(count)]
+
+
+def steps(count):
+    found = []
+    for step in range(1, count // 2 + 1):
+        found += [step, count - step]
+    return list(dict.fromkeys(found)) + [0]
+
+
+def ahead(step, count):
+    me, names = lax.axis_index("ex"), tour(count)
+    found = jnp.int32(0)
+    for at, name in enumerate(names):
+        found = found + jnp.where(me == name, names[(at + step) % count], 0)
+    return found
 
 
 def shift(value, axis, step):
     count = lax.axis_size(axis)
-    return lax.ppermute(value, axis, [(i, (i + step) % count) for i in range(count)])
+    names = tour(count)
+    return lax.ppermute(
+        value, axis, [(name, names[(at + step) % count]) for at, name in enumerate(names)]
+    )
 
 
 def swap(value, axis, bit):
@@ -440,7 +457,7 @@
         flops=weight_flops,
         traffic=weight_bytes,
     )
-    home = [shift(part, "ex", step) if step else part for part, step in zip(back, shifts(experts))]
+    home = [shift(part, "ex", step) if step else part for part, step in zip(back, steps(experts))]
     pair_grad, down_grad = call(
         weight_grads,
         [sds((1, 2, hidden, width), BF), sds((1, hidden, width), BF)],

time: 43.9 us -> 43.6 us (level)
  starting transfers between devices: 17.6 us -> 17 us
    ppermute x3, starting transfers between devices: 5 us -> 4.35 us  [shift(): lax.ppermute(value, axis, [(name, names[(at + step) % count]) for at, nam...]
  transfers between devices with their start and end apart: 14 -> 14, of which waited for: 9 -> 8; matrix products, arithmetic and copies ran while one was open for 0% -> 0% of each run, Pallas kernels for 30% -> 30%
where the time goes in v15:
time: 43.6 us; the launch traced here: 43.3 us
  starting transfers between devices  17 us (39%)
  Pallas kernels  16.4 us (38%)
  waiting for transfers between devices  9.15 us (21%)
  between operations  0.75 us (2%)
    pallas_call x14, Pallas kernels, call(): pl.pallas_call(body, out_shape=outs, in_specs=specs, out_specs=out_specs...  16.4 us
    ppermute x11, starting transfers between devices, swap(): return lax.ppermute(value, axis, [(i, i ^ bit) for i in range(count)])  12.6 us
    ppermute x11, waiting for transfers between devices, swap(): return lax.ppermute(value, axis, [(i, i ^ bit) for i in range(count)])  7.54 us
    ppermute x3, starting transfers between devices, shift(): lax.ppermute(value, axis, [(name, names[(at + step) % count]) for at, nam...  4.35 us
    ppermute x3, waiting for transfers between devices, shift(): lax.ppermute(value, axis, [(name, names[(at + step) % count]) for at, nam...  1.61 us
  transfers between devices with their start and end apart: 14, of which 8 were waited for; matrix products, arithmetic and copies ran while one was open for 0% of the time, Pallas kernels for 30%

profile of v15, /device:TPU:0, one launch (start us, length us, event | category | flops | bytes accessed | tf_op | source)
XLA Modules:
  0.0 43.3 jit_solution(10994797376760028182)
XLA Ops:
  0.6 1.5 %shard_map.85 = (bf16[160,256]{1,0:T(8,128)(2,1)S(1)}, f32[160,1]{1,0:T(8,128)S(1)}, bf16[256,1024]{1,0:T(8,128)(2,1)S(1)}, bf16[40,1024]{1,0:T(8,128)(2,1)S(1)}...) custom-call(s32[8,256]{1,0:T(8,128)} %bitcast.2, ...), custom_call_target="tpu_custom_call" | custom-call | flops 83886080 | bytes 1048576 | tf_op jit(solution)/shard_map/pallas_call | solution.py:69
  2.1 4.1 %collective-permute-start.3 = (bf16[40,1024]{1,0:T(8,128)(2,1)S(1)}, bf16[40,1024]{1,0:T(8,128)(2,1)S(1)}, u32[]{:S(2)}, u32[]{:S(2)}) collective-permute-start(bf16[40,1024]{1,0:T(8,128)(2,1)S(1)} %get-tuple-element.46), channel_id=1, source_target_pairs={{0,8},{4,12},{8,0},{12,4},{1,9},{5,13},{9,1},{13,5},{2,10},{6,14},... | collective-permute-start | bytes 245768 | tf_op jit(solution)/shard_map/ppermute | solution.py:316
  6.2 1.3 %collective-permute-start.4 = (bf16[40,1024]{1,0:T(8,128)(2,1)S(1)}, bf16[40,1024]{1,0:T(8,128)(2,1)S(1)}, u32[]{:S(2)}, u32[]{:S(2)}) collective-permute-start(bf16[40,1024]{1,0:T(8,128)(2,1)S(1)} %get-tuple-element.47), channel_id=1, source_target_pairs={{0,12},{4,8},{8,4},{12,0},{1,13},{5,9},{9,5},{13,1},{2,14},{6,10},... | collective-permute-start | bytes 245768 | tf_op jit(solution)/shard_map/ppermute | solution.py:316
  8.1 3.8 %shard_map.87 = (bf16[3,768,1024]{2,1,0:T(8,128)(2,1)S(1)}, bf16[3,768,1024]{2,1,0:T(8,128)(2,1)S(1)}, bf16[40,1024]{1,0:T(8,128)(2,1)S(1)}, bf16[40,1024]{1,0:T(8,128)(2,1)S(1)}, bf16[40,1024]{1,0:T(8,128)(2,1)S(1)}) custom-call(bf16[1,2,1536,1024]{3,2,1,0:T(8,128)(2,1)} %gate_up.1, bf16[1,1536,1024]{2,1,0:T(8,128)(2,1)} %down.1, ...), custom_call_target="tpu_custom_call" | custom-call | flops 25165824000 | bytes 314572800 | tf_op jit(solution)/shard_map/pallas_call | solution.py:69
  11.9 3.0 %collective-permute-start = (bf16[40,1024]{1,0:T(8,128)(2,1)S(1)}, bf16[40,1024]{1,0:T(8,128)(2,1)S(1)}, u32[]{:S(2)}, u32[]{:S(2)}) collective-permute-start(bf16[40,1024]{1,0:T(8,128)(2,1)S(1)} %get-tuple-element.42), channel_id=1, source_target_pairs={{0,12},{4,8},{8,4},{12,0},{1,13},{5,9},{9,5},{13,1},{2,14},{6,10},... | collective-permute-start | bytes 245768 | tf_op jit(solution)/shard_map/ppermute | solution.py:316
  15.5 1.4 %shard_map.88 = (bf16[2,80,768]{2,1,0:T(8,128)(2,1)S(1)}, bf16[160,80]{1,0:T(8,128)(2,1)S(1)}, bf16[80,1024]{1,0:T(8,128)(2,1)S(1)}) custom-call(bf16[40,1024]{1,0:T(8,128)(2,1)S(1)} %collective-permute-done.3.refs_0_, bf16[40,1024]{1,0:T(8,128)(2,1)S(1)} %collective-permute-done.4.refs_1_, bf16[80,1024]{1,0:T(8,128)(2,1)S(1)} %collective-permute-done.2.refs_2_, ...), custom_call_target="tpu_custom_call" | custom-call | flops 503316480 | bytes 3145728 | tf_op jit(solution)/shard_map/pallas_call | solution.py:69
  17.0 1.1 %shard_map.90.mine = bf16[2,80,768]{2,1,0:T(8,128)(2,1)S(1)} custom-call(bf16[80,1024]{1,0:T(8,128)(2,1)S(1)} %get-tuple-element.53.rows_in, bf16[3,768,1024]{2,1,0:T(8,128)(2,1)S(1)} %get-tuple-element.51.refs_5_.held), custom_call_target="tpu_custom_call" | custom-call | flops 25165824000 | bytes 314572800 | tf_op jit(solution)/shard_map/pallas_call | solution.py:69
  18.6 1.7 %collective-permute-start.8 = (bf16[2,80,768]{2,1,0:T(8,128)(2,1)S(1)}, bf16[2,80,768]{2,1,0:T(8,128)(2,1)S(1)}, u32[]{:S(2)}, u32[]{:S(2)}) collective-permute-start(bf16[2,80,768]{2,1,0:T(8,128)(2,1)S(1)} %get-tuple-element.55.refs_6_), channel_id=1, source_target_pairs={{0,2},{1,3},{2,0},{3,1},{4,6},{5,7},{6,4},{7,5},{8,10},{9,11},{10,... | collective-permute-start | bytes 737288 | tf_op jit(solution)/shard_map/ppermute | solution.py:316
  20.3 1.7 %collective-permute-done.1.refs_1_ = bf16[40,1024]{1,0:T(8,128)(2,1)S(1)} collective-permute-done((bf16[40,1024]{1,0:T(8,128)(2,1)S(1)}, bf16[40,1024]{1,0:T(8,128)(2,1)S(1)}, u32[]{:S(2)}, u32[]{:S(2)}) %collective-permute-start.1) | collective-permute-done | bytes 81952 | tf_op jit(solution)/shard_map/ppermute | solution.py:316
  22.1 0.7 %shard_map.92 = bf16[80,768]{1,0:T(8,128)(2,1)S(1)} custom-call(bf16[40,1024]{1,0:T(8,128)(2,1)S(1)} %collective-permute-done.refs_0_, bf16[40,1024]{1,0:T(8,128)(2,1)S(1)} %collective-permute-done.1.refs_1_, bf16[80,1024]{1,0:T(8,128)(2,1)S(1)} %collective-permute-done.2.refs_2_, bf16[40,1024]{1,0:T(8,128)(2,1)S(1)} %get-tuple-element.45.refs_3_, ...), custom_call_target="tpu_custom_call" | custom-call | flops 251658240 | bytes 3145728 | tf_op jit(solution)/shard_map/pallas_call | solution.py:69
  22.8 0.7 %shard_map.89 = (bf16[80,1024]{1,0:T(8,128)(2,1)S(1)}, bf16[80,768]{1,0:T(8,128)(2,1)S(1)}) custom-call(bf16[40,1024]{1,0:T(8,128)(2,1)S(1)} %collective-permute-done.refs_0_, bf16[40,1024]{1,0:T(8,128)(2,1)S(1)} %collective-permute-done.1.refs_1_, bf16[80,1024]{1,0:T(8,128)(2,1)S(1)} %collective-permute-done.2.refs_2_, ...), custom_call_target="tpu_custom_call" | custom-call | flops 25165824000 | bytes 314572800 | tf_op jit(solution)/shard_map/pallas_call | solution.py:69
  23.5 0.6 %collective-permute-done.6 = bf16[80,768]{1,0:T(8,128)(2,1)S(1)} collective-permute-done((bf16[80,768]{1,0:T(8,128)(2,1)S(1)}, bf16[80,768]{1,0:T(8,128)(2,1)S(1)}, u32[]{:S(2)}, u32[]{:S(2)}) %collective-permute-start.6) | collective-permute-done | bytes 122912 | tf_op jit(solution)/shard_map/ppermute | solution.py:316
  24.2 1.6 %collective-permute-start.7 = (bf16[80,768]{1,0:T(8,128)(2,1)S(1)}, bf16[80,768]{1,0:T(8,128)(2,1)S(1)}, u32[]{:S(2)}, u32[]{:S(2)}) collective-permute-start(bf16[80,768]{1,0:T(8,128)(2,1)S(1)} %get-tuple-element.67), channel_id=1, source_target_pairs={{0,2},{1,3},{2,0},{3,1},{4,6},{5,7},{6,4},{7,5},{8,10},{9,11},{10,... | collective-permute-start | bytes 368648 | tf_op jit(solution)/shard_map/ppermute | solution.py:316
  25.7 0.9 %collective-permute-done.8.pair_far = bf16[2,80,768]{2,1,0:T(8,128)(2,1)S(1)} collective-permute-done((bf16[2,80,768]{2,1,0:T(8,128)(2,1)S(1)}, bf16[2,80,768]{2,1,0:T(8,128)(2,1)S(1)}, u32[]{:S(2)}, u32[]{:S(2)}) %collective-permute-start.8) | collective-permute-done | bytes 245792 | tf_op jit(solution)/shard_map/ppermute | solution.py:316
  26.9 2.8 %collective-permute-done.7.act_far = bf16[80,768]{1,0:T(8,128)(2,1)S(1)} collective-permute-done((bf16[80,768]{1,0:T(8,128)(2,1)S(1)}, bf16[80,768]{1,0:T(8,128)(2,1)S(1)}, u32[]{:S(2)}, u32[]{:S(2)}) %collective-permute-start.7) | collective-permute-done | bytes 122912 | tf_op jit(solution)/shard_map/ppermute | solution.py:316
  29.8 0.7 %shard_map.95.total = f32[80,1024]{1,0:T(8,128)S(1)} custom-call(bf16[2,80,768]{2,1,0:T(8,128)(2,1)S(1)} %shard_map.94.mine, bf16[3,768,1024]{2,1,0:T(8,128)(2,1)S(1)} %get-tuple-element.51.refs_5_.held), custom_call_target="tpu_custom_call" | custom-call | flops 251658240 | bytes 3145728 | tf_op jit(solution)/shard_map/pallas_call | solution.py:69
  30.4 0.8 %collective-permute-done.10.other = bf16[2,80,768]{2,1,0:T(8,128)(2,1)S(1)} collective-permute-done((bf16[2,80,768]{2,1,0:T(8,128)(2,1)S(1)}, bf16[2,80,768]{2,1,0:T(8,128)(2,1)S(1)}, u32[]{:S(2)}, u32[]{:S(2)}) %collective-permute-start.10) | collective-permute-done | bytes 245792 | tf_op jit(solution)/shard_map/ppermute | solution.py:316
  31.3 0.9 %shard_map.96 = (bf16[40,1024]{1,0:T(8,128)(2,1)S(1)}, bf16[40,1024]{1,0:T(8,128)(2,1)S(1)}, bf16[40,1024]{1,0:T(8,128)(2,1)S(1)}, bf16[40,1024]{1,0:T(8,128)(2,1)S(1)}) custom-call(f32[80,1024]{1,0:T(8,128)S(1)} %shard_map.95.total, bf16[2,80,768]{2,1,0:T(8,128)(2,1)S(1)} %collective-permute-done.10.other, ...), custom_call_target="tpu_custom_call" | custom-call | flops 251658240 | bytes 3145728 | tf_op jit(solution)/shard_map/pallas_call | solution.py:69
  32.2 2.1 %collective-permute-start.11 = (bf16[40,1024]{1,0:T(8,128)(2,1)S(1)}, bf16[40,1024]{1,0:T(8,128)(2,1)S(1)}, u32[]{:S(2)}, u32[]{:S(2)}) collective-permute-start(bf16[40,1024]{1,0:T(8,128)(2,1)S(1)} %get-tuple-element.60), channel_id=1, source_target_pairs={{0,8},{8,4},{4,12},{12,0},{1,9},{9,5},{5,13},{13,1},{2,10},{10,6},... | collective-permute-start | bytes 245768 | tf_op jit(solution)/shard_map/ppermute | solution.py:309
  34.2 1.8 %collective-permute-start.12 = (bf16[40,1024]{1,0:T(8,128)(2,1)S(1)}, bf16[40,1024]{1,0:T(8,128)(2,1)S(1)}, u32[]{:S(2)}, u32[]{:S(2)}) collective-permute-start(bf16[40,1024]{1,0:T(8,128)(2,1)S(1)} %get-tuple-element.61), channel_id=1, source_target_pairs={{0,12},{8,0},{4,8},{12,4},{1,13},{9,1},{5,9},{13,5},{2,14},{10,2},... | collective-permute-start | bytes 245768 | tf_op jit(solution)/shard_map/ppermute | solution.py:309
  36.0 0.5 %collective-permute-start.13 = (bf16[40,1024]{1,0:T(8,128)(2,1)S(1)}, bf16[40,1024]{1,0:T(8,128)(2,1)S(1)}, u32[]{:S(2)}, u32[]{:S(2)}) collective-permute-start(bf16[40,1024]{1,0:T(8,128)(2,1)S(1)} %get-tuple-element.62), channel_id=1, source_target_pairs={{0,4},{8,12},{4,0},{12,8},{1,5},{9,13},{5,1},{13,9},{2,6},{10,14},... | collective-permute-start | bytes 245768 | tf_op jit(solution)/shard_map/ppermute | solution.py:309
  36.5 4.1 %shard_map.98 = (bf16[1,2,1536,1024]{3,2,1,0:T(8,128)(2,1)}, bf16[1,1536,1024]{2,1,0:T(8,128)(2,1)}) custom-call(bf16[80,768]{1,0:T(8,128)(2,1)S(1)} %get-tuple-element.59.mine_act, bf16[80,768]{1,0:T(8,128)(2,1)S(1)} %collective-permute-done.9._.other_act, bf16[2,80,768]{2,1,0:T(8,128)(2,1)S(1)} %shard_map.94.mine, ...), custom_call_target="tpu_custom_call" | custom-call | flops 754974720 | bytes 9437184 | tf_op jit(solution)/shard_map/pallas_call | solution.py:69
  40.6 1.6 %collective-permute-done.12.refs_1_ = bf16[40,1024]{1,0:T(8,128)(2,1)S(1)} collective-permute-done((bf16[40,1024]{1,0:T(8,128)(2,1)S(1)}, bf16[40,1024]{1,0:T(8,128)(2,1)S(1)}, u32[]{:S(2)}, u32[]{:S(2)}) %collective-permute-start.12) | collective-permute-done | bytes 81952 | tf_op jit(solution)/shard_map/ppermute | solution.py:309
  42.3 1.1 %shard_map.97 = bf16[256,1024]{1,0:T(8,128)(2,1)} custom-call(bf16[160,256]{1,0:T(8,128)(2,1)S(1)} %get-tuple-element.35.pick, bf16[40,1024]{1,0:T(8,128)(2,1)S(1)} %collective-permute-done.11.refs_0_, bf16[40,1024]{1,0:T(8,128)(2,1)S(1)} %collective-permute-done.12.refs_1_, bf16[40,1024]{1,0:T(8,128)(2,1)S(1)} %collective-permute-done.13.refs_2_, ...), custom_call_target="tpu_custom_call" | custom-call | flops 83886080 | bytes 1048576 | tf_op jit(solution)/shard_map/pallas_call | solution.py:69
  (19 shorter events, 2.1 us)
Async XLA Ops:
  2.1 13.1 %collective-permute-start.3 = (bf16[40,1024]{1,0:T(8,128)(2,1)S(1)}, bf16[40,1024]{1,0:T(8,128)(2,1)S(1)}, u32[]{:S(2)}, u32[]{:S(2)}) collective-permute-start(bf16[40,1024]{1,0:T(8,128)(2,1)S(1)} %get-tuple-element.46), channel_id=1, source_target_pairs={{0,8},{4,12},{8,0},{12,4},{1,9},{5,13},{9,1},{13,5},{2,10},{6,14},... | collective-permute-start | bytes 245768 | tf_op jit(solution)/shard_map/ppermute | solution.py:316
  6.2 9.0 %collective-permute-start.4 = (bf16[40,1024]{1,0:T(8,128)(2,1)S(1)}, bf16[40,1024]{1,0:T(8,128)(2,1)S(1)}, u32[]{:S(2)}, u32[]{:S(2)}) collective-permute-start(bf16[40,1024]{1,0:T(8,128)(2,1)S(1)} %get-tuple-element.47), channel_id=1, source_target_pairs={{0,12},{4,8},{8,4},{12,0},{1,13},{5,9},{9,5},{13,1},{2,14},{6,10},... | collective-permute-start | bytes 245768 | tf_op jit(solution)/shard_map/ppermute | solution.py:316
  7.8 7.7 %collective-permute-start.2 = (bf16[80,1024]{1,0:T(8,128)(2,1)S(1)}, bf16[80,1024]{1,0:T(8,128)(2,1)S(1)}, u32[]{:S(2)}, u32[]{:S(2)}) collective-permute-start(bf16[80,1024]{1,0:T(8,128)(2,1)S(1)} %get-tuple-element.44), channel_id=1, source_target_pairs={{0,4},{4,0},{8,12},{12,8},{1,5},{5,1},{9,13},{13,9},{2,6},{6,2},{1... | collective-permute-start | bytes 491528 | tf_op jit(solution)/shard_map/ppermute | solution.py:316
  11.9 8.4 %collective-permute-start = (bf16[40,1024]{1,0:T(8,128)(2,1)S(1)}, bf16[40,1024]{1,0:T(8,128)(2,1)S(1)}, u32[]{:S(2)}, u32[]{:S(2)}) collective-permute-start(bf16[40,1024]{1,0:T(8,128)(2,1)S(1)} %get-tuple-element.42), channel_id=1, source_target_pairs={{0,12},{4,8},{8,4},{12,0},{1,13},{5,9},{9,5},{13,1},{2,14},{6,10},... | collective-permute-start | bytes 245768 | tf_op jit(solution)/shard_map/ppermute | solution.py:316
  14.9 7.1 %collective-permute-start.1 = (bf16[40,1024]{1,0:T(8,128)(2,1)S(1)}, bf16[40,1024]{1,0:T(8,128)(2,1)S(1)}, u32[]{:S(2)}, u32[]{:S(2)}) collective-permute-start(bf16[40,1024]{1,0:T(8,128)(2,1)S(1)} %get-tuple-element.43), channel_id=1, source_target_pairs={{0,8},{4,12},{8,0},{12,4},{1,9},{5,13},{9,1},{13,5},{2,10},{6,14},... | collective-permute-start | bytes 245768 | tf_op jit(solution)/shard_map/ppermute | solution.py:316
  16.9 1.6 %collective-permute-start.5 = (bf16[2,80,768]{2,1,0:T(8,128)(2,1)S(1)}, bf16[2,80,768]{2,1,0:T(8,128)(2,1)S(1)}, u32[]{:S(2)}, u32[]{:S(2)}) collective-permute-start(bf16[2,80,768]{2,1,0:T(8,128)(2,1)S(1)} %get-tuple-element.54), channel_id=1, source_target_pairs={{0,1},{1,0},{2,3},{3,2},{4,5},{5,4},{6,7},{7,6},{8,9},{9,8},{10,11... | collective-permute-start | bytes 737288 | tf_op jit(solution)/shard_map/ppermute | solution.py:316
  18.6 8.1 %collective-permute-start.8 = (bf16[2,80,768]{2,1,0:T(8,128)(2,1)S(1)}, bf16[2,80,768]{2,1,0:T(8,128)(2,1)S(1)}, u32[]{:S(2)}, u32[]{:S(2)}) collective-permute-start(bf16[2,80,768]{2,1,0:T(8,128)(2,1)S(1)} %get-tuple-element.55.refs_6_), channel_id=1, source_target_pairs={{0,2},{1,3},{2,0},{3,1},{4,6},{5,7},{6,4},{7,5},{8,10},{9,11},{10,... | collective-permute-start | bytes 737288 | tf_op jit(solution)/shard_map/ppermute | solution.py:316
  22.8 1.4 %collective-permute-start.6 = (bf16[80,768]{1,0:T(8,128)(2,1)S(1)}, bf16[80,768]{1,0:T(8,128)(2,1)S(1)}, u32[]{:S(2)}, u32[]{:S(2)}) collective-permute-start(bf16[80,768]{1,0:T(8,128)(2,1)S(1)} %shard_map.92), channel_id=1, source_target_pairs={{0,1},{1,0},{2,3},{3,2},{4,5},{5,4},{6,7},{7,6},{8,9},{9,8},{10,11... | collective-permute-start | bytes 368648 | tf_op jit(solution)/shard_map/ppermute | solution.py:316
  24.2 5.4 %collective-permute-start.7 = (bf16[80,768]{1,0:T(8,128)(2,1)S(1)}, bf16[80,768]{1,0:T(8,128)(2,1)S(1)}, u32[]{:S(2)}, u32[]{:S(2)}) collective-permute-start(bf16[80,768]{1,0:T(8,128)(2,1)S(1)} %get-tuple-element.67), channel_id=1, source_target_pairs={{0,2},{1,3},{2,0},{3,1},{4,6},{5,7},{6,4},{7,5},{8,10},{9,11},{10,... | collective-permute-start | bytes 368648 | tf_op jit(solution)/shard_map/ppermute | solution.py:316
  26.8 2.8 %collective-permute-start.9 = (bf16[80,768]{1,0:T(8,128)(2,1)S(1)}, bf16[80,768]{1,0:T(8,128)(2,1)S(1)}, u32[]{:S(2)}, u32[]{:S(2)}) collective-permute-start(bf16[80,768]{1,0:T(8,128)(2,1)S(1)} %get-tuple-element.59.mine_act), channel_id=1, source_target_pairs={{0,1},{1,0},{2,3},{3,2},{4,5},{5,4},{6,7},{7,6},{8,9},{9,8},{10,11... | collective-permute-start | bytes 368648 | tf_op jit(solution)/shard_map/ppermute | solution.py:316
  29.7 1.6 %collective-permute-start.10 = (bf16[2,80,768]{2,1,0:T(8,128)(2,1)S(1)}, bf16[2,80,768]{2,1,0:T(8,128)(2,1)S(1)}, u32[]{:S(2)}, u32[]{:S(2)}) collective-permute-start(bf16[2,80,768]{2,1,0:T(8,128)(2,1)S(1)} %shard_map.94.mine), channel_id=1, source_target_pairs={{0,1},{1,0},{2,3},{3,2},{4,5},{5,4},{6,7},{7,6},{8,9},{9,8},{10,11... | collective-permute-start | bytes 737288 | tf_op jit(solution)/shard_map/ppermute | solution.py:316
  32.2 8.5 %collective-permute-start.11 = (bf16[40,1024]{1,0:T(8,128)(2,1)S(1)}, bf16[40,1024]{1,0:T(8,128)(2,1)S(1)}, u32[]{:S(2)}, u32[]{:S(2)}) collective-permute-start(bf16[40,1024]{1,0:T(8,128)(2,1)S(1)} %get-tuple-element.60), channel_id=1, source_target_pairs={{0,8},{8,4},{4,12},{12,0},{1,9},{9,5},{5,13},{13,1},{2,10},{10,6},... | collective-permute-start | bytes 245768 | tf_op jit(solution)/shard_map/ppermute | solution.py:309
  34.2 8.0 %collective-permute-start.12 = (bf16[40,1024]{1,0:T(8,128)(2,1)S(1)}, bf16[40,1024]{1,0:T(8,128)(2,1)S(1)}, u32[]{:S(2)}, u32[]{:S(2)}) collective-permute-start(bf16[40,1024]{1,0:T(8,128)(2,1)S(1)} %get-tuple-element.61), channel_id=1, source_target_pairs={{0,12},{8,0},{4,8},{12,4},{1,13},{9,1},{5,9},{13,5},{2,14},{10,2},... | collective-permute-start | bytes 245768 | tf_op jit(solution)/shard_map/ppermute | solution.py:309
  36.0 6.2 %collective-permute-start.13 = (bf16[40,1024]{1,0:T(8,128)(2,1)S(1)}, bf16[40,1024]{1,0:T(8,128)(2,1)S(1)}, u32[]{:S(2)}, u32[]{:S(2)}) collective-permute-start(bf16[40,1024]{1,0:T(8,128)(2,1)S(1)} %get-tuple-element.62), channel_id=1, source_target_pairs={{0,4},{8,12},{4,0},{12,8},{1,5},{9,13},{5,1},{13,9},{2,6},{10,14},... | collective-permute-start | bytes 245768 | tf_op jit(solution)/shard_map/ppermute | solution.py:309

commit v16 on v15

--- a/solution.py
+++ b/solution.py
@@ -14,7 +14,8 @@
 F32 = jnp.float32
 MIB = 1 << 20
 C2COST = 100
-WCOST = 100
+C0COST = 4.75
+WCOST = 1
 GFLOP = 100
 D1COST = 1
 D2COST = 100
@@ -140,6 +141,10 @@
     return pl.ds(pl.multiple_of((core if own else 1 - core) * half, 128), half)
 
 
+def early_rows(first, out):
+    out[...] = first[...]
+
+
 def place_rows(experts, capacity, pieces):
     me = lax.axis_index("ex")
     rows = experts * MOST
@@ -195,8 +200,7 @@
 
 def act_part(experts, own, *refs):
     place, held = refs[experts : experts + 2]
-    pieces = refs[: experts - 2][::-1] + refs[experts - 2 : experts]
-    rows_grad = mm(place[...], stacked(pieces, 1).astype(BF), ROWS).astype(BF)
+    rows_grad = mm(place[...], stacked(refs[:experts], 1).astype(BF), ROWS).astype(BF)
     if own:
         refs[-2][...] = rows_grad
     refs[-1][...] = mm(rows_grad, held[2], LANES).astype(BF)
@@ -365,6 +369,14 @@
     )
     near = swap(near, "ex", 1)
     got_in = [swap(part, "ex", k) for part, k in zip(send_in[:-1], order)] + [near, own_in]
+    got_in[0] = call(
+        early_rows,
+        piece[0],
+        (got_in[0],),
+        [VMEM],
+        flops=int(C0COST * weight_flops),
+        traffic=weight_bytes,
+    )
     held_other, held_mine, *send_grad = call(
         functools.partial(stage, experts - 1),
         [pltpu.VMEM((3, half, width), BF)] * 2 + piece[1:],
@@ -374,7 +386,7 @@
         flops=WCOST * weight_flops,
         traffic=WCOST * weight_bytes,
     )
-    got_grad = [swap(part, "ex", k) for part, k in zip(send_grad[:-1], order)][::-1]
+    got_grad = [swap(part, "ex", k) for part, k in zip(send_grad[:-1], order)]
     got_grad = got_grad + [near, send_grad[-1]]
     pair_other, place, rows_in = call(
         functools.partial(other_pair, experts, capacity),

time: 43.6 us -> 43.7 us (level)
    ppermute x3, waiting for transfers between devices: 1.61 us -> 2.15 us  [shift(): lax.ppermute(value, axis, [(name, names[(at + step) % count]) for at, nam...]
    ppermute x11, starting transfers between devices: 12.6 us -> 13.1 us  [swap(): return lax.ppermute(value, axis, [(i, i ^ bit) for i in range(count)])]
    ppermute x3, starting transfers between devices: 4.35 us -> 3.88 us  [shift(): lax.ppermute(value, axis, [(name, names[(at + step) % count]) for at, nam...]
    pallas_call x14 -> x15, Pallas kernels: 16.4 us -> 16.4 us  [call(): pl.pallas_call(body, out_shape=outs, in_specs=specs, out_specs=out_specs...]
  transfers between devices with their start and end apart: 14 -> 14, of which waited for: 8 -> 7; matrix products, arithmetic and copies ran while one was open for 0% -> 0% of each run, Pallas kernels for 30% -> 30%
where the time goes in v16:
time: 43.7 us; the launch traced here: 43.5 us
  starting transfers between devices  17 us (39%)
  Pallas kernels  16.4 us (38%)
  waiting for transfers between devices  9.26 us (21%)
  between operations  0.77 us (2%)
    pallas_call x15, Pallas kernels, call(): pl.pallas_call(body, out_shape=outs, in_specs=specs, out_specs=out_specs...  16.4 us
    ppermute x11, starting transfers between devices, swap(): return lax.ppermute(value, axis, [(i, i ^ bit) for i in range(count)])  13.1 us
    ppermute x11, waiting for transfers between devices, swap(): return lax.ppermute(value, axis, [(i, i ^ bit) for i in range(count)])  7.11 us
    ppermute x3, starting transfers between devices, shift(): lax.ppermute(value, axis, [(name, names[(at + step) % count]) for at, nam...  3.88 us
    ppermute x3, waiting for transfers between devices, shift(): lax.ppermute(value, axis, [(name, names[(at + step) % count]) for at, nam...  2.15 us
  transfers between devices with their start and end apart: 14, of which 7 were waited for; matrix products, arithmetic and copies ran while one was open for 0% of the time, Pallas kernels for 30%

profile of v16, /device:TPU:0, one launch (start us, length us, event | category | flops | bytes accessed | tf_op | source)
XLA Modules:
  0.0 43.5 jit_solution(18407125130026626646)
XLA Ops:
  0.6 1.5 %shard_map.85 = (bf16[160,256]{1,0:T(8,128)(2,1)S(1)}, f32[160,1]{1,0:T(8,128)S(1)}, bf16[256,1024]{1,0:T(8,128)(2,1)S(1)}, bf16[40,1024]{1,0:T(8,128)(2,1)S(1)}...) custom-call(s32[8,256]{1,0:T(8,128)} %bitcast.2, ...), custom_call_target="tpu_custom_call" | custom-call | flops 83886080 | bytes 1048576 | tf_op jit(solution)/shard_map/pallas_call | solution.py:70
  2.1 4.1 %collective-permute-start.3 = (bf16[40,1024]{1,0:T(8,128)(2,1)S(1)}, bf16[40,1024]{1,0:T(8,128)(2,1)S(1)}, u32[]{:S(2)}, u32[]{:S(2)}) collective-permute-start(bf16[40,1024]{1,0:T(8,128)(2,1)S(1)} %get-tuple-element.46), channel_id=1, source_target_pairs={{0,8},{4,12},{8,0},{12,4},{1,9},{5,13},{9,1},{13,5},{2,10},{6,14},... | collective-permute-start | bytes 245768 | tf_op jit(solution)/shard_map/ppermute | solution.py:320
  6.5 1.6 %collective-permute-start.2 = (bf16[80,1024]{1,0:T(8,128)(2,1)S(1)}, bf16[80,1024]{1,0:T(8,128)(2,1)S(1)}, u32[]{:S(2)}, u32[]{:S(2)}) collective-permute-start(bf16[80,1024]{1,0:T(8,128)(2,1)S(1)} %get-tuple-element.44), channel_id=1, source_target_pairs={{0,4},{4,0},{8,12},{12,8},{1,5},{5,1},{9,13},{13,9},{2,6},{6,2},{1... | collective-permute-start | bytes 491528 | tf_op jit(solution)/shard_map/ppermute | solution.py:320
  8.1 3.8 %shard_map.87 = (bf16[3,768,1024]{2,1,0:T(8,128)(2,1)S(1)}, bf16[3,768,1024]{2,1,0:T(8,128)(2,1)S(1)}, bf16[40,1024]{1,0:T(8,128)(2,1)S(1)}, bf16[40,1024]{1,0:T(8,128)(2,1)S(1)}, bf16[40,1024]{1,0:T(8,128)(2,1)S(1)}) custom-call(bf16[1,2,1536,1024]{3,2,1,0:T(8,128)(2,1)} %gate_up.1, bf16[1,1536,1024]{2,1,0:T(8,128)(2,1)} %down.1, ...), custom_call_target="tpu_custom_call" | custom-call | flops 251658240 | bytes 3145728 | tf_op jit(solution)/shard_map/pallas_call | solution.py:70
  11.9 2.0 %collective-permute-start = (bf16[40,1024]{1,0:T(8,128)(2,1)S(1)}, bf16[40,1024]{1,0:T(8,128)(2,1)S(1)}, u32[]{:S(2)}, u32[]{:S(2)}) collective-permute-start(bf16[40,1024]{1,0:T(8,128)(2,1)S(1)} %get-tuple-element.42), channel_id=1, source_target_pairs={{0,8},{4,12},{8,0},{12,4},{1,9},{5,13},{9,1},{13,5},{2,10},{6,14},... | collective-permute-start | bytes 245768 | tf_op jit(solution)/shard_map/ppermute | solution.py:320
  13.9 2.0 %collective-permute-start.1 = (bf16[40,1024]{1,0:T(8,128)(2,1)S(1)}, bf16[40,1024]{1,0:T(8,128)(2,1)S(1)}, u32[]{:S(2)}, u32[]{:S(2)}) collective-permute-start(bf16[40,1024]{1,0:T(8,128)(2,1)S(1)} %get-tuple-element.43), channel_id=1, source_target_pairs={{0,12},{4,8},{8,4},{12,0},{1,13},{5,9},{9,5},{13,1},{2,14},{6,10},... | collective-permute-start | bytes 245768 | tf_op jit(solution)/shard_map/ppermute | solution.py:320
  15.9 1.4 %shard_map.89 = (bf16[2,80,768]{2,1,0:T(8,128)(2,1)S(1)}, bf16[160,80]{1,0:T(8,128)(2,1)S(1)}, bf16[80,1024]{1,0:T(8,128)(2,1)S(1)}) custom-call(bf16[40,1024]{1,0:T(8,128)(2,1)S(1)} %shard_map.88.refs_0_, bf16[40,1024]{1,0:T(8,128)(2,1)S(1)} %collective-permute-done.4.refs_1_, bf16[80,1024]{1,0:T(8,128)(2,1)S(1)} %collective-permute-done.2.refs_2_, ...), custom_call_target="tpu_custom_call" | custom-call | flops 503316480 | bytes 3145728 | tf_op jit(solution)/shard_map/pallas_call | solution.py:70
  17.5 1.1 %shard_map.91.mine = bf16[2,80,768]{2,1,0:T(8,128)(2,1)S(1)} custom-call(bf16[80,1024]{1,0:T(8,128)(2,1)S(1)} %get-tuple-element.53.rows_in, bf16[3,768,1024]{2,1,0:T(8,128)(2,1)S(1)} %get-tuple-element.51.refs_5_.held), custom_call_target="tpu_custom_call" | custom-call | flops 25165824000 | bytes 314572800 | tf_op jit(solution)/shard_map/pallas_call | solution.py:70
  18.5 0.4 collective-permute-done.5.other
  19.0 1.6 %collective-permute-start.8 = (bf16[2,80,768]{2,1,0:T(8,128)(2,1)S(1)}, bf16[2,80,768]{2,1,0:T(8,128)(2,1)S(1)}, u32[]{:S(2)}, u32[]{:S(2)}) collective-permute-start(bf16[2,80,768]{2,1,0:T(8,128)(2,1)S(1)} %get-tuple-element.55.refs_6_), channel_id=1, source_target_pairs={{0,2},{1,3},{2,0},{3,1},{4,6},{5,7},{6,4},{7,5},{8,10},{9,11},{10,... | collective-permute-start | bytes 737288 | tf_op jit(solution)/shard_map/ppermute | solution.py:320
  20.9 0.7 %shard_map.93 = bf16[80,768]{1,0:T(8,128)(2,1)S(1)} custom-call(bf16[40,1024]{1,0:T(8,128)(2,1)S(1)} %collective-permute-done.refs_0_, bf16[40,1024]{1,0:T(8,128)(2,1)S(1)} %collective-permute-done.1.refs_1_, bf16[80,1024]{1,0:T(8,128)(2,1)S(1)} %collective-permute-done.2.refs_2_, bf16[40,1024]{1,0:T(8,128)(2,1)S(1)} %get-tuple-element.45.refs_3_, ...), custom_call_target="tpu_custom_call" | custom-call | flops 251658240 | bytes 3145728 | tf_op jit(solution)/shard_map/pallas_call | solution.py:70
  21.6 0.7 %shard_map.90 = (bf16[80,1024]{1,0:T(8,128)(2,1)S(1)}, bf16[80,768]{1,0:T(8,128)(2,1)S(1)}) custom-call(bf16[40,1024]{1,0:T(8,128)(2,1)S(1)} %collective-permute-done.refs_0_, bf16[40,1024]{1,0:T(8,128)(2,1)S(1)} %collective-permute-done.1.refs_1_, bf16[80,1024]{1,0:T(8,128)(2,1)S(1)} %collective-permute-done.2.refs_2_, ...), custom_call_target="tpu_custom_call" | custom-call | flops 25165824000 | bytes 314572800 | tf_op jit(solution)/shard_map/pallas_call | solution.py:70
  22.3 0.6 %collective-permute-done.6 = bf16[80,768]{1,0:T(8,128)(2,1)S(1)} collective-permute-done((bf16[80,768]{1,0:T(8,128)(2,1)S(1)}, bf16[80,768]{1,0:T(8,128)(2,1)S(1)}, u32[]{:S(2)}, u32[]{:S(2)}) %collective-permute-start.6) | collective-permute-done | bytes 122912 | tf_op jit(solution)/shard_map/ppermute | solution.py:320
  23.0 1.6 %collective-permute-start.7 = (bf16[80,768]{1,0:T(8,128)(2,1)S(1)}, bf16[80,768]{1,0:T(8,128)(2,1)S(1)}, u32[]{:S(2)}, u32[]{:S(2)}) collective-permute-start(bf16[80,768]{1,0:T(8,128)(2,1)S(1)} %get-tuple-element.67), channel_id=1, source_target_pairs={{0,2},{1,3},{2,0},{3,1},{4,6},{5,7},{6,4},{7,5},{8,10},{9,11},{10,... | collective-permute-start | bytes 368648 | tf_op jit(solution)/shard_map/ppermute | solution.py:320
  24.6 3.3 %collective-permute-done.8.pair_far = bf16[2,80,768]{2,1,0:T(8,128)(2,1)S(1)} collective-permute-done((bf16[2,80,768]{2,1,0:T(8,128)(2,1)S(1)}, bf16[2,80,768]{2,1,0:T(8,128)(2,1)S(1)}, u32[]{:S(2)}, u32[]{:S(2)}) %collective-permute-start.8) | collective-permute-done | bytes 245792 | tf_op jit(solution)/shard_map/ppermute | solution.py:320
  28.1 1.6 %collective-permute-done.7.act_far = bf16[80,768]{1,0:T(8,128)(2,1)S(1)} collective-permute-done((bf16[80,768]{1,0:T(8,128)(2,1)S(1)}, bf16[80,768]{1,0:T(8,128)(2,1)S(1)}, u32[]{:S(2)}, u32[]{:S(2)}) %collective-permute-start.7) | collective-permute-done | bytes 122912 | tf_op jit(solution)/shard_map/ppermute | solution.py:320
  29.9 0.7 %shard_map.96.total = f32[80,1024]{1,0:T(8,128)S(1)} custom-call(bf16[2,80,768]{2,1,0:T(8,128)(2,1)S(1)} %shard_map.95.mine, bf16[3,768,1024]{2,1,0:T(8,128)(2,1)S(1)} %get-tuple-element.51.refs_5_.held), custom_call_target="tpu_custom_call" | custom-call | flops 251658240 | bytes 3145728 | tf_op jit(solution)/shard_map/pallas_call | solution.py:70
  30.5 0.8 %collective-permute-done.10.other = bf16[2,80,768]{2,1,0:T(8,128)(2,1)S(1)} collective-permute-done((bf16[2,80,768]{2,1,0:T(8,128)(2,1)S(1)}, bf16[2,80,768]{2,1,0:T(8,128)(2,1)S(1)}, u32[]{:S(2)}, u32[]{:S(2)}) %collective-permute-start.10) | collective-permute-done | bytes 245792 | tf_op jit(solution)/shard_map/ppermute | solution.py:320
  31.4 0.9 %shard_map.97 = (bf16[40,1024]{1,0:T(8,128)(2,1)S(1)}, bf16[40,1024]{1,0:T(8,128)(2,1)S(1)}, bf16[40,1024]{1,0:T(8,128)(2,1)S(1)}, bf16[40,1024]{1,0:T(8,128)(2,1)S(1)}) custom-call(f32[80,1024]{1,0:T(8,128)S(1)} %shard_map.96.total, bf16[2,80,768]{2,1,0:T(8,128)(2,1)S(1)} %collective-permute-done.10.other, ...), custom_call_target="tpu_custom_call" | custom-call | flops 251658240 | bytes 3145728 | tf_op jit(solution)/shard_map/pallas_call | solution.py:70
  32.3 2.0 %collective-permute-start.11 = (bf16[40,1024]{1,0:T(8,128)(2,1)S(1)}, bf16[40,1024]{1,0:T(8,128)(2,1)S(1)}, u32[]{:S(2)}, u32[]{:S(2)}) collective-permute-start(bf16[40,1024]{1,0:T(8,128)(2,1)S(1)} %get-tuple-element.60), channel_id=1, source_target_pairs={{0,8},{8,4},{4,12},{12,0},{1,9},{9,5},{5,13},{13,1},{2,10},{10,6},... | collective-permute-start | bytes 245768 | tf_op jit(solution)/shard_map/ppermute | solution.py:313
  34.3 1.9 %collective-permute-start.12 = (bf16[40,1024]{1,0:T(8,128)(2,1)S(1)}, bf16[40,1024]{1,0:T(8,128)(2,1)S(1)}, u32[]{:S(2)}, u32[]{:S(2)}) collective-permute-start(bf16[40,1024]{1,0:T(8,128)(2,1)S(1)} %get-tuple-element.61), channel_id=1, source_target_pairs={{0,12},{8,0},{4,8},{12,4},{1,13},{9,1},{5,9},{13,5},{2,14},{10,2},... | collective-permute-start | bytes 245768 | tf_op jit(solution)/shard_map/ppermute | solution.py:313
  36.1 4.1 %shard_map.99 = (bf16[1,2,1536,1024]{3,2,1,0:T(8,128)(2,1)}, bf16[1,1536,1024]{2,1,0:T(8,128)(2,1)}) custom-call(bf16[80,768]{1,0:T(8,128)(2,1)S(1)} %get-tuple-element.59.mine_act, bf16[80,768]{1,0:T(8,128)(2,1)S(1)} %collective-permute-done.9._.other_act, bf16[2,80,768]{2,1,0:T(8,128)(2,1)S(1)} %shard_map.95.mine, ...), custom_call_target="tpu_custom_call" | custom-call | flops 754974720 | bytes 9437184 | tf_op jit(solution)/shard_map/pallas_call | solution.py:70
  40.3 2.1 %collective-permute-done.12.refs_1_ = bf16[40,1024]{1,0:T(8,128)(2,1)S(1)} collective-permute-done((bf16[40,1024]{1,0:T(8,128)(2,1)S(1)}, bf16[40,1024]{1,0:T(8,128)(2,1)S(1)}, u32[]{:S(2)}, u32[]{:S(2)}) %collective-permute-start.12) | collective-permute-done | bytes 81952 | tf_op jit(solution)/shard_map/ppermute | solution.py:313
  42.4 1.1 %shard_map.98 = bf16[256,1024]{1,0:T(8,128)(2,1)} custom-call(bf16[160,256]{1,0:T(8,128)(2,1)S(1)} %get-tuple-element.35.pick, bf16[40,1024]{1,0:T(8,128)(2,1)S(1)} %collective-permute-done.11.refs_0_, bf16[40,1024]{1,0:T(8,128)(2,1)S(1)} %collective-permute-done.12.refs_1_, bf16[40,1024]{1,0:T(8,128)(2,1)S(1)} %collective-permute-done.13.refs_2_, ...), custom_call_target="tpu_custom_call" | custom-call | flops 83886080 | bytes 1048576 | tf_op jit(solution)/shard_map/pallas_call | solution.py:70
  (20 shorter events, 1.2 us)
Async XLA Ops:
  2.1 13.8 %collective-permute-start.3 = (bf16[40,1024]{1,0:T(8,128)(2,1)S(1)}, bf16[40,1024]{1,0:T(8,128)(2,1)S(1)}, u32[]{:S(2)}, u32[]{:S(2)}) collective-permute-start(bf16[40,1024]{1,0:T(8,128)(2,1)S(1)} %get-tuple-element.46), channel_id=1, source_target_pairs={{0,8},{4,12},{8,0},{12,4},{1,9},{5,13},{9,1},{13,5},{2,10},{6,14},... | collective-permute-start | bytes 245768 | tf_op jit(solution)/shard_map/ppermute | solution.py:320
  6.5 9.4 %collective-permute-start.2 = (bf16[80,1024]{1,0:T(8,128)(2,1)S(1)}, bf16[80,1024]{1,0:T(8,128)(2,1)S(1)}, u32[]{:S(2)}, u32[]{:S(2)}) collective-permute-start(bf16[80,1024]{1,0:T(8,128)(2,1)S(1)} %get-tuple-element.44), channel_id=1, source_target_pairs={{0,4},{4,0},{8,12},{12,8},{1,5},{5,1},{9,13},{13,9},{2,6},{6,2},{1... | collective-permute-start | bytes 491528 | tf_op jit(solution)/shard_map/ppermute | solution.py:320
  8.1 7.8 %collective-permute-start.4 = (bf16[40,1024]{1,0:T(8,128)(2,1)S(1)}, bf16[40,1024]{1,0:T(8,128)(2,1)S(1)}, u32[]{:S(2)}, u32[]{:S(2)}) collective-permute-start(bf16[40,1024]{1,0:T(8,128)(2,1)S(1)} %get-tuple-element.47), channel_id=1, source_target_pairs={{0,12},{4,8},{8,4},{12,0},{1,13},{5,9},{9,5},{13,1},{2,14},{6,10},... | collective-permute-start | bytes 245768 | tf_op jit(solution)/shard_map/ppermute | solution.py:320
  11.9 8.9 %collective-permute-start = (bf16[40,1024]{1,0:T(8,128)(2,1)S(1)}, bf16[40,1024]{1,0:T(8,128)(2,1)S(1)}, u32[]{:S(2)}, u32[]{:S(2)}) collective-permute-start(bf16[40,1024]{1,0:T(8,128)(2,1)S(1)} %get-tuple-element.42), channel_id=1, source_target_pairs={{0,8},{4,12},{8,0},{12,4},{1,9},{5,13},{9,1},{13,5},{2,10},{6,14},... | collective-permute-start | bytes 245768 | tf_op jit(solution)/shard_map/ppermute | solution.py:320
  13.9 7.0 %collective-permute-start.1 = (bf16[40,1024]{1,0:T(8,128)(2,1)S(1)}, bf16[40,1024]{1,0:T(8,128)(2,1)S(1)}, u32[]{:S(2)}, u32[]{:S(2)}) collective-permute-start(bf16[40,1024]{1,0:T(8,128)(2,1)S(1)} %get-tuple-element.43), channel_id=1, source_target_pairs={{0,12},{4,8},{8,4},{12,0},{1,13},{5,9},{9,5},{13,1},{2,14},{6,10},... | collective-permute-start | bytes 245768 | tf_op jit(solution)/shard_map/ppermute | solution.py:320
  17.4 1.6 %collective-permute-start.5 = (bf16[2,80,768]{2,1,0:T(8,128)(2,1)S(1)}, bf16[2,80,768]{2,1,0:T(8,128)(2,1)S(1)}, u32[]{:S(2)}, u32[]{:S(2)}) collective-permute-start(bf16[2,80,768]{2,1,0:T(8,128)(2,1)S(1)} %get-tuple-element.54), channel_id=1, source_target_pairs={{0,1},{1,0},{2,3},{3,2},{4,5},{5,4},{6,7},{7,6},{8,9},{9,8},{10,11... | collective-permute-start | bytes 737288 | tf_op jit(solution)/shard_map/ppermute | solution.py:320
  19.0 8.9 %collective-permute-start.8 = (bf16[2,80,768]{2,1,0:T(8,128)(2,1)S(1)}, bf16[2,80,768]{2,1,0:T(8,128)(2,1)S(1)}, u32[]{:S(2)}, u32[]{:S(2)}) collective-permute-start(bf16[2,80,768]{2,1,0:T(8,128)(2,1)S(1)} %get-tuple-element.55.refs_6_), channel_id=1, source_target_pairs={{0,2},{1,3},{2,0},{3,1},{4,6},{5,7},{6,4},{7,5},{8,10},{9,11},{10,... | collective-permute-start | bytes 737288 | tf_op jit(solution)/shard_map/ppermute | solution.py:320
  21.6 1.4 %collective-permute-start.6 = (bf16[80,768]{1,0:T(8,128)(2,1)S(1)}, bf16[80,768]{1,0:T(8,128)(2,1)S(1)}, u32[]{:S(2)}, u32[]{:S(2)}) collective-permute-start(bf16[80,768]{1,0:T(8,128)(2,1)S(1)} %shard_map.93), channel_id=1, source_target_pairs={{0,1},{1,0},{2,3},{3,2},{4,5},{5,4},{6,7},{7,6},{8,9},{9,8},{10,11... | collective-permute-start | bytes 368648 | tf_op jit(solution)/shard_map/ppermute | solution.py:320
  23.0 6.7 %collective-permute-start.7 = (bf16[80,768]{1,0:T(8,128)(2,1)S(1)}, bf16[80,768]{1,0:T(8,128)(2,1)S(1)}, u32[]{:S(2)}, u32[]{:S(2)}) collective-permute-start(bf16[80,768]{1,0:T(8,128)(2,1)S(1)} %get-tuple-element.67), channel_id=1, source_target_pairs={{0,2},{1,3},{2,0},{3,1},{4,6},{5,7},{6,4},{7,5},{8,10},{9,11},{10,... | collective-permute-start | bytes 368648 | tf_op jit(solution)/shard_map/ppermute | solution.py:320
  28.0 1.7 %collective-permute-start.9 = (bf16[80,768]{1,0:T(8,128)(2,1)S(1)}, bf16[80,768]{1,0:T(8,128)(2,1)S(1)}, u32[]{:S(2)}, u32[]{:S(2)}) collective-permute-start(bf16[80,768]{1,0:T(8,128)(2,1)S(1)} %get-tuple-element.59.mine_act), channel_id=1, source_target_pairs={{0,1},{1,0},{2,3},{3,2},{4,5},{5,4},{6,7},{7,6},{8,9},{9,8},{10,11... | collective-permute-start | bytes 368648 | tf_op jit(solution)/shard_map/ppermute | solution.py:320
  29.8 1.6 %collective-permute-start.10 = (bf16[2,80,768]{2,1,0:T(8,128)(2,1)S(1)}, bf16[2,80,768]{2,1,0:T(8,128)(2,1)S(1)}, u32[]{:S(2)}, u32[]{:S(2)}) collective-permute-start(bf16[2,80,768]{2,1,0:T(8,128)(2,1)S(1)} %shard_map.95.mine), channel_id=1, source_target_pairs={{0,1},{1,0},{2,3},{3,2},{4,5},{5,4},{6,7},{7,6},{8,9},{9,8},{10,11... | collective-permute-start | bytes 737288 | tf_op jit(solution)/shard_map/ppermute | solution.py:320
  32.3 8.0 %collective-permute-start.11 = (bf16[40,1024]{1,0:T(8,128)(2,1)S(1)}, bf16[40,1024]{1,0:T(8,128)(2,1)S(1)}, u32[]{:S(2)}, u32[]{:S(2)}) collective-permute-start(bf16[40,1024]{1,0:T(8,128)(2,1)S(1)} %get-tuple-element.60), channel_id=1, source_target_pairs={{0,8},{8,4},{4,12},{12,0},{1,9},{9,5},{5,13},{13,1},{2,10},{10,6},... | collective-permute-start | bytes 245768 | tf_op jit(solution)/shard_map/ppermute | solution.py:313
  34.3 8.1 %collective-permute-start.12 = (bf16[40,1024]{1,0:T(8,128)(2,1)S(1)}, bf16[40,1024]{1,0:T(8,128)(2,1)S(1)}, u32[]{:S(2)}, u32[]{:S(2)}) collective-permute-start(bf16[40,1024]{1,0:T(8,128)(2,1)S(1)} %get-tuple-element.61), channel_id=1, source_target_pairs={{0,12},{8,0},{4,8},{12,4},{1,13},{9,1},{5,9},{13,5},{2,14},{10,2},... | collective-permute-start | bytes 245768 | tf_op jit(solution)/shard_map/ppermute | solution.py:313
  36.1 6.3 %collective-permute-start.13 = (bf16[40,1024]{1,0:T(8,128)(2,1)S(1)}, bf16[40,1024]{1,0:T(8,128)(2,1)S(1)}, u32[]{:S(2)}, u32[]{:S(2)}) collective-permute-start(bf16[40,1024]{1,0:T(8,128)(2,1)S(1)} %get-tuple-element.62), channel_id=1, source_target_pairs={{0,4},{8,12},{4,0},{12,8},{1,5},{9,13},{5,1},{13,9},{2,6},{10,14},... | collective-permute-start | bytes 245768 | tf_op jit(solution)/shard_map/ppermute | solution.py:313

commit v17 on v16

--- a/solution.py
+++ b/solution.py
@@ -227,11 +227,15 @@
 
 
 def other_rows(experts, total, other, place, held, *refs):
-    pieces, whole = refs[:experts], refs[experts]
+    *pieces, whole = refs
     rows = total[...] + mm(other[0], held[0]) + mm(other[1], held[1])
     whole[...] = mm(place[...], rows.astype(BF))
-    for piece, step in zip(pieces, steps(experts)):
-        piece[...] = whole[place_of(ahead(step, experts), experts)].astype(BF)
+    me = lax.axis_index("ex")
+    for piece, trip in zip(pieces, rounds(experts)):
+        target = target_of(trip)
+        target = jnp.where(target < 0, me, target)
+        piece[...] = whole[place_of(target, experts)].astype(BF)
+    pieces[-1][...] = whole[place_of(me, experts)].astype(BF)
 
 
 def weight_grads(mine_act, other_act, mine, other, rows_in, rows_grad, pair_out, down_out, held, sems):
@@ -261,10 +265,16 @@
 
 
 def combine(experts, pick, *refs):
-    out, whole, held, sems = refs[experts:]
-    for piece, step in zip(refs[:experts], steps(experts)):
-        whole[place_of(ahead(experts - step, experts), experts)] = piece[...].astype(F32)
-    home = whole[...].astype(BF)
+    *pieces, own, out, whole, held, sems = refs
+    me = lax.axis_index("ex")
+    spare = pl.ds(experts * MOST, MOST)
+    for piece, trip in zip(pieces, rounds(experts)):
+        source = source_of(trip)
+        spot = place_of(jnp.where(source < 0, me, source), experts).start
+        spot = jnp.where(source < 0, spare.start, spot)
+        whole[pl.ds(pl.multiple_of(spot, 8), MOST)] = piece[...].astype(F32)
+    whole[place_of(me, experts)] = own[...].astype(F32)
+    home = whole[: experts * MOST].astype(BF)
     rows = out.shape[0] // held.shape[0]
     stores = []
     for at in range(held.shape[0]):
@@ -287,32 +297,31 @@
     return pl.ds(pl.multiple_of(spot, 8), MOST)
 
 
-def tour(count):
-    bits = count.bit_length() - 1
-    return [sum(((i >> b) & 1) << (bits - 1 - b) for b in range(bits)) for i in range(count)]
-
-
-def steps(count):
-    found = []
-    for step in range(1, count // 2 + 1):
-        found += [step, count - step]
-    return list(dict.fromkeys(found)) + [0]
-
-
-def ahead(step, count):
-    me, names = lax.axis_index("ex"), tour(count)
-    found = jnp.int32(0)
-    for at, name in enumerate(names):
-        found = found + jnp.where(me == name, names[(at + step) % count], 0)
+def rounds(count):
+    if count == 4:
+        return [
+            {0: 1, 1: 2, 2: 3, 3: 0},
+            {1: 3, 2: 0, 3: 2},
+            {0: 2, 2: 1},
+            {0: 3, 1: 0, 3: 1},
+        ]
+    return [{i: (i + step) % count for i in range(count)} for step in range(1, count)]
+
+
+def partner(pairs):
+    me = lax.axis_index("ex")
+    found = jnp.int32(-1)
+    for name, other in pairs:
+        found = jnp.where(me == name, other, found)
     return found
 
 
-def shift(value, axis, step):
-    count = lax.axis_size(axis)
-    names = tour(count)
-    return lax.ppermute(
-        value, axis, [(name, names[(at + step) % count]) for at, name in enumerate(names)]
-    )
+def target_of(trip):
+    return partner(trip.items())
+
+
+def source_of(trip):
+    return partner((other, name) for name, other in trip.items())
 
 
 def swap(value, axis, bit):
@@ -460,16 +469,19 @@
         flops=weight_flops,
         traffic=weight_bytes,
     )
+    trips = rounds(experts)
     back = call(
         functools.partial(other_rows, experts),
-        piece,
+        piece[:1] * (len(trips) + 1),
         (own, other, place, held_other),
         [VMEM] * 4,
         [pltpu.VMEM((rows, width), F32)],
         flops=weight_flops,
         traffic=weight_bytes,
     )
-    home = [shift(part, "ex", step) if step else part for part, step in zip(back, steps(experts))]
+    *back, own_back = back
+    home = [lax.ppermute(part, "ex", list(trip.items())) for part, trip in zip(back, trips)]
+    home = home + [own_back]
     pair_grad, down_grad = call(
         weight_grads,
         [sds((1, 2, hidden, width), BF), sds((1, hidden, width), BF)],
@@ -485,8 +497,8 @@
         functools.partial(combine, experts),
         sds((tokens, width), BF),
         (pick, *home),
-        [VMEM] * (experts + 1),
-        [pltpu.VMEM((rows, width), F32), pltpu.VMEM((2, tokens // 2, width), BF), dma(2)],
+        [VMEM] * (len(home) + 1),
+        [pltpu.VMEM((rows + MOST, width), F32), pltpu.VMEM((2, tokens // 2, width), BF), dma(2)],
         flops=2 * rows * tokens * width,
         traffic=4 * tokens * width,
         out_specs=ANY,

time: 43.7 us -> 47.2 us (1.080)
  starting transfers between devices: 17 us -> 22.3 us
  waiting for transfers between devices: 9.26 us -> 7.38 us
    ppermute x3 -> x4, starting transfers between devices: 3.88 us -> 9.19 us  [local(): lax.ppermute(part, 'ex', list(trip.items()))]
    ppermute x3 -> x4, waiting for transfers between devices: 2.15 us -> 0.27 us  [local(): lax.ppermute(part, 'ex', list(trip.items()))]
  transfers between devices with their start and end apart: 14 -> 15, of which waited for: 7 -> 7; matrix products, arithmetic and copies ran while one was open for 0% -> 0% of each run, Pallas kernels for 30% -> 28%
where the time goes in v17:
time: 47.2 us; the launch traced here: 47 us
  starting transfers between devices  22.3 us (47%)
  Pallas kernels  16.5 us (35%)
  waiting for transfers between devices  7.38 us (16%)
  between operations  0.81 us (2%)
    pallas_call x15, Pallas kernels, call(): pl.pallas_call(body, out_shape=outs, in_specs=specs, out_specs=out_specs...  16.5 us
    ppermute x11, starting transfers between devices, swap(): return lax.ppermute(value, axis, [(i, i ^ bit) for i in range(count)])  13.1 us
    ppermute x4, starting transfers between devices, local(): lax.ppermute(part, 'ex', list(trip.items()))  9.19 us
    ppermute x11, waiting for transfers between devices, swap(): return lax.ppermute(value, axis, [(i, i ^ bit) for i in range(count)])  7.11 us
  transfers between devices with their start and end apart: 15, of which 7 were waited for; matrix products, arithmetic and copies ran while one was open for 0% of the time, Pallas kernels for 28%

profile of v17, /device:TPU:0, one launch (start us, length us, event | category | flops | bytes accessed | tf_op | source)
XLA Modules:
  0.0 47.0 jit_solution(8650308610408712979)
XLA Ops:
  0.6 1.5 %shard_map.85 = (bf16[160,256]{1,0:T(8,128)(2,1)S(1)}, f32[160,1]{1,0:T(8,128)S(1)}, bf16[256,1024]{1,0:T(8,128)(2,1)S(1)}, bf16[40,1024]{1,0:T(8,128)(2,1)S(1)}...) custom-call(s32[8,256]{1,0:T(8,128)} %bitcast.2, ...), custom_call_target="tpu_custom_call" | custom-call | flops 83886080 | bytes 1048576 | tf_op jit(solution)/shard_map/pallas_call | solution.py:70
  2.1 4.1 %collective-permute-start.3 = (bf16[40,1024]{1,0:T(8,128)(2,1)S(1)}, bf16[40,1024]{1,0:T(8,128)(2,1)S(1)}, u32[]{:S(2)}, u32[]{:S(2)}) collective-permute-start(bf16[40,1024]{1,0:T(8,128)(2,1)S(1)} %get-tuple-element.47), channel_id=1, source_target_pairs={{0,8},{4,12},{8,0},{12,4},{1,9},{5,13},{9,1},{13,5},{2,10},{6,14},... | collective-permute-start | bytes 245768 | tf_op jit(solution)/shard_map/ppermute | solution.py:329
  6.5 1.6 %collective-permute-start.2 = (bf16[80,1024]{1,0:T(8,128)(2,1)S(1)}, bf16[80,1024]{1,0:T(8,128)(2,1)S(1)}, u32[]{:S(2)}, u32[]{:S(2)}) collective-permute-start(bf16[80,1024]{1,0:T(8,128)(2,1)S(1)} %get-tuple-element.45), channel_id=1, source_target_pairs={{0,4},{4,0},{8,12},{12,8},{1,5},{5,1},{9,13},{13,9},{2,6},{6,2},{1... | collective-permute-start | bytes 491528 | tf_op jit(solution)/shard_map/ppermute | solution.py:329
  8.1 3.8 %shard_map.87 = (bf16[3,768,1024]{2,1,0:T(8,128)(2,1)S(1)}, bf16[3,768,1024]{2,1,0:T(8,128)(2,1)S(1)}, bf16[40,1024]{1,0:T(8,128)(2,1)S(1)}, bf16[40,1024]{1,0:T(8,128)(2,1)S(1)}, bf16[40,1024]{1,0:T(8,128)(2,1)S(1)}) custom-call(bf16[1,2,1536,1024]{3,2,1,0:T(8,128)(2,1)} %gate_up.1, bf16[1,1536,1024]{2,1,0:T(8,128)(2,1)} %down.1, ...), custom_call_target="tpu_custom_call" | custom-call | flops 251658240 | bytes 3145728 | tf_op jit(solution)/shard_map/pallas_call | solution.py:70
  11.9 2.0 %collective-permute-start = (bf16[40,1024]{1,0:T(8,128)(2,1)S(1)}, bf16[40,1024]{1,0:T(8,128)(2,1)S(1)}, u32[]{:S(2)}, u32[]{:S(2)}) collective-permute-start(bf16[40,1024]{1,0:T(8,128)(2,1)S(1)} %get-tuple-element.43), channel_id=1, source_target_pairs={{0,8},{4,12},{8,0},{12,4},{1,9},{5,13},{9,1},{13,5},{2,10},{6,14},... | collective-permute-start | bytes 245768 | tf_op jit(solution)/shard_map/ppermute | solution.py:329
  13.9 2.0 %collective-permute-start.1 = (bf16[40,1024]{1,0:T(8,128)(2,1)S(1)}, bf16[40,1024]{1,0:T(8,128)(2,1)S(1)}, u32[]{:S(2)}, u32[]{:S(2)}) collective-permute-start(bf16[40,1024]{1,0:T(8,128)(2,1)S(1)} %get-tuple-element.44), channel_id=1, source_target_pairs={{0,12},{4,8},{8,4},{12,0},{1,13},{5,9},{9,5},{13,1},{2,14},{6,10},... | collective-permute-start | bytes 245768 | tf_op jit(solution)/shard_map/ppermute | solution.py:329
  15.9 1.4 %shard_map.89 = (bf16[2,80,768]{2,1,0:T(8,128)(2,1)S(1)}, bf16[160,80]{1,0:T(8,128)(2,1)S(1)}, bf16[80,1024]{1,0:T(8,128)(2,1)S(1)}) custom-call(bf16[40,1024]{1,0:T(8,128)(2,1)S(1)} %shard_map.88.refs_0_, bf16[40,1024]{1,0:T(8,128)(2,1)S(1)} %collective-permute-done.4.refs_1_, bf16[80,1024]{1,0:T(8,128)(2,1)S(1)} %collective-permute-done.2.refs_2_, ...), custom_call_target="tpu_custom_call" | custom-call | flops 503316480 | bytes 3145728 | tf_op jit(solution)/shard_map/pallas_call | solution.py:70
  17.5 1.1 %shard_map.91.mine = bf16[2,80,768]{2,1,0:T(8,128)(2,1)S(1)} custom-call(bf16[80,1024]{1,0:T(8,128)(2,1)S(1)} %get-tuple-element.54.rows_in, bf16[3,768,1024]{2,1,0:T(8,128)(2,1)S(1)} %get-tuple-element.52.refs_5_.held), custom_call_target="tpu_custom_call" | custom-call | flops 25165824000 | bytes 314572800 | tf_op jit(solution)/shard_map/pallas_call | solution.py:70
  19.0 1.6 %collective-permute-start.8 = (bf16[2,80,768]{2,1,0:T(8,128)(2,1)S(1)}, bf16[2,80,768]{2,1,0:T(8,128)(2,1)S(1)}, u32[]{:S(2)}, u32[]{:S(2)}) collective-permute-start(bf16[2,80,768]{2,1,0:T(8,128)(2,1)S(1)} %get-tuple-element.56.refs_6_), channel_id=1, source_target_pairs={{0,2},{1,3},{2,0},{3,1},{4,6},{5,7},{6,4},{7,5},{8,10},{9,11},{10,... | collective-permute-start | bytes 737288 | tf_op jit(solution)/shard_map/ppermute | solution.py:329
  20.9 0.7 %shard_map.93 = bf16[80,768]{1,0:T(8,128)(2,1)S(1)} custom-call(bf16[40,1024]{1,0:T(8,128)(2,1)S(1)} %collective-permute-done.refs_0_, bf16[40,1024]{1,0:T(8,128)(2,1)S(1)} %collective-permute-done.1.refs_1_, bf16[80,1024]{1,0:T(8,128)(2,1)S(1)} %collective-permute-done.2.refs_2_, bf16[40,1024]{1,0:T(8,128)(2,1)S(1)} %get-tuple-element.46.refs_3_, ...), custom_call_target="tpu_custom_call" | custom-call | flops 251658240 | bytes 3145728 | tf_op jit(solution)/shard_map/pallas_call | solution.py:70
  21.6 0.7 %shard_map.90 = (bf16[80,1024]{1,0:T(8,128)(2,1)S(1)}, bf16[80,768]{1,0:T(8,128)(2,1)S(1)}) custom-call(bf16[40,1024]{1,0:T(8,128)(2,1)S(1)} %collective-permute-done.refs_0_, bf16[40,1024]{1,0:T(8,128)(2,1)S(1)} %collective-permute-done.1.refs_1_, bf16[80,1024]{1,0:T(8,128)(2,1)S(1)} %collective-permute-done.2.refs_2_, ...), custom_call_target="tpu_custom_call" | custom-call | flops 25165824000 | bytes 314572800 | tf_op jit(solution)/shard_map/pallas_call | solution.py:70
  22.3 0.6 %collective-permute-done.6 = bf16[80,768]{1,0:T(8,128)(2,1)S(1)} collective-permute-done((bf16[80,768]{1,0:T(8,128)(2,1)S(1)}, bf16[80,768]{1,0:T(8,128)(2,1)S(1)}, u32[]{:S(2)}, u32[]{:S(2)}) %collective-permute-start.6) | collective-permute-done | bytes 122912 | tf_op jit(solution)/shard_map/ppermute | solution.py:329
  23.0 1.6 %collective-permute-start.7 = (bf16[80,768]{1,0:T(8,128)(2,1)S(1)}, bf16[80,768]{1,0:T(8,128)(2,1)S(1)}, u32[]{:S(2)}, u32[]{:S(2)}) collective-permute-start(bf16[80,768]{1,0:T(8,128)(2,1)S(1)} %get-tuple-element.69), channel_id=1, source_target_pairs={{0,2},{1,3},{2,0},{3,1},{4,6},{5,7},{6,4},{7,5},{8,10},{9,11},{10,... | collective-permute-start | bytes 368648 | tf_op jit(solution)/shard_map/ppermute | solution.py:329
  24.6 3.3 %collective-permute-done.8.pair_far = bf16[2,80,768]{2,1,0:T(8,128)(2,1)S(1)} collective-permute-done((bf16[2,80,768]{2,1,0:T(8,128)(2,1)S(1)}, bf16[2,80,768]{2,1,0:T(8,128)(2,1)S(1)}, u32[]{:S(2)}, u32[]{:S(2)}) %collective-permute-start.8) | collective-permute-done | bytes 245792 | tf_op jit(solution)/shard_map/ppermute | solution.py:329
  28.1 1.6 %collective-permute-done.7.act_far = bf16[80,768]{1,0:T(8,128)(2,1)S(1)} collective-permute-done((bf16[80,768]{1,0:T(8,128)(2,1)S(1)}, bf16[80,768]{1,0:T(8,128)(2,1)S(1)}, u32[]{:S(2)}, u32[]{:S(2)}) %collective-permute-start.7) | collective-permute-done | bytes 122912 | tf_op jit(solution)/shard_map/ppermute | solution.py:329
  29.9 0.7 %shard_map.96.total = f32[80,1024]{1,0:T(8,128)S(1)} custom-call(bf16[2,80,768]{2,1,0:T(8,128)(2,1)S(1)} %shard_map.95.mine, bf16[3,768,1024]{2,1,0:T(8,128)(2,1)S(1)} %get-tuple-element.52.refs_5_.held), custom_call_target="tpu_custom_call" | custom-call | flops 251658240 | bytes 3145728 | tf_op jit(solution)/shard_map/pallas_call | solution.py:70
  30.5 0.8 %collective-permute-done.10.other = bf16[2,80,768]{2,1,0:T(8,128)(2,1)S(1)} collective-permute-done((bf16[2,80,768]{2,1,0:T(8,128)(2,1)S(1)}, bf16[2,80,768]{2,1,0:T(8,128)(2,1)S(1)}, u32[]{:S(2)}, u32[]{:S(2)}) %collective-permute-start.10) | collective-permute-done | bytes 245792 | tf_op jit(solution)/shard_map/ppermute | solution.py:329
  31.4 0.9 %shard_map.97 = (bf16[40,1024]{1,0:T(8,128)(2,1)S(1)}, bf16[40,1024]{1,0:T(8,128)(2,1)S(1)}, bf16[40,1024]{1,0:T(8,128)(2,1)S(1)}, bf16[40,1024]{1,0:T(8,128)(2,1)S(1)}, bf16[40,1024]{1,0:T(8,128)(2,1)S(1)}) custom-call(f32[80,1024]{1,0:T(8,128)S(1)} %shard_map.96.total, bf16[2,80,768]{2,1,0:T(8,128)(2,1)S(1)} %collective-permute-done.10.other, ...), custom_call_target="tpu_custom_call" | custom-call | flops 251658240 | bytes 3145728 | tf_op jit(solution)/shard_map/pallas_call | solution.py:70
  32.3 0.5 %collective-permute-start.11 = (bf16[40,1024]{1,0:T(8,128)(2,1)S(1)}, bf16[40,1024]{1,0:T(8,128)(2,1)S(1)}, u32[]{:S(2)}, u32[]{:S(2)}) collective-permute-start(bf16[40,1024]{1,0:T(8,128)(2,1)S(1)} %get-tuple-element.61), channel_id=1, source_target_pairs={{0,4},{4,8},{8,12},{12,0},{1,5},{5,9},{9,13},{13,1},{2,6},{6,10},{... | collective-permute-start | bytes 245768 | tf_op jit(solution)/shard_map/ppermute | solution.py:483
  32.8 1.3 %collective-permute-start.12 = (bf16[40,1024]{1,0:T(8,128)(2,1)S(1)}, bf16[40,1024]{1,0:T(8,128)(2,1)S(1)}, u32[]{:S(2)}, u32[]{:S(2)}) collective-permute-start(bf16[40,1024]{1,0:T(8,128)(2,1)S(1)} %get-tuple-element.62), channel_id=1, source_target_pairs={{4,12},{8,0},{12,8},{5,13},{9,1},{13,9},{6,14},{10,2},{14,10},{7,1... | collective-permute-start | bytes 245768 | tf_op jit(solution)/shard_map/ppermute | solution.py:483
  34.1 5.4 %collective-permute-start.13 = (bf16[40,1024]{1,0:T(8,128)(2,1)S(1)}, bf16[40,1024]{1,0:T(8,128)(2,1)S(1)}, u32[]{:S(2)}, u32[]{:S(2)}) collective-permute-start(bf16[40,1024]{1,0:T(8,128)(2,1)S(1)} %get-tuple-element.63), channel_id=1, source_target_pairs={{0,8},{8,4},{1,9},{9,5},{2,10},{10,6},{3,11},{11,7},{16,24},{24,20... | collective-permute-start | bytes 245768 | tf_op jit(solution)/shard_map/ppermute | solution.py:483
  39.6 1.9 %collective-permute-start.14 = (bf16[40,1024]{1,0:T(8,128)(2,1)S(1)}, bf16[40,1024]{1,0:T(8,128)(2,1)S(1)}, u32[]{:S(2)}, u32[]{:S(2)}) collective-permute-start(bf16[40,1024]{1,0:T(8,128)(2,1)S(1)} %get-tuple-element.64), channel_id=1, source_target_pairs={{0,12},{4,0},{12,4},{1,13},{5,1},{13,5},{2,14},{6,2},{14,6},{3,15}... | collective-permute-start | bytes 245768 | tf_op jit(solution)/shard_map/ppermute | solution.py:483
  41.5 4.1 %shard_map.99 = (bf16[1,2,1536,1024]{3,2,1,0:T(8,128)(2,1)}, bf16[1,1536,1024]{2,1,0:T(8,128)(2,1)}) custom-call(bf16[80,768]{1,0:T(8,128)(2,1)S(1)} %get-tuple-element.60.mine_act, bf16[80,768]{1,0:T(8,128)(2,1)S(1)} %collective-permute-done.9._.other_act, bf16[2,80,768]{2,1,0:T(8,128)(2,1)S(1)} %shard_map.95.mine, ...), custom_call_target="tpu_custom_call" | custom-call | flops 754974720 | bytes 9437184 | tf_op jit(solution)/shard_map/pallas_call | solution.py:70
  45.9 1.1 %shard_map.98 = bf16[256,1024]{1,0:T(8,128)(2,1)} custom-call(bf16[160,256]{1,0:T(8,128)(2,1)S(1)} %get-tuple-element.36.pick, bf16[40,1024]{1,0:T(8,128)(2,1)S(1)} %collective-permute-done.11.refs_0_, bf16[40,1024]{1,0:T(8,128)(2,1)S(1)} %collective-permute-done.12.refs_1_, bf16[40,1024]{1,0:T(8,128)(2,1)S(1)} %collective-permute-done.13.refs_2_, ...), custom_call_target="tpu_custom_call" | custom-call | flops 83886080 | bytes 1048576 | tf_op jit(solution)/shard_map/pallas_call | solution.py:70
  (22 shorter events, 1.8 us)
Async XLA Ops:
  2.1 13.8 %collective-permute-start.3 = (bf16[40,1024]{1,0:T(8,128)(2,1)S(1)}, bf16[40,1024]{1,0:T(8,128)(2,1)S(1)}, u32[]{:S(2)}, u32[]{:S(2)}) collective-permute-start(bf16[40,1024]{1,0:T(8,128)(2,1)S(1)} %get-tuple-element.47), channel_id=1, source_target_pairs={{0,8},{4,12},{8,0},{12,4},{1,9},{5,13},{9,1},{13,5},{2,10},{6,14},... | collective-permute-start | bytes 245768 | tf_op jit(solution)/shard_map/ppermute | solution.py:329
  6.5 9.4 %collective-permute-start.2 = (bf16[80,1024]{1,0:T(8,128)(2,1)S(1)}, bf16[80,1024]{1,0:T(8,128)(2,1)S(1)}, u32[]{:S(2)}, u32[]{:S(2)}) collective-permute-start(bf16[80,1024]{1,0:T(8,128)(2,1)S(1)} %get-tuple-element.45), channel_id=1, source_target_pairs={{0,4},{4,0},{8,12},{12,8},{1,5},{5,1},{9,13},{13,9},{2,6},{6,2},{1... | collective-permute-start | bytes 491528 | tf_op jit(solution)/shard_map/ppermute | solution.py:329
  8.1 7.8 %collective-permute-start.4 = (bf16[40,1024]{1,0:T(8,128)(2,1)S(1)}, bf16[40,1024]{1,0:T(8,128)(2,1)S(1)}, u32[]{:S(2)}, u32[]{:S(2)}) collective-permute-start(bf16[40,1024]{1,0:T(8,128)(2,1)S(1)} %get-tuple-element.48), channel_id=1, source_target_pairs={{0,12},{4,8},{8,4},{12,0},{1,13},{5,9},{9,5},{13,1},{2,14},{6,10},... | collective-permute-start | bytes 245768 | tf_op jit(solution)/shard_map/ppermute | solution.py:329
  11.9 8.9 %collective-permute-start = (bf16[40,1024]{1,0:T(8,128)(2,1)S(1)}, bf16[40,1024]{1,0:T(8,128)(2,1)S(1)}, u32[]{:S(2)}, u32[]{:S(2)}) collective-permute-start(bf16[40,1024]{1,0:T(8,128)(2,1)S(1)} %get-tuple-element.43), channel_id=1, source_target_pairs={{0,8},{4,12},{8,0},{12,4},{1,9},{5,13},{9,1},{13,5},{2,10},{6,14},... | collective-permute-start | bytes 245768 | tf_op jit(solution)/shard_map/ppermute | solution.py:329
  13.9 7.0 %collective-permute-start.1 = (bf16[40,1024]{1,0:T(8,128)(2,1)S(1)}, bf16[40,1024]{1,0:T(8,128)(2,1)S(1)}, u32[]{:S(2)}, u32[]{:S(2)}) collective-permute-start(bf16[40,1024]{1,0:T(8,128)(2,1)S(1)} %get-tuple-element.44), channel_id=1, source_target_pairs={{0,12},{4,8},{8,4},{12,0},{1,13},{5,9},{9,5},{13,1},{2,14},{6,10},... | collective-permute-start | bytes 245768 | tf_op jit(solution)/shard_map/ppermute | solution.py:329
  17.4 1.6 %collective-permute-start.5 = (bf16[2,80,768]{2,1,0:T(8,128)(2,1)S(1)}, bf16[2,80,768]{2,1,0:T(8,128)(2,1)S(1)}, u32[]{:S(2)}, u32[]{:S(2)}) collective-permute-start(bf16[2,80,768]{2,1,0:T(8,128)(2,1)S(1)} %get-tuple-element.55), channel_id=1, source_target_pairs={{0,1},{1,0},{2,3},{3,2},{4,5},{5,4},{6,7},{7,6},{8,9},{9,8},{10,11... | collective-permute-start | bytes 737288 | tf_op jit(solution)/shard_map/ppermute | solution.py:329
  19.0 8.9 %collective-permute-start.8 = (bf16[2,80,768]{2,1,0:T(8,128)(2,1)S(1)}, bf16[2,80,768]{2,1,0:T(8,128)(2,1)S(1)}, u32[]{:S(2)}, u32[]{:S(2)}) collective-permute-start(bf16[2,80,768]{2,1,0:T(8,128)(2,1)S(1)} %get-tuple-element.56.refs_6_), channel_id=1, source_target_pairs={{0,2},{1,3},{2,0},{3,1},{4,6},{5,7},{6,4},{7,5},{8,10},{9,11},{10,... | collective-permute-start | bytes 737288 | tf_op jit(solution)/shard_map/ppermute | solution.py:329
  21.6 1.4 %collective-permute-start.6 = (bf16[80,768]{1,0:T(8,128)(2,1)S(1)}, bf16[80,768]{1,0:T(8,128)(2,1)S(1)}, u32[]{:S(2)}, u32[]{:S(2)}) collective-permute-start(bf16[80,768]{1,0:T(8,128)(2,1)S(1)} %shard_map.93), channel_id=1, source_target_pairs={{0,1},{1,0},{2,3},{3,2},{4,5},{5,4},{6,7},{7,6},{8,9},{9,8},{10,11... | collective-permute-start | bytes 368648 | tf_op jit(solution)/shard_map/ppermute | solution.py:329
  23.0 6.7 %collective-permute-start.7 = (bf16[80,768]{1,0:T(8,128)(2,1)S(1)}, bf16[80,768]{1,0:T(8,128)(2,1)S(1)}, u32[]{:S(2)}, u32[]{:S(2)}) collective-permute-start(bf16[80,768]{1,0:T(8,128)(2,1)S(1)} %get-tuple-element.69), channel_id=1, source_target_pairs={{0,2},{1,3},{2,0},{3,1},{4,6},{5,7},{6,4},{7,5},{8,10},{9,11},{10,... | collective-permute-start | bytes 368648 | tf_op jit(solution)/shard_map/ppermute | solution.py:329
  28.0 1.7 %collective-permute-start.9 = (bf16[80,768]{1,0:T(8,128)(2,1)S(1)}, bf16[80,768]{1,0:T(8,128)(2,1)S(1)}, u32[]{:S(2)}, u32[]{:S(2)}) collective-permute-start(bf16[80,768]{1,0:T(8,128)(2,1)S(1)} %get-tuple-element.60.mine_act), channel_id=1, source_target_pairs={{0,1},{1,0},{2,3},{3,2},{4,5},{5,4},{6,7},{7,6},{8,9},{9,8},{10,11... | collective-permute-start | bytes 368648 | tf_op jit(solution)/shard_map/ppermute | solution.py:329
  29.8 1.6 %collective-permute-start.10 = (bf16[2,80,768]{2,1,0:T(8,128)(2,1)S(1)}, bf16[2,80,768]{2,1,0:T(8,128)(2,1)S(1)}, u32[]{:S(2)}, u32[]{:S(2)}) collective-permute-start(bf16[2,80,768]{2,1,0:T(8,128)(2,1)S(1)} %shard_map.95.mine), channel_id=1, source_target_pairs={{0,1},{1,0},{2,3},{3,2},{4,5},{5,4},{6,7},{7,6},{8,9},{9,8},{10,11... | collective-permute-start | bytes 737288 | tf_op jit(solution)/shard_map/ppermute | solution.py:329
  32.3 13.3 %collective-permute-start.11 = (bf16[40,1024]{1,0:T(8,128)(2,1)S(1)}, bf16[40,1024]{1,0:T(8,128)(2,1)S(1)}, u32[]{:S(2)}, u32[]{:S(2)}) collective-permute-start(bf16[40,1024]{1,0:T(8,128)(2,1)S(1)} %get-tuple-element.61), channel_id=1, source_target_pairs={{0,4},{4,8},{8,12},{12,0},{1,5},{5,9},{9,13},{13,1},{2,6},{6,10},{... | collective-permute-start | bytes 245768 | tf_op jit(solution)/shard_map/ppermute | solution.py:483
  32.8 12.8 %collective-permute-start.12 = (bf16[40,1024]{1,0:T(8,128)(2,1)S(1)}, bf16[40,1024]{1,0:T(8,128)(2,1)S(1)}, u32[]{:S(2)}, u32[]{:S(2)}) collective-permute-start(bf16[40,1024]{1,0:T(8,128)(2,1)S(1)} %get-tuple-element.62), channel_id=1, source_target_pairs={{4,12},{8,0},{12,8},{5,13},{9,1},{13,9},{6,14},{10,2},{14,10},{7,1... | collective-permute-start | bytes 245768 | tf_op jit(solution)/shard_map/ppermute | solution.py:483
  34.1 11.5 %collective-permute-start.13 = (bf16[40,1024]{1,0:T(8,128)(2,1)S(1)}, bf16[40,1024]{1,0:T(8,128)(2,1)S(1)}, u32[]{:S(2)}, u32[]{:S(2)}) collective-permute-start(bf16[40,1024]{1,0:T(8,128)(2,1)S(1)} %get-tuple-element.63), channel_id=1, source_target_pairs={{0,8},{8,4},{1,9},{9,5},{2,10},{10,6},{3,11},{11,7},{16,24},{24,20... | collective-permute-start | bytes 245768 | tf_op jit(solution)/shard_map/ppermute | solution.py:483
  39.6 6.3 %collective-permute-start.14 = (bf16[40,1024]{1,0:T(8,128)(2,1)S(1)}, bf16[40,1024]{1,0:T(8,128)(2,1)S(1)}, u32[]{:S(2)}, u32[]{:S(2)}) collective-permute-start(bf16[40,1024]{1,0:T(8,128)(2,1)S(1)} %get-tuple-element.64), channel_id=1, source_target_pairs={{0,12},{4,0},{12,4},{1,13},{5,1},{13,5},{2,14},{6,2},{14,6},{3,15}... | collective-permute-start | bytes 245768 | tf_op jit(solution)/shard_map/ppermute | solution.py:483

commit v18 on v15

--- a/solution.py
+++ b/solution.py
@@ -91,9 +91,12 @@
     tokens = inputs.shape[0]
     rows = experts * MOST
     order = far_first(experts)
-    owner = block_of(iota((rows, routes.shape[0]), 0), order)
-    named = jnp.zeros((rows, tokens), F32)
-    weight = jnp.zeros((rows, tokens), F32)
+    width = routes.shape[0]
+    cells = (rows, experts * width)
+    spread = block_of(iota(cells, 0), range(experts)) == lax.shift_right_logical(
+        iota(cells, 1), width.bit_length() - 1
+    )
+    spread = jnp.where(spread, 1.0, 0.0).astype(BF)
     earlier = iota((tokens, tokens), 0) < iota((tokens, tokens), 1)
     earlier = jnp.where(earlier, 1.0, 0.0).astype(BF)
     row = iota((rows, tokens), 0)
@@ -101,11 +104,10 @@
     wait(loads)
     chosen = routes[...]
     wide = probs[...].astype(F32)
-    for k in range(experts):
-        spread = jnp.where(owner == k, 1.0, 0.0).astype(BF)
-        hit = chosen == (me ^ k)
-        named = named + mm(spread, jnp.where(hit, 1.0, 0.0).astype(BF))
-        weight = weight + mm(spread, jnp.where(hit, wide, 0.0).astype(BF))
+    hits = jnp.concatenate([jnp.where(chosen == (me ^ k), 1.0, 0.0) for k in order], axis=0)
+    odds = hits * jnp.concatenate([wide] * experts, axis=0)
+    both = mm(spread, jnp.concatenate([hits, odds], axis=1).astype(BF))
+    named, weight = both[:, :tokens], both[:, tokens:]
     rank = mm(named.astype(BF), earlier).astype(jnp.int32)
     picks = (rank == slot) & (named > 0.5)
     pick = jnp.where(picks, 1.0, 0.0)
@@ -146,8 +148,8 @@
     got = stacked(pieces)
     full = got[:, :1] < EMPTY / 2
     key = []
-    for dim in (0, 1):
-        row = iota((rows, rows), dim)
+    for shape, dim in (((rows, 1), 0), ((1, rows), 1)):
+        row = iota(shape, dim)
         local_row = row - block_of(row, range(experts)) * MOST
         key.append((me ^ block_of(row, far_first(experts))) * MOST + local_row)
     earlier = jnp.where(key[1] < key[0], 1.0, 0.0).astype(BF)

time: 43.6 us -> 43.5 us (level)
  no operation moved by 1% of the time
where the time goes in v18:
time: 43.5 us; the launch traced here: 43.3 us
  starting transfers between devices  17 us (39%)
  Pallas kernels  16.3 us (37%)
  waiting for transfers between devices  9.14 us (21%)
  between operations  0.75 us (2%)
    pallas_call x14, Pallas kernels, call(): pl.pallas_call(body, out_shape=outs, in_specs=specs, out_specs=out_specs...  16.3 us
    ppermute x11, starting transfers between devices, swap(): return lax.ppermute(value, axis, [(i, i ^ bit) for i in range(count)])  12.6 us
    ppermute x11, waiting for transfers between devices, swap(): return lax.ppermute(value, axis, [(i, i ^ bit) for i in range(count)])  7.51 us
    ppermute x3, starting transfers between devices, shift(): lax.ppermute(value, axis, [(name, names[(at + step) % count]) for at, nam...  4.33 us
    ppermute x3, waiting for transfers between devices, shift(): lax.ppermute(value, axis, [(name, names[(at + step) % count]) for at, nam...  1.63 us
  transfers between devices with their start and end apart: 14, of which 8 were waited for; matrix products, arithmetic and copies ran while one was open for 0% of the time, Pallas kernels for 30%

profile of v18, /device:TPU:0, one launch (start us, length us, event | category | flops | bytes accessed | tf_op | source)
XLA Modules:
  0.0 43.3 jit_solution(2998408943430200697)
XLA Ops:
  0.6 1.4 %shard_map.85 = (bf16[160,256]{1,0:T(8,128)(2,1)S(1)}, f32[160,1]{1,0:T(8,128)S(1)}, bf16[256,1024]{1,0:T(8,128)(2,1)S(1)}, bf16[40,1024]{1,0:T(8,128)(2,1)S(1)}...) custom-call(s32[8,256]{1,0:T(8,128)} %bitcast.2, ...), custom_call_target="tpu_custom_call" | custom-call | flops 83886080 | bytes 1048576 | tf_op jit(solution)/shard_map/pallas_call | solution.py:69
  2.0 4.1 %collective-permute-start.3 = (bf16[40,1024]{1,0:T(8,128)(2,1)S(1)}, bf16[40,1024]{1,0:T(8,128)(2,1)S(1)}, u32[]{:S(2)}, u32[]{:S(2)}) collective-permute-start(bf16[40,1024]{1,0:T(8,128)(2,1)S(1)} %get-tuple-element.46), channel_id=1, source_target_pairs={{0,8},{4,12},{8,0},{12,4},{1,9},{5,13},{9,1},{13,5},{2,10},{6,14},... | collective-permute-start | bytes 245768 | tf_op jit(solution)/shard_map/ppermute | solution.py:318
  6.1 1.4 %collective-permute-start.4 = (bf16[40,1024]{1,0:T(8,128)(2,1)S(1)}, bf16[40,1024]{1,0:T(8,128)(2,1)S(1)}, u32[]{:S(2)}, u32[]{:S(2)}) collective-permute-start(bf16[40,1024]{1,0:T(8,128)(2,1)S(1)} %get-tuple-element.47), channel_id=1, source_target_pairs={{0,12},{4,8},{8,4},{12,0},{1,13},{5,9},{9,5},{13,1},{2,14},{6,10},... | collective-permute-start | bytes 245768 | tf_op jit(solution)/shard_map/ppermute | solution.py:318
  8.0 3.8 %shard_map.87 = (bf16[3,768,1024]{2,1,0:T(8,128)(2,1)S(1)}, bf16[3,768,1024]{2,1,0:T(8,128)(2,1)S(1)}, bf16[40,1024]{1,0:T(8,128)(2,1)S(1)}, bf16[40,1024]{1,0:T(8,128)(2,1)S(1)}, bf16[40,1024]{1,0:T(8,128)(2,1)S(1)}) custom-call(bf16[1,2,1536,1024]{3,2,1,0:T(8,128)(2,1)} %gate_up.1, bf16[1,1536,1024]{2,1,0:T(8,128)(2,1)} %down.1, ...), custom_call_target="tpu_custom_call" | custom-call | flops 25165824000 | bytes 314572800 | tf_op jit(solution)/shard_map/pallas_call | solution.py:69
  11.8 3.0 %collective-permute-start = (bf16[40,1024]{1,0:T(8,128)(2,1)S(1)}, bf16[40,1024]{1,0:T(8,128)(2,1)S(1)}, u32[]{:S(2)}, u32[]{:S(2)}) collective-permute-start(bf16[40,1024]{1,0:T(8,128)(2,1)S(1)} %get-tuple-element.42), channel_id=1, source_target_pairs={{0,12},{4,8},{8,4},{12,0},{1,13},{5,9},{9,5},{13,1},{2,14},{6,10},... | collective-permute-start | bytes 245768 | tf_op jit(solution)/shard_map/ppermute | solution.py:318
  15.4 1.4 %shard_map.88 = (bf16[2,80,768]{2,1,0:T(8,128)(2,1)S(1)}, bf16[160,80]{1,0:T(8,128)(2,1)S(1)}, bf16[80,1024]{1,0:T(8,128)(2,1)S(1)}) custom-call(bf16[40,1024]{1,0:T(8,128)(2,1)S(1)} %collective-permute-done.3.refs_0_, bf16[40,1024]{1,0:T(8,128)(2,1)S(1)} %collective-permute-done.4.refs_1_, bf16[80,1024]{1,0:T(8,128)(2,1)S(1)} %collective-permute-done.2.refs_2_, ...), custom_call_target="tpu_custom_call" | custom-call | flops 503316480 | bytes 3145728 | tf_op jit(solution)/shard_map/pallas_call | solution.py:69
  16.9 1.1 %shard_map.90.mine = bf16[2,80,768]{2,1,0:T(8,128)(2,1)S(1)} custom-call(bf16[80,1024]{1,0:T(8,128)(2,1)S(1)} %get-tuple-element.53.rows_in, bf16[3,768,1024]{2,1,0:T(8,128)(2,1)S(1)} %get-tuple-element.51.refs_5_.held), custom_call_target="tpu_custom_call" | custom-call | flops 25165824000 | bytes 314572800 | tf_op jit(solution)/shard_map/pallas_call | solution.py:69
  18.5 1.7 %collective-permute-start.8 = (bf16[2,80,768]{2,1,0:T(8,128)(2,1)S(1)}, bf16[2,80,768]{2,1,0:T(8,128)(2,1)S(1)}, u32[]{:S(2)}, u32[]{:S(2)}) collective-permute-start(bf16[2,80,768]{2,1,0:T(8,128)(2,1)S(1)} %get-tuple-element.55.refs_6_), channel_id=1, source_target_pairs={{0,2},{1,3},{2,0},{3,1},{4,6},{5,7},{6,4},{7,5},{8,10},{9,11},{10,... | collective-permute-start | bytes 737288 | tf_op jit(solution)/shard_map/ppermute | solution.py:318
  20.2 1.7 %collective-permute-done.1.refs_1_ = bf16[40,1024]{1,0:T(8,128)(2,1)S(1)} collective-permute-done((bf16[40,1024]{1,0:T(8,128)(2,1)S(1)}, bf16[40,1024]{1,0:T(8,128)(2,1)S(1)}, u32[]{:S(2)}, u32[]{:S(2)}) %collective-permute-start.1) | collective-permute-done | bytes 81952 | tf_op jit(solution)/shard_map/ppermute | solution.py:318
  22.0 0.7 %shard_map.92 = bf16[80,768]{1,0:T(8,128)(2,1)S(1)} custom-call(bf16[40,1024]{1,0:T(8,128)(2,1)S(1)} %collective-permute-done.refs_0_, bf16[40,1024]{1,0:T(8,128)(2,1)S(1)} %collective-permute-done.1.refs_1_, bf16[80,1024]{1,0:T(8,128)(2,1)S(1)} %collective-permute-done.2.refs_2_, bf16[40,1024]{1,0:T(8,128)(2,1)S(1)} %get-tuple-element.45.refs_3_, ...), custom_call_target="tpu_custom_call" | custom-call | flops 251658240 | bytes 3145728 | tf_op jit(solution)/shard_map/pallas_call | solution.py:69
  22.7 0.7 %shard_map.89 = (bf16[80,1024]{1,0:T(8,128)(2,1)S(1)}, bf16[80,768]{1,0:T(8,128)(2,1)S(1)}) custom-call(bf16[40,1024]{1,0:T(8,128)(2,1)S(1)} %collective-permute-done.refs_0_, bf16[40,1024]{1,0:T(8,128)(2,1)S(1)} %collective-permute-done.1.refs_1_, bf16[80,1024]{1,0:T(8,128)(2,1)S(1)} %collective-permute-done.2.refs_2_, ...), custom_call_target="tpu_custom_call" | custom-call | flops 25165824000 | bytes 314572800 | tf_op jit(solution)/shard_map/pallas_call | solution.py:69
  23.4 0.6 %collective-permute-done.6 = bf16[80,768]{1,0:T(8,128)(2,1)S(1)} collective-permute-done((bf16[80,768]{1,0:T(8,128)(2,1)S(1)}, bf16[80,768]{1,0:T(8,128)(2,1)S(1)}, u32[]{:S(2)}, u32[]{:S(2)}) %collective-permute-start.6) | collective-permute-done | bytes 122912 | tf_op jit(solution)/shard_map/ppermute | solution.py:318
  24.1 1.6 %collective-permute-start.7 = (bf16[80,768]{1,0:T(8,128)(2,1)S(1)}, bf16[80,768]{1,0:T(8,128)(2,1)S(1)}, u32[]{:S(2)}, u32[]{:S(2)}) collective-permute-start(bf16[80,768]{1,0:T(8,128)(2,1)S(1)} %get-tuple-element.67), channel_id=1, source_target_pairs={{0,2},{1,3},{2,0},{3,1},{4,6},{5,7},{6,4},{7,5},{8,10},{9,11},{10,... | collective-permute-start | bytes 368648 | tf_op jit(solution)/shard_map/ppermute | solution.py:318
  25.7 0.9 %collective-permute-done.8.pair_far = bf16[2,80,768]{2,1,0:T(8,128)(2,1)S(1)} collective-permute-done((bf16[2,80,768]{2,1,0:T(8,128)(2,1)S(1)}, bf16[2,80,768]{2,1,0:T(8,128)(2,1)S(1)}, u32[]{:S(2)}, u32[]{:S(2)}) %collective-permute-start.8) | collective-permute-done | bytes 245792 | tf_op jit(solution)/shard_map/ppermute | solution.py:318
  26.8 2.8 %collective-permute-done.7.act_far = bf16[80,768]{1,0:T(8,128)(2,1)S(1)} collective-permute-done((bf16[80,768]{1,0:T(8,128)(2,1)S(1)}, bf16[80,768]{1,0:T(8,128)(2,1)S(1)}, u32[]{:S(2)}, u32[]{:S(2)}) %collective-permute-start.7) | collective-permute-done | bytes 122912 | tf_op jit(solution)/shard_map/ppermute | solution.py:318
  29.7 0.7 %shard_map.95.total = f32[80,1024]{1,0:T(8,128)S(1)} custom-call(bf16[2,80,768]{2,1,0:T(8,128)(2,1)S(1)} %shard_map.94.mine, bf16[3,768,1024]{2,1,0:T(8,128)(2,1)S(1)} %get-tuple-element.51.refs_5_.held), custom_call_target="tpu_custom_call" | custom-call | flops 251658240 | bytes 3145728 | tf_op jit(solution)/shard_map/pallas_call | solution.py:69
  30.4 0.8 %collective-permute-done.10.other = bf16[2,80,768]{2,1,0:T(8,128)(2,1)S(1)} collective-permute-done((bf16[2,80,768]{2,1,0:T(8,128)(2,1)S(1)}, bf16[2,80,768]{2,1,0:T(8,128)(2,1)S(1)}, u32[]{:S(2)}, u32[]{:S(2)}) %collective-permute-start.10) | collective-permute-done | bytes 245792 | tf_op jit(solution)/shard_map/ppermute | solution.py:318
  31.2 0.9 %shard_map.96 = (bf16[40,1024]{1,0:T(8,128)(2,1)S(1)}, bf16[40,1024]{1,0:T(8,128)(2,1)S(1)}, bf16[40,1024]{1,0:T(8,128)(2,1)S(1)}, bf16[40,1024]{1,0:T(8,128)(2,1)S(1)}) custom-call(f32[80,1024]{1,0:T(8,128)S(1)} %shard_map.95.total, bf16[2,80,768]{2,1,0:T(8,128)(2,1)S(1)} %collective-permute-done.10.other, ...), custom_call_target="tpu_custom_call" | custom-call | flops 251658240 | bytes 3145728 | tf_op jit(solution)/shard_map/pallas_call | solution.py:69
  32.1 2.1 %collective-permute-start.11 = (bf16[40,1024]{1,0:T(8,128)(2,1)S(1)}, bf16[40,1024]{1,0:T(8,128)(2,1)S(1)}, u32[]{:S(2)}, u32[]{:S(2)}) collective-permute-start(bf16[40,1024]{1,0:T(8,128)(2,1)S(1)} %get-tuple-element.60), channel_id=1, source_target_pairs={{0,8},{8,4},{4,12},{12,0},{1,9},{9,5},{5,13},{13,1},{2,10},{10,6},... | collective-permute-start | bytes 245768 | tf_op jit(solution)/shard_map/ppermute | solution.py:311
  34.1 1.8 %collective-permute-start.12 = (bf16[40,1024]{1,0:T(8,128)(2,1)S(1)}, bf16[40,1024]{1,0:T(8,128)(2,1)S(1)}, u32[]{:S(2)}, u32[]{:S(2)}) collective-permute-start(bf16[40,1024]{1,0:T(8,128)(2,1)S(1)} %get-tuple-element.61), channel_id=1, source_target_pairs={{0,12},{8,0},{4,8},{12,4},{1,13},{9,1},{5,9},{13,5},{2,14},{10,2},... | collective-permute-start | bytes 245768 | tf_op jit(solution)/shard_map/ppermute | solution.py:311
  36.0 0.5 %collective-permute-start.13 = (bf16[40,1024]{1,0:T(8,128)(2,1)S(1)}, bf16[40,1024]{1,0:T(8,128)(2,1)S(1)}, u32[]{:S(2)}, u32[]{:S(2)}) collective-permute-start(bf16[40,1024]{1,0:T(8,128)(2,1)S(1)} %get-tuple-element.62), channel_id=1, source_target_pairs={{0,4},{8,12},{4,0},{12,8},{1,5},{9,13},{5,1},{13,9},{2,6},{10,14},... | collective-permute-start | bytes 245768 | tf_op jit(solution)/shard_map/ppermute | solution.py:311
  36.4 4.1 %shard_map.98 = (bf16[1,2,1536,1024]{3,2,1,0:T(8,128)(2,1)}, bf16[1,1536,1024]{2,1,0:T(8,128)(2,1)}) custom-call(bf16[80,768]{1,0:T(8,128)(2,1)S(1)} %get-tuple-element.59.mine_act, bf16[80,768]{1,0:T(8,128)(2,1)S(1)} %collective-permute-done.9._.other_act, bf16[2,80,768]{2,1,0:T(8,128)(2,1)S(1)} %shard_map.94.mine, ...), custom_call_target="tpu_custom_call" | custom-call | flops 754974720 | bytes 9437184 | tf_op jit(solution)/shard_map/pallas_call | solution.py:69
  40.5 1.6 %collective-permute-done.12.refs_1_ = bf16[40,1024]{1,0:T(8,128)(2,1)S(1)} collective-permute-done((bf16[40,1024]{1,0:T(8,128)(2,1)S(1)}, bf16[40,1024]{1,0:T(8,128)(2,1)S(1)}, u32[]{:S(2)}, u32[]{:S(2)}) %collective-permute-start.12) | collective-permute-done | bytes 81952 | tf_op jit(solution)/shard_map/ppermute | solution.py:311
  42.2 1.1 %shard_map.97 = bf16[256,1024]{1,0:T(8,128)(2,1)} custom-call(bf16[160,256]{1,0:T(8,128)(2,1)S(1)} %get-tuple-element.35.pick, bf16[40,1024]{1,0:T(8,128)(2,1)S(1)} %collective-permute-done.11.refs_0_, bf16[40,1024]{1,0:T(8,128)(2,1)S(1)} %collective-permute-done.12.refs_1_, bf16[40,1024]{1,0:T(8,128)(2,1)S(1)} %collective-permute-done.13.refs_2_, ...), custom_call_target="tpu_custom_call" | custom-call | flops 83886080 | bytes 1048576 | tf_op jit(solution)/shard_map/pallas_call | solution.py:69
  (19 shorter events, 2.1 us)
Async XLA Ops:
  2.0 13.1 %collective-permute-start.3 = (bf16[40,1024]{1,0:T(8,128)(2,1)S(1)}, bf16[40,1024]{1,0:T(8,128)(2,1)S(1)}, u32[]{:S(2)}, u32[]{:S(2)}) collective-permute-start(bf16[40,1024]{1,0:T(8,128)(2,1)S(1)} %get-tuple-element.46), channel_id=1, source_target_pairs={{0,8},{4,12},{8,0},{12,4},{1,9},{5,13},{9,1},{13,5},{2,10},{6,14},... | collective-permute-start | bytes 245768 | tf_op jit(solution)/shard_map/ppermute | solution.py:318
  6.1 9.0 %collective-permute-start.4 = (bf16[40,1024]{1,0:T(8,128)(2,1)S(1)}, bf16[40,1024]{1,0:T(8,128)(2,1)S(1)}, u32[]{:S(2)}, u32[]{:S(2)}) collective-permute-start(bf16[40,1024]{1,0:T(8,128)(2,1)S(1)} %get-tuple-element.47), channel_id=1, source_target_pairs={{0,12},{4,8},{8,4},{12,0},{1,13},{5,9},{9,5},{13,1},{2,14},{6,10},... | collective-permute-start | bytes 245768 | tf_op jit(solution)/shard_map/ppermute | solution.py:318
  7.7 7.6 %collective-permute-start.2 = (bf16[80,1024]{1,0:T(8,128)(2,1)S(1)}, bf16[80,1024]{1,0:T(8,128)(2,1)S(1)}, u32[]{:S(2)}, u32[]{:S(2)}) collective-permute-start(bf16[80,1024]{1,0:T(8,128)(2,1)S(1)} %get-tuple-element.44), channel_id=1, source_target_pairs={{0,4},{4,0},{8,12},{12,8},{1,5},{5,1},{9,13},{13,9},{2,6},{6,2},{1... | collective-permute-start | bytes 491528 | tf_op jit(solution)/shard_map/ppermute | solution.py:318
  11.8 8.4 %collective-permute-start = (bf16[40,1024]{1,0:T(8,128)(2,1)S(1)}, bf16[40,1024]{1,0:T(8,128)(2,1)S(1)}, u32[]{:S(2)}, u32[]{:S(2)}) collective-permute-start(bf16[40,1024]{1,0:T(8,128)(2,1)S(1)} %get-tuple-element.42), channel_id=1, source_target_pairs={{0,12},{4,8},{8,4},{12,0},{1,13},{5,9},{9,5},{13,1},{2,14},{6,10},... | collective-permute-start | bytes 245768 | tf_op jit(solution)/shard_map/ppermute | solution.py:318
  14.8 7.1 %collective-permute-start.1 = (bf16[40,1024]{1,0:T(8,128)(2,1)S(1)}, bf16[40,1024]{1,0:T(8,128)(2,1)S(1)}, u32[]{:S(2)}, u32[]{:S(2)}) collective-permute-start(bf16[40,1024]{1,0:T(8,128)(2,1)S(1)} %get-tuple-element.43), channel_id=1, source_target_pairs={{0,8},{4,12},{8,0},{12,4},{1,9},{5,13},{9,1},{13,5},{2,10},{6,14},... | collective-permute-start | bytes 245768 | tf_op jit(solution)/shard_map/ppermute | solution.py:318
  16.8 1.6 %collective-permute-start.5 = (bf16[2,80,768]{2,1,0:T(8,128)(2,1)S(1)}, bf16[2,80,768]{2,1,0:T(8,128)(2,1)S(1)}, u32[]{:S(2)}, u32[]{:S(2)}) collective-permute-start(bf16[2,80,768]{2,1,0:T(8,128)(2,1)S(1)} %get-tuple-element.54), channel_id=1, source_target_pairs={{0,1},{1,0},{2,3},{3,2},{4,5},{5,4},{6,7},{7,6},{8,9},{9,8},{10,11... | collective-permute-start | bytes 737288 | tf_op jit(solution)/shard_map/ppermute | solution.py:318
  18.5 8.1 %collective-permute-start.8 = (bf16[2,80,768]{2,1,0:T(8,128)(2,1)S(1)}, bf16[2,80,768]{2,1,0:T(8,128)(2,1)S(1)}, u32[]{:S(2)}, u32[]{:S(2)}) collective-permute-start(bf16[2,80,768]{2,1,0:T(8,128)(2,1)S(1)} %get-tuple-element.55.refs_6_), channel_id=1, source_target_pairs={{0,2},{1,3},{2,0},{3,1},{4,6},{5,7},{6,4},{7,5},{8,10},{9,11},{10,... | collective-permute-start | bytes 737288 | tf_op jit(solution)/shard_map/ppermute | solution.py:318
  22.7 1.4 %collective-permute-start.6 = (bf16[80,768]{1,0:T(8,128)(2,1)S(1)}, bf16[80,768]{1,0:T(8,128)(2,1)S(1)}, u32[]{:S(2)}, u32[]{:S(2)}) collective-permute-start(bf16[80,768]{1,0:T(8,128)(2,1)S(1)} %shard_map.92), channel_id=1, source_target_pairs={{0,1},{1,0},{2,3},{3,2},{4,5},{5,4},{6,7},{7,6},{8,9},{9,8},{10,11... | collective-permute-start | bytes 368648 | tf_op jit(solution)/shard_map/ppermute | solution.py:318
  24.1 5.4 %collective-permute-start.7 = (bf16[80,768]{1,0:T(8,128)(2,1)S(1)}, bf16[80,768]{1,0:T(8,128)(2,1)S(1)}, u32[]{:S(2)}, u32[]{:S(2)}) collective-permute-start(bf16[80,768]{1,0:T(8,128)(2,1)S(1)} %get-tuple-element.67), channel_id=1, source_target_pairs={{0,2},{1,3},{2,0},{3,1},{4,6},{5,7},{6,4},{7,5},{8,10},{9,11},{10,... | collective-permute-start | bytes 368648 | tf_op jit(solution)/shard_map/ppermute | solution.py:318
  26.7 2.9 %collective-permute-start.9 = (bf16[80,768]{1,0:T(8,128)(2,1)S(1)}, bf16[80,768]{1,0:T(8,128)(2,1)S(1)}, u32[]{:S(2)}, u32[]{:S(2)}) collective-permute-start(bf16[80,768]{1,0:T(8,128)(2,1)S(1)} %get-tuple-element.59.mine_act), channel_id=1, source_target_pairs={{0,1},{1,0},{2,3},{3,2},{4,5},{5,4},{6,7},{7,6},{8,9},{9,8},{10,11... | collective-permute-start | bytes 368648 | tf_op jit(solution)/shard_map/ppermute | solution.py:318
  29.6 1.6 %collective-permute-start.10 = (bf16[2,80,768]{2,1,0:T(8,128)(2,1)S(1)}, bf16[2,80,768]{2,1,0:T(8,128)(2,1)S(1)}, u32[]{:S(2)}, u32[]{:S(2)}) collective-permute-start(bf16[2,80,768]{2,1,0:T(8,128)(2,1)S(1)} %shard_map.94.mine), channel_id=1, source_target_pairs={{0,1},{1,0},{2,3},{3,2},{4,5},{5,4},{6,7},{7,6},{8,9},{9,8},{10,11... | collective-permute-start | bytes 737288 | tf_op jit(solution)/shard_map/ppermute | solution.py:318
  32.1 8.4 %collective-permute-start.11 = (bf16[40,1024]{1,0:T(8,128)(2,1)S(1)}, bf16[40,1024]{1,0:T(8,128)(2,1)S(1)}, u32[]{:S(2)}, u32[]{:S(2)}) collective-permute-start(bf16[40,1024]{1,0:T(8,128)(2,1)S(1)} %get-tuple-element.60), channel_id=1, source_target_pairs={{0,8},{8,4},{4,12},{12,0},{1,9},{9,5},{5,13},{13,1},{2,10},{10,6},... | collective-permute-start | bytes 245768 | tf_op jit(solution)/shard_map/ppermute | solution.py:311
  34.1 8.0 %collective-permute-start.12 = (bf16[40,1024]{1,0:T(8,128)(2,1)S(1)}, bf16[40,1024]{1,0:T(8,128)(2,1)S(1)}, u32[]{:S(2)}, u32[]{:S(2)}) collective-permute-start(bf16[40,1024]{1,0:T(8,128)(2,1)S(1)} %get-tuple-element.61), channel_id=1, source_target_pairs={{0,12},{8,0},{4,8},{12,4},{1,13},{9,1},{5,9},{13,5},{2,14},{10,2},... | collective-permute-start | bytes 245768 | tf_op jit(solution)/shard_map/ppermute | solution.py:311
  36.0 6.2 %collective-permute-start.13 = (bf16[40,1024]{1,0:T(8,128)(2,1)S(1)}, bf16[40,1024]{1,0:T(8,128)(2,1)S(1)}, u32[]{:S(2)}, u32[]{:S(2)}) collective-permute-start(bf16[40,1024]{1,0:T(8,128)(2,1)S(1)} %get-tuple-element.62), channel_id=1, source_target_pairs={{0,4},{8,12},{4,0},{12,8},{1,5},{9,13},{5,1},{13,9},{2,6},{10,14},... | collective-permute-start | bytes 245768 | tf_op jit(solution)/shard_map/ppermute | solution.py:311

commit v19 on v18

--- a/solution.py
+++ b/solution.py
@@ -14,7 +14,8 @@
 F32 = jnp.float32
 MIB = 1 << 20
 C2COST = 100
-WCOST = 100
+C0COST = 4.75
+WCOST = 1
 GFLOP = 100
 D1COST = 1
 D2COST = 100
@@ -142,6 +143,10 @@
     return pl.ds(pl.multiple_of((core if own else 1 - core) * half, 128), half)
 
 
+def early_rows(first, out):
+    out[...] = first[...]
+
+
 def place_rows(experts, capacity, pieces):
     me = lax.axis_index("ex")
     rows = experts * MOST
@@ -197,8 +202,7 @@
 
 def act_part(experts, own, *refs):
     place, held = refs[experts : experts + 2]
-    pieces = refs[: experts - 2][::-1] + refs[experts - 2 : experts]
-    rows_grad = mm(place[...], stacked(pieces, 1).astype(BF), ROWS).astype(BF)
+    rows_grad = mm(place[...], stacked(refs[:experts], 1).astype(BF), ROWS).astype(BF)
     if own:
         refs[-2][...] = rows_grad
     refs[-1][...] = mm(rows_grad, held[2], LANES).astype(BF)
@@ -286,15 +290,11 @@
 
 
 def tour(count):
-    bits = count.bit_length() - 1
-    return [sum(((i >> b) & 1) << (bits - 1 - b) for b in range(bits)) for i in range(count)]
+    return list(range(count))
 
 
 def steps(count):
-    found = []
-    for step in range(1, count // 2 + 1):
-        found += [step, count - step]
-    return list(dict.fromkeys(found)) + [0]
+    return list(range(1, count)) + [0]
 
 
 def ahead(step, count):
@@ -367,6 +367,14 @@
     )
     near = swap(near, "ex", 1)
     got_in = [swap(part, "ex", k) for part, k in zip(send_in[:-1], order)] + [near, own_in]
+    got_in[0] = call(
+        early_rows,
+        piece[0],
+        (got_in[0],),
+        [VMEM],
+        flops=int(C0COST * weight_flops),
+        traffic=weight_bytes,
+    )
     held_other, held_mine, *send_grad = call(
         functools.partial(stage, experts - 1),
         [pltpu.VMEM((3, half, width), BF)] * 2 + piece[1:],
@@ -376,7 +384,7 @@
         flops=WCOST * weight_flops,
         traffic=WCOST * weight_bytes,
     )
-    got_grad = [swap(part, "ex", k) for part, k in zip(send_grad[:-1], order)][::-1]
+    got_grad = [swap(part, "ex", k) for part, k in zip(send_grad[:-1], order)]
     got_grad = got_grad + [near, send_grad[-1]]
     pair_other, place, rows_in = call(
         functools.partial(other_pair, experts, capacity),

time: 43.5 us -> 43.4 us (level)
  waiting for transfers between devices: 9.14 us -> 8.02 us
  starting transfers between devices: 17 us -> 18 us
    ppermute x3, waiting for transfers between devices: 1.63 us -> 0.92 us  [shift(): lax.ppermute(value, axis, [(name, names[(at + step) % count]) for at, nam...]
    ppermute x3, starting transfers between devices: 4.33 us -> 4.92 us  [shift(): lax.ppermute(value, axis, [(name, names[(at + step) % count]) for at, nam...]
    ppermute x11, starting transfers between devices: 12.6 us -> 13.1 us  [swap(): return lax.ppermute(value, axis, [(i, i ^ bit) for i in range(count)])]
    pallas_call x14 -> x15, Pallas kernels: 16.3 us -> 16.4 us  [call(): pl.pallas_call(body, out_shape=outs, in_specs=specs, out_specs=out_specs...]
  transfers between devices with their start and end apart: 14 -> 14, of which waited for: 8 -> 7; matrix products, arithmetic and copies ran while one was open for 0% -> 0% of each run, Pallas kernels for 30% -> 30%
where the time goes in v19:
time: 43.4 us; the launch traced here: 43.2 us
  starting transfers between devices  18 us (41%)
  Pallas kernels  16.4 us (38%)
  waiting for transfers between devices  8.02 us (18%)
  between operations  0.77 us (2%)
    pallas_call x15, Pallas kernels, call(): pl.pallas_call(body, out_shape=outs, in_specs=specs, out_specs=out_specs...  16.4 us
    ppermute x11, starting transfers between devices, swap(): return lax.ppermute(value, axis, [(i, i ^ bit) for i in range(count)])  13.1 us
    ppermute x11, waiting for transfers between devices, swap(): return lax.ppermute(value, axis, [(i, i ^ bit) for i in range(count)])  7.11 us
    ppermute x3, starting transfers between devices, shift(): lax.ppermute(value, axis, [(name, names[(at + step) % count]) for at, nam...  4.92 us
    ppermute x3, waiting for transfers between devices, shift(): lax.ppermute(value, axis, [(name, names[(at + step) % count]) for at, nam...  0.92 us
  transfers between devices with their start and end apart: 14, of which 7 were waited for; matrix products, arithmetic and copies ran while one was open for 0% of the time, Pallas kernels for 30%

profile of v19, /device:TPU:0, one launch (start us, length us, event | category | flops | bytes accessed | tf_op | source)
XLA Modules:
  0.0 43.2 jit_solution(6910128084418759810)
XLA Ops:
  0.6 1.4 %shard_map.85 = (bf16[160,256]{1,0:T(8,128)(2,1)S(1)}, f32[160,1]{1,0:T(8,128)S(1)}, bf16[256,1024]{1,0:T(8,128)(2,1)S(1)}, bf16[40,1024]{1,0:T(8,128)(2,1)S(1)}...) custom-call(s32[8,256]{1,0:T(8,128)} %bitcast.2, ...), custom_call_target="tpu_custom_call" | custom-call | flops 83886080 | bytes 1048576 | tf_op jit(solution)/shard_map/pallas_call | solution.py:70
  2.0 4.1 %collective-permute-start.3 = (bf16[40,1024]{1,0:T(8,128)(2,1)S(1)}, bf16[40,1024]{1,0:T(8,128)(2,1)S(1)}, u32[]{:S(2)}, u32[]{:S(2)}) collective-permute-start(bf16[40,1024]{1,0:T(8,128)(2,1)S(1)} %get-tuple-element.46), channel_id=1, source_target_pairs={{0,8},{4,12},{8,0},{12,4},{1,9},{5,13},{9,1},{13,5},{2,10},{6,14},... | collective-permute-start | bytes 245768 | tf_op jit(solution)/shard_map/ppermute | solution.py:318
  6.4 1.6 %collective-permute-start.2 = (bf16[80,1024]{1,0:T(8,128)(2,1)S(1)}, bf16[80,1024]{1,0:T(8,128)(2,1)S(1)}, u32[]{:S(2)}, u32[]{:S(2)}) collective-permute-start(bf16[80,1024]{1,0:T(8,128)(2,1)S(1)} %get-tuple-element.44), channel_id=1, source_target_pairs={{0,4},{4,0},{8,12},{12,8},{1,5},{5,1},{9,13},{13,9},{2,6},{6,2},{1... | collective-permute-start | bytes 491528 | tf_op jit(solution)/shard_map/ppermute | solution.py:318
  8.0 3.8 %shard_map.87 = (bf16[3,768,1024]{2,1,0:T(8,128)(2,1)S(1)}, bf16[3,768,1024]{2,1,0:T(8,128)(2,1)S(1)}, bf16[40,1024]{1,0:T(8,128)(2,1)S(1)}, bf16[40,1024]{1,0:T(8,128)(2,1)S(1)}, bf16[40,1024]{1,0:T(8,128)(2,1)S(1)}) custom-call(bf16[1,2,1536,1024]{3,2,1,0:T(8,128)(2,1)} %gate_up.1, bf16[1,1536,1024]{2,1,0:T(8,128)(2,1)} %down.1, ...), custom_call_target="tpu_custom_call" | custom-call | flops 251658240 | bytes 3145728 | tf_op jit(solution)/shard_map/pallas_call | solution.py:70
  11.8 2.0 %collective-permute-start = (bf16[40,1024]{1,0:T(8,128)(2,1)S(1)}, bf16[40,1024]{1,0:T(8,128)(2,1)S(1)}, u32[]{:S(2)}, u32[]{:S(2)}) collective-permute-start(bf16[40,1024]{1,0:T(8,128)(2,1)S(1)} %get-tuple-element.42), channel_id=1, source_target_pairs={{0,8},{4,12},{8,0},{12,4},{1,9},{5,13},{9,1},{13,5},{2,10},{6,14},... | collective-permute-start | bytes 245768 | tf_op jit(solution)/shard_map/ppermute | solution.py:318
  13.8 2.0 %collective-permute-start.1 = (bf16[40,1024]{1,0:T(8,128)(2,1)S(1)}, bf16[40,1024]{1,0:T(8,128)(2,1)S(1)}, u32[]{:S(2)}, u32[]{:S(2)}) collective-permute-start(bf16[40,1024]{1,0:T(8,128)(2,1)S(1)} %get-tuple-element.43), channel_id=1, source_target_pairs={{0,12},{4,8},{8,4},{12,0},{1,13},{5,9},{9,5},{13,1},{2,14},{6,10},... | collective-permute-start | bytes 245768 | tf_op jit(solution)/shard_map/ppermute | solution.py:318
  15.8 1.4 %shard_map.89 = (bf16[2,80,768]{2,1,0:T(8,128)(2,1)S(1)}, bf16[160,80]{1,0:T(8,128)(2,1)S(1)}, bf16[80,1024]{1,0:T(8,128)(2,1)S(1)}) custom-call(bf16[40,1024]{1,0:T(8,128)(2,1)S(1)} %shard_map.88.refs_0_, bf16[40,1024]{1,0:T(8,128)(2,1)S(1)} %collective-permute-done.4.refs_1_, bf16[80,1024]{1,0:T(8,128)(2,1)S(1)} %collective-permute-done.2.refs_2_, ...), custom_call_target="tpu_custom_call" | custom-call | flops 503316480 | bytes 3145728 | tf_op jit(solution)/shard_map/pallas_call | solution.py:70
  17.4 1.1 %shard_map.91.mine = bf16[2,80,768]{2,1,0:T(8,128)(2,1)S(1)} custom-call(bf16[80,1024]{1,0:T(8,128)(2,1)S(1)} %get-tuple-element.53.rows_in, bf16[3,768,1024]{2,1,0:T(8,128)(2,1)S(1)} %get-tuple-element.51.refs_5_.held), custom_call_target="tpu_custom_call" | custom-call | flops 25165824000 | bytes 314572800 | tf_op jit(solution)/shard_map/pallas_call | solution.py:70
  18.9 1.6 %collective-permute-start.8 = (bf16[2,80,768]{2,1,0:T(8,128)(2,1)S(1)}, bf16[2,80,768]{2,1,0:T(8,128)(2,1)S(1)}, u32[]{:S(2)}, u32[]{:S(2)}) collective-permute-start(bf16[2,80,768]{2,1,0:T(8,128)(2,1)S(1)} %get-tuple-element.55.refs_6_), channel_id=1, source_target_pairs={{0,2},{1,3},{2,0},{3,1},{4,6},{5,7},{6,4},{7,5},{8,10},{9,11},{10,... | collective-permute-start | bytes 737288 | tf_op jit(solution)/shard_map/ppermute | solution.py:318
  20.8 0.7 %shard_map.93 = bf16[80,768]{1,0:T(8,128)(2,1)S(1)} custom-call(bf16[40,1024]{1,0:T(8,128)(2,1)S(1)} %collective-permute-done.refs_0_, bf16[40,1024]{1,0:T(8,128)(2,1)S(1)} %collective-permute-done.1.refs_1_, bf16[80,1024]{1,0:T(8,128)(2,1)S(1)} %collective-permute-done.2.refs_2_, bf16[40,1024]{1,0:T(8,128)(2,1)S(1)} %get-tuple-element.45.refs_3_, ...), custom_call_target="tpu_custom_call" | custom-call | flops 251658240 | bytes 3145728 | tf_op jit(solution)/shard_map/pallas_call | solution.py:70
  21.6 0.7 %shard_map.90 = (bf16[80,1024]{1,0:T(8,128)(2,1)S(1)}, bf16[80,768]{1,0:T(8,128)(2,1)S(1)}) custom-call(bf16[40,1024]{1,0:T(8,128)(2,1)S(1)} %collective-permute-done.refs_0_, bf16[40,1024]{1,0:T(8,128)(2,1)S(1)} %collective-permute-done.1.refs_1_, bf16[80,1024]{1,0:T(8,128)(2,1)S(1)} %collective-permute-done.2.refs_2_, ...), custom_call_target="tpu_custom_call" | custom-call | flops 25165824000 | bytes 314572800 | tf_op jit(solution)/shard_map/pallas_call | solution.py:70
  22.3 0.6 %collective-permute-done.6 = bf16[80,768]{1,0:T(8,128)(2,1)S(1)} collective-permute-done((bf16[80,768]{1,0:T(8,128)(2,1)S(1)}, bf16[80,768]{1,0:T(8,128)(2,1)S(1)}, u32[]{:S(2)}, u32[]{:S(2)}) %collective-permute-start.6) | collective-permute-done | bytes 122912 | tf_op jit(solution)/shard_map/ppermute | solution.py:318
  22.9 1.6 %collective-permute-start.7 = (bf16[80,768]{1,0:T(8,128)(2,1)S(1)}, bf16[80,768]{1,0:T(8,128)(2,1)S(1)}, u32[]{:S(2)}, u32[]{:S(2)}) collective-permute-start(bf16[80,768]{1,0:T(8,128)(2,1)S(1)} %get-tuple-element.67), channel_id=1, source_target_pairs={{0,2},{1,3},{2,0},{3,1},{4,6},{5,7},{6,4},{7,5},{8,10},{9,11},{10,... | collective-permute-start | bytes 368648 | tf_op jit(solution)/shard_map/ppermute | solution.py:318
  24.5 3.3 %collective-permute-done.8.pair_far = bf16[2,80,768]{2,1,0:T(8,128)(2,1)S(1)} collective-permute-done((bf16[2,80,768]{2,1,0:T(8,128)(2,1)S(1)}, bf16[2,80,768]{2,1,0:T(8,128)(2,1)S(1)}, u32[]{:S(2)}, u32[]{:S(2)}) %collective-permute-start.8) | collective-permute-done | bytes 245792 | tf_op jit(solution)/shard_map/ppermute | solution.py:318
  28.0 1.6 %collective-permute-done.7.act_far = bf16[80,768]{1,0:T(8,128)(2,1)S(1)} collective-permute-done((bf16[80,768]{1,0:T(8,128)(2,1)S(1)}, bf16[80,768]{1,0:T(8,128)(2,1)S(1)}, u32[]{:S(2)}, u32[]{:S(2)}) %collective-permute-start.7) | collective-permute-done | bytes 122912 | tf_op jit(solution)/shard_map/ppermute | solution.py:318
  29.8 0.7 %shard_map.96.total = f32[80,1024]{1,0:T(8,128)S(1)} custom-call(bf16[2,80,768]{2,1,0:T(8,128)(2,1)S(1)} %shard_map.95.mine, bf16[3,768,1024]{2,1,0:T(8,128)(2,1)S(1)} %get-tuple-element.51.refs_5_.held), custom_call_target="tpu_custom_call" | custom-call | flops 251658240 | bytes 3145728 | tf_op jit(solution)/shard_map/pallas_call | solution.py:70
  30.4 0.8 %collective-permute-done.10.other = bf16[2,80,768]{2,1,0:T(8,128)(2,1)S(1)} collective-permute-done((bf16[2,80,768]{2,1,0:T(8,128)(2,1)S(1)}, bf16[2,80,768]{2,1,0:T(8,128)(2,1)S(1)}, u32[]{:S(2)}, u32[]{:S(2)}) %collective-permute-start.10) | collective-permute-done | bytes 245792 | tf_op jit(solution)/shard_map/ppermute | solution.py:318
  31.3 0.9 %shard_map.97 = (bf16[40,1024]{1,0:T(8,128)(2,1)S(1)}, bf16[40,1024]{1,0:T(8,128)(2,1)S(1)}, bf16[40,1024]{1,0:T(8,128)(2,1)S(1)}, bf16[40,1024]{1,0:T(8,128)(2,1)S(1)}) custom-call(f32[80,1024]{1,0:T(8,128)S(1)} %shard_map.96.total, bf16[2,80,768]{2,1,0:T(8,128)(2,1)S(1)} %collective-permute-done.10.other, ...), custom_call_target="tpu_custom_call" | custom-call | flops 251658240 | bytes 3145728 | tf_op jit(solution)/shard_map/pallas_call | solution.py:70
  32.2 0.5 %collective-permute-start.11 = (bf16[40,1024]{1,0:T(8,128)(2,1)S(1)}, bf16[40,1024]{1,0:T(8,128)(2,1)S(1)}, u32[]{:S(2)}, u32[]{:S(2)}) collective-permute-start(bf16[40,1024]{1,0:T(8,128)(2,1)S(1)} %get-tuple-element.60), channel_id=1, source_target_pairs={{0,4},{4,8},{8,12},{12,0},{1,5},{5,9},{9,13},{13,1},{2,6},{6,10},{... | collective-permute-start | bytes 245768 | tf_op jit(solution)/shard_map/ppermute | solution.py:311
  32.7 2.2 %collective-permute-start.12 = (bf16[40,1024]{1,0:T(8,128)(2,1)S(1)}, bf16[40,1024]{1,0:T(8,128)(2,1)S(1)}, u32[]{:S(2)}, u32[]{:S(2)}) collective-permute-start(bf16[40,1024]{1,0:T(8,128)(2,1)S(1)} %get-tuple-element.61), channel_id=1, source_target_pairs={{0,8},{4,12},{8,0},{12,4},{1,9},{5,13},{9,1},{13,5},{2,10},{6,14},... | collective-permute-start | bytes 245768 | tf_op jit(solution)/shard_map/ppermute | solution.py:311
  34.9 2.1 %collective-permute-start.13 = (bf16[40,1024]{1,0:T(8,128)(2,1)S(1)}, bf16[40,1024]{1,0:T(8,128)(2,1)S(1)}, u32[]{:S(2)}, u32[]{:S(2)}) collective-permute-start(bf16[40,1024]{1,0:T(8,128)(2,1)S(1)} %get-tuple-element.62), channel_id=1, source_target_pairs={{0,12},{4,0},{8,4},{12,8},{1,13},{5,1},{9,5},{13,9},{2,14},{6,2},{... | collective-permute-start | bytes 245768 | tf_op jit(solution)/shard_map/ppermute | solution.py:311
  37.1 4.1 %shard_map.99 = (bf16[1,2,1536,1024]{3,2,1,0:T(8,128)(2,1)}, bf16[1,1536,1024]{2,1,0:T(8,128)(2,1)}) custom-call(bf16[80,768]{1,0:T(8,128)(2,1)S(1)} %get-tuple-element.59.mine_act, bf16[80,768]{1,0:T(8,128)(2,1)S(1)} %collective-permute-done.9._.other_act, bf16[2,80,768]{2,1,0:T(8,128)(2,1)S(1)} %shard_map.95.mine, ...), custom_call_target="tpu_custom_call" | custom-call | flops 754974720 | bytes 9437184 | tf_op jit(solution)/shard_map/pallas_call | solution.py:70
  41.2 0.9 %collective-permute-done.12.refs_1_ = bf16[40,1024]{1,0:T(8,128)(2,1)S(1)} collective-permute-done((bf16[40,1024]{1,0:T(8,128)(2,1)S(1)}, bf16[40,1024]{1,0:T(8,128)(2,1)S(1)}, u32[]{:S(2)}, u32[]{:S(2)}) %collective-permute-start.12) | collective-permute-done | bytes 81952 | tf_op jit(solution)/shard_map/ppermute | solution.py:311
  42.1 1.1 %shard_map.98 = bf16[256,1024]{1,0:T(8,128)(2,1)} custom-call(bf16[160,256]{1,0:T(8,128)(2,1)S(1)} %get-tuple-element.35.pick, bf16[40,1024]{1,0:T(8,128)(2,1)S(1)} %collective-permute-done.11.refs_0_, bf16[40,1024]{1,0:T(8,128)(2,1)S(1)} %collective-permute-done.12.refs_1_, bf16[40,1024]{1,0:T(8,128)(2,1)S(1)} %collective-permute-done.13.refs_2_, ...), custom_call_target="tpu_custom_call" | custom-call | flops 83886080 | bytes 1048576 | tf_op jit(solution)/shard_map/pallas_call | solution.py:70
  (20 shorter events, 1.6 us)
Async XLA Ops:
  2.0 13.8 %collective-permute-start.3 = (bf16[40,1024]{1,0:T(8,128)(2,1)S(1)}, bf16[40,1024]{1,0:T(8,128)(2,1)S(1)}, u32[]{:S(2)}, u32[]{:S(2)}) collective-permute-start(bf16[40,1024]{1,0:T(8,128)(2,1)S(1)} %get-tuple-element.46), channel_id=1, source_target_pairs={{0,8},{4,12},{8,0},{12,4},{1,9},{5,13},{9,1},{13,5},{2,10},{6,14},... | collective-permute-start | bytes 245768 | tf_op jit(solution)/shard_map/ppermute | solution.py:318
  6.4 9.4 %collective-permute-start.2 = (bf16[80,1024]{1,0:T(8,128)(2,1)S(1)}, bf16[80,1024]{1,0:T(8,128)(2,1)S(1)}, u32[]{:S(2)}, u32[]{:S(2)}) collective-permute-start(bf16[80,1024]{1,0:T(8,128)(2,1)S(1)} %get-tuple-element.44), channel_id=1, source_target_pairs={{0,4},{4,0},{8,12},{12,8},{1,5},{5,1},{9,13},{13,9},{2,6},{6,2},{1... | collective-permute-start | bytes 491528 | tf_op jit(solution)/shard_map/ppermute | solution.py:318
  8.0 7.8 %collective-permute-start.4 = (bf16[40,1024]{1,0:T(8,128)(2,1)S(1)}, bf16[40,1024]{1,0:T(8,128)(2,1)S(1)}, u32[]{:S(2)}, u32[]{:S(2)}) collective-permute-start(bf16[40,1024]{1,0:T(8,128)(2,1)S(1)} %get-tuple-element.47), channel_id=1, source_target_pairs={{0,12},{4,8},{8,4},{12,0},{1,13},{5,9},{9,5},{13,1},{2,14},{6,10},... | collective-permute-start | bytes 245768 | tf_op jit(solution)/shard_map/ppermute | solution.py:318
  11.8 8.9 %collective-permute-start = (bf16[40,1024]{1,0:T(8,128)(2,1)S(1)}, bf16[40,1024]{1,0:T(8,128)(2,1)S(1)}, u32[]{:S(2)}, u32[]{:S(2)}) collective-permute-start(bf16[40,1024]{1,0:T(8,128)(2,1)S(1)} %get-tuple-element.42), channel_id=1, source_target_pairs={{0,8},{4,12},{8,0},{12,4},{1,9},{5,13},{9,1},{13,5},{2,10},{6,14},... | collective-permute-start | bytes 245768 | tf_op jit(solution)/shard_map/ppermute | solution.py:318
  13.8 7.0 %collective-permute-start.1 = (bf16[40,1024]{1,0:T(8,128)(2,1)S(1)}, bf16[40,1024]{1,0:T(8,128)(2,1)S(1)}, u32[]{:S(2)}, u32[]{:S(2)}) collective-permute-start(bf16[40,1024]{1,0:T(8,128)(2,1)S(1)} %get-tuple-element.43), channel_id=1, source_target_pairs={{0,12},{4,8},{8,4},{12,0},{1,13},{5,9},{9,5},{13,1},{2,14},{6,10},... | collective-permute-start | bytes 245768 | tf_op jit(solution)/shard_map/ppermute | solution.py:318
  17.3 1.6 %collective-permute-start.5 = (bf16[2,80,768]{2,1,0:T(8,128)(2,1)S(1)}, bf16[2,80,768]{2,1,0:T(8,128)(2,1)S(1)}, u32[]{:S(2)}, u32[]{:S(2)}) collective-permute-start(bf16[2,80,768]{2,1,0:T(8,128)(2,1)S(1)} %get-tuple-element.54), channel_id=1, source_target_pairs={{0,1},{1,0},{2,3},{3,2},{4,5},{5,4},{6,7},{7,6},{8,9},{9,8},{10,11... | collective-permute-start | bytes 737288 | tf_op jit(solution)/shard_map/ppermute | solution.py:318
  18.9 8.9 %collective-permute-start.8 = (bf16[2,80,768]{2,1,0:T(8,128)(2,1)S(1)}, bf16[2,80,768]{2,1,0:T(8,128)(2,1)S(1)}, u32[]{:S(2)}, u32[]{:S(2)}) collective-permute-start(bf16[2,80,768]{2,1,0:T(8,128)(2,1)S(1)} %get-tuple-element.55.refs_6_), channel_id=1, source_target_pairs={{0,2},{1,3},{2,0},{3,1},{4,6},{5,7},{6,4},{7,5},{8,10},{9,11},{10,... | collective-permute-start | bytes 737288 | tf_op jit(solution)/shard_map/ppermute | solution.py:318
  21.5 1.4 %collective-permute-start.6 = (bf16[80,768]{1,0:T(8,128)(2,1)S(1)}, bf16[80,768]{1,0:T(8,128)(2,1)S(1)}, u32[]{:S(2)}, u32[]{:S(2)}) collective-permute-start(bf16[80,768]{1,0:T(8,128)(2,1)S(1)} %shard_map.93), channel_id=1, source_target_pairs={{0,1},{1,0},{2,3},{3,2},{4,5},{5,4},{6,7},{7,6},{8,9},{9,8},{10,11... | collective-permute-start | bytes 368648 | tf_op jit(solution)/shard_map/ppermute | solution.py:318
  22.9 6.7 %collective-permute-start.7 = (bf16[80,768]{1,0:T(8,128)(2,1)S(1)}, bf16[80,768]{1,0:T(8,128)(2,1)S(1)}, u32[]{:S(2)}, u32[]{:S(2)}) collective-permute-start(bf16[80,768]{1,0:T(8,128)(2,1)S(1)} %get-tuple-element.67), channel_id=1, source_target_pairs={{0,2},{1,3},{2,0},{3,1},{4,6},{5,7},{6,4},{7,5},{8,10},{9,11},{10,... | collective-permute-start | bytes 368648 | tf_op jit(solution)/shard_map/ppermute | solution.py:318
  27.9 1.7 %collective-permute-start.9 = (bf16[80,768]{1,0:T(8,128)(2,1)S(1)}, bf16[80,768]{1,0:T(8,128)(2,1)S(1)}, u32[]{:S(2)}, u32[]{:S(2)}) collective-permute-start(bf16[80,768]{1,0:T(8,128)(2,1)S(1)} %get-tuple-element.59.mine_act), channel_id=1, source_target_pairs={{0,1},{1,0},{2,3},{3,2},{4,5},{5,4},{6,7},{7,6},{8,9},{9,8},{10,11... | collective-permute-start | bytes 368648 | tf_op jit(solution)/shard_map/ppermute | solution.py:318
  29.7 1.6 %collective-permute-start.10 = (bf16[2,80,768]{2,1,0:T(8,128)(2,1)S(1)}, bf16[2,80,768]{2,1,0:T(8,128)(2,1)S(1)}, u32[]{:S(2)}, u32[]{:S(2)}) collective-permute-start(bf16[2,80,768]{2,1,0:T(8,128)(2,1)S(1)} %shard_map.95.mine), channel_id=1, source_target_pairs={{0,1},{1,0},{2,3},{3,2},{4,5},{5,4},{6,7},{7,6},{8,9},{9,8},{10,11... | collective-permute-start | bytes 737288 | tf_op jit(solution)/shard_map/ppermute | solution.py:318
  32.2 9.0 %collective-permute-start.11 = (bf16[40,1024]{1,0:T(8,128)(2,1)S(1)}, bf16[40,1024]{1,0:T(8,128)(2,1)S(1)}, u32[]{:S(2)}, u32[]{:S(2)}) collective-permute-start(bf16[40,1024]{1,0:T(8,128)(2,1)S(1)} %get-tuple-element.60), channel_id=1, source_target_pairs={{0,4},{4,8},{8,12},{12,0},{1,5},{5,9},{9,13},{13,1},{2,6},{6,10},{... | collective-permute-start | bytes 245768 | tf_op jit(solution)/shard_map/ppermute | solution.py:311
  32.7 9.4 %collective-permute-start.12 = (bf16[40,1024]{1,0:T(8,128)(2,1)S(1)}, bf16[40,1024]{1,0:T(8,128)(2,1)S(1)}, u32[]{:S(2)}, u32[]{:S(2)}) collective-permute-start(bf16[40,1024]{1,0:T(8,128)(2,1)S(1)} %get-tuple-element.61), channel_id=1, source_target_pairs={{0,8},{4,12},{8,0},{12,4},{1,9},{5,13},{9,1},{13,5},{2,10},{6,14},... | collective-permute-start | bytes 245768 | tf_op jit(solution)/shard_map/ppermute | solution.py:311
  34.9 7.2 %collective-permute-start.13 = (bf16[40,1024]{1,0:T(8,128)(2,1)S(1)}, bf16[40,1024]{1,0:T(8,128)(2,1)S(1)}, u32[]{:S(2)}, u32[]{:S(2)}) collective-permute-start(bf16[40,1024]{1,0:T(8,128)(2,1)S(1)} %get-tuple-element.62), channel_id=1, source_target_pairs={{0,12},{4,0},{8,4},{12,8},{1,13},{5,1},{9,5},{13,9},{2,14},{6,2},{... | collective-permute-start | bytes 245768 | tf_op jit(solution)/shard_map/ppermute | solution.py:311

commit v20 on v19

--- a/solution.py
+++ b/solution.py
@@ -16,6 +16,7 @@
 C2COST = 100
 C0COST = 4.75
 WCOST = 1
+CUTS = 3
 GFLOP = 100
 D1COST = 1
 D2COST = 100
@@ -173,7 +174,7 @@
         rows = rows_of(half, own == 1)
         for matrix in range(3):
             source = down.at[0, rows] if matrix == 2 else gate_up.at[0, matrix, rows]
-            loads.append(pltpu.make_async_copy(source, out.at[matrix], sems.at[len(loads)]))
+            loads += cut(source, out.at[matrix], sems, len(loads), CUTS)
     run(loads)
     for source, target in zip(pieces, pieces_out):
         target[...] = source[...]
@@ -380,7 +381,7 @@
         [pltpu.VMEM((3, half, width), BF)] * 2 + piece[1:],
         (far(gate_up), far(down_proj), *send_grad),
         [HBM] * 2 + [VMEM] * (experts - 1),
-        [dma(6)],
+        [dma(6 * CUTS)],
         flops=WCOST * weight_flops,
         traffic=WCOST * weight_bytes,
     )
@@ -484,7 +485,7 @@
         sds((tokens, width), BF),
         (pick, *home),
         [VMEM] * (experts + 1),
-        [pltpu.VMEM((rows, width), F32), pltpu.VMEM((2, tokens // 2, width), BF), dma(2)],
+        [pltpu.VMEM((rows, width), F32), pltpu.VMEM((4, tokens // 4, width), BF), dma(4)],
         flops=2 * rows * tokens * width,
         traffic=4 * tokens * width,
         out_specs=ANY,

time: 43.4 us -> 43.5 us (level)
  no operation moved by 1% of the time
where the time goes in v20:
time: 43.5 us; the launch traced here: 43.3 us
  starting transfers between devices  18 us (41%)
  Pallas kernels  16.4 us (38%)
  waiting for transfers between devices  8.03 us (18%)
  between operations  0.77 us (2%)
    pallas_call x15, Pallas kernels, call(): pl.pallas_call(body, out_shape=outs, in_specs=specs, out_specs=out_specs...  16.4 us
    ppermute x11, starting transfers between devices, swap(): return lax.ppermute(value, axis, [(i, i ^ bit) for i in range(count)])  13.1 us
    ppermute x11, waiting for transfers between devices, swap(): return lax.ppermute(value, axis, [(i, i ^ bit) for i in range(count)])  7.11 us
    ppermute x3, starting transfers between devices, shift(): lax.ppermute(value, axis, [(name, names[(at + step) % count]) for at, nam...  4.92 us
    ppermute x3, waiting for transfers between devices, shift(): lax.ppermute(value, axis, [(name, names[(at + step) % count]) for at, nam...  0.92 us
  transfers between devices with their start and end apart: 14, of which 7 were waited for; matrix products, arithmetic and copies ran while one was open for 0% of the time, Pallas kernels for 30%

profile of v20, /device:TPU:0, one launch (start us, length us, event | category | flops | bytes accessed | tf_op | source)
XLA Modules:
  0.0 43.3 jit_solution(6900344373033047200)
XLA Ops:
  0.6 1.4 %shard_map.85 = (bf16[160,256]{1,0:T(8,128)(2,1)S(1)}, f32[160,1]{1,0:T(8,128)S(1)}, bf16[256,1024]{1,0:T(8,128)(2,1)S(1)}, bf16[40,1024]{1,0:T(8,128)(2,1)S(1)}...) custom-call(s32[8,256]{1,0:T(8,128)} %bitcast.2, ...), custom_call_target="tpu_custom_call" | custom-call | flops 83886080 | bytes 1048576 | tf_op jit(solution)/shard_map/pallas_call | solution.py:71
  2.0 4.1 %collective-permute-start.3 = (bf16[40,1024]{1,0:T(8,128)(2,1)S(1)}, bf16[40,1024]{1,0:T(8,128)(2,1)S(1)}, u32[]{:S(2)}, u32[]{:S(2)}) collective-permute-start(bf16[40,1024]{1,0:T(8,128)(2,1)S(1)} %get-tuple-element.46), channel_id=1, source_target_pairs={{0,8},{4,12},{8,0},{12,4},{1,9},{5,13},{9,1},{13,5},{2,10},{6,14},... | collective-permute-start | bytes 245768 | tf_op jit(solution)/shard_map/ppermute | solution.py:319
  6.4 1.6 %collective-permute-start.2 = (bf16[80,1024]{1,0:T(8,128)(2,1)S(1)}, bf16[80,1024]{1,0:T(8,128)(2,1)S(1)}, u32[]{:S(2)}, u32[]{:S(2)}) collective-permute-start(bf16[80,1024]{1,0:T(8,128)(2,1)S(1)} %get-tuple-element.44), channel_id=1, source_target_pairs={{0,4},{4,0},{8,12},{12,8},{1,5},{5,1},{9,13},{13,9},{2,6},{6,2},{1... | collective-permute-start | bytes 491528 | tf_op jit(solution)/shard_map/ppermute | solution.py:319
  8.0 3.8 %shard_map.87 = (bf16[3,768,1024]{2,1,0:T(8,128)(2,1)S(1)}, bf16[3,768,1024]{2,1,0:T(8,128)(2,1)S(1)}, bf16[40,1024]{1,0:T(8,128)(2,1)S(1)}, bf16[40,1024]{1,0:T(8,128)(2,1)S(1)}, bf16[40,1024]{1,0:T(8,128)(2,1)S(1)}) custom-call(bf16[1,2,1536,1024]{3,2,1,0:T(8,128)(2,1)} %gate_up.1, bf16[1,1536,1024]{2,1,0:T(8,128)(2,1)} %down.1, ...), custom_call_target="tpu_custom_call" | custom-call | flops 251658240 | bytes 3145728 | tf_op jit(solution)/shard_map/pallas_call | solution.py:71
  11.9 2.0 %collective-permute-start = (bf16[40,1024]{1,0:T(8,128)(2,1)S(1)}, bf16[40,1024]{1,0:T(8,128)(2,1)S(1)}, u32[]{:S(2)}, u32[]{:S(2)}) collective-permute-start(bf16[40,1024]{1,0:T(8,128)(2,1)S(1)} %get-tuple-element.42), channel_id=1, source_target_pairs={{0,8},{4,12},{8,0},{12,4},{1,9},{5,13},{9,1},{13,5},{2,10},{6,14},... | collective-permute-start | bytes 245768 | tf_op jit(solution)/shard_map/ppermute | solution.py:319
  13.9 2.0 %collective-permute-start.1 = (bf16[40,1024]{1,0:T(8,128)(2,1)S(1)}, bf16[40,1024]{1,0:T(8,128)(2,1)S(1)}, u32[]{:S(2)}, u32[]{:S(2)}) collective-permute-start(bf16[40,1024]{1,0:T(8,128)(2,1)S(1)} %get-tuple-element.43), channel_id=1, source_target_pairs={{0,12},{4,8},{8,4},{12,0},{1,13},{5,9},{9,5},{13,1},{2,14},{6,10},... | collective-permute-start | bytes 245768 | tf_op jit(solution)/shard_map/ppermute | solution.py:319
  15.9 1.4 %shard_map.89 = (bf16[2,80,768]{2,1,0:T(8,128)(2,1)S(1)}, bf16[160,80]{1,0:T(8,128)(2,1)S(1)}, bf16[80,1024]{1,0:T(8,128)(2,1)S(1)}) custom-call(bf16[40,1024]{1,0:T(8,128)(2,1)S(1)} %shard_map.88.refs_0_, bf16[40,1024]{1,0:T(8,128)(2,1)S(1)} %collective-permute-done.4.refs_1_, bf16[80,1024]{1,0:T(8,128)(2,1)S(1)} %collective-permute-done.2.refs_2_, ...), custom_call_target="tpu_custom_call" | custom-call | flops 503316480 | bytes 3145728 | tf_op jit(solution)/shard_map/pallas_call | solution.py:71
  17.4 1.1 %shard_map.91.mine = bf16[2,80,768]{2,1,0:T(8,128)(2,1)S(1)} custom-call(bf16[80,1024]{1,0:T(8,128)(2,1)S(1)} %get-tuple-element.53.rows_in, bf16[3,768,1024]{2,1,0:T(8,128)(2,1)S(1)} %get-tuple-element.51.refs_5_.held), custom_call_target="tpu_custom_call" | custom-call | flops 25165824000 | bytes 314572800 | tf_op jit(solution)/shard_map/pallas_call | solution.py:71
  19.0 1.6 %collective-permute-start.8 = (bf16[2,80,768]{2,1,0:T(8,128)(2,1)S(1)}, bf16[2,80,768]{2,1,0:T(8,128)(2,1)S(1)}, u32[]{:S(2)}, u32[]{:S(2)}) collective-permute-start(bf16[2,80,768]{2,1,0:T(8,128)(2,1)S(1)} %get-tuple-element.55.refs_6_), channel_id=1, source_target_pairs={{0,2},{1,3},{2,0},{3,1},{4,6},{5,7},{6,4},{7,5},{8,10},{9,11},{10,... | collective-permute-start | bytes 737288 | tf_op jit(solution)/shard_map/ppermute | solution.py:319
  20.7 0.7 %shard_map.93 = bf16[80,768]{1,0:T(8,128)(2,1)S(1)} custom-call(bf16[40,1024]{1,0:T(8,128)(2,1)S(1)} %collective-permute-done.refs_0_, bf16[40,1024]{1,0:T(8,128)(2,1)S(1)} %collective-permute-done.1.refs_1_, bf16[80,1024]{1,0:T(8,128)(2,1)S(1)} %collective-permute-done.2.refs_2_, bf16[40,1024]{1,0:T(8,128)(2,1)S(1)} %get-tuple-element.45.refs_3_, ...), custom_call_target="tpu_custom_call" | custom-call | flops 251658240 | bytes 3145728 | tf_op jit(solution)/shard_map/pallas_call | solution.py:71
  21.5 0.7 %shard_map.90 = (bf16[80,1024]{1,0:T(8,128)(2,1)S(1)}, bf16[80,768]{1,0:T(8,128)(2,1)S(1)}) custom-call(bf16[40,1024]{1,0:T(8,128)(2,1)S(1)} %collective-permute-done.refs_0_, bf16[40,1024]{1,0:T(8,128)(2,1)S(1)} %collective-permute-done.1.refs_1_, bf16[80,1024]{1,0:T(8,128)(2,1)S(1)} %collective-permute-done.2.refs_2_, ...), custom_call_target="tpu_custom_call" | custom-call | flops 25165824000 | bytes 314572800 | tf_op jit(solution)/shard_map/pallas_call | solution.py:71
  22.2 0.6 %collective-permute-done.6 = bf16[80,768]{1,0:T(8,128)(2,1)S(1)} collective-permute-done((bf16[80,768]{1,0:T(8,128)(2,1)S(1)}, bf16[80,768]{1,0:T(8,128)(2,1)S(1)}, u32[]{:S(2)}, u32[]{:S(2)}) %collective-permute-start.6) | collective-permute-done | bytes 122912 | tf_op jit(solution)/shard_map/ppermute | solution.py:319
  22.9 1.6 %collective-permute-start.7 = (bf16[80,768]{1,0:T(8,128)(2,1)S(1)}, bf16[80,768]{1,0:T(8,128)(2,1)S(1)}, u32[]{:S(2)}, u32[]{:S(2)}) collective-permute-start(bf16[80,768]{1,0:T(8,128)(2,1)S(1)} %get-tuple-element.67), channel_id=1, source_target_pairs={{0,2},{1,3},{2,0},{3,1},{4,6},{5,7},{6,4},{7,5},{8,10},{9,11},{10,... | collective-permute-start | bytes 368648 | tf_op jit(solution)/shard_map/ppermute | solution.py:319
  24.4 3.4 %collective-permute-done.8.pair_far = bf16[2,80,768]{2,1,0:T(8,128)(2,1)S(1)} collective-permute-done((bf16[2,80,768]{2,1,0:T(8,128)(2,1)S(1)}, bf16[2,80,768]{2,1,0:T(8,128)(2,1)S(1)}, u32[]{:S(2)}, u32[]{:S(2)}) %collective-permute-start.8) | collective-permute-done | bytes 245792 | tf_op jit(solution)/shard_map/ppermute | solution.py:319
  28.1 1.6 %collective-permute-done.7.act_far = bf16[80,768]{1,0:T(8,128)(2,1)S(1)} collective-permute-done((bf16[80,768]{1,0:T(8,128)(2,1)S(1)}, bf16[80,768]{1,0:T(8,128)(2,1)S(1)}, u32[]{:S(2)}, u32[]{:S(2)}) %collective-permute-start.7) | collective-permute-done | bytes 122912 | tf_op jit(solution)/shard_map/ppermute | solution.py:319
  29.8 0.7 %shard_map.96.total = f32[80,1024]{1,0:T(8,128)S(1)} custom-call(bf16[2,80,768]{2,1,0:T(8,128)(2,1)S(1)} %shard_map.95.mine, bf16[3,768,1024]{2,1,0:T(8,128)(2,1)S(1)} %get-tuple-element.51.refs_5_.held), custom_call_target="tpu_custom_call" | custom-call | flops 251658240 | bytes 3145728 | tf_op jit(solution)/shard_map/pallas_call | solution.py:71
  30.5 0.8 %collective-permute-done.10.other = bf16[2,80,768]{2,1,0:T(8,128)(2,1)S(1)} collective-permute-done((bf16[2,80,768]{2,1,0:T(8,128)(2,1)S(1)}, bf16[2,80,768]{2,1,0:T(8,128)(2,1)S(1)}, u32[]{:S(2)}, u32[]{:S(2)}) %collective-permute-start.10) | collective-permute-done | bytes 245792 | tf_op jit(solution)/shard_map/ppermute | solution.py:319
  31.3 0.9 %shard_map.97 = (bf16[40,1024]{1,0:T(8,128)(2,1)S(1)}, bf16[40,1024]{1,0:T(8,128)(2,1)S(1)}, bf16[40,1024]{1,0:T(8,128)(2,1)S(1)}, bf16[40,1024]{1,0:T(8,128)(2,1)S(1)}) custom-call(f32[80,1024]{1,0:T(8,128)S(1)} %shard_map.96.total, bf16[2,80,768]{2,1,0:T(8,128)(2,1)S(1)} %collective-permute-done.10.other, ...), custom_call_target="tpu_custom_call" | custom-call | flops 251658240 | bytes 3145728 | tf_op jit(solution)/shard_map/pallas_call | solution.py:71
  32.2 0.5 %collective-permute-start.11 = (bf16[40,1024]{1,0:T(8,128)(2,1)S(1)}, bf16[40,1024]{1,0:T(8,128)(2,1)S(1)}, u32[]{:S(2)}, u32[]{:S(2)}) collective-permute-start(bf16[40,1024]{1,0:T(8,128)(2,1)S(1)} %get-tuple-element.60), channel_id=1, source_target_pairs={{0,4},{4,8},{8,12},{12,0},{1,5},{5,9},{9,13},{13,1},{2,6},{6,10},{... | collective-permute-start | bytes 245768 | tf_op jit(solution)/shard_map/ppermute | solution.py:312
  32.7 2.2 %collective-permute-start.12 = (bf16[40,1024]{1,0:T(8,128)(2,1)S(1)}, bf16[40,1024]{1,0:T(8,128)(2,1)S(1)}, u32[]{:S(2)}, u32[]{:S(2)}) collective-permute-start(bf16[40,1024]{1,0:T(8,128)(2,1)S(1)} %get-tuple-element.61), channel_id=1, source_target_pairs={{0,8},{4,12},{8,0},{12,4},{1,9},{5,13},{9,1},{13,5},{2,10},{6,14},... | collective-permute-start | bytes 245768 | tf_op jit(solution)/shard_map/ppermute | solution.py:312
  34.9 2.2 %collective-permute-start.13 = (bf16[40,1024]{1,0:T(8,128)(2,1)S(1)}, bf16[40,1024]{1,0:T(8,128)(2,1)S(1)}, u32[]{:S(2)}, u32[]{:S(2)}) collective-permute-start(bf16[40,1024]{1,0:T(8,128)(2,1)S(1)} %get-tuple-element.62), channel_id=1, source_target_pairs={{0,12},{4,0},{8,4},{12,8},{1,13},{5,1},{9,5},{13,9},{2,14},{6,2},{... | collective-permute-start | bytes 245768 | tf_op jit(solution)/shard_map/ppermute | solution.py:312
  37.1 4.1 %shard_map.99 = (bf16[1,2,1536,1024]{3,2,1,0:T(8,128)(2,1)}, bf16[1,1536,1024]{2,1,0:T(8,128)(2,1)}) custom-call(bf16[80,768]{1,0:T(8,128)(2,1)S(1)} %get-tuple-element.59.mine_act, bf16[80,768]{1,0:T(8,128)(2,1)S(1)} %collective-permute-done.9._.other_act, bf16[2,80,768]{2,1,0:T(8,128)(2,1)S(1)} %shard_map.95.mine, ...), custom_call_target="tpu_custom_call" | custom-call | flops 754974720 | bytes 9437184 | tf_op jit(solution)/shard_map/pallas_call | solution.py:71
  41.2 0.9 %collective-permute-done.12.refs_1_ = bf16[40,1024]{1,0:T(8,128)(2,1)S(1)} collective-permute-done((bf16[40,1024]{1,0:T(8,128)(2,1)S(1)}, bf16[40,1024]{1,0:T(8,128)(2,1)S(1)}, u32[]{:S(2)}, u32[]{:S(2)}) %collective-permute-start.12) | collective-permute-done | bytes 81952 | tf_op jit(solution)/shard_map/ppermute | solution.py:312
  42.2 1.1 %shard_map.98 = bf16[256,1024]{1,0:T(8,128)(2,1)} custom-call(bf16[160,256]{1,0:T(8,128)(2,1)S(1)} %get-tuple-element.35.pick, bf16[40,1024]{1,0:T(8,128)(2,1)S(1)} %collective-permute-done.11.refs_0_, bf16[40,1024]{1,0:T(8,128)(2,1)S(1)} %collective-permute-done.12.refs_1_, bf16[40,1024]{1,0:T(8,128)(2,1)S(1)} %collective-permute-done.13.refs_2_, ...), custom_call_target="tpu_custom_call" | custom-call | flops 83886080 | bytes 1048576 | tf_op jit(solution)/shard_map/pallas_call | solution.py:71
  (20 shorter events, 1.5 us)
Async XLA Ops:
  2.0 13.8 %collective-permute-start.3 = (bf16[40,1024]{1,0:T(8,128)(2,1)S(1)}, bf16[40,1024]{1,0:T(8,128)(2,1)S(1)}, u32[]{:S(2)}, u32[]{:S(2)}) collective-permute-start(bf16[40,1024]{1,0:T(8,128)(2,1)S(1)} %get-tuple-element.46), channel_id=1, source_target_pairs={{0,8},{4,12},{8,0},{12,4},{1,9},{5,13},{9,1},{13,5},{2,10},{6,14},... | collective-permute-start | bytes 245768 | tf_op jit(solution)/shard_map/ppermute | solution.py:319
  6.4 9.5 %collective-permute-start.2 = (bf16[80,1024]{1,0:T(8,128)(2,1)S(1)}, bf16[80,1024]{1,0:T(8,128)(2,1)S(1)}, u32[]{:S(2)}, u32[]{:S(2)}) collective-permute-start(bf16[80,1024]{1,0:T(8,128)(2,1)S(1)} %get-tuple-element.44), channel_id=1, source_target_pairs={{0,4},{4,0},{8,12},{12,8},{1,5},{5,1},{9,13},{13,9},{2,6},{6,2},{1... | collective-permute-start | bytes 491528 | tf_op jit(solution)/shard_map/ppermute | solution.py:319
  8.0 7.8 %collective-permute-start.4 = (bf16[40,1024]{1,0:T(8,128)(2,1)S(1)}, bf16[40,1024]{1,0:T(8,128)(2,1)S(1)}, u32[]{:S(2)}, u32[]{:S(2)}) collective-permute-start(bf16[40,1024]{1,0:T(8,128)(2,1)S(1)} %get-tuple-element.47), channel_id=1, source_target_pairs={{0,12},{4,8},{8,4},{12,0},{1,13},{5,9},{9,5},{13,1},{2,14},{6,10},... | collective-permute-start | bytes 245768 | tf_op jit(solution)/shard_map/ppermute | solution.py:319
  11.9 8.9 %collective-permute-start = (bf16[40,1024]{1,0:T(8,128)(2,1)S(1)}, bf16[40,1024]{1,0:T(8,128)(2,1)S(1)}, u32[]{:S(2)}, u32[]{:S(2)}) collective-permute-start(bf16[40,1024]{1,0:T(8,128)(2,1)S(1)} %get-tuple-element.42), channel_id=1, source_target_pairs={{0,8},{4,12},{8,0},{12,4},{1,9},{5,13},{9,1},{13,5},{2,10},{6,14},... | collective-permute-start | bytes 245768 | tf_op jit(solution)/shard_map/ppermute | solution.py:319
  13.9 6.9 %collective-permute-start.1 = (bf16[40,1024]{1,0:T(8,128)(2,1)S(1)}, bf16[40,1024]{1,0:T(8,128)(2,1)S(1)}, u32[]{:S(2)}, u32[]{:S(2)}) collective-permute-start(bf16[40,1024]{1,0:T(8,128)(2,1)S(1)} %get-tuple-element.43), channel_id=1, source_target_pairs={{0,12},{4,8},{8,4},{12,0},{1,13},{5,9},{9,5},{13,1},{2,14},{6,10},... | collective-permute-start | bytes 245768 | tf_op jit(solution)/shard_map/ppermute | solution.py:319
  17.3 1.6 %collective-permute-start.5 = (bf16[2,80,768]{2,1,0:T(8,128)(2,1)S(1)}, bf16[2,80,768]{2,1,0:T(8,128)(2,1)S(1)}, u32[]{:S(2)}, u32[]{:S(2)}) collective-permute-start(bf16[2,80,768]{2,1,0:T(8,128)(2,1)S(1)} %get-tuple-element.54), channel_id=1, source_target_pairs={{0,1},{1,0},{2,3},{3,2},{4,5},{5,4},{6,7},{7,6},{8,9},{9,8},{10,11... | collective-permute-start | bytes 737288 | tf_op jit(solution)/shard_map/ppermute | solution.py:319
  19.0 8.9 %collective-permute-start.8 = (bf16[2,80,768]{2,1,0:T(8,128)(2,1)S(1)}, bf16[2,80,768]{2,1,0:T(8,128)(2,1)S(1)}, u32[]{:S(2)}, u32[]{:S(2)}) collective-permute-start(bf16[2,80,768]{2,1,0:T(8,128)(2,1)S(1)} %get-tuple-element.55.refs_6_), channel_id=1, source_target_pairs={{0,2},{1,3},{2,0},{3,1},{4,6},{5,7},{6,4},{7,5},{8,10},{9,11},{10,... | collective-permute-start | bytes 737288 | tf_op jit(solution)/shard_map/ppermute | solution.py:319
  21.4 1.4 %collective-permute-start.6 = (bf16[80,768]{1,0:T(8,128)(2,1)S(1)}, bf16[80,768]{1,0:T(8,128)(2,1)S(1)}, u32[]{:S(2)}, u32[]{:S(2)}) collective-permute-start(bf16[80,768]{1,0:T(8,128)(2,1)S(1)} %shard_map.93), channel_id=1, source_target_pairs={{0,1},{1,0},{2,3},{3,2},{4,5},{5,4},{6,7},{7,6},{8,9},{9,8},{10,11... | collective-permute-start | bytes 368648 | tf_op jit(solution)/shard_map/ppermute | solution.py:319
  22.9 6.8 %collective-permute-start.7 = (bf16[80,768]{1,0:T(8,128)(2,1)S(1)}, bf16[80,768]{1,0:T(8,128)(2,1)S(1)}, u32[]{:S(2)}, u32[]{:S(2)}) collective-permute-start(bf16[80,768]{1,0:T(8,128)(2,1)S(1)} %get-tuple-element.67), channel_id=1, source_target_pairs={{0,2},{1,3},{2,0},{3,1},{4,6},{5,7},{6,4},{7,5},{8,10},{9,11},{10,... | collective-permute-start | bytes 368648 | tf_op jit(solution)/shard_map/ppermute | solution.py:319
  28.0 1.7 %collective-permute-start.9 = (bf16[80,768]{1,0:T(8,128)(2,1)S(1)}, bf16[80,768]{1,0:T(8,128)(2,1)S(1)}, u32[]{:S(2)}, u32[]{:S(2)}) collective-permute-start(bf16[80,768]{1,0:T(8,128)(2,1)S(1)} %get-tuple-element.59.mine_act), channel_id=1, source_target_pairs={{0,1},{1,0},{2,3},{3,2},{4,5},{5,4},{6,7},{7,6},{8,9},{9,8},{10,11... | collective-permute-start | bytes 368648 | tf_op jit(solution)/shard_map/ppermute | solution.py:319
  29.7 1.6 %collective-permute-start.10 = (bf16[2,80,768]{2,1,0:T(8,128)(2,1)S(1)}, bf16[2,80,768]{2,1,0:T(8,128)(2,1)S(1)}, u32[]{:S(2)}, u32[]{:S(2)}) collective-permute-start(bf16[2,80,768]{2,1,0:T(8,128)(2,1)S(1)} %shard_map.95.mine), channel_id=1, source_target_pairs={{0,1},{1,0},{2,3},{3,2},{4,5},{5,4},{6,7},{7,6},{8,9},{9,8},{10,11... | collective-permute-start | bytes 737288 | tf_op jit(solution)/shard_map/ppermute | solution.py:319
  32.2 9.0 %collective-permute-start.11 = (bf16[40,1024]{1,0:T(8,128)(2,1)S(1)}, bf16[40,1024]{1,0:T(8,128)(2,1)S(1)}, u32[]{:S(2)}, u32[]{:S(2)}) collective-permute-start(bf16[40,1024]{1,0:T(8,128)(2,1)S(1)} %get-tuple-element.60), channel_id=1, source_target_pairs={{0,4},{4,8},{8,12},{12,0},{1,5},{5,9},{9,13},{13,1},{2,6},{6,10},{... | collective-permute-start | bytes 245768 | tf_op jit(solution)/shard_map/ppermute | solution.py:312
  32.7 9.4 %collective-permute-start.12 = (bf16[40,1024]{1,0:T(8,128)(2,1)S(1)}, bf16[40,1024]{1,0:T(8,128)(2,1)S(1)}, u32[]{:S(2)}, u32[]{:S(2)}) collective-permute-start(bf16[40,1024]{1,0:T(8,128)(2,1)S(1)} %get-tuple-element.61), channel_id=1, source_target_pairs={{0,8},{4,12},{8,0},{12,4},{1,9},{5,13},{9,1},{13,5},{2,10},{6,14},... | collective-permute-start | bytes 245768 | tf_op jit(solution)/shard_map/ppermute | solution.py:312
  34.9 7.3 %collective-permute-start.13 = (bf16[40,1024]{1,0:T(8,128)(2,1)S(1)}, bf16[40,1024]{1,0:T(8,128)(2,1)S(1)}, u32[]{:S(2)}, u32[]{:S(2)}) collective-permute-start(bf16[40,1024]{1,0:T(8,128)(2,1)S(1)} %get-tuple-element.62), channel_id=1, source_target_pairs={{0,12},{4,0},{8,4},{12,8},{1,13},{5,1},{9,5},{13,9},{2,14},{6,2},{... | collective-permute-start | bytes 245768 | tf_op jit(solution)/shard_map/ppermute | solution.py:312

commit v21 on v19

--- a/solution.py
+++ b/solution.py
@@ -132,12 +132,6 @@
         target[...] = part.astype(BF)
 
 
-def stacked(pieces, part=0):
-    rows = [piece[...].astype(F32) for piece in pieces]
-    rows = [row[part * MOST : (part + 1) * MOST] if row.shape[0] > MOST else row for row in rows]
-    return jnp.concatenate(rows, axis=0)
-
-
 def rows_of(half, own):
     core = lax.axis_index("ey") & 1
     return pl.ds(pl.multiple_of((core if own else 1 - core) * half, 128), half)
@@ -147,11 +141,23 @@
     out[...] = first[...]
 
 
+def joined(place, pieces, part):
+    total = None
+    for at, piece in enumerate(pieces):
+        rows = place[at * MOST : (at + 1) * MOST]
+        if piece.shape[0] > MOST:
+            blank = jnp.zeros_like(rows)
+            rows = jnp.concatenate([blank, rows] if part else [rows, blank], axis=0)
+        term = mm(rows.astype(BF), piece[...], ROWS)
+        total = term if total is None else total + term
+    return total.astype(BF)
+
+
 def place_rows(experts, capacity, pieces):
     me = lax.axis_index("ex")
     rows = experts * MOST
-    got = stacked(pieces)
-    full = got[:, :1] < EMPTY / 2
+    first = [piece[:, :128].astype(F32)[:MOST] for piece in pieces]
+    full = jnp.concatenate(first, axis=0)[:, :1] < EMPTY / 2
     key = []
     for shape, dim in (((rows, 1), 0), ((1, rows), 1)):
         row = iota(shape, dim)
@@ -160,8 +166,8 @@
     earlier = jnp.where(key[1] < key[0], 1.0, 0.0).astype(BF)
     wide = jnp.broadcast_to(full, (rows, capacity))
     slot = mm(earlier, jnp.where(wide, 1.0, 0.0).astype(BF)).astype(jnp.int32)
-    place = jnp.where((slot == iota((rows, capacity), 1)) & wide, 1.0, 0.0).astype(BF)
-    return place, mm(place, got.astype(BF), ROWS).astype(BF)
+    place = jnp.where((slot == iota((rows, capacity), 1)) & wide, 1.0, 0.0)
+    return place.astype(BF), joined(place, pieces, 0)
 
 
 def stage(count, gate_up, down, *refs):
@@ -202,7 +208,7 @@
 
 def act_part(experts, own, *refs):
     place, held = refs[experts : experts + 2]
-    rows_grad = mm(place[...], stacked(refs[:experts], 1).astype(BF), ROWS).astype(BF)
+    rows_grad = joined(place[...].astype(F32), refs[:experts], 1)
     if own:
         refs[-2][...] = rows_grad
     refs[-1][...] = mm(rows_grad, held[2], LANES).astype(BF)

time: 43.4 us -> 43.6 us (level)
  transfers between devices with their start and end apart: 14 -> 14, of which waited for: 7 -> 7; matrix products, arithmetic and copies ran while one was open for 0% -> 0% of each run, Pallas kernels for 30% -> 31%
where the time goes in v21:
time: 43.6 us; the launch traced here: 43.4 us
  starting transfers between devices  18.1 us (42%)
  Pallas kernels  16.8 us (39%)
  waiting for transfers between devices  7.75 us (18%)
  between operations  0.78 us (2%)
    pallas_call x15, Pallas kernels, call(): pl.pallas_call(body, out_shape=outs, in_specs=specs, out_specs=out_specs...  16.8 us
    ppermute x11, starting transfers between devices, swap(): return lax.ppermute(value, axis, [(i, i ^ bit) for i in range(count)])  13.1 us
    ppermute x11, waiting for transfers between devices, swap(): return lax.ppermute(value, axis, [(i, i ^ bit) for i in range(count)])  6.84 us
    ppermute x3, starting transfers between devices, shift(): lax.ppermute(value, axis, [(name, names[(at + step) % count]) for at, nam...  4.93 us
    ppermute x3, waiting for transfers between devices, shift(): lax.ppermute(value, axis, [(name, names[(at + step) % count]) for at, nam...  0.91 us
  transfers between devices with their start and end apart: 14, of which 7 were waited for; matrix products, arithmetic and copies ran while one was open for 0% of the time, Pallas kernels for 31%

profile of v21, /device:TPU:0, one launch (start us, length us, event | category | flops | bytes accessed | tf_op | source)
XLA Modules:
  0.0 43.4 jit_solution(12297420953228842797)
XLA Ops:
  0.6 1.4 %shard_map.85 = (bf16[160,256]{1,0:T(8,128)(2,1)S(1)}, f32[160,1]{1,0:T(8,128)S(1)}, bf16[256,1024]{1,0:T(8,128)(2,1)S(1)}, bf16[40,1024]{1,0:T(8,128)(2,1)S(1)}...) custom-call(s32[8,256]{1,0:T(8,128)} %bitcast.2, ...), custom_call_target="tpu_custom_call" | custom-call | flops 83886080 | bytes 1048576 | tf_op jit(solution)/shard_map/pallas_call | solution.py:70
  2.0 4.1 %collective-permute-start.3 = (bf16[40,1024]{1,0:T(8,128)(2,1)S(1)}, bf16[40,1024]{1,0:T(8,128)(2,1)S(1)}, u32[]{:S(2)}, u32[]{:S(2)}) collective-permute-start(bf16[40,1024]{1,0:T(8,128)(2,1)S(1)} %get-tuple-element.46), channel_id=1, source_target_pairs={{0,8},{4,12},{8,0},{12,4},{1,9},{5,13},{9,1},{13,5},{2,10},{6,14},... | collective-permute-start | bytes 245768 | tf_op jit(solution)/shard_map/ppermute | solution.py:324
  6.4 1.6 %collective-permute-start.2 = (bf16[80,1024]{1,0:T(8,128)(2,1)S(1)}, bf16[80,1024]{1,0:T(8,128)(2,1)S(1)}, u32[]{:S(2)}, u32[]{:S(2)}) collective-permute-start(bf16[80,1024]{1,0:T(8,128)(2,1)S(1)} %get-tuple-element.44), channel_id=1, source_target_pairs={{0,4},{4,0},{8,12},{12,8},{1,5},{5,1},{9,13},{13,9},{2,6},{6,2},{1... | collective-permute-start | bytes 491528 | tf_op jit(solution)/shard_map/ppermute | solution.py:324
  8.0 3.8 %shard_map.87 = (bf16[3,768,1024]{2,1,0:T(8,128)(2,1)S(1)}, bf16[3,768,1024]{2,1,0:T(8,128)(2,1)S(1)}, bf16[40,1024]{1,0:T(8,128)(2,1)S(1)}, bf16[40,1024]{1,0:T(8,128)(2,1)S(1)}, bf16[40,1024]{1,0:T(8,128)(2,1)S(1)}) custom-call(bf16[1,2,1536,1024]{3,2,1,0:T(8,128)(2,1)} %gate_up.1, bf16[1,1536,1024]{2,1,0:T(8,128)(2,1)} %down.1, ...), custom_call_target="tpu_custom_call" | custom-call | flops 251658240 | bytes 3145728 | tf_op jit(solution)/shard_map/pallas_call | solution.py:70
  11.8 2.0 %collective-permute-start = (bf16[40,1024]{1,0:T(8,128)(2,1)S(1)}, bf16[40,1024]{1,0:T(8,128)(2,1)S(1)}, u32[]{:S(2)}, u32[]{:S(2)}) collective-permute-start(bf16[40,1024]{1,0:T(8,128)(2,1)S(1)} %get-tuple-element.42), channel_id=1, source_target_pairs={{0,8},{4,12},{8,0},{12,4},{1,9},{5,13},{9,1},{13,5},{2,10},{6,14},... | collective-permute-start | bytes 245768 | tf_op jit(solution)/shard_map/ppermute | solution.py:324
  13.8 2.0 %collective-permute-start.1 = (bf16[40,1024]{1,0:T(8,128)(2,1)S(1)}, bf16[40,1024]{1,0:T(8,128)(2,1)S(1)}, u32[]{:S(2)}, u32[]{:S(2)}) collective-permute-start(bf16[40,1024]{1,0:T(8,128)(2,1)S(1)} %get-tuple-element.43), channel_id=1, source_target_pairs={{0,12},{4,8},{8,4},{12,0},{1,13},{5,9},{9,5},{13,1},{2,14},{6,10},... | collective-permute-start | bytes 245768 | tf_op jit(solution)/shard_map/ppermute | solution.py:324
  15.8 1.6 %shard_map.89 = (bf16[2,80,768]{2,1,0:T(8,128)(2,1)S(1)}, bf16[160,80]{1,0:T(8,128)(2,1)S(1)}, bf16[80,1024]{1,0:T(8,128)(2,1)S(1)}) custom-call(bf16[40,1024]{1,0:T(8,128)(2,1)S(1)} %shard_map.88.refs_0_, bf16[40,1024]{1,0:T(8,128)(2,1)S(1)} %collective-permute-done.4.refs_1_, bf16[80,1024]{1,0:T(8,128)(2,1)S(1)} %collective-permute-done.2.refs_2_, ...), custom_call_target="tpu_custom_call" | custom-call | flops 503316480 | bytes 3145728 | tf_op jit(solution)/shard_map/pallas_call | solution.py:70
  17.5 1.1 %shard_map.91.mine = bf16[2,80,768]{2,1,0:T(8,128)(2,1)S(1)} custom-call(bf16[80,1024]{1,0:T(8,128)(2,1)S(1)} %get-tuple-element.53.rows_in, bf16[3,768,1024]{2,1,0:T(8,128)(2,1)S(1)} %get-tuple-element.51.refs_5_.held), custom_call_target="tpu_custom_call" | custom-call | flops 25165824000 | bytes 314572800 | tf_op jit(solution)/shard_map/pallas_call | solution.py:70
  19.1 1.6 %collective-permute-start.8 = (bf16[2,80,768]{2,1,0:T(8,128)(2,1)S(1)}, bf16[2,80,768]{2,1,0:T(8,128)(2,1)S(1)}, u32[]{:S(2)}, u32[]{:S(2)}) collective-permute-start(bf16[2,80,768]{2,1,0:T(8,128)(2,1)S(1)} %get-tuple-element.55.refs_6_), channel_id=1, source_target_pairs={{0,2},{1,3},{2,0},{3,1},{4,6},{5,7},{6,4},{7,5},{8,10},{9,11},{10,... | collective-permute-start | bytes 737288 | tf_op jit(solution)/shard_map/ppermute | solution.py:324
  20.8 0.8 %shard_map.93 = bf16[80,768]{1,0:T(8,128)(2,1)S(1)} custom-call(bf16[40,1024]{1,0:T(8,128)(2,1)S(1)} %collective-permute-done.refs_0_, bf16[40,1024]{1,0:T(8,128)(2,1)S(1)} %collective-permute-done.1.refs_1_, bf16[80,1024]{1,0:T(8,128)(2,1)S(1)} %collective-permute-done.2.refs_2_, bf16[40,1024]{1,0:T(8,128)(2,1)S(1)} %get-tuple-element.45.refs_3_, ...), custom_call_target="tpu_custom_call" | custom-call | flops 251658240 | bytes 3145728 | tf_op jit(solution)/shard_map/pallas_call | solution.py:70
  21.7 0.8 %shard_map.90 = (bf16[80,1024]{1,0:T(8,128)(2,1)S(1)}, bf16[80,768]{1,0:T(8,128)(2,1)S(1)}) custom-call(bf16[40,1024]{1,0:T(8,128)(2,1)S(1)} %collective-permute-done.refs_0_, bf16[40,1024]{1,0:T(8,128)(2,1)S(1)} %collective-permute-done.1.refs_1_, bf16[80,1024]{1,0:T(8,128)(2,1)S(1)} %collective-permute-done.2.refs_2_, ...), custom_call_target="tpu_custom_call" | custom-call | flops 25165824000 | bytes 314572800 | tf_op jit(solution)/shard_map/pallas_call | solution.py:70
  22.5 0.5 %collective-permute-done.6 = bf16[80,768]{1,0:T(8,128)(2,1)S(1)} collective-permute-done((bf16[80,768]{1,0:T(8,128)(2,1)S(1)}, bf16[80,768]{1,0:T(8,128)(2,1)S(1)}, u32[]{:S(2)}, u32[]{:S(2)}) %collective-permute-start.6) | collective-permute-done | bytes 122912 | tf_op jit(solution)/shard_map/ppermute | solution.py:324
  23.0 1.6 %collective-permute-start.7 = (bf16[80,768]{1,0:T(8,128)(2,1)S(1)}, bf16[80,768]{1,0:T(8,128)(2,1)S(1)}, u32[]{:S(2)}, u32[]{:S(2)}) collective-permute-start(bf16[80,768]{1,0:T(8,128)(2,1)S(1)} %get-tuple-element.67), channel_id=1, source_target_pairs={{0,2},{1,3},{2,0},{3,1},{4,6},{5,7},{6,4},{7,5},{8,10},{9,11},{10,... | collective-permute-start | bytes 368648 | tf_op jit(solution)/shard_map/ppermute | solution.py:324
  24.6 3.3 %collective-permute-done.8.pair_far = bf16[2,80,768]{2,1,0:T(8,128)(2,1)S(1)} collective-permute-done((bf16[2,80,768]{2,1,0:T(8,128)(2,1)S(1)}, bf16[2,80,768]{2,1,0:T(8,128)(2,1)S(1)}, u32[]{:S(2)}, u32[]{:S(2)}) %collective-permute-start.8) | collective-permute-done | bytes 245792 | tf_op jit(solution)/shard_map/ppermute | solution.py:324
  28.2 1.6 %collective-permute-done.7.act_far = bf16[80,768]{1,0:T(8,128)(2,1)S(1)} collective-permute-done((bf16[80,768]{1,0:T(8,128)(2,1)S(1)}, bf16[80,768]{1,0:T(8,128)(2,1)S(1)}, u32[]{:S(2)}, u32[]{:S(2)}) %collective-permute-start.7) | collective-permute-done | bytes 122912 | tf_op jit(solution)/shard_map/ppermute | solution.py:324
  29.9 0.7 %shard_map.96.total = f32[80,1024]{1,0:T(8,128)S(1)} custom-call(bf16[2,80,768]{2,1,0:T(8,128)(2,1)S(1)} %shard_map.95.mine, bf16[3,768,1024]{2,1,0:T(8,128)(2,1)S(1)} %get-tuple-element.51.refs_5_.held), custom_call_target="tpu_custom_call" | custom-call | flops 251658240 | bytes 3145728 | tf_op jit(solution)/shard_map/pallas_call | solution.py:70
  30.6 0.8 %collective-permute-done.10.other = bf16[2,80,768]{2,1,0:T(8,128)(2,1)S(1)} collective-permute-done((bf16[2,80,768]{2,1,0:T(8,128)(2,1)S(1)}, bf16[2,80,768]{2,1,0:T(8,128)(2,1)S(1)}, u32[]{:S(2)}, u32[]{:S(2)}) %collective-permute-start.10) | collective-permute-done | bytes 245792 | tf_op jit(solution)/shard_map/ppermute | solution.py:324
  31.4 0.9 %shard_map.97 = (bf16[40,1024]{1,0:T(8,128)(2,1)S(1)}, bf16[40,1024]{1,0:T(8,128)(2,1)S(1)}, bf16[40,1024]{1,0:T(8,128)(2,1)S(1)}, bf16[40,1024]{1,0:T(8,128)(2,1)S(1)}) custom-call(f32[80,1024]{1,0:T(8,128)S(1)} %shard_map.96.total, bf16[2,80,768]{2,1,0:T(8,128)(2,1)S(1)} %collective-permute-done.10.other, ...), custom_call_target="tpu_custom_call" | custom-call | flops 251658240 | bytes 3145728 | tf_op jit(solution)/shard_map/pallas_call | solution.py:70
  32.3 0.5 %collective-permute-start.11 = (bf16[40,1024]{1,0:T(8,128)(2,1)S(1)}, bf16[40,1024]{1,0:T(8,128)(2,1)S(1)}, u32[]{:S(2)}, u32[]{:S(2)}) collective-permute-start(bf16[40,1024]{1,0:T(8,128)(2,1)S(1)} %get-tuple-element.60), channel_id=1, source_target_pairs={{0,4},{4,8},{8,12},{12,0},{1,5},{5,9},{9,13},{13,1},{2,6},{6,10},{... | collective-permute-start | bytes 245768 | tf_op jit(solution)/shard_map/ppermute | solution.py:317
  32.9 2.2 %collective-permute-start.12 = (bf16[40,1024]{1,0:T(8,128)(2,1)S(1)}, bf16[40,1024]{1,0:T(8,128)(2,1)S(1)}, u32[]{:S(2)}, u32[]{:S(2)}) collective-permute-start(bf16[40,1024]{1,0:T(8,128)(2,1)S(1)} %get-tuple-element.61), channel_id=1, source_target_pairs={{0,8},{4,12},{8,0},{12,4},{1,9},{5,13},{9,1},{13,5},{2,10},{6,14},... | collective-permute-start | bytes 245768 | tf_op jit(solution)/shard_map/ppermute | solution.py:317
  35.1 2.1 %collective-permute-start.13 = (bf16[40,1024]{1,0:T(8,128)(2,1)S(1)}, bf16[40,1024]{1,0:T(8,128)(2,1)S(1)}, u32[]{:S(2)}, u32[]{:S(2)}) collective-permute-start(bf16[40,1024]{1,0:T(8,128)(2,1)S(1)} %get-tuple-element.62), channel_id=1, source_target_pairs={{0,12},{4,0},{8,4},{12,8},{1,13},{5,1},{9,5},{13,9},{2,14},{6,2},{... | collective-permute-start | bytes 245768 | tf_op jit(solution)/shard_map/ppermute | solution.py:317
  37.2 4.1 %shard_map.99 = (bf16[1,2,1536,1024]{3,2,1,0:T(8,128)(2,1)}, bf16[1,1536,1024]{2,1,0:T(8,128)(2,1)}) custom-call(bf16[80,768]{1,0:T(8,128)(2,1)S(1)} %get-tuple-element.59.mine_act, bf16[80,768]{1,0:T(8,128)(2,1)S(1)} %collective-permute-done.9._.other_act, bf16[2,80,768]{2,1,0:T(8,128)(2,1)S(1)} %shard_map.95.mine, ...), custom_call_target="tpu_custom_call" | custom-call | flops 754974720 | bytes 9437184 | tf_op jit(solution)/shard_map/pallas_call | solution.py:70
  41.4 0.9 %collective-permute-done.12.refs_1_ = bf16[40,1024]{1,0:T(8,128)(2,1)S(1)} collective-permute-done((bf16[40,1024]{1,0:T(8,128)(2,1)S(1)}, bf16[40,1024]{1,0:T(8,128)(2,1)S(1)}, u32[]{:S(2)}, u32[]{:S(2)}) %collective-permute-start.12) | collective-permute-done | bytes 81952 | tf_op jit(solution)/shard_map/ppermute | solution.py:317
  42.3 1.1 %shard_map.98 = bf16[256,1024]{1,0:T(8,128)(2,1)} custom-call(bf16[160,256]{1,0:T(8,128)(2,1)S(1)} %get-tuple-element.35.pick, bf16[40,1024]{1,0:T(8,128)(2,1)S(1)} %collective-permute-done.11.refs_0_, bf16[40,1024]{1,0:T(8,128)(2,1)S(1)} %collective-permute-done.12.refs_1_, bf16[40,1024]{1,0:T(8,128)(2,1)S(1)} %collective-permute-done.13.refs_2_, ...), custom_call_target="tpu_custom_call" | custom-call | flops 83886080 | bytes 1048576 | tf_op jit(solution)/shard_map/pallas_call | solution.py:70
  (20 shorter events, 1.4 us)
Async XLA Ops:
  2.0 13.8 %collective-permute-start.3 = (bf16[40,1024]{1,0:T(8,128)(2,1)S(1)}, bf16[40,1024]{1,0:T(8,128)(2,1)S(1)}, u32[]{:S(2)}, u32[]{:S(2)}) collective-permute-start(bf16[40,1024]{1,0:T(8,128)(2,1)S(1)} %get-tuple-element.46), channel_id=1, source_target_pairs={{0,8},{4,12},{8,0},{12,4},{1,9},{5,13},{9,1},{13,5},{2,10},{6,14},... | collective-permute-start | bytes 245768 | tf_op jit(solution)/shard_map/ppermute | solution.py:324
  6.4 9.4 %collective-permute-start.2 = (bf16[80,1024]{1,0:T(8,128)(2,1)S(1)}, bf16[80,1024]{1,0:T(8,128)(2,1)S(1)}, u32[]{:S(2)}, u32[]{:S(2)}) collective-permute-start(bf16[80,1024]{1,0:T(8,128)(2,1)S(1)} %get-tuple-element.44), channel_id=1, source_target_pairs={{0,4},{4,0},{8,12},{12,8},{1,5},{5,1},{9,13},{13,9},{2,6},{6,2},{1... | collective-permute-start | bytes 491528 | tf_op jit(solution)/shard_map/ppermute | solution.py:324
  8.0 7.8 %collective-permute-start.4 = (bf16[40,1024]{1,0:T(8,128)(2,1)S(1)}, bf16[40,1024]{1,0:T(8,128)(2,1)S(1)}, u32[]{:S(2)}, u32[]{:S(2)}) collective-permute-start(bf16[40,1024]{1,0:T(8,128)(2,1)S(1)} %get-tuple-element.47), channel_id=1, source_target_pairs={{0,12},{4,8},{8,4},{12,0},{1,13},{5,9},{9,5},{13,1},{2,14},{6,10},... | collective-permute-start | bytes 245768 | tf_op jit(solution)/shard_map/ppermute | solution.py:324
  11.8 8.9 %collective-permute-start = (bf16[40,1024]{1,0:T(8,128)(2,1)S(1)}, bf16[40,1024]{1,0:T(8,128)(2,1)S(1)}, u32[]{:S(2)}, u32[]{:S(2)}) collective-permute-start(bf16[40,1024]{1,0:T(8,128)(2,1)S(1)} %get-tuple-element.42), channel_id=1, source_target_pairs={{0,8},{4,12},{8,0},{12,4},{1,9},{5,13},{9,1},{13,5},{2,10},{6,14},... | collective-permute-start | bytes 245768 | tf_op jit(solution)/shard_map/ppermute | solution.py:324
  13.8 7.0 %collective-permute-start.1 = (bf16[40,1024]{1,0:T(8,128)(2,1)S(1)}, bf16[40,1024]{1,0:T(8,128)(2,1)S(1)}, u32[]{:S(2)}, u32[]{:S(2)}) collective-permute-start(bf16[40,1024]{1,0:T(8,128)(2,1)S(1)} %get-tuple-element.43), channel_id=1, source_target_pairs={{0,12},{4,8},{8,4},{12,0},{1,13},{5,9},{9,5},{13,1},{2,14},{6,10},... | collective-permute-start | bytes 245768 | tf_op jit(solution)/shard_map/ppermute | solution.py:324
  17.4 1.6 %collective-permute-start.5 = (bf16[2,80,768]{2,1,0:T(8,128)(2,1)S(1)}, bf16[2,80,768]{2,1,0:T(8,128)(2,1)S(1)}, u32[]{:S(2)}, u32[]{:S(2)}) collective-permute-start(bf16[2,80,768]{2,1,0:T(8,128)(2,1)S(1)} %get-tuple-element.54), channel_id=1, source_target_pairs={{0,1},{1,0},{2,3},{3,2},{4,5},{5,4},{6,7},{7,6},{8,9},{9,8},{10,11... | collective-permute-start | bytes 737288 | tf_op jit(solution)/shard_map/ppermute | solution.py:324
  19.1 8.9 %collective-permute-start.8 = (bf16[2,80,768]{2,1,0:T(8,128)(2,1)S(1)}, bf16[2,80,768]{2,1,0:T(8,128)(2,1)S(1)}, u32[]{:S(2)}, u32[]{:S(2)}) collective-permute-start(bf16[2,80,768]{2,1,0:T(8,128)(2,1)S(1)} %get-tuple-element.55.refs_6_), channel_id=1, source_target_pairs={{0,2},{1,3},{2,0},{3,1},{4,6},{5,7},{6,4},{7,5},{8,10},{9,11},{10,... | collective-permute-start | bytes 737288 | tf_op jit(solution)/shard_map/ppermute | solution.py:324
  21.6 1.4 %collective-permute-start.6 = (bf16[80,768]{1,0:T(8,128)(2,1)S(1)}, bf16[80,768]{1,0:T(8,128)(2,1)S(1)}, u32[]{:S(2)}, u32[]{:S(2)}) collective-permute-start(bf16[80,768]{1,0:T(8,128)(2,1)S(1)} %shard_map.93), channel_id=1, source_target_pairs={{0,1},{1,0},{2,3},{3,2},{4,5},{5,4},{6,7},{7,6},{8,9},{9,8},{10,11... | collective-permute-start | bytes 368648 | tf_op jit(solution)/shard_map/ppermute | solution.py:324
  23.0 6.7 %collective-permute-start.7 = (bf16[80,768]{1,0:T(8,128)(2,1)S(1)}, bf16[80,768]{1,0:T(8,128)(2,1)S(1)}, u32[]{:S(2)}, u32[]{:S(2)}) collective-permute-start(bf16[80,768]{1,0:T(8,128)(2,1)S(1)} %get-tuple-element.67), channel_id=1, source_target_pairs={{0,2},{1,3},{2,0},{3,1},{4,6},{5,7},{6,4},{7,5},{8,10},{9,11},{10,... | collective-permute-start | bytes 368648 | tf_op jit(solution)/shard_map/ppermute | solution.py:324
  28.1 1.7 %collective-permute-start.9 = (bf16[80,768]{1,0:T(8,128)(2,1)S(1)}, bf16[80,768]{1,0:T(8,128)(2,1)S(1)}, u32[]{:S(2)}, u32[]{:S(2)}) collective-permute-start(bf16[80,768]{1,0:T(8,128)(2,1)S(1)} %get-tuple-element.59.mine_act), channel_id=1, source_target_pairs={{0,1},{1,0},{2,3},{3,2},{4,5},{5,4},{6,7},{7,6},{8,9},{9,8},{10,11... | collective-permute-start | bytes 368648 | tf_op jit(solution)/shard_map/ppermute | solution.py:324
  29.9 1.6 %collective-permute-start.10 = (bf16[2,80,768]{2,1,0:T(8,128)(2,1)S(1)}, bf16[2,80,768]{2,1,0:T(8,128)(2,1)S(1)}, u32[]{:S(2)}, u32[]{:S(2)}) collective-permute-start(bf16[2,80,768]{2,1,0:T(8,128)(2,1)S(1)} %shard_map.95.mine), channel_id=1, source_target_pairs={{0,1},{1,0},{2,3},{3,2},{4,5},{5,4},{6,7},{7,6},{8,9},{9,8},{10,11... | collective-permute-start | bytes 737288 | tf_op jit(solution)/shard_map/ppermute | solution.py:324
  32.3 9.0 %collective-permute-start.11 = (bf16[40,1024]{1,0:T(8,128)(2,1)S(1)}, bf16[40,1024]{1,0:T(8,128)(2,1)S(1)}, u32[]{:S(2)}, u32[]{:S(2)}) collective-permute-start(bf16[40,1024]{1,0:T(8,128)(2,1)S(1)} %get-tuple-element.60), channel_id=1, source_target_pairs={{0,4},{4,8},{8,12},{12,0},{1,5},{5,9},{9,13},{13,1},{2,6},{6,10},{... | collective-permute-start | bytes 245768 | tf_op jit(solution)/shard_map/ppermute | solution.py:317
  32.9 9.4 %collective-permute-start.12 = (bf16[40,1024]{1,0:T(8,128)(2,1)S(1)}, bf16[40,1024]{1,0:T(8,128)(2,1)S(1)}, u32[]{:S(2)}, u32[]{:S(2)}) collective-permute-start(bf16[40,1024]{1,0:T(8,128)(2,1)S(1)} %get-tuple-element.61), channel_id=1, source_target_pairs={{0,8},{4,12},{8,0},{12,4},{1,9},{5,13},{9,1},{13,5},{2,10},{6,14},... | collective-permute-start | bytes 245768 | tf_op jit(solution)/shard_map/ppermute | solution.py:317
  35.1 7.2 %collective-permute-start.13 = (bf16[40,1024]{1,0:T(8,128)(2,1)S(1)}, bf16[40,1024]{1,0:T(8,128)(2,1)S(1)}, u32[]{:S(2)}, u32[]{:S(2)}) collective-permute-start(bf16[40,1024]{1,0:T(8,128)(2,1)S(1)} %get-tuple-element.62), channel_id=1, source_target_pairs={{0,12},{4,0},{8,4},{12,8},{1,13},{5,1},{9,5},{13,9},{2,14},{6,2},{... | collective-permute-start | bytes 245768 | tf_op jit(solution)/shard_map/ppermute | solution.py:317

commit v22 on v19

--- a/solution.py
+++ b/solution.py
@@ -290,11 +290,11 @@
 
 
 def tour(count):
-    return list(range(count))
+    return [i ^ (i >> 1) for i in range(count)]
 
 
 def steps(count):
-    return list(range(1, count)) + [0]
+    return list(range(2, count)) + [1, 0]
 
 
 def ahead(step, count):

time: 43.4 us -> 43.5 us (level)
  waiting for transfers between devices: 8.02 us -> 8.74 us
  starting transfers between devices: 18 us -> 17.4 us
    ppermute x3, waiting for transfers between devices: 0.92 us -> 1.64 us  [shift(): lax.ppermute(value, axis, [(name, names[(at + step) % count]) for at, nam...]
    ppermute x3, starting transfers between devices: 4.92 us -> 4.26 us  [shift(): lax.ppermute(value, axis, [(name, names[(at + step) % count]) for at, nam...]
  transfers between devices with their start and end apart: 14 -> 14, of which waited for: 7 -> 8; matrix products, arithmetic and copies ran while one was open for 0% -> 0% of each run, Pallas kernels for 30% -> 30%
where the time goes in v22:
time: 43.5 us; the launch traced here: 43.3 us
  starting transfers between devices  17.4 us (40%)
  Pallas kernels  16.4 us (38%)
  waiting for transfers between devices  8.74 us (20%)
  between operations  0.77 us (2%)
    pallas_call x15, Pallas kernels, call(): pl.pallas_call(body, out_shape=outs, in_specs=specs, out_specs=out_specs...  16.4 us
    ppermute x11, starting transfers between devices, swap(): return lax.ppermute(value, axis, [(i, i ^ bit) for i in range(count)])  13.1 us
    ppermute x11, waiting for transfers between devices, swap(): return lax.ppermute(value, axis, [(i, i ^ bit) for i in range(count)])  7.11 us
    ppermute x3, starting transfers between devices, shift(): lax.ppermute(value, axis, [(name, names[(at + step) % count]) for at, nam...  4.26 us
    ppermute x3, waiting for transfers between devices, shift(): lax.ppermute(value, axis, [(name, names[(at + step) % count]) for at, nam...  1.64 us
  transfers between devices with their start and end apart: 14, of which 8 were waited for; matrix products, arithmetic and copies ran while one was open for 0% of the time, Pallas kernels for 30%

profile of v22, /device:TPU:0, one launch (start us, length us, event | category | flops | bytes accessed | tf_op | source)
XLA Modules:
  0.0 43.3 jit_solution(6443554294886739483)
XLA Ops:
  0.6 1.4 %shard_map.85 = (bf16[160,256]{1,0:T(8,128)(2,1)S(1)}, f32[160,1]{1,0:T(8,128)S(1)}, bf16[256,1024]{1,0:T(8,128)(2,1)S(1)}, bf16[40,1024]{1,0:T(8,128)(2,1)S(1)}...) custom-call(s32[8,256]{1,0:T(8,128)} %bitcast.2, ...), custom_call_target="tpu_custom_call" | custom-call | flops 83886080 | bytes 1048576 | tf_op jit(solution)/shard_map/pallas_call | solution.py:70
  2.0 4.1 %collective-permute-start.3 = (bf16[40,1024]{1,0:T(8,128)(2,1)S(1)}, bf16[40,1024]{1,0:T(8,128)(2,1)S(1)}, u32[]{:S(2)}, u32[]{:S(2)}) collective-permute-start(bf16[40,1024]{1,0:T(8,128)(2,1)S(1)} %get-tuple-element.46), channel_id=1, source_target_pairs={{0,8},{4,12},{8,0},{12,4},{1,9},{5,13},{9,1},{13,5},{2,10},{6,14},... | collective-permute-start | bytes 245768 | tf_op jit(solution)/shard_map/ppermute | solution.py:318
  6.4 1.6 %collective-permute-start.2 = (bf16[80,1024]{1,0:T(8,128)(2,1)S(1)}, bf16[80,1024]{1,0:T(8,128)(2,1)S(1)}, u32[]{:S(2)}, u32[]{:S(2)}) collective-permute-start(bf16[80,1024]{1,0:T(8,128)(2,1)S(1)} %get-tuple-element.44), channel_id=1, source_target_pairs={{0,4},{4,0},{8,12},{12,8},{1,5},{5,1},{9,13},{13,9},{2,6},{6,2},{1... | collective-permute-start | bytes 491528 | tf_op jit(solution)/shard_map/ppermute | solution.py:318
  8.0 3.8 %shard_map.87 = (bf16[3,768,1024]{2,1,0:T(8,128)(2,1)S(1)}, bf16[3,768,1024]{2,1,0:T(8,128)(2,1)S(1)}, bf16[40,1024]{1,0:T(8,128)(2,1)S(1)}, bf16[40,1024]{1,0:T(8,128)(2,1)S(1)}, bf16[40,1024]{1,0:T(8,128)(2,1)S(1)}) custom-call(bf16[1,2,1536,1024]{3,2,1,0:T(8,128)(2,1)} %gate_up.1, bf16[1,1536,1024]{2,1,0:T(8,128)(2,1)} %down.1, ...), custom_call_target="tpu_custom_call" | custom-call | flops 251658240 | bytes 3145728 | tf_op jit(solution)/shard_map/pallas_call | solution.py:70
  11.8 2.0 %collective-permute-start = (bf16[40,1024]{1,0:T(8,128)(2,1)S(1)}, bf16[40,1024]{1,0:T(8,128)(2,1)S(1)}, u32[]{:S(2)}, u32[]{:S(2)}) collective-permute-start(bf16[40,1024]{1,0:T(8,128)(2,1)S(1)} %get-tuple-element.42), channel_id=1, source_target_pairs={{0,8},{4,12},{8,0},{12,4},{1,9},{5,13},{9,1},{13,5},{2,10},{6,14},... | collective-permute-start | bytes 245768 | tf_op jit(solution)/shard_map/ppermute | solution.py:318
  13.8 2.0 %collective-permute-start.1 = (bf16[40,1024]{1,0:T(8,128)(2,1)S(1)}, bf16[40,1024]{1,0:T(8,128)(2,1)S(1)}, u32[]{:S(2)}, u32[]{:S(2)}) collective-permute-start(bf16[40,1024]{1,0:T(8,128)(2,1)S(1)} %get-tuple-element.43), channel_id=1, source_target_pairs={{0,12},{4,8},{8,4},{12,0},{1,13},{5,9},{9,5},{13,1},{2,14},{6,10},... | collective-permute-start | bytes 245768 | tf_op jit(solution)/shard_map/ppermute | solution.py:318
  15.8 1.4 %shard_map.89 = (bf16[2,80,768]{2,1,0:T(8,128)(2,1)S(1)}, bf16[160,80]{1,0:T(8,128)(2,1)S(1)}, bf16[80,1024]{1,0:T(8,128)(2,1)S(1)}) custom-call(bf16[40,1024]{1,0:T(8,128)(2,1)S(1)} %shard_map.88.refs_0_, bf16[40,1024]{1,0:T(8,128)(2,1)S(1)} %collective-permute-done.4.refs_1_, bf16[80,1024]{1,0:T(8,128)(2,1)S(1)} %collective-permute-done.2.refs_2_, ...), custom_call_target="tpu_custom_call" | custom-call | flops 503316480 | bytes 3145728 | tf_op jit(solution)/shard_map/pallas_call | solution.py:70
  17.4 1.1 %shard_map.91.mine = bf16[2,80,768]{2,1,0:T(8,128)(2,1)S(1)} custom-call(bf16[80,1024]{1,0:T(8,128)(2,1)S(1)} %get-tuple-element.53.rows_in, bf16[3,768,1024]{2,1,0:T(8,128)(2,1)S(1)} %get-tuple-element.51.refs_5_.held), custom_call_target="tpu_custom_call" | custom-call | flops 25165824000 | bytes 314572800 | tf_op jit(solution)/shard_map/pallas_call | solution.py:70
  18.4 0.4 collective-permute-done.5.other
  18.9 1.6 %collective-permute-start.8 = (bf16[2,80,768]{2,1,0:T(8,128)(2,1)S(1)}, bf16[2,80,768]{2,1,0:T(8,128)(2,1)S(1)}, u32[]{:S(2)}, u32[]{:S(2)}) collective-permute-start(bf16[2,80,768]{2,1,0:T(8,128)(2,1)S(1)} %get-tuple-element.55.refs_6_), channel_id=1, source_target_pairs={{0,2},{1,3},{2,0},{3,1},{4,6},{5,7},{6,4},{7,5},{8,10},{9,11},{10,... | collective-permute-start | bytes 737288 | tf_op jit(solution)/shard_map/ppermute | solution.py:318
  20.8 0.7 %shard_map.93 = bf16[80,768]{1,0:T(8,128)(2,1)S(1)} custom-call(bf16[40,1024]{1,0:T(8,128)(2,1)S(1)} %collective-permute-done.refs_0_, bf16[40,1024]{1,0:T(8,128)(2,1)S(1)} %collective-permute-done.1.refs_1_, bf16[80,1024]{1,0:T(8,128)(2,1)S(1)} %collective-permute-done.2.refs_2_, bf16[40,1024]{1,0:T(8,128)(2,1)S(1)} %get-tuple-element.45.refs_3_, ...), custom_call_target="tpu_custom_call" | custom-call | flops 251658240 | bytes 3145728 | tf_op jit(solution)/shard_map/pallas_call | solution.py:70
  21.6 0.7 %shard_map.90 = (bf16[80,1024]{1,0:T(8,128)(2,1)S(1)}, bf16[80,768]{1,0:T(8,128)(2,1)S(1)}) custom-call(bf16[40,1024]{1,0:T(8,128)(2,1)S(1)} %collective-permute-done.refs_0_, bf16[40,1024]{1,0:T(8,128)(2,1)S(1)} %collective-permute-done.1.refs_1_, bf16[80,1024]{1,0:T(8,128)(2,1)S(1)} %collective-permute-done.2.refs_2_, ...), custom_call_target="tpu_custom_call" | custom-call | flops 25165824000 | bytes 314572800 | tf_op jit(solution)/shard_map/pallas_call | solution.py:70
  22.3 0.6 %collective-permute-done.6 = bf16[80,768]{1,0:T(8,128)(2,1)S(1)} collective-permute-done((bf16[80,768]{1,0:T(8,128)(2,1)S(1)}, bf16[80,768]{1,0:T(8,128)(2,1)S(1)}, u32[]{:S(2)}, u32[]{:S(2)}) %collective-permute-start.6) | collective-permute-done | bytes 122912 | tf_op jit(solution)/shard_map/ppermute | solution.py:318
  22.9 1.6 %collective-permute-start.7 = (bf16[80,768]{1,0:T(8,128)(2,1)S(1)}, bf16[80,768]{1,0:T(8,128)(2,1)S(1)}, u32[]{:S(2)}, u32[]{:S(2)}) collective-permute-start(bf16[80,768]{1,0:T(8,128)(2,1)S(1)} %get-tuple-element.67), channel_id=1, source_target_pairs={{0,2},{1,3},{2,0},{3,1},{4,6},{5,7},{6,4},{7,5},{8,10},{9,11},{10,... | collective-permute-start | bytes 368648 | tf_op jit(solution)/shard_map/ppermute | solution.py:318
  24.5 3.3 %collective-permute-done.8.pair_far = bf16[2,80,768]{2,1,0:T(8,128)(2,1)S(1)} collective-permute-done((bf16[2,80,768]{2,1,0:T(8,128)(2,1)S(1)}, bf16[2,80,768]{2,1,0:T(8,128)(2,1)S(1)}, u32[]{:S(2)}, u32[]{:S(2)}) %collective-permute-start.8) | collective-permute-done | bytes 245792 | tf_op jit(solution)/shard_map/ppermute | solution.py:318
  28.0 1.6 %collective-permute-done.7.act_far = bf16[80,768]{1,0:T(8,128)(2,1)S(1)} collective-permute-done((bf16[80,768]{1,0:T(8,128)(2,1)S(1)}, bf16[80,768]{1,0:T(8,128)(2,1)S(1)}, u32[]{:S(2)}, u32[]{:S(2)}) %collective-permute-start.7) | collective-permute-done | bytes 122912 | tf_op jit(solution)/shard_map/ppermute | solution.py:318
  29.8 0.7 %shard_map.96.total = f32[80,1024]{1,0:T(8,128)S(1)} custom-call(bf16[2,80,768]{2,1,0:T(8,128)(2,1)S(1)} %shard_map.95.mine, bf16[3,768,1024]{2,1,0:T(8,128)(2,1)S(1)} %get-tuple-element.51.refs_5_.held), custom_call_target="tpu_custom_call" | custom-call | flops 251658240 | bytes 3145728 | tf_op jit(solution)/shard_map/pallas_call | solution.py:70
  30.4 0.8 %collective-permute-done.10.other = bf16[2,80,768]{2,1,0:T(8,128)(2,1)S(1)} collective-permute-done((bf16[2,80,768]{2,1,0:T(8,128)(2,1)S(1)}, bf16[2,80,768]{2,1,0:T(8,128)(2,1)S(1)}, u32[]{:S(2)}, u32[]{:S(2)}) %collective-permute-start.10) | collective-permute-done | bytes 245792 | tf_op jit(solution)/shard_map/ppermute | solution.py:318
  31.3 0.9 %shard_map.97 = (bf16[40,1024]{1,0:T(8,128)(2,1)S(1)}, bf16[40,1024]{1,0:T(8,128)(2,1)S(1)}, bf16[40,1024]{1,0:T(8,128)(2,1)S(1)}, bf16[40,1024]{1,0:T(8,128)(2,1)S(1)}) custom-call(f32[80,1024]{1,0:T(8,128)S(1)} %shard_map.96.total, bf16[2,80,768]{2,1,0:T(8,128)(2,1)S(1)} %collective-permute-done.10.other, ...), custom_call_target="tpu_custom_call" | custom-call | flops 251658240 | bytes 3145728 | tf_op jit(solution)/shard_map/pallas_call | solution.py:70
  32.2 2.2 %collective-permute-start.11 = (bf16[40,1024]{1,0:T(8,128)(2,1)S(1)}, bf16[40,1024]{1,0:T(8,128)(2,1)S(1)}, u32[]{:S(2)}, u32[]{:S(2)}) collective-permute-start(bf16[40,1024]{1,0:T(8,128)(2,1)S(1)} %get-tuple-element.60), channel_id=1, source_target_pairs={{0,12},{4,8},{12,0},{8,4},{1,13},{5,9},{13,1},{9,5},{2,14},{6,10},... | collective-permute-start | bytes 245768 | tf_op jit(solution)/shard_map/ppermute | solution.py:311
  34.4 2.0 %collective-permute-start.13 = (bf16[40,1024]{1,0:T(8,128)(2,1)S(1)}, bf16[40,1024]{1,0:T(8,128)(2,1)S(1)}, u32[]{:S(2)}, u32[]{:S(2)}) collective-permute-start(bf16[40,1024]{1,0:T(8,128)(2,1)S(1)} %get-tuple-element.62), channel_id=1, source_target_pairs={{0,4},{4,12},{12,8},{8,0},{1,5},{5,13},{13,9},{9,1},{2,6},{6,14},{... | collective-permute-start | bytes 245768 | tf_op jit(solution)/shard_map/ppermute | solution.py:311
  36.4 4.1 %shard_map.99 = (bf16[1,2,1536,1024]{3,2,1,0:T(8,128)(2,1)}, bf16[1,1536,1024]{2,1,0:T(8,128)(2,1)}) custom-call(bf16[80,768]{1,0:T(8,128)(2,1)S(1)} %get-tuple-element.59.mine_act, bf16[80,768]{1,0:T(8,128)(2,1)S(1)} %collective-permute-done.9._.other_act, bf16[2,80,768]{2,1,0:T(8,128)(2,1)S(1)} %shard_map.95.mine, ...), custom_call_target="tpu_custom_call" | custom-call | flops 754974720 | bytes 9437184 | tf_op jit(solution)/shard_map/pallas_call | solution.py:70
  41.0 1.2 %collective-permute-done.13.refs_2_ = bf16[40,1024]{1,0:T(8,128)(2,1)S(1)} collective-permute-done((bf16[40,1024]{1,0:T(8,128)(2,1)S(1)}, bf16[40,1024]{1,0:T(8,128)(2,1)S(1)}, u32[]{:S(2)}, u32[]{:S(2)}) %collective-permute-start.13) | collective-permute-done | bytes 81952 | tf_op jit(solution)/shard_map/ppermute | solution.py:311
  42.2 1.1 %shard_map.98 = bf16[256,1024]{1,0:T(8,128)(2,1)} custom-call(bf16[160,256]{1,0:T(8,128)(2,1)S(1)} %get-tuple-element.35.pick, bf16[40,1024]{1,0:T(8,128)(2,1)S(1)} %collective-permute-done.11.refs_0_, bf16[40,1024]{1,0:T(8,128)(2,1)S(1)} %collective-permute-done.12.refs_1_, bf16[40,1024]{1,0:T(8,128)(2,1)S(1)} %collective-permute-done.13.refs_2_, ...), custom_call_target="tpu_custom_call" | custom-call | flops 83886080 | bytes 1048576 | tf_op jit(solution)/shard_map/pallas_call | solution.py:70
  (20 shorter events, 1.6 us)
Async XLA Ops:
  2.0 13.8 %collective-permute-start.3 = (bf16[40,1024]{1,0:T(8,128)(2,1)S(1)}, bf16[40,1024]{1,0:T(8,128)(2,1)S(1)}, u32[]{:S(2)}, u32[]{:S(2)}) collective-permute-start(bf16[40,1024]{1,0:T(8,128)(2,1)S(1)} %get-tuple-element.46), channel_id=1, source_target_pairs={{0,8},{4,12},{8,0},{12,4},{1,9},{5,13},{9,1},{13,5},{2,10},{6,14},... | collective-permute-start | bytes 245768 | tf_op jit(solution)/shard_map/ppermute | solution.py:318
  6.4 9.4 %collective-permute-start.2 = (bf16[80,1024]{1,0:T(8,128)(2,1)S(1)}, bf16[80,1024]{1,0:T(8,128)(2,1)S(1)}, u32[]{:S(2)}, u32[]{:S(2)}) collective-permute-start(bf16[80,1024]{1,0:T(8,128)(2,1)S(1)} %get-tuple-element.44), channel_id=1, source_target_pairs={{0,4},{4,0},{8,12},{12,8},{1,5},{5,1},{9,13},{13,9},{2,6},{6,2},{1... | collective-permute-start | bytes 491528 | tf_op jit(solution)/shard_map/ppermute | solution.py:318
  8.0 7.8 %collective-permute-start.4 = (bf16[40,1024]{1,0:T(8,128)(2,1)S(1)}, bf16[40,1024]{1,0:T(8,128)(2,1)S(1)}, u32[]{:S(2)}, u32[]{:S(2)}) collective-permute-start(bf16[40,1024]{1,0:T(8,128)(2,1)S(1)} %get-tuple-element.47), channel_id=1, source_target_pairs={{0,12},{4,8},{8,4},{12,0},{1,13},{5,9},{9,5},{13,1},{2,14},{6,10},... | collective-permute-start | bytes 245768 | tf_op jit(solution)/shard_map/ppermute | solution.py:318
  11.8 8.9 %collective-permute-start = (bf16[40,1024]{1,0:T(8,128)(2,1)S(1)}, bf16[40,1024]{1,0:T(8,128)(2,1)S(1)}, u32[]{:S(2)}, u32[]{:S(2)}) collective-permute-start(bf16[40,1024]{1,0:T(8,128)(2,1)S(1)} %get-tuple-element.42), channel_id=1, source_target_pairs={{0,8},{4,12},{8,0},{12,4},{1,9},{5,13},{9,1},{13,5},{2,10},{6,14},... | collective-permute-start | bytes 245768 | tf_op jit(solution)/shard_map/ppermute | solution.py:318
  13.8 7.0 %collective-permute-start.1 = (bf16[40,1024]{1,0:T(8,128)(2,1)S(1)}, bf16[40,1024]{1,0:T(8,128)(2,1)S(1)}, u32[]{:S(2)}, u32[]{:S(2)}) collective-permute-start(bf16[40,1024]{1,0:T(8,128)(2,1)S(1)} %get-tuple-element.43), channel_id=1, source_target_pairs={{0,12},{4,8},{8,4},{12,0},{1,13},{5,9},{9,5},{13,1},{2,14},{6,10},... | collective-permute-start | bytes 245768 | tf_op jit(solution)/shard_map/ppermute | solution.py:318
  17.3 1.6 %collective-permute-start.5 = (bf16[2,80,768]{2,1,0:T(8,128)(2,1)S(1)}, bf16[2,80,768]{2,1,0:T(8,128)(2,1)S(1)}, u32[]{:S(2)}, u32[]{:S(2)}) collective-permute-start(bf16[2,80,768]{2,1,0:T(8,128)(2,1)S(1)} %get-tuple-element.54), channel_id=1, source_target_pairs={{0,1},{1,0},{2,3},{3,2},{4,5},{5,4},{6,7},{7,6},{8,9},{9,8},{10,11... | collective-permute-start | bytes 737288 | tf_op jit(solution)/shard_map/ppermute | solution.py:318
  18.9 8.9 %collective-permute-start.8 = (bf16[2,80,768]{2,1,0:T(8,128)(2,1)S(1)}, bf16[2,80,768]{2,1,0:T(8,128)(2,1)S(1)}, u32[]{:S(2)}, u32[]{:S(2)}) collective-permute-start(bf16[2,80,768]{2,1,0:T(8,128)(2,1)S(1)} %get-tuple-element.55.refs_6_), channel_id=1, source_target_pairs={{0,2},{1,3},{2,0},{3,1},{4,6},{5,7},{6,4},{7,5},{8,10},{9,11},{10,... | collective-permute-start | bytes 737288 | tf_op jit(solution)/shard_map/ppermute | solution.py:318
  21.5 1.4 %collective-permute-start.6 = (bf16[80,768]{1,0:T(8,128)(2,1)S(1)}, bf16[80,768]{1,0:T(8,128)(2,1)S(1)}, u32[]{:S(2)}, u32[]{:S(2)}) collective-permute-start(bf16[80,768]{1,0:T(8,128)(2,1)S(1)} %shard_map.93), channel_id=1, source_target_pairs={{0,1},{1,0},{2,3},{3,2},{4,5},{5,4},{6,7},{7,6},{8,9},{9,8},{10,11... | collective-permute-start | bytes 368648 | tf_op jit(solution)/shard_map/ppermute | solution.py:318
  22.9 6.7 %collective-permute-start.7 = (bf16[80,768]{1,0:T(8,128)(2,1)S(1)}, bf16[80,768]{1,0:T(8,128)(2,1)S(1)}, u32[]{:S(2)}, u32[]{:S(2)}) collective-permute-start(bf16[80,768]{1,0:T(8,128)(2,1)S(1)} %get-tuple-element.67), channel_id=1, source_target_pairs={{0,2},{1,3},{2,0},{3,1},{4,6},{5,7},{6,4},{7,5},{8,10},{9,11},{10,... | collective-permute-start | bytes 368648 | tf_op jit(solution)/shard_map/ppermute | solution.py:318
  27.9 1.7 %collective-permute-start.9 = (bf16[80,768]{1,0:T(8,128)(2,1)S(1)}, bf16[80,768]{1,0:T(8,128)(2,1)S(1)}, u32[]{:S(2)}, u32[]{:S(2)}) collective-permute-start(bf16[80,768]{1,0:T(8,128)(2,1)S(1)} %get-tuple-element.59.mine_act), channel_id=1, source_target_pairs={{0,1},{1,0},{2,3},{3,2},{4,5},{5,4},{6,7},{7,6},{8,9},{9,8},{10,11... | collective-permute-start | bytes 368648 | tf_op jit(solution)/shard_map/ppermute | solution.py:318
  29.7 1.6 %collective-permute-start.10 = (bf16[2,80,768]{2,1,0:T(8,128)(2,1)S(1)}, bf16[2,80,768]{2,1,0:T(8,128)(2,1)S(1)}, u32[]{:S(2)}, u32[]{:S(2)}) collective-permute-start(bf16[2,80,768]{2,1,0:T(8,128)(2,1)S(1)} %shard_map.95.mine), channel_id=1, source_target_pairs={{0,1},{1,0},{2,3},{3,2},{4,5},{5,4},{6,7},{7,6},{8,9},{9,8},{10,11... | collective-permute-start | bytes 737288 | tf_op jit(solution)/shard_map/ppermute | solution.py:318
  32.2 8.4 %collective-permute-start.11 = (bf16[40,1024]{1,0:T(8,128)(2,1)S(1)}, bf16[40,1024]{1,0:T(8,128)(2,1)S(1)}, u32[]{:S(2)}, u32[]{:S(2)}) collective-permute-start(bf16[40,1024]{1,0:T(8,128)(2,1)S(1)} %get-tuple-element.60), channel_id=1, source_target_pairs={{0,12},{4,8},{12,0},{8,4},{1,13},{5,9},{13,1},{9,5},{2,14},{6,10},... | collective-permute-start | bytes 245768 | tf_op jit(solution)/shard_map/ppermute | solution.py:311
  34.4 6.6 %collective-permute-start.12 = (bf16[40,1024]{1,0:T(8,128)(2,1)S(1)}, bf16[40,1024]{1,0:T(8,128)(2,1)S(1)}, u32[]{:S(2)}, u32[]{:S(2)}) collective-permute-start(bf16[40,1024]{1,0:T(8,128)(2,1)S(1)} %get-tuple-element.61), channel_id=1, source_target_pairs={{0,8},{4,0},{12,4},{8,12},{1,9},{5,1},{13,5},{9,13},{2,10},{6,2},{... | collective-permute-start | bytes 245768 | tf_op jit(solution)/shard_map/ppermute | solution.py:311
  34.4 7.8 %collective-permute-start.13 = (bf16[40,1024]{1,0:T(8,128)(2,1)S(1)}, bf16[40,1024]{1,0:T(8,128)(2,1)S(1)}, u32[]{:S(2)}, u32[]{:S(2)}) collective-permute-start(bf16[40,1024]{1,0:T(8,128)(2,1)S(1)} %get-tuple-element.62), channel_id=1, source_target_pairs={{0,4},{4,12},{12,8},{8,0},{1,5},{5,13},{13,9},{9,1},{2,6},{6,14},{... | collective-permute-start | bytes 245768 | tf_op jit(solution)/shard_map/ppermute | solution.py:311

commit v23 on v19

--- a/solution.py
+++ b/solution.py
@@ -202,7 +202,8 @@
 
 def act_part(experts, own, *refs):
     place, held = refs[experts : experts + 2]
-    rows_grad = mm(place[...], stacked(refs[:experts], 1).astype(BF), ROWS).astype(BF)
+    pieces = refs[: experts - 2][::-1] + refs[experts - 2 : experts]
+    rows_grad = mm(place[...], stacked(pieces, 1).astype(BF), ROWS).astype(BF)
     if own:
         refs[-2][...] = rows_grad
     refs[-1][...] = mm(rows_grad, held[2], LANES).astype(BF)
@@ -384,7 +385,7 @@
         flops=WCOST * weight_flops,
         traffic=WCOST * weight_bytes,
     )
-    got_grad = [swap(part, "ex", k) for part, k in zip(send_grad[:-1], order)]
+    got_grad = [swap(part, "ex", k) for part, k in zip(send_grad[:-1], order)][::-1]
     got_grad = got_grad + [near, send_grad[-1]]
     pair_other, place, rows_in = call(
         functools.partial(other_pair, experts, capacity),

time: 43.4 us -> 43.4 us (level)
  waiting for transfers between devices: 8.02 us -> 7.11 us
  starting transfers between devices: 18 us -> 18.9 us
    ppermute x3, starting transfers between devices: 4.92 us -> 5.89 us  [shift(): lax.ppermute(value, axis, [(name, names[(at + step) % count]) for at, nam...]
    ppermute x3, waiting for transfers between devices: 0.92 us -> 0.01 us  [shift(): lax.ppermute(value, axis, [(name, names[(at + step) % count]) for at, nam...]
  transfers between devices with their start and end apart: 14 -> 14, of which waited for: 7 -> 6; matrix products, arithmetic and copies ran while one was open for 0% -> 0% of each run, Pallas kernels for 30% -> 30%
where the time goes in v23:
time: 43.4 us; the launch traced here: 43.2 us
  starting transfers between devices  18.9 us (44%)
  Pallas kernels  16.4 us (38%)
  waiting for transfers between devices  7.11 us (16%)
  between operations  0.79 us (2%)
    pallas_call x15, Pallas kernels, call(): pl.pallas_call(body, out_shape=outs, in_specs=specs, out_specs=out_specs...  16.4 us
    ppermute x11, starting transfers between devices, swap(): return lax.ppermute(value, axis, [(i, i ^ bit) for i in range(count)])  13 us
    ppermute x11, waiting for transfers between devices, swap(): return lax.ppermute(value, axis, [(i, i ^ bit) for i in range(count)])  7.11 us
    ppermute x3, starting transfers between devices, shift(): lax.ppermute(value, axis, [(name, names[(at + step) % count]) for at, nam...  5.89 us
  transfers between devices with their start and end apart: 14, of which 6 were waited for; matrix products, arithmetic and copies ran while one was open for 0% of the time, Pallas kernels for 30%

profile of v23, /device:TPU:0, one launch (start us, length us, event | category | flops | bytes accessed | tf_op | source)
XLA Modules:
  0.0 43.2 jit_solution(5134653281043290463)
XLA Ops:
  0.6 1.4 %shard_map.85 = (bf16[160,256]{1,0:T(8,128)(2,1)S(1)}, f32[160,1]{1,0:T(8,128)S(1)}, bf16[256,1024]{1,0:T(8,128)(2,1)S(1)}, bf16[40,1024]{1,0:T(8,128)(2,1)S(1)}...) custom-call(s32[8,256]{1,0:T(8,128)} %bitcast.2, ...), custom_call_target="tpu_custom_call" | custom-call | flops 83886080 | bytes 1048576 | tf_op jit(solution)/shard_map/pallas_call | solution.py:70
  2.0 4.1 %collective-permute-start.3 = (bf16[40,1024]{1,0:T(8,128)(2,1)S(1)}, bf16[40,1024]{1,0:T(8,128)(2,1)S(1)}, u32[]{:S(2)}, u32[]{:S(2)}) collective-permute-start(bf16[40,1024]{1,0:T(8,128)(2,1)S(1)} %get-tuple-element.46), channel_id=1, source_target_pairs={{0,8},{4,12},{8,0},{12,4},{1,9},{5,13},{9,1},{13,5},{2,10},{6,14},... | collective-permute-start | bytes 245768 | tf_op jit(solution)/shard_map/ppermute | solution.py:319
  6.4 1.6 %collective-permute-start.2 = (bf16[80,1024]{1,0:T(8,128)(2,1)S(1)}, bf16[80,1024]{1,0:T(8,128)(2,1)S(1)}, u32[]{:S(2)}, u32[]{:S(2)}) collective-permute-start(bf16[80,1024]{1,0:T(8,128)(2,1)S(1)} %get-tuple-element.44), channel_id=1, source_target_pairs={{0,4},{4,0},{8,12},{12,8},{1,5},{5,1},{9,13},{13,9},{2,6},{6,2},{1... | collective-permute-start | bytes 491528 | tf_op jit(solution)/shard_map/ppermute | solution.py:319
  8.0 3.8 %shard_map.87 = (bf16[3,768,1024]{2,1,0:T(8,128)(2,1)S(1)}, bf16[3,768,1024]{2,1,0:T(8,128)(2,1)S(1)}, bf16[40,1024]{1,0:T(8,128)(2,1)S(1)}, bf16[40,1024]{1,0:T(8,128)(2,1)S(1)}, bf16[40,1024]{1,0:T(8,128)(2,1)S(1)}) custom-call(bf16[1,2,1536,1024]{3,2,1,0:T(8,128)(2,1)} %gate_up.1, bf16[1,1536,1024]{2,1,0:T(8,128)(2,1)} %down.1, ...), custom_call_target="tpu_custom_call" | custom-call | flops 251658240 | bytes 3145728 | tf_op jit(solution)/shard_map/pallas_call | solution.py:70
  11.8 3.9 %collective-permute-start = (bf16[40,1024]{1,0:T(8,128)(2,1)S(1)}, bf16[40,1024]{1,0:T(8,128)(2,1)S(1)}, u32[]{:S(2)}, u32[]{:S(2)}) collective-permute-start(bf16[40,1024]{1,0:T(8,128)(2,1)S(1)} %get-tuple-element.42), channel_id=1, source_target_pairs={{0,12},{4,8},{8,4},{12,0},{1,13},{5,9},{9,5},{13,1},{2,14},{6,10},... | collective-permute-start | bytes 245768 | tf_op jit(solution)/shard_map/ppermute | solution.py:319
  15.8 1.4 %shard_map.89 = (bf16[2,80,768]{2,1,0:T(8,128)(2,1)S(1)}, bf16[160,80]{1,0:T(8,128)(2,1)S(1)}, bf16[80,1024]{1,0:T(8,128)(2,1)S(1)}) custom-call(bf16[40,1024]{1,0:T(8,128)(2,1)S(1)} %shard_map.88.refs_0_, bf16[40,1024]{1,0:T(8,128)(2,1)S(1)} %collective-permute-done.4.refs_1_, bf16[80,1024]{1,0:T(8,128)(2,1)S(1)} %collective-permute-done.2.refs_2_, ...), custom_call_target="tpu_custom_call" | custom-call | flops 503316480 | bytes 3145728 | tf_op jit(solution)/shard_map/pallas_call | solution.py:70
  17.3 1.1 %shard_map.91.mine = bf16[2,80,768]{2,1,0:T(8,128)(2,1)S(1)} custom-call(bf16[80,1024]{1,0:T(8,128)(2,1)S(1)} %get-tuple-element.53.rows_in, bf16[3,768,1024]{2,1,0:T(8,128)(2,1)S(1)} %get-tuple-element.51.refs_5_.held), custom_call_target="tpu_custom_call" | custom-call | flops 25165824000 | bytes 314572800 | tf_op jit(solution)/shard_map/pallas_call | solution.py:70
  18.4 0.4 collective-permute-done.5.other
  18.9 1.6 %collective-permute-start.8 = (bf16[2,80,768]{2,1,0:T(8,128)(2,1)S(1)}, bf16[2,80,768]{2,1,0:T(8,128)(2,1)S(1)}, u32[]{:S(2)}, u32[]{:S(2)}) collective-permute-start(bf16[2,80,768]{2,1,0:T(8,128)(2,1)S(1)} %get-tuple-element.55.refs_6_), channel_id=1, source_target_pairs={{0,2},{1,3},{2,0},{3,1},{4,6},{5,7},{6,4},{7,5},{8,10},{9,11},{10,... | collective-permute-start | bytes 737288 | tf_op jit(solution)/shard_map/ppermute | solution.py:319
  20.4 1.3 %collective-permute-done.1.refs_1_ = bf16[40,1024]{1,0:T(8,128)(2,1)S(1)} collective-permute-done((bf16[40,1024]{1,0:T(8,128)(2,1)S(1)}, bf16[40,1024]{1,0:T(8,128)(2,1)S(1)}, u32[]{:S(2)}, u32[]{:S(2)}) %collective-permute-start.1) | collective-permute-done | bytes 81952 | tf_op jit(solution)/shard_map/ppermute | solution.py:319
  21.7 0.7 %shard_map.93 = bf16[80,768]{1,0:T(8,128)(2,1)S(1)} custom-call(bf16[40,1024]{1,0:T(8,128)(2,1)S(1)} %collective-permute-done.refs_0_, bf16[40,1024]{1,0:T(8,128)(2,1)S(1)} %collective-permute-done.1.refs_1_, bf16[80,1024]{1,0:T(8,128)(2,1)S(1)} %collective-permute-done.2.refs_2_, bf16[40,1024]{1,0:T(8,128)(2,1)S(1)} %get-tuple-element.45.refs_3_, ...), custom_call_target="tpu_custom_call" | custom-call | flops 251658240 | bytes 3145728 | tf_op jit(solution)/shard_map/pallas_call | solution.py:70
  22.5 0.7 %shard_map.90 = (bf16[80,1024]{1,0:T(8,128)(2,1)S(1)}, bf16[80,768]{1,0:T(8,128)(2,1)S(1)}) custom-call(bf16[40,1024]{1,0:T(8,128)(2,1)S(1)} %collective-permute-done.refs_0_, bf16[40,1024]{1,0:T(8,128)(2,1)S(1)} %collective-permute-done.1.refs_1_, bf16[80,1024]{1,0:T(8,128)(2,1)S(1)} %collective-permute-done.2.refs_2_, ...), custom_call_target="tpu_custom_call" | custom-call | flops 25165824000 | bytes 314572800 | tf_op jit(solution)/shard_map/pallas_call | solution.py:70
  23.2 0.6 %collective-permute-done.6 = bf16[80,768]{1,0:T(8,128)(2,1)S(1)} collective-permute-done((bf16[80,768]{1,0:T(8,128)(2,1)S(1)}, bf16[80,768]{1,0:T(8,128)(2,1)S(1)}, u32[]{:S(2)}, u32[]{:S(2)}) %collective-permute-start.6) | collective-permute-done | bytes 122912 | tf_op jit(solution)/shard_map/ppermute | solution.py:319
  23.9 1.6 %collective-permute-start.7 = (bf16[80,768]{1,0:T(8,128)(2,1)S(1)}, bf16[80,768]{1,0:T(8,128)(2,1)S(1)}, u32[]{:S(2)}, u32[]{:S(2)}) collective-permute-start(bf16[80,768]{1,0:T(8,128)(2,1)S(1)} %get-tuple-element.67), channel_id=1, source_target_pairs={{0,2},{1,3},{2,0},{3,1},{4,6},{5,7},{6,4},{7,5},{8,10},{9,11},{10,... | collective-permute-start | bytes 368648 | tf_op jit(solution)/shard_map/ppermute | solution.py:319
  25.4 1.7 %collective-permute-done.8.pair_far = bf16[2,80,768]{2,1,0:T(8,128)(2,1)S(1)} collective-permute-done((bf16[2,80,768]{2,1,0:T(8,128)(2,1)S(1)}, bf16[2,80,768]{2,1,0:T(8,128)(2,1)S(1)}, u32[]{:S(2)}, u32[]{:S(2)}) %collective-permute-start.8) | collective-permute-done | bytes 245792 | tf_op jit(solution)/shard_map/ppermute | solution.py:319
  27.3 2.2 %collective-permute-done.7.act_far = bf16[80,768]{1,0:T(8,128)(2,1)S(1)} collective-permute-done((bf16[80,768]{1,0:T(8,128)(2,1)S(1)}, bf16[80,768]{1,0:T(8,128)(2,1)S(1)}, u32[]{:S(2)}, u32[]{:S(2)}) %collective-permute-start.7) | collective-permute-done | bytes 122912 | tf_op jit(solution)/shard_map/ppermute | solution.py:319
  29.7 0.7 %shard_map.96.total = f32[80,1024]{1,0:T(8,128)S(1)} custom-call(bf16[2,80,768]{2,1,0:T(8,128)(2,1)S(1)} %shard_map.95.mine, bf16[3,768,1024]{2,1,0:T(8,128)(2,1)S(1)} %get-tuple-element.51.refs_5_.held), custom_call_target="tpu_custom_call" | custom-call | flops 251658240 | bytes 3145728 | tf_op jit(solution)/shard_map/pallas_call | solution.py:70
  30.4 0.8 %collective-permute-done.10.other = bf16[2,80,768]{2,1,0:T(8,128)(2,1)S(1)} collective-permute-done((bf16[2,80,768]{2,1,0:T(8,128)(2,1)S(1)}, bf16[2,80,768]{2,1,0:T(8,128)(2,1)S(1)}, u32[]{:S(2)}, u32[]{:S(2)}) %collective-permute-start.10) | collective-permute-done | bytes 245792 | tf_op jit(solution)/shard_map/ppermute | solution.py:319
  31.2 0.9 %shard_map.97 = (bf16[40,1024]{1,0:T(8,128)(2,1)S(1)}, bf16[40,1024]{1,0:T(8,128)(2,1)S(1)}, bf16[40,1024]{1,0:T(8,128)(2,1)S(1)}, bf16[40,1024]{1,0:T(8,128)(2,1)S(1)}) custom-call(f32[80,1024]{1,0:T(8,128)S(1)} %shard_map.96.total, bf16[2,80,768]{2,1,0:T(8,128)(2,1)S(1)} %collective-permute-done.10.other, ...), custom_call_target="tpu_custom_call" | custom-call | flops 251658240 | bytes 3145728 | tf_op jit(solution)/shard_map/pallas_call | solution.py:70
  32.1 0.7 %collective-permute-start.11 = (bf16[40,1024]{1,0:T(8,128)(2,1)S(1)}, bf16[40,1024]{1,0:T(8,128)(2,1)S(1)}, u32[]{:S(2)}, u32[]{:S(2)}) collective-permute-start(bf16[40,1024]{1,0:T(8,128)(2,1)S(1)} %get-tuple-element.60), channel_id=1, source_target_pairs={{0,4},{4,8},{8,12},{12,0},{1,5},{5,9},{9,13},{13,1},{2,6},{6,10},{... | collective-permute-start | bytes 245768 | tf_op jit(solution)/shard_map/ppermute | solution.py:312
  32.8 2.4 %collective-permute-start.12 = (bf16[40,1024]{1,0:T(8,128)(2,1)S(1)}, bf16[40,1024]{1,0:T(8,128)(2,1)S(1)}, u32[]{:S(2)}, u32[]{:S(2)}) collective-permute-start(bf16[40,1024]{1,0:T(8,128)(2,1)S(1)} %get-tuple-element.61), channel_id=1, source_target_pairs={{0,8},{4,12},{8,0},{12,4},{1,9},{5,13},{9,1},{13,5},{2,10},{6,14},... | collective-permute-start | bytes 245768 | tf_op jit(solution)/shard_map/ppermute | solution.py:312
  35.1 2.8 %collective-permute-start.13 = (bf16[40,1024]{1,0:T(8,128)(2,1)S(1)}, bf16[40,1024]{1,0:T(8,128)(2,1)S(1)}, u32[]{:S(2)}, u32[]{:S(2)}) collective-permute-start(bf16[40,1024]{1,0:T(8,128)(2,1)S(1)} %get-tuple-element.62), channel_id=1, source_target_pairs={{0,12},{4,0},{8,4},{12,8},{1,13},{5,1},{9,5},{13,9},{2,14},{6,2},{... | collective-permute-start | bytes 245768 | tf_op jit(solution)/shard_map/ppermute | solution.py:312
  38.0 4.1 %shard_map.99 = (bf16[1,2,1536,1024]{3,2,1,0:T(8,128)(2,1)}, bf16[1,1536,1024]{2,1,0:T(8,128)(2,1)}) custom-call(bf16[80,768]{1,0:T(8,128)(2,1)S(1)} %get-tuple-element.59.mine_act, bf16[80,768]{1,0:T(8,128)(2,1)S(1)} %collective-permute-done.9._.other_act, bf16[2,80,768]{2,1,0:T(8,128)(2,1)S(1)} %shard_map.95.mine, ...), custom_call_target="tpu_custom_call" | custom-call | flops 754974720 | bytes 9437184 | tf_op jit(solution)/shard_map/pallas_call | solution.py:70
  42.1 1.1 %shard_map.98 = bf16[256,1024]{1,0:T(8,128)(2,1)} custom-call(bf16[160,256]{1,0:T(8,128)(2,1)S(1)} %get-tuple-element.35.pick, bf16[40,1024]{1,0:T(8,128)(2,1)S(1)} %collective-permute-done.11.refs_0_, bf16[40,1024]{1,0:T(8,128)(2,1)S(1)} %collective-permute-done.12.refs_1_, bf16[40,1024]{1,0:T(8,128)(2,1)S(1)} %collective-permute-done.13.refs_2_, ...), custom_call_target="tpu_custom_call" | custom-call | flops 83886080 | bytes 1048576 | tf_op jit(solution)/shard_map/pallas_call | solution.py:70
  (20 shorter events, 0.9 us)
Async XLA Ops:
  2.0 13.7 %collective-permute-start.3 = (bf16[40,1024]{1,0:T(8,128)(2,1)S(1)}, bf16[40,1024]{1,0:T(8,128)(2,1)S(1)}, u32[]{:S(2)}, u32[]{:S(2)}) collective-permute-start(bf16[40,1024]{1,0:T(8,128)(2,1)S(1)} %get-tuple-element.46), channel_id=1, source_target_pairs={{0,8},{4,12},{8,0},{12,4},{1,9},{5,13},{9,1},{13,5},{2,10},{6,14},... | collective-permute-start | bytes 245768 | tf_op jit(solution)/shard_map/ppermute | solution.py:319
  6.4 9.4 %collective-permute-start.2 = (bf16[80,1024]{1,0:T(8,128)(2,1)S(1)}, bf16[80,1024]{1,0:T(8,128)(2,1)S(1)}, u32[]{:S(2)}, u32[]{:S(2)}) collective-permute-start(bf16[80,1024]{1,0:T(8,128)(2,1)S(1)} %get-tuple-element.44), channel_id=1, source_target_pairs={{0,4},{4,0},{8,12},{12,8},{1,5},{5,1},{9,13},{13,9},{2,6},{6,2},{1... | collective-permute-start | bytes 491528 | tf_op jit(solution)/shard_map/ppermute | solution.py:319
  8.0 7.7 %collective-permute-start.4 = (bf16[40,1024]{1,0:T(8,128)(2,1)S(1)}, bf16[40,1024]{1,0:T(8,128)(2,1)S(1)}, u32[]{:S(2)}, u32[]{:S(2)}) collective-permute-start(bf16[40,1024]{1,0:T(8,128)(2,1)S(1)} %get-tuple-element.47), channel_id=1, source_target_pairs={{0,12},{4,8},{8,4},{12,0},{1,13},{5,9},{9,5},{13,1},{2,14},{6,10},... | collective-permute-start | bytes 245768 | tf_op jit(solution)/shard_map/ppermute | solution.py:319
  11.8 8.6 %collective-permute-start = (bf16[40,1024]{1,0:T(8,128)(2,1)S(1)}, bf16[40,1024]{1,0:T(8,128)(2,1)S(1)}, u32[]{:S(2)}, u32[]{:S(2)}) collective-permute-start(bf16[40,1024]{1,0:T(8,128)(2,1)S(1)} %get-tuple-element.42), channel_id=1, source_target_pairs={{0,12},{4,8},{8,4},{12,0},{1,13},{5,9},{9,5},{13,1},{2,14},{6,10},... | collective-permute-start | bytes 245768 | tf_op jit(solution)/shard_map/ppermute | solution.py:319
  15.7 6.0 %collective-permute-start.1 = (bf16[40,1024]{1,0:T(8,128)(2,1)S(1)}, bf16[40,1024]{1,0:T(8,128)(2,1)S(1)}, u32[]{:S(2)}, u32[]{:S(2)}) collective-permute-start(bf16[40,1024]{1,0:T(8,128)(2,1)S(1)} %get-tuple-element.43), channel_id=1, source_target_pairs={{0,8},{4,12},{8,0},{12,4},{1,9},{5,13},{9,1},{13,5},{2,10},{6,14},... | collective-permute-start | bytes 245768 | tf_op jit(solution)/shard_map/ppermute | solution.py:319
  17.2 1.6 %collective-permute-start.5 = (bf16[2,80,768]{2,1,0:T(8,128)(2,1)S(1)}, bf16[2,80,768]{2,1,0:T(8,128)(2,1)S(1)}, u32[]{:S(2)}, u32[]{:S(2)}) collective-permute-start(bf16[2,80,768]{2,1,0:T(8,128)(2,1)S(1)} %get-tuple-element.54), channel_id=1, source_target_pairs={{0,1},{1,0},{2,3},{3,2},{4,5},{5,4},{6,7},{7,6},{8,9},{9,8},{10,11... | collective-permute-start | bytes 737288 | tf_op jit(solution)/shard_map/ppermute | solution.py:319
  18.9 8.2 %collective-permute-start.8 = (bf16[2,80,768]{2,1,0:T(8,128)(2,1)S(1)}, bf16[2,80,768]{2,1,0:T(8,128)(2,1)S(1)}, u32[]{:S(2)}, u32[]{:S(2)}) collective-permute-start(bf16[2,80,768]{2,1,0:T(8,128)(2,1)S(1)} %get-tuple-element.55.refs_6_), channel_id=1, source_target_pairs={{0,2},{1,3},{2,0},{3,1},{4,6},{5,7},{6,4},{7,5},{8,10},{9,11},{10,... | collective-permute-start | bytes 737288 | tf_op jit(solution)/shard_map/ppermute | solution.py:319
  22.4 1.4 %collective-permute-start.6 = (bf16[80,768]{1,0:T(8,128)(2,1)S(1)}, bf16[80,768]{1,0:T(8,128)(2,1)S(1)}, u32[]{:S(2)}, u32[]{:S(2)}) collective-permute-start(bf16[80,768]{1,0:T(8,128)(2,1)S(1)} %shard_map.93), channel_id=1, source_target_pairs={{0,1},{1,0},{2,3},{3,2},{4,5},{5,4},{6,7},{7,6},{8,9},{9,8},{10,11... | collective-permute-start | bytes 368648 | tf_op jit(solution)/shard_map/ppermute | solution.py:319
  23.9 5.7 %collective-permute-start.7 = (bf16[80,768]{1,0:T(8,128)(2,1)S(1)}, bf16[80,768]{1,0:T(8,128)(2,1)S(1)}, u32[]{:S(2)}, u32[]{:S(2)}) collective-permute-start(bf16[80,768]{1,0:T(8,128)(2,1)S(1)} %get-tuple-element.67), channel_id=1, source_target_pairs={{0,2},{1,3},{2,0},{3,1},{4,6},{5,7},{6,4},{7,5},{8,10},{9,11},{10,... | collective-permute-start | bytes 368648 | tf_op jit(solution)/shard_map/ppermute | solution.py:319
  27.2 2.3 %collective-permute-start.9 = (bf16[80,768]{1,0:T(8,128)(2,1)S(1)}, bf16[80,768]{1,0:T(8,128)(2,1)S(1)}, u32[]{:S(2)}, u32[]{:S(2)}) collective-permute-start(bf16[80,768]{1,0:T(8,128)(2,1)S(1)} %get-tuple-element.59.mine_act), channel_id=1, source_target_pairs={{0,1},{1,0},{2,3},{3,2},{4,5},{5,4},{6,7},{7,6},{8,9},{9,8},{10,11... | collective-permute-start | bytes 368648 | tf_op jit(solution)/shard_map/ppermute | solution.py:319
  29.6 1.6 %collective-permute-start.10 = (bf16[2,80,768]{2,1,0:T(8,128)(2,1)S(1)}, bf16[2,80,768]{2,1,0:T(8,128)(2,1)S(1)}, u32[]{:S(2)}, u32[]{:S(2)}) collective-permute-start(bf16[2,80,768]{2,1,0:T(8,128)(2,1)S(1)} %shard_map.95.mine), channel_id=1, source_target_pairs={{0,1},{1,0},{2,3},{3,2},{4,5},{5,4},{6,7},{7,6},{8,9},{9,8},{10,11... | collective-permute-start | bytes 737288 | tf_op jit(solution)/shard_map/ppermute | solution.py:319
  32.1 10.0 %collective-permute-start.11 = (bf16[40,1024]{1,0:T(8,128)(2,1)S(1)}, bf16[40,1024]{1,0:T(8,128)(2,1)S(1)}, u32[]{:S(2)}, u32[]{:S(2)}) collective-permute-start(bf16[40,1024]{1,0:T(8,128)(2,1)S(1)} %get-tuple-element.60), channel_id=1, source_target_pairs={{0,4},{4,8},{8,12},{12,0},{1,5},{5,9},{9,13},{13,1},{2,6},{6,10},{... | collective-permute-start | bytes 245768 | tf_op jit(solution)/shard_map/ppermute | solution.py:312
  32.8 9.3 %collective-permute-start.12 = (bf16[40,1024]{1,0:T(8,128)(2,1)S(1)}, bf16[40,1024]{1,0:T(8,128)(2,1)S(1)}, u32[]{:S(2)}, u32[]{:S(2)}) collective-permute-start(bf16[40,1024]{1,0:T(8,128)(2,1)S(1)} %get-tuple-element.61), channel_id=1, source_target_pairs={{0,8},{4,12},{8,0},{12,4},{1,9},{5,13},{9,1},{13,5},{2,10},{6,14},... | collective-permute-start | bytes 245768 | tf_op jit(solution)/shard_map/ppermute | solution.py:312
  35.1 7.0 %collective-permute-start.13 = (bf16[40,1024]{1,0:T(8,128)(2,1)S(1)}, bf16[40,1024]{1,0:T(8,128)(2,1)S(1)}, u32[]{:S(2)}, u32[]{:S(2)}) collective-permute-start(bf16[40,1024]{1,0:T(8,128)(2,1)S(1)} %get-tuple-element.62), channel_id=1, source_target_pairs={{0,12},{4,0},{8,4},{12,8},{1,13},{5,1},{9,5},{13,9},{2,14},{6,2},{... | collective-permute-start | bytes 245768 | tf_op jit(solution)/shard_map/ppermute | solution.py:312

commit v24 on v23

--- a/solution.py
+++ b/solution.py
@@ -240,23 +240,25 @@
 def weight_grads(mine_act, other_act, mine, other, rows_in, rows_grad, pair_out, down_out, held, sems):
     core = lax.axis_index("ey") & 1
     half = mine_act.shape[1]
-    step = half // 2
     stores = []
     for matrix in range(3):
         right = rows_grad[...] if matrix == 0 else rows_in[...]
         for own in range(2):
             start = (core if own else 1 - core) * half
-            for part in range(2):
+            parts = 2 if (matrix, own) == (2, 1) else 1
+            step = half // parts
+            for part in range(parts):
                 columns = slice(part * step, (part + 1) * step)
                 if matrix == 0:
                     left = (mine_act if own else other_act)[:, columns]
                 else:
                     left = (mine if own else other)[matrix - 1, :, columns]
                 at = len(stores)
-                held[at] = mm(left, right, ROWS).astype(BF)
+                block = held.at[2 * matrix + own, pl.ds(part * step, step)]
+                block[...] = mm(left, right, ROWS).astype(BF)
                 rows = pl.ds(start + part * step, step)
                 target = down_out.at[0, rows] if matrix == 0 else pair_out.at[0, matrix - 1, rows]
-                store = pltpu.make_async_copy(held.at[at], target, sems.at[at])
+                store = pltpu.make_async_copy(block, target, sems.at[at])
                 store.start()
                 stores.append(store)
     for store in stores:
@@ -474,7 +476,7 @@
         [sds((1, 2, hidden, width), BF), sds((1, hidden, width), BF)],
         (mine_act, other_act, mine, other, rows_in, rows_grad),
         [VMEM] * 6,
-        [pltpu.VMEM((12, half // 2, width), BF), dma(12)],
+        [pltpu.VMEM((6, half, width), BF), dma(7)],
         limit=24,
         flops=3 * weight_flops,
         traffic=3 * weight_bytes,

time: 43.4 us -> 43.6 us (level)
  no operation moved by 1% of the time
where the time goes in v24:
time: 43.6 us; the launch traced here: 43.4 us
  starting transfers between devices  18.9 us (43%)
  Pallas kernels  16.5 us (38%)
  waiting for transfers between devices  7.11 us (16%)
  between operations  0.79 us (2%)
    pallas_call x15, Pallas kernels, call(): pl.pallas_call(body, out_shape=outs, in_specs=specs, out_specs=out_specs...  16.5 us
    ppermute x11, starting transfers between devices, swap(): return lax.ppermute(value, axis, [(i, i ^ bit) for i in range(count)])  13 us
    ppermute x11, waiting for transfers between devices, swap(): return lax.ppermute(value, axis, [(i, i ^ bit) for i in range(count)])  7.11 us
    ppermute x3, starting transfers between devices, shift(): lax.ppermute(value, axis, [(name, names[(at + step) % count]) for at, nam...  5.89 us
  transfers between devices with their start and end apart: 14, of which 6 were waited for; matrix products, arithmetic and copies ran while one was open for 0% of the time, Pallas kernels for 30%

profile of v24, /device:TPU:0, one launch (start us, length us, event | category | flops | bytes accessed | tf_op | source)
XLA Modules:
  0.0 43.4 jit_solution(13915006048604166661)
XLA Ops:
  0.6 1.4 %shard_map.85 = (bf16[160,256]{1,0:T(8,128)(2,1)S(1)}, f32[160,1]{1,0:T(8,128)S(1)}, bf16[256,1024]{1,0:T(8,128)(2,1)S(1)}, bf16[40,1024]{1,0:T(8,128)(2,1)S(1)}...) custom-call(s32[8,256]{1,0:T(8,128)} %bitcast.2, ...), custom_call_target="tpu_custom_call" | custom-call | flops 83886080 | bytes 1048576 | tf_op jit(solution)/shard_map/pallas_call | solution.py:70
  2.0 4.1 %collective-permute-start.3 = (bf16[40,1024]{1,0:T(8,128)(2,1)S(1)}, bf16[40,1024]{1,0:T(8,128)(2,1)S(1)}, u32[]{:S(2)}, u32[]{:S(2)}) collective-permute-start(bf16[40,1024]{1,0:T(8,128)(2,1)S(1)} %get-tuple-element.46), channel_id=1, source_target_pairs={{0,8},{4,12},{8,0},{12,4},{1,9},{5,13},{9,1},{13,5},{2,10},{6,14},... | collective-permute-start | bytes 245768 | tf_op jit(solution)/shard_map/ppermute | solution.py:321
  6.4 1.6 %collective-permute-start.2 = (bf16[80,1024]{1,0:T(8,128)(2,1)S(1)}, bf16[80,1024]{1,0:T(8,128)(2,1)S(1)}, u32[]{:S(2)}, u32[]{:S(2)}) collective-permute-start(bf16[80,1024]{1,0:T(8,128)(2,1)S(1)} %get-tuple-element.44), channel_id=1, source_target_pairs={{0,4},{4,0},{8,12},{12,8},{1,5},{5,1},{9,13},{13,9},{2,6},{6,2},{1... | collective-permute-start | bytes 491528 | tf_op jit(solution)/shard_map/ppermute | solution.py:321
  8.0 3.8 %shard_map.87 = (bf16[3,768,1024]{2,1,0:T(8,128)(2,1)S(1)}, bf16[3,768,1024]{2,1,0:T(8,128)(2,1)S(1)}, bf16[40,1024]{1,0:T(8,128)(2,1)S(1)}, bf16[40,1024]{1,0:T(8,128)(2,1)S(1)}, bf16[40,1024]{1,0:T(8,128)(2,1)S(1)}) custom-call(bf16[1,2,1536,1024]{3,2,1,0:T(8,128)(2,1)} %gate_up.1, bf16[1,1536,1024]{2,1,0:T(8,128)(2,1)} %down.1, ...), custom_call_target="tpu_custom_call" | custom-call | flops 251658240 | bytes 3145728 | tf_op jit(solution)/shard_map/pallas_call | solution.py:70
  11.8 3.9 %collective-permute-start = (bf16[40,1024]{1,0:T(8,128)(2,1)S(1)}, bf16[40,1024]{1,0:T(8,128)(2,1)S(1)}, u32[]{:S(2)}, u32[]{:S(2)}) collective-permute-start(bf16[40,1024]{1,0:T(8,128)(2,1)S(1)} %get-tuple-element.42), channel_id=1, source_target_pairs={{0,12},{4,8},{8,4},{12,0},{1,13},{5,9},{9,5},{13,1},{2,14},{6,10},... | collective-permute-start | bytes 245768 | tf_op jit(solution)/shard_map/ppermute | solution.py:321
  15.8 1.4 %shard_map.89 = (bf16[2,80,768]{2,1,0:T(8,128)(2,1)S(1)}, bf16[160,80]{1,0:T(8,128)(2,1)S(1)}, bf16[80,1024]{1,0:T(8,128)(2,1)S(1)}) custom-call(bf16[40,1024]{1,0:T(8,128)(2,1)S(1)} %shard_map.88.refs_0_, bf16[40,1024]{1,0:T(8,128)(2,1)S(1)} %collective-permute-done.4.refs_1_, bf16[80,1024]{1,0:T(8,128)(2,1)S(1)} %collective-permute-done.2.refs_2_, ...), custom_call_target="tpu_custom_call" | custom-call | flops 503316480 | bytes 3145728 | tf_op jit(solution)/shard_map/pallas_call | solution.py:70
  17.3 1.1 %shard_map.91.mine = bf16[2,80,768]{2,1,0:T(8,128)(2,1)S(1)} custom-call(bf16[80,1024]{1,0:T(8,128)(2,1)S(1)} %get-tuple-element.53.rows_in, bf16[3,768,1024]{2,1,0:T(8,128)(2,1)S(1)} %get-tuple-element.51.refs_5_.held), custom_call_target="tpu_custom_call" | custom-call | flops 25165824000 | bytes 314572800 | tf_op jit(solution)/shard_map/pallas_call | solution.py:70
  18.4 0.4 collective-permute-done.5.other
  18.9 1.6 %collective-permute-start.8 = (bf16[2,80,768]{2,1,0:T(8,128)(2,1)S(1)}, bf16[2,80,768]{2,1,0:T(8,128)(2,1)S(1)}, u32[]{:S(2)}, u32[]{:S(2)}) collective-permute-start(bf16[2,80,768]{2,1,0:T(8,128)(2,1)S(1)} %get-tuple-element.55.refs_6_), channel_id=1, source_target_pairs={{0,2},{1,3},{2,0},{3,1},{4,6},{5,7},{6,4},{7,5},{8,10},{9,11},{10,... | collective-permute-start | bytes 737288 | tf_op jit(solution)/shard_map/ppermute | solution.py:321
  20.4 1.3 %collective-permute-done.1.refs_1_ = bf16[40,1024]{1,0:T(8,128)(2,1)S(1)} collective-permute-done((bf16[40,1024]{1,0:T(8,128)(2,1)S(1)}, bf16[40,1024]{1,0:T(8,128)(2,1)S(1)}, u32[]{:S(2)}, u32[]{:S(2)}) %collective-permute-start.1) | collective-permute-done | bytes 81952 | tf_op jit(solution)/shard_map/ppermute | solution.py:321
  21.7 0.7 %shard_map.93 = bf16[80,768]{1,0:T(8,128)(2,1)S(1)} custom-call(bf16[40,1024]{1,0:T(8,128)(2,1)S(1)} %collective-permute-done.refs_0_, bf16[40,1024]{1,0:T(8,128)(2,1)S(1)} %collective-permute-done.1.refs_1_, bf16[80,1024]{1,0:T(8,128)(2,1)S(1)} %collective-permute-done.2.refs_2_, bf16[40,1024]{1,0:T(8,128)(2,1)S(1)} %get-tuple-element.45.refs_3_, ...), custom_call_target="tpu_custom_call" | custom-call | flops 251658240 | bytes 3145728 | tf_op jit(solution)/shard_map/pallas_call | solution.py:70
  22.5 0.7 %shard_map.90 = (bf16[80,1024]{1,0:T(8,128)(2,1)S(1)}, bf16[80,768]{1,0:T(8,128)(2,1)S(1)}) custom-call(bf16[40,1024]{1,0:T(8,128)(2,1)S(1)} %collective-permute-done.refs_0_, bf16[40,1024]{1,0:T(8,128)(2,1)S(1)} %collective-permute-done.1.refs_1_, bf16[80,1024]{1,0:T(8,128)(2,1)S(1)} %collective-permute-done.2.refs_2_, ...), custom_call_target="tpu_custom_call" | custom-call | flops 25165824000 | bytes 314572800 | tf_op jit(solution)/shard_map/pallas_call | solution.py:70
  23.2 0.6 %collective-permute-done.6 = bf16[80,768]{1,0:T(8,128)(2,1)S(1)} collective-permute-done((bf16[80,768]{1,0:T(8,128)(2,1)S(1)}, bf16[80,768]{1,0:T(8,128)(2,1)S(1)}, u32[]{:S(2)}, u32[]{:S(2)}) %collective-permute-start.6) | collective-permute-done | bytes 122912 | tf_op jit(solution)/shard_map/ppermute | solution.py:321
  23.9 1.6 %collective-permute-start.7 = (bf16[80,768]{1,0:T(8,128)(2,1)S(1)}, bf16[80,768]{1,0:T(8,128)(2,1)S(1)}, u32[]{:S(2)}, u32[]{:S(2)}) collective-permute-start(bf16[80,768]{1,0:T(8,128)(2,1)S(1)} %get-tuple-element.67), channel_id=1, source_target_pairs={{0,2},{1,3},{2,0},{3,1},{4,6},{5,7},{6,4},{7,5},{8,10},{9,11},{10,... | collective-permute-start | bytes 368648 | tf_op jit(solution)/shard_map/ppermute | solution.py:321
  25.4 1.7 %collective-permute-done.8.pair_far = bf16[2,80,768]{2,1,0:T(8,128)(2,1)S(1)} collective-permute-done((bf16[2,80,768]{2,1,0:T(8,128)(2,1)S(1)}, bf16[2,80,768]{2,1,0:T(8,128)(2,1)S(1)}, u32[]{:S(2)}, u32[]{:S(2)}) %collective-permute-start.8) | collective-permute-done | bytes 245792 | tf_op jit(solution)/shard_map/ppermute | solution.py:321
  27.3 2.2 %collective-permute-done.7.act_far = bf16[80,768]{1,0:T(8,128)(2,1)S(1)} collective-permute-done((bf16[80,768]{1,0:T(8,128)(2,1)S(1)}, bf16[80,768]{1,0:T(8,128)(2,1)S(1)}, u32[]{:S(2)}, u32[]{:S(2)}) %collective-permute-start.7) | collective-permute-done | bytes 122912 | tf_op jit(solution)/shard_map/ppermute | solution.py:321
  29.7 0.7 %shard_map.96.total = f32[80,1024]{1,0:T(8,128)S(1)} custom-call(bf16[2,80,768]{2,1,0:T(8,128)(2,1)S(1)} %shard_map.95.mine, bf16[3,768,1024]{2,1,0:T(8,128)(2,1)S(1)} %get-tuple-element.51.refs_5_.held), custom_call_target="tpu_custom_call" | custom-call | flops 251658240 | bytes 3145728 | tf_op jit(solution)/shard_map/pallas_call | solution.py:70
  30.4 0.8 %collective-permute-done.10.other = bf16[2,80,768]{2,1,0:T(8,128)(2,1)S(1)} collective-permute-done((bf16[2,80,768]{2,1,0:T(8,128)(2,1)S(1)}, bf16[2,80,768]{2,1,0:T(8,128)(2,1)S(1)}, u32[]{:S(2)}, u32[]{:S(2)}) %collective-permute-start.10) | collective-permute-done | bytes 245792 | tf_op jit(solution)/shard_map/ppermute | solution.py:321
  31.2 0.9 %shard_map.97 = (bf16[40,1024]{1,0:T(8,128)(2,1)S(1)}, bf16[40,1024]{1,0:T(8,128)(2,1)S(1)}, bf16[40,1024]{1,0:T(8,128)(2,1)S(1)}, bf16[40,1024]{1,0:T(8,128)(2,1)S(1)}) custom-call(f32[80,1024]{1,0:T(8,128)S(1)} %shard_map.96.total, bf16[2,80,768]{2,1,0:T(8,128)(2,1)S(1)} %collective-permute-done.10.other, ...), custom_call_target="tpu_custom_call" | custom-call | flops 251658240 | bytes 3145728 | tf_op jit(solution)/shard_map/pallas_call | solution.py:70
  32.1 0.7 %collective-permute-start.11 = (bf16[40,1024]{1,0:T(8,128)(2,1)S(1)}, bf16[40,1024]{1,0:T(8,128)(2,1)S(1)}, u32[]{:S(2)}, u32[]{:S(2)}) collective-permute-start(bf16[40,1024]{1,0:T(8,128)(2,1)S(1)} %get-tuple-element.60), channel_id=1, source_target_pairs={{0,4},{4,8},{8,12},{12,0},{1,5},{5,9},{9,13},{13,1},{2,6},{6,10},{... | collective-permute-start | bytes 245768 | tf_op jit(solution)/shard_map/ppermute | solution.py:314
  32.8 2.4 %collective-permute-start.12 = (bf16[40,1024]{1,0:T(8,128)(2,1)S(1)}, bf16[40,1024]{1,0:T(8,128)(2,1)S(1)}, u32[]{:S(2)}, u32[]{:S(2)}) collective-permute-start(bf16[40,1024]{1,0:T(8,128)(2,1)S(1)} %get-tuple-element.61), channel_id=1, source_target_pairs={{0,8},{4,12},{8,0},{12,4},{1,9},{5,13},{9,1},{13,5},{2,10},{6,14},... | collective-permute-start | bytes 245768 | tf_op jit(solution)/shard_map/ppermute | solution.py:314
  35.1 2.8 %collective-permute-start.13 = (bf16[40,1024]{1,0:T(8,128)(2,1)S(1)}, bf16[40,1024]{1,0:T(8,128)(2,1)S(1)}, u32[]{:S(2)}, u32[]{:S(2)}) collective-permute-start(bf16[40,1024]{1,0:T(8,128)(2,1)S(1)} %get-tuple-element.62), channel_id=1, source_target_pairs={{0,12},{4,0},{8,4},{12,8},{1,13},{5,1},{9,5},{13,9},{2,14},{6,2},{... | collective-permute-start | bytes 245768 | tf_op jit(solution)/shard_map/ppermute | solution.py:314
  38.0 4.3 %shard_map.99 = (bf16[1,2,1536,1024]{3,2,1,0:T(8,128)(2,1)}, bf16[1,1536,1024]{2,1,0:T(8,128)(2,1)}) custom-call(bf16[80,768]{1,0:T(8,128)(2,1)S(1)} %get-tuple-element.59.mine_act, bf16[80,768]{1,0:T(8,128)(2,1)S(1)} %collective-permute-done.9._.other_act, bf16[2,80,768]{2,1,0:T(8,128)(2,1)S(1)} %shard_map.95.mine, ...), custom_call_target="tpu_custom_call" | custom-call | flops 754974720 | bytes 9437184 | tf_op jit(solution)/shard_map/pallas_call | solution.py:70
  42.3 1.1 %shard_map.98 = bf16[256,1024]{1,0:T(8,128)(2,1)} custom-call(bf16[160,256]{1,0:T(8,128)(2,1)S(1)} %get-tuple-element.35.pick, bf16[40,1024]{1,0:T(8,128)(2,1)S(1)} %collective-permute-done.11.refs_0_, bf16[40,1024]{1,0:T(8,128)(2,1)S(1)} %collective-permute-done.12.refs_1_, bf16[40,1024]{1,0:T(8,128)(2,1)S(1)} %collective-permute-done.13.refs_2_, ...), custom_call_target="tpu_custom_call" | custom-call | flops 83886080 | bytes 1048576 | tf_op jit(solution)/shard_map/pallas_call | solution.py:70
  (20 shorter events, 0.9 us)
Async XLA Ops:
  2.0 13.7 %collective-permute-start.3 = (bf16[40,1024]{1,0:T(8,128)(2,1)S(1)}, bf16[40,1024]{1,0:T(8,128)(2,1)S(1)}, u32[]{:S(2)}, u32[]{:S(2)}) collective-permute-start(bf16[40,1024]{1,0:T(8,128)(2,1)S(1)} %get-tuple-element.46), channel_id=1, source_target_pairs={{0,8},{4,12},{8,0},{12,4},{1,9},{5,13},{9,1},{13,5},{2,10},{6,14},... | collective-permute-start | bytes 245768 | tf_op jit(solution)/shard_map/ppermute | solution.py:321
  6.4 9.4 %collective-permute-start.2 = (bf16[80,1024]{1,0:T(8,128)(2,1)S(1)}, bf16[80,1024]{1,0:T(8,128)(2,1)S(1)}, u32[]{:S(2)}, u32[]{:S(2)}) collective-permute-start(bf16[80,1024]{1,0:T(8,128)(2,1)S(1)} %get-tuple-element.44), channel_id=1, source_target_pairs={{0,4},{4,0},{8,12},{12,8},{1,5},{5,1},{9,13},{13,9},{2,6},{6,2},{1... | collective-permute-start | bytes 491528 | tf_op jit(solution)/shard_map/ppermute | solution.py:321
  8.0 7.7 %collective-permute-start.4 = (bf16[40,1024]{1,0:T(8,128)(2,1)S(1)}, bf16[40,1024]{1,0:T(8,128)(2,1)S(1)}, u32[]{:S(2)}, u32[]{:S(2)}) collective-permute-start(bf16[40,1024]{1,0:T(8,128)(2,1)S(1)} %get-tuple-element.47), channel_id=1, source_target_pairs={{0,12},{4,8},{8,4},{12,0},{1,13},{5,9},{9,5},{13,1},{2,14},{6,10},... | collective-permute-start | bytes 245768 | tf_op jit(solution)/shard_map/ppermute | solution.py:321
  11.8 8.6 %collective-permute-start = (bf16[40,1024]{1,0:T(8,128)(2,1)S(1)}, bf16[40,1024]{1,0:T(8,128)(2,1)S(1)}, u32[]{:S(2)}, u32[]{:S(2)}) collective-permute-start(bf16[40,1024]{1,0:T(8,128)(2,1)S(1)} %get-tuple-element.42), channel_id=1, source_target_pairs={{0,12},{4,8},{8,4},{12,0},{1,13},{5,9},{9,5},{13,1},{2,14},{6,10},... | collective-permute-start | bytes 245768 | tf_op jit(solution)/shard_map/ppermute | solution.py:321
  15.7 6.0 %collective-permute-start.1 = (bf16[40,1024]{1,0:T(8,128)(2,1)S(1)}, bf16[40,1024]{1,0:T(8,128)(2,1)S(1)}, u32[]{:S(2)}, u32[]{:S(2)}) collective-permute-start(bf16[40,1024]{1,0:T(8,128)(2,1)S(1)} %get-tuple-element.43), channel_id=1, source_target_pairs={{0,8},{4,12},{8,0},{12,4},{1,9},{5,13},{9,1},{13,5},{2,10},{6,14},... | collective-permute-start | bytes 245768 | tf_op jit(solution)/shard_map/ppermute | solution.py:321
  17.2 1.6 %collective-permute-start.5 = (bf16[2,80,768]{2,1,0:T(8,128)(2,1)S(1)}, bf16[2,80,768]{2,1,0:T(8,128)(2,1)S(1)}, u32[]{:S(2)}, u32[]{:S(2)}) collective-permute-start(bf16[2,80,768]{2,1,0:T(8,128)(2,1)S(1)} %get-tuple-element.54), channel_id=1, source_target_pairs={{0,1},{1,0},{2,3},{3,2},{4,5},{5,4},{6,7},{7,6},{8,9},{9,8},{10,11... | collective-permute-start | bytes 737288 | tf_op jit(solution)/shard_map/ppermute | solution.py:321
  18.9 8.2 %collective-permute-start.8 = (bf16[2,80,768]{2,1,0:T(8,128)(2,1)S(1)}, bf16[2,80,768]{2,1,0:T(8,128)(2,1)S(1)}, u32[]{:S(2)}, u32[]{:S(2)}) collective-permute-start(bf16[2,80,768]{2,1,0:T(8,128)(2,1)S(1)} %get-tuple-element.55.refs_6_), channel_id=1, source_target_pairs={{0,2},{1,3},{2,0},{3,1},{4,6},{5,7},{6,4},{7,5},{8,10},{9,11},{10,... | collective-permute-start | bytes 737288 | tf_op jit(solution)/shard_map/ppermute | solution.py:321
  22.4 1.4 %collective-permute-start.6 = (bf16[80,768]{1,0:T(8,128)(2,1)S(1)}, bf16[80,768]{1,0:T(8,128)(2,1)S(1)}, u32[]{:S(2)}, u32[]{:S(2)}) collective-permute-start(bf16[80,768]{1,0:T(8,128)(2,1)S(1)} %shard_map.93), channel_id=1, source_target_pairs={{0,1},{1,0},{2,3},{3,2},{4,5},{5,4},{6,7},{7,6},{8,9},{9,8},{10,11... | collective-permute-start | bytes 368648 | tf_op jit(solution)/shard_map/ppermute | solution.py:321
  23.9 5.7 %collective-permute-start.7 = (bf16[80,768]{1,0:T(8,128)(2,1)S(1)}, bf16[80,768]{1,0:T(8,128)(2,1)S(1)}, u32[]{:S(2)}, u32[]{:S(2)}) collective-permute-start(bf16[80,768]{1,0:T(8,128)(2,1)S(1)} %get-tuple-element.67), channel_id=1, source_target_pairs={{0,2},{1,3},{2,0},{3,1},{4,6},{5,7},{6,4},{7,5},{8,10},{9,11},{10,... | collective-permute-start | bytes 368648 | tf_op jit(solution)/shard_map/ppermute | solution.py:321
  27.2 2.3 %collective-permute-start.9 = (bf16[80,768]{1,0:T(8,128)(2,1)S(1)}, bf16[80,768]{1,0:T(8,128)(2,1)S(1)}, u32[]{:S(2)}, u32[]{:S(2)}) collective-permute-start(bf16[80,768]{1,0:T(8,128)(2,1)S(1)} %get-tuple-element.59.mine_act), channel_id=1, source_target_pairs={{0,1},{1,0},{2,3},{3,2},{4,5},{5,4},{6,7},{7,6},{8,9},{9,8},{10,11... | collective-permute-start | bytes 368648 | tf_op jit(solution)/shard_map/ppermute | solution.py:321
  29.6 1.6 %collective-permute-start.10 = (bf16[2,80,768]{2,1,0:T(8,128)(2,1)S(1)}, bf16[2,80,768]{2,1,0:T(8,128)(2,1)S(1)}, u32[]{:S(2)}, u32[]{:S(2)}) collective-permute-start(bf16[2,80,768]{2,1,0:T(8,128)(2,1)S(1)} %shard_map.95.mine), channel_id=1, source_target_pairs={{0,1},{1,0},{2,3},{3,2},{4,5},{5,4},{6,7},{7,6},{8,9},{9,8},{10,11... | collective-permute-start | bytes 737288 | tf_op jit(solution)/shard_map/ppermute | solution.py:321
  32.1 10.2 %collective-permute-start.11 = (bf16[40,1024]{1,0:T(8,128)(2,1)S(1)}, bf16[40,1024]{1,0:T(8,128)(2,1)S(1)}, u32[]{:S(2)}, u32[]{:S(2)}) collective-permute-start(bf16[40,1024]{1,0:T(8,128)(2,1)S(1)} %get-tuple-element.60), channel_id=1, source_target_pairs={{0,4},{4,8},{8,12},{12,0},{1,5},{5,9},{9,13},{13,1},{2,6},{6,10},{... | collective-permute-start | bytes 245768 | tf_op jit(solution)/shard_map/ppermute | solution.py:314
  32.8 9.5 %collective-permute-start.12 = (bf16[40,1024]{1,0:T(8,128)(2,1)S(1)}, bf16[40,1024]{1,0:T(8,128)(2,1)S(1)}, u32[]{:S(2)}, u32[]{:S(2)}) collective-permute-start(bf16[40,1024]{1,0:T(8,128)(2,1)S(1)} %get-tuple-element.61), channel_id=1, source_target_pairs={{0,8},{4,12},{8,0},{12,4},{1,9},{5,13},{9,1},{13,5},{2,10},{6,14},... | collective-permute-start | bytes 245768 | tf_op jit(solution)/shard_map/ppermute | solution.py:314
  35.1 7.1 %collective-permute-start.13 = (bf16[40,1024]{1,0:T(8,128)(2,1)S(1)}, bf16[40,1024]{1,0:T(8,128)(2,1)S(1)}, u32[]{:S(2)}, u32[]{:S(2)}) collective-permute-start(bf16[40,1024]{1,0:T(8,128)(2,1)S(1)} %get-tuple-element.62), channel_id=1, source_target_pairs={{0,12},{4,0},{8,4},{12,8},{1,13},{5,1},{9,5},{13,9},{2,14},{6,2},{... | collective-permute-start | bytes 245768 | tf_op jit(solution)/shard_map/ppermute | solution.py:314

commit v25 on v23

--- a/solution.py
+++ b/solution.py
@@ -240,13 +240,13 @@
 def weight_grads(mine_act, other_act, mine, other, rows_in, rows_grad, pair_out, down_out, held, sems):
     core = lax.axis_index("ey") & 1
     half = mine_act.shape[1]
-    step = half // 2
+    step = half // 4
     stores = []
     for matrix in range(3):
         right = rows_grad[...] if matrix == 0 else rows_in[...]
         for own in range(2):
             start = (core if own else 1 - core) * half
-            for part in range(2):
+            for part in range(4):
                 columns = slice(part * step, (part + 1) * step)
                 if matrix == 0:
                     left = (mine_act if own else other_act)[:, columns]
@@ -474,7 +474,7 @@
         [sds((1, 2, hidden, width), BF), sds((1, hidden, width), BF)],
         (mine_act, other_act, mine, other, rows_in, rows_grad),
         [VMEM] * 6,
-        [pltpu.VMEM((12, half // 2, width), BF), dma(12)],
+        [pltpu.VMEM((24, half // 4, width), BF), dma(24)],
         limit=24,
         flops=3 * weight_flops,
         traffic=3 * weight_bytes,

time: 43.4 us -> 43.4 us (level)
  no operation moved by 1% of the time
where the time goes in v25:
time: 43.4 us; the launch traced here: 43.2 us
  starting transfers between devices  18.9 us (44%)
  Pallas kernels  16.3 us (38%)
  waiting for transfers between devices  7.11 us (16%)
  between operations  0.79 us (2%)
    pallas_call x15, Pallas kernels, call(): pl.pallas_call(body, out_shape=outs, in_specs=specs, out_specs=out_specs...  16.3 us
    ppermute x11, starting transfers between devices, swap(): return lax.ppermute(value, axis, [(i, i ^ bit) for i in range(count)])  13 us
    ppermute x11, waiting for transfers between devices, swap(): return lax.ppermute(value, axis, [(i, i ^ bit) for i in range(count)])  7.11 us
    ppermute x3, starting transfers between devices, shift(): lax.ppermute(value, axis, [(name, names[(at + step) % count]) for at, nam...  5.89 us
  transfers between devices with their start and end apart: 14, of which 6 were waited for; matrix products, arithmetic and copies ran while one was open for 0% of the time, Pallas kernels for 30%

profile of v25, /device:TPU:0, one launch (start us, length us, event | category | flops | bytes accessed | tf_op | source)
XLA Modules:
  0.0 43.2 jit_solution(641942479082288844)
XLA Ops:
  0.6 1.4 %shard_map.85 = (bf16[160,256]{1,0:T(8,128)(2,1)S(1)}, f32[160,1]{1,0:T(8,128)S(1)}, bf16[256,1024]{1,0:T(8,128)(2,1)S(1)}, bf16[40,1024]{1,0:T(8,128)(2,1)S(1)}...) custom-call(s32[8,256]{1,0:T(8,128)} %bitcast.2, ...), custom_call_target="tpu_custom_call" | custom-call | flops 83886080 | bytes 1048576 | tf_op jit(solution)/shard_map/pallas_call | solution.py:70
  2.0 4.1 %collective-permute-start.3 = (bf16[40,1024]{1,0:T(8,128)(2,1)S(1)}, bf16[40,1024]{1,0:T(8,128)(2,1)S(1)}, u32[]{:S(2)}, u32[]{:S(2)}) collective-permute-start(bf16[40,1024]{1,0:T(8,128)(2,1)S(1)} %get-tuple-element.46), channel_id=1, source_target_pairs={{0,8},{4,12},{8,0},{12,4},{1,9},{5,13},{9,1},{13,5},{2,10},{6,14},... | collective-permute-start | bytes 245768 | tf_op jit(solution)/shard_map/ppermute | solution.py:319
  6.4 1.6 %collective-permute-start.2 = (bf16[80,1024]{1,0:T(8,128)(2,1)S(1)}, bf16[80,1024]{1,0:T(8,128)(2,1)S(1)}, u32[]{:S(2)}, u32[]{:S(2)}) collective-permute-start(bf16[80,1024]{1,0:T(8,128)(2,1)S(1)} %get-tuple-element.44), channel_id=1, source_target_pairs={{0,4},{4,0},{8,12},{12,8},{1,5},{5,1},{9,13},{13,9},{2,6},{6,2},{1... | collective-permute-start | bytes 491528 | tf_op jit(solution)/shard_map/ppermute | solution.py:319
  8.0 3.8 %shard_map.87 = (bf16[3,768,1024]{2,1,0:T(8,128)(2,1)S(1)}, bf16[3,768,1024]{2,1,0:T(8,128)(2,1)S(1)}, bf16[40,1024]{1,0:T(8,128)(2,1)S(1)}, bf16[40,1024]{1,0:T(8,128)(2,1)S(1)}, bf16[40,1024]{1,0:T(8,128)(2,1)S(1)}) custom-call(bf16[1,2,1536,1024]{3,2,1,0:T(8,128)(2,1)} %gate_up.1, bf16[1,1536,1024]{2,1,0:T(8,128)(2,1)} %down.1, ...), custom_call_target="tpu_custom_call" | custom-call | flops 251658240 | bytes 3145728 | tf_op jit(solution)/shard_map/pallas_call | solution.py:70
  11.8 3.9 %collective-permute-start = (bf16[40,1024]{1,0:T(8,128)(2,1)S(1)}, bf16[40,1024]{1,0:T(8,128)(2,1)S(1)}, u32[]{:S(2)}, u32[]{:S(2)}) collective-permute-start(bf16[40,1024]{1,0:T(8,128)(2,1)S(1)} %get-tuple-element.42), channel_id=1, source_target_pairs={{0,12},{4,8},{8,4},{12,0},{1,13},{5,9},{9,5},{13,1},{2,14},{6,10},... | collective-permute-start | bytes 245768 | tf_op jit(solution)/shard_map/ppermute | solution.py:319
  15.8 1.4 %shard_map.89 = (bf16[2,80,768]{2,1,0:T(8,128)(2,1)S(1)}, bf16[160,80]{1,0:T(8,128)(2,1)S(1)}, bf16[80,1024]{1,0:T(8,128)(2,1)S(1)}) custom-call(bf16[40,1024]{1,0:T(8,128)(2,1)S(1)} %shard_map.88.refs_0_, bf16[40,1024]{1,0:T(8,128)(2,1)S(1)} %collective-permute-done.4.refs_1_, bf16[80,1024]{1,0:T(8,128)(2,1)S(1)} %collective-permute-done.2.refs_2_, ...), custom_call_target="tpu_custom_call" | custom-call | flops 503316480 | bytes 3145728 | tf_op jit(solution)/shard_map/pallas_call | solution.py:70
  17.3 1.1 %shard_map.91.mine = bf16[2,80,768]{2,1,0:T(8,128)(2,1)S(1)} custom-call(bf16[80,1024]{1,0:T(8,128)(2,1)S(1)} %get-tuple-element.53.rows_in, bf16[3,768,1024]{2,1,0:T(8,128)(2,1)S(1)} %get-tuple-element.51.refs_5_.held), custom_call_target="tpu_custom_call" | custom-call | flops 25165824000 | bytes 314572800 | tf_op jit(solution)/shard_map/pallas_call | solution.py:70
  18.4 0.4 collective-permute-done.5.other
  18.9 1.6 %collective-permute-start.8 = (bf16[2,80,768]{2,1,0:T(8,128)(2,1)S(1)}, bf16[2,80,768]{2,1,0:T(8,128)(2,1)S(1)}, u32[]{:S(2)}, u32[]{:S(2)}) collective-permute-start(bf16[2,80,768]{2,1,0:T(8,128)(2,1)S(1)} %get-tuple-element.55.refs_6_), channel_id=1, source_target_pairs={{0,2},{1,3},{2,0},{3,1},{4,6},{5,7},{6,4},{7,5},{8,10},{9,11},{10,... | collective-permute-start | bytes 737288 | tf_op jit(solution)/shard_map/ppermute | solution.py:319
  20.4 1.3 %collective-permute-done.1.refs_1_ = bf16[40,1024]{1,0:T(8,128)(2,1)S(1)} collective-permute-done((bf16[40,1024]{1,0:T(8,128)(2,1)S(1)}, bf16[40,1024]{1,0:T(8,128)(2,1)S(1)}, u32[]{:S(2)}, u32[]{:S(2)}) %collective-permute-start.1) | collective-permute-done | bytes 81952 | tf_op jit(solution)/shard_map/ppermute | solution.py:319
  21.7 0.7 %shard_map.93 = bf16[80,768]{1,0:T(8,128)(2,1)S(1)} custom-call(bf16[40,1024]{1,0:T(8,128)(2,1)S(1)} %collective-permute-done.refs_0_, bf16[40,1024]{1,0:T(8,128)(2,1)S(1)} %collective-permute-done.1.refs_1_, bf16[80,1024]{1,0:T(8,128)(2,1)S(1)} %collective-permute-done.2.refs_2_, bf16[40,1024]{1,0:T(8,128)(2,1)S(1)} %get-tuple-element.45.refs_3_, ...), custom_call_target="tpu_custom_call" | custom-call | flops 251658240 | bytes 3145728 | tf_op jit(solution)/shard_map/pallas_call | solution.py:70
  22.5 0.7 %shard_map.90 = (bf16[80,1024]{1,0:T(8,128)(2,1)S(1)}, bf16[80,768]{1,0:T(8,128)(2,1)S(1)}) custom-call(bf16[40,1024]{1,0:T(8,128)(2,1)S(1)} %collective-permute-done.refs_0_, bf16[40,1024]{1,0:T(8,128)(2,1)S(1)} %collective-permute-done.1.refs_1_, bf16[80,1024]{1,0:T(8,128)(2,1)S(1)} %collective-permute-done.2.refs_2_, ...), custom_call_target="tpu_custom_call" | custom-call | flops 25165824000 | bytes 314572800 | tf_op jit(solution)/shard_map/pallas_call | solution.py:70
  23.2 0.6 %collective-permute-done.6 = bf16[80,768]{1,0:T(8,128)(2,1)S(1)} collective-permute-done((bf16[80,768]{1,0:T(8,128)(2,1)S(1)}, bf16[80,768]{1,0:T(8,128)(2,1)S(1)}, u32[]{:S(2)}, u32[]{:S(2)}) %collective-permute-start.6) | collective-permute-done | bytes 122912 | tf_op jit(solution)/shard_map/ppermute | solution.py:319
  23.9 1.6 %collective-permute-start.7 = (bf16[80,768]{1,0:T(8,128)(2,1)S(1)}, bf16[80,768]{1,0:T(8,128)(2,1)S(1)}, u32[]{:S(2)}, u32[]{:S(2)}) collective-permute-start(bf16[80,768]{1,0:T(8,128)(2,1)S(1)} %get-tuple-element.67), channel_id=1, source_target_pairs={{0,2},{1,3},{2,0},{3,1},{4,6},{5,7},{6,4},{7,5},{8,10},{9,11},{10,... | collective-permute-start | bytes 368648 | tf_op jit(solution)/shard_map/ppermute | solution.py:319
  25.4 1.7 %collective-permute-done.8.pair_far = bf16[2,80,768]{2,1,0:T(8,128)(2,1)S(1)} collective-permute-done((bf16[2,80,768]{2,1,0:T(8,128)(2,1)S(1)}, bf16[2,80,768]{2,1,0:T(8,128)(2,1)S(1)}, u32[]{:S(2)}, u32[]{:S(2)}) %collective-permute-start.8) | collective-permute-done | bytes 245792 | tf_op jit(solution)/shard_map/ppermute | solution.py:319
  27.3 2.2 %collective-permute-done.7.act_far = bf16[80,768]{1,0:T(8,128)(2,1)S(1)} collective-permute-done((bf16[80,768]{1,0:T(8,128)(2,1)S(1)}, bf16[80,768]{1,0:T(8,128)(2,1)S(1)}, u32[]{:S(2)}, u32[]{:S(2)}) %collective-permute-start.7) | collective-permute-done | bytes 122912 | tf_op jit(solution)/shard_map/ppermute | solution.py:319
  29.7 0.7 %shard_map.96.total = f32[80,1024]{1,0:T(8,128)S(1)} custom-call(bf16[2,80,768]{2,1,0:T(8,128)(2,1)S(1)} %shard_map.95.mine, bf16[3,768,1024]{2,1,0:T(8,128)(2,1)S(1)} %get-tuple-element.51.refs_5_.held), custom_call_target="tpu_custom_call" | custom-call | flops 251658240 | bytes 3145728 | tf_op jit(solution)/shard_map/pallas_call | solution.py:70
  30.4 0.8 %collective-permute-done.10.other = bf16[2,80,768]{2,1,0:T(8,128)(2,1)S(1)} collective-permute-done((bf16[2,80,768]{2,1,0:T(8,128)(2,1)S(1)}, bf16[2,80,768]{2,1,0:T(8,128)(2,1)S(1)}, u32[]{:S(2)}, u32[]{:S(2)}) %collective-permute-start.10) | collective-permute-done | bytes 245792 | tf_op jit(solution)/shard_map/ppermute | solution.py:319
  31.2 0.9 %shard_map.97 = (bf16[40,1024]{1,0:T(8,128)(2,1)S(1)}, bf16[40,1024]{1,0:T(8,128)(2,1)S(1)}, bf16[40,1024]{1,0:T(8,128)(2,1)S(1)}, bf16[40,1024]{1,0:T(8,128)(2,1)S(1)}) custom-call(f32[80,1024]{1,0:T(8,128)S(1)} %shard_map.96.total, bf16[2,80,768]{2,1,0:T(8,128)(2,1)S(1)} %collective-permute-done.10.other, ...), custom_call_target="tpu_custom_call" | custom-call | flops 251658240 | bytes 3145728 | tf_op jit(solution)/shard_map/pallas_call | solution.py:70
  32.1 0.7 %collective-permute-start.11 = (bf16[40,1024]{1,0:T(8,128)(2,1)S(1)}, bf16[40,1024]{1,0:T(8,128)(2,1)S(1)}, u32[]{:S(2)}, u32[]{:S(2)}) collective-permute-start(bf16[40,1024]{1,0:T(8,128)(2,1)S(1)} %get-tuple-element.60), channel_id=1, source_target_pairs={{0,4},{4,8},{8,12},{12,0},{1,5},{5,9},{9,13},{13,1},{2,6},{6,10},{... | collective-permute-start | bytes 245768 | tf_op jit(solution)/shard_map/ppermute | solution.py:312
  32.8 2.4 %collective-permute-start.12 = (bf16[40,1024]{1,0:T(8,128)(2,1)S(1)}, bf16[40,1024]{1,0:T(8,128)(2,1)S(1)}, u32[]{:S(2)}, u32[]{:S(2)}) collective-permute-start(bf16[40,1024]{1,0:T(8,128)(2,1)S(1)} %get-tuple-element.61), channel_id=1, source_target_pairs={{0,8},{4,12},{8,0},{12,4},{1,9},{5,13},{9,1},{13,5},{2,10},{6,14},... | collective-permute-start | bytes 245768 | tf_op jit(solution)/shard_map/ppermute | solution.py:312
  35.1 2.8 %collective-permute-start.13 = (bf16[40,1024]{1,0:T(8,128)(2,1)S(1)}, bf16[40,1024]{1,0:T(8,128)(2,1)S(1)}, u32[]{:S(2)}, u32[]{:S(2)}) collective-permute-start(bf16[40,1024]{1,0:T(8,128)(2,1)S(1)} %get-tuple-element.62), channel_id=1, source_target_pairs={{0,12},{4,0},{8,4},{12,8},{1,13},{5,1},{9,5},{13,9},{2,14},{6,2},{... | collective-permute-start | bytes 245768 | tf_op jit(solution)/shard_map/ppermute | solution.py:312
  38.0 4.1 %shard_map.99 = (bf16[1,2,1536,1024]{3,2,1,0:T(8,128)(2,1)}, bf16[1,1536,1024]{2,1,0:T(8,128)(2,1)}) custom-call(bf16[80,768]{1,0:T(8,128)(2,1)S(1)} %get-tuple-element.59.mine_act, bf16[80,768]{1,0:T(8,128)(2,1)S(1)} %collective-permute-done.9._.other_act, bf16[2,80,768]{2,1,0:T(8,128)(2,1)S(1)} %shard_map.95.mine, ...), custom_call_target="tpu_custom_call" | custom-call | flops 754974720 | bytes 9437184 | tf_op jit(solution)/shard_map/pallas_call | solution.py:70
  42.1 1.1 %shard_map.98 = bf16[256,1024]{1,0:T(8,128)(2,1)} custom-call(bf16[160,256]{1,0:T(8,128)(2,1)S(1)} %get-tuple-element.35.pick, bf16[40,1024]{1,0:T(8,128)(2,1)S(1)} %collective-permute-done.11.refs_0_, bf16[40,1024]{1,0:T(8,128)(2,1)S(1)} %collective-permute-done.12.refs_1_, bf16[40,1024]{1,0:T(8,128)(2,1)S(1)} %collective-permute-done.13.refs_2_, ...), custom_call_target="tpu_custom_call" | custom-call | flops 83886080 | bytes 1048576 | tf_op jit(solution)/shard_map/pallas_call | solution.py:70
  (20 shorter events, 0.9 us)
Async XLA Ops:
  2.0 13.7 %collective-permute-start.3 = (bf16[40,1024]{1,0:T(8,128)(2,1)S(1)}, bf16[40,1024]{1,0:T(8,128)(2,1)S(1)}, u32[]{:S(2)}, u32[]{:S(2)}) collective-permute-start(bf16[40,1024]{1,0:T(8,128)(2,1)S(1)} %get-tuple-element.46), channel_id=1, source_target_pairs={{0,8},{4,12},{8,0},{12,4},{1,9},{5,13},{9,1},{13,5},{2,10},{6,14},... | collective-permute-start | bytes 245768 | tf_op jit(solution)/shard_map/ppermute | solution.py:319
  6.4 9.4 %collective-permute-start.2 = (bf16[80,1024]{1,0:T(8,128)(2,1)S(1)}, bf16[80,1024]{1,0:T(8,128)(2,1)S(1)}, u32[]{:S(2)}, u32[]{:S(2)}) collective-permute-start(bf16[80,1024]{1,0:T(8,128)(2,1)S(1)} %get-tuple-element.44), channel_id=1, source_target_pairs={{0,4},{4,0},{8,12},{12,8},{1,5},{5,1},{9,13},{13,9},{2,6},{6,2},{1... | collective-permute-start | bytes 491528 | tf_op jit(solution)/shard_map/ppermute | solution.py:319
  8.0 7.7 %collective-permute-start.4 = (bf16[40,1024]{1,0:T(8,128)(2,1)S(1)}, bf16[40,1024]{1,0:T(8,128)(2,1)S(1)}, u32[]{:S(2)}, u32[]{:S(2)}) collective-permute-start(bf16[40,1024]{1,0:T(8,128)(2,1)S(1)} %get-tuple-element.47), channel_id=1, source_target_pairs={{0,12},{4,8},{8,4},{12,0},{1,13},{5,9},{9,5},{13,1},{2,14},{6,10},... | collective-permute-start | bytes 245768 | tf_op jit(solution)/shard_map/ppermute | solution.py:319
  11.8 8.6 %collective-permute-start = (bf16[40,1024]{1,0:T(8,128)(2,1)S(1)}, bf16[40,1024]{1,0:T(8,128)(2,1)S(1)}, u32[]{:S(2)}, u32[]{:S(2)}) collective-permute-start(bf16[40,1024]{1,0:T(8,128)(2,1)S(1)} %get-tuple-element.42), channel_id=1, source_target_pairs={{0,12},{4,8},{8,4},{12,0},{1,13},{5,9},{9,5},{13,1},{2,14},{6,10},... | collective-permute-start | bytes 245768 | tf_op jit(solution)/shard_map/ppermute | solution.py:319
  15.7 6.0 %collective-permute-start.1 = (bf16[40,1024]{1,0:T(8,128)(2,1)S(1)}, bf16[40,1024]{1,0:T(8,128)(2,1)S(1)}, u32[]{:S(2)}, u32[]{:S(2)}) collective-permute-start(bf16[40,1024]{1,0:T(8,128)(2,1)S(1)} %get-tuple-element.43), channel_id=1, source_target_pairs={{0,8},{4,12},{8,0},{12,4},{1,9},{5,13},{9,1},{13,5},{2,10},{6,14},... | collective-permute-start | bytes 245768 | tf_op jit(solution)/shard_map/ppermute | solution.py:319
  17.2 1.6 %collective-permute-start.5 = (bf16[2,80,768]{2,1,0:T(8,128)(2,1)S(1)}, bf16[2,80,768]{2,1,0:T(8,128)(2,1)S(1)}, u32[]{:S(2)}, u32[]{:S(2)}) collective-permute-start(bf16[2,80,768]{2,1,0:T(8,128)(2,1)S(1)} %get-tuple-element.54), channel_id=1, source_target_pairs={{0,1},{1,0},{2,3},{3,2},{4,5},{5,4},{6,7},{7,6},{8,9},{9,8},{10,11... | collective-permute-start | bytes 737288 | tf_op jit(solution)/shard_map/ppermute | solution.py:319
  18.9 8.2 %collective-permute-start.8 = (bf16[2,80,768]{2,1,0:T(8,128)(2,1)S(1)}, bf16[2,80,768]{2,1,0:T(8,128)(2,1)S(1)}, u32[]{:S(2)}, u32[]{:S(2)}) collective-permute-start(bf16[2,80,768]{2,1,0:T(8,128)(2,1)S(1)} %get-tuple-element.55.refs_6_), channel_id=1, source_target_pairs={{0,2},{1,3},{2,0},{3,1},{4,6},{5,7},{6,4},{7,5},{8,10},{9,11},{10,... | collective-permute-start | bytes 737288 | tf_op jit(solution)/shard_map/ppermute | solution.py:319
  22.4 1.4 %collective-permute-start.6 = (bf16[80,768]{1,0:T(8,128)(2,1)S(1)}, bf16[80,768]{1,0:T(8,128)(2,1)S(1)}, u32[]{:S(2)}, u32[]{:S(2)}) collective-permute-start(bf16[80,768]{1,0:T(8,128)(2,1)S(1)} %shard_map.93), channel_id=1, source_target_pairs={{0,1},{1,0},{2,3},{3,2},{4,5},{5,4},{6,7},{7,6},{8,9},{9,8},{10,11... | collective-permute-start | bytes 368648 | tf_op jit(solution)/shard_map/ppermute | solution.py:319
  23.9 5.7 %collective-permute-start.7 = (bf16[80,768]{1,0:T(8,128)(2,1)S(1)}, bf16[80,768]{1,0:T(8,128)(2,1)S(1)}, u32[]{:S(2)}, u32[]{:S(2)}) collective-permute-start(bf16[80,768]{1,0:T(8,128)(2,1)S(1)} %get-tuple-element.67), channel_id=1, source_target_pairs={{0,2},{1,3},{2,0},{3,1},{4,6},{5,7},{6,4},{7,5},{8,10},{9,11},{10,... | collective-permute-start | bytes 368648 | tf_op jit(solution)/shard_map/ppermute | solution.py:319
  27.2 2.3 %collective-permute-start.9 = (bf16[80,768]{1,0:T(8,128)(2,1)S(1)}, bf16[80,768]{1,0:T(8,128)(2,1)S(1)}, u32[]{:S(2)}, u32[]{:S(2)}) collective-permute-start(bf16[80,768]{1,0:T(8,128)(2,1)S(1)} %get-tuple-element.59.mine_act), channel_id=1, source_target_pairs={{0,1},{1,0},{2,3},{3,2},{4,5},{5,4},{6,7},{7,6},{8,9},{9,8},{10,11... | collective-permute-start | bytes 368648 | tf_op jit(solution)/shard_map/ppermute | solution.py:319
  29.6 1.6 %collective-permute-start.10 = (bf16[2,80,768]{2,1,0:T(8,128)(2,1)S(1)}, bf16[2,80,768]{2,1,0:T(8,128)(2,1)S(1)}, u32[]{:S(2)}, u32[]{:S(2)}) collective-permute-start(bf16[2,80,768]{2,1,0:T(8,128)(2,1)S(1)} %shard_map.95.mine), channel_id=1, source_target_pairs={{0,1},{1,0},{2,3},{3,2},{4,5},{5,4},{6,7},{7,6},{8,9},{9,8},{10,11... | collective-permute-start | bytes 737288 | tf_op jit(solution)/shard_map/ppermute | solution.py:319
  32.1 10.0 %collective-permute-start.11 = (bf16[40,1024]{1,0:T(8,128)(2,1)S(1)}, bf16[40,1024]{1,0:T(8,128)(2,1)S(1)}, u32[]{:S(2)}, u32[]{:S(2)}) collective-permute-start(bf16[40,1024]{1,0:T(8,128)(2,1)S(1)} %get-tuple-element.60), channel_id=1, source_target_pairs={{0,4},{4,8},{8,12},{12,0},{1,5},{5,9},{9,13},{13,1},{2,6},{6,10},{... | collective-permute-start | bytes 245768 | tf_op jit(solution)/shard_map/ppermute | solution.py:312
  32.8 9.3 %collective-permute-start.12 = (bf16[40,1024]{1,0:T(8,128)(2,1)S(1)}, bf16[40,1024]{1,0:T(8,128)(2,1)S(1)}, u32[]{:S(2)}, u32[]{:S(2)}) collective-permute-start(bf16[40,1024]{1,0:T(8,128)(2,1)S(1)} %get-tuple-element.61), channel_id=1, source_target_pairs={{0,8},{4,12},{8,0},{12,4},{1,9},{5,13},{9,1},{13,5},{2,10},{6,14},... | collective-permute-start | bytes 245768 | tf_op jit(solution)/shard_map/ppermute | solution.py:312
  35.1 7.0 %collective-permute-start.13 = (bf16[40,1024]{1,0:T(8,128)(2,1)S(1)}, bf16[40,1024]{1,0:T(8,128)(2,1)S(1)}, u32[]{:S(2)}, u32[]{:S(2)}) collective-permute-start(bf16[40,1024]{1,0:T(8,128)(2,1)S(1)} %get-tuple-element.62), channel_id=1, source_target_pairs={{0,12},{4,0},{8,4},{12,8},{1,13},{5,1},{9,5},{13,9},{2,14},{6,2},{... | collective-permute-start | bytes 245768 | tf_op jit(solution)/shard_map/ppermute | solution.py:312
